TPU v7x, 32 devices: a whole 2x2x4 slice. The times are simulated.
32 devices in a mesh: groups: 2 (over y), mesh: 4 (over z), feat: 2 (over x), rep: 2 (over core).
Axes of the slice: x: 2, y: 2, z: 4, core: 2. Of those that a mesh axis runs over, the one named last changes fastest.
Arguments:
- grid_feats: bfloat16 [8192, 512], P(('groups', 'mesh', 'feat', 'rep')), parts along dimension 0, may hold values from -6 to 6
- g2m_shard: int32 [8192, 2], P(('groups', 'mesh', 'feat', 'rep')), parts along dimension 0, may hold values from 0 to 3, all different within a row; in each aligned block of 256 rows (0 to 255, 256 to 511, ...) at most 256 rows name the same one
- g2m_node: int32 [8192, 2], P(('groups', 'mesh', 'feat', 'rep')), parts along dimension 0, may hold values from 0 to 511
- mesh_init: bfloat16 [4096, 512], P(('groups', 'mesh')), parts along dimension 0, may hold values from -6 to 6
- sender_slots: int32 [16384], P(('groups', 'mesh', 'feat', 'rep')), parts along dimension 0, may hold values from 0 to 639, as said below
- receivers: int32 [16384], P(('groups', 'mesh', 'feat', 'rep')), parts along dimension 0, may hold values from 0 to 511
- halo_index: int32 [8, 4, 32], P(('groups', 'mesh')), parts along dimension 0, may hold values from 0 to 512, as said below
- w_enc_grid: bfloat16 [512, 512], replicated, may hold values from -0.25 to 0.25
- w_enc_mesh: bfloat16 [512, 512], replicated, may hold values from -0.25 to 0.25
- w_enc_out: bfloat16 [512, 512], replicated, may hold values from -0.25 to 0.25
- enc_gain: float32 [512], replicated, may hold values from 0.1 to 1.9
- w_send: bfloat16 [3, 512, 512], replicated, may hold values from -0.25 to 0.25
- w_recv: bfloat16 [3, 512, 512], replicated, may hold values from -0.25 to 0.25
- w_out: bfloat16 [3, 512, 512], replicated, may hold values from -0.25 to 0.25
- layer_gain: float32 [3, 512], replicated, may hold values from 0.1 to 1.9
- out_cot: bfloat16 [4096, 512], P(('groups', 'mesh')), parts along dimension 0, may hold values from -6 to 6
Outputs:
- final_mesh: bfloat16 [4096, 512], P(('groups', 'mesh')), parts along dimension 0
- grid_grad: float32 [8192, 512], P(('groups', 'mesh', 'feat', 'rep')), parts along dimension 0
There are 2 independent parts, one for each index of `groups`. A program takes and returns all parts, laid end to end along the dimension named above; an argument that names none is the same for every part. Nothing has to cross between parts.
Inputs may be any that keep to these rules, and one draw needn't show every extreme that they name: `g2m_shard`: in each aligned block of 256 rows (the rows of one device) no shard is named more than 256 times, a bound that some block reaches; the 2 shards of a row differ. halo_index[s, d] lists distinct nodes of shard s, numbered within the shard, followed by padding 512; it holds at least half of 32 nodes when s differs from d, the list of a shard for itself is all padding, the lists of shard 3 for every other shard are full, and for some d every list of another shard is full. `sender_slots`: A value below 512 is a node of the edge's own shard. A value 512 + s * 32 + k names entry k of halo_index[s, o] for the edge's shard o, with s other than o, and that entry is never padding.
All inputs are finite; a program needn't handle non-finite values.
Results may differ from a plain program's by a relative error of at most 0.018.
Values may be sent and summed in bfloat16 or wider, within the bound.
No kernel may reach another device: no remote copies, remote signals or barrier semaphores. Data moves between devices by JAX's collectives and lax.ppermute only.
A program may use at most 128 MiB of HBM per device.

v0:
```python
import jax
import jax.numpy as jnp
from jax import lax
from jax.sharding import PartitionSpec as P

LAYERS = 3


eps = 1e-05


def silu_slope(values):
    sigma = jax.nn.sigmoid(values)
    return sigma * (1.0 + values * (1.0 - sigma))


def norm_scale(totals):
    return lax.rsqrt(jnp.mean(totals * totals, axis=-1, keepdims=True) + eps)


def norm_back(totals, scaled, gain_row, upstream):
    normed = totals * scaled
    slope = upstream * gain_row
    return scaled * (slope - normed * jnp.mean(slope * normed, axis=-1, keepdims=True))


def product(left, right):
    return jnp.dot(left, right, preferred_element_type=jnp.float32)


def product_back(left, right):
    return lax.dot_general(
        left, right, (((1,), (1,)), ((), ())), preferred_element_type=jnp.float32
    )


def on_device(
    grid_feats,
    g2m_shard,
    g2m_node,
    mesh_init,
    sender_slots,
    receivers,
    halo_index,
    w_enc_grid,
    w_enc_mesh,
    w_enc_out,
    enc_gain,
    w_send,
    w_recv,
    w_out,
    layer_gain,
    out_cot,
):
    shard_count = lax.axis_size("mesh")
    group_size = lax.axis_size(("feat", "rep"))
    member_index = lax.axis_index(("feat", "rep"))
    node_rows = mesh_init.shape[0]
    features = mesh_init.shape[1]
    share_rows = node_rows // group_size
    grid_rows, top_count = g2m_shard.shape
    bucket = 2 * grid_rows * top_count // shard_count
    halo_lists = halo_index[0]
    halo_depth = halo_lists.shape[1]

    def combine(partial_value, base_rows, gain_row):
        node_agg = lax.psum_scatter(
            partial_value.astype(jnp.bfloat16), ("feat", "rep"), scatter_dimension=0, tiled=True
        ).astype(jnp.float32)
        scaled = norm_scale(node_agg)
        own_rows = lax.dynamic_slice_in_dim(base_rows, member_index * share_rows, share_rows, 0)
        fresh = (own_rows.astype(jnp.float32) + node_agg * scaled * gain_row).astype(jnp.bfloat16)
        whole = lax.all_gather(fresh, ("feat", "rep"), axis=0, tiled=True)
        return (whole, node_agg, scaled)

    def spread(node_agg, scaled, gain_row, upstream):
        grad_rows_local = norm_back(node_agg, scaled, gain_row, upstream).astype(jnp.bfloat16)
        return lax.all_gather(grad_rows_local, ("feat", "rep"), axis=0, tiled=True)

    pair_shard = g2m_shard.reshape(-1)
    pair_node = g2m_node.reshape(-1)
    shard_hits = (pair_shard[:, None] == jnp.arange(shard_count, dtype=jnp.int32)[None, :]).astype(
        jnp.int32
    )
    bucket_rank = jnp.sum((jnp.cumsum(shard_hits, axis=0) - shard_hits) * shard_hits, axis=1)
    pair_slot = pair_shard * bucket + bucket_rank
    outgoing_rows = (
        jnp.zeros((shard_count * bucket, features), jnp.bfloat16)
        .at[pair_slot]
        .set(jnp.repeat(grid_feats, top_count, axis=0))
    )
    target_node = (
        jnp.full((shard_count * bucket,), node_rows, jnp.int32).at[pair_slot].set(pair_node)
    )
    incoming, slot_node = (
        lax.all_to_all(
            outgoing_rows.reshape(shard_count, bucket, features),
            "mesh",
            split_axis=0,
            concat_axis=0,
            tiled=True,
        ),
        lax.all_to_all(
            target_node.reshape(shard_count, bucket),
            "mesh",
            split_axis=0,
            concat_axis=0,
            tiled=True,
        ),
    )
    incoming = incoming.reshape(-1, features)
    slot_node = slot_node.reshape(-1)
    mesh_rows = jnp.take(mesh_init, slot_node, axis=0, mode="fill", fill_value=0)
    enc_pre = product(incoming, w_enc_grid) + product(mesh_rows, w_enc_mesh)
    enc_act = jax.nn.silu(enc_pre).astype(jnp.bfloat16)
    enc_msg = product(enc_act, w_enc_out)
    enc_part = jax.ops.segment_sum(enc_msg, slot_node, num_segments=node_rows + 1)[:node_rows]
    hidden, enc_agg, enc_scale = combine(enc_part, mesh_init, enc_gain)
    records = []
    for layer_index in range(LAYERS):
        outgoing = jnp.take(hidden, halo_lists, axis=0, mode="fill", fill_value=0)
        gathered = lax.all_to_all(outgoing, "mesh", split_axis=0, concat_axis=0, tiled=True)
        remote_rows = gathered.reshape(-1, features)
        lookup_rows = jnp.concatenate([hidden, remote_rows], axis=0)
        send_rows = jnp.take(lookup_rows, sender_slots, axis=0)
        recv_rows = jnp.take(hidden, receivers, axis=0)
        edge_pre = product(send_rows, w_send[layer_index]) + product(recv_rows, w_recv[layer_index])
        edge_act = jax.nn.silu(edge_pre).astype(jnp.bfloat16)
        edge_msg = product(edge_act, w_out[layer_index])
        partial_value = jax.ops.segment_sum(edge_msg, receivers, num_segments=node_rows)
        hidden, node_agg, scaled = combine(partial_value, hidden, layer_gain[layer_index])
        records.append((edge_pre, node_agg, scaled))
    upstream = lax.dynamic_slice_in_dim(out_cot, member_index * share_rows, share_rows, 0).astype(
        jnp.float32
    )
    for layer_index in reversed(range(LAYERS)):
        edge_pre, node_agg, scaled = records[layer_index]
        grad_agg = spread(node_agg, scaled, layer_gain[layer_index], upstream)
        grad_msg = jnp.take(grad_agg, receivers, axis=0)
        grad_act = product_back(grad_msg, w_out[layer_index])
        grad_pre = (grad_act * silu_slope(edge_pre)).astype(jnp.bfloat16)
        grad_send = product_back(grad_pre, w_send[layer_index])
        grad_recv = product_back(grad_pre, w_recv[layer_index])
        by_slot = jax.ops.segment_sum(
            grad_send, sender_slots, num_segments=node_rows + shard_count * halo_depth
        )
        giveback_slot_grad = by_slot[node_rows:].reshape(shard_count, halo_depth, features)
        giveback_returned = lax.all_to_all(
            giveback_slot_grad.astype(jnp.bfloat16), "mesh", split_axis=0, concat_axis=0, tiled=True
        ).astype(giveback_slot_grad.dtype)
        targets = halo_lists.reshape(-1)
        totals = jax.ops.segment_sum(
            giveback_returned.reshape(-1, features), targets, num_segments=node_rows + 1
        )
        partial_value = (
            jax.ops.segment_sum(grad_recv, receivers, num_segments=node_rows)
            + by_slot[:node_rows]
            + totals[:node_rows]
        )
        upstream = upstream + lax.psum_scatter(
            partial_value.astype(jnp.bfloat16), ("feat", "rep"), scatter_dimension=0, tiled=True
        ).astype(jnp.float32)
    grad_sum = spread(enc_agg, enc_scale, enc_gain, upstream)
    grad_msg = jnp.take(grad_sum, slot_node, axis=0, mode="fill", fill_value=0)
    grad_act = product_back(grad_msg, w_enc_out)
    grad_enc = (grad_act * silu_slope(enc_pre)).astype(jnp.bfloat16)
    slot_grad = product_back(grad_enc, w_enc_grid)
    returned = lax.all_to_all(
        slot_grad.reshape(shard_count, bucket, features).astype(jnp.bfloat16),
        "mesh",
        split_axis=0,
        concat_axis=0,
        tiled=True,
    ).astype(jnp.float32)
    pair_grad = jnp.take(returned.reshape(-1, features), pair_slot, axis=0)
    grid_grad = jnp.sum(pair_grad.reshape(grid_rows, top_count, features), axis=1)
    return (hidden, grid_grad)


def solution(mesh):
    return jax.shard_map(
        on_device,
        mesh=mesh,
        in_specs=(
            P(("groups", "mesh", "feat", "rep"), None),
            P(("groups", "mesh", "feat", "rep"), None),
            P(("groups", "mesh", "feat", "rep"), None),
            P(("groups", "mesh"), None),
            P(("groups", "mesh", "feat", "rep")),
            P(("groups", "mesh", "feat", "rep")),
            P(("groups", "mesh"), None, None),
            P(),
            P(),
            P(),
            P(),
            P(),
            P(),
            P(),
            P(),
            P(("groups", "mesh"), None),
        ),
        out_specs=(P(("groups", "mesh"), None), P(("groups", "mesh", "feat", "rep"), None)),
        check_vma=False,
    )
```

profile of v0, /device:TPU:0, one launch (start us, length us, event | category | flops | bytes accessed | tf_op | source)
XLA Modules:
  0.0 523.2 jit_solution(6229749470420560259)
XLA Ops:
  12.0 3.0 scatter_custom_fusion
  15.1 6.3 %all-to-all-start = ((s32[4,1,256]{2,1,0:T(1,128)}), s32[4,1,256]{2,1,0:T(1,128)S(1)}, u32[]{:S(2)}, u32[]{:S(2)}) async-start(s32[4,1,256]{2,1,0:T(1,128)} %bitcast.3), calls=%async_computation | async-start | bytes 8192 | tf_op jit(solution)/shard_map/all_to_all | solution.py:103
  22.8 3.5 scatter_custom_fusion.1
  26.9 4.5 all-to-all-start.1
  31.4 4.0 gather_fusion.1
  35.4 21.1 %all-to-all-done.1 = bf16[4,256,512]{2,1,0:T(8,128)(2,1)S(1)} async-done(((bf16[4,256,512]{2,1,0:T(8,128)(2,1)}), bf16[4,256,512]{2,1,0:T(8,128)(2,1)S(1)}, u32[]{:S(2)}, u32[]{:S(2)}) %all-to-all-start.1) | async-done | bytes 1048608 | tf_op jit(solution)/shard_map/all_to_all | solution.py:96
  62.6 8.2 %scatter_custom_fusion.2 = f32[513,512]{1,0:T(8,128)S(1)} fusion(s32[1024]{0:T(1024)S(1)} %bitcast.121, f32[1024,512]{1,0:T(8,128)} %fusion.7, f32[]{:T(128)} %constant.71.clone.1), kind=kCustom, calls=%fused_computation.77 | custom fusion | flops 524288 | bytes 1051136 | tf_op jit(solution)/shard_map/scatter-add | solution.py:117
  71.8 20.8 %reduce-scatter.8.cloned.1.call-done = bf16[128,512]{1,0:T(8,128)(2,1)} async-done(((bf16[512,512]{1,0:T(8,128)(2,1)}), bf16[128,512]{1,0:T(8,128)(2,1)}) %reduce-scatter.8.cloned.1.call-update) | async-done | bytes 131088 | tf_op jit(solution)/shard_map/reduce_scatter | solution.py:67
  94.7 6.8 %all_gather.24 = bf16[512,512]{1,0:T(8,128)(2,1)S(1)} all-gather(bf16[128,512]{1,0:T(8,128)(2,1)S(1)} %fusion.118), channel_id=1, replica_groups=mesh['groups'=2,'mesh'=4,'feat'=2,'rep'=2] {'feat','rep'}, dimensions={0}, use_global_device_ids=true | all-gather | bytes 655360 | tf_op jit(solution)/shard_map/all_gather | solution.py:73
  103.1 4.6 all-to-all-start.2
  107.9 2.6 gather_fusion.4
  110.6 3.5 all-to-all-done.2
  114.2 2.6 gather_fusion.3
  120.1 2.5 fusion.46
  122.6 5.2 %scatter_custom_fusion.3 = f32[512,512]{1,0:T(8,128)} fusion(s32[512]{0:T(512)S(1)} %copy-done.19, f32[512,512]{1,0:T(8,128)} %fusion.46, f32[]{:T(128)} %constant.71.clone.1), kind=kCustom, calls=%fused_computation.122 | custom fusion | flops 262144 | bytes 1049088 | tf_op jit(solution)/shard_map/scatter-add | solution.py:130
  127.9 2.1 convert_element_type.140
  130.0 20.4 %reduce-scatter.10.cloned.1.call-done = bf16[128,512]{1,0:T(8,128)(2,1)} async-done(((bf16[512,512]{1,0:T(8,128)(2,1)}), bf16[128,512]{1,0:T(8,128)(2,1)}) %reduce-scatter.10.cloned.1.call-update) | async-done | bytes 131088 | tf_op jit(solution)/shard_map/reduce_scatter | solution.py:67
  152.5 6.8 %all_gather.25 = bf16[512,512]{1,0:T(8,128)(2,1)S(1)} all-gather(bf16[128,512]{1,0:T(8,128)(2,1)S(1)} %fusion.125), channel_id=1, replica_groups=mesh['groups'=2,'mesh'=4,'feat'=2,'rep'=2] {'feat','rep'}, dimensions={0}, use_global_device_ids=true | all-gather | bytes 655360 | tf_op jit(solution)/shard_map/all_gather | solution.py:73
  160.9 4.6 all-to-all-start.3
  165.5 2.6 gather_fusion.7
  168.1 3.8 all-to-all-done.3
  172.0 2.6 gather_fusion.6
  177.8 2.5 fusion.36
  180.3 5.2 %scatter_custom_fusion.4 = f32[512,512]{1,0:T(8,128)} fusion(s32[512]{0:T(512)S(1)} %copy-done.19, f32[512,512]{1,0:T(8,128)} %fusion.36, f32[]{:T(128)} %constant.71.clone.1), kind=kCustom, calls=%fused_computation.120 | custom fusion | flops 262144 | bytes 1049088 | tf_op jit(solution)/shard_map/scatter-add | solution.py:130
  187.7 20.5 %reduce-scatter.12.cloned.1.call-done = bf16[128,512]{1,0:T(8,128)(2,1)} async-done(((bf16[512,512]{1,0:T(8,128)(2,1)}), bf16[128,512]{1,0:T(8,128)(2,1)}) %reduce-scatter.12.cloned.1.call-update) | async-done | bytes 131088 | tf_op jit(solution)/shard_map/reduce_scatter | solution.py:67
  210.2 6.8 %all_gather.26 = bf16[512,512]{1,0:T(8,128)(2,1)S(1)} all-gather(bf16[128,512]{1,0:T(8,128)(2,1)S(1)} %fusion.132), channel_id=1, replica_groups=mesh['groups'=2,'mesh'=4,'feat'=2,'rep'=2] {'feat','rep'}, dimensions={0}, use_global_device_ids=true | all-gather | bytes 655360 | tf_op jit(solution)/shard_map/all_gather | solution.py:73
  218.6 4.6 all-to-all-start.4
  223.6 2.6 gather_fusion.10
  226.2 3.4 all-to-all-done.4
  229.7 2.6 gather_fusion.9
  235.5 2.5 fusion.26
  238.0 5.3 %scatter_custom_fusion.5 = f32[512,512]{1,0:T(8,128)} fusion(s32[512]{0:T(512)S(1)} %copy-done.19, f32[512,512]{1,0:T(8,128)} %fusion.26, f32[]{:T(128)} %constant.71.clone.1), kind=kCustom, calls=%fused_computation.118 | custom fusion | flops 262144 | bytes 1049088 | tf_op jit(solution)/shard_map/scatter-add | solution.py:130
  245.5 20.4 %reduce-scatter.14.cloned.1.call-done = bf16[128,512]{1,0:T(8,128)(2,1)} async-done(((bf16[512,512]{1,0:T(8,128)(2,1)}), bf16[128,512]{1,0:T(8,128)(2,1)}) %reduce-scatter.14.cloned.1.call-update) | async-done | bytes 131088 | tf_op jit(solution)/shard_map/reduce_scatter | solution.py:67
  269.1 6.8 %all_gather.28 = bf16[512,512]{1,0:T(8,128)(2,1)S(1)} all-gather(bf16[128,512]{1,0:T(8,128)(2,1)S(1)} %get-tuple-element.4), channel_id=1, replica_groups=mesh['groups'=2,'mesh'=4,'feat'=2,'rep'=2] {'feat','rep'}, dimensions={0}, use_global_device_ids=true | all-gather | bytes 655360 | tf_op jit(solution)/shard_map/all_gather | solution.py:78
  280.0 2.5 fusion.31
  282.5 5.3 %scatter_custom_fusion.6 = f32[640,512]{1,0:T(8,128)} fusion(s32[512]{0:T(512)} %param.28, f32[512,512]{1,0:T(8,128)} %fusion.31, f32[]{:T(128)} %constant.71.clone.1), kind=kCustom, calls=%fused_computation.69 | custom fusion | flops 262144 | bytes 1311232 | tf_op jit(solution)/shard_map/scatter-add | solution.py:144
  289.4 4.6 all-to-all-start.5
  295.7 4.8 all-to-all-done.5
  300.4 2.4 scatter_custom_fusion.7
  304.6 4.7 scatter_fusion
  310.2 20.5 %reduce-scatter.16.cloned.1.call-done = bf16[128,512]{1,0:T(8,128)(2,1)} async-done(((bf16[512,512]{1,0:T(8,128)(2,1)}), bf16[128,512]{1,0:T(8,128)(2,1)}) %reduce-scatter.16.cloned.1.call-update) | async-done | bytes 131088 | tf_op jit(solution)/shard_map/reduce_scatter | solution.py:160
  333.0 6.8 %all_gather.29 = bf16[512,512]{1,0:T(8,128)(2,1)S(1)} all-gather(bf16[128,512]{1,0:T(8,128)(2,1)S(1)} %fusion.136), channel_id=1, replica_groups=mesh['groups'=2,'mesh'=4,'feat'=2,'rep'=2] {'feat','rep'}, dimensions={0}, use_global_device_ids=true | all-gather | bytes 655360 | tf_op jit(solution)/shard_map/all_gather | solution.py:78
  343.8 2.5 fusion.41
  346.3 5.3 %scatter_custom_fusion.9 = f32[640,512]{1,0:T(8,128)} fusion(s32[512]{0:T(512)} %param.28, f32[512,512]{1,0:T(8,128)} %fusion.41, f32[]{:T(128)} %constant.71.clone.1), kind=kCustom, calls=%fused_computation.67 | custom fusion | flops 262144 | bytes 1311232 | tf_op jit(solution)/shard_map/scatter-add | solution.py:144
  353.2 4.6 all-to-all-start.6
  359.3 4.9 all-to-all-done.6
  364.3 2.4 scatter_custom_fusion.10
  368.4 4.9 scatter_fusion.1
  374.2 20.5 %reduce-scatter.18.cloned.1.call-done = bf16[128,512]{1,0:T(8,128)(2,1)} async-done(((bf16[512,512]{1,0:T(8,128)(2,1)}), bf16[128,512]{1,0:T(8,128)(2,1)}) %reduce-scatter.18.cloned.1.call-update) | async-done | bytes 131088 | tf_op jit(solution)/shard_map/reduce_scatter | solution.py:160
  397.0 6.8 %all_gather.30 = bf16[512,512]{1,0:T(8,128)(2,1)S(1)} all-gather(bf16[128,512]{1,0:T(8,128)(2,1)S(1)} %fusion.129), channel_id=1, replica_groups=mesh['groups'=2,'mesh'=4,'feat'=2,'rep'=2] {'feat','rep'}, dimensions={0}, use_global_device_ids=true | all-gather | bytes 655360 | tf_op jit(solution)/shard_map/all_gather | solution.py:78
  407.8 2.5 fusion.51
  410.4 5.3 %scatter_custom_fusion.12 = f32[640,512]{1,0:T(8,128)} fusion(s32[512]{0:T(512)} %param.28, f32[512,512]{1,0:T(8,128)} %fusion.51, f32[]{:T(128)} %constant.71.clone.1), kind=kCustom, calls=%fused_computation.65 | custom fusion | flops 262144 | bytes 1311232 | tf_op jit(solution)/shard_map/scatter-add | solution.py:144
  417.3 4.6 all-to-all-start.7
  423.4 5.0 all-to-all-done.7
  431.5 4.9 scatter_fusion.2
  437.4 20.5 %reduce-scatter.20.cloned.1.call-done = bf16[128,512]{1,0:T(8,128)(2,1)} async-done(((bf16[512,512]{1,0:T(8,128)(2,1)}), bf16[128,512]{1,0:T(8,128)(2,1)}) %reduce-scatter.20.cloned.1.call-update) | async-done | bytes 131088 | tf_op jit(solution)/shard_map/reduce_scatter | solution.py:160
  460.0 6.8 %all_gather.31 = bf16[512,512]{1,0:T(8,128)(2,1)S(1)} all-gather(bf16[128,512]{1,0:T(8,128)(2,1)S(1)} %fusion.122), channel_id=1, replica_groups=mesh['groups'=2,'mesh'=4,'feat'=2,'rep'=2] {'feat','rep'}, dimensions={0}, use_global_device_ids=true | all-gather | bytes 655360 | tf_op jit(solution)/shard_map/all_gather | solution.py:78
  466.8 5.1 gather_fusion.14
  471.9 4.0 convolution_convert_fusion
  475.9 4.7 all-to-all-start.8
  481.1 7.0 %all_gather.27 = bf16[512,512]{1,0:T(8,128)(2,1)S(1)} all-gather(bf16[128,512]{1,0:T(8,128)(2,1)S(1)} %get-tuple-element.6), channel_id=1, replica_groups=mesh['groups'=2,'mesh'=4,'feat'=2,'rep'=2] {'feat','rep'}, dimensions={0}, use_global_device_ids=true | all-gather | bytes 655360 | tf_op jit(solution)/shard_map/all_gather | solution.py:73
  488.1 18.9 %all-to-all-done.8 = bf16[4,256,512]{2,1,0:T(8,128)(2,1)} async-done(((bf16[4,256,512]{2,1,0:T(8,128)(2,1)}), bf16[4,256,512]{2,1,0:T(8,128)(2,1)}, u32[]{:S(2)}, u32[]{:S(2)}) %all-to-all-start.8) | async-done | bytes 1048608 | tf_op jit(solution)/shard_map/all_to_all | solution.py:168
  508.5 2.3 gather_fusion
  512.6 2.5 select_reduce_fusion
  (205 shorter events, 84.9 us)
Async XLA Ops:
  7.2 53.4 %copy-start = (bf16[512,512]{1,0:T(8,128)(2,1)S(1)}, bf16[512,512]{1,0:T(8,128)(2,1)}, u32[]{:S(2)}) copy-start(bf16[512,512]{1,0:T(8,128)(2,1)} %param.33) | copy-start | bytes 1572868
  12.0 3.0 copy-start.26
  12.0 14.9 %copy-start.29 = (s32[512,1]{0,1:T(1,128)}, s32[512,1]{0,1:T(1,128)S(1)}, u32[]{:S(2)}) copy-start(s32[512,1]{0,1:T(1,128)S(1)} %compare_select_fusion) | copy-start | bytes 6148
  15.1 11.9 %all-to-all-start = ((s32[4,1,256]{2,1,0:T(1,128)}), s32[4,1,256]{2,1,0:T(1,128)S(1)}, u32[]{:S(2)}, u32[]{:S(2)}) async-start(s32[4,1,256]{2,1,0:T(1,128)} %bitcast.3), calls=%async_computation | async-start | bytes 8192 | tf_op jit(solution)/shard_map/all_to_all | solution.py:103
  22.8 8.6 %copy-start.28 = (s32[1,4,32]{2,1,0:T(4,128)S(1)}, s32[1,4,32]{2,1,0:T(4,128)}, u32[]{:S(2)}) copy-start(s32[1,4,32]{2,1,0:T(4,128)} %param.30) | copy-start | bytes 1540
  22.8 8.6 %copy-start.1 = (bf16[512,512]{1,0:T(8,128)(2,1)S(1)}, bf16[512,512]{1,0:T(8,128)(2,1)}, u32[]{:S(2)}) copy-start(bf16[512,512]{1,0:T(8,128)(2,1)} %param.27) | copy-start | bytes 1572868
  26.9 29.6 %all-to-all-start.1 = ((bf16[4,256,512]{2,1,0:T(8,128)(2,1)}), bf16[4,256,512]{2,1,0:T(8,128)(2,1)S(1)}, u32[]{:S(2)}, u32[]{:S(2)}) async-start(bf16[4,256,512]{2,1,0:T(8,128)(2,1)} %bitcast.5), calls=%async_computation.1 | async-start | bytes 2097152 | tf_op jit(solution)/shard_map/all_to_all | solution.py:96
  31.4 61.2 %reduce-scatter.8.cloned.1.call-start = ((), (), s32[]{:S(2)}) async-start(), calls=%async_computation.16 | async-start | bytes 655360 | tf_op jit(solution)/shard_map/reduce_scatter | solution.py:67
  35.4 22.9 %copy-start.41 = (pred[1024]{0:T(1024)(128)(4,1)}, pred[1024]{0:T(1024)(128)(4,1)S(1)}, u32[]{:S(2)}) copy-start(pred[1024]{0:T(1024)(128)(4,1)S(1)} %compare_and_fusion) | copy-start | bytes 3076
  56.6 1.8 copy-start.18
  59.2 1.4 copy-start.4
  62.6 9.1 %copy-start.31 = (s32[512]{0:T(512)S(1)}, s32[512]{0:T(512)}, u32[]{:S(2)}) copy-start(s32[512]{0:T(512)} %param.28) | copy-start | bytes 6148
  62.6 9.2 %copy-start.19 = (s32[512]{0:T(512)S(1)}, s32[512]{0:T(512)}, u32[]{:S(2)}) copy-start(s32[512]{0:T(512)} %param.29) | copy-start | bytes 6148
  62.6 31.1 %copy-start.22 = (f32[512]{0:T(512)S(1)}, f32[512]{0:T(512)}, u32[]{:S(2)}) copy-start(f32[512]{0:T(512)} %param.34) | copy-start | bytes 6148
  93.7 14.0 %copy-start.39 = (f32[128]{0:T(128)}, f32[128]{0:T(128)S(1)}, u32[]{:S(2)}) copy-start(f32[128]{0:T(128)S(1)} %add_rsqrt_fusion.3) | copy-start | bytes 1540
  103.1 11.0 %all-to-all-start.2 = ((bf16[4,32,512]{2,1,0:T(8,128)(2,1)}), bf16[4,32,512]{2,1,0:T(8,128)(2,1)S(1)}, u32[]{:S(2)}, u32[]{:S(2)}) async-start(bf16[4,32,512]{2,1,0:T(8,128)(2,1)} %broadcast_select_fusion.2), calls=%async_computation.3 | async-start | bytes 262144 | tf_op jit(solution)/shard_map/all_to_all | solution.py:122
  107.7 42.7 %reduce-scatter.10.cloned.1.call-start = ((), (), s32[]{:S(2)}) async-start(), calls=%async_computation.17 | async-start | bytes 655360 | tf_op jit(solution)/shard_map/reduce_scatter | solution.py:67
  107.9 126.1 %copy-start.32 = (pred[512]{0:T(512)(128)(4,1)}, pred[512]{0:T(512)(128)(4,1)S(1)}, u32[]{:S(2)}) copy-start(pred[512]{0:T(512)(128)(4,1)S(1)} %compare_and_fusion.2) | copy-start | bytes 1540
  116.8 1.8 copy-start.2
  116.8 1.9 copy-start.11
  119.2 1.0 copy-start.15
  122.6 7.4 %copy-start.37 = (f32[3,512]{1,0:T(4,128)S(1)}, f32[3,512]{1,0:T(4,128)}, u32[]{:S(2)}) copy-start(f32[3,512]{1,0:T(4,128)} %param.38) | copy-start | bytes 18436
  130.0 79.2 %copy-start.20 = (f32[1,512]{1,0:T(1,128)}, f32[1,512]{1,0:T(1,128)S(1)}, u32[]{:S(2)}) copy-start(f32[1,512]{1,0:T(1,128)S(1)} %get-tuple-element.10) | copy-start | bytes 6148
  130.0 136.9 %copy-start.24 = (f32[1,512]{1,0:T(1,128)}, f32[1,512]{1,0:T(1,128)S(1)}, u32[]{:S(2)}) copy-start(f32[1,512]{1,0:T(1,128)S(1)} %get-tuple-element.8) | copy-start | bytes 6148
  151.5 16.6 %copy-start.38 = (f32[128]{0:T(128)}, f32[128]{0:T(128)S(1)}, u32[]{:S(2)}) copy-start(f32[128]{0:T(128)S(1)} %add_rsqrt_fusion.2) | copy-start | bytes 1540
  160.9 11.0 %all-to-all-start.3 = ((bf16[4,32,512]{2,1,0:T(8,128)(2,1)}), bf16[4,32,512]{2,1,0:T(8,128)(2,1)S(1)}, u32[]{:S(2)}, u32[]{:S(2)}) async-start(bf16[4,32,512]{2,1,0:T(8,128)(2,1)} %broadcast_select_fusion.1), calls=%async_computation.5 | async-start | bytes 262144 | tf_op jit(solution)/shard_map/all_to_all | solution.py:122
  165.5 42.7 %reduce-scatter.12.cloned.1.call-start = ((), (), s32[]{:S(2)}) async-start(), calls=%async_computation.18 | async-start | bytes 655360 | tf_op jit(solution)/shard_map/reduce_scatter | solution.py:67
  174.6 1.7 copy-start.12
  176.8 1.0 copy-start.16
  209.2 17.1 %copy-start.35 = (f32[128]{0:T(128)}, f32[128]{0:T(128)S(1)}, u32[]{:S(2)}) copy-start(f32[128]{0:T(128)S(1)} %add_rsqrt_fusion.1) | copy-start | bytes 1540
  218.6 11.0 %all-to-all-start.4 = ((bf16[4,32,512]{2,1,0:T(8,128)(2,1)}), bf16[4,32,512]{2,1,0:T(8,128)(2,1)S(1)}, u32[]{:S(2)}, u32[]{:S(2)}) async-start(bf16[4,32,512]{2,1,0:T(8,128)(2,1)} %broadcast_select_fusion), calls=%async_computation.7 | async-start | bytes 262144 | tf_op jit(solution)/shard_map/all_to_all | solution.py:122
  223.2 42.7 %reduce-scatter.14.cloned.1.call-start = ((), (), s32[]{:S(2)}) async-start(), calls=%async_computation.19 | async-start | bytes 655360 | tf_op jit(solution)/shard_map/reduce_scatter | solution.py:67
  232.3 1.8 copy-start.10
  234.6 1.0 copy-start.17
  238.0 28.9 %copy-start.8 = (bf16[512,512]{1,0:T(8,128)(2,1)S(1)}, bf16[512,512]{1,0:T(8,128)(2,1)}, u32[]{:S(2)}) copy-start(bf16[512,512]{1,0:T(8,128)(2,1)} %param.39) | copy-start | bytes 1572868
  245.5 118.7 %copy-start.43 = (s32[128]{0:T(128)}, s32[128]{0:T(128)S(1)}, u32[]{:S(2)}) copy-start(s32[128]{0:T(128)S(1)} %reshape.398) | copy-start | bytes 1540
  275.9 2.0 copy-start.33
  289.4 11.0 %all-to-all-start.5 = ((bf16[4,32,512]{2,1,0:T(8,128)(2,1)}), bf16[4,32,512]{2,1,0:T(8,128)(2,1)S(1)}, u32[]{:S(2)}, u32[]{:S(2)}) async-start(bf16[4,32,512]{2,1,0:T(8,128)(2,1)} %bitcast.26), calls=%async_computation.9 | async-start | bytes 262144 | tf_op jit(solution)/shard_map/all_to_all | solution.py:148
  294.0 36.7 %reduce-scatter.16.cloned.1.call-start = ((), (), s32[]{:S(2)}) async-start(), calls=%async_computation.20 | async-start | bytes 655360 | tf_op jit(solution)/shard_map/reduce_scatter | solution.py:160
  309.3 21.4 %copy-start.6 = (bf16[128,512]{1,0:T(8,128)(2,1)S(1)}, bf16[128,512]{1,0:T(8,128)(2,1)}, u32[]{:S(2)}) copy-start(bf16[128,512]{1,0:T(8,128)(2,1)} %reduce-scatter.12.cloned.1.call-done) | copy-start | bytes 393220
  309.3 21.4 %copy-start.21 = (f32[1,512]{1,0:T(1,128)S(1)}, f32[1,512]{1,0:T(1,128)}, u32[]{:S(2)}) copy-start(f32[1,512]{1,0:T(1,128)} %copy-done.20) | copy-start | bytes 6148
  309.3 21.4 %copy-start.36 = (f32[128]{0:T(128)S(1)}, f32[128]{0:T(128)}, u32[]{:S(2)}) copy-start(f32[128]{0:T(128)} %copy-done.35) | copy-start | bytes 1540
  353.2 11.0 %all-to-all-start.6 = ((bf16[4,32,512]{2,1,0:T(8,128)(2,1)}), bf16[4,32,512]{2,1,0:T(8,128)(2,1)S(1)}, u32[]{:S(2)}, u32[]{:S(2)}) async-start(bf16[4,32,512]{2,1,0:T(8,128)(2,1)} %bitcast.28), calls=%async_computation.11 | async-start | bytes 262144 | tf_op jit(solution)/shard_map/all_to_all | solution.py:148
  357.8 36.9 %reduce-scatter.18.cloned.1.call-start = ((), (), s32[]{:S(2)}) async-start(), calls=%async_computation.21 | async-start | bytes 655360 | tf_op jit(solution)/shard_map/reduce_scatter | solution.py:160
  373.3 21.4 %copy-start.3 = (bf16[128,512]{1,0:T(8,128)(2,1)S(1)}, bf16[128,512]{1,0:T(8,128)(2,1)}, u32[]{:S(2)}) copy-start(bf16[128,512]{1,0:T(8,128)(2,1)} %reduce-scatter.16.cloned.1.call-done) | copy-start | bytes 393220
  373.3 21.4 %copy-start.7 = (bf16[128,512]{1,0:T(8,128)(2,1)S(1)}, bf16[128,512]{1,0:T(8,128)(2,1)}, u32[]{:S(2)}) copy-start(bf16[128,512]{1,0:T(8,128)(2,1)} %reduce-scatter.10.cloned.1.call-done) | copy-start | bytes 393220
  403.8 2.0 copy-start.34
  417.3 11.0 %all-to-all-start.7 = ((bf16[4,32,512]{2,1,0:T(8,128)(2,1)}), bf16[4,32,512]{2,1,0:T(8,128)(2,1)S(1)}, u32[]{:S(2)}, u32[]{:S(2)}) async-start(bf16[4,32,512]{2,1,0:T(8,128)(2,1)} %bitcast.30), calls=%async_computation.13 | async-start | bytes 262144 | tf_op jit(solution)/shard_map/all_to_all | solution.py:148
  421.9 35.9 %reduce-scatter.20.cloned.1.call-start = ((), (), s32[]{:S(2)}) async-start(), calls=%async_computation.22 | async-start | bytes 655360 | tf_op jit(solution)/shard_map/reduce_scatter | solution.py:160
  436.4 21.4 %copy-start.9 = (bf16[512,512]{1,0:T(8,128)(2,1)S(1)}, bf16[512,512]{1,0:T(8,128)(2,1)}, u32[]{:S(2)}) copy-start(bf16[512,512]{1,0:T(8,128)(2,1)} %param.39) | copy-start | bytes 1572868
  436.5 21.4 %copy-start.13 = (bf16[128,512]{1,0:T(8,128)(2,1)S(1)}, bf16[128,512]{1,0:T(8,128)(2,1)}, u32[]{:S(2)}) copy-start(bf16[128,512]{1,0:T(8,128)(2,1)} %reduce-scatter.8.cloned.1.call-done) | copy-start | bytes 393220
  436.5 21.4 %copy-start.14 = (bf16[128,512]{1,0:T(8,128)(2,1)S(1)}, bf16[128,512]{1,0:T(8,128)(2,1)}, u32[]{:S(2)}) copy-start(bf16[128,512]{1,0:T(8,128)(2,1)} %reduce-scatter.18.cloned.1.call-done) | copy-start | bytes 393220
  436.5 21.4 %copy-start.23 = (f32[512]{0:T(512)S(1)}, f32[512]{0:T(512)}, u32[]{:S(2)}) copy-start(f32[512]{0:T(512)} %param.34) | copy-start | bytes 6148
  436.5 21.4 %copy-start.40 = (f32[128]{0:T(128)S(1)}, f32[128]{0:T(128)}, u32[]{:S(2)}) copy-start(f32[128]{0:T(128)} %copy-done.39) | copy-start | bytes 1540
  466.8 5.1 copy-start.5
  466.8 5.1 copy-start.42
  475.9 4.7 copy-start.27
  475.9 5.0 copy-start.25
  475.9 5.2 copy-start.30
  475.9 31.1 %all-to-all-start.8 = ((bf16[4,256,512]{2,1,0:T(8,128)(2,1)}), bf16[4,256,512]{2,1,0:T(8,128)(2,1)}, u32[]{:S(2)}, u32[]{:S(2)}) async-start(bf16[4,256,512]{2,1,0:T(8,128)(2,1)} %bitcast.109), calls=%async_computation.15 | async-start | bytes 2097152 | tf_op jit(solution)/shard_map/all_to_all | solution.py:168
Sparse Core Ops, SparseCore 0:
  71.8 20.8 reduce-scatter.7
  130.1 20.2 reduce-scatter.9
  187.8 20.2 reduce-scatter.11
  245.6 20.3 reduce-scatter.13
  310.3 20.3 reduce-scatter.15
  374.3 20.3 reduce-scatter.17
  437.5 20.2 reduce-scatter.19
where the time goes:
time: 534 us; the launch traced here: 523 us
  waiting for transfers between devices  210 us (39%)
  other arithmetic  99.4 us (19%)
  local copies, waits for them, and re-layouts  59.5 us (11%)
  blocking collectives  54.5 us (10%)
  starting transfers between devices  43.9 us (8%)
  matrix products  40.9 us (8%)
  between operations  15.4 us (3%)
    reduce_scatter x4, waiting for transfers between devices, combine(): lax.psum_scatter(partial_value.astype(jnp.bfloat16), ('feat', 'rep'), sca...  82.1 us
    reduce_scatter x3, waiting for transfers between devices, on_device(): lax.psum_scatter(partial_value.astype(jnp.bfloat16), ('feat', 'rep'), sca...  61.4 us
    all_gather x4, blocking collectives, combine(): whole = lax.all_gather(fresh, ('feat', 'rep'), axis=0, tiled=True)  27.4 us
    all_gather x4, blocking collectives, spread(): return lax.all_gather(grad_rows_local, ('feat', 'rep'), axis=0, tiled=True)  27.1 us
    dot_general x10, matrix products, product_back(): lax.dot_general(left, right, (((1,), (1,)), ((), ())), preferred_element_...  22.1 us
    all_to_all x1, waiting for transfers between devices, on_device(): lax.all_to_all(outgoing_rows.reshape(shard_count, bucket, features), 'mes...  21.1 us
    all_to_all x1, waiting for transfers between devices, on_device(): lax.all_to_all(slot_grad.reshape(shard_count, bucket, features).astype(jn...  18.9 us
    dot_general x12, matrix products, product(): return jnp.dot(left, right, preferred_element_type=jnp.float32)  18.8 us
  transfers between devices with their start and end apart: 16, of which 16 were waited for; matrix products, arithmetic and copies ran while one was open for 4% of the time, Pallas kernels for 0%

commit v1 on v0

v1 whole, which is shorter than its diff:
```python
import functools

import jax
import jax.numpy as jnp
from jax import lax
from jax.experimental import pallas as pl
from jax.experimental.pallas import tpu as pltpu
from jax.sharding import PartitionSpec as P

LAYERS = 3
LANES = 128
BLOCK = 512
EXTRA = 16
eps = 1e-05

f32 = jnp.float32
bf16 = jnp.bfloat16
i32 = jnp.int32


def norm_scale(totals):
    return lax.rsqrt(jnp.mean(totals * totals, axis=-1, keepdims=True) + eps)


def norm_back(totals, gain_row, upstream):
    scaled = norm_scale(totals)
    normed = totals * scaled
    slope = upstream * gain_row
    return scaled * (slope - normed * jnp.mean(slope * normed, axis=-1, keepdims=True))


def dot(left, right):
    return jnp.dot(left, right, preferred_element_type=f32)


def dot_back(left, right):
    return lax.dot_general(left, right, (((1,), (1,)), ((), ())), preferred_element_type=f32)


def gated(pre):
    sigma = 0.5 * jnp.tanh(0.5 * pre) + 0.5
    act = pre * sigma
    return act, sigma + act * (1.0 - sigma)


def as_mask(hit):
    return jnp.where(hit, 1.0, 0.0).astype(bf16)


def pick_columns(index, first, height):
    place = lax.broadcasted_iota(i32, (height, index.shape[1]), 0) + first
    return as_mask(place == index)


def upright(index):
    count = index.shape[1]
    if count < LANES:
        index = jnp.concatenate([index, jnp.full((1, LANES - count), -1, i32)], axis=1)
    return jnp.broadcast_to(index, (LANES, LANES)).T[:count]


def pick_rows(column, first, width):
    lane = lax.broadcasted_iota(i32, column.shape, 1) + first
    return jnp.concatenate([as_mask(column == lane + at) for at in range(0, width, LANES)], axis=1)


def call(body, outs, scratch=()):
    def run(*args):
        def where(array):
            return pl.BlockSpec(memory_space=pltpu.SMEM if array.dtype == i32 and array.ndim == 1 else pltpu.VMEM)

        held = [(shape, dtype) for shape, dtype in scratch]
        room = sum(jnp.dtype(dtype).itemsize * shape[0] * shape[1] for shape, dtype in held)
        room += sum(array.dtype.itemsize * array.size for array in args)
        room += sum(jnp.dtype(dtype).itemsize * shape[0] * shape[1] for shape, dtype in outs)
        return pl.pallas_call(
            body,
            out_shape=tuple(jax.ShapeDtypeStruct(shape, dtype) for shape, dtype in outs),
            in_specs=[where(array) for array in args],
            out_specs=tuple(pl.BlockSpec(memory_space=pltpu.VMEM) for _ in outs),
            scratch_shapes=[pltpu.VMEM(shape, dtype) for shape, dtype in held],
            compiler_params=pltpu.CompilerParams(vmem_limit_bytes=min(room + (8 << 20), 60 << 20)),
        )(*args)

    return run


def place_kernel(slots, receivers, order, here, there, halo_here, halo_there, list_here, list_there):
    nodes = here.shape[1] // 2
    wide = halo_here.shape[1]

    def body(at):
        block = pl.ds(pl.multiple_of(at * LANES, LANES), LANES)
        slot, receiver = slots[:, block], receivers[:, block]
        slot_column, receiver_column = upright(slot), upright(receiver)
        here[block, 0:nodes] = pick_rows(slot_column, 0, nodes)
        here[block, nodes:] = pick_rows(receiver_column, 0, nodes)
        halo_here[block, :] = pick_rows(slot_column, nodes, wide)
        there[0:nodes, block] = pick_columns(slot, 0, nodes)
        there[nodes:, block] = pick_columns(receiver, 0, nodes)
        halo_there[:, block] = pick_columns(slot, nodes, wide)

    pl.loop(0, slots.shape[1] // LANES)(body)
    count = order.shape[1]
    for at in range(0, count, LANES):
        end = min(at + LANES, count)
        list_here[at:end, :] = pick_rows(upright(order[:, at:end]), 0, nodes)
    list_there[...] = pick_columns(order[...], 0, nodes)


def encode_kernel(steps, first, last, halves, *refs):
    refs = list(refs)
    meta, base, w_grid = refs[:3]
    del refs[:3]
    if first:
        w_mesh = refs.pop(0)
        projected = dot(base[...], w_mesh[...]).astype(bf16)
    else:
        total_in = refs.pop(0)
        projected = base[...]
    payloads = refs[:steps]
    del refs[:steps]
    picks, slopes = refs[:steps], refs[steps : 2 * steps]
    del refs[: 2 * steps]
    total = None if first else total_in[...]
    nodes = projected.shape[0]
    for payload, pick, slope_out in zip(payloads, picks, slopes):
        grid = pick.shape[0]
        notes = payload[grid:, 0:grid].astype(f32)
        target = jnp.full((1, grid), -1.0, f32)
        for at in range(0, notes.shape[0] // 3 * 3, 3):
            named = notes[at : at + 1] == meta[1].astype(f32)
            target = jnp.where(named, notes[at + 1 : at + 2] + 256.0 * notes[at + 2 : at + 3], target)
        target = target.astype(i32)
        column = jnp.concatenate([upright(target[:, at : at + LANES]) for at in range(0, grid, LANES)], axis=0)
        picked = pick_rows(column, 0, nodes)
        pick[...] = picked
        pre = dot(payload[0:grid, :], w_grid[...]) + dot(picked, projected)
        act, slope = gated(pre)
        slope_out[...] = slope.astype(bf16)
        added = dot(pick_columns(target, 0, nodes), act.astype(bf16))
        total = added if total is None else total + added
    if first:
        refs.pop(0)[...] = projected
    if not last:
        refs[0][...] = total
        return
    keep, sends, whole = refs[0], refs[1:halves], refs[-1]
    whole[...] = total
    part = nodes // halves

    def half(shift):
        at = lax.rem(meta[0] + shift, halves)
        return whole[pl.ds(pl.multiple_of(at * part, part), part), :]

    keep[...] = half(0)
    for shift in range(1, halves):
        sends[shift - 1][...] = half(shift).astype(bf16)


def list_rows(list_here, projected, outs):
    listed = dot(list_here[...], projected).astype(bf16)
    at = 0
    for out in outs:
        out[...] = listed[at : at + out.shape[0]]
        at += out.shape[0]


def start_kernel(halves, shifts, *refs):
    meta = refs[0]
    parts = refs[1 : 1 + halves]
    mesh_init, w_enc_out, gain, w_send, list_here = refs[1 + halves : 6 + halves]
    hidden_out, enc_sum_out, sent = refs[6 + halves : 9 + halves]
    outs = refs[9 + halves : 9 + halves + shifts]
    whole = refs[-1]
    part = parts[0].shape[0]
    for shift in range(halves):
        at = lax.rem(meta[0] + shift, halves)
        whole[pl.ds(pl.multiple_of(at * part, part), part), :] = parts[shift][...]
    enc_sum = dot(whole[...], w_enc_out[...])
    enc_sum_out[...] = enc_sum
    hidden = (mesh_init[...].astype(f32) + enc_sum * norm_scale(enc_sum) * gain[...]).astype(bf16)
    hidden_out[...] = hidden
    projected = dot(hidden, w_send[0]).astype(bf16)
    sent[...] = projected
    list_rows(list_here, projected, outs)


def local_kernel(layer, hidden, sent, here, w_recv, pre, table):
    nodes = hidden.shape[0]
    table[0:nodes, :] = sent[...]
    table[nodes:, :] = dot(hidden[...], w_recv[layer]).astype(bf16)
    for at in range(0, pre.shape[0], BLOCK):
        pre[at : at + BLOCK, :] = dot(here[at : at + BLOCK, :], table[...])


def stack_halo(halos, halo):
    at = 0
    for block in halos:
        halo[at : at + block.shape[0], :] = block[...]
        at += block.shape[0]
    if at < halo.shape[0]:
        halo[at:, :] = jnp.zeros((halo.shape[0] - at, halo.shape[1]), bf16)


def node_sum(pre, halos, halo_here, there, slope_out, halo, act_out):
    nodes = there.shape[0] // 2
    stack_halo(halos, halo)
    for at in range(0, pre.shape[0], BLOCK):
        block = slice(at, at + BLOCK)
        act, slope = gated(pre[block, :] + dot(halo_here[block, :], halo[...]))
        slope_out[block, :] = slope.astype(bf16)
        act_out[block, :] = act.astype(bf16)
    return dot(there[nodes:, :], act_out[...])


def layer_kernel(layer, shifts, *refs):
    hidden, pre = refs[:2]
    halos = refs[2 : 2 + shifts]
    halo_here, there, w_out, gain, w_send, list_here = refs[2 + shifts : 8 + shifts]
    hidden_out, agg_out, slope_out, sent_out = refs[8 + shifts : 12 + shifts]
    outs = refs[12 + shifts : 12 + 2 * shifts]
    halo, act = refs[-2:]
    total = node_sum(pre, halos, halo_here, there, slope_out, halo, act)
    agg = dot(total.astype(bf16), w_out[layer])
    agg_out[...] = agg
    fresh = (hidden[...].astype(f32) + agg * norm_scale(agg) * gain[layer : layer + 1, :]).astype(bf16)
    hidden_out[...] = fresh
    projected = dot(fresh, w_send[layer + 1]).astype(bf16)
    sent_out[...] = projected
    list_rows(list_here, projected, outs)


def edge_grads(grad_agg, w_out, here, halo_there, slope, grad_pre, outs):
    nodes = grad_agg.shape[0]
    spread = dot_back(grad_agg.astype(bf16), w_out).astype(bf16)
    for at in range(0, slope.shape[0], BLOCK):
        block = slice(at, at + BLOCK)
        grad_act = dot(here[block, nodes:], spread)
        grad_pre[block, :] = (grad_act * slope[block, :].astype(f32)).astype(bf16)
    given = dot(halo_there[...], grad_pre[...]).astype(bf16)
    at = 0
    for out in outs:
        out[...] = given[at : at + out.shape[0]]
        at += out.shape[0]


def turn_kernel(layer, shifts, *refs):
    hidden, pre = refs[:2]
    halos = refs[2 : 2 + shifts]
    halo_here, there, w_out, gain, here, halo_there, cot = refs[2 + shifts : 9 + shifts]
    hidden_out, grad_pre = refs[9 + shifts : 11 + shifts]
    outs = refs[11 + shifts : 11 + 2 * shifts]
    slope, halo = refs[-2:]
    total = node_sum(pre, halos, halo_here, there, slope, halo, grad_pre)
    agg = dot(total.astype(bf16), w_out[layer])
    gain_row = gain[layer : layer + 1, :]
    hidden_out[...] = (hidden[...].astype(f32) + agg * norm_scale(agg) * gain_row).astype(bf16)
    edge_grads(norm_back(agg, gain_row, cot[...].astype(f32)), w_out[layer], here, halo_there, slope, grad_pre, outs)


def rest_kernel(layer, upstream, grad_pre, there, w_send, w_recv, rest):
    nodes = upstream.shape[0]
    sums = dot(there[...], grad_pre[...]).astype(bf16)
    rest[...] = (
        upstream[...].astype(f32)
        + dot_back(sums[0:nodes], w_send[layer])
        + dot_back(sums[nodes:], w_recv[layer])
    )


def arrived(rest, returned, list_there, w_send, halo):
    at = 0
    for block in returned:
        halo[at : at + block.shape[0], :] = block[...]
        at += block.shape[0]
    projected = dot_back(halo[...], w_send).astype(bf16)
    return rest[...] + dot(list_there[...], projected)


def back_kernel(layer, shifts, *refs):
    rest = refs[0]
    returned = refs[1 : 1 + shifts]
    list_there, w_send, agg, slope, gain, w_out, here, halo_there = refs[1 + shifts : 9 + shifts]
    upstream_out, grad_pre = refs[9 + shifts : 11 + shifts]
    outs = refs[11 + shifts : 11 + 2 * shifts]
    halo = refs[-1]
    upstream = arrived(rest, returned, list_there, w_send[layer + 1], halo)
    upstream_out[...] = upstream
    grad_agg = norm_back(agg[...], gain[layer : layer + 1, :], upstream)
    edge_grads(grad_agg, w_out[layer], here, halo_there, slope, grad_pre, outs)


def finish_kernel(count, shifts, *refs):
    rest = refs[0]
    returned = refs[1 : 1 + shifts]
    list_there, w_send, enc_sum, gain, w_enc_out = refs[1 + shifts : 6 + shifts]
    picks, slopes = refs[6 + shifts : 6 + shifts + count], refs[6 + shifts + count : 6 + shifts + 2 * count]
    outs = refs[6 + shifts + 2 * count : -1]
    halo = refs[-1]
    upstream = arrived(rest, returned, list_there, w_send[0], halo)
    spread = dot_back(norm_back(enc_sum[...], gain[...], upstream).astype(bf16), w_enc_out[...]).astype(bf16)
    for pick, slope, out in zip(picks, slopes, outs):
        out[...] = (dot(pick[...], spread) * slope[...].astype(f32)).astype(bf16)


def grid_kernel(count, *refs):
    blocks, w_grid, out = refs[:count], refs[count], refs[count + 1]
    total = blocks[0][...].astype(f32)
    for block in blocks[1:]:
        total = total + block[...].astype(f32)
    out[...] = dot_back(total.astype(bf16), w_grid[...])


def shifted(value, axis, by):
    size = lax.axis_size(axis)
    return lax.ppermute(value, axis, [(at, (at + by) % size) for at in range(size)])


def in_order(pieces, axis):
    return jnp.roll(jnp.stack(pieces)[::-1], lax.axis_index(axis) + 1, axis=0)


def on_device(
    grid_feats,
    g2m_shard,
    g2m_node,
    mesh_init,
    sender_slots,
    receivers,
    halo_index,
    w_enc_grid,
    w_enc_mesh,
    w_enc_out,
    enc_gain,
    w_send,
    w_recv,
    w_out,
    layer_gain,
    out_cot,
):
    shards = lax.axis_size("mesh")
    shard = lax.axis_index("mesh")
    halves = lax.axis_size("rep")
    feats = lax.axis_size("feat")
    nodes, width = mesh_init.shape
    grid, tops = g2m_shard.shape
    edges = sender_slots.shape[0]
    depth = halo_index.shape[2]
    shifts = shards - 1
    listed_rows = shifts * depth
    wide = -(-listed_rows // LANES) * LANES
    all_edges = edges * halves * feats
    enc_gain = enc_gain[None, :]

    notes = jnp.stack([g2m_shard, g2m_node % 256, g2m_node // 256], axis=2).reshape(grid, 3 * tops).T.astype(bf16)
    notes = jnp.pad(notes, ((0, EXTRA - 3 * tops), (0, width - grid)), constant_values=-1)
    payload = jnp.concatenate([grid_feats, notes], axis=0)
    order = sorted(range(shards), key=lambda step: min(step, shards - step))
    payloads = [payload] + [shifted(payload, "mesh", step) for step in order[1:]]

    place = sender_slots - nodes
    away = lax.rem(shard - place // depth + shards, shards)
    slots = jnp.where(sender_slots < nodes, sender_slots, nodes + (away - 1) * depth + place % depth)
    both = jnp.stack([slots, receivers])
    both = in_order([both] + [shifted(both, "rep", step) for step in range(1, halves)], "rep")
    both = in_order([both] + [shifted(both, "feat", step) for step in range(1, feats)], "feat")
    both = both.reshape(feats * halves, 2, edges)
    lists = jnp.roll(halo_index[0], -shard, axis=0)[1:].reshape(1, -1)
    here, there, halo_here, halo_there, list_here, list_there = call(
        place_kernel,
        [
            ((all_edges, 2 * nodes), bf16),
            ((2 * nodes, all_edges), bf16),
            ((all_edges, wide), bf16),
            ((wide, all_edges), bf16),
            ((listed_rows, nodes), bf16),
            ((nodes, listed_rows), bf16),
        ],
    )(both[:, 0].reshape(1, -1), both[:, 1].reshape(1, -1), lists)

    meta = jnp.stack([lax.axis_index("rep"), shard]).astype(i32)
    node_f32, node_bf16 = ((nodes, width), f32), ((nodes, width), bf16)
    row_shape, half = ((grid, width), bf16), nodes // halves
    enc_picks, enc_slopes = [], []
    base, total = mesh_init, None
    groups = [payloads[:2]] + [payloads[at : at + 1] for at in range(2, shards)]
    for at, group in enumerate(groups):
        first, last = at == 0, at == len(groups) - 1
        count = len(group)
        outs = [((grid, nodes), bf16)] * count + [row_shape] * count
        outs += [node_bf16] if first else []
        outs += [((half, width), f32)] + [((half, width), bf16)] * (halves - 1) if last else [node_f32]
        got = list(
            call(functools.partial(encode_kernel, count, first, last, halves), outs, [node_f32] if last else [])(
                meta, base, w_enc_grid, w_enc_mesh if first else total, *group
            )
        )
        enc_picks += got[:count]
        enc_slopes += got[count : 2 * count]
        del got[: 2 * count]
        if first:
            base = got.pop(0)
        total = got[0]
    part = got[0]
    for step in range(1, halves):
        part = part + shifted(got[step], "rep", step).astype(f32)
    part = part.astype(bf16)
    pieces = [part] + [shifted(part, "feat", step) for step in range(1, feats)]
    if feats > 2:
        pieces = list(in_order(pieces, "feat"))
    part = sum(piece.astype(f32) for piece in pieces).astype(bf16)
    parts = [part] + [shifted(part, "rep", -step) for step in range(1, halves)]

    listed = [((depth, width), bf16)] * shifts
    hidden, enc_sum, sent, *outgoing = call(
        functools.partial(start_kernel, halves, shifts), [node_bf16, node_f32, node_bf16] + listed, [node_bf16]
    )(meta, *parts, mesh_init, w_enc_out, enc_gain, w_send, list_here)

    edge_f32, edge_bf16 = ((all_edges, width), f32), ((all_edges, width), bf16)
    halo, back_halo = ((wide, width), bf16), ((listed_rows, width), bf16)

    def local(layer):
        (pre,) = call(functools.partial(local_kernel, layer), [edge_f32], [((2 * nodes, width), bf16)])(
            hidden, sent, here, w_recv
        )
        return pre

    records = []
    for layer in range(LAYERS - 1):
        halos = [shifted(block, "mesh", step + 1) for step, block in enumerate(outgoing)]
        hidden, agg, slope, sent, *outgoing = call(
            functools.partial(layer_kernel, layer, shifts),
            [node_bf16, node_f32, edge_bf16, node_bf16] + listed,
            [halo, edge_bf16],
        )(hidden, local(layer), *halos, halo_here, there, w_out, layer_gain, w_send, list_here)
        records.append((agg, slope))
    last = LAYERS - 1
    halos = [shifted(block, "mesh", step + 1) for step, block in enumerate(outgoing)]
    final_mesh, grad_pre, *outgoing = call(
        functools.partial(turn_kernel, last, shifts), [node_bf16, edge_bf16] + listed, [edge_bf16, halo]
    )(hidden, local(last), *halos, halo_here, there, w_out, layer_gain, here, halo_there, out_cot)
    upstream = out_cot
    for layer in reversed(range(LAYERS)):
        returned = [shifted(block, "mesh", -step - 1) for step, block in enumerate(outgoing)]
        (rest,) = call(functools.partial(rest_kernel, layer), [node_f32])(upstream, grad_pre, there, w_send, w_recv)
        if layer:
            agg, slope = records[layer - 1]
            upstream, grad_pre, *outgoing = call(
                functools.partial(back_kernel, layer - 1, shifts), [node_f32, edge_bf16] + listed, [back_halo]
            )(rest, *returned, list_there, w_send, agg, slope, layer_gain, w_out, here, halo_there)
    blocks = call(functools.partial(finish_kernel, shards, shifts), [row_shape] * shards, [back_halo])(
        rest, *returned, list_there, w_send, enc_sum, enc_gain, w_enc_out, *enc_picks, *enc_slopes
    )
    blocks = [blocks[0]] + [shifted(block, "mesh", -step) for step, block in zip(order[1:], blocks[1:])]
    (grid_grad,) = call(functools.partial(grid_kernel, shards), [((grid, width), f32)])(*blocks, w_enc_grid)
    return (final_mesh, grid_grad)


def solution(mesh):
    return jax.shard_map(
        on_device,
        mesh=mesh,
        in_specs=(
            P(("groups", "mesh", "feat", "rep"), None),
            P(("groups", "mesh", "feat", "rep"), None),
            P(("groups", "mesh", "feat", "rep"), None),
            P(("groups", "mesh"), None),
            P(("groups", "mesh", "feat", "rep")),
            P(("groups", "mesh", "feat", "rep")),
            P(("groups", "mesh"), None, None),
            P(),
            P(),
            P(),
            P(),
            P(),
            P(),
            P(),
            P(),
            P(("groups", "mesh"), None),
        ),
        out_specs=(P(("groups", "mesh"), None), P(("groups", "mesh", "feat", "rep"), None)),
        check_vma=False,
    )
```

time: 534 us -> 151 us (0.28); the launches traced: 523 us -> 150 us
  waiting for transfers between devices: 210 us -> 48.5 us
  other arithmetic: 99.4 us -> 4.6 us
  blocking collectives: 54.5 us -> 0 us
  local copies, waits for them, and re-layouts: 59.5 us -> 9.83 us
  Pallas kernels: 0 us -> 47.6 us
  matrix products: 40.9 us -> 0 us
  between operations: 15.4 us -> 1.27 us
  starting transfers between devices: 43.9 us -> 38.4 us
    reduce_scatter x7 -> x0, waiting for transfers between devices: 144 us -> none  [the longest x4 82.1 us: combine(): lax.psum_scatter(partial_value.astype(jnp.bfloat16), ('feat', 'rep'), sca...]
    all_to_all x9 -> x0, waiting for transfers between devices: 66 us -> none  [the longest x1 21.1 us: on_device(): lax.all_to_all(outgoing_rows.reshape(shard_count, bucket, features), 'mes...]
    scatter-add x13 -> x0, other arithmetic: 61 us -> none  [the longest x3 16 us: on_device(): jax.ops.segment_sum(grad_send, sender_slots, num_segments=node_rows + sha...]
    all_gather x8 -> x0, blocking collectives: 54.5 us -> none  [the longest x4 27.4 us: combine(): whole = lax.all_gather(fresh, ('feat', 'rep'), axis=0, tiled=True)]
    ppermute x0 -> x29, waiting for transfers between devices: none -> 48.5 us  [shifted(): lax.ppermute(value, axis, [(at, (at + by) % size) for at in range(size)])]
    pallas_call x0 -> x18, Pallas kernels: none -> 47.6 us  [run(): pl.pallas_call(body, out_shape=tuple((jax.ShapeDtypeStruct(shape, dtype)...]
    all_to_all x9 -> x0, starting transfers between devices: 43.1 us -> none  [the longest x3 13.8 us: on_device(): lax.all_to_all(outgoing, 'mesh', split_axis=0, concat_axis=0, tiled=True)]
    dot_general x22 -> x0, matrix products: 40.9 us -> none  [the longest x10 22.1 us: product_back(): lax.dot_general(left, right, (((1,), (1,)), ((), ())), preferred_element_...]
  transfers between devices with their start and end apart: 16 -> 29, of which waited for: 16 -> 13; matrix products, arithmetic and copies ran while one was open for 4% -> 1% of each run, Pallas kernels for 0% -> 17%
where the time goes in v1:
time: 151 us; the launch traced here: 150 us
  waiting for transfers between devices  48.5 us (32%)
  Pallas kernels  47.6 us (32%)
  starting transfers between devices  38.4 us (25%)
  local copies, waits for them, and re-layouts  9.83 us (7%)
  other arithmetic  4.6 us (3%)
    ppermute x29, waiting for transfers between devices, shifted(): lax.ppermute(value, axis, [(at, (at + by) % size) for at in range(size)])  48.5 us
    pallas_call x18, Pallas kernels, run(): pl.pallas_call(body, out_shape=tuple((jax.ShapeDtypeStruct(shape, dtype)...  47.6 us
    ppermute x29, starting transfers between devices, shifted(): lax.ppermute(value, axis, [(at, (at + by) % size) for at in range(size)])  38.4 us
    unnamed x67, local copies, waits for them, and re-layouts  9.53 us
  transfers between devices with their start and end apart: 29, of which 13 were waited for; matrix products, arithmetic and copies ran while one was open for 1% of the time, Pallas kernels for 17%

profile of v1, /device:TPU:0, one launch (start us, length us, event | category | flops | bytes accessed | tf_op | source)
XLA Modules:
  0.0 150.2 jit_solution(3113351103135700902)
XLA Ops:
  0.6 0.8 fusion.12
  1.5 1.0 fusion.1.refs_4_
  2.4 4.1 %collective-permute-start.2 = (bf16[272,512]{1,0:T(8,128)(2,1)S(1)}, bf16[272,512]{1,0:T(8,128)(2,1)S(1)}, u32[]{:S(2)}, u32[]{:S(2)}) collective-permute-start(bf16[272,512]{1,0:T(8,128)(2,1)S(1)} %fusion.1.refs_4_), channel_id=1, source_target_pairs={{0,8},{4,12},{8,0},{12,4},{1,9},{5,13},{9,1},{13,5},{2,10},{6,14},... | collective-permute-start | bytes 835592 | tf_op jit(solution)/shard_map/ppermute | solution.py:317
  6.5 1.3 collective-permute-start.1
  8.6 0.7 compare_select_fusion
  9.3 0.7 fusion.14
  10.0 16.3 %collective-permute-done.refs_5_ = bf16[272,512]{1,0:T(8,128)(2,1)S(1)} collective-permute-done((bf16[272,512]{1,0:T(8,128)(2,1)S(1)}, bf16[272,512]{1,0:T(8,128)(2,1)S(1)}, u32[]{:S(2)}, u32[]{:S(2)}) %collective-permute-start) | collective-permute-done | bytes 278560 | tf_op jit(solution)/shard_map/ppermute | solution.py:317
  26.3 1.0 copy-done.3
  27.4 1.0 copy-done.6
  28.4 1.0 copy-done.11
  29.5 2.2 %shard_map.167 = (bf16[256,512]{1,0:T(8,128)(2,1)S(1)}, bf16[256,512]{1,0:T(8,128)(2,1)S(1)}, bf16[256,512]{1,0:T(8,128)(2,1)S(1)}, bf16[256,512]{1,0:T(8,128)(2...) custom-call(s32[2]{0:T(128)S(1)} %pad_add_fusion.4.refs_0_, bf16[512,512]{1,0:T(8,128)(2,1)S(1)} %copy-done.6, ...), custom_call_target="tpu_custom_call" | custom-call | tf_op jit(solution)/shard_map/pallas_call | solution.py:76
  31.7 0.7 copy-done.12
  32.4 0.7 copy-done.14
  33.1 1.4 shard_map.168
  34.6 0.7 copy-done.20
  35.3 0.7 copy-done.22
  36.0 1.6 %shard_map.169 = (bf16[256,512]{1,0:T(8,128)(2,1)S(1)}, bf16[256,512]{1,0:T(8,128)(2,1)S(1)}, f32[256,512]{1,0:T(8,128)S(1)}, bf16[256,512]{1,0:T(8,128)(2,1)S(1)}) custom-call(s32[2]{0:T(128)S(1)} %pad_add_fusion.4.refs_0_, bf16[512,512]{1,0:T(8,128)(2,1)S(1)} %get-tuple-element.60.refs_1_, bf16[512,512]{1,0:T(8,128)(2,1)S(1)} %copy-done.4, ...), custom_call_target="tpu_custom_call" | custom-call | tf_op jit(solution)/shard_map/pallas_call | solution.py:76
  38.3 0.7 copy-done.26
  39.4 1.2 collective-permute-done.3
  40.6 1.5 %collective-permute-start.4 = (bf16[256,512]{1,0:T(8,128)(2,1)S(1)}, bf16[256,512]{1,0:T(8,128)(2,1)}, u32[]{:S(2)}, u32[]{:S(2)}) collective-permute-start(bf16[256,512]{1,0:T(8,128)(2,1)S(1)} %add_convert_fusion.1), channel_id=1, source_target_pairs={{0,2},{2,0},{1,3},{3,1},{4,6},{6,4},{5,7},{7,5},{8,10},{10,8},{9,1... | collective-permute-start | bytes 786440 | tf_op jit(solution)/shard_map/ppermute | solution.py:317
  42.8 6.4 %collective-permute-done.7 = s32[2,2,512]{2,0,1:T(2,128)S(1)} collective-permute-done((s32[2,2,512]{2,0,1:T(2,128)S(1)}, s32[2,2,512]{2,0,1:T(2,128)S(1)}, u32[]{:S(2)}, u32[]{:S(2)}) %collective-permute-start.7) | collective-permute-done | bytes 8224 | tf_op jit(solution)/shard_map/ppermute | solution.py:317
  49.3 1.2 add_convert_fusion.refs_1_
  50.7 3.5 %shard_map.170 = (bf16[2048,1024]{1,0:T(8,128)(2,1)S(1)}, bf16[1024,2048]{1,0:T(8,128)(2,1)S(1)}, bf16[2048,128]{1,0:T(8,128)(2,1)S(1)}, bf16[128,2048]{1,0:T(8,...) custom-call(s32[1,2048]{1,0:T(1,128)S(1)} %bitcast.31, s32[1,2048]{1,0:T(1,128)S(1)} %bitcast.30, ...), custom_call_target="tpu_custom_call" | custom-call | tf_op jit(solution)/shard_map/pallas_call | solution.py:76
  54.2 1.0 copy-done.7
  55.3 1.0 copy-done.8
  56.3 2.0 %shard_map.171 = (bf16[512,512]{1,0:T(8,128)(2,1)S(1)}, f32[512,512]{1,0:T(8,128)S(1)}, bf16[512,512]{1,0:T(8,128)(2,1)S(1)}, bf16[32,512]{1,0:T(8,128)(2,1)S(1)...) custom-call(s32[2]{0:T(128)S(1)} %pad_add_fusion.4.refs_0_, bf16[256,512]{1,0:T(8,128)(2,1)S(1)} %add_convert_fusion.refs_1_, ...), custom_call_target="tpu_custom_call" | custom-call | tf_op jit(solution)/shard_map/pallas_call | solution.py:76
  58.3 5.6 %collective-permute-start.8 = (bf16[32,512]{1,0:T(8,128)(2,1)S(1)}, bf16[32,512]{1,0:T(8,128)(2,1)S(1)}, u32[]{:S(2)}, u32[]{:S(2)}) collective-permute-start(bf16[32,512]{1,0:T(8,128)(2,1)S(1)} %get-tuple-element.69), channel_id=1, source_target_pairs={{0,4},{4,8},{8,12},{12,0},{1,5},{5,9},{9,13},{13,1},{2,6},{6,10},{... | collective-permute-start | bytes 98312 | tf_op jit(solution)/shard_map/ppermute | solution.py:317
  63.9 2.0 %collective-permute-start.9 = (bf16[32,512]{1,0:T(8,128)(2,1)S(1)}, bf16[32,512]{1,0:T(8,128)(2,1)S(1)}, u32[]{:S(2)}, u32[]{:S(2)}) collective-permute-start(bf16[32,512]{1,0:T(8,128)(2,1)S(1)} %get-tuple-element.70), channel_id=1, source_target_pairs={{0,8},{4,12},{8,0},{12,4},{1,9},{5,13},{9,1},{13,5},{2,10},{6,14},... | collective-permute-start | bytes 98312 | tf_op jit(solution)/shard_map/ppermute | solution.py:317
  65.8 2.8 %collective-permute-start.10 = (bf16[32,512]{1,0:T(8,128)(2,1)S(1)}, bf16[32,512]{1,0:T(8,128)(2,1)S(1)}, u32[]{:S(2)}, u32[]{:S(2)}) collective-permute-start(bf16[32,512]{1,0:T(8,128)(2,1)S(1)} %get-tuple-element.71), channel_id=1, source_target_pairs={{0,12},{4,0},{8,4},{12,8},{1,13},{5,1},{9,5},{13,9},{2,14},{6,2},{... | collective-permute-start | bytes 98312 | tf_op jit(solution)/shard_map/ppermute | solution.py:317
  68.7 2.6 %shard_map.172.refs_1_ = f32[2048,512]{1,0:T(8,128)S(1)} custom-call(bf16[512,512]{1,0:T(8,128)(2,1)S(1)} %get-tuple-element.66.hidden.refs_0_, bf16[512,512]{1,0:T(8,128)(2,1)S(1)} %get-tuple-element.67.sent, bf16[2048,1024]{1,0:T(8,128)(2,1)S(1)} %get-tuple-element.68.here.refs_9_.refs_10_, bf16[3,512,512]{2,1,0:T(8,128)(2,1)S(1)} %copy-done.1), custom_call_target="tpu_custom_call" | custom-call | tf_op jit(solution)/shard_map/pallas_call | solution.py:76
  71.4 3.3 %shard_map.173 = (bf16[512,512]{1,0:T(8,128)(2,1)S(1)}, f32[512,512]{1,0:T(8,128)S(1)}, bf16[2048,512]{1,0:T(8,128)(2,1)S(1)}, bf16[512,512]{1,0:T(8,128)(2,1)S(...) custom-call(bf16[512,512]{1,0:T(8,128)(2,1)S(1)} %get-tuple-element.66.hidden.refs_0_, ...), custom_call_target="tpu_custom_call" | custom-call | tf_op jit(solution)/shard_map/pallas_call | solution.py:76
  74.7 3.6 %collective-permute-start.12 = (bf16[32,512]{1,0:T(8,128)(2,1)S(1)}, bf16[32,512]{1,0:T(8,128)(2,1)S(1)}, u32[]{:S(2)}, u32[]{:S(2)}) collective-permute-start(bf16[32,512]{1,0:T(8,128)(2,1)S(1)} %get-tuple-element.77), channel_id=1, source_target_pairs={{0,8},{4,12},{8,0},{12,4},{1,9},{5,13},{9,1},{13,5},{2,10},{6,14},... | collective-permute-start | bytes 98312 | tf_op jit(solution)/shard_map/ppermute | solution.py:317
  78.6 2.6 %shard_map.174.refs_1_ = f32[2048,512]{1,0:T(8,128)S(1)} custom-call(bf16[512,512]{1,0:T(8,128)(2,1)S(1)} %get-tuple-element.74.hidden.refs_0_, bf16[512,512]{1,0:T(8,128)(2,1)S(1)} %get-tuple-element.75.sent, bf16[2048,1024]{1,0:T(8,128)(2,1)S(1)} %get-tuple-element.68.here.refs_9_.refs_10_, bf16[3,512,512]{2,1,0:T(8,128)(2,1)S(1)} %copy-done.1), custom_call_target="tpu_custom_call" | custom-call | tf_op jit(solution)/shard_map/pallas_call | solution.py:76
  81.2 1.1 collective-permute-done.13.refs_4_
  82.3 3.3 %shard_map.175 = (bf16[512,512]{1,0:T(8,128)(2,1)S(1)}, f32[512,512]{1,0:T(8,128)S(1)}, bf16[2048,512]{1,0:T(8,128)(2,1)S(1)}, bf16[512,512]{1,0:T(8,128)(2,1)S(...) custom-call(bf16[512,512]{1,0:T(8,128)(2,1)S(1)} %get-tuple-element.74.hidden.refs_0_, ...), custom_call_target="tpu_custom_call" | custom-call | tf_op jit(solution)/shard_map/pallas_call | solution.py:76
  85.6 0.8 collective-permute-start.14
  86.4 1.9 %collective-permute-start.15 = (bf16[32,512]{1,0:T(8,128)(2,1)S(1)}, bf16[32,512]{1,0:T(8,128)(2,1)S(1)}, u32[]{:S(2)}, u32[]{:S(2)}) collective-permute-start(bf16[32,512]{1,0:T(8,128)(2,1)S(1)} %get-tuple-element.82), channel_id=1, source_target_pairs={{0,8},{4,12},{8,0},{12,4},{1,9},{5,13},{9,1},{13,5},{2,10},{6,14},... | collective-permute-start | bytes 98312 | tf_op jit(solution)/shard_map/ppermute | solution.py:317
  88.3 1.2 collective-permute-start.16
  89.5 2.6 %shard_map.176.refs_1_ = f32[2048,512]{1,0:T(8,128)S(1)} custom-call(bf16[512,512]{1,0:T(8,128)(2,1)S(1)} %get-tuple-element.79.hidden.refs_0_, bf16[512,512]{1,0:T(8,128)(2,1)S(1)} %get-tuple-element.80.sent, bf16[2048,1024]{1,0:T(8,128)(2,1)S(1)} %get-tuple-element.68.here.refs_9_.refs_10_, bf16[3,512,512]{2,1,0:T(8,128)(2,1)S(1)} %copy-done.1), custom_call_target="tpu_custom_call" | custom-call | tf_op jit(solution)/shard_map/pallas_call | solution.py:76
  92.3 5.8 %shard_map.177 = (bf16[512,512]{1,0:T(8,128)(2,1)}, bf16[2048,512]{1,0:T(8,128)(2,1)S(1)}, bf16[32,512]{1,0:T(8,128)(2,1)S(1)}, bf16[32,512]{1,0:T(8,128)(2,1)S(1)}, bf16[32,512]{1,0:T(8,128)(2,1)S(1)}) custom-call(bf16[512,512]{1,0:T(8,128)(2,1)S(1)} %get-tuple-element.79.hidden.refs_0_, f32[2048,512]{1,0:T(8,128)S(1)} %shard_map.176.refs_1_, ...), custom_call_target="tpu_custom_call" | custom-call | tf_op jit(solution)/shard_map/pallas_call | solution.py:76
  98.1 3.0 %collective-permute-start.17 = (bf16[32,512]{1,0:T(8,128)(2,1)S(1)}, bf16[32,512]{1,0:T(8,128)(2,1)S(1)}, u32[]{:S(2)}, u32[]{:S(2)}) collective-permute-start(bf16[32,512]{1,0:T(8,128)(2,1)S(1)} %get-tuple-element.87), channel_id=1, source_target_pairs={{0,12},{4,0},{8,4},{12,8},{1,13},{5,1},{9,5},{13,9},{2,14},{6,2},{... | collective-permute-start | bytes 98312 | tf_op jit(solution)/shard_map/ppermute | solution.py:317
  101.2 0.8 collective-permute-start.19
  102.0 2.9 %shard_map.178.refs_0_ = f32[512,512]{1,0:T(8,128)S(1)} custom-call(bf16[512,512]{1,0:T(8,128)(2,1)S(1)} %copy-done.10, bf16[2048,512]{1,0:T(8,128)(2,1)S(1)} %get-tuple-element.86.grad_pre, bf16[1024,2048]{1,0:T(8,128)(2,1)S(1)} %get-tuple-element.73.refs_6_.there, bf16[3,512,512]{2,1,0:T(8,128)(2,1)S(1)} %copy-done, bf16[3,512,512]{2,1,0:T(8,128)(2,1)S(1)} %copy-done.1), custom_call_target="tpu_custom_call" | custom-call | tf_op jit(solution)/shard_map/pallas_call | solution.py:76
  104.8 1.0 collective-permute-done.18.refs_2_
  105.8 1.1 collective-permute-done.19.refs_3_
  106.9 2.6 %shard_map.179 = (f32[512,512]{1,0:T(8,128)S(1)}, bf16[2048,512]{1,0:T(8,128)(2,1)S(1)}, bf16[32,512]{1,0:T(8,128)(2,1)S(1)}, bf16[32,512]{1,0:T(8,128)(2,1)S(1)}, bf16[32,512]{1,0:T(8,128)(2,1)S(1)}) custom-call(f32[512,512]{1,0:T(8,128)S(1)} %shard_map.178.refs_0_, bf16[32,512]{1,0:T(8,128)(2,1)S(1)} %collective-permute-done.17.refs_1_, ...), custom_call_target="tpu_custom_call" | custom-call | tf_op jit(solution)/shard_map/pallas_call | solution.py:76
  109.5 1.1 collective-permute-start.20
  110.6 1.0 collective-permute-start.21
  111.6 1.0 collective-permute-start.22
  112.6 2.9 %shard_map.180.refs_0_ = f32[512,512]{1,0:T(8,128)S(1)} custom-call(f32[512,512]{1,0:T(8,128)S(1)} %get-tuple-element.93.upstream, bf16[2048,512]{1,0:T(8,128)(2,1)S(1)} %get-tuple-element.94.grad_pre, bf16[1024,2048]{1,0:T(8,128)(2,1)S(1)} %get-tuple-element.73.refs_6_.there, bf16[3,512,512]{2,1,0:T(8,128)(2,1)S(1)} %copy-done, ...), custom_call_target="tpu_custom_call" | custom-call | tf_op jit(solution)/shard_map/pallas_call | solution.py:76
  115.5 1.9 %collective-permute-done.22.refs_3_ = bf16[32,512]{1,0:T(8,128)(2,1)S(1)} collective-permute-done((bf16[32,512]{1,0:T(8,128)(2,1)S(1)}, bf16[32,512]{1,0:T(8,128)(2,1)S(1)}, u32[]{:S(2)}, u32[]{:S(2)}) %collective-permute-start.22) | collective-permute-done | bytes 32800 | tf_op jit(solution)/shard_map/ppermute | solution.py:317
  117.3 2.6 %shard_map.181 = (f32[512,512]{1,0:T(8,128)S(1)}, bf16[2048,512]{1,0:T(8,128)(2,1)S(1)}, bf16[32,512]{1,0:T(8,128)(2,1)S(1)}, bf16[32,512]{1,0:T(8,128)(2,1)S(1)}, bf16[32,512]{1,0:T(8,128)(2,1)S(1)}) custom-call(f32[512,512]{1,0:T(8,128)S(1)} %shard_map.180.refs_0_, bf16[32,512]{1,0:T(8,128)(2,1)S(1)} %collective-permute-done.20.refs_1_, ...), custom_call_target="tpu_custom_call" | custom-call | tf_op jit(solution)/shard_map/pallas_call | solution.py:76
  119.9 1.0 collective-permute-start.23
  121.1 1.0 collective-permute-start.25
  122.2 2.9 %shard_map.182.refs_0_ = f32[512,512]{1,0:T(8,128)S(1)} custom-call(f32[512,512]{1,0:T(8,128)S(1)} %get-tuple-element.100.upstream, bf16[2048,512]{1,0:T(8,128)(2,1)S(1)} %get-tuple-element.101.grad_pre, bf16[1024,2048]{1,0:T(8,128)(2,1)S(1)} %get-tuple-element.73.refs_6_.there, bf16[3,512,512]{2,1,0:T(8,128)(2,1)S(1)} %copy-done, ...), custom_call_target="tpu_custom_call" | custom-call | tf_op jit(solution)/shard_map/pallas_call | solution.py:76
  125.1 0.8 collective-permute-done.24.refs_2_
  125.9 1.4 collective-permute-done.25.refs_3_
  127.4 1.8 %shard_map.183 = (bf16[256,512]{1,0:T(8,128)(2,1)S(1)}, bf16[256,512]{1,0:T(8,128)(2,1)S(1)}, bf16[256,512]{1,0:T(8,128)(2,1)S(1)}, bf16[256,512]{1,0:T(8,128)(2,1)S(1)}) custom-call(f32[512,512]{1,0:T(8,128)S(1)} %shard_map.182.refs_0_, bf16[32,512]{1,0:T(8,128)(2,1)S(1)} %collective-permute-done.23.refs_1_, ...), custom_call_target="tpu_custom_call" | custom-call | tf_op jit(solution)/shard_map/pallas_call | solution.py:76
  129.2 1.3 collective-permute-start.26
  130.5 0.8 collective-permute-start.27
  131.9 4.4 %collective-permute-done.26.refs_1_ = bf16[256,512]{1,0:T(8,128)(2,1)S(1)} collective-permute-done((bf16[256,512]{1,0:T(8,128)(2,1)S(1)}, bf16[256,512]{1,0:T(8,128)(2,1)S(1)}, u32[]{:S(2)}, u32[]{:S(2)}) %collective-permute-start.26) | collective-permute-done | bytes 262176 | tf_op jit(solution)/shard_map/ppermute | solution.py:317
  136.3 4.3 %collective-permute-done.27.refs_2_ = bf16[256,512]{1,0:T(8,128)(2,1)S(1)} collective-permute-done((bf16[256,512]{1,0:T(8,128)(2,1)S(1)}, bf16[256,512]{1,0:T(8,128)(2,1)S(1)}, u32[]{:S(2)}, u32[]{:S(2)}) %collective-permute-start.27) | collective-permute-done | bytes 262176 | tf_op jit(solution)/shard_map/ppermute | solution.py:317
  140.5 8.6 %collective-permute-done.28.refs_3_ = bf16[256,512]{1,0:T(8,128)(2,1)S(1)} collective-permute-done((bf16[256,512]{1,0:T(8,128)(2,1)S(1)}, bf16[256,512]{1,0:T(8,128)(2,1)S(1)}, u32[]{:S(2)}, u32[]{:S(2)}) %collective-permute-start.28) | collective-permute-done | bytes 262176 | tf_op jit(solution)/shard_map/ppermute | solution.py:317
  149.1 1.2 shard_map.184
  (103 shorter events, 4.1 us)
Async XLA Ops:
  0.6 32.5 %copy-start.4 = (bf16[512,512]{1,0:T(8,128)(2,1)S(1)}, bf16[512,512]{1,0:T(8,128)(2,1)}, u32[]{:S(2)}) copy-start(bf16[512,512]{1,0:T(8,128)(2,1)} %refs_4_.3) | copy-start | bytes 1572868
  2.4 33.6 %collective-permute-start.2 = (bf16[272,512]{1,0:T(8,128)(2,1)S(1)}, bf16[272,512]{1,0:T(8,128)(2,1)S(1)}, u32[]{:S(2)}, u32[]{:S(2)}) collective-permute-start(bf16[272,512]{1,0:T(8,128)(2,1)S(1)} %fusion.1.refs_4_), channel_id=1, source_target_pairs={{0,8},{4,12},{8,0},{12,4},{1,9},{5,13},{9,1},{13,5},{2,10},{6,14},... | collective-permute-start | bytes 835592 | tf_op jit(solution)/shard_map/ppermute | solution.py:317
  6.5 26.6 %collective-permute-start.1 = (bf16[272,512]{1,0:T(8,128)(2,1)S(1)}, bf16[272,512]{1,0:T(8,128)(2,1)S(1)}, u32[]{:S(2)}, u32[]{:S(2)}) collective-permute-start(bf16[272,512]{1,0:T(8,128)(2,1)S(1)} %fusion.1.refs_4_), channel_id=1, source_target_pairs={{0,12},{4,0},{8,4},{12,8},{1,13},{5,1},{9,5},{13,9},{2,14},{6,2},{... | collective-permute-start | bytes 835592 | tf_op jit(solution)/shard_map/ppermute | solution.py:317
  7.9 18.5 %collective-permute-start = (bf16[272,512]{1,0:T(8,128)(2,1)S(1)}, bf16[272,512]{1,0:T(8,128)(2,1)S(1)}, u32[]{:S(2)}, u32[]{:S(2)}) collective-permute-start(bf16[272,512]{1,0:T(8,128)(2,1)S(1)} %fusion.1.refs_4_), channel_id=1, source_target_pairs={{0,4},{4,8},{8,12},{12,0},{1,5},{5,9},{9,13},{13,1},{2,6},{6,10},{... | collective-permute-start | bytes 835592 | tf_op jit(solution)/shard_map/ppermute | solution.py:317
  10.0 29.2 %collective-permute-start.6 = (s32[2,512]{1,0:T(2,128)S(1)}, s32[2,512]{1,0:T(2,128)S(1)}, u32[]{:S(2)}, u32[]{:S(2)}) collective-permute-start(s32[2,512]{1,0:T(2,128)S(1)} %get-tuple-element.121), channel_id=1, source_target_pairs={{0,1},{1,0},{2,3},{3,2},{4,5},{5,4},{6,7},{7,6},{8,9},{9,8},{10,11... | collective-permute-start | bytes 12296 | tf_op jit(solution)/shard_map/ppermute | solution.py:317
  26.3 1.0 copy-start.3
  27.4 1.0 copy-start.6
  28.4 1.0 copy-start.11
  31.7 0.7 copy-start.12
  32.4 0.7 copy-start.14
  33.1 2.9 %copy-start.18 = (bf16[256,512]{1,0:T(8,128)(2,1)}, bf16[256,512]{1,0:T(8,128)(2,1)S(1)}, u32[]{:S(2)}) copy-start(bf16[256,512]{1,0:T(8,128)(2,1)S(1)} %get-tuple-element.111.refs_14_) | copy-start | bytes 786436
  33.1 4.5 %copy-start.16 = (bf16[256,512]{1,0:T(8,128)(2,1)}, bf16[256,512]{1,0:T(8,128)(2,1)S(1)}, u32[]{:S(2)}) copy-start(bf16[256,512]{1,0:T(8,128)(2,1)S(1)} %get-tuple-element.110.refs_13_) | copy-start | bytes 786436
  33.1 5.9 %copy-start.31 = (s32[1,4,32]{2,1,0:T(4,128)S(1)}, s32[1,4,32]{2,1,0:T(4,128)}, u32[]{:S(2)}) copy-start(s32[1,4,32]{2,1,0:T(4,128)} %param.22) | copy-start | bytes 1540
  34.6 0.7 copy-start.20
  35.3 0.7 copy-start.22
  36.0 18.2 %copy-start = (bf16[3,512,512]{2,1,0:T(8,128)(2,1)S(1)}, bf16[3,512,512]{2,1,0:T(8,128)(2,1)}, u32[]{:S(2)}) copy-start(bf16[3,512,512]{2,1,0:T(8,128)(2,1)} %refs_5_.5) | copy-start | bytes 4718596
  36.0 18.2 %copy-start.29 = (f32[512]{0:T(512)S(1)}, f32[512]{0:T(512)}, u32[]{:S(2)}) copy-start(f32[512]{0:T(512)} %param.26) | copy-start | bytes 6148
  37.6 0.7 copy-start.24
  38.3 0.7 copy-start.26
  39.0 1.5 %collective-permute-start.3 = (bf16[256,512]{1,0:T(8,128)(2,1)S(1)}, bf16[256,512]{1,0:T(8,128)(2,1)S(1)}, u32[]{:S(2)}, u32[]{:S(2)}) collective-permute-start(bf16[256,512]{1,0:T(8,128)(2,1)S(1)} %get-tuple-element.64), channel_id=1, source_target_pairs={{0,1},{1,0},{2,3},{3,2},{4,5},{5,4},{6,7},{7,6},{8,9},{9,8},{10,11... | collective-permute-start | bytes 786440 | tf_op jit(solution)/shard_map/ppermute | solution.py:317
  40.6 8.6 %copy-start.30 = (bf16[256,512]{1,0:T(8,128)(2,1)}, bf16[256,512]{1,0:T(8,128)(2,1)S(1)}, u32[]{:S(2)}) copy-start(bf16[256,512]{1,0:T(8,128)(2,1)S(1)} %add_convert_fusion.1) | copy-start | bytes 786436
  40.6 8.6 %collective-permute-start.4 = (bf16[256,512]{1,0:T(8,128)(2,1)S(1)}, bf16[256,512]{1,0:T(8,128)(2,1)}, u32[]{:S(2)}, u32[]{:S(2)}) collective-permute-start(bf16[256,512]{1,0:T(8,128)(2,1)S(1)} %add_convert_fusion.1), channel_id=1, source_target_pairs={{0,2},{2,0},{1,3},{3,1},{4,6},{6,4},{5,7},{7,5},{8,10},{10,8},{9,1... | collective-permute-start | bytes 786440 | tf_op jit(solution)/shard_map/ppermute | solution.py:317
  42.2 7.0 %collective-permute-start.7 = (s32[2,2,512]{2,0,1:T(2,128)S(1)}, s32[2,2,512]{2,0,1:T(2,128)S(1)}, u32[]{:S(2)}, u32[]{:S(2)}) collective-permute-start(s32[2,2,512]{2,0,1:T(2,128)S(1)} %fusion.3), channel_id=1, source_target_pairs={{0,2},{2,0},{1,3},{3,1},{4,6},{6,4},{5,7},{7,5},{8,10},{10,8},{9,1... | collective-permute-start | bytes 24584 | tf_op jit(solution)/shard_map/ppermute | solution.py:317
  49.3 19.4 %copy-start.1 = (bf16[3,512,512]{2,1,0:T(8,128)(2,1)S(1)}, bf16[3,512,512]{2,1,0:T(8,128)(2,1)}, u32[]{:S(2)}) copy-start(bf16[3,512,512]{2,1,0:T(8,128)(2,1)} %w_recv.11) | copy-start | bytes 4718596
  50.5 3.7 %collective-permute-start.5 = (bf16[256,512]{1,0:T(8,128)(2,1)S(1)}, bf16[256,512]{1,0:T(8,128)(2,1)}, u32[]{:S(2)}, u32[]{:S(2)}) collective-permute-start(bf16[256,512]{1,0:T(8,128)(2,1)S(1)} %add_convert_fusion.refs_1_), channel_id=1, source_target_pairs={{0,1},{1,0},{2,3},{3,2},{4,5},{5,4},{6,7},{7,6},{8,9},{9,8},{10,11... | collective-permute-start | bytes 786440 | tf_op jit(solution)/shard_map/ppermute | solution.py:317
  54.2 1.0 copy-start.7
  55.3 1.0 copy-start.8
  58.3 13.0 %collective-permute-start.8 = (bf16[32,512]{1,0:T(8,128)(2,1)S(1)}, bf16[32,512]{1,0:T(8,128)(2,1)S(1)}, u32[]{:S(2)}, u32[]{:S(2)}) collective-permute-start(bf16[32,512]{1,0:T(8,128)(2,1)S(1)} %get-tuple-element.69), channel_id=1, source_target_pairs={{0,4},{4,8},{8,12},{12,0},{1,5},{5,9},{9,13},{13,1},{2,6},{6,10},{... | collective-permute-start | bytes 98312 | tf_op jit(solution)/shard_map/ppermute | solution.py:317
  63.9 7.5 %collective-permute-start.9 = (bf16[32,512]{1,0:T(8,128)(2,1)S(1)}, bf16[32,512]{1,0:T(8,128)(2,1)S(1)}, u32[]{:S(2)}, u32[]{:S(2)}) collective-permute-start(bf16[32,512]{1,0:T(8,128)(2,1)S(1)} %get-tuple-element.70), channel_id=1, source_target_pairs={{0,8},{4,12},{8,0},{12,4},{1,9},{5,13},{9,1},{13,5},{2,10},{6,14},... | collective-permute-start | bytes 98312 | tf_op jit(solution)/shard_map/ppermute | solution.py:317
  65.8 5.5 %collective-permute-start.10 = (bf16[32,512]{1,0:T(8,128)(2,1)S(1)}, bf16[32,512]{1,0:T(8,128)(2,1)S(1)}, u32[]{:S(2)}, u32[]{:S(2)}) collective-permute-start(bf16[32,512]{1,0:T(8,128)(2,1)S(1)} %get-tuple-element.71), channel_id=1, source_target_pairs={{0,12},{4,0},{8,4},{12,8},{1,13},{5,1},{9,5},{13,9},{2,14},{6,2},{... | collective-permute-start | bytes 98312 | tf_op jit(solution)/shard_map/ppermute | solution.py:317
  68.7 2.6 %copy-start.2 = (bf16[3,512,512]{2,1,0:T(8,128)(2,1)S(1)}, bf16[3,512,512]{2,1,0:T(8,128)(2,1)}, u32[]{:S(2)}) copy-start(bf16[3,512,512]{2,1,0:T(8,128)(2,1)} %refs_9_.7) | copy-start | bytes 4718596
  68.7 2.7 %copy-start.28 = (f32[3,512]{1,0:T(4,128)S(1)}, f32[3,512]{1,0:T(4,128)}, u32[]{:S(2)}) copy-start(f32[3,512]{1,0:T(4,128)} %refs_8_.10) | copy-start | bytes 18436
  74.7 6.5 %collective-permute-start.11 = (bf16[32,512]{1,0:T(8,128)(2,1)S(1)}, bf16[32,512]{1,0:T(8,128)(2,1)S(1)}, u32[]{:S(2)}, u32[]{:S(2)}) collective-permute-start(bf16[32,512]{1,0:T(8,128)(2,1)S(1)} %get-tuple-element.76), channel_id=1, source_target_pairs={{0,4},{4,8},{8,12},{12,0},{1,5},{5,9},{9,13},{13,1},{2,6},{6,10},{... | collective-permute-start | bytes 98312 | tf_op jit(solution)/shard_map/ppermute | solution.py:317
  74.7 6.4 %collective-permute-start.12 = (bf16[32,512]{1,0:T(8,128)(2,1)S(1)}, bf16[32,512]{1,0:T(8,128)(2,1)S(1)}, u32[]{:S(2)}, u32[]{:S(2)}) collective-permute-start(bf16[32,512]{1,0:T(8,128)(2,1)S(1)} %get-tuple-element.77), channel_id=1, source_target_pairs={{0,8},{4,12},{8,0},{12,4},{1,9},{5,13},{9,1},{13,5},{2,10},{6,14},... | collective-permute-start | bytes 98312 | tf_op jit(solution)/shard_map/ppermute | solution.py:317
  78.3 3.9 %collective-permute-start.13 = (bf16[32,512]{1,0:T(8,128)(2,1)S(1)}, bf16[32,512]{1,0:T(8,128)(2,1)S(1)}, u32[]{:S(2)}, u32[]{:S(2)}) collective-permute-start(bf16[32,512]{1,0:T(8,128)(2,1)S(1)} %get-tuple-element.78), channel_id=1, source_target_pairs={{0,12},{4,0},{8,4},{12,8},{1,13},{5,1},{9,5},{13,9},{2,14},{6,2},{... | collective-permute-start | bytes 98312 | tf_op jit(solution)/shard_map/ppermute | solution.py:317
  85.6 6.6 %collective-permute-start.14 = (bf16[32,512]{1,0:T(8,128)(2,1)S(1)}, bf16[32,512]{1,0:T(8,128)(2,1)S(1)}, u32[]{:S(2)}, u32[]{:S(2)}) collective-permute-start(bf16[32,512]{1,0:T(8,128)(2,1)S(1)} %get-tuple-element.81), channel_id=1, source_target_pairs={{0,4},{4,8},{8,12},{12,0},{1,5},{5,9},{9,13},{13,1},{2,6},{6,10},{... | collective-permute-start | bytes 98312 | tf_op jit(solution)/shard_map/ppermute | solution.py:317
  86.4 5.7 %collective-permute-start.15 = (bf16[32,512]{1,0:T(8,128)(2,1)S(1)}, bf16[32,512]{1,0:T(8,128)(2,1)S(1)}, u32[]{:S(2)}, u32[]{:S(2)}) collective-permute-start(bf16[32,512]{1,0:T(8,128)(2,1)S(1)} %get-tuple-element.82), channel_id=1, source_target_pairs={{0,8},{4,12},{8,0},{12,4},{1,9},{5,13},{9,1},{13,5},{2,10},{6,14},... | collective-permute-start | bytes 98312 | tf_op jit(solution)/shard_map/ppermute | solution.py:317
  88.3 3.9 %collective-permute-start.16 = (bf16[32,512]{1,0:T(8,128)(2,1)S(1)}, bf16[32,512]{1,0:T(8,128)(2,1)S(1)}, u32[]{:S(2)}, u32[]{:S(2)}) collective-permute-start(bf16[32,512]{1,0:T(8,128)(2,1)S(1)} %get-tuple-element.83), channel_id=1, source_target_pairs={{0,12},{4,0},{8,4},{12,8},{1,13},{5,1},{9,5},{13,9},{2,14},{6,2},{... | collective-permute-start | bytes 98312 | tf_op jit(solution)/shard_map/ppermute | solution.py:317
  89.5 2.8 %copy-start.10 = (bf16[512,512]{1,0:T(8,128)(2,1)S(1)}, bf16[512,512]{1,0:T(8,128)(2,1)}, u32[]{:S(2)}) copy-start(bf16[512,512]{1,0:T(8,128)(2,1)} %upstream.1) | copy-start | bytes 1572868
  98.1 6.8 %collective-permute-start.17 = (bf16[32,512]{1,0:T(8,128)(2,1)S(1)}, bf16[32,512]{1,0:T(8,128)(2,1)S(1)}, u32[]{:S(2)}, u32[]{:S(2)}) collective-permute-start(bf16[32,512]{1,0:T(8,128)(2,1)S(1)} %get-tuple-element.87), channel_id=1, source_target_pairs={{0,12},{4,0},{8,4},{12,8},{1,13},{5,1},{9,5},{13,9},{2,14},{6,2},{... | collective-permute-start | bytes 98312 | tf_op jit(solution)/shard_map/ppermute | solution.py:317
  101.0 4.8 %collective-permute-start.18 = (bf16[32,512]{1,0:T(8,128)(2,1)S(1)}, bf16[32,512]{1,0:T(8,128)(2,1)S(1)}, u32[]{:S(2)}, u32[]{:S(2)}) collective-permute-start(bf16[32,512]{1,0:T(8,128)(2,1)S(1)} %get-tuple-element.88), channel_id=1, source_target_pairs={{0,8},{4,12},{8,0},{12,4},{1,9},{5,13},{9,1},{13,5},{2,10},{6,14},... | collective-permute-start | bytes 98312 | tf_op jit(solution)/shard_map/ppermute | solution.py:317
  101.2 5.7 %collective-permute-start.19 = (bf16[32,512]{1,0:T(8,128)(2,1)S(1)}, bf16[32,512]{1,0:T(8,128)(2,1)S(1)}, u32[]{:S(2)}, u32[]{:S(2)}) collective-permute-start(bf16[32,512]{1,0:T(8,128)(2,1)S(1)} %get-tuple-element.89), channel_id=1, source_target_pairs={{0,4},{4,8},{8,12},{12,0},{1,5},{5,9},{9,13},{13,1},{2,6},{6,10},{... | collective-permute-start | bytes 98312 | tf_op jit(solution)/shard_map/ppermute | solution.py:317
  109.5 5.9 %collective-permute-start.20 = (bf16[32,512]{1,0:T(8,128)(2,1)S(1)}, bf16[32,512]{1,0:T(8,128)(2,1)S(1)}, u32[]{:S(2)}, u32[]{:S(2)}) collective-permute-start(bf16[32,512]{1,0:T(8,128)(2,1)S(1)} %get-tuple-element.95), channel_id=1, source_target_pairs={{0,12},{4,0},{8,4},{12,8},{1,13},{5,1},{9,5},{13,9},{2,14},{6,2},{... | collective-permute-start | bytes 98312 | tf_op jit(solution)/shard_map/ppermute | solution.py:317
  110.6 4.9 %collective-permute-start.21 = (bf16[32,512]{1,0:T(8,128)(2,1)S(1)}, bf16[32,512]{1,0:T(8,128)(2,1)S(1)}, u32[]{:S(2)}, u32[]{:S(2)}) collective-permute-start(bf16[32,512]{1,0:T(8,128)(2,1)S(1)} %get-tuple-element.96), channel_id=1, source_target_pairs={{0,8},{4,12},{8,0},{12,4},{1,9},{5,13},{9,1},{13,5},{2,10},{6,14},... | collective-permute-start | bytes 98312 | tf_op jit(solution)/shard_map/ppermute | solution.py:317
  111.6 5.8 %collective-permute-start.22 = (bf16[32,512]{1,0:T(8,128)(2,1)S(1)}, bf16[32,512]{1,0:T(8,128)(2,1)S(1)}, u32[]{:S(2)}, u32[]{:S(2)}) collective-permute-start(bf16[32,512]{1,0:T(8,128)(2,1)S(1)} %get-tuple-element.97), channel_id=1, source_target_pairs={{0,4},{4,8},{8,12},{12,0},{1,5},{5,9},{9,13},{13,1},{2,6},{6,10},{... | collective-permute-start | bytes 98312 | tf_op jit(solution)/shard_map/ppermute | solution.py:317
  119.9 5.1 %collective-permute-start.23 = (bf16[32,512]{1,0:T(8,128)(2,1)S(1)}, bf16[32,512]{1,0:T(8,128)(2,1)S(1)}, u32[]{:S(2)}, u32[]{:S(2)}) collective-permute-start(bf16[32,512]{1,0:T(8,128)(2,1)S(1)} %get-tuple-element.102), channel_id=1, source_target_pairs={{0,12},{4,0},{8,4},{12,8},{1,13},{5,1},{9,5},{13,9},{2,14},{6,2},{... | collective-permute-start | bytes 98312 | tf_op jit(solution)/shard_map/ppermute | solution.py:317
  120.9 4.9 %collective-permute-start.24 = (bf16[32,512]{1,0:T(8,128)(2,1)S(1)}, bf16[32,512]{1,0:T(8,128)(2,1)S(1)}, u32[]{:S(2)}, u32[]{:S(2)}) collective-permute-start(bf16[32,512]{1,0:T(8,128)(2,1)S(1)} %get-tuple-element.103), channel_id=1, source_target_pairs={{0,8},{4,12},{8,0},{12,4},{1,9},{5,13},{9,1},{13,5},{2,10},{6,14},... | collective-permute-start | bytes 98312 | tf_op jit(solution)/shard_map/ppermute | solution.py:317
  121.1 6.2 %collective-permute-start.25 = (bf16[32,512]{1,0:T(8,128)(2,1)S(1)}, bf16[32,512]{1,0:T(8,128)(2,1)S(1)}, u32[]{:S(2)}, u32[]{:S(2)}) collective-permute-start(bf16[32,512]{1,0:T(8,128)(2,1)S(1)} %get-tuple-element.104), channel_id=1, source_target_pairs={{0,4},{4,8},{8,12},{12,0},{1,5},{5,9},{9,13},{13,1},{2,6},{6,10},{... | collective-permute-start | bytes 98312 | tf_op jit(solution)/shard_map/ppermute | solution.py:317
  122.1 5.2 %copy-start.9 = (bf16[512,512]{1,0:T(8,128)(2,1)S(1)}, bf16[512,512]{1,0:T(8,128)(2,1)}, u32[]{:S(2)}) copy-start(bf16[512,512]{1,0:T(8,128)(2,1)} %refs_8_.11) | copy-start | bytes 1572868
  122.1 5.2 %copy-start.13 = (bf16[256,512]{1,0:T(8,128)(2,1)S(1)}, bf16[256,512]{1,0:T(8,128)(2,1)}, u32[]{:S(2)}) copy-start(bf16[256,512]{1,0:T(8,128)(2,1)} %copy-done.12) | copy-start | bytes 786436
  122.1 5.2 %copy-start.15 = (bf16[256,512]{1,0:T(8,128)(2,1)S(1)}, bf16[256,512]{1,0:T(8,128)(2,1)}, u32[]{:S(2)}) copy-start(bf16[256,512]{1,0:T(8,128)(2,1)} %copy-done.14) | copy-start | bytes 786436
  122.1 5.2 %copy-start.17 = (bf16[256,512]{1,0:T(8,128)(2,1)S(1)}, bf16[256,512]{1,0:T(8,128)(2,1)}, u32[]{:S(2)}) copy-start(bf16[256,512]{1,0:T(8,128)(2,1)} %copy-done.16) | copy-start | bytes 786436
  122.1 5.2 %copy-start.19 = (bf16[256,512]{1,0:T(8,128)(2,1)S(1)}, bf16[256,512]{1,0:T(8,128)(2,1)}, u32[]{:S(2)}) copy-start(bf16[256,512]{1,0:T(8,128)(2,1)} %copy-done.18) | copy-start | bytes 786436
  122.2 5.2 %copy-start.21 = (bf16[256,512]{1,0:T(8,128)(2,1)S(1)}, bf16[256,512]{1,0:T(8,128)(2,1)}, u32[]{:S(2)}) copy-start(bf16[256,512]{1,0:T(8,128)(2,1)} %copy-done.20) | copy-start | bytes 786436
  122.2 5.2 %copy-start.23 = (bf16[256,512]{1,0:T(8,128)(2,1)S(1)}, bf16[256,512]{1,0:T(8,128)(2,1)}, u32[]{:S(2)}) copy-start(bf16[256,512]{1,0:T(8,128)(2,1)} %copy-done.22) | copy-start | bytes 786436
  122.2 5.2 %copy-start.25 = (bf16[256,512]{1,0:T(8,128)(2,1)S(1)}, bf16[256,512]{1,0:T(8,128)(2,1)}, u32[]{:S(2)}) copy-start(bf16[256,512]{1,0:T(8,128)(2,1)} %copy-done.24) | copy-start | bytes 786436
  122.2 5.2 %copy-start.27 = (bf16[256,512]{1,0:T(8,128)(2,1)S(1)}, bf16[256,512]{1,0:T(8,128)(2,1)}, u32[]{:S(2)}) copy-start(bf16[256,512]{1,0:T(8,128)(2,1)} %copy-done.26) | copy-start | bytes 786436
  127.4 21.7 %copy-start.5 = (bf16[512,512]{1,0:T(8,128)(2,1)S(1)}, bf16[512,512]{1,0:T(8,128)(2,1)}, u32[]{:S(2)}) copy-start(bf16[512,512]{1,0:T(8,128)(2,1)} %refs_4_.3) | copy-start | bytes 1572868
  129.2 7.1 %collective-permute-start.26 = (bf16[256,512]{1,0:T(8,128)(2,1)S(1)}, bf16[256,512]{1,0:T(8,128)(2,1)S(1)}, u32[]{:S(2)}, u32[]{:S(2)}) collective-permute-start(bf16[256,512]{1,0:T(8,128)(2,1)S(1)} %get-tuple-element.115), channel_id=1, source_target_pairs={{0,12},{4,0},{8,4},{12,8},{1,13},{5,1},{9,5},{13,9},{2,14},{6,2},{... | collective-permute-start | bytes 786440 | tf_op jit(solution)/shard_map/ppermute | solution.py:317
  130.5 10.1 %collective-permute-start.27 = (bf16[256,512]{1,0:T(8,128)(2,1)S(1)}, bf16[256,512]{1,0:T(8,128)(2,1)S(1)}, u32[]{:S(2)}, u32[]{:S(2)}) collective-permute-start(bf16[256,512]{1,0:T(8,128)(2,1)S(1)} %get-tuple-element.116), channel_id=1, source_target_pairs={{0,4},{4,8},{8,12},{12,0},{1,5},{5,9},{9,13},{13,1},{2,6},{6,10},{... | collective-permute-start | bytes 786440 | tf_op jit(solution)/shard_map/ppermute | solution.py:317
  131.2 17.8 %collective-permute-start.28 = (bf16[256,512]{1,0:T(8,128)(2,1)S(1)}, bf16[256,512]{1,0:T(8,128)(2,1)S(1)}, u32[]{:S(2)}, u32[]{:S(2)}) collective-permute-start(bf16[256,512]{1,0:T(8,128)(2,1)S(1)} %get-tuple-element.117), channel_id=1, source_target_pairs={{0,8},{4,12},{8,0},{12,4},{1,9},{5,13},{9,1},{13,5},{2,10},{6,14},... | collective-permute-start | bytes 786440 | tf_op jit(solution)/shard_map/ppermute | solution.py:317

commit v2 on v1

--- a/solution.py
+++ b/solution.py
@@ -70,16 +70,17 @@
             return pl.BlockSpec(memory_space=pltpu.SMEM if array.dtype == i32 and array.ndim == 1 else pltpu.VMEM)
 
         held = [(shape, dtype) for shape, dtype in scratch]
-        room = sum(jnp.dtype(dtype).itemsize * shape[0] * shape[1] for shape, dtype in held)
-        room += sum(array.dtype.itemsize * array.size for array in args)
+        own = sum(jnp.dtype(dtype).itemsize * shape[0] * shape[1] for shape, dtype in held) + (10 << 20)
+        room = own + sum(array.dtype.itemsize * array.size for array in args)
         room += sum(jnp.dtype(dtype).itemsize * shape[0] * shape[1] for shape, dtype in outs)
+        limit = own if room < 40 << 20 else min(room, 60 << 20)
         return pl.pallas_call(
             body,
             out_shape=tuple(jax.ShapeDtypeStruct(shape, dtype) for shape, dtype in outs),
             in_specs=[where(array) for array in args],
             out_specs=tuple(pl.BlockSpec(memory_space=pltpu.VMEM) for _ in outs),
             scratch_shapes=[pltpu.VMEM(shape, dtype) for shape, dtype in held],
-            compiler_params=pltpu.CompilerParams(vmem_limit_bytes=min(room + (8 << 20), 60 << 20)),
+            compiler_params=pltpu.CompilerParams(vmem_limit_bytes=limit),
         )(*args)
 
     return run
@@ -108,12 +109,26 @@
     list_there[...] = pick_columns(order[...], 0, nodes)
 
 
+def note_kernel(rows, shards, nodes, payload):
+    grid = rows.shape[0]
+    payload[0:grid, :] = rows[...]
+    row = lax.broadcasted_iota(i32, (EXTRA, grid), 0)
+    notes = jnp.full((EXTRA, grid), -1, i32)
+    for top in range(shards.shape[0]):
+        node = nodes[top : top + 1, :]
+        for at, value in enumerate((shards[top : top + 1, :], node & 255, node >> 8)):
+            notes = jnp.where(row == 3 * top + at, value, notes)
+    payload[grid:, 0:grid] = notes.astype(f32).astype(bf16)
+    if grid < payload.shape[1]:
+        payload[grid:, grid:] = jnp.zeros((EXTRA, payload.shape[1] - grid), bf16)
+
+
 def encode_kernel(steps, first, last, halves, *refs):
     refs = list(refs)
     meta, base, w_grid = refs[:3]
     del refs[:3]
     if first:
-        w_mesh = refs.pop(0)
+        w_mesh, _ = refs.pop(0), refs.pop(0)
         projected = dot(base[...], w_mesh[...]).astype(bf16)
     else:
         total_in = refs.pop(0)
@@ -317,6 +332,10 @@
     return lax.ppermute(value, axis, [(at, (at + by) % size) for at in range(size)])
 
 
+def swapped(value, by):
+    return lax.ppermute(value, "mesh", [(at, at ^ by) for at in range(lax.axis_size("mesh"))])
+
+
 def in_order(pieces, axis):
     return jnp.roll(jnp.stack(pieces)[::-1], lax.axis_index(axis) + 1, axis=0)
 
@@ -353,11 +372,12 @@
     all_edges = edges * halves * feats
     enc_gain = enc_gain[None, :]
 
-    notes = jnp.stack([g2m_shard, g2m_node % 256, g2m_node // 256], axis=2).reshape(grid, 3 * tops).T.astype(bf16)
-    notes = jnp.pad(notes, ((0, EXTRA - 3 * tops), (0, width - grid)), constant_values=-1)
-    payload = jnp.concatenate([grid_feats, notes], axis=0)
-    order = sorted(range(shards), key=lambda step: min(step, shards - step))
-    payloads = [payload] + [shifted(payload, "mesh", step) for step in order[1:]]
+    (payload,) = call(note_kernel, [((grid + EXTRA, width), bf16)])(grid_feats, g2m_shard.T, g2m_node.T)
+    if shards == 4:
+        across = swapped(payload, 2)
+        payloads = [payload, swapped(payload, 1), across, swapped(across, 1)]
+    else:
+        payloads = [payload] + [shifted(payload, "mesh", step) for step in range(1, shards)]
 
     place = sender_slots - nodes
     away = lax.rem(shard - place // depth + shards, shards)
@@ -393,7 +413,7 @@
         outs += [((half, width), f32)] + [((half, width), bf16)] * (halves - 1) if last else [node_f32]
         got = list(
             call(functools.partial(encode_kernel, count, first, last, halves), outs, [node_f32] if last else [])(
-                meta, base, w_enc_grid, w_enc_mesh if first else total, *group
+                meta, base, w_enc_grid, *((w_enc_mesh, list_here) if first else (total,)), *group
             )
         )
         enc_picks += got[:count]
@@ -452,8 +472,13 @@
     blocks = call(functools.partial(finish_kernel, shards, shifts), [row_shape] * shards, [back_halo])(
         rest, *returned, list_there, w_send, enc_sum, enc_gain, w_enc_out, *enc_picks, *enc_slopes
     )
-    blocks = [blocks[0]] + [shifted(block, "mesh", -step) for step, block in zip(order[1:], blocks[1:])]
-    (grid_grad,) = call(functools.partial(grid_kernel, shards), [((grid, width), f32)])(*blocks, w_enc_grid)
+    if shards == 4:
+        passed = swapped(blocks[3], 1)
+        near = swapped(blocks[1], 1)
+        blocks = [blocks[0], near, swapped((blocks[2].astype(f32) + passed.astype(f32)).astype(bf16), 2)]
+    else:
+        blocks = [blocks[0]] + [shifted(block, "mesh", -step) for step, block in enumerate(blocks) if step]
+    (grid_grad,) = call(functools.partial(grid_kernel, len(blocks)), [((grid, width), f32)])(*blocks, w_enc_grid)
     return (final_mesh, grid_grad)
 
 

time: 151 us -> 132 us (0.87)
  waiting for transfers between devices: 48.5 us -> 40.6 us
  local copies, waits for them, and re-layouts: 9.83 us -> 5.83 us
  starting transfers between devices: 38.4 us -> 34.9 us
  other arithmetic: 4.6 us -> 2.53 us
    ppermute x29 -> x23, waiting for transfers between devices: 48.5 us -> 19.7 us  [shifted(): lax.ppermute(value, axis, [(at, (at + by) % size) for at in range(size)])]
    ppermute x0 -> x6, waiting for transfers between devices: none -> 20.8 us  [swapped(): lax.ppermute(value, 'mesh', [(at, at ^ by) for at in range(lax.axis_size(...]
    ppermute x29 -> x23, starting transfers between devices: 38.4 us -> 26.5 us  [shifted(): lax.ppermute(value, axis, [(at, (at + by) % size) for at in range(size)])]
    ppermute x0 -> x6, starting transfers between devices: none -> 8.46 us  [swapped(): lax.ppermute(value, 'mesh', [(at, at ^ by) for at in range(lax.axis_size(...]
    unnamed x67 -> x33, local copies, waits for them, and re-layouts: 9.53 us -> 5.55 us
    pallas_call x18 -> x19, Pallas kernels: 47.6 us -> 46.9 us  [run(): pl.pallas_call(body, out_shape=tuple((jax.ShapeDtypeStruct(shape, dtype)...]
  transfers between devices with their start and end apart: 29 -> 29, of which waited for: 13 -> 17; matrix products, arithmetic and copies ran while one was open for 1% -> 2% of each run, Pallas kernels for 17% -> 18%
where the time goes in v2:
time: 132 us
  Pallas kernels  46.9 us (36%)
  waiting for transfers between devices  40.6 us (31%)
  starting transfers between devices  34.9 us (26%)
  local copies, waits for them, and re-layouts  5.83 us (4%)
  other arithmetic  2.53 us (2%)
    pallas_call x19, Pallas kernels, run(): pl.pallas_call(body, out_shape=tuple((jax.ShapeDtypeStruct(shape, dtype)...  46.9 us
    ppermute x23, starting transfers between devices, shifted(): lax.ppermute(value, axis, [(at, (at + by) % size) for at in range(size)])  26.5 us
    ppermute x6, waiting for transfers between devices, swapped(): lax.ppermute(value, 'mesh', [(at, at ^ by) for at in range(lax.axis_size(...  20.8 us
    ppermute x23, waiting for transfers between devices, shifted(): lax.ppermute(value, axis, [(at, (at + by) % size) for at in range(size)])  19.7 us
    ppermute x6, starting transfers between devices, swapped(): lax.ppermute(value, 'mesh', [(at, at ^ by) for at in range(lax.axis_size(...  8.46 us
    unnamed x33, local copies, waits for them, and re-layouts  5.55 us
  transfers between devices with their start and end apart: 29, of which 17 were waited for; matrix products, arithmetic and copies ran while one was open for 2% of the time, Pallas kernels for 18%

profile of v2, /device:TPU:0, one launch (start us, length us, event | category | flops | bytes accessed | tf_op | source)
XLA Modules:
  0.0 131.9 jit_solution(11808465855563566243)
XLA Ops:
  0.7 1.0 copy-done.10
  1.7 0.7 copy-done.13
  2.3 0.7 copy-done.14
  3.0 4.1 %collective-permute-start.3 = (bf16[272,512]{1,0:T(8,128)(2,1)S(1)}, bf16[272,512]{1,0:T(8,128)(2,1)S(1)}, u32[]{:S(2)}, u32[]{:S(2)}) collective-permute-start(bf16[272,512]{1,0:T(8,128)(2,1)S(1)} %shard_map.168.refs_5_), channel_id=1, source_target_pairs={{0,8},{4,12},{8,0},{12,4},{1,9},{5,13},{9,1},{13,5},{2,10},{6,14},... | collective-permute-start | bytes 835592 | tf_op jit(solution)/shard_map/ppermute | solution.py:336
  7.1 1.6 %collective-permute-start.2 = (bf16[272,512]{1,0:T(8,128)(2,1)S(1)}, bf16[272,512]{1,0:T(8,128)(2,1)S(1)}, u32[]{:S(2)}, u32[]{:S(2)}) collective-permute-start(bf16[272,512]{1,0:T(8,128)(2,1)S(1)} %shard_map.168.refs_5_), channel_id=1, source_target_pairs={{0,4},{4,0},{8,12},{12,8},{1,5},{5,1},{9,13},{13,9},{2,6},{6,2},{1... | collective-permute-start | bytes 835592 | tf_op jit(solution)/shard_map/ppermute | solution.py:336
  8.7 0.7 compare_select_fusion
  9.4 0.7 fusion.8
  10.1 0.8 pad_add_fusion.3
  11.1 0.2 collective-permute-done
  11.5 1.6 %collective-permute-start.1 = (s32[2,2,512]{2,0,1:T(2,128)S(1)}, s32[2,2,512]{2,0,1:T(2,128)S(1)}, u32[]{:S(2)}, u32[]{:S(2)}) collective-permute-start(s32[2,2,512]{2,0,1:T(2,128)S(1)} %fusion.1), channel_id=1, source_target_pairs={{0,2},{2,0},{1,3},{3,1},{4,6},{6,4},{5,7},{7,5},{8,10},{10,8},{9,1... | collective-permute-start | bytes 24584 | tf_op jit(solution)/shard_map/ppermute | solution.py:332
  13.1 2.1 %collective-permute-done.1 = s32[2,2,512]{2,0,1:T(2,128)S(1)} collective-permute-done((s32[2,2,512]{2,0,1:T(2,128)S(1)}, s32[2,2,512]{2,0,1:T(2,128)S(1)}, u32[]{:S(2)}, u32[]{:S(2)}) %collective-permute-start.1) | collective-permute-done | bytes 8224 | tf_op jit(solution)/shard_map/ppermute | solution.py:332
  15.2 4.7 %collective-permute-done.3.refs_4_ = bf16[272,512]{1,0:T(8,128)(2,1)S(1)} collective-permute-done((bf16[272,512]{1,0:T(8,128)(2,1)S(1)}, bf16[272,512]{1,0:T(8,128)(2,1)S(1)}, u32[]{:S(2)}, u32[]{:S(2)}) %collective-permute-start.3) | collective-permute-done | bytes 278560 | tf_op jit(solution)/shard_map/ppermute | solution.py:336
  19.9 0.6 collective-permute-start.4
  20.6 3.5 %shard_map.167 = (bf16[2048,1024]{1,0:T(8,128)(2,1)S(1)}, bf16[1024,2048]{1,0:T(8,128)(2,1)S(1)}, bf16[2048,128]{1,0:T(8,128)(2,1)S(1)}, bf16[128,2048]{1,0:T(8,...) custom-call(s32[1,2048]{1,0:T(1,128)S(1)} %bitcast.24, s32[1,2048]{1,0:T(1,128)S(1)} %bitcast.23, ...), custom_call_target="tpu_custom_call" | custom-call | tf_op jit(solution)/shard_map/pallas_call | solution.py:77
  24.1 1.0 copy-done.3
  25.1 1.0 copy-done.5
  26.2 1.0 copy-done.9
  27.2 2.2 %shard_map.169 = (bf16[256,512]{1,0:T(8,128)(2,1)S(1)}, bf16[256,512]{1,0:T(8,128)(2,1)S(1)}, bf16[256,512]{1,0:T(8,128)(2,1)S(1)}, bf16[256,512]{1,0:T(8,128)(2...) custom-call(s32[2]{0:T(128)S(1)} %pad_add_fusion.4.refs_0_, bf16[512,512]{1,0:T(8,128)(2,1)S(1)} %copy-done.5, ...), custom_call_target="tpu_custom_call" | custom-call | tf_op jit(solution)/shard_map/pallas_call | solution.py:77
  29.4 1.4 %shard_map.170 = (bf16[256,512]{1,0:T(8,128)(2,1)S(1)}, bf16[256,512]{1,0:T(8,128)(2,1)S(1)}, f32[512,512]{1,0:T(8,128)S(1)}) custom-call(s32[2]{0:T(128)S(1)} %pad_add_fusion.4.refs_0_, bf16[512,512]{1,0:T(8,128)(2,1)S(1)} %get-tuple-element.61.refs_1_, bf16[512,512]{1,0:T(8,128)(2,1)S(1)} %copy-done.4, f32[512,512]{1,0:T(8,128)S(1)} %get-tuple-element.62.refs_3_, ...), custom_call_target="tpu_custom_call" | custom-call | tf_op jit(solution)/shard_map/pallas_call | solution.py:77
  30.9 1.6 %shard_map.171 = (bf16[256,512]{1,0:T(8,128)(2,1)S(1)}, bf16[256,512]{1,0:T(8,128)(2,1)S(1)}, f32[256,512]{1,0:T(8,128)S(1)}, bf16[256,512]{1,0:T(8,128)(2,1)S(1)}) custom-call(s32[2]{0:T(128)S(1)} %pad_add_fusion.4.refs_0_, bf16[512,512]{1,0:T(8,128)(2,1)S(1)} %get-tuple-element.61.refs_1_, bf16[512,512]{1,0:T(8,128)(2,1)S(1)} %copy-done.4, ...), custom_call_target="tpu_custom_call" | custom-call | tf_op jit(solution)/shard_map/pallas_call | solution.py:77
  32.6 1.5 %collective-permute-done.5 = bf16[256,512]{1,0:T(8,128)(2,1)S(1)} collective-permute-done((bf16[256,512]{1,0:T(8,128)(2,1)S(1)}, bf16[256,512]{1,0:T(8,128)(2,1)S(1)}, u32[]{:S(2)}, u32[]{:S(2)}) %collective-permute-start.5) | collective-permute-done | bytes 262176 | tf_op jit(solution)/shard_map/ppermute | solution.py:332
  34.2 1.6 %collective-permute-start.6 = (bf16[256,512]{1,0:T(8,128)(2,1)S(1)}, bf16[256,512]{1,0:T(8,128)(2,1)S(1)}, u32[]{:S(2)}, u32[]{:S(2)}) collective-permute-start(bf16[256,512]{1,0:T(8,128)(2,1)S(1)} %add_convert_fusion.2), channel_id=1, source_target_pairs={{0,2},{2,0},{1,3},{3,1},{4,6},{6,4},{5,7},{7,5},{8,10},{10,8},{9,1... | collective-permute-start | bytes 786440 | tf_op jit(solution)/shard_map/ppermute | solution.py:332
  35.8 6.8 %collective-permute-done.6 = bf16[256,512]{1,0:T(8,128)(2,1)S(1)} collective-permute-done((bf16[256,512]{1,0:T(8,128)(2,1)S(1)}, bf16[256,512]{1,0:T(8,128)(2,1)S(1)}, u32[]{:S(2)}, u32[]{:S(2)}) %collective-permute-start.6) | collective-permute-done | bytes 262176 | tf_op jit(solution)/shard_map/ppermute | solution.py:332
  42.8 1.5 %collective-permute-done.7.refs_2_ = bf16[256,512]{1,0:T(8,128)(2,1)S(1)} collective-permute-done((bf16[256,512]{1,0:T(8,128)(2,1)S(1)}, bf16[256,512]{1,0:T(8,128)(2,1)S(1)}, u32[]{:S(2)}, u32[]{:S(2)}) %collective-permute-start.7) | collective-permute-done | bytes 262176 | tf_op jit(solution)/shard_map/ppermute | solution.py:332
  44.3 1.6 %shard_map.172 = (bf16[512,512]{1,0:T(8,128)(2,1)S(1)}, f32[512,512]{1,0:T(8,128)S(1)}, bf16[512,512]{1,0:T(8,128)(2,1)S(1)}, bf16[32,512]{1,0:T(8,128)(2,1)S(1)...) custom-call(s32[2]{0:T(128)S(1)} %pad_add_fusion.4.refs_0_, bf16[256,512]{1,0:T(8,128)(2,1)S(1)} %add_convert_fusion.1.refs_1_, ...), custom_call_target="tpu_custom_call" | custom-call | tf_op jit(solution)/shard_map/pallas_call | solution.py:77
  45.9 1.5 %collective-permute-start.8 = (bf16[32,512]{1,0:T(8,128)(2,1)S(1)}, bf16[32,512]{1,0:T(8,128)(2,1)S(1)}, u32[]{:S(2)}, u32[]{:S(2)}) collective-permute-start(bf16[32,512]{1,0:T(8,128)(2,1)S(1)} %get-tuple-element.69), channel_id=1, source_target_pairs={{0,4},{4,8},{8,12},{12,0},{1,5},{5,9},{9,13},{13,1},{2,6},{6,10},{... | collective-permute-start | bytes 98312 | tf_op jit(solution)/shard_map/ppermute | solution.py:332
  47.4 2.0 %collective-permute-start.9 = (bf16[32,512]{1,0:T(8,128)(2,1)S(1)}, bf16[32,512]{1,0:T(8,128)(2,1)S(1)}, u32[]{:S(2)}, u32[]{:S(2)}) collective-permute-start(bf16[32,512]{1,0:T(8,128)(2,1)S(1)} %get-tuple-element.70), channel_id=1, source_target_pairs={{0,8},{4,12},{8,0},{12,4},{1,9},{5,13},{9,1},{13,5},{2,10},{6,14},... | collective-permute-start | bytes 98312 | tf_op jit(solution)/shard_map/ppermute | solution.py:332
  49.4 2.8 %collective-permute-start.10 = (bf16[32,512]{1,0:T(8,128)(2,1)S(1)}, bf16[32,512]{1,0:T(8,128)(2,1)S(1)}, u32[]{:S(2)}, u32[]{:S(2)}) collective-permute-start(bf16[32,512]{1,0:T(8,128)(2,1)S(1)} %get-tuple-element.71), channel_id=1, source_target_pairs={{0,12},{4,0},{8,4},{12,8},{1,13},{5,1},{9,5},{13,9},{2,14},{6,2},{... | collective-permute-start | bytes 98312 | tf_op jit(solution)/shard_map/ppermute | solution.py:332
  52.3 2.6 %shard_map.173.refs_1_ = f32[2048,512]{1,0:T(8,128)S(1)} custom-call(bf16[512,512]{1,0:T(8,128)(2,1)S(1)} %get-tuple-element.66.hidden.refs_0_, bf16[512,512]{1,0:T(8,128)(2,1)S(1)} %get-tuple-element.67.sent, bf16[2048,1024]{1,0:T(8,128)(2,1)S(1)} %get-tuple-element.68.here.refs_9_.refs_10_, bf16[3,512,512]{2,1,0:T(8,128)(2,1)S(1)} %copy-done.1), custom_call_target="tpu_custom_call" | custom-call | tf_op jit(solution)/shard_map/pallas_call | solution.py:77
  54.9 3.2 %shard_map.174 = (bf16[512,512]{1,0:T(8,128)(2,1)S(1)}, f32[512,512]{1,0:T(8,128)S(1)}, bf16[2048,512]{1,0:T(8,128)(2,1)S(1)}, bf16[512,512]{1,0:T(8,128)(2,1)S(...) custom-call(bf16[512,512]{1,0:T(8,128)(2,1)S(1)} %get-tuple-element.66.hidden.refs_0_, ...), custom_call_target="tpu_custom_call" | custom-call | tf_op jit(solution)/shard_map/pallas_call | solution.py:77
  58.2 3.6 %collective-permute-start.12 = (bf16[32,512]{1,0:T(8,128)(2,1)S(1)}, bf16[32,512]{1,0:T(8,128)(2,1)S(1)}, u32[]{:S(2)}, u32[]{:S(2)}) collective-permute-start(bf16[32,512]{1,0:T(8,128)(2,1)S(1)} %get-tuple-element.77), channel_id=1, source_target_pairs={{0,8},{4,12},{8,0},{12,4},{1,9},{5,13},{9,1},{13,5},{2,10},{6,14},... | collective-permute-start | bytes 98312 | tf_op jit(solution)/shard_map/ppermute | solution.py:332
  61.8 0.2 collective-permute-start.13
  62.0 2.6 %shard_map.175.refs_1_ = f32[2048,512]{1,0:T(8,128)S(1)} custom-call(bf16[512,512]{1,0:T(8,128)(2,1)S(1)} %get-tuple-element.74.hidden.refs_0_, bf16[512,512]{1,0:T(8,128)(2,1)S(1)} %get-tuple-element.75.sent, bf16[2048,1024]{1,0:T(8,128)(2,1)S(1)} %get-tuple-element.68.here.refs_9_.refs_10_, bf16[3,512,512]{2,1,0:T(8,128)(2,1)S(1)} %copy-done.1), custom_call_target="tpu_custom_call" | custom-call | tf_op jit(solution)/shard_map/pallas_call | solution.py:77
  64.7 1.0 collective-permute-done.13.refs_4_
  65.7 3.3 %shard_map.176 = (bf16[512,512]{1,0:T(8,128)(2,1)S(1)}, f32[512,512]{1,0:T(8,128)S(1)}, bf16[2048,512]{1,0:T(8,128)(2,1)S(1)}, bf16[512,512]{1,0:T(8,128)(2,1)S(...) custom-call(bf16[512,512]{1,0:T(8,128)(2,1)S(1)} %get-tuple-element.74.hidden.refs_0_, ...), custom_call_target="tpu_custom_call" | custom-call | tf_op jit(solution)/shard_map/pallas_call | solution.py:77
  69.0 0.8 collective-permute-start.14
  69.8 1.9 %collective-permute-start.15 = (bf16[32,512]{1,0:T(8,128)(2,1)S(1)}, bf16[32,512]{1,0:T(8,128)(2,1)S(1)}, u32[]{:S(2)}, u32[]{:S(2)}) collective-permute-start(bf16[32,512]{1,0:T(8,128)(2,1)S(1)} %get-tuple-element.82), channel_id=1, source_target_pairs={{0,8},{4,12},{8,0},{12,4},{1,9},{5,13},{9,1},{13,5},{2,10},{6,14},... | collective-permute-start | bytes 98312 | tf_op jit(solution)/shard_map/ppermute | solution.py:332
  71.7 1.2 collective-permute-start.16
  72.9 2.6 %shard_map.177.refs_1_ = f32[2048,512]{1,0:T(8,128)S(1)} custom-call(bf16[512,512]{1,0:T(8,128)(2,1)S(1)} %get-tuple-element.79.hidden.refs_0_, bf16[512,512]{1,0:T(8,128)(2,1)S(1)} %get-tuple-element.80.sent, bf16[2048,1024]{1,0:T(8,128)(2,1)S(1)} %get-tuple-element.68.here.refs_9_.refs_10_, bf16[3,512,512]{2,1,0:T(8,128)(2,1)S(1)} %copy-done.1), custom_call_target="tpu_custom_call" | custom-call | tf_op jit(solution)/shard_map/pallas_call | solution.py:77
  75.7 5.7 %shard_map.178 = (bf16[512,512]{1,0:T(8,128)(2,1)}, bf16[2048,512]{1,0:T(8,128)(2,1)S(1)}, bf16[32,512]{1,0:T(8,128)(2,1)S(1)}, bf16[32,512]{1,0:T(8,128)(2,1)S(1)}, bf16[32,512]{1,0:T(8,128)(2,1)S(1)}) custom-call(bf16[512,512]{1,0:T(8,128)(2,1)S(1)} %get-tuple-element.79.hidden.refs_0_, f32[2048,512]{1,0:T(8,128)S(1)} %shard_map.177.refs_1_, ...), custom_call_target="tpu_custom_call" | custom-call | tf_op jit(solution)/shard_map/pallas_call | solution.py:77
  81.4 3.0 %collective-permute-start.17 = (bf16[32,512]{1,0:T(8,128)(2,1)S(1)}, bf16[32,512]{1,0:T(8,128)(2,1)S(1)}, u32[]{:S(2)}, u32[]{:S(2)}) collective-permute-start(bf16[32,512]{1,0:T(8,128)(2,1)S(1)} %get-tuple-element.87), channel_id=1, source_target_pairs={{0,12},{4,0},{8,4},{12,8},{1,13},{5,1},{9,5},{13,9},{2,14},{6,2},{... | collective-permute-start | bytes 98312 | tf_op jit(solution)/shard_map/ppermute | solution.py:332
  84.5 0.8 collective-permute-start.19
  85.3 2.9 %shard_map.179.refs_0_ = f32[512,512]{1,0:T(8,128)S(1)} custom-call(bf16[512,512]{1,0:T(8,128)(2,1)S(1)} %copy-done.8, bf16[2048,512]{1,0:T(8,128)(2,1)S(1)} %get-tuple-element.86.grad_pre, bf16[1024,2048]{1,0:T(8,128)(2,1)S(1)} %get-tuple-element.73.refs_6_.there, bf16[3,512,512]{2,1,0:T(8,128)(2,1)S(1)} %copy-done, bf16[3,512,512]{2,1,0:T(8,128)(2,1)S(1)} %copy-done.1), custom_call_target="tpu_custom_call" | custom-call | tf_op jit(solution)/shard_map/pallas_call | solution.py:77
  88.2 1.0 collective-permute-done.18.refs_2_
  89.2 1.1 collective-permute-done.19.refs_3_
  90.2 2.6 %shard_map.180 = (f32[512,512]{1,0:T(8,128)S(1)}, bf16[2048,512]{1,0:T(8,128)(2,1)S(1)}, bf16[32,512]{1,0:T(8,128)(2,1)S(1)}, bf16[32,512]{1,0:T(8,128)(2,1)S(1)}, bf16[32,512]{1,0:T(8,128)(2,1)S(1)}) custom-call(f32[512,512]{1,0:T(8,128)S(1)} %shard_map.179.refs_0_, bf16[32,512]{1,0:T(8,128)(2,1)S(1)} %collective-permute-done.17.refs_1_, ...), custom_call_target="tpu_custom_call" | custom-call | tf_op jit(solution)/shard_map/pallas_call | solution.py:77
  92.8 1.1 collective-permute-start.20
  93.9 1.0 collective-permute-start.21
  94.9 1.0 collective-permute-start.22
  95.9 2.9 %shard_map.181.refs_0_ = f32[512,512]{1,0:T(8,128)S(1)} custom-call(f32[512,512]{1,0:T(8,128)S(1)} %get-tuple-element.93.upstream, bf16[2048,512]{1,0:T(8,128)(2,1)S(1)} %get-tuple-element.94.grad_pre, bf16[1024,2048]{1,0:T(8,128)(2,1)S(1)} %get-tuple-element.73.refs_6_.there, bf16[3,512,512]{2,1,0:T(8,128)(2,1)S(1)} %copy-done, ...), custom_call_target="tpu_custom_call" | custom-call | tf_op jit(solution)/shard_map/pallas_call | solution.py:77
  98.8 1.9 %collective-permute-done.22.refs_3_ = bf16[32,512]{1,0:T(8,128)(2,1)S(1)} collective-permute-done((bf16[32,512]{1,0:T(8,128)(2,1)S(1)}, bf16[32,512]{1,0:T(8,128)(2,1)S(1)}, u32[]{:S(2)}, u32[]{:S(2)}) %collective-permute-start.22) | collective-permute-done | bytes 32800 | tf_op jit(solution)/shard_map/ppermute | solution.py:332
  100.7 2.6 %shard_map.182 = (f32[512,512]{1,0:T(8,128)S(1)}, bf16[2048,512]{1,0:T(8,128)(2,1)S(1)}, bf16[32,512]{1,0:T(8,128)(2,1)S(1)}, bf16[32,512]{1,0:T(8,128)(2,1)S(1)}, bf16[32,512]{1,0:T(8,128)(2,1)S(1)}) custom-call(f32[512,512]{1,0:T(8,128)S(1)} %shard_map.181.refs_0_, bf16[32,512]{1,0:T(8,128)(2,1)S(1)} %collective-permute-done.20.refs_1_, ...), custom_call_target="tpu_custom_call" | custom-call | tf_op jit(solution)/shard_map/pallas_call | solution.py:77
  103.3 0.9 collective-permute-start.23
  104.2 0.2 collective-permute-start.24
  104.4 1.0 collective-permute-start.25
  105.4 2.9 %shard_map.183.refs_0_ = f32[512,512]{1,0:T(8,128)S(1)} custom-call(f32[512,512]{1,0:T(8,128)S(1)} %get-tuple-element.100.upstream, bf16[2048,512]{1,0:T(8,128)(2,1)S(1)} %get-tuple-element.101.grad_pre, bf16[1024,2048]{1,0:T(8,128)(2,1)S(1)} %get-tuple-element.73.refs_6_.there, bf16[3,512,512]{2,1,0:T(8,128)(2,1)S(1)} %copy-done, ...), custom_call_target="tpu_custom_call" | custom-call | tf_op jit(solution)/shard_map/pallas_call | solution.py:77
  108.3 0.9 collective-permute-done.24.refs_2_
  109.1 1.4 %collective-permute-done.25.refs_3_ = bf16[32,512]{1,0:T(8,128)(2,1)S(1)} collective-permute-done((bf16[32,512]{1,0:T(8,128)(2,1)S(1)}, bf16[32,512]{1,0:T(8,128)(2,1)S(1)}, u32[]{:S(2)}, u32[]{:S(2)}) %collective-permute-start.25) | collective-permute-done | bytes 32800 | tf_op jit(solution)/shard_map/ppermute | solution.py:332
  110.6 1.7 %shard_map.184 = (bf16[256,512]{1,0:T(8,128)(2,1)S(1)}, bf16[256,512]{1,0:T(8,128)(2,1)S(1)}, bf16[256,512]{1,0:T(8,128)(2,1)S(1)}, bf16[256,512]{1,0:T(8,128)(2,1)S(1)}) custom-call(f32[512,512]{1,0:T(8,128)S(1)} %shard_map.183.refs_0_, bf16[32,512]{1,0:T(8,128)(2,1)S(1)} %collective-permute-done.23.refs_1_, ...), custom_call_target="tpu_custom_call" | custom-call | tf_op jit(solution)/shard_map/pallas_call | solution.py:77
  112.4 2.0 %collective-permute-start.26 = (bf16[256,512]{1,0:T(8,128)(2,1)S(1)}, bf16[256,512]{1,0:T(8,128)(2,1)S(1)}, u32[]{:S(2)}, u32[]{:S(2)}) collective-permute-start(bf16[256,512]{1,0:T(8,128)(2,1)S(1)} %get-tuple-element.115), channel_id=1, source_target_pairs={{0,4},{4,0},{8,12},{12,8},{1,5},{5,1},{9,13},{13,9},{2,6},{6,2},{1... | collective-permute-start | bytes 786440 | tf_op jit(solution)/shard_map/ppermute | solution.py:336
  114.4 7.1 %collective-permute-done.27 = bf16[256,512]{1,0:T(8,128)(2,1)S(1)} collective-permute-done((bf16[256,512]{1,0:T(8,128)(2,1)S(1)}, bf16[256,512]{1,0:T(8,128)(2,1)S(1)}, u32[]{:S(2)}, u32[]{:S(2)}) %collective-permute-start.27) | collective-permute-done | bytes 262176 | tf_op jit(solution)/shard_map/ppermute | solution.py:336
  121.7 2.7 %collective-permute-done.26.refs_1_ = bf16[256,512]{1,0:T(8,128)(2,1)S(1)} collective-permute-done((bf16[256,512]{1,0:T(8,128)(2,1)S(1)}, bf16[256,512]{1,0:T(8,128)(2,1)S(1)}, u32[]{:S(2)}, u32[]{:S(2)}) %collective-permute-start.26) | collective-permute-done | bytes 262176 | tf_op jit(solution)/shard_map/ppermute | solution.py:336
  124.3 6.4 %collective-permute-done.28.refs_2_ = bf16[256,512]{1,0:T(8,128)(2,1)S(1)} collective-permute-done((bf16[256,512]{1,0:T(8,128)(2,1)S(1)}, bf16[256,512]{1,0:T(8,128)(2,1)S(1)}, u32[]{:S(2)}, u32[]{:S(2)}) %collective-permute-start.28) | collective-permute-done | bytes 262176 | tf_op jit(solution)/shard_map/ppermute | solution.py:336
  130.7 1.1 shard_map.185
  (66 shorter events, 1.5 us)
Async XLA Ops:
  0.6 28.8 %copy-start.4 = (bf16[512,512]{1,0:T(8,128)(2,1)S(1)}, bf16[512,512]{1,0:T(8,128)(2,1)}, u32[]{:S(2)}) copy-start(bf16[512,512]{1,0:T(8,128)(2,1)} %refs_3_.5) | copy-start | bytes 1572868
  0.6 1.0 copy-start.10
  1.6 0.7 copy-start.13
  2.3 0.7 copy-start.14
  3.0 16.8 %collective-permute-start.3 = (bf16[272,512]{1,0:T(8,128)(2,1)S(1)}, bf16[272,512]{1,0:T(8,128)(2,1)S(1)}, u32[]{:S(2)}, u32[]{:S(2)}) collective-permute-start(bf16[272,512]{1,0:T(8,128)(2,1)S(1)} %shard_map.168.refs_5_), channel_id=1, source_target_pairs={{0,8},{4,12},{8,0},{12,4},{1,9},{5,13},{9,1},{13,5},{2,10},{6,14},... | collective-permute-start | bytes 835592 | tf_op jit(solution)/shard_map/ppermute | solution.py:336
  7.1 16.9 %collective-permute-start.2 = (bf16[272,512]{1,0:T(8,128)(2,1)S(1)}, bf16[272,512]{1,0:T(8,128)(2,1)S(1)}, u32[]{:S(2)}, u32[]{:S(2)}) collective-permute-start(bf16[272,512]{1,0:T(8,128)(2,1)S(1)} %shard_map.168.refs_5_), channel_id=1, source_target_pairs={{0,4},{4,0},{8,12},{12,8},{1,5},{5,1},{9,13},{13,9},{2,6},{6,2},{1... | collective-permute-start | bytes 835592 | tf_op jit(solution)/shard_map/ppermute | solution.py:336
  10.1 1.2 collective-permute-start
  11.5 3.7 %collective-permute-start.1 = (s32[2,2,512]{2,0,1:T(2,128)S(1)}, s32[2,2,512]{2,0,1:T(2,128)S(1)}, u32[]{:S(2)}, u32[]{:S(2)}) collective-permute-start(s32[2,2,512]{2,0,1:T(2,128)S(1)} %fusion.1), channel_id=1, source_target_pairs={{0,2},{2,0},{1,3},{3,1},{4,6},{6,4},{5,7},{7,5},{8,10},{10,8},{9,1... | collective-permute-start | bytes 24584 | tf_op jit(solution)/shard_map/ppermute | solution.py:332
  19.9 11.0 %collective-permute-start.4 = (bf16[272,512]{1,0:T(8,128)(2,1)S(1)}, bf16[272,512]{1,0:T(8,128)(2,1)S(1)}, u32[]{:S(2)}, u32[]{:S(2)}) collective-permute-start(bf16[272,512]{1,0:T(8,128)(2,1)S(1)} %collective-permute-done.3.refs_4_), channel_id=1, source_target_pairs={{0,4},{4,0},{8,12},{12,8},{1,5},{5,1},{9,13},{13,9},{2,6},{6,2},{1... | collective-permute-start | bytes 835592 | tf_op jit(solution)/shard_map/ppermute | solution.py:336
  24.1 1.0 copy-start.3
  25.1 1.0 copy-start.5
  26.2 1.0 copy-start.9
  30.9 13.4 %copy-start = (bf16[3,512,512]{2,1,0:T(8,128)(2,1)S(1)}, bf16[3,512,512]{2,1,0:T(8,128)(2,1)}, u32[]{:S(2)}) copy-start(bf16[3,512,512]{2,1,0:T(8,128)(2,1)} %refs_5_.5) | copy-start | bytes 4718596
  30.9 13.4 %copy-start.6 = (bf16[512,512]{1,0:T(8,128)(2,1)S(1)}, bf16[512,512]{1,0:T(8,128)(2,1)}, u32[]{:S(2)}) copy-start(bf16[512,512]{1,0:T(8,128)(2,1)} %refs_3_.4) | copy-start | bytes 1572868
  30.9 13.4 %copy-start.7 = (bf16[512,512]{1,0:T(8,128)(2,1)S(1)}, bf16[512,512]{1,0:T(8,128)(2,1)}, u32[]{:S(2)}) copy-start(bf16[512,512]{1,0:T(8,128)(2,1)} %refs_8_.11) | copy-start | bytes 1572868
  30.9 13.4 %copy-start.12 = (f32[512]{0:T(512)S(1)}, f32[512]{0:T(512)}, u32[]{:S(2)}) copy-start(f32[512]{0:T(512)} %param.26) | copy-start | bytes 6148
  32.5 1.6 %collective-permute-start.5 = (bf16[256,512]{1,0:T(8,128)(2,1)S(1)}, bf16[256,512]{1,0:T(8,128)(2,1)S(1)}, u32[]{:S(2)}, u32[]{:S(2)}) collective-permute-start(bf16[256,512]{1,0:T(8,128)(2,1)S(1)} %get-tuple-element.65), channel_id=1, source_target_pairs={{0,1},{1,0},{2,3},{3,2},{4,5},{5,4},{6,7},{7,6},{8,9},{9,8},{10,11... | collective-permute-start | bytes 786440 | tf_op jit(solution)/shard_map/ppermute | solution.py:332
  34.2 18.0 %copy-start.1 = (bf16[3,512,512]{2,1,0:T(8,128)(2,1)S(1)}, bf16[3,512,512]{2,1,0:T(8,128)(2,1)}, u32[]{:S(2)}) copy-start(bf16[3,512,512]{2,1,0:T(8,128)(2,1)} %w_recv.11) | copy-start | bytes 4718596
  34.2 8.4 %collective-permute-start.6 = (bf16[256,512]{1,0:T(8,128)(2,1)S(1)}, bf16[256,512]{1,0:T(8,128)(2,1)S(1)}, u32[]{:S(2)}, u32[]{:S(2)}) collective-permute-start(bf16[256,512]{1,0:T(8,128)(2,1)S(1)} %add_convert_fusion.2), channel_id=1, source_target_pairs={{0,2},{2,0},{1,3},{3,1},{4,6},{6,4},{5,7},{7,5},{8,10},{10,8},{9,1... | collective-permute-start | bytes 786440 | tf_op jit(solution)/shard_map/ppermute | solution.py:332
  42.7 1.6 %collective-permute-start.7 = (bf16[256,512]{1,0:T(8,128)(2,1)S(1)}, bf16[256,512]{1,0:T(8,128)(2,1)S(1)}, u32[]{:S(2)}, u32[]{:S(2)}) collective-permute-start(bf16[256,512]{1,0:T(8,128)(2,1)S(1)} %add_convert_fusion.1.refs_1_), channel_id=1, source_target_pairs={{0,1},{1,0},{2,3},{3,2},{4,5},{5,4},{6,7},{7,6},{8,9},{9,8},{10,11... | collective-permute-start | bytes 786440 | tf_op jit(solution)/shard_map/ppermute | solution.py:332
  45.9 9.0 %collective-permute-start.8 = (bf16[32,512]{1,0:T(8,128)(2,1)S(1)}, bf16[32,512]{1,0:T(8,128)(2,1)S(1)}, u32[]{:S(2)}, u32[]{:S(2)}) collective-permute-start(bf16[32,512]{1,0:T(8,128)(2,1)S(1)} %get-tuple-element.69), channel_id=1, source_target_pairs={{0,4},{4,8},{8,12},{12,0},{1,5},{5,9},{9,13},{13,1},{2,6},{6,10},{... | collective-permute-start | bytes 98312 | tf_op jit(solution)/shard_map/ppermute | solution.py:332
  47.4 7.5 %collective-permute-start.9 = (bf16[32,512]{1,0:T(8,128)(2,1)S(1)}, bf16[32,512]{1,0:T(8,128)(2,1)S(1)}, u32[]{:S(2)}, u32[]{:S(2)}) collective-permute-start(bf16[32,512]{1,0:T(8,128)(2,1)S(1)} %get-tuple-element.70), channel_id=1, source_target_pairs={{0,8},{4,12},{8,0},{12,4},{1,9},{5,13},{9,1},{13,5},{2,10},{6,14},... | collective-permute-start | bytes 98312 | tf_op jit(solution)/shard_map/ppermute | solution.py:332
  49.4 5.5 %collective-permute-start.10 = (bf16[32,512]{1,0:T(8,128)(2,1)S(1)}, bf16[32,512]{1,0:T(8,128)(2,1)S(1)}, u32[]{:S(2)}, u32[]{:S(2)}) collective-permute-start(bf16[32,512]{1,0:T(8,128)(2,1)S(1)} %get-tuple-element.71), channel_id=1, source_target_pairs={{0,12},{4,0},{8,4},{12,8},{1,13},{5,1},{9,5},{13,9},{2,14},{6,2},{... | collective-permute-start | bytes 98312 | tf_op jit(solution)/shard_map/ppermute | solution.py:332
  52.3 2.7 %copy-start.2 = (bf16[3,512,512]{2,1,0:T(8,128)(2,1)S(1)}, bf16[3,512,512]{2,1,0:T(8,128)(2,1)}, u32[]{:S(2)}) copy-start(bf16[3,512,512]{2,1,0:T(8,128)(2,1)} %refs_9_.7) | copy-start | bytes 4718596
  52.3 2.7 %copy-start.11 = (f32[3,512]{1,0:T(4,128)S(1)}, f32[3,512]{1,0:T(4,128)}, u32[]{:S(2)}) copy-start(f32[3,512]{1,0:T(4,128)} %refs_8_.10) | copy-start | bytes 18436
  58.1 6.5 %collective-permute-start.11 = (bf16[32,512]{1,0:T(8,128)(2,1)S(1)}, bf16[32,512]{1,0:T(8,128)(2,1)S(1)}, u32[]{:S(2)}, u32[]{:S(2)}) collective-permute-start(bf16[32,512]{1,0:T(8,128)(2,1)S(1)} %get-tuple-element.76), channel_id=1, source_target_pairs={{0,4},{4,8},{8,12},{12,0},{1,5},{5,9},{9,13},{13,1},{2,6},{6,10},{... | collective-permute-start | bytes 98312 | tf_op jit(solution)/shard_map/ppermute | solution.py:332
  58.2 6.5 %collective-permute-start.12 = (bf16[32,512]{1,0:T(8,128)(2,1)S(1)}, bf16[32,512]{1,0:T(8,128)(2,1)S(1)}, u32[]{:S(2)}, u32[]{:S(2)}) collective-permute-start(bf16[32,512]{1,0:T(8,128)(2,1)S(1)} %get-tuple-element.77), channel_id=1, source_target_pairs={{0,8},{4,12},{8,0},{12,4},{1,9},{5,13},{9,1},{13,5},{2,10},{6,14},... | collective-permute-start | bytes 98312 | tf_op jit(solution)/shard_map/ppermute | solution.py:332
  61.8 3.9 %collective-permute-start.13 = (bf16[32,512]{1,0:T(8,128)(2,1)S(1)}, bf16[32,512]{1,0:T(8,128)(2,1)S(1)}, u32[]{:S(2)}, u32[]{:S(2)}) collective-permute-start(bf16[32,512]{1,0:T(8,128)(2,1)S(1)} %get-tuple-element.78), channel_id=1, source_target_pairs={{0,12},{4,0},{8,4},{12,8},{1,13},{5,1},{9,5},{13,9},{2,14},{6,2},{... | collective-permute-start | bytes 98312 | tf_op jit(solution)/shard_map/ppermute | solution.py:332
  69.0 6.6 %collective-permute-start.14 = (bf16[32,512]{1,0:T(8,128)(2,1)S(1)}, bf16[32,512]{1,0:T(8,128)(2,1)S(1)}, u32[]{:S(2)}, u32[]{:S(2)}) collective-permute-start(bf16[32,512]{1,0:T(8,128)(2,1)S(1)} %get-tuple-element.81), channel_id=1, source_target_pairs={{0,4},{4,8},{8,12},{12,0},{1,5},{5,9},{9,13},{13,1},{2,6},{6,10},{... | collective-permute-start | bytes 98312 | tf_op jit(solution)/shard_map/ppermute | solution.py:332
  69.8 5.7 %collective-permute-start.15 = (bf16[32,512]{1,0:T(8,128)(2,1)S(1)}, bf16[32,512]{1,0:T(8,128)(2,1)S(1)}, u32[]{:S(2)}, u32[]{:S(2)}) collective-permute-start(bf16[32,512]{1,0:T(8,128)(2,1)S(1)} %get-tuple-element.82), channel_id=1, source_target_pairs={{0,8},{4,12},{8,0},{12,4},{1,9},{5,13},{9,1},{13,5},{2,10},{6,14},... | collective-permute-start | bytes 98312 | tf_op jit(solution)/shard_map/ppermute | solution.py:332
  71.7 3.9 %collective-permute-start.16 = (bf16[32,512]{1,0:T(8,128)(2,1)S(1)}, bf16[32,512]{1,0:T(8,128)(2,1)S(1)}, u32[]{:S(2)}, u32[]{:S(2)}) collective-permute-start(bf16[32,512]{1,0:T(8,128)(2,1)S(1)} %get-tuple-element.83), channel_id=1, source_target_pairs={{0,12},{4,0},{8,4},{12,8},{1,13},{5,1},{9,5},{13,9},{2,14},{6,2},{... | collective-permute-start | bytes 98312 | tf_op jit(solution)/shard_map/ppermute | solution.py:332
  72.9 2.8 %copy-start.8 = (bf16[512,512]{1,0:T(8,128)(2,1)S(1)}, bf16[512,512]{1,0:T(8,128)(2,1)}, u32[]{:S(2)}) copy-start(bf16[512,512]{1,0:T(8,128)(2,1)} %upstream.1) | copy-start | bytes 1572868
  81.4 6.7 %collective-permute-start.17 = (bf16[32,512]{1,0:T(8,128)(2,1)S(1)}, bf16[32,512]{1,0:T(8,128)(2,1)S(1)}, u32[]{:S(2)}, u32[]{:S(2)}) collective-permute-start(bf16[32,512]{1,0:T(8,128)(2,1)S(1)} %get-tuple-element.87), channel_id=1, source_target_pairs={{0,12},{4,0},{8,4},{12,8},{1,13},{5,1},{9,5},{13,9},{2,14},{6,2},{... | collective-permute-start | bytes 98312 | tf_op jit(solution)/shard_map/ppermute | solution.py:332
  84.4 4.8 %collective-permute-start.18 = (bf16[32,512]{1,0:T(8,128)(2,1)S(1)}, bf16[32,512]{1,0:T(8,128)(2,1)S(1)}, u32[]{:S(2)}, u32[]{:S(2)}) collective-permute-start(bf16[32,512]{1,0:T(8,128)(2,1)S(1)} %get-tuple-element.88), channel_id=1, source_target_pairs={{0,8},{4,12},{8,0},{12,4},{1,9},{5,13},{9,1},{13,5},{2,10},{6,14},... | collective-permute-start | bytes 98312 | tf_op jit(solution)/shard_map/ppermute | solution.py:332
  84.5 5.7 %collective-permute-start.19 = (bf16[32,512]{1,0:T(8,128)(2,1)S(1)}, bf16[32,512]{1,0:T(8,128)(2,1)S(1)}, u32[]{:S(2)}, u32[]{:S(2)}) collective-permute-start(bf16[32,512]{1,0:T(8,128)(2,1)S(1)} %get-tuple-element.89), channel_id=1, source_target_pairs={{0,4},{4,8},{8,12},{12,0},{1,5},{5,9},{9,13},{13,1},{2,6},{6,10},{... | collective-permute-start | bytes 98312 | tf_op jit(solution)/shard_map/ppermute | solution.py:332
  92.8 5.9 %collective-permute-start.20 = (bf16[32,512]{1,0:T(8,128)(2,1)S(1)}, bf16[32,512]{1,0:T(8,128)(2,1)S(1)}, u32[]{:S(2)}, u32[]{:S(2)}) collective-permute-start(bf16[32,512]{1,0:T(8,128)(2,1)S(1)} %get-tuple-element.95), channel_id=1, source_target_pairs={{0,12},{4,0},{8,4},{12,8},{1,13},{5,1},{9,5},{13,9},{2,14},{6,2},{... | collective-permute-start | bytes 98312 | tf_op jit(solution)/shard_map/ppermute | solution.py:332
  93.9 4.9 %collective-permute-start.21 = (bf16[32,512]{1,0:T(8,128)(2,1)S(1)}, bf16[32,512]{1,0:T(8,128)(2,1)S(1)}, u32[]{:S(2)}, u32[]{:S(2)}) collective-permute-start(bf16[32,512]{1,0:T(8,128)(2,1)S(1)} %get-tuple-element.96), channel_id=1, source_target_pairs={{0,8},{4,12},{8,0},{12,4},{1,9},{5,13},{9,1},{13,5},{2,10},{6,14},... | collective-permute-start | bytes 98312 | tf_op jit(solution)/shard_map/ppermute | solution.py:332
  94.9 5.8 %collective-permute-start.22 = (bf16[32,512]{1,0:T(8,128)(2,1)S(1)}, bf16[32,512]{1,0:T(8,128)(2,1)S(1)}, u32[]{:S(2)}, u32[]{:S(2)}) collective-permute-start(bf16[32,512]{1,0:T(8,128)(2,1)S(1)} %get-tuple-element.97), channel_id=1, source_target_pairs={{0,4},{4,8},{8,12},{12,0},{1,5},{5,9},{9,13},{13,1},{2,6},{6,10},{... | collective-permute-start | bytes 98312 | tf_op jit(solution)/shard_map/ppermute | solution.py:332
  103.3 5.0 %collective-permute-start.23 = (bf16[32,512]{1,0:T(8,128)(2,1)S(1)}, bf16[32,512]{1,0:T(8,128)(2,1)S(1)}, u32[]{:S(2)}, u32[]{:S(2)}) collective-permute-start(bf16[32,512]{1,0:T(8,128)(2,1)S(1)} %get-tuple-element.102), channel_id=1, source_target_pairs={{0,12},{4,0},{8,4},{12,8},{1,13},{5,1},{9,5},{13,9},{2,14},{6,2},{... | collective-permute-start | bytes 98312 | tf_op jit(solution)/shard_map/ppermute | solution.py:332
  104.2 4.9 %collective-permute-start.24 = (bf16[32,512]{1,0:T(8,128)(2,1)S(1)}, bf16[32,512]{1,0:T(8,128)(2,1)S(1)}, u32[]{:S(2)}, u32[]{:S(2)}) collective-permute-start(bf16[32,512]{1,0:T(8,128)(2,1)S(1)} %get-tuple-element.103), channel_id=1, source_target_pairs={{0,8},{4,12},{8,0},{12,4},{1,9},{5,13},{9,1},{13,5},{2,10},{6,14},... | collective-permute-start | bytes 98312 | tf_op jit(solution)/shard_map/ppermute | solution.py:332
  104.4 6.2 %collective-permute-start.25 = (bf16[32,512]{1,0:T(8,128)(2,1)S(1)}, bf16[32,512]{1,0:T(8,128)(2,1)S(1)}, u32[]{:S(2)}, u32[]{:S(2)}) collective-permute-start(bf16[32,512]{1,0:T(8,128)(2,1)S(1)} %get-tuple-element.104), channel_id=1, source_target_pairs={{0,4},{4,8},{8,12},{12,0},{1,5},{5,9},{9,13},{13,1},{2,6},{6,10},{... | collective-permute-start | bytes 98312 | tf_op jit(solution)/shard_map/ppermute | solution.py:332
  112.3 9.2 %collective-permute-start.27 = (bf16[256,512]{1,0:T(8,128)(2,1)S(1)}, bf16[256,512]{1,0:T(8,128)(2,1)S(1)}, u32[]{:S(2)}, u32[]{:S(2)}) collective-permute-start(bf16[256,512]{1,0:T(8,128)(2,1)S(1)} %get-tuple-element.117), channel_id=1, source_target_pairs={{0,4},{4,0},{8,12},{12,8},{1,5},{5,1},{9,13},{13,9},{2,6},{6,2},{1... | collective-permute-start | bytes 786440 | tf_op jit(solution)/shard_map/ppermute | solution.py:336
  112.4 11.9 %collective-permute-start.26 = (bf16[256,512]{1,0:T(8,128)(2,1)S(1)}, bf16[256,512]{1,0:T(8,128)(2,1)S(1)}, u32[]{:S(2)}, u32[]{:S(2)}) collective-permute-start(bf16[256,512]{1,0:T(8,128)(2,1)S(1)} %get-tuple-element.115), channel_id=1, source_target_pairs={{0,4},{4,0},{8,12},{12,8},{1,5},{5,1},{9,13},{13,9},{2,6},{6,2},{1... | collective-permute-start | bytes 786440 | tf_op jit(solution)/shard_map/ppermute | solution.py:336
  121.6 9.2 %collective-permute-start.28 = (bf16[256,512]{1,0:T(8,128)(2,1)S(1)}, bf16[256,512]{1,0:T(8,128)(2,1)S(1)}, u32[]{:S(2)}, u32[]{:S(2)}) collective-permute-start(bf16[256,512]{1,0:T(8,128)(2,1)S(1)} %add_convert_fusion), channel_id=1, source_target_pairs={{0,8},{4,12},{8,0},{12,4},{1,9},{5,13},{9,1},{13,5},{2,10},{6,14},... | collective-permute-start | bytes 786440 | tf_op jit(solution)/shard_map/ppermute | solution.py:336

commit v3 on v2

--- a/solution.py
+++ b/solution.py
@@ -1,4 +1,5 @@
 import functools
+import math
 
 import jax
 import jax.numpy as jnp
@@ -64,23 +65,30 @@
     return jnp.concatenate([as_mask(column == lane + at) for at in range(0, width, LANES)], axis=1)
 
 
-def call(body, outs, scratch=()):
+def call(body, outs, scratch=(), products=(), copied=False):
     def run(*args):
         def where(array):
+            if copied:
+                return pl.BlockSpec(memory_space=pltpu.HBM)
             return pl.BlockSpec(memory_space=pltpu.SMEM if array.dtype == i32 and array.ndim == 1 else pltpu.VMEM)
 
-        held = [(shape, dtype) for shape, dtype in scratch]
-        own = sum(jnp.dtype(dtype).itemsize * shape[0] * shape[1] for shape, dtype in held) + (10 << 20)
-        room = own + sum(array.dtype.itemsize * array.size for array in args)
-        room += sum(jnp.dtype(dtype).itemsize * shape[0] * shape[1] for shape, dtype in outs)
-        limit = own if room < 40 << 20 else min(room, 60 << 20)
+        def size(shape, dtype):
+            return jnp.dtype(dtype).itemsize * math.prod(shape)
+
+        own = sum(size(*held) for held in scratch) + (10 << 20)
+        moved = sum(array.dtype.itemsize * array.size for array in args) + sum(size(*out) for out in outs)
+        limit = own if own + moved < 40 << 20 else min(own + moved, 60 << 20)
+        semaphores = [pltpu.SemaphoreType.DMA((len(args),))] if copied else []
         return pl.pallas_call(
             body,
             out_shape=tuple(jax.ShapeDtypeStruct(shape, dtype) for shape, dtype in outs),
             in_specs=[where(array) for array in args],
             out_specs=tuple(pl.BlockSpec(memory_space=pltpu.VMEM) for _ in outs),
-            scratch_shapes=[pltpu.VMEM(shape, dtype) for shape, dtype in held],
+            scratch_shapes=[pltpu.VMEM(shape, dtype) for shape, dtype in scratch] + semaphores,
             compiler_params=pltpu.CompilerParams(vmem_limit_bytes=limit),
+            cost_estimate=pl.CostEstimate(
+                flops=2 * sum(math.prod(product) for product in products), bytes_accessed=moved, transcendentals=0
+            ),
         )(*args)
 
     return run
@@ -109,18 +117,27 @@
     list_there[...] = pick_columns(order[...], 0, nodes)
 
 
-def note_kernel(rows, shards, nodes, payload):
+def note_kernel(rows, shards, nodes, payload, shard_rows, node_rows, arrived):
     grid = rows.shape[0]
-    payload[0:grid, :] = rows[...]
+    copies = [
+        pltpu.make_async_copy(rows, payload.at[0:grid], arrived.at[0]),
+        pltpu.make_async_copy(shards, shard_rows, arrived.at[1]),
+        pltpu.make_async_copy(nodes, node_rows, arrived.at[2]),
+    ]
+    for copy in copies:
+        copy.start()
+    copies[1].wait()
+    copies[2].wait()
     row = lax.broadcasted_iota(i32, (EXTRA, grid), 0)
     notes = jnp.full((EXTRA, grid), -1, i32)
     for top in range(shards.shape[0]):
-        node = nodes[top : top + 1, :]
-        for at, value in enumerate((shards[top : top + 1, :], node & 255, node >> 8)):
+        node = node_rows[top : top + 1, :]
+        for at, value in enumerate((shard_rows[top : top + 1, :], node & 255, node >> 8)):
             notes = jnp.where(row == 3 * top + at, value, notes)
     payload[grid:, 0:grid] = notes.astype(f32).astype(bf16)
     if grid < payload.shape[1]:
         payload[grid:, grid:] = jnp.zeros((EXTRA, payload.shape[1] - grid), bf16)
+    copies[0].wait()
 
 
 def encode_kernel(steps, first, last, halves, *refs):
@@ -218,15 +235,18 @@
         halo[at:, :] = jnp.zeros((halo.shape[0] - at, halo.shape[1]), bf16)
 
 
-def node_sum(pre, halos, halo_here, there, slope_out, halo, act_out):
+def node_sum(pre, halos, halo_here, there, slope_out, halo):
     nodes = there.shape[0] // 2
     stack_halo(halos, halo)
+    table = halo[...]
+    total = None
     for at in range(0, pre.shape[0], BLOCK):
         block = slice(at, at + BLOCK)
-        act, slope = gated(pre[block, :] + dot(halo_here[block, :], halo[...]))
+        act, slope = gated(pre[block, :] + dot(halo_here[block, :], table))
         slope_out[block, :] = slope.astype(bf16)
-        act_out[block, :] = act.astype(bf16)
-    return dot(there[nodes:, :], act_out[...])
+        added = dot(there[nodes:, block], act.astype(bf16))
+        total = added if total is None else total + added
+    return total
 
 
 def layer_kernel(layer, shifts, *refs):
@@ -235,8 +255,7 @@
     halo_here, there, w_out, gain, w_send, list_here = refs[2 + shifts : 8 + shifts]
     hidden_out, agg_out, slope_out, sent_out = refs[8 + shifts : 12 + shifts]
     outs = refs[12 + shifts : 12 + 2 * shifts]
-    halo, act = refs[-2:]
-    total = node_sum(pre, halos, halo_here, there, slope_out, halo, act)
+    total = node_sum(pre, halos, halo_here, there, slope_out, refs[-1])
     agg = dot(total.astype(bf16), w_out[layer])
     agg_out[...] = agg
     fresh = (hidden[...].astype(f32) + agg * norm_scale(agg) * gain[layer : layer + 1, :]).astype(bf16)
@@ -249,11 +268,14 @@
 def edge_grads(grad_agg, w_out, here, halo_there, slope, grad_pre, outs):
     nodes = grad_agg.shape[0]
     spread = dot_back(grad_agg.astype(bf16), w_out).astype(bf16)
+    given = None
     for at in range(0, slope.shape[0], BLOCK):
         block = slice(at, at + BLOCK)
-        grad_act = dot(here[block, nodes:], spread)
-        grad_pre[block, :] = (grad_act * slope[block, :].astype(f32)).astype(bf16)
-    given = dot(halo_there[...], grad_pre[...]).astype(bf16)
+        grad = (dot(here[block, nodes:], spread) * slope[block, :].astype(f32)).astype(bf16)
+        grad_pre[block, :] = grad
+        added = dot(halo_there[:, block], grad)
+        given = added if given is None else given + added
+    given = given.astype(bf16)
     at = 0
     for out in outs:
         out[...] = given[at : at + out.shape[0]]
@@ -267,7 +289,7 @@
     hidden_out, grad_pre = refs[9 + shifts : 11 + shifts]
     outs = refs[11 + shifts : 11 + 2 * shifts]
     slope, halo = refs[-2:]
-    total = node_sum(pre, halos, halo_here, there, slope, halo, grad_pre)
+    total = node_sum(pre, halos, halo_here, there, slope, halo)
     agg = dot(total.astype(bf16), w_out[layer])
     gain_row = gain[layer : layer + 1, :]
     hidden_out[...] = (hidden[...].astype(f32) + agg * norm_scale(agg) * gain_row).astype(bf16)
@@ -306,25 +328,47 @@
     edge_grads(grad_agg, w_out[layer], here, halo_there, slope, grad_pre, outs)
 
 
-def finish_kernel(count, shifts, *refs):
+def pair_grads(spread, pick, slope):
+    return (dot(pick, spread) * slope.astype(f32)).astype(bf16)
+
+
+def finish_kernel(shifts, *refs):
     rest = refs[0]
     returned = refs[1 : 1 + shifts]
-    list_there, w_send, enc_sum, gain, w_enc_out = refs[1 + shifts : 6 + shifts]
-    picks, slopes = refs[6 + shifts : 6 + shifts + count], refs[6 + shifts + count : 6 + shifts + 2 * count]
-    outs = refs[6 + shifts + 2 * count : -1]
-    halo = refs[-1]
+    list_there, w_send, enc_sum, gain, w_enc_out, pick, slope = refs[1 + shifts : 8 + shifts]
+    spread_out, outs, halo = refs[8 + shifts], refs[9 + shifts : -1], refs[-1]
     upstream = arrived(rest, returned, list_there, w_send[0], halo)
     spread = dot_back(norm_back(enc_sum[...], gain[...], upstream).astype(bf16), w_enc_out[...]).astype(bf16)
+    spread_out[...] = spread
+    at = 0
+    for out in outs:
+        piece = slice(at, at + out.shape[0])
+        out[...] = pair_grads(spread, pick[piece, :], slope[piece, :])
+        at += out.shape[0]
+
+
+def others_kernel(count, *refs):
+    spread = refs[0][...]
+    picks, slopes, outs = refs[1 : 1 + count], refs[1 + count : 1 + 2 * count], refs[1 + 2 * count :]
     for pick, slope, out in zip(picks, slopes, outs):
-        out[...] = (dot(pick[...], spread) * slope[...].astype(f32)).astype(bf16)
-
-
-def grid_kernel(count, *refs):
-    blocks, w_grid, out = refs[:count], refs[count], refs[count + 1]
-    total = blocks[0][...].astype(f32)
-    for block in blocks[1:]:
-        total = total + block[...].astype(f32)
-    out[...] = dot_back(total.astype(bf16), w_grid[...])
+        out[...] = pair_grads(spread, pick[...], slope[...])
+
+
+def relay_kernel(first, count, own, passed, held, *refs):
+    rows = passed.shape[0]
+    refs[0][...] = (own[first : first + rows, :].astype(f32) + passed[...].astype(f32)).astype(bf16)
+    if count > 1:
+        refs[1][...] = held[...]
+
+
+def grid_kernel(whole, *refs):
+    blocks, pieces, w_grid, out = refs[:whole], refs[whole:-2], refs[-2], refs[-1]
+    step = out.shape[0] // max(len(pieces), 1)
+    for at in range(0, out.shape[0], step):
+        total = pieces[at // step][...].astype(f32) if pieces else 0.0
+        for block in blocks:
+            total = total + block[at : at + step, :].astype(f32)
+        out[at : at + step, :] = dot_back(total.astype(bf16), w_grid[...])
 
 
 def shifted(value, axis, by):
@@ -332,8 +376,18 @@
     return lax.ppermute(value, axis, [(at, (at + by) % size) for at in range(size)])
 
 
-def swapped(value, by):
-    return lax.ppermute(value, "mesh", [(at, at ^ by) for at in range(lax.axis_size("mesh"))])
+def partner(at, step, size):
+    return at ^ step if size & (size - 1) == 0 else (at + step) % size
+
+
+def sent_to(value, step):
+    size = lax.axis_size("mesh")
+    return lax.ppermute(value, "mesh", [(at, partner(at, step, size)) for at in range(size)])
+
+
+def sent_back(value, step):
+    size = lax.axis_size("mesh")
+    return lax.ppermute(value, "mesh", [(partner(at, step, size), at) for at in range(size)])
 
 
 def in_order(pieces, axis):
@@ -372,21 +426,26 @@
     all_edges = edges * halves * feats
     enc_gain = enc_gain[None, :]
 
-    (payload,) = call(note_kernel, [((grid + EXTRA, width), bf16)])(grid_feats, g2m_shard.T, g2m_node.T)
+    (payload,) = call(
+        note_kernel, [((grid + EXTRA, width), bf16)], [((tops, grid), i32), ((tops, grid), i32)], copied=True
+    )(*(pltpu.with_memory_space_constraint(array, pltpu.HBM) for array in (grid_feats, g2m_shard.T, g2m_node.T)))
     if shards == 4:
-        across = swapped(payload, 2)
-        payloads = [payload, swapped(payload, 1), across, swapped(across, 1)]
+        across = sent_to(payload, 2)
+        payloads = [payload, sent_to(payload, 1), across]
     else:
-        payloads = [payload] + [shifted(payload, "mesh", step) for step in range(1, shards)]
+        payloads = [payload] + [sent_to(payload, step) for step in range(1, shards)]
 
     place = sender_slots - nodes
-    away = lax.rem(shard - place // depth + shards, shards)
+    away = partner(shard, place // depth, shards)
+    if shards & (shards - 1):
+        away = lax.rem(shard - place // depth + shards, shards)
     slots = jnp.where(sender_slots < nodes, sender_slots, nodes + (away - 1) * depth + place % depth)
     both = jnp.stack([slots, receivers])
     both = in_order([both] + [shifted(both, "rep", step) for step in range(1, halves)], "rep")
     both = in_order([both] + [shifted(both, "feat", step) for step in range(1, feats)], "feat")
     both = both.reshape(feats * halves, 2, edges)
-    lists = jnp.roll(halo_index[0], -shard, axis=0)[1:].reshape(1, -1)
+    readers = partner(shard, jnp.arange(1, shards, dtype=i32), shards)
+    lists = jnp.take(halo_index[0], readers, axis=0).reshape(1, -1)
     here, there, halo_here, halo_there, list_here, list_there = call(
         place_kernel,
         [
@@ -397,11 +456,17 @@
             ((listed_rows, nodes), bf16),
             ((nodes, listed_rows), bf16),
         ],
+        products=[(all_edges, nodes, width), (all_edges, 2 * nodes, width)],
     )(both[:, 0].reshape(1, -1), both[:, 1].reshape(1, -1), lists)
+
+    if shards == 4:
+        across, list_here = lax.optimization_barrier((across, list_here))
+        payloads.append(sent_to(across, 1))
 
     meta = jnp.stack([lax.axis_index("rep"), shard]).astype(i32)
     node_f32, node_bf16 = ((nodes, width), f32), ((nodes, width), bf16)
     row_shape, half = ((grid, width), bf16), nodes // halves
+    square = (nodes, width, width)
     enc_picks, enc_slopes = [], []
     base, total = mesh_init, None
     groups = [payloads[:2]] + [payloads[at : at + 1] for at in range(2, shards)]
@@ -412,7 +477,12 @@
         outs += [node_bf16] if first else []
         outs += [((half, width), f32)] + [((half, width), bf16)] * (halves - 1) if last else [node_f32]
         got = list(
-            call(functools.partial(encode_kernel, count, first, last, halves), outs, [node_f32] if last else [])(
+            call(
+                functools.partial(encode_kernel, count, first, last, halves),
+                outs,
+                [node_f32] if last else [],
+                [square] * first + [(grid, width, width), (grid, nodes, width), (nodes, grid, width)] * count,
+            )(
                 meta, base, w_enc_grid, *((w_enc_mesh, list_here) if first else (total,)), *group
             )
         )
@@ -434,51 +504,80 @@
 
     listed = [((depth, width), bf16)] * shifts
     hidden, enc_sum, sent, *outgoing = call(
-        functools.partial(start_kernel, halves, shifts), [node_bf16, node_f32, node_bf16] + listed, [node_bf16]
+        functools.partial(start_kernel, halves, shifts), [node_bf16, node_f32, node_bf16] + listed, [node_bf16],
+        [square, square, (listed_rows, nodes, width)],
     )(meta, *parts, mesh_init, w_enc_out, enc_gain, w_send, list_here)
 
     edge_f32, edge_bf16 = ((all_edges, width), f32), ((all_edges, width), bf16)
     halo, back_halo = ((wide, width), bf16), ((listed_rows, width), bf16)
 
+    forward_products = [(all_edges, wide, width), (nodes, all_edges, width), square]
+    backward_products = [square, (all_edges, nodes, width), (wide, all_edges, width)]
+
     def local(layer):
-        (pre,) = call(functools.partial(local_kernel, layer), [edge_f32], [((2 * nodes, width), bf16)])(
+        (pre,) = call(functools.partial(local_kernel, layer), [edge_f32], [((2 * nodes, width), bf16)], [square, (all_edges, 2 * nodes, width)])(
             hidden, sent, here, w_recv
         )
         return pre
 
     records = []
     for layer in range(LAYERS - 1):
-        halos = [shifted(block, "mesh", step + 1) for step, block in enumerate(outgoing)]
+        halos = [sent_to(block, step + 1) for step, block in enumerate(outgoing)]
         hidden, agg, slope, sent, *outgoing = call(
             functools.partial(layer_kernel, layer, shifts),
             [node_bf16, node_f32, edge_bf16, node_bf16] + listed,
-            [halo, edge_bf16],
+            [halo],
+            forward_products + [square, (listed_rows, nodes, width)],
         )(hidden, local(layer), *halos, halo_here, there, w_out, layer_gain, w_send, list_here)
         records.append((agg, slope))
     last = LAYERS - 1
-    halos = [shifted(block, "mesh", step + 1) for step, block in enumerate(outgoing)]
+    halos = [sent_to(block, step + 1) for step, block in enumerate(outgoing)]
     final_mesh, grad_pre, *outgoing = call(
-        functools.partial(turn_kernel, last, shifts), [node_bf16, edge_bf16] + listed, [edge_bf16, halo]
+        functools.partial(turn_kernel, last, shifts), [node_bf16, edge_bf16] + listed, [edge_bf16, halo],
+        forward_products + backward_products,
     )(hidden, local(last), *halos, halo_here, there, w_out, layer_gain, here, halo_there, out_cot)
     upstream = out_cot
     for layer in reversed(range(LAYERS)):
-        returned = [shifted(block, "mesh", -step - 1) for step, block in enumerate(outgoing)]
-        (rest,) = call(functools.partial(rest_kernel, layer), [node_f32])(upstream, grad_pre, there, w_send, w_recv)
+        returned = [sent_back(block, step + 1) for step, block in enumerate(outgoing)]
+        (rest,) = call(
+            functools.partial(rest_kernel, layer), [node_f32], (), [(2 * nodes, all_edges, width), square, square]
+        )(upstream, grad_pre, there, w_send, w_recv)
         if layer:
             agg, slope = records[layer - 1]
             upstream, grad_pre, *outgoing = call(
-                functools.partial(back_kernel, layer - 1, shifts), [node_f32, edge_bf16] + listed, [back_halo]
+                functools.partial(back_kernel, layer - 1, shifts), [node_f32, edge_bf16] + listed, [back_halo],
+                backward_products + [(listed_rows, width, width), (nodes, listed_rows, width)],
             )(rest, *returned, list_there, w_send, agg, slope, layer_gain, w_out, here, halo_there)
-    blocks = call(functools.partial(finish_kernel, shards, shifts), [row_shape] * shards, [back_halo])(
-        rest, *returned, list_there, w_send, enc_sum, enc_gain, w_enc_out, *enc_picks, *enc_slopes
-    )
-    if shards == 4:
-        passed = swapped(blocks[3], 1)
-        near = swapped(blocks[1], 1)
-        blocks = [blocks[0], near, swapped((blocks[2].astype(f32) + passed.astype(f32)).astype(bf16), 2)]
+    relayed = shards == 4
+    pieces = 2 if relayed else 1
+    piece = ((grid // pieces, width), bf16)
+    one = (grid, nodes, width)
+    spread, *far = call(
+        functools.partial(finish_kernel, shifts),
+        [node_bf16] + [piece] * pieces,
+        [back_halo],
+        [square, (listed_rows, width, width), (nodes, listed_rows, width), one],
+    )(rest, *returned, list_there, w_send, enc_sum, enc_gain, w_enc_out, enc_picks[-1], enc_slopes[-1])
+    if relayed:
+        passed = [sent_back(block, 1) for block in far]
+    blocks = call(
+        functools.partial(others_kernel, shards - 1), [row_shape] * (shards - 1), products=[one] * (shards - 1)
+    )(spread, *enc_picks[:-1], *enc_slopes[:-1])
+    if relayed:
+        summed, near = [], blocks[1]
+        for at, block in enumerate(passed):
+            last = at == pieces - 1
+            got = call(
+                functools.partial(relay_kernel, at * piece[0][0], 1 + last), [piece] + [row_shape] * last
+            )(blocks[2], block, blocks[1])
+            summed.append(sent_back(got[0], 2))
+        parts = [blocks[0], sent_back(got[1], 1)], summed
     else:
-        blocks = [blocks[0]] + [shifted(block, "mesh", -step) for step, block in enumerate(blocks) if step]
-    (grid_grad,) = call(functools.partial(grid_kernel, len(blocks)), [((grid, width), f32)])(*blocks, w_enc_grid)
+        blocks = [*blocks, far[0]]
+        parts = [blocks[0]] + [sent_back(block, step) for step, block in enumerate(blocks) if step], []
+    (grid_grad,) = call(
+        functools.partial(grid_kernel, len(parts[0])), [((grid, width), f32)], products=[(grid, width, width)]
+    )(*parts[0], *parts[1], w_enc_grid)
     return (final_mesh, grid_grad)
 
 

time: 132 us -> 130 us (0.985)
  waiting for transfers between devices: 40.6 us -> 34.2 us
  starting transfers between devices: 34.9 us -> 41.2 us
  local copies, waits for them, and re-layouts: 5.83 us -> 0.9 us
  Pallas kernels: 46.9 us -> 50.8 us
    ppermute x6 -> x26, starting transfers between devices: 8.46 us -> 38 us  [the longest x12 19.5 us: sent_to(): lax.ppermute(value, 'mesh', [(at, partner(at, step, size)) for at in rang...]
    ppermute x23 -> x5, starting transfers between devices: 26.5 us -> 3.25 us  [shifted(): lax.ppermute(value, axis, [(at, (at + by) % size) for at in range(size)])]
    ppermute x23 -> x5, waiting for transfers between devices: 19.7 us -> 12.4 us  [shifted(): lax.ppermute(value, axis, [(at, (at + by) % size) for at in range(size)])]
    unnamed x33 -> x25, local copies, waits for them, and re-layouts: 5.55 us -> 0.08 us
    pallas_call x19 -> x22, Pallas kernels: 46.9 us -> 50.8 us  [run(): pl.pallas_call(body, out_shape=tuple((jax.ShapeDtypeStruct(shape, dtype)...]
    ppermute x6 -> x26, waiting for transfers between devices: 20.8 us -> 21.8 us  [the longest x14 13 us: sent_back(): lax.ppermute(value, 'mesh', [(partner(at, step, size), at) for at in rang...]
  transfers between devices with their start and end apart: 29 -> 31, of which waited for: 17 -> 16; matrix products, arithmetic and copies ran while one was open for 2% -> 2% of each run, Pallas kernels for 18% -> 19%
where the time goes in v3:
time: 130 us
  Pallas kernels  50.8 us (39%)
  starting transfers between devices  41.2 us (32%)
  waiting for transfers between devices  34.2 us (26%)
  other arithmetic  1.78 us (1%)
    pallas_call x22, Pallas kernels, run(): pl.pallas_call(body, out_shape=tuple((jax.ShapeDtypeStruct(shape, dtype)...  50.8 us
    ppermute x12, starting transfers between devices, sent_to(): lax.ppermute(value, 'mesh', [(at, partner(at, step, size)) for at in rang...  19.5 us
    ppermute x14, starting transfers between devices, sent_back(): lax.ppermute(value, 'mesh', [(partner(at, step, size), at) for at in rang...  18.5 us
    ppermute x14, waiting for transfers between devices, sent_back(): lax.ppermute(value, 'mesh', [(partner(at, step, size), at) for at in rang...  13 us
    ppermute x5, waiting for transfers between devices, shifted(): lax.ppermute(value, axis, [(at, (at + by) % size) for at in range(size)])  12.4 us
    ppermute x12, waiting for transfers between devices, sent_to(): lax.ppermute(value, 'mesh', [(at, partner(at, step, size)) for at in rang...  8.82 us
    ppermute x5, starting transfers between devices, shifted(): lax.ppermute(value, axis, [(at, (at + by) % size) for at in range(size)])  3.25 us
  transfers between devices with their start and end apart: 31, of which 16 were waited for; matrix products, arithmetic and copies ran while one was open for 2% of the time, Pallas kernels for 19%

profile of v3, /device:TPU:0, one launch (start us, length us, event | category | flops | bytes accessed | tf_op | source)
XLA Modules:
  0.0 130.0 jit_solution(14007316239211378143)
XLA Ops:
  0.6 1.0 shard_map.167.refs_5_
  1.6 3.1 %collective-permute-start.3 = (bf16[272,512]{1,0:T(8,128)(2,1)S(1)}, bf16[272,512]{1,0:T(8,128)(2,1)S(1)}, u32[]{:S(2)}, u32[]{:S(2)}) collective-permute-start(bf16[272,512]{1,0:T(8,128)(2,1)S(1)} %shard_map.167.refs_5_), channel_id=1, source_target_pairs={{0,4},{4,0},{8,12},{12,8},{1,5},{5,1},{9,13},{13,9},{2,6},{6,2},{1... | collective-permute-start | bytes 835592 | tf_op jit(solution)/shard_map/ppermute | solution.py:385
  4.7 2.6 %collective-permute-start = (bf16[272,512]{1,0:T(8,128)(2,1)S(1)}, bf16[272,512]{1,0:T(8,128)(2,1)S(1)}, u32[]{:S(2)}, u32[]{:S(2)}) collective-permute-start(bf16[272,512]{1,0:T(8,128)(2,1)S(1)} %shard_map.167.refs_5_), channel_id=1, source_target_pairs={{0,8},{4,12},{8,0},{12,4},{1,9},{5,13},{9,1},{13,5},{2,10},{6,14},... | collective-permute-start | bytes 835592 | tf_op jit(solution)/shard_map/ppermute | solution.py:385
  7.3 0.7 compare_select_fusion
  8.0 0.7 fusion.10
  8.8 0.6 gather_fusion
  9.3 0.1 broadcast_select_fusion
  9.4 0.1 select_n.77.order
  9.5 0.4 collective-permute-done.1
  9.9 0.1 rev.6
  10.1 1.6 %collective-permute-start.2 = (s32[2,2,512]{2,0,1:T(2,128)S(1)}, s32[2,2,512]{2,0,1:T(2,128)S(1)}, u32[]{:S(2)}, u32[]{:S(2)}) collective-permute-start(s32[2,2,512]{2,0,1:T(2,128)S(1)} %fusion.1), channel_id=1, source_target_pairs={{0,2},{2,0},{1,3},{3,1},{4,6},{6,4},{5,7},{7,5},{8,10},{10,8},{9,1... | collective-permute-start | bytes 24584 | tf_op jit(solution)/shard_map/ppermute | solution.py:376
  11.7 2.1 %collective-permute-done.2 = s32[2,2,512]{2,0,1:T(2,128)S(1)} collective-permute-done((s32[2,2,512]{2,0,1:T(2,128)S(1)}, s32[2,2,512]{2,0,1:T(2,128)S(1)}, u32[]{:S(2)}, u32[]{:S(2)}) %collective-permute-start.2) | collective-permute-done | bytes 8224 | tf_op jit(solution)/shard_map/ppermute | solution.py:376
  13.9 3.5 %shard_map.168 = (bf16[2048,1024]{1,0:T(8,128)(2,1)S(1)}, bf16[1024,2048]{1,0:T(8,128)(2,1)S(1)}, bf16[2048,128]{1,0:T(8,128)(2,1)S(1)}, bf16[128,2048]{1,0:T(8,...) custom-call(s32[1,2048]{1,0:T(1,128)S(1)} %bitcast.29, s32[1,2048]{1,0:T(1,128)S(1)} %bitcast.28, ...), custom_call_target="tpu_custom_call" | custom-call | flops 3221225472 | bytes 9650560 | tf_op jit(solution)/shard_map/pallas_call | solution.py:82
  17.4 2.3 %collective-permute-done.refs_4_ = bf16[272,512]{1,0:T(8,128)(2,1)S(1)} collective-permute-done((bf16[272,512]{1,0:T(8,128)(2,1)S(1)}, bf16[272,512]{1,0:T(8,128)(2,1)S(1)}, u32[]{:S(2)}, u32[]{:S(2)}) %collective-permute-start) | collective-permute-done | bytes 278560 | tf_op jit(solution)/shard_map/ppermute | solution.py:385
  19.8 0.4 collective-permute-start.4
  20.2 0.1 pad_add_fusion.3.refs_0_
  20.3 2.2 %shard_map.169 = (bf16[256,512]{1,0:T(8,128)(2,1)S(1)}, bf16[256,512]{1,0:T(8,128)(2,1)S(1)}, bf16[256,512]{1,0:T(8,128)(2,1)S(1)}, bf16[256,512]{1,0:T(8,128)(2...) custom-call(s32[2]{0:T(128)S(1)} %pad_add_fusion.3.refs_0_, bf16[512,512]{1,0:T(8,128)(2,1)S(1)} %copy-done.7, ...), custom_call_target="tpu_custom_call" | custom-call | flops 1073741824 | bytes 4849672 | tf_op jit(solution)/shard_map/pallas_call | solution.py:82
  22.5 1.4 %shard_map.170 = (bf16[256,512]{1,0:T(8,128)(2,1)S(1)}, bf16[256,512]{1,0:T(8,128)(2,1)S(1)}, f32[512,512]{1,0:T(8,128)S(1)}) custom-call(s32[2]{0:T(128)S(1)} %pad_add_fusion.3.refs_0_, bf16[512,512]{1,0:T(8,128)(2,1)S(1)} %get-tuple-element.68.refs_1_, bf16[512,512]{1,0:T(8,128)(2,1)S(1)} %copy-done.4, f32[512,512]{1,0:T(8,128)S(1)} %get-tuple-element.69.refs_3_, ...), custom_call_target="tpu_custom_call" | custom-call | flops 402653184 | bytes 3948552 | tf_op jit(solution)/shard_map/pallas_call | solution.py:82
  24.0 2.3 %collective-permute-done.4.refs_4_ = bf16[272,512]{1,0:T(8,128)(2,1)S(1)} collective-permute-done((bf16[272,512]{1,0:T(8,128)(2,1)S(1)}, bf16[272,512]{1,0:T(8,128)(2,1)S(1)}, u32[]{:S(2)}, u32[]{:S(2)}) %collective-permute-start.4) | collective-permute-done | bytes 278560 | tf_op jit(solution)/shard_map/ppermute | solution.py:385
  26.3 1.6 %shard_map.171 = (bf16[256,512]{1,0:T(8,128)(2,1)S(1)}, bf16[256,512]{1,0:T(8,128)(2,1)S(1)}, f32[256,512]{1,0:T(8,128)S(1)}, bf16[256,512]{1,0:T(8,128)(2,1)S(1)}) custom-call(s32[2]{0:T(128)S(1)} %pad_add_fusion.3.refs_0_, bf16[512,512]{1,0:T(8,128)(2,1)S(1)} %get-tuple-element.68.refs_1_, bf16[512,512]{1,0:T(8,128)(2,1)S(1)} %copy-done.4, ...), custom_call_target="tpu_custom_call" | custom-call | flops 402653184 | bytes 3686408 | tf_op jit(solution)/shard_map/pallas_call | solution.py:82
  28.0 1.5 %collective-permute-done.5 = bf16[256,512]{1,0:T(8,128)(2,1)S(1)} collective-permute-done((bf16[256,512]{1,0:T(8,128)(2,1)S(1)}, bf16[256,512]{1,0:T(8,128)(2,1)S(1)}, u32[]{:S(2)}, u32[]{:S(2)}) %collective-permute-start.5) | collective-permute-done | bytes 262176 | tf_op jit(solution)/shard_map/ppermute | solution.py:376
  29.6 1.6 %collective-permute-start.6 = (bf16[256,512]{1,0:T(8,128)(2,1)S(1)}, bf16[256,512]{1,0:T(8,128)(2,1)S(1)}, u32[]{:S(2)}, u32[]{:S(2)}) collective-permute-start(bf16[256,512]{1,0:T(8,128)(2,1)S(1)} %add_convert_fusion.1), channel_id=1, source_target_pairs={{0,2},{2,0},{1,3},{3,1},{4,6},{6,4},{5,7},{7,5},{8,10},{10,8},{9,1... | collective-permute-start | bytes 786440 | tf_op jit(solution)/shard_map/ppermute | solution.py:376
  31.1 6.9 %collective-permute-done.6 = bf16[256,512]{1,0:T(8,128)(2,1)S(1)} collective-permute-done((bf16[256,512]{1,0:T(8,128)(2,1)S(1)}, bf16[256,512]{1,0:T(8,128)(2,1)S(1)}, u32[]{:S(2)}, u32[]{:S(2)}) %collective-permute-start.6) | collective-permute-done | bytes 262176 | tf_op jit(solution)/shard_map/ppermute | solution.py:376
  38.2 1.5 %collective-permute-done.7.refs_2_ = bf16[256,512]{1,0:T(8,128)(2,1)S(1)} collective-permute-done((bf16[256,512]{1,0:T(8,128)(2,1)S(1)}, bf16[256,512]{1,0:T(8,128)(2,1)S(1)}, u32[]{:S(2)}, u32[]{:S(2)}) %collective-permute-start.7) | collective-permute-done | bytes 262176 | tf_op jit(solution)/shard_map/ppermute | solution.py:376
  39.7 1.6 %shard_map.172 = (bf16[512,512]{1,0:T(8,128)(2,1)S(1)}, f32[512,512]{1,0:T(8,128)S(1)}, bf16[512,512]{1,0:T(8,128)(2,1)S(1)}, bf16[32,512]{1,0:T(8,128)(2,1)S(1)...) custom-call(s32[2]{0:T(128)S(1)} %pad_add_fusion.3.refs_0_, bf16[256,512]{1,0:T(8,128)(2,1)S(1)} %add_convert_fusion.refs_1_, ...), custom_call_target="tpu_custom_call" | custom-call | flops 587202560 | bytes 5441544 | tf_op jit(solution)/shard_map/pallas_call | solution.py:82
  41.3 1.4 %collective-permute-start.8 = (bf16[32,512]{1,0:T(8,128)(2,1)S(1)}, bf16[32,512]{1,0:T(8,128)(2,1)S(1)}, u32[]{:S(2)}, u32[]{:S(2)}) collective-permute-start(bf16[32,512]{1,0:T(8,128)(2,1)S(1)} %get-tuple-element.77), channel_id=1, source_target_pairs={{0,4},{4,0},{8,12},{12,8},{1,5},{5,1},{9,13},{13,9},{2,6},{6,2},{1... | collective-permute-start | bytes 98312 | tf_op jit(solution)/shard_map/ppermute | solution.py:385
  42.7 1.8 %collective-permute-start.9 = (bf16[32,512]{1,0:T(8,128)(2,1)S(1)}, bf16[32,512]{1,0:T(8,128)(2,1)S(1)}, u32[]{:S(2)}, u32[]{:S(2)}) collective-permute-start(bf16[32,512]{1,0:T(8,128)(2,1)S(1)} %get-tuple-element.78), channel_id=1, source_target_pairs={{0,8},{4,12},{8,0},{12,4},{1,9},{5,13},{9,1},{13,5},{2,10},{6,14},... | collective-permute-start | bytes 98312 | tf_op jit(solution)/shard_map/ppermute | solution.py:385
  44.5 1.3 collective-permute-start.10
  45.7 2.6 %shard_map.173.refs_1_ = f32[2048,512]{1,0:T(8,128)S(1)} custom-call(bf16[512,512]{1,0:T(8,128)(2,1)S(1)} %get-tuple-element.74.hidden.refs_0_, bf16[512,512]{1,0:T(8,128)(2,1)S(1)} %get-tuple-element.75.sent, bf16[2048,1024]{1,0:T(8,128)(2,1)S(1)} %get-tuple-element.76.here.refs_9_.refs_10_, bf16[3,512,512]{2,1,0:T(8,128)(2,1)S(1)} %copy-done.2), custom_call_target="tpu_custom_call" | custom-call | flops 2415919104 | bytes 11010048 | tf_op jit(solution)/shard_map/pallas_call | solution.py:82
  48.3 1.8 %collective-permute-done.10.refs_4_ = bf16[32,512]{1,0:T(8,128)(2,1)S(1)} collective-permute-done((bf16[32,512]{1,0:T(8,128)(2,1)S(1)}, bf16[32,512]{1,0:T(8,128)(2,1)S(1)}, u32[]{:S(2)}, u32[]{:S(2)}) %collective-permute-start.10) | collective-permute-done | bytes 32800 | tf_op jit(solution)/shard_map/ppermute | solution.py:385
  50.2 3.6 %shard_map.174 = (bf16[512,512]{1,0:T(8,128)(2,1)S(1)}, f32[512,512]{1,0:T(8,128)S(1)}, bf16[2048,512]{1,0:T(8,128)(2,1)S(1)}, bf16[512,512]{1,0:T(8,128)(2,1)S(...) custom-call(bf16[512,512]{1,0:T(8,128)(2,1)S(1)} %get-tuple-element.74.hidden.refs_0_, ...), custom_call_target="tpu_custom_call" | custom-call | flops 1929379840 | bytes 17078272 | tf_op jit(solution)/shard_map/pallas_call | solution.py:82
  53.9 1.8 %collective-permute-start.12 = (bf16[32,512]{1,0:T(8,128)(2,1)S(1)}, bf16[32,512]{1,0:T(8,128)(2,1)S(1)}, u32[]{:S(2)}, u32[]{:S(2)}) collective-permute-start(bf16[32,512]{1,0:T(8,128)(2,1)S(1)} %get-tuple-element.85), channel_id=1, source_target_pairs={{0,8},{4,12},{8,0},{12,4},{1,9},{5,13},{9,1},{13,5},{2,10},{6,14},... | collective-permute-start | bytes 98312 | tf_op jit(solution)/shard_map/ppermute | solution.py:385
  55.7 2.6 %collective-permute-start.13 = (bf16[32,512]{1,0:T(8,128)(2,1)S(1)}, bf16[32,512]{1,0:T(8,128)(2,1)S(1)}, u32[]{:S(2)}, u32[]{:S(2)}) collective-permute-start(bf16[32,512]{1,0:T(8,128)(2,1)S(1)} %get-tuple-element.86), channel_id=1, source_target_pairs={{0,12},{4,8},{8,4},{12,0},{1,13},{5,9},{9,5},{13,1},{2,14},{6,10},... | collective-permute-start | bytes 98312 | tf_op jit(solution)/shard_map/ppermute | solution.py:385
  58.3 2.6 %shard_map.175.refs_1_ = f32[2048,512]{1,0:T(8,128)S(1)} custom-call(bf16[512,512]{1,0:T(8,128)(2,1)S(1)} %get-tuple-element.82.hidden.refs_0_, bf16[512,512]{1,0:T(8,128)(2,1)S(1)} %get-tuple-element.83.sent, bf16[2048,1024]{1,0:T(8,128)(2,1)S(1)} %get-tuple-element.76.here.refs_9_.refs_10_, bf16[3,512,512]{2,1,0:T(8,128)(2,1)S(1)} %copy-done.2), custom_call_target="tpu_custom_call" | custom-call | flops 2415919104 | bytes 11010048 | tf_op jit(solution)/shard_map/pallas_call | solution.py:82
  60.9 0.5 collective-permute-done.13.refs_4_
  61.4 3.9 %shard_map.176 = (bf16[512,512]{1,0:T(8,128)(2,1)S(1)}, f32[512,512]{1,0:T(8,128)S(1)}, bf16[2048,512]{1,0:T(8,128)(2,1)S(1)}, bf16[512,512]{1,0:T(8,128)(2,1)S(...) custom-call(bf16[512,512]{1,0:T(8,128)(2,1)S(1)} %get-tuple-element.82.hidden.refs_0_, ...), custom_call_target="tpu_custom_call" | custom-call | flops 1929379840 | bytes 17078272 | tf_op jit(solution)/shard_map/pallas_call | solution.py:82
  65.4 3.1 %collective-permute-start.15 = (bf16[32,512]{1,0:T(8,128)(2,1)S(1)}, bf16[32,512]{1,0:T(8,128)(2,1)S(1)}, u32[]{:S(2)}, u32[]{:S(2)}) collective-permute-start(bf16[32,512]{1,0:T(8,128)(2,1)S(1)} %get-tuple-element.90), channel_id=1, source_target_pairs={{0,8},{4,12},{8,0},{12,4},{1,9},{5,13},{9,1},{13,5},{2,10},{6,14},... | collective-permute-start | bytes 98312 | tf_op jit(solution)/shard_map/ppermute | solution.py:385
  68.5 1.3 collective-permute-start.16
  69.8 2.6 %shard_map.177.refs_1_ = f32[2048,512]{1,0:T(8,128)S(1)} custom-call(bf16[512,512]{1,0:T(8,128)(2,1)S(1)} %get-tuple-element.87.hidden.refs_0_, bf16[512,512]{1,0:T(8,128)(2,1)S(1)} %get-tuple-element.88.sent, bf16[2048,1024]{1,0:T(8,128)(2,1)S(1)} %get-tuple-element.76.here.refs_9_.refs_10_, bf16[3,512,512]{2,1,0:T(8,128)(2,1)S(1)} %copy-done.2), custom_call_target="tpu_custom_call" | custom-call | flops 2415919104 | bytes 11010048 | tf_op jit(solution)/shard_map/pallas_call | solution.py:82
  72.4 1.8 %collective-permute-done.16.refs_4_ = bf16[32,512]{1,0:T(8,128)(2,1)S(1)} collective-permute-done((bf16[32,512]{1,0:T(8,128)(2,1)S(1)}, bf16[32,512]{1,0:T(8,128)(2,1)S(1)}, u32[]{:S(2)}, u32[]{:S(2)}) %collective-permute-start.16) | collective-permute-done | bytes 32800 | tf_op jit(solution)/shard_map/ppermute | solution.py:385
  74.2 6.1 %shard_map.178 = (bf16[512,512]{1,0:T(8,128)(2,1)}, bf16[2048,512]{1,0:T(8,128)(2,1)S(1)}, bf16[32,512]{1,0:T(8,128)(2,1)S(1)}, bf16[32,512]{1,0:T(8,128)(2,1)S(1)}, bf16[32,512]{1,0:T(8,128)(2,1)S(1)}) custom-call(bf16[512,512]{1,0:T(8,128)(2,1)S(1)} %get-tuple-element.87.hidden.refs_0_, f32[2048,512]{1,0:T(8,128)S(1)} %shard_map.177.refs_1_, ...), custom_call_target="tpu_custom_call" | custom-call | flops 3221225472 | bytes 19077120 | tf_op jit(solution)/shard_map/pallas_call | solution.py:82
  80.4 1.8 %collective-permute-start.18 = (bf16[32,512]{1,0:T(8,128)(2,1)S(1)}, bf16[32,512]{1,0:T(8,128)(2,1)S(1)}, u32[]{:S(2)}, u32[]{:S(2)}) collective-permute-start(bf16[32,512]{1,0:T(8,128)(2,1)S(1)} %get-tuple-element.96), channel_id=1, source_target_pairs={{8,0},{12,4},{0,8},{4,12},{9,1},{13,5},{1,9},{5,13},{10,2},{14,6},... | collective-permute-start | bytes 98312 | tf_op jit(solution)/shard_map/ppermute | solution.py:390
  82.2 2.6 %collective-permute-start.19 = (bf16[32,512]{1,0:T(8,128)(2,1)S(1)}, bf16[32,512]{1,0:T(8,128)(2,1)S(1)}, u32[]{:S(2)}, u32[]{:S(2)}) collective-permute-start(bf16[32,512]{1,0:T(8,128)(2,1)S(1)} %get-tuple-element.97), channel_id=1, source_target_pairs={{12,0},{8,4},{4,8},{0,12},{13,1},{9,5},{5,9},{1,13},{14,2},{10,6},... | collective-permute-start | bytes 98312 | tf_op jit(solution)/shard_map/ppermute | solution.py:390
  84.7 2.9 %shard_map.179.refs_0_ = f32[512,512]{1,0:T(8,128)S(1)} custom-call(bf16[512,512]{1,0:T(8,128)(2,1)S(1)} %copy-done.6, bf16[2048,512]{1,0:T(8,128)(2,1)S(1)} %get-tuple-element.94.grad_pre, bf16[1024,2048]{1,0:T(8,128)(2,1)S(1)} %get-tuple-element.81.refs_6_.there, bf16[3,512,512]{2,1,0:T(8,128)(2,1)S(1)} %copy-done.1, bf16[3,512,512]{2,1,0:T(8,128)(2,1)S(1)} %copy-done.2), custom_call_target="tpu_custom_call" | custom-call | flops 2684354560 | bytes 11010048 | tf_op jit(solution)/shard_map/pallas_call | solution.py:82
  87.6 0.4 collective-permute-done.19.refs_3_
  88.1 3.0 %shard_map.180 = (f32[512,512]{1,0:T(8,128)S(1)}, bf16[2048,512]{1,0:T(8,128)(2,1)S(1)}, bf16[32,512]{1,0:T(8,128)(2,1)S(1)}, bf16[32,512]{1,0:T(8,128)(2,1)S(1)}, bf16[32,512]{1,0:T(8,128)(2,1)S(1)}) custom-call(f32[512,512]{1,0:T(8,128)S(1)} %shard_map.179.refs_0_, bf16[32,512]{1,0:T(8,128)(2,1)S(1)} %collective-permute-done.17.refs_1_, ...), custom_call_target="tpu_custom_call" | custom-call | flops 1711276032 | bytes 15505408 | tf_op jit(solution)/shard_map/pallas_call | solution.py:82
  91.1 3.0 %collective-permute-start.21 = (bf16[32,512]{1,0:T(8,128)(2,1)S(1)}, bf16[32,512]{1,0:T(8,128)(2,1)S(1)}, u32[]{:S(2)}, u32[]{:S(2)}) collective-permute-start(bf16[32,512]{1,0:T(8,128)(2,1)S(1)} %get-tuple-element.104), channel_id=1, source_target_pairs={{8,0},{12,4},{0,8},{4,12},{9,1},{13,5},{1,9},{5,13},{10,2},{14,6},... | collective-permute-start | bytes 98312 | tf_op jit(solution)/shard_map/ppermute | solution.py:390
  94.0 1.4 %collective-permute-start.22 = (bf16[32,512]{1,0:T(8,128)(2,1)S(1)}, bf16[32,512]{1,0:T(8,128)(2,1)S(1)}, u32[]{:S(2)}, u32[]{:S(2)}) collective-permute-start(bf16[32,512]{1,0:T(8,128)(2,1)S(1)} %get-tuple-element.105), channel_id=1, source_target_pairs={{12,0},{8,4},{4,8},{0,12},{13,1},{9,5},{5,9},{1,13},{14,2},{10,6},... | collective-permute-start | bytes 98312 | tf_op jit(solution)/shard_map/ppermute | solution.py:390
  95.5 3.1 %shard_map.181.refs_0_ = f32[512,512]{1,0:T(8,128)S(1)} custom-call(f32[512,512]{1,0:T(8,128)S(1)} %get-tuple-element.101.upstream, bf16[2048,512]{1,0:T(8,128)(2,1)S(1)} %get-tuple-element.102.grad_pre, bf16[1024,2048]{1,0:T(8,128)(2,1)S(1)} %get-tuple-element.81.refs_6_.there, bf16[3,512,512]{2,1,0:T(8,128)(2,1)S(1)} %copy-done.1, ...), custom_call_target="tpu_custom_call" | custom-call | flops 2684354560 | bytes 11534336 | tf_op jit(solution)/shard_map/pallas_call | solution.py:82
  98.6 1.4 %collective-permute-done.22.refs_3_ = bf16[32,512]{1,0:T(8,128)(2,1)S(1)} collective-permute-done((bf16[32,512]{1,0:T(8,128)(2,1)S(1)}, bf16[32,512]{1,0:T(8,128)(2,1)S(1)}, u32[]{:S(2)}, u32[]{:S(2)}) %collective-permute-start.22) | collective-permute-done | bytes 32800 | tf_op jit(solution)/shard_map/ppermute | solution.py:390
  100.0 2.9 %shard_map.182 = (f32[512,512]{1,0:T(8,128)S(1)}, bf16[2048,512]{1,0:T(8,128)(2,1)S(1)}, bf16[32,512]{1,0:T(8,128)(2,1)S(1)}, bf16[32,512]{1,0:T(8,128)(2,1)S(1)}, bf16[32,512]{1,0:T(8,128)(2,1)S(1)}) custom-call(f32[512,512]{1,0:T(8,128)S(1)} %shard_map.181.refs_0_, bf16[32,512]{1,0:T(8,128)(2,1)S(1)} %collective-permute-done.20.refs_1_, ...), custom_call_target="tpu_custom_call" | custom-call | flops 1711276032 | bytes 15505408 | tf_op jit(solution)/shard_map/pallas_call | solution.py:82
  103.0 1.8 %collective-permute-start.24 = (bf16[32,512]{1,0:T(8,128)(2,1)S(1)}, bf16[32,512]{1,0:T(8,128)(2,1)S(1)}, u32[]{:S(2)}, u32[]{:S(2)}) collective-permute-start(bf16[32,512]{1,0:T(8,128)(2,1)S(1)} %get-tuple-element.111), channel_id=1, source_target_pairs={{8,0},{12,4},{0,8},{4,12},{9,1},{13,5},{1,9},{5,13},{10,2},{14,6},... | collective-permute-start | bytes 98312 | tf_op jit(solution)/shard_map/ppermute | solution.py:390
  104.9 2.5 %collective-permute-start.25 = (bf16[32,512]{1,0:T(8,128)(2,1)S(1)}, bf16[32,512]{1,0:T(8,128)(2,1)S(1)}, u32[]{:S(2)}, u32[]{:S(2)}) collective-permute-start(bf16[32,512]{1,0:T(8,128)(2,1)S(1)} %get-tuple-element.112), channel_id=1, source_target_pairs={{12,0},{8,4},{4,8},{0,12},{13,1},{9,5},{5,9},{1,13},{14,2},{10,6},... | collective-permute-start | bytes 98312 | tf_op jit(solution)/shard_map/ppermute | solution.py:390
  107.4 2.9 %shard_map.183.refs_0_ = f32[512,512]{1,0:T(8,128)S(1)} custom-call(f32[512,512]{1,0:T(8,128)S(1)} %get-tuple-element.108.upstream, bf16[2048,512]{1,0:T(8,128)(2,1)S(1)} %get-tuple-element.109.grad_pre, bf16[1024,2048]{1,0:T(8,128)(2,1)S(1)} %get-tuple-element.81.refs_6_.there, bf16[3,512,512]{2,1,0:T(8,128)(2,1)S(1)} %copy-done.1, ...), custom_call_target="tpu_custom_call" | custom-call | flops 2684354560 | bytes 11534336 | tf_op jit(solution)/shard_map/pallas_call | solution.py:82
  110.3 0.6 collective-permute-done.25.refs_3_
  110.9 1.4 %shard_map.184 = (bf16[512,512]{1,0:T(8,128)(2,1)S(1)}, bf16[128,512]{1,0:T(8,128)(2,1)S(1)}, bf16[128,512]{1,0:T(8,128)(2,1)S(1)}) custom-call(f32[512,512]{1,0:T(8,128)S(1)} %shard_map.183.refs_0_, bf16[32,512]{1,0:T(8,128)(2,1)S(1)} %collective-permute-done.23.refs_1_, bf16[32,512]{1,0:T(8,128)(2,1)S(1)} %collective-permute-done.24.refs_2_, ...), custom_call_target="tpu_custom_call" | custom-call | flops 503316480 | bytes 5703680 | tf_op jit(solution)/shard_map/pallas_call | solution.py:82
  112.4 2.0 %collective-permute-start.28 = (bf16[128,512]{1,0:T(8,128)(2,1)S(1)}, bf16[128,512]{1,0:T(8,128)(2,1)S(1)}, u32[]{:S(2)}, u32[]{:S(2)}) collective-permute-start(bf16[128,512]{1,0:T(8,128)(2,1)S(1)} %get-tuple-element.128), channel_id=1, source_target_pairs={{4,0},{0,4},{12,8},{8,12},{5,1},{1,5},{13,9},{9,13},{6,2},{2,6},{1... | collective-permute-start | bytes 393224 | tf_op jit(solution)/shard_map/ppermute | solution.py:390
  114.4 0.6 shard_map.185
  115.0 3.0 %collective-permute-done.26.passed = bf16[128,512]{1,0:T(8,128)(2,1)S(1)} collective-permute-done((bf16[128,512]{1,0:T(8,128)(2,1)S(1)}, bf16[128,512]{1,0:T(8,128)(2,1)S(1)}, u32[]{:S(2)}, u32[]{:S(2)}) %collective-permute-start.26) | collective-permute-done | bytes 131104 | tf_op jit(solution)/shard_map/ppermute | solution.py:390
  118.1 2.6 %collective-permute-start.30 = (bf16[128,512]{1,0:T(8,128)(2,1)S(1)}, bf16[128,512]{1,0:T(8,128)(2,1)S(1)}, u32[]{:S(2)}, u32[]{:S(2)}) collective-permute-start(bf16[128,512]{1,0:T(8,128)(2,1)S(1)} %get-tuple-element.129), channel_id=1, source_target_pairs={{8,0},{12,4},{0,8},{4,12},{9,1},{13,5},{1,9},{5,13},{10,2},{14,6},... | collective-permute-start | bytes 393224 | tf_op jit(solution)/shard_map/ppermute | solution.py:390
  120.7 0.5 collective-permute-start.29
  121.2 2.9 %collective-permute-done.30.refs_3_ = bf16[128,512]{1,0:T(8,128)(2,1)S(1)} collective-permute-done((bf16[128,512]{1,0:T(8,128)(2,1)S(1)}, bf16[128,512]{1,0:T(8,128)(2,1)S(1)}, u32[]{:S(2)}, u32[]{:S(2)}) %collective-permute-start.30) | collective-permute-done | bytes 131104 | tf_op jit(solution)/shard_map/ppermute | solution.py:390
  124.1 4.6 %collective-permute-done.29.refs_2_ = bf16[128,512]{1,0:T(8,128)(2,1)S(1)} collective-permute-done((bf16[128,512]{1,0:T(8,128)(2,1)S(1)}, bf16[128,512]{1,0:T(8,128)(2,1)S(1)}, u32[]{:S(2)}, u32[]{:S(2)}) %collective-permute-start.29) | collective-permute-done | bytes 131104 | tf_op jit(solution)/shard_map/ppermute | solution.py:390
  128.7 1.3 shard_map.188
  (66 shorter events, 1.0 us)
Async XLA Ops:
  0.6 8.1 %copy-start = (s32[1,4,32]{2,1,0:T(4,128)S(1)}, s32[1,4,32]{2,1,0:T(4,128)}, u32[]{:S(2)}) copy-start(s32[1,4,32]{2,1,0:T(4,128)} %param.22) | copy-start | bytes 1540
  1.6 18.6 %collective-permute-start.3 = (bf16[272,512]{1,0:T(8,128)(2,1)S(1)}, bf16[272,512]{1,0:T(8,128)(2,1)S(1)}, u32[]{:S(2)}, u32[]{:S(2)}) collective-permute-start(bf16[272,512]{1,0:T(8,128)(2,1)S(1)} %shard_map.167.refs_5_), channel_id=1, source_target_pairs={{0,4},{4,0},{8,12},{12,8},{1,5},{5,1},{9,13},{13,9},{2,6},{6,2},{1... | collective-permute-start | bytes 835592 | tf_op jit(solution)/shard_map/ppermute | solution.py:385
  4.7 15.0 %collective-permute-start = (bf16[272,512]{1,0:T(8,128)(2,1)S(1)}, bf16[272,512]{1,0:T(8,128)(2,1)S(1)}, u32[]{:S(2)}, u32[]{:S(2)}) collective-permute-start(bf16[272,512]{1,0:T(8,128)(2,1)S(1)} %shard_map.167.refs_5_), channel_id=1, source_target_pairs={{0,8},{4,12},{8,0},{12,4},{1,9},{5,13},{9,1},{13,5},{2,10},{6,14},... | collective-permute-start | bytes 835592 | tf_op jit(solution)/shard_map/ppermute | solution.py:385
  8.7 1.2 collective-permute-start.1
  10.1 3.7 %collective-permute-start.2 = (s32[2,2,512]{2,0,1:T(2,128)S(1)}, s32[2,2,512]{2,0,1:T(2,128)S(1)}, u32[]{:S(2)}, u32[]{:S(2)}) collective-permute-start(s32[2,2,512]{2,0,1:T(2,128)S(1)} %fusion.1), channel_id=1, source_target_pairs={{0,2},{2,0},{1,3},{3,1},{4,6},{6,4},{5,7},{7,5},{8,10},{10,8},{9,1... | collective-permute-start | bytes 24584 | tf_op jit(solution)/shard_map/ppermute | solution.py:376
  13.9 6.4 %copy-start.4 = (bf16[512,512]{1,0:T(8,128)(2,1)S(1)}, bf16[512,512]{1,0:T(8,128)(2,1)}, u32[]{:S(2)}) copy-start(bf16[512,512]{1,0:T(8,128)(2,1)} %refs_4_.3) | copy-start | bytes 1572868
  13.9 6.4 %copy-start.7 = (bf16[512,512]{1,0:T(8,128)(2,1)S(1)}, bf16[512,512]{1,0:T(8,128)(2,1)}, u32[]{:S(2)}) copy-start(bf16[512,512]{1,0:T(8,128)(2,1)} %refs_3_.3) | copy-start | bytes 1572868
  13.9 6.4 %copy-start.10 = (bf16[512,512]{1,0:T(8,128)(2,1)S(1)}, bf16[512,512]{1,0:T(8,128)(2,1)}, u32[]{:S(2)}) copy-start(bf16[512,512]{1,0:T(8,128)(2,1)} %refs_3_.2) | copy-start | bytes 1572868
  19.8 6.5 %collective-permute-start.4 = (bf16[272,512]{1,0:T(8,128)(2,1)S(1)}, bf16[272,512]{1,0:T(8,128)(2,1)S(1)}, u32[]{:S(2)}, u32[]{:S(2)}) collective-permute-start(bf16[272,512]{1,0:T(8,128)(2,1)S(1)} %collective-permute-done.refs_4_), channel_id=1, source_target_pairs={{0,4},{4,0},{8,12},{12,8},{1,5},{5,1},{9,13},{13,9},{2,6},{6,2},{1... | collective-permute-start | bytes 835592 | tf_op jit(solution)/shard_map/ppermute | solution.py:385
  26.3 13.4 %copy-start.1 = (bf16[3,512,512]{2,1,0:T(8,128)(2,1)S(1)}, bf16[3,512,512]{2,1,0:T(8,128)(2,1)}, u32[]{:S(2)}) copy-start(bf16[3,512,512]{2,1,0:T(8,128)(2,1)} %refs_5_.5) | copy-start | bytes 4718596
  26.3 13.4 %copy-start.5 = (bf16[512,512]{1,0:T(8,128)(2,1)S(1)}, bf16[512,512]{1,0:T(8,128)(2,1)}, u32[]{:S(2)}) copy-start(bf16[512,512]{1,0:T(8,128)(2,1)} %refs_8_.11) | copy-start | bytes 1572868
  26.3 13.4 %copy-start.9 = (f32[512]{0:T(512)S(1)}, f32[512]{0:T(512)}, u32[]{:S(2)}) copy-start(f32[512]{0:T(512)} %param.26) | copy-start | bytes 6148
  27.9 1.6 %collective-permute-start.5 = (bf16[256,512]{1,0:T(8,128)(2,1)S(1)}, bf16[256,512]{1,0:T(8,128)(2,1)S(1)}, u32[]{:S(2)}, u32[]{:S(2)}) collective-permute-start(bf16[256,512]{1,0:T(8,128)(2,1)S(1)} %get-tuple-element.73), channel_id=1, source_target_pairs={{0,1},{1,0},{2,3},{3,2},{4,5},{5,4},{6,7},{7,6},{8,9},{9,8},{10,11... | collective-permute-start | bytes 786440 | tf_op jit(solution)/shard_map/ppermute | solution.py:376
  29.6 16.1 %copy-start.2 = (bf16[3,512,512]{2,1,0:T(8,128)(2,1)S(1)}, bf16[3,512,512]{2,1,0:T(8,128)(2,1)}, u32[]{:S(2)}) copy-start(bf16[3,512,512]{2,1,0:T(8,128)(2,1)} %w_recv.11) | copy-start | bytes 4718596
  29.6 8.4 %collective-permute-start.6 = (bf16[256,512]{1,0:T(8,128)(2,1)S(1)}, bf16[256,512]{1,0:T(8,128)(2,1)S(1)}, u32[]{:S(2)}, u32[]{:S(2)}) collective-permute-start(bf16[256,512]{1,0:T(8,128)(2,1)S(1)} %add_convert_fusion.1), channel_id=1, source_target_pairs={{0,2},{2,0},{1,3},{3,1},{4,6},{6,4},{5,7},{7,5},{8,10},{10,8},{9,1... | collective-permute-start | bytes 786440 | tf_op jit(solution)/shard_map/ppermute | solution.py:376
  38.1 1.6 %collective-permute-start.7 = (bf16[256,512]{1,0:T(8,128)(2,1)S(1)}, bf16[256,512]{1,0:T(8,128)(2,1)S(1)}, u32[]{:S(2)}, u32[]{:S(2)}) collective-permute-start(bf16[256,512]{1,0:T(8,128)(2,1)S(1)} %add_convert_fusion.refs_1_), channel_id=1, source_target_pairs={{0,1},{1,0},{2,3},{3,2},{4,5},{5,4},{6,7},{7,6},{8,9},{9,8},{10,11... | collective-permute-start | bytes 786440 | tf_op jit(solution)/shard_map/ppermute | solution.py:376
  41.3 7.1 %collective-permute-start.8 = (bf16[32,512]{1,0:T(8,128)(2,1)S(1)}, bf16[32,512]{1,0:T(8,128)(2,1)S(1)}, u32[]{:S(2)}, u32[]{:S(2)}) collective-permute-start(bf16[32,512]{1,0:T(8,128)(2,1)S(1)} %get-tuple-element.77), channel_id=1, source_target_pairs={{0,4},{4,0},{8,12},{12,8},{1,5},{5,1},{9,13},{13,9},{2,6},{6,2},{1... | collective-permute-start | bytes 98312 | tf_op jit(solution)/shard_map/ppermute | solution.py:385
  42.7 5.7 %collective-permute-start.9 = (bf16[32,512]{1,0:T(8,128)(2,1)S(1)}, bf16[32,512]{1,0:T(8,128)(2,1)S(1)}, u32[]{:S(2)}, u32[]{:S(2)}) collective-permute-start(bf16[32,512]{1,0:T(8,128)(2,1)S(1)} %get-tuple-element.78), channel_id=1, source_target_pairs={{0,8},{4,12},{8,0},{12,4},{1,9},{5,13},{9,1},{13,5},{2,10},{6,14},... | collective-permute-start | bytes 98312 | tf_op jit(solution)/shard_map/ppermute | solution.py:385
  44.5 5.7 %collective-permute-start.10 = (bf16[32,512]{1,0:T(8,128)(2,1)S(1)}, bf16[32,512]{1,0:T(8,128)(2,1)S(1)}, u32[]{:S(2)}, u32[]{:S(2)}) collective-permute-start(bf16[32,512]{1,0:T(8,128)(2,1)S(1)} %get-tuple-element.79), channel_id=1, source_target_pairs={{0,12},{4,8},{8,4},{12,0},{1,13},{5,9},{9,5},{13,1},{2,14},{6,10},... | collective-permute-start | bytes 98312 | tf_op jit(solution)/shard_map/ppermute | solution.py:385
  45.7 4.5 %copy-start.3 = (bf16[3,512,512]{2,1,0:T(8,128)(2,1)S(1)}, bf16[3,512,512]{2,1,0:T(8,128)(2,1)}, u32[]{:S(2)}) copy-start(bf16[3,512,512]{2,1,0:T(8,128)(2,1)} %refs_9_.7) | copy-start | bytes 4718596
  45.7 4.5 %copy-start.8 = (f32[3,512]{1,0:T(4,128)S(1)}, f32[3,512]{1,0:T(4,128)}, u32[]{:S(2)}) copy-start(f32[3,512]{1,0:T(4,128)} %refs_8_.10) | copy-start | bytes 18436
  53.8 7.1 %collective-permute-start.11 = (bf16[32,512]{1,0:T(8,128)(2,1)S(1)}, bf16[32,512]{1,0:T(8,128)(2,1)S(1)}, u32[]{:S(2)}, u32[]{:S(2)}) collective-permute-start(bf16[32,512]{1,0:T(8,128)(2,1)S(1)} %get-tuple-element.84), channel_id=1, source_target_pairs={{0,4},{4,0},{8,12},{12,8},{1,5},{5,1},{9,13},{13,9},{2,6},{6,2},{1... | collective-permute-start | bytes 98312 | tf_op jit(solution)/shard_map/ppermute | solution.py:385
  53.9 7.0 %collective-permute-start.12 = (bf16[32,512]{1,0:T(8,128)(2,1)S(1)}, bf16[32,512]{1,0:T(8,128)(2,1)S(1)}, u32[]{:S(2)}, u32[]{:S(2)}) collective-permute-start(bf16[32,512]{1,0:T(8,128)(2,1)S(1)} %get-tuple-element.85), channel_id=1, source_target_pairs={{0,8},{4,12},{8,0},{12,4},{1,9},{5,13},{9,1},{13,5},{2,10},{6,14},... | collective-permute-start | bytes 98312 | tf_op jit(solution)/shard_map/ppermute | solution.py:385
  55.7 5.7 %collective-permute-start.13 = (bf16[32,512]{1,0:T(8,128)(2,1)S(1)}, bf16[32,512]{1,0:T(8,128)(2,1)S(1)}, u32[]{:S(2)}, u32[]{:S(2)}) collective-permute-start(bf16[32,512]{1,0:T(8,128)(2,1)S(1)} %get-tuple-element.86), channel_id=1, source_target_pairs={{0,12},{4,8},{8,4},{12,0},{1,13},{5,9},{9,5},{13,1},{2,14},{6,10},... | collective-permute-start | bytes 98312 | tf_op jit(solution)/shard_map/ppermute | solution.py:385
  65.3 7.1 %collective-permute-start.14 = (bf16[32,512]{1,0:T(8,128)(2,1)S(1)}, bf16[32,512]{1,0:T(8,128)(2,1)S(1)}, u32[]{:S(2)}, u32[]{:S(2)}) collective-permute-start(bf16[32,512]{1,0:T(8,128)(2,1)S(1)} %get-tuple-element.89), channel_id=1, source_target_pairs={{0,4},{4,0},{8,12},{12,8},{1,5},{5,1},{9,13},{13,9},{2,6},{6,2},{1... | collective-permute-start | bytes 98312 | tf_op jit(solution)/shard_map/ppermute | solution.py:385
  65.4 7.0 %collective-permute-start.15 = (bf16[32,512]{1,0:T(8,128)(2,1)S(1)}, bf16[32,512]{1,0:T(8,128)(2,1)S(1)}, u32[]{:S(2)}, u32[]{:S(2)}) collective-permute-start(bf16[32,512]{1,0:T(8,128)(2,1)S(1)} %get-tuple-element.90), channel_id=1, source_target_pairs={{0,8},{4,12},{8,0},{12,4},{1,9},{5,13},{9,1},{13,5},{2,10},{6,14},... | collective-permute-start | bytes 98312 | tf_op jit(solution)/shard_map/ppermute | solution.py:385
  68.5 5.7 %collective-permute-start.16 = (bf16[32,512]{1,0:T(8,128)(2,1)S(1)}, bf16[32,512]{1,0:T(8,128)(2,1)S(1)}, u32[]{:S(2)}, u32[]{:S(2)}) collective-permute-start(bf16[32,512]{1,0:T(8,128)(2,1)S(1)} %get-tuple-element.91), channel_id=1, source_target_pairs={{0,12},{4,8},{8,4},{12,0},{1,13},{5,9},{9,5},{13,1},{2,14},{6,10},... | collective-permute-start | bytes 98312 | tf_op jit(solution)/shard_map/ppermute | solution.py:385
  69.7 4.5 %copy-start.6 = (bf16[512,512]{1,0:T(8,128)(2,1)S(1)}, bf16[512,512]{1,0:T(8,128)(2,1)}, u32[]{:S(2)}) copy-start(bf16[512,512]{1,0:T(8,128)(2,1)} %upstream.1) | copy-start | bytes 1572868
  80.4 7.3 %collective-permute-start.17 = (bf16[32,512]{1,0:T(8,128)(2,1)S(1)}, bf16[32,512]{1,0:T(8,128)(2,1)S(1)}, u32[]{:S(2)}, u32[]{:S(2)}) collective-permute-start(bf16[32,512]{1,0:T(8,128)(2,1)S(1)} %get-tuple-element.95), channel_id=1, source_target_pairs={{4,0},{0,4},{12,8},{8,12},{5,1},{1,5},{13,9},{9,13},{6,2},{2,6},{1... | collective-permute-start | bytes 98312 | tf_op jit(solution)/shard_map/ppermute | solution.py:390
  80.4 7.3 %collective-permute-start.18 = (bf16[32,512]{1,0:T(8,128)(2,1)S(1)}, bf16[32,512]{1,0:T(8,128)(2,1)S(1)}, u32[]{:S(2)}, u32[]{:S(2)}) collective-permute-start(bf16[32,512]{1,0:T(8,128)(2,1)S(1)} %get-tuple-element.96), channel_id=1, source_target_pairs={{8,0},{12,4},{0,8},{4,12},{9,1},{13,5},{1,9},{5,13},{10,2},{14,6},... | collective-permute-start | bytes 98312 | tf_op jit(solution)/shard_map/ppermute | solution.py:390
  82.2 5.9 %collective-permute-start.19 = (bf16[32,512]{1,0:T(8,128)(2,1)S(1)}, bf16[32,512]{1,0:T(8,128)(2,1)S(1)}, u32[]{:S(2)}, u32[]{:S(2)}) collective-permute-start(bf16[32,512]{1,0:T(8,128)(2,1)S(1)} %get-tuple-element.97), channel_id=1, source_target_pairs={{12,0},{8,4},{4,8},{0,12},{13,1},{9,5},{5,9},{1,13},{14,2},{10,6},... | collective-permute-start | bytes 98312 | tf_op jit(solution)/shard_map/ppermute | solution.py:390
  91.0 7.5 %collective-permute-start.20 = (bf16[32,512]{1,0:T(8,128)(2,1)S(1)}, bf16[32,512]{1,0:T(8,128)(2,1)S(1)}, u32[]{:S(2)}, u32[]{:S(2)}) collective-permute-start(bf16[32,512]{1,0:T(8,128)(2,1)S(1)} %get-tuple-element.103), channel_id=1, source_target_pairs={{4,0},{0,4},{12,8},{8,12},{5,1},{1,5},{13,9},{9,13},{6,2},{2,6},{1... | collective-permute-start | bytes 98312 | tf_op jit(solution)/shard_map/ppermute | solution.py:390
  91.1 7.5 %collective-permute-start.21 = (bf16[32,512]{1,0:T(8,128)(2,1)S(1)}, bf16[32,512]{1,0:T(8,128)(2,1)S(1)}, u32[]{:S(2)}, u32[]{:S(2)}) collective-permute-start(bf16[32,512]{1,0:T(8,128)(2,1)S(1)} %get-tuple-element.104), channel_id=1, source_target_pairs={{8,0},{12,4},{0,8},{4,12},{9,1},{13,5},{1,9},{5,13},{10,2},{14,6},... | collective-permute-start | bytes 98312 | tf_op jit(solution)/shard_map/ppermute | solution.py:390
  94.0 5.9 %collective-permute-start.22 = (bf16[32,512]{1,0:T(8,128)(2,1)S(1)}, bf16[32,512]{1,0:T(8,128)(2,1)S(1)}, u32[]{:S(2)}, u32[]{:S(2)}) collective-permute-start(bf16[32,512]{1,0:T(8,128)(2,1)S(1)} %get-tuple-element.105), channel_id=1, source_target_pairs={{12,0},{8,4},{4,8},{0,12},{13,1},{9,5},{5,9},{1,13},{14,2},{10,6},... | collective-permute-start | bytes 98312 | tf_op jit(solution)/shard_map/ppermute | solution.py:390
  102.9 7.3 %collective-permute-start.23 = (bf16[32,512]{1,0:T(8,128)(2,1)S(1)}, bf16[32,512]{1,0:T(8,128)(2,1)S(1)}, u32[]{:S(2)}, u32[]{:S(2)}) collective-permute-start(bf16[32,512]{1,0:T(8,128)(2,1)S(1)} %get-tuple-element.110), channel_id=1, source_target_pairs={{4,0},{0,4},{12,8},{8,12},{5,1},{1,5},{13,9},{9,13},{6,2},{2,6},{1... | collective-permute-start | bytes 98312 | tf_op jit(solution)/shard_map/ppermute | solution.py:390
  103.0 7.3 %collective-permute-start.24 = (bf16[32,512]{1,0:T(8,128)(2,1)S(1)}, bf16[32,512]{1,0:T(8,128)(2,1)S(1)}, u32[]{:S(2)}, u32[]{:S(2)}) collective-permute-start(bf16[32,512]{1,0:T(8,128)(2,1)S(1)} %get-tuple-element.111), channel_id=1, source_target_pairs={{8,0},{12,4},{0,8},{4,12},{9,1},{13,5},{1,9},{5,13},{10,2},{14,6},... | collective-permute-start | bytes 98312 | tf_op jit(solution)/shard_map/ppermute | solution.py:390
  104.9 6.0 %collective-permute-start.25 = (bf16[32,512]{1,0:T(8,128)(2,1)S(1)}, bf16[32,512]{1,0:T(8,128)(2,1)S(1)}, u32[]{:S(2)}, u32[]{:S(2)}) collective-permute-start(bf16[32,512]{1,0:T(8,128)(2,1)S(1)} %get-tuple-element.112), channel_id=1, source_target_pairs={{12,0},{8,4},{4,8},{0,12},{13,1},{9,5},{5,9},{1,13},{14,2},{10,6},... | collective-permute-start | bytes 98312 | tf_op jit(solution)/shard_map/ppermute | solution.py:390
  112.3 5.7 %collective-permute-start.26 = (bf16[128,512]{1,0:T(8,128)(2,1)S(1)}, bf16[128,512]{1,0:T(8,128)(2,1)S(1)}, u32[]{:S(2)}, u32[]{:S(2)}) collective-permute-start(bf16[128,512]{1,0:T(8,128)(2,1)S(1)} %get-tuple-element.125), channel_id=1, source_target_pairs={{4,0},{0,4},{12,8},{8,12},{5,1},{1,5},{13,9},{9,13},{6,2},{2,6},{1... | collective-permute-start | bytes 393224 | tf_op jit(solution)/shard_map/ppermute | solution.py:390
  112.4 8.3 %collective-permute-start.28 = (bf16[128,512]{1,0:T(8,128)(2,1)S(1)}, bf16[128,512]{1,0:T(8,128)(2,1)S(1)}, u32[]{:S(2)}, u32[]{:S(2)}) collective-permute-start(bf16[128,512]{1,0:T(8,128)(2,1)S(1)} %get-tuple-element.128), channel_id=1, source_target_pairs={{4,0},{0,4},{12,8},{8,12},{5,1},{1,5},{13,9},{9,13},{6,2},{2,6},{1... | collective-permute-start | bytes 393224 | tf_op jit(solution)/shard_map/ppermute | solution.py:390
  118.0 10.7 %collective-permute-start.27 = (bf16[256,512]{1,0:T(8,128)(2,1)S(1)}, bf16[256,512]{1,0:T(8,128)(2,1)S(1)}, u32[]{:S(2)}, u32[]{:S(2)}) collective-permute-start(bf16[256,512]{1,0:T(8,128)(2,1)S(1)} %get-tuple-element.127), channel_id=1, source_target_pairs={{4,0},{0,4},{12,8},{8,12},{5,1},{1,5},{13,9},{9,13},{6,2},{2,6},{1... | collective-permute-start | bytes 786440 | tf_op jit(solution)/shard_map/ppermute | solution.py:390
  118.1 6.0 %collective-permute-start.30 = (bf16[128,512]{1,0:T(8,128)(2,1)S(1)}, bf16[128,512]{1,0:T(8,128)(2,1)S(1)}, u32[]{:S(2)}, u32[]{:S(2)}) collective-permute-start(bf16[128,512]{1,0:T(8,128)(2,1)S(1)} %get-tuple-element.129), channel_id=1, source_target_pairs={{8,0},{12,4},{0,8},{4,12},{9,1},{13,5},{1,9},{5,13},{10,2},{14,6},... | collective-permute-start | bytes 393224 | tf_op jit(solution)/shard_map/ppermute | solution.py:390
  120.7 8.0 %collective-permute-start.29 = (bf16[128,512]{1,0:T(8,128)(2,1)S(1)}, bf16[128,512]{1,0:T(8,128)(2,1)S(1)}, u32[]{:S(2)}, u32[]{:S(2)}) collective-permute-start(bf16[128,512]{1,0:T(8,128)(2,1)S(1)} %shard_map.187), channel_id=1, source_target_pairs={{8,0},{12,4},{0,8},{4,12},{9,1},{13,5},{1,9},{5,13},{10,2},{14,6},... | collective-permute-start | bytes 393224 | tf_op jit(solution)/shard_map/ppermute | solution.py:390

commit v4 on v3

--- a/solution.py
+++ b/solution.py
@@ -190,20 +190,18 @@
         sends[shift - 1][...] = half(shift).astype(bf16)
 
 
-def list_rows(list_here, projected, outs):
-    listed = dot(list_here[...], projected).astype(bf16)
-    at = 0
-    for out in outs:
-        out[...] = listed[at : at + out.shape[0]]
-        at += out.shape[0]
-
-
-def start_kernel(halves, shifts, *refs):
+def hand_out(rows, outs, spots):
+    rows = rows.astype(bf16)
+    for out, spot in zip(outs, spots):
+        out[...] = rows[spot : spot + out.shape[0]]
+
+
+def start_kernel(halves, spots, *refs):
     meta = refs[0]
     parts = refs[1 : 1 + halves]
     mesh_init, w_enc_out, gain, w_send, list_here = refs[1 + halves : 6 + halves]
     hidden_out, enc_sum_out, sent = refs[6 + halves : 9 + halves]
-    outs = refs[9 + halves : 9 + halves + shifts]
+    outs = refs[9 + halves : -1]
     whole = refs[-1]
     part = parts[0].shape[0]
     for shift in range(halves):
@@ -215,7 +213,7 @@
     hidden_out[...] = hidden
     projected = dot(hidden, w_send[0]).astype(bf16)
     sent[...] = projected
-    list_rows(list_here, projected, outs)
+    hand_out(dot(list_here[...], projected), outs, spots)
 
 
 def local_kernel(layer, hidden, sent, here, w_recv, pre, table):
@@ -226,117 +224,119 @@
         pre[at : at + BLOCK, :] = dot(here[at : at + BLOCK, :], table[...])
 
 
+def local_more_kernel(table, here, pre):
+    skip = here.shape[0] - pre.shape[0]
+    for at in range(0, pre.shape[0], BLOCK):
+        pre[at : at + BLOCK, :] = dot(here[skip + at : skip + at + BLOCK, :], table[...])
+
+
 def stack_halo(halos, halo):
     at = 0
-    for block in halos:
-        halo[at : at + block.shape[0], :] = block[...]
-        at += block.shape[0]
+    for blocks in halos:
+        rows = blocks[0][...]
+        if len(blocks) > 1:
+            rows = (rows.astype(f32) + blocks[1][...].astype(f32)).astype(bf16)
+        halo[at : at + rows.shape[0], :] = rows
+        at += rows.shape[0]
     if at < halo.shape[0]:
         halo[at:, :] = jnp.zeros((halo.shape[0] - at, halo.shape[1]), bf16)
 
 
-def node_sum(pre, halos, halo_here, there, slope_out, halo):
+def node_sum(pres, halos, halo_here, there, slope_out, halo, act_out):
     nodes = there.shape[0] // 2
     stack_halo(halos, halo)
-    table = halo[...]
-    total = None
-    for at in range(0, pre.shape[0], BLOCK):
+    half = pres[0].shape[0]
+    for at in range(0, 2 * half, BLOCK):
         block = slice(at, at + BLOCK)
-        act, slope = gated(pre[block, :] + dot(halo_here[block, :], table))
+        pre = pres[at // half][at % half : at % half + BLOCK, :]
+        act, slope = gated(pre + dot(halo_here[block, :], halo[...]))
         slope_out[block, :] = slope.astype(bf16)
-        added = dot(there[nodes:, block], act.astype(bf16))
-        total = added if total is None else total + added
-    return total
-
-
-def layer_kernel(layer, shifts, *refs):
-    hidden, pre = refs[:2]
-    halos = refs[2 : 2 + shifts]
-    halo_here, there, w_out, gain, w_send, list_here = refs[2 + shifts : 8 + shifts]
-    hidden_out, agg_out, slope_out, sent_out = refs[8 + shifts : 12 + shifts]
-    outs = refs[12 + shifts : 12 + 2 * shifts]
-    total = node_sum(pre, halos, halo_here, there, slope_out, refs[-1])
+        act_out[block, :] = act.astype(bf16)
+    return dot(there[nodes:, :], act_out[...])
+
+
+def split(refs, inward):
+    groups = []
+    for count in inward:
+        groups.append(refs[:count])
+        refs = refs[count:]
+    return groups, refs
+
+
+def layer_kernel(layer, inward, spots, *refs):
+    hidden, pres = refs[0], refs[1:3]
+    halos, refs = split(refs[3:], inward)
+    halo_here, there, w_out, gain, w_send, list_here = refs[:6]
+    hidden_out, agg_out, slope_out, sent_out = refs[6:10]
+    outs = refs[10:-2]
+    total = node_sum(pres, halos, halo_here, there, slope_out, *refs[-2:])
     agg = dot(total.astype(bf16), w_out[layer])
     agg_out[...] = agg
     fresh = (hidden[...].astype(f32) + agg * norm_scale(agg) * gain[layer : layer + 1, :]).astype(bf16)
     hidden_out[...] = fresh
     projected = dot(fresh, w_send[layer + 1]).astype(bf16)
     sent_out[...] = projected
-    list_rows(list_here, projected, outs)
-
-
-def edge_grads(grad_agg, w_out, here, halo_there, slope, grad_pre, outs):
+    hand_out(dot(list_here[...], projected), outs, spots)
+
+
+def edge_grads(grad_agg, w_out, here, halo_there, slope, grad_pre, outs, spots):
     nodes = grad_agg.shape[0]
     spread = dot_back(grad_agg.astype(bf16), w_out).astype(bf16)
-    given = None
     for at in range(0, slope.shape[0], BLOCK):
         block = slice(at, at + BLOCK)
-        grad = (dot(here[block, nodes:], spread) * slope[block, :].astype(f32)).astype(bf16)
-        grad_pre[block, :] = grad
-        added = dot(halo_there[:, block], grad)
-        given = added if given is None else given + added
-    given = given.astype(bf16)
-    at = 0
-    for out in outs:
-        out[...] = given[at : at + out.shape[0]]
-        at += out.shape[0]
-
-
-def turn_kernel(layer, shifts, *refs):
-    hidden, pre = refs[:2]
-    halos = refs[2 : 2 + shifts]
-    halo_here, there, w_out, gain, here, halo_there, cot = refs[2 + shifts : 9 + shifts]
-    hidden_out, grad_pre = refs[9 + shifts : 11 + shifts]
-    outs = refs[11 + shifts : 11 + 2 * shifts]
+        grad_act = dot(here[block, nodes:], spread)
+        grad_pre[block, :] = (grad_act * slope[block, :].astype(f32)).astype(bf16)
+    hand_out(dot(halo_there[...], grad_pre[...]), outs, spots)
+
+
+def turn_kernel(layer, inward, spots, *refs):
+    hidden, pres = refs[0], refs[1:3]
+    halos, refs = split(refs[3:], inward)
+    halo_here, there, w_out, gain, here, halo_there, cot = refs[:7]
+    hidden_out, grad_pre = refs[7:9]
+    outs = refs[9:-2]
     slope, halo = refs[-2:]
-    total = node_sum(pre, halos, halo_here, there, slope, halo)
+    total = node_sum(pres, halos, halo_here, there, slope, halo, grad_pre)
     agg = dot(total.astype(bf16), w_out[layer])
     gain_row = gain[layer : layer + 1, :]
     hidden_out[...] = (hidden[...].astype(f32) + agg * norm_scale(agg) * gain_row).astype(bf16)
-    edge_grads(norm_back(agg, gain_row, cot[...].astype(f32)), w_out[layer], here, halo_there, slope, grad_pre, outs)
-
-
-def rest_kernel(layer, upstream, grad_pre, there, w_send, w_recv, rest):
+    edge_grads(norm_back(agg, gain_row, cot[...].astype(f32)), w_out[layer], here, halo_there, slope, grad_pre, outs, spots)
+
+
+def rest_kernel(layer, side, upstream, grad_pre, there, weights, rest):
     nodes = upstream.shape[0]
-    sums = dot(there[...], grad_pre[...]).astype(bf16)
-    rest[...] = (
-        upstream[...].astype(f32)
-        + dot_back(sums[0:nodes], w_send[layer])
-        + dot_back(sums[nodes:], w_recv[layer])
-    )
+    sums = dot(there[side * nodes : (side + 1) * nodes, :], grad_pre[...]).astype(bf16)
+    rest[...] = upstream[...].astype(f32) + dot_back(sums, weights[layer])
 
 
 def arrived(rest, returned, list_there, w_send, halo):
-    at = 0
-    for block in returned:
-        halo[at : at + block.shape[0], :] = block[...]
-        at += block.shape[0]
+    stack_halo(returned, halo)
     projected = dot_back(halo[...], w_send).astype(bf16)
     return rest[...] + dot(list_there[...], projected)
 
 
-def back_kernel(layer, shifts, *refs):
+def back_kernel(layer, inward, spots, *refs):
     rest = refs[0]
-    returned = refs[1 : 1 + shifts]
-    list_there, w_send, agg, slope, gain, w_out, here, halo_there = refs[1 + shifts : 9 + shifts]
-    upstream_out, grad_pre = refs[9 + shifts : 11 + shifts]
-    outs = refs[11 + shifts : 11 + 2 * shifts]
+    returned, refs = split(refs[1:], inward)
+    list_there, w_send, agg, slope, gain, w_out, here, halo_there = refs[:8]
+    upstream_out, grad_pre = refs[8:10]
+    outs = refs[10:-1]
     halo = refs[-1]
     upstream = arrived(rest, returned, list_there, w_send[layer + 1], halo)
     upstream_out[...] = upstream
     grad_agg = norm_back(agg[...], gain[layer : layer + 1, :], upstream)
-    edge_grads(grad_agg, w_out[layer], here, halo_there, slope, grad_pre, outs)
+    edge_grads(grad_agg, w_out[layer], here, halo_there, slope, grad_pre, outs, spots)
 
 
 def pair_grads(spread, pick, slope):
     return (dot(pick, spread) * slope.astype(f32)).astype(bf16)
 
 
-def finish_kernel(shifts, *refs):
+def finish_kernel(inward, *refs):
     rest = refs[0]
-    returned = refs[1 : 1 + shifts]
-    list_there, w_send, enc_sum, gain, w_enc_out, pick, slope = refs[1 + shifts : 8 + shifts]
-    spread_out, outs, halo = refs[8 + shifts], refs[9 + shifts : -1], refs[-1]
+    returned, refs = split(refs[1:], inward)
+    list_there, w_send, enc_sum, gain, w_enc_out, pick, slope = refs[:7]
+    spread_out, outs, halo = refs[7], refs[8:-1], refs[-1]
     upstream = arrived(rest, returned, list_there, w_send[0], halo)
     spread = dot_back(norm_back(enc_sum[...], gain[...], upstream).astype(bf16), w_enc_out[...]).astype(bf16)
     spread_out[...] = spread
@@ -439,12 +439,23 @@
     away = partner(shard, place // depth, shards)
     if shards & (shards - 1):
         away = lax.rem(shard - place // depth + shards, shards)
+    core = lax.axis_index("rep")
+    shared = shards == 4 and halves == 2
+    steps = jnp.arange(1, shards, dtype=i32)
+    if shared:
+        steps = jnp.where((core == 1) & (steps < 3), 3 - steps, steps)
     slots = jnp.where(sender_slots < nodes, sender_slots, nodes + (away - 1) * depth + place % depth)
     both = jnp.stack([slots, receivers])
     both = in_order([both] + [shifted(both, "rep", step) for step in range(1, halves)], "rep")
     both = in_order([both] + [shifted(both, "feat", step) for step in range(1, feats)], "feat")
     both = both.reshape(feats * halves, 2, edges)
-    readers = partner(shard, jnp.arange(1, shards, dtype=i32), shards)
+    all_slots, all_receivers = both[:, 0].reshape(1, -1), both[:, 1].reshape(1, -1)
+    if shared:
+        entry = all_slots - nodes
+        moved = jnp.where(entry < depth, depth, -depth)
+        turned = (core == 1) & (entry >= 0) & (entry < 2 * depth)
+        all_slots = all_slots + jnp.where(turned, moved, 0)
+    readers = partner(shard, steps, shards)
     lists = jnp.take(halo_index[0], readers, axis=0).reshape(1, -1)
     here, there, halo_here, halo_there, list_here, list_there = call(
         place_kernel,
@@ -457,7 +468,7 @@
             ((nodes, listed_rows), bf16),
         ],
         products=[(all_edges, nodes, width), (all_edges, 2 * nodes, width)],
-    )(both[:, 0].reshape(1, -1), both[:, 1].reshape(1, -1), lists)
+    )(all_slots, all_receivers, lists)
 
     if shards == 4:
         across, list_here = lax.optimization_barrier((across, list_here))
@@ -502,50 +513,75 @@
     part = sum(piece.astype(f32) for piece in pieces).astype(bf16)
     parts = [part] + [shifted(part, "rep", -step) for step in range(1, halves)]
 
-    listed = [((depth, width), bf16)] * shifts
+    spots = (0, 2 * depth) if shared else tuple(range(0, listed_rows, depth))
+    inward = (1, 1, 2) if shared else (1,) * shifts
+    listed = [((depth, width), bf16)] * len(spots)
+
+    def exchange(blocks, send, early):
+        if not shared:
+            return [send(block, step + 1) for step, block in enumerate(blocks)], early
+        first = lax.ppermute(
+            blocks[0], ("mesh", "rep"), [(2 * at + side, 2 * (at ^ 1 + side) + side) for at in range(4) for side in range(2)]
+        )
+        third = lax.ppermute(blocks[1], ("mesh", "rep"), [(2 * at + 1, 2 * (at ^ 3) + 1) for at in range(4)])
+        first, third, early = lax.optimization_barrier((first, third, early))
+        return [
+            first,
+            lax.ppermute(first, "rep", [(0, 1), (1, 0)]),
+            third,
+            lax.ppermute(third, "rep", [(1, 0)]),
+        ], early
+
     hidden, enc_sum, sent, *outgoing = call(
-        functools.partial(start_kernel, halves, shifts), [node_bf16, node_f32, node_bf16] + listed, [node_bf16],
+        functools.partial(start_kernel, halves, spots), [node_bf16, node_f32, node_bf16] + listed, [node_bf16],
         [square, square, (listed_rows, nodes, width)],
     )(meta, *parts, mesh_init, w_enc_out, enc_gain, w_send, list_here)
 
-    edge_f32, edge_bf16 = ((all_edges, width), f32), ((all_edges, width), bf16)
+    half_f32, edge_bf16 = ((all_edges // 2, width), f32), ((all_edges, width), bf16)
     halo, back_halo = ((wide, width), bf16), ((listed_rows, width), bf16)
-
     forward_products = [(all_edges, wide, width), (nodes, all_edges, width), square]
     backward_products = [square, (all_edges, nodes, width), (wide, all_edges, width)]
-
-    def local(layer):
-        (pre,) = call(functools.partial(local_kernel, layer), [edge_f32], [((2 * nodes, width), bf16)], [square, (all_edges, 2 * nodes, width)])(
-            hidden, sent, here, w_recv
-        )
-        return pre
+    half_product = (all_edges // 2, 2 * nodes, width)
+
+    def arriving(layer):
+        early = call(
+            functools.partial(local_kernel, layer), [half_f32, ((2 * nodes, width), bf16)], (), [square, half_product]
+        )(hidden, sent, here, w_recv)
+        halos, (pre, both_tables) = exchange(outgoing, sent_to, early)
+        (more,) = call(local_more_kernel, [half_f32], (), [half_product])(both_tables, here)
+        return hidden, pre, more, *halos
 
     records = []
     for layer in range(LAYERS - 1):
-        halos = [sent_to(block, step + 1) for step, block in enumerate(outgoing)]
         hidden, agg, slope, sent, *outgoing = call(
-            functools.partial(layer_kernel, layer, shifts),
+            functools.partial(layer_kernel, layer, inward, spots),
             [node_bf16, node_f32, edge_bf16, node_bf16] + listed,
-            [halo],
+            [halo, edge_bf16],
             forward_products + [square, (listed_rows, nodes, width)],
-        )(hidden, local(layer), *halos, halo_here, there, w_out, layer_gain, w_send, list_here)
+        )(*arriving(layer), halo_here, there, w_out, layer_gain, w_send, list_here)
         records.append((agg, slope))
     last = LAYERS - 1
-    halos = [sent_to(block, step + 1) for step, block in enumerate(outgoing)]
     final_mesh, grad_pre, *outgoing = call(
-        functools.partial(turn_kernel, last, shifts), [node_bf16, edge_bf16] + listed, [edge_bf16, halo],
+        functools.partial(turn_kernel, last, inward, spots), [node_bf16, edge_bf16] + listed, [edge_bf16, halo],
         forward_products + backward_products,
-    )(hidden, local(last), *halos, halo_here, there, w_out, layer_gain, here, halo_there, out_cot)
+    )(*arriving(last), halo_here, there, w_out, layer_gain, here, halo_there, out_cot)
     upstream = out_cot
     for layer in reversed(range(LAYERS)):
-        returned = [sent_back(block, step + 1) for step, block in enumerate(outgoing)]
-        (rest,) = call(
-            functools.partial(rest_kernel, layer), [node_f32], (), [(2 * nodes, all_edges, width), square, square]
-        )(upstream, grad_pre, there, w_send, w_recv)
+
+        def rest_of(side, upstream, weights):
+            (rest,) = call(
+                functools.partial(rest_kernel, layer, side), [node_f32], (), [(nodes, all_edges, width), square]
+            )(upstream, grad_pre, there, weights)
+            return rest
+
+        returned, early = exchange(outgoing, sent_back, rest_of(0, upstream, w_send))
+        rest = rest_of(1, early, w_recv)
         if layer:
             agg, slope = records[layer - 1]
             upstream, grad_pre, *outgoing = call(
-                functools.partial(back_kernel, layer - 1, shifts), [node_f32, edge_bf16] + listed, [back_halo],
+                functools.partial(back_kernel, layer - 1, inward, spots),
+                [node_f32, edge_bf16] + listed,
+                [back_halo],
                 backward_products + [(listed_rows, width, width), (nodes, listed_rows, width)],
             )(rest, *returned, list_there, w_send, agg, slope, layer_gain, w_out, here, halo_there)
     relayed = shards == 4
@@ -553,7 +589,7 @@
     piece = ((grid // pieces, width), bf16)
     one = (grid, nodes, width)
     spread, *far = call(
-        functools.partial(finish_kernel, shifts),
+        functools.partial(finish_kernel, inward),
         [node_bf16] + [piece] * pieces,
         [back_halo],
         [square, (listed_rows, width, width), (nodes, listed_rows, width), one],

time: 130 us -> 148 us (1.14)
  starting transfers between devices: 41.2 us -> 52.8 us
  waiting for transfers between devices: 34.2 us -> 41.2 us
  Pallas kernels: 50.8 us -> 49.3 us
    ppermute x0 -> x24, starting transfers between devices: none -> 37.4 us  [the longest x6 21.3 us: exchange(): lax.ppermute(first, 'rep', [(0, 1), (1, 0)])]
    ppermute x12 -> x3, starting transfers between devices: 19.5 us -> 6.13 us  [sent_to(): lax.ppermute(value, 'mesh', [(at, partner(at, step, size)) for at in rang...]
    ppermute x14 -> x5, starting transfers between devices: 18.5 us -> 6.05 us  [sent_back(): lax.ppermute(value, 'mesh', [(partner(at, step, size), at) for at in rang...]
    ppermute x0 -> x24, waiting for transfers between devices: none -> 9.01 us  [the longest x6 6.95 us: exchange(): lax.ppermute(blocks[0], ('mesh', 'rep'), [(2 * at + side, 2 * (at ^ 1 + s...]
    ppermute x12 -> x3, waiting for transfers between devices: 8.82 us -> 4.61 us  [sent_to(): lax.ppermute(value, 'mesh', [(at, partner(at, step, size)) for at in rang...]
    ppermute x14 -> x5, waiting for transfers between devices: 13 us -> 15.1 us  [sent_back(): lax.ppermute(value, 'mesh', [(partner(at, step, size), at) for at in rang...]
    pallas_call x22 -> x28, Pallas kernels: 50.8 us -> 49.3 us  [run(): pl.pallas_call(body, out_shape=tuple((jax.ShapeDtypeStruct(shape, dtype)...]
  transfers between devices with their start and end apart: 31 -> 37, of which waited for: 16 -> 21; matrix products, arithmetic and copies ran while one was open for 2% -> 2% of each run, Pallas kernels for 19% -> 17%
where the time goes in v4:
time: 148 us; the launch traced here: 147 us
  starting transfers between devices  52.8 us (36%)
  Pallas kernels  49.3 us (33%)
  waiting for transfers between devices  41.2 us (28%)
  other arithmetic  1.83 us (1%)
    pallas_call x28, Pallas kernels, run(): pl.pallas_call(body, out_shape=tuple((jax.ShapeDtypeStruct(shape, dtype)...  49.3 us
    ppermute x6, starting transfers between devices, exchange(): lax.ppermute(first, 'rep', [(0, 1), (1, 0)])  21.3 us
    ppermute x5, waiting for transfers between devices, sent_back(): lax.ppermute(value, 'mesh', [(partner(at, step, size), at) for at in rang...  15.1 us
    ppermute x5, waiting for transfers between devices, shifted(): lax.ppermute(value, axis, [(at, (at + by) % size) for at in range(size)])  12.4 us
    ppermute x6, starting transfers between devices, exchange(): lax.ppermute(third, 'rep', [(1, 0)])  8.08 us
    ppermute x6, waiting for transfers between devices, exchange(): lax.ppermute(blocks[0], ('mesh', 'rep'), [(2 * at + side, 2 * (at ^ 1 + s...  6.95 us
    ppermute x3, starting transfers between devices, sent_to(): lax.ppermute(value, 'mesh', [(at, partner(at, step, size)) for at in rang...  6.13 us
    ppermute x5, starting transfers between devices, sent_back(): lax.ppermute(value, 'mesh', [(partner(at, step, size), at) for at in rang...  6.05 us
  transfers between devices with their start and end apart: 37, of which 21 were waited for; matrix products, arithmetic and copies ran while one was open for 2% of the time, Pallas kernels for 17%

profile of v4, /device:TPU:0, one launch (start us, length us, event | category | flops | bytes accessed | tf_op | source)
XLA Modules:
  0.0 147.1 jit_solution(2227349691167909187)
XLA Ops:
  0.6 1.0 shard_map.167.refs_5_
  1.6 3.1 %collective-permute-start.3 = (bf16[272,512]{1,0:T(8,128)(2,1)S(1)}, bf16[272,512]{1,0:T(8,128)(2,1)S(1)}, u32[]{:S(2)}, u32[]{:S(2)}) collective-permute-start(bf16[272,512]{1,0:T(8,128)(2,1)S(1)} %shard_map.167.refs_5_), channel_id=1, source_target_pairs={{0,4},{4,0},{8,12},{12,8},{1,5},{5,1},{9,13},{13,9},{2,6},{6,2},{1... | collective-permute-start | bytes 835592 | tf_op jit(solution)/shard_map/ppermute | solution.py:385
  4.7 2.6 %collective-permute-start = (bf16[272,512]{1,0:T(8,128)(2,1)S(1)}, bf16[272,512]{1,0:T(8,128)(2,1)S(1)}, u32[]{:S(2)}, u32[]{:S(2)}) collective-permute-start(bf16[272,512]{1,0:T(8,128)(2,1)S(1)} %shard_map.167.refs_5_), channel_id=1, source_target_pairs={{0,8},{4,12},{8,0},{12,4},{1,9},{5,13},{9,1},{13,5},{2,10},{6,14},... | collective-permute-start | bytes 835592 | tf_op jit(solution)/shard_map/ppermute | solution.py:385
  7.3 0.7 compare_select_fusion.1
  10.1 1.6 %collective-permute-start.2 = (s32[2,2,512]{2,0,1:T(2,128)S(1)}, s32[2,2,512]{2,0,1:T(2,128)S(1)}, u32[]{:S(2)}, u32[]{:S(2)}) collective-permute-start(s32[2,2,512]{2,0,1:T(2,128)S(1)} %fusion.1), channel_id=1, source_target_pairs={{0,2},{2,0},{1,3},{3,1},{4,6},{6,4},{5,7},{7,5},{8,10},{10,8},{9,1... | collective-permute-start | bytes 24584 | tf_op jit(solution)/shard_map/ppermute | solution.py:376
  11.7 2.1 %collective-permute-done.2 = s32[2,2,512]{2,0,1:T(2,128)S(1)} collective-permute-done((s32[2,2,512]{2,0,1:T(2,128)S(1)}, s32[2,2,512]{2,0,1:T(2,128)S(1)}, u32[]{:S(2)}, u32[]{:S(2)}) %collective-permute-start.2) | collective-permute-done | bytes 8224 | tf_op jit(solution)/shard_map/ppermute | solution.py:376
  14.0 3.5 %shard_map.168 = (bf16[2048,1024]{1,0:T(8,128)(2,1)S(1)}, bf16[1024,2048]{1,0:T(8,128)(2,1)S(1)}, bf16[2048,128]{1,0:T(8,128)(2,1)S(1)}, bf16[128,2048]{1,0:T(8,...) custom-call(s32[1,2048]{1,0:T(1,128)S(1)} %fusion.2.slots, s32[1,2048]{1,0:T(1,128)S(1)} %bitcast.28, ...), custom_call_target="tpu_custom_call" | custom-call | flops 3221225472 | bytes 9650560 | tf_op jit(solution)/shard_map/pallas_call | solution.py:82
  17.5 2.3 %collective-permute-done.refs_4_ = bf16[272,512]{1,0:T(8,128)(2,1)S(1)} collective-permute-done((bf16[272,512]{1,0:T(8,128)(2,1)S(1)}, bf16[272,512]{1,0:T(8,128)(2,1)S(1)}, u32[]{:S(2)}, u32[]{:S(2)}) %collective-permute-start) | collective-permute-done | bytes 278560 | tf_op jit(solution)/shard_map/ppermute | solution.py:385
  20.3 2.2 %shard_map.169 = (bf16[256,512]{1,0:T(8,128)(2,1)S(1)}, bf16[256,512]{1,0:T(8,128)(2,1)S(1)}, bf16[256,512]{1,0:T(8,128)(2,1)S(1)}, bf16[256,512]{1,0:T(8,128)(2...) custom-call(s32[2]{0:T(128)S(1)} %pad_add_fusion.3.refs_0_, bf16[512,512]{1,0:T(8,128)(2,1)S(1)} %copy-done.8, ...), custom_call_target="tpu_custom_call" | custom-call | flops 1073741824 | bytes 4849672 | tf_op jit(solution)/shard_map/pallas_call | solution.py:82
  22.5 1.4 shard_map.170
  24.0 2.3 %collective-permute-done.4.refs_4_ = bf16[272,512]{1,0:T(8,128)(2,1)S(1)} collective-permute-done((bf16[272,512]{1,0:T(8,128)(2,1)S(1)}, bf16[272,512]{1,0:T(8,128)(2,1)S(1)}, u32[]{:S(2)}, u32[]{:S(2)}) %collective-permute-start.4) | collective-permute-done | bytes 278560 | tf_op jit(solution)/shard_map/ppermute | solution.py:385
  26.3 1.6 %shard_map.171 = (bf16[256,512]{1,0:T(8,128)(2,1)S(1)}, bf16[256,512]{1,0:T(8,128)(2,1)S(1)}, f32[256,512]{1,0:T(8,128)S(1)}, bf16[256,512]{1,0:T(8,128)(2,1)S(1)}) custom-call(s32[2]{0:T(128)S(1)} %pad_add_fusion.3.refs_0_, bf16[512,512]{1,0:T(8,128)(2,1)S(1)} %get-tuple-element.89.refs_1_, bf16[512,512]{1,0:T(8,128)(2,1)S(1)} %copy-done.5, ...), custom_call_target="tpu_custom_call" | custom-call | flops 402653184 | bytes 3686408 | tf_op jit(solution)/shard_map/pallas_call | solution.py:82
  28.0 1.5 %collective-permute-done.5 = bf16[256,512]{1,0:T(8,128)(2,1)S(1)} collective-permute-done((bf16[256,512]{1,0:T(8,128)(2,1)S(1)}, bf16[256,512]{1,0:T(8,128)(2,1)S(1)}, u32[]{:S(2)}, u32[]{:S(2)}) %collective-permute-start.5) | collective-permute-done | bytes 262176 | tf_op jit(solution)/shard_map/ppermute | solution.py:376
  29.6 1.6 %collective-permute-start.6 = (bf16[256,512]{1,0:T(8,128)(2,1)S(1)}, bf16[256,512]{1,0:T(8,128)(2,1)S(1)}, u32[]{:S(2)}, u32[]{:S(2)}) collective-permute-start(bf16[256,512]{1,0:T(8,128)(2,1)S(1)} %add_convert_fusion.1), channel_id=1, source_target_pairs={{0,2},{2,0},{1,3},{3,1},{4,6},{6,4},{5,7},{7,5},{8,10},{10,8},{9,1... | collective-permute-start | bytes 786440 | tf_op jit(solution)/shard_map/ppermute | solution.py:376
  31.1 6.9 %collective-permute-done.6 = bf16[256,512]{1,0:T(8,128)(2,1)S(1)} collective-permute-done((bf16[256,512]{1,0:T(8,128)(2,1)S(1)}, bf16[256,512]{1,0:T(8,128)(2,1)S(1)}, u32[]{:S(2)}, u32[]{:S(2)}) %collective-permute-start.6) | collective-permute-done | bytes 262176 | tf_op jit(solution)/shard_map/ppermute | solution.py:376
  38.2 1.5 %collective-permute-done.7.refs_2_ = bf16[256,512]{1,0:T(8,128)(2,1)S(1)} collective-permute-done((bf16[256,512]{1,0:T(8,128)(2,1)S(1)}, bf16[256,512]{1,0:T(8,128)(2,1)S(1)}, u32[]{:S(2)}, u32[]{:S(2)}) %collective-permute-start.7) | collective-permute-done | bytes 262176 | tf_op jit(solution)/shard_map/ppermute | solution.py:376
  39.7 1.6 %shard_map.172 = (bf16[512,512]{1,0:T(8,128)(2,1)S(1)}, f32[512,512]{1,0:T(8,128)S(1)}, bf16[512,512]{1,0:T(8,128)(2,1)S(1)}, bf16[32,512]{1,0:T(8,128)(2,1)S(1)}, bf16[32,512]{1,0:T(8,128)(2,1)S(1)}) custom-call(s32[2]{0:T(128)S(1)} %pad_add_fusion.3.refs_0_, bf16[256,512]{1,0:T(8,128)(2,1)S(1)} %add_convert_fusion.refs_1_, ...), custom_call_target="tpu_custom_call" | custom-call | flops 587202560 | bytes 5408776 | tf_op jit(solution)/shard_map/pallas_call | solution.py:82
  41.3 1.5 collective-permute-start.8
  43.4 1.5 %shard_map.173 = (f32[1024,512]{1,0:T(8,128)S(1)}, bf16[1024,512]{1,0:T(8,128)(2,1)S(1)}) custom-call(bf16[512,512]{1,0:T(8,128)(2,1)S(1)} %get-tuple-element.95.hidden.refs_0_, bf16[512,512]{1,0:T(8,128)(2,1)S(1)} %get-tuple-element.98.sent, bf16[2048,1024]{1,0:T(8,128)(2,1)S(1)} %get-tuple-element.99.here.refs_11_, bf16[3,512,512]{2,1,0:T(8,128)(2,1)S(1)} %copy-done.3), custom_call_target="tpu_custom_call" | custom-call | flops 1342177280 | bytes 9961472 | tf_op jit(solution)/shard_map/pallas_call | solution.py:82
  45.6 3.3 %collective-permute-start.10 = (bf16[32,512]{1,0:T(8,128)(2,1)S(1)}, bf16[32,512]{1,0:T(8,128)(2,1)S(1)}, u32[]{:S(2)}, u32[]{:S(2)}) collective-permute-start(bf16[32,512]{1,0:T(8,128)(2,1)S(1)} %collective-permute-done.8.refs_3_), channel_id=1, source_target_pairs={{0,1},{1,0},{2,3},{3,2},{4,5},{5,4},{6,7},{7,6},{8,9},{9,8},{10,11... | collective-permute-start | bytes 98312 | tf_op jit(solution)/shard_map/ppermute | solution.py:530
  48.9 1.3 collective-permute-start.11
  50.2 1.2 shard_map.174.refs_2_
  52.0 3.2 %shard_map.175 = (bf16[512,512]{1,0:T(8,128)(2,1)S(1)}, f32[512,512]{1,0:T(8,128)S(1)}, bf16[2048,512]{1,0:T(8,128)(2,1)S(1)}, bf16[512,512]{1,0:T(8,128)(2,1)S(...) custom-call(bf16[512,512]{1,0:T(8,128)(2,1)S(1)} %get-tuple-element.95.hidden.refs_0_, ...), custom_call_target="tpu_custom_call" | custom-call | flops 1929379840 | bytes 17078272 | tf_op jit(solution)/shard_map/pallas_call | solution.py:82
  56.0 1.5 %shard_map.176 = (f32[1024,512]{1,0:T(8,128)S(1)}, bf16[1024,512]{1,0:T(8,128)(2,1)S(1)}) custom-call(bf16[512,512]{1,0:T(8,128)(2,1)S(1)} %get-tuple-element.108.hidden.refs_0_, bf16[512,512]{1,0:T(8,128)(2,1)S(1)} %get-tuple-element.111.sent, bf16[2048,1024]{1,0:T(8,128)(2,1)S(1)} %get-tuple-element.99.here.refs_11_, bf16[3,512,512]{2,1,0:T(8,128)(2,1)S(1)} %copy-done.3), custom_call_target="tpu_custom_call" | custom-call | flops 1342177280 | bytes 9961472 | tf_op jit(solution)/shard_map/pallas_call | solution.py:82
  57.5 1.6 %collective-permute-done.12.refs_3_ = bf16[32,512]{1,0:T(8,128)(2,1)S(1)} collective-permute-done((bf16[32,512]{1,0:T(8,128)(2,1)S(1)}, bf16[32,512]{1,0:T(8,128)(2,1)S(1)}, u32[]{:S(2)}, u32[]{:S(2)}) %collective-permute-start.12) | collective-permute-done | bytes 32800 | tf_op jit(solution)/shard_map/ppermute | solution.py:523
  59.1 3.2 %collective-permute-start.14 = (bf16[32,512]{1,0:T(8,128)(2,1)S(1)}, bf16[32,512]{1,0:T(8,128)(2,1)S(1)}, u32[]{:S(2)}, u32[]{:S(2)}) collective-permute-start(bf16[32,512]{1,0:T(8,128)(2,1)S(1)} %collective-permute-done.12.refs_3_), channel_id=1, source_target_pairs={{0,1},{1,0},{2,3},{3,2},{4,5},{5,4},{6,7},{7,6},{8,9},{9,8},{10,11... | collective-permute-start | bytes 98312 | tf_op jit(solution)/shard_map/ppermute | solution.py:530
  62.3 1.5 collective-permute-start.15
  63.8 1.2 shard_map.177.refs_2_
  65.4 3.2 %shard_map.178 = (bf16[512,512]{1,0:T(8,128)(2,1)S(1)}, f32[512,512]{1,0:T(8,128)S(1)}, bf16[2048,512]{1,0:T(8,128)(2,1)S(1)}, bf16[512,512]{1,0:T(8,128)(2,1)S(...) custom-call(bf16[512,512]{1,0:T(8,128)(2,1)S(1)} %get-tuple-element.108.hidden.refs_0_, ...), custom_call_target="tpu_custom_call" | custom-call | flops 1929379840 | bytes 17078272 | tf_op jit(solution)/shard_map/pallas_call | solution.py:82
  68.7 1.0 collective-permute-start.16
  70.3 1.5 %shard_map.179 = (f32[1024,512]{1,0:T(8,128)S(1)}, bf16[1024,512]{1,0:T(8,128)(2,1)S(1)}) custom-call(bf16[512,512]{1,0:T(8,128)(2,1)S(1)} %get-tuple-element.118.hidden.refs_0_, bf16[512,512]{1,0:T(8,128)(2,1)S(1)} %get-tuple-element.121.sent, bf16[2048,1024]{1,0:T(8,128)(2,1)S(1)} %get-tuple-element.99.here.refs_11_, bf16[3,512,512]{2,1,0:T(8,128)(2,1)S(1)} %copy-done.3), custom_call_target="tpu_custom_call" | custom-call | flops 1342177280 | bytes 9961472 | tf_op jit(solution)/shard_map/pallas_call | solution.py:82
  71.9 0.8 collective-permute-done.16.refs_3_
  72.6 4.1 %collective-permute-start.18 = (bf16[32,512]{1,0:T(8,128)(2,1)S(1)}, bf16[32,512]{1,0:T(8,128)(2,1)S(1)}, u32[]{:S(2)}, u32[]{:S(2)}) collective-permute-start(bf16[32,512]{1,0:T(8,128)(2,1)S(1)} %collective-permute-done.16.refs_3_), channel_id=1, source_target_pairs={{0,1},{1,0},{2,3},{3,2},{4,5},{5,4},{6,7},{7,6},{8,9},{9,8},{10,11... | collective-permute-start | bytes 98312 | tf_op jit(solution)/shard_map/ppermute | solution.py:530
  76.7 1.3 collective-permute-start.19
  78.0 1.2 shard_map.180.refs_2_
  79.8 5.7 %shard_map.181 = (bf16[512,512]{1,0:T(8,128)(2,1)}, bf16[2048,512]{1,0:T(8,128)(2,1)S(1)}, bf16[32,512]{1,0:T(8,128)(2,1)S(1)}, bf16[32,512]{1,0:T(8,128)(2,1)S(1)}) custom-call(bf16[512,512]{1,0:T(8,128)(2,1)S(1)} %get-tuple-element.118.hidden.refs_0_, f32[1024,512]{1,0:T(8,128)S(1)} %get-tuple-element.124.refs_1_, f32[1024,512]{1,0:T(8,128)S(1)} %shard_map.180.refs_2_, ...), custom_call_target="tpu_custom_call" | custom-call | flops 3221225472 | bytes 19077120 | tf_op jit(solution)/shard_map/pallas_call | solution.py:82
  86.4 1.5 %shard_map.182.upstream = f32[512,512]{1,0:T(8,128)S(1)} custom-call(bf16[512,512]{1,0:T(8,128)(2,1)S(1)} %copy-done.6, bf16[2048,512]{1,0:T(8,128)(2,1)S(1)} %get-tuple-element.132.grad_pre, bf16[1024,2048]{1,0:T(8,128)(2,1)S(1)} %get-tuple-element.107.refs_8_.there, bf16[3,512,512]{2,1,0:T(8,128)(2,1)S(1)} %copy-done.2), custom_call_target="tpu_custom_call" | custom-call | flops 1342177280 | bytes 9437184 | tf_op jit(solution)/shard_map/pallas_call | solution.py:82
  87.9 1.5 %collective-permute-done.20.refs_1_ = bf16[32,512]{1,0:T(8,128)(2,1)S(1)} collective-permute-done((bf16[32,512]{1,0:T(8,128)(2,1)S(1)}, bf16[32,512]{1,0:T(8,128)(2,1)S(1)}, u32[]{:S(2)}, u32[]{:S(2)}) %collective-permute-start.20) | collective-permute-done | bytes 32800 | tf_op jit(solution)/shard_map/ppermute | solution.py:523
  89.4 3.1 %collective-permute-start.22 = (bf16[32,512]{1,0:T(8,128)(2,1)S(1)}, bf16[32,512]{1,0:T(8,128)(2,1)S(1)}, u32[]{:S(2)}, u32[]{:S(2)}) collective-permute-start(bf16[32,512]{1,0:T(8,128)(2,1)S(1)} %collective-permute-done.20.refs_1_), channel_id=1, source_target_pairs={{0,1},{1,0},{2,3},{3,2},{4,5},{5,4},{6,7},{7,6},{8,9},{9,8},{10,11... | collective-permute-start | bytes 98312 | tf_op jit(solution)/shard_map/ppermute | solution.py:530
  92.6 1.5 %collective-permute-start.23 = (bf16[32,512]{1,0:T(8,128)(2,1)S(1)}, bf16[32,512]{1,0:T(8,128)(2,1)S(1)}, u32[]{:S(2)}, u32[]{:S(2)}) collective-permute-start(bf16[32,512]{1,0:T(8,128)(2,1)S(1)} %collective-permute-done.21.refs_3_), channel_id=1, source_target_pairs={{1,0},{3,2},{5,4},{7,6},{9,8},{11,10},{13,12},{15,14},{17,16},{19,... | collective-permute-start | bytes 98312 | tf_op jit(solution)/shard_map/ppermute | solution.py:532
  94.1 1.5 %shard_map.183.refs_0_ = f32[512,512]{1,0:T(8,128)S(1)} custom-call(f32[512,512]{1,0:T(8,128)S(1)} %shard_map.182.upstream, bf16[2048,512]{1,0:T(8,128)(2,1)S(1)} %get-tuple-element.132.grad_pre, bf16[1024,2048]{1,0:T(8,128)(2,1)S(1)} %get-tuple-element.107.refs_8_.there, bf16[3,512,512]{2,1,0:T(8,128)(2,1)S(1)} %copy-done.3), custom_call_target="tpu_custom_call" | custom-call | flops 1342177280 | bytes 9961472 | tf_op jit(solution)/shard_map/pallas_call | solution.py:82
  95.6 2.6 %shard_map.184 = (f32[512,512]{1,0:T(8,128)S(1)}, bf16[2048,512]{1,0:T(8,128)(2,1)S(1)}, bf16[32,512]{1,0:T(8,128)(2,1)S(1)}, bf16[32,512]{1,0:T(8,128)(2,1)S(1)}) custom-call(f32[512,512]{1,0:T(8,128)S(1)} %shard_map.183.refs_0_, bf16[32,512]{1,0:T(8,128)(2,1)S(1)} %collective-permute-done.20.refs_1_, bf16[32,512]{1,0:T(8,128)(2,1)S(1)} %collective-permute-done.22.refs_2_, ...), custom_call_target="tpu_custom_call" | custom-call | flops 1711276032 | bytes 15505408 | tf_op jit(solution)/shard_map/pallas_call | solution.py:82
  98.2 1.0 collective-permute-start.24
  99.8 1.5 %shard_map.185.upstream = f32[512,512]{1,0:T(8,128)S(1)} custom-call(f32[512,512]{1,0:T(8,128)S(1)} %get-tuple-element.141.upstream, bf16[2048,512]{1,0:T(8,128)(2,1)S(1)} %get-tuple-element.142.grad_pre, bf16[1024,2048]{1,0:T(8,128)(2,1)S(1)} %get-tuple-element.107.refs_8_.there, bf16[3,512,512]{2,1,0:T(8,128)(2,1)S(1)} %copy-done.2), custom_call_target="tpu_custom_call" | custom-call | flops 1342177280 | bytes 9961472 | tf_op jit(solution)/shard_map/pallas_call | solution.py:82
  101.4 0.8 collective-permute-done.24.refs_1_
  102.2 4.2 %collective-permute-start.26 = (bf16[32,512]{1,0:T(8,128)(2,1)S(1)}, bf16[32,512]{1,0:T(8,128)(2,1)S(1)}, u32[]{:S(2)}, u32[]{:S(2)}) collective-permute-start(bf16[32,512]{1,0:T(8,128)(2,1)S(1)} %collective-permute-done.24.refs_1_), channel_id=1, source_target_pairs={{0,1},{1,0},{2,3},{3,2},{4,5},{5,4},{6,7},{7,6},{8,9},{9,8},{10,11... | collective-permute-start | bytes 98312 | tf_op jit(solution)/shard_map/ppermute | solution.py:530
  106.4 1.3 collective-permute-start.27
  107.7 1.5 %shard_map.186.refs_0_ = f32[512,512]{1,0:T(8,128)S(1)} custom-call(f32[512,512]{1,0:T(8,128)S(1)} %shard_map.185.upstream, bf16[2048,512]{1,0:T(8,128)(2,1)S(1)} %get-tuple-element.142.grad_pre, bf16[1024,2048]{1,0:T(8,128)(2,1)S(1)} %get-tuple-element.107.refs_8_.there, bf16[3,512,512]{2,1,0:T(8,128)(2,1)S(1)} %copy-done.3), custom_call_target="tpu_custom_call" | custom-call | flops 1342177280 | bytes 9961472 | tf_op jit(solution)/shard_map/pallas_call | solution.py:82
  109.5 2.6 %shard_map.187 = (f32[512,512]{1,0:T(8,128)S(1)}, bf16[2048,512]{1,0:T(8,128)(2,1)S(1)}, bf16[32,512]{1,0:T(8,128)(2,1)S(1)}, bf16[32,512]{1,0:T(8,128)(2,1)S(1)}) custom-call(f32[512,512]{1,0:T(8,128)S(1)} %shard_map.186.refs_0_, bf16[32,512]{1,0:T(8,128)(2,1)S(1)} %collective-permute-done.24.refs_1_, bf16[32,512]{1,0:T(8,128)(2,1)S(1)} %collective-permute-done.26.refs_2_, ...), custom_call_target="tpu_custom_call" | custom-call | flops 1711276032 | bytes 15505408 | tf_op jit(solution)/shard_map/pallas_call | solution.py:82
  113.0 1.5 %shard_map.188.upstream = f32[512,512]{1,0:T(8,128)S(1)} custom-call(f32[512,512]{1,0:T(8,128)S(1)} %get-tuple-element.150.upstream, bf16[2048,512]{1,0:T(8,128)(2,1)S(1)} %get-tuple-element.151.grad_pre, bf16[1024,2048]{1,0:T(8,128)(2,1)S(1)} %get-tuple-element.107.refs_8_.there, bf16[3,512,512]{2,1,0:T(8,128)(2,1)S(1)} %copy-done.2), custom_call_target="tpu_custom_call" | custom-call | flops 1342177280 | bytes 9961472 | tf_op jit(solution)/shard_map/pallas_call | solution.py:82
  114.5 1.5 %collective-permute-done.28.refs_1_ = bf16[32,512]{1,0:T(8,128)(2,1)S(1)} collective-permute-done((bf16[32,512]{1,0:T(8,128)(2,1)S(1)}, bf16[32,512]{1,0:T(8,128)(2,1)S(1)}, u32[]{:S(2)}, u32[]{:S(2)}) %collective-permute-start.28) | collective-permute-done | bytes 32800 | tf_op jit(solution)/shard_map/ppermute | solution.py:523
  116.0 3.4 %collective-permute-start.30 = (bf16[32,512]{1,0:T(8,128)(2,1)S(1)}, bf16[32,512]{1,0:T(8,128)(2,1)S(1)}, u32[]{:S(2)}, u32[]{:S(2)}) collective-permute-start(bf16[32,512]{1,0:T(8,128)(2,1)S(1)} %collective-permute-done.28.refs_1_), channel_id=1, source_target_pairs={{0,1},{1,0},{2,3},{3,2},{4,5},{5,4},{6,7},{7,6},{8,9},{9,8},{10,11... | collective-permute-start | bytes 98312 | tf_op jit(solution)/shard_map/ppermute | solution.py:530
  119.5 1.3 collective-permute-start.31
  120.8 1.5 %shard_map.189.refs_0_ = f32[512,512]{1,0:T(8,128)S(1)} custom-call(f32[512,512]{1,0:T(8,128)S(1)} %shard_map.188.upstream, bf16[2048,512]{1,0:T(8,128)(2,1)S(1)} %get-tuple-element.151.grad_pre, bf16[1024,2048]{1,0:T(8,128)(2,1)S(1)} %get-tuple-element.107.refs_8_.there, bf16[3,512,512]{2,1,0:T(8,128)(2,1)S(1)} %copy-done.3), custom_call_target="tpu_custom_call" | custom-call | flops 1342177280 | bytes 9961472 | tf_op jit(solution)/shard_map/pallas_call | solution.py:82
  122.6 1.4 shard_map.190
  124.0 1.0 collective-permute-start.32
  124.9 1.1 collective-permute-start.34
  126.6 3.8 %collective-permute-done.32.passed = bf16[128,512]{1,0:T(8,128)(2,1)S(1)} collective-permute-done((bf16[128,512]{1,0:T(8,128)(2,1)S(1)}, bf16[128,512]{1,0:T(8,128)(2,1)S(1)}, u32[]{:S(2)}, u32[]{:S(2)}) %collective-permute-start.32) | collective-permute-done | bytes 131104 | tf_op jit(solution)/shard_map/ppermute | solution.py:390
  130.4 1.0 collective-permute-start.33
  131.4 2.1 %collective-permute-start.36 = (bf16[128,512]{1,0:T(8,128)(2,1)S(1)}, bf16[128,512]{1,0:T(8,128)(2,1)S(1)}, u32[]{:S(2)}, u32[]{:S(2)}) collective-permute-start(bf16[128,512]{1,0:T(8,128)(2,1)S(1)} %get-tuple-element.171), channel_id=1, source_target_pairs={{8,0},{12,4},{0,8},{4,12},{9,1},{13,5},{1,9},{5,13},{10,2},{14,6},... | collective-permute-start | bytes 393224 | tf_op jit(solution)/shard_map/ppermute | solution.py:390
  133.5 0.9 collective-permute-start.35
  134.4 6.5 %collective-permute-done.36.refs_3_ = bf16[128,512]{1,0:T(8,128)(2,1)S(1)} collective-permute-done((bf16[128,512]{1,0:T(8,128)(2,1)S(1)}, bf16[128,512]{1,0:T(8,128)(2,1)S(1)}, u32[]{:S(2)}, u32[]{:S(2)}) %collective-permute-start.36) | collective-permute-done | bytes 131104 | tf_op jit(solution)/shard_map/ppermute | solution.py:390
  141.0 4.9 %collective-permute-done.35.refs_2_ = bf16[128,512]{1,0:T(8,128)(2,1)S(1)} collective-permute-done((bf16[128,512]{1,0:T(8,128)(2,1)S(1)}, bf16[128,512]{1,0:T(8,128)(2,1)S(1)}, u32[]{:S(2)}, u32[]{:S(2)}) %collective-permute-start.35) | collective-permute-done | bytes 131104 | tf_op jit(solution)/shard_map/ppermute | solution.py:390
  145.8 1.3 shard_map.194
  (87 shorter events, 11.0 us)
Async XLA Ops:
  0.6 8.1 %copy-start = (s32[1,4,32]{2,1,0:T(4,128)S(1)}, s32[1,4,32]{2,1,0:T(4,128)}, u32[]{:S(2)}) copy-start(s32[1,4,32]{2,1,0:T(4,128)} %param.22) | copy-start | bytes 1540
  1.6 18.6 %collective-permute-start.3 = (bf16[272,512]{1,0:T(8,128)(2,1)S(1)}, bf16[272,512]{1,0:T(8,128)(2,1)S(1)}, u32[]{:S(2)}, u32[]{:S(2)}) collective-permute-start(bf16[272,512]{1,0:T(8,128)(2,1)S(1)} %shard_map.167.refs_5_), channel_id=1, source_target_pairs={{0,4},{4,0},{8,12},{12,8},{1,5},{5,1},{9,13},{13,9},{2,6},{6,2},{1... | collective-permute-start | bytes 835592 | tf_op jit(solution)/shard_map/ppermute | solution.py:385
  4.7 15.0 %collective-permute-start = (bf16[272,512]{1,0:T(8,128)(2,1)S(1)}, bf16[272,512]{1,0:T(8,128)(2,1)S(1)}, u32[]{:S(2)}, u32[]{:S(2)}) collective-permute-start(bf16[272,512]{1,0:T(8,128)(2,1)S(1)} %shard_map.167.refs_5_), channel_id=1, source_target_pairs={{0,8},{4,12},{8,0},{12,4},{1,9},{5,13},{9,1},{13,5},{2,10},{6,14},... | collective-permute-start | bytes 835592 | tf_op jit(solution)/shard_map/ppermute | solution.py:385
  8.7 1.2 collective-permute-start.1
  10.1 3.7 %collective-permute-start.2 = (s32[2,2,512]{2,0,1:T(2,128)S(1)}, s32[2,2,512]{2,0,1:T(2,128)S(1)}, u32[]{:S(2)}, u32[]{:S(2)}) collective-permute-start(s32[2,2,512]{2,0,1:T(2,128)S(1)} %fusion.1), channel_id=1, source_target_pairs={{0,2},{2,0},{1,3},{3,1},{4,6},{6,4},{5,7},{7,5},{8,10},{10,8},{9,1... | collective-permute-start | bytes 24584 | tf_op jit(solution)/shard_map/ppermute | solution.py:376
  13.9 6.4 %copy-start.5 = (bf16[512,512]{1,0:T(8,128)(2,1)S(1)}, bf16[512,512]{1,0:T(8,128)(2,1)}, u32[]{:S(2)}) copy-start(bf16[512,512]{1,0:T(8,128)(2,1)} %refs_4_.3) | copy-start | bytes 1572868
  13.9 6.3 %copy-start.8 = (bf16[512,512]{1,0:T(8,128)(2,1)S(1)}, bf16[512,512]{1,0:T(8,128)(2,1)}, u32[]{:S(2)}) copy-start(bf16[512,512]{1,0:T(8,128)(2,1)} %refs_3_.3) | copy-start | bytes 1572868
  14.0 6.3 %copy-start.11 = (bf16[512,512]{1,0:T(8,128)(2,1)S(1)}, bf16[512,512]{1,0:T(8,128)(2,1)}, u32[]{:S(2)}) copy-start(bf16[512,512]{1,0:T(8,128)(2,1)} %refs_3_.2) | copy-start | bytes 1572868
  19.8 6.5 %collective-permute-start.4 = (bf16[272,512]{1,0:T(8,128)(2,1)S(1)}, bf16[272,512]{1,0:T(8,128)(2,1)S(1)}, u32[]{:S(2)}, u32[]{:S(2)}) collective-permute-start(bf16[272,512]{1,0:T(8,128)(2,1)S(1)} %collective-permute-done.refs_4_), channel_id=1, source_target_pairs={{0,4},{4,0},{8,12},{12,8},{1,5},{5,1},{9,13},{13,9},{2,6},{6,2},{1... | collective-permute-start | bytes 835592 | tf_op jit(solution)/shard_map/ppermute | solution.py:385
  26.3 13.4 %copy-start.2 = (bf16[3,512,512]{2,1,0:T(8,128)(2,1)S(1)}, bf16[3,512,512]{2,1,0:T(8,128)(2,1)}, u32[]{:S(2)}) copy-start(bf16[3,512,512]{2,1,0:T(8,128)(2,1)} %refs_6_.7) | copy-start | bytes 4718596
  26.3 13.4 %copy-start.7 = (bf16[512,512]{1,0:T(8,128)(2,1)S(1)}, bf16[512,512]{1,0:T(8,128)(2,1)}, u32[]{:S(2)}) copy-start(bf16[512,512]{1,0:T(8,128)(2,1)} %refs_9_.11) | copy-start | bytes 1572868
  26.3 13.4 %copy-start.10 = (f32[512]{0:T(512)S(1)}, f32[512]{0:T(512)}, u32[]{:S(2)}) copy-start(f32[512]{0:T(512)} %param.26) | copy-start | bytes 6148
  27.9 1.6 %collective-permute-start.5 = (bf16[256,512]{1,0:T(8,128)(2,1)S(1)}, bf16[256,512]{1,0:T(8,128)(2,1)S(1)}, u32[]{:S(2)}, u32[]{:S(2)}) collective-permute-start(bf16[256,512]{1,0:T(8,128)(2,1)S(1)} %get-tuple-element.94), channel_id=1, source_target_pairs={{0,1},{1,0},{2,3},{3,2},{4,5},{5,4},{6,7},{7,6},{8,9},{9,8},{10,11... | collective-permute-start | bytes 786440 | tf_op jit(solution)/shard_map/ppermute | solution.py:376
  29.6 13.8 %copy-start.3 = (bf16[3,512,512]{2,1,0:T(8,128)(2,1)S(1)}, bf16[3,512,512]{2,1,0:T(8,128)(2,1)}, u32[]{:S(2)}) copy-start(bf16[3,512,512]{2,1,0:T(8,128)(2,1)} %weights.11) | copy-start | bytes 4718596
  29.6 8.4 %collective-permute-start.6 = (bf16[256,512]{1,0:T(8,128)(2,1)S(1)}, bf16[256,512]{1,0:T(8,128)(2,1)S(1)}, u32[]{:S(2)}, u32[]{:S(2)}) collective-permute-start(bf16[256,512]{1,0:T(8,128)(2,1)S(1)} %add_convert_fusion.1), channel_id=1, source_target_pairs={{0,2},{2,0},{1,3},{3,1},{4,6},{6,4},{5,7},{7,5},{8,10},{10,8},{9,1... | collective-permute-start | bytes 786440 | tf_op jit(solution)/shard_map/ppermute | solution.py:376
  38.1 1.6 %collective-permute-start.7 = (bf16[256,512]{1,0:T(8,128)(2,1)S(1)}, bf16[256,512]{1,0:T(8,128)(2,1)S(1)}, u32[]{:S(2)}, u32[]{:S(2)}) collective-permute-start(bf16[256,512]{1,0:T(8,128)(2,1)S(1)} %add_convert_fusion.refs_1_), channel_id=1, source_target_pairs={{0,1},{1,0},{2,3},{3,2},{4,5},{5,4},{6,7},{7,6},{8,9},{9,8},{10,11... | collective-permute-start | bytes 786440 | tf_op jit(solution)/shard_map/ppermute | solution.py:376
  41.3 4.3 %collective-permute-start.8 = (bf16[32,512]{1,0:T(8,128)(2,1)S(1)}, bf16[32,512]{1,0:T(8,128)(2,1)S(1)}, u32[]{:S(2)}, u32[]{:S(2)}) collective-permute-start(bf16[32,512]{1,0:T(8,128)(2,1)S(1)} %get-tuple-element.96), channel_id=1, source_target_pairs={{0,4},{1,9},{4,0},{5,13},{8,12},{9,1},{12,8},{13,5},{2,6},{3,11},{... | collective-permute-start | bytes 98312 | tf_op jit(solution)/shard_map/ppermute | solution.py:523
  42.7 2.9 %collective-permute-start.9 = (bf16[32,512]{1,0:T(8,128)(2,1)S(1)}, bf16[32,512]{1,0:T(8,128)(2,1)S(1)}, u32[]{:S(2)}, u32[]{:S(2)}) collective-permute-start(bf16[32,512]{1,0:T(8,128)(2,1)S(1)} %get-tuple-element.97), channel_id=1, source_target_pairs={{1,13},{5,9},{9,5},{13,1},{3,15},{7,11},{11,7},{15,3},{17,29},{21,... | collective-permute-start | bytes 98312 | tf_op jit(solution)/shard_map/ppermute | solution.py:526
  45.6 6.4 %copy-start.4 = (bf16[3,512,512]{2,1,0:T(8,128)(2,1)S(1)}, bf16[3,512,512]{2,1,0:T(8,128)(2,1)}, u32[]{:S(2)}) copy-start(bf16[3,512,512]{2,1,0:T(8,128)(2,1)} %refs_10_.9) | copy-start | bytes 4718596
  45.6 6.4 %copy-start.9 = (f32[3,512]{1,0:T(4,128)S(1)}, f32[3,512]{1,0:T(4,128)}, u32[]{:S(2)}) copy-start(f32[3,512]{1,0:T(4,128)} %refs_9_.10) | copy-start | bytes 18436
  45.6 5.8 %collective-permute-start.10 = (bf16[32,512]{1,0:T(8,128)(2,1)S(1)}, bf16[32,512]{1,0:T(8,128)(2,1)S(1)}, u32[]{:S(2)}, u32[]{:S(2)}) collective-permute-start(bf16[32,512]{1,0:T(8,128)(2,1)S(1)} %collective-permute-done.8.refs_3_), channel_id=1, source_target_pairs={{0,1},{1,0},{2,3},{3,2},{4,5},{5,4},{6,7},{7,6},{8,9},{9,8},{10,11... | collective-permute-start | bytes 98312 | tf_op jit(solution)/shard_map/ppermute | solution.py:530
  48.9 3.1 %collective-permute-start.11 = (bf16[32,512]{1,0:T(8,128)(2,1)S(1)}, bf16[32,512]{1,0:T(8,128)(2,1)S(1)}, u32[]{:S(2)}, u32[]{:S(2)}) collective-permute-start(bf16[32,512]{1,0:T(8,128)(2,1)S(1)} %collective-permute-done.9.refs_5_), channel_id=1, source_target_pairs={{1,0},{3,2},{5,4},{7,6},{9,8},{11,10},{13,12},{15,14},{17,16},{19,... | collective-permute-start | bytes 98312 | tf_op jit(solution)/shard_map/ppermute | solution.py:532
  55.2 4.0 %collective-permute-start.12 = (bf16[32,512]{1,0:T(8,128)(2,1)S(1)}, bf16[32,512]{1,0:T(8,128)(2,1)S(1)}, u32[]{:S(2)}, u32[]{:S(2)}) collective-permute-start(bf16[32,512]{1,0:T(8,128)(2,1)S(1)} %get-tuple-element.109), channel_id=1, source_target_pairs={{0,4},{1,9},{4,0},{5,13},{8,12},{9,1},{12,8},{13,5},{2,6},{3,11},{... | collective-permute-start | bytes 98312 | tf_op jit(solution)/shard_map/ppermute | solution.py:523
  55.3 3.8 %collective-permute-start.13 = (bf16[32,512]{1,0:T(8,128)(2,1)S(1)}, bf16[32,512]{1,0:T(8,128)(2,1)S(1)}, u32[]{:S(2)}, u32[]{:S(2)}) collective-permute-start(bf16[32,512]{1,0:T(8,128)(2,1)S(1)} %get-tuple-element.110), channel_id=1, source_target_pairs={{1,13},{5,9},{9,5},{13,1},{3,15},{7,11},{11,7},{15,3},{17,29},{21,... | collective-permute-start | bytes 98312 | tf_op jit(solution)/shard_map/ppermute | solution.py:526
  59.1 5.9 %collective-permute-start.14 = (bf16[32,512]{1,0:T(8,128)(2,1)S(1)}, bf16[32,512]{1,0:T(8,128)(2,1)S(1)}, u32[]{:S(2)}, u32[]{:S(2)}) collective-permute-start(bf16[32,512]{1,0:T(8,128)(2,1)S(1)} %collective-permute-done.12.refs_3_), channel_id=1, source_target_pairs={{0,1},{1,0},{2,3},{3,2},{4,5},{5,4},{6,7},{7,6},{8,9},{9,8},{10,11... | collective-permute-start | bytes 98312 | tf_op jit(solution)/shard_map/ppermute | solution.py:530
  62.3 3.1 %collective-permute-start.15 = (bf16[32,512]{1,0:T(8,128)(2,1)S(1)}, bf16[32,512]{1,0:T(8,128)(2,1)S(1)}, u32[]{:S(2)}, u32[]{:S(2)}) collective-permute-start(bf16[32,512]{1,0:T(8,128)(2,1)S(1)} %collective-permute-done.13.refs_5_), channel_id=1, source_target_pairs={{1,0},{3,2},{5,4},{7,6},{9,8},{11,10},{13,12},{15,14},{17,16},{19,... | collective-permute-start | bytes 98312 | tf_op jit(solution)/shard_map/ppermute | solution.py:532
  68.7 4.0 %collective-permute-start.16 = (bf16[32,512]{1,0:T(8,128)(2,1)S(1)}, bf16[32,512]{1,0:T(8,128)(2,1)S(1)}, u32[]{:S(2)}, u32[]{:S(2)}) collective-permute-start(bf16[32,512]{1,0:T(8,128)(2,1)S(1)} %get-tuple-element.119), channel_id=1, source_target_pairs={{0,4},{1,9},{4,0},{5,13},{8,12},{9,1},{12,8},{13,5},{2,6},{3,11},{... | collective-permute-start | bytes 98312 | tf_op jit(solution)/shard_map/ppermute | solution.py:523
  69.7 3.0 %collective-permute-start.17 = (bf16[32,512]{1,0:T(8,128)(2,1)S(1)}, bf16[32,512]{1,0:T(8,128)(2,1)S(1)}, u32[]{:S(2)}, u32[]{:S(2)}) collective-permute-start(bf16[32,512]{1,0:T(8,128)(2,1)S(1)} %get-tuple-element.120), channel_id=1, source_target_pairs={{1,13},{5,9},{9,5},{13,1},{3,15},{7,11},{11,7},{15,3},{17,29},{21,... | collective-permute-start | bytes 98312 | tf_op jit(solution)/shard_map/ppermute | solution.py:526
  72.6 7.2 %copy-start.6 = (bf16[512,512]{1,0:T(8,128)(2,1)S(1)}, bf16[512,512]{1,0:T(8,128)(2,1)}, u32[]{:S(2)}) copy-start(bf16[512,512]{1,0:T(8,128)(2,1)} %upstream.1) | copy-start | bytes 1572868
  72.6 6.6 %collective-permute-start.18 = (bf16[32,512]{1,0:T(8,128)(2,1)S(1)}, bf16[32,512]{1,0:T(8,128)(2,1)S(1)}, u32[]{:S(2)}, u32[]{:S(2)}) collective-permute-start(bf16[32,512]{1,0:T(8,128)(2,1)S(1)} %collective-permute-done.16.refs_3_), channel_id=1, source_target_pairs={{0,1},{1,0},{2,3},{3,2},{4,5},{5,4},{6,7},{7,6},{8,9},{9,8},{10,11... | collective-permute-start | bytes 98312 | tf_op jit(solution)/shard_map/ppermute | solution.py:530
  76.7 3.1 %collective-permute-start.19 = (bf16[32,512]{1,0:T(8,128)(2,1)S(1)}, bf16[32,512]{1,0:T(8,128)(2,1)S(1)}, u32[]{:S(2)}, u32[]{:S(2)}) collective-permute-start(bf16[32,512]{1,0:T(8,128)(2,1)S(1)} %collective-permute-done.17.refs_5_), channel_id=1, source_target_pairs={{1,0},{3,2},{5,4},{7,6},{9,8},{11,10},{13,12},{15,14},{17,16},{19,... | collective-permute-start | bytes 98312 | tf_op jit(solution)/shard_map/ppermute | solution.py:532
  85.5 3.9 %collective-permute-start.20 = (bf16[32,512]{1,0:T(8,128)(2,1)S(1)}, bf16[32,512]{1,0:T(8,128)(2,1)S(1)}, u32[]{:S(2)}, u32[]{:S(2)}) collective-permute-start(bf16[32,512]{1,0:T(8,128)(2,1)S(1)} %get-tuple-element.130), channel_id=1, source_target_pairs={{0,4},{1,9},{4,0},{5,13},{8,12},{9,1},{12,8},{13,5},{2,6},{3,11},{... | collective-permute-start | bytes 98312 | tf_op jit(solution)/shard_map/ppermute | solution.py:523
  85.7 3.7 %collective-permute-start.21 = (bf16[32,512]{1,0:T(8,128)(2,1)S(1)}, bf16[32,512]{1,0:T(8,128)(2,1)S(1)}, u32[]{:S(2)}, u32[]{:S(2)}) collective-permute-start(bf16[32,512]{1,0:T(8,128)(2,1)S(1)} %get-tuple-element.131), channel_id=1, source_target_pairs={{1,13},{5,9},{9,5},{13,1},{3,15},{7,11},{11,7},{15,3},{17,29},{21,... | collective-permute-start | bytes 98312 | tf_op jit(solution)/shard_map/ppermute | solution.py:526
  89.4 6.2 %collective-permute-start.22 = (bf16[32,512]{1,0:T(8,128)(2,1)S(1)}, bf16[32,512]{1,0:T(8,128)(2,1)S(1)}, u32[]{:S(2)}, u32[]{:S(2)}) collective-permute-start(bf16[32,512]{1,0:T(8,128)(2,1)S(1)} %collective-permute-done.20.refs_1_), channel_id=1, source_target_pairs={{0,1},{1,0},{2,3},{3,2},{4,5},{5,4},{6,7},{7,6},{8,9},{9,8},{10,11... | collective-permute-start | bytes 98312 | tf_op jit(solution)/shard_map/ppermute | solution.py:530
  92.6 3.1 %collective-permute-start.23 = (bf16[32,512]{1,0:T(8,128)(2,1)S(1)}, bf16[32,512]{1,0:T(8,128)(2,1)S(1)}, u32[]{:S(2)}, u32[]{:S(2)}) collective-permute-start(bf16[32,512]{1,0:T(8,128)(2,1)S(1)} %collective-permute-done.21.refs_3_), channel_id=1, source_target_pairs={{1,0},{3,2},{5,4},{7,6},{9,8},{11,10},{13,12},{15,14},{17,16},{19,... | collective-permute-start | bytes 98312 | tf_op jit(solution)/shard_map/ppermute | solution.py:532
  98.2 4.0 %collective-permute-start.24 = (bf16[32,512]{1,0:T(8,128)(2,1)S(1)}, bf16[32,512]{1,0:T(8,128)(2,1)S(1)}, u32[]{:S(2)}, u32[]{:S(2)}) collective-permute-start(bf16[32,512]{1,0:T(8,128)(2,1)S(1)} %get-tuple-element.139), channel_id=1, source_target_pairs={{0,4},{1,9},{4,0},{5,13},{8,12},{9,1},{12,8},{13,5},{2,6},{3,11},{... | collective-permute-start | bytes 98312 | tf_op jit(solution)/shard_map/ppermute | solution.py:523
  99.2 3.0 %collective-permute-start.25 = (bf16[32,512]{1,0:T(8,128)(2,1)S(1)}, bf16[32,512]{1,0:T(8,128)(2,1)S(1)}, u32[]{:S(2)}, u32[]{:S(2)}) collective-permute-start(bf16[32,512]{1,0:T(8,128)(2,1)S(1)} %get-tuple-element.140), channel_id=1, source_target_pairs={{1,13},{5,9},{9,5},{13,1},{3,15},{7,11},{11,7},{15,3},{17,29},{21,... | collective-permute-start | bytes 98312 | tf_op jit(solution)/shard_map/ppermute | solution.py:526
  102.2 7.0 %collective-permute-start.26 = (bf16[32,512]{1,0:T(8,128)(2,1)S(1)}, bf16[32,512]{1,0:T(8,128)(2,1)S(1)}, u32[]{:S(2)}, u32[]{:S(2)}) collective-permute-start(bf16[32,512]{1,0:T(8,128)(2,1)S(1)} %collective-permute-done.24.refs_1_), channel_id=1, source_target_pairs={{0,1},{1,0},{2,3},{3,2},{4,5},{5,4},{6,7},{7,6},{8,9},{9,8},{10,11... | collective-permute-start | bytes 98312 | tf_op jit(solution)/shard_map/ppermute | solution.py:530
  106.4 3.1 %collective-permute-start.27 = (bf16[32,512]{1,0:T(8,128)(2,1)S(1)}, bf16[32,512]{1,0:T(8,128)(2,1)S(1)}, u32[]{:S(2)}, u32[]{:S(2)}) collective-permute-start(bf16[32,512]{1,0:T(8,128)(2,1)S(1)} %collective-permute-done.25.refs_3_), channel_id=1, source_target_pairs={{1,0},{3,2},{5,4},{7,6},{9,8},{11,10},{13,12},{15,14},{17,16},{19,... | collective-permute-start | bytes 98312 | tf_op jit(solution)/shard_map/ppermute | solution.py:532
  112.1 4.0 %collective-permute-start.28 = (bf16[32,512]{1,0:T(8,128)(2,1)S(1)}, bf16[32,512]{1,0:T(8,128)(2,1)S(1)}, u32[]{:S(2)}, u32[]{:S(2)}) collective-permute-start(bf16[32,512]{1,0:T(8,128)(2,1)S(1)} %get-tuple-element.148), channel_id=1, source_target_pairs={{0,4},{1,9},{4,0},{5,13},{8,12},{9,1},{12,8},{13,5},{2,6},{3,11},{... | collective-permute-start | bytes 98312 | tf_op jit(solution)/shard_map/ppermute | solution.py:523
  112.3 3.7 %collective-permute-start.29 = (bf16[32,512]{1,0:T(8,128)(2,1)S(1)}, bf16[32,512]{1,0:T(8,128)(2,1)S(1)}, u32[]{:S(2)}, u32[]{:S(2)}) collective-permute-start(bf16[32,512]{1,0:T(8,128)(2,1)S(1)} %get-tuple-element.149), channel_id=1, source_target_pairs={{1,13},{5,9},{9,5},{13,1},{3,15},{7,11},{11,7},{15,3},{17,29},{21,... | collective-permute-start | bytes 98312 | tf_op jit(solution)/shard_map/ppermute | solution.py:526
  116.0 6.2 %collective-permute-start.30 = (bf16[32,512]{1,0:T(8,128)(2,1)S(1)}, bf16[32,512]{1,0:T(8,128)(2,1)S(1)}, u32[]{:S(2)}, u32[]{:S(2)}) collective-permute-start(bf16[32,512]{1,0:T(8,128)(2,1)S(1)} %collective-permute-done.28.refs_1_), channel_id=1, source_target_pairs={{0,1},{1,0},{2,3},{3,2},{4,5},{5,4},{6,7},{7,6},{8,9},{9,8},{10,11... | collective-permute-start | bytes 98312 | tf_op jit(solution)/shard_map/ppermute | solution.py:530
  119.5 3.1 %collective-permute-start.31 = (bf16[32,512]{1,0:T(8,128)(2,1)S(1)}, bf16[32,512]{1,0:T(8,128)(2,1)S(1)}, u32[]{:S(2)}, u32[]{:S(2)}) collective-permute-start(bf16[32,512]{1,0:T(8,128)(2,1)S(1)} %collective-permute-done.29.refs_3_), channel_id=1, source_target_pairs={{1,0},{3,2},{5,4},{7,6},{9,8},{11,10},{13,12},{15,14},{17,16},{19,... | collective-permute-start | bytes 98312 | tf_op jit(solution)/shard_map/ppermute | solution.py:532
  124.0 6.4 %collective-permute-start.32 = (bf16[128,512]{1,0:T(8,128)(2,1)S(1)}, bf16[128,512]{1,0:T(8,128)(2,1)S(1)}, u32[]{:S(2)}, u32[]{:S(2)}) collective-permute-start(bf16[128,512]{1,0:T(8,128)(2,1)S(1)} %get-tuple-element.167), channel_id=1, source_target_pairs={{4,0},{0,4},{12,8},{8,12},{5,1},{1,5},{13,9},{9,13},{6,2},{2,6},{1... | collective-permute-start | bytes 393224 | tf_op jit(solution)/shard_map/ppermute | solution.py:390
  124.9 8.6 %collective-permute-start.34 = (bf16[128,512]{1,0:T(8,128)(2,1)S(1)}, bf16[128,512]{1,0:T(8,128)(2,1)S(1)}, u32[]{:S(2)}, u32[]{:S(2)}) collective-permute-start(bf16[128,512]{1,0:T(8,128)(2,1)S(1)} %get-tuple-element.170), channel_id=1, source_target_pairs={{4,0},{0,4},{12,8},{8,12},{5,1},{1,5},{13,9},{9,13},{6,2},{2,6},{1... | collective-permute-start | bytes 393224 | tf_op jit(solution)/shard_map/ppermute | solution.py:390
  126.1 21.1 %copy-start.1 = (s32[1,4,32]{2,1,0:T(4,128)S(1)}, s32[1,4,32]{2,1,0:T(4,128)}, u32[]{:S(2)}) copy-start(s32[1,4,32]{2,1,0:T(4,128)} %param.22) | copy-start | bytes 1540
  130.4 15.4 %collective-permute-start.33 = (bf16[256,512]{1,0:T(8,128)(2,1)S(1)}, bf16[256,512]{1,0:T(8,128)(2,1)S(1)}, u32[]{:S(2)}, u32[]{:S(2)}) collective-permute-start(bf16[256,512]{1,0:T(8,128)(2,1)S(1)} %get-tuple-element.169), channel_id=1, source_target_pairs={{4,0},{0,4},{12,8},{8,12},{5,1},{1,5},{13,9},{9,13},{6,2},{2,6},{1... | collective-permute-start | bytes 786440 | tf_op jit(solution)/shard_map/ppermute | solution.py:390
  131.4 9.6 %collective-permute-start.36 = (bf16[128,512]{1,0:T(8,128)(2,1)S(1)}, bf16[128,512]{1,0:T(8,128)(2,1)S(1)}, u32[]{:S(2)}, u32[]{:S(2)}) collective-permute-start(bf16[128,512]{1,0:T(8,128)(2,1)S(1)} %get-tuple-element.171), channel_id=1, source_target_pairs={{8,0},{12,4},{0,8},{4,12},{9,1},{13,5},{1,9},{5,13},{10,2},{14,6},... | collective-permute-start | bytes 393224 | tf_op jit(solution)/shard_map/ppermute | solution.py:390
  133.5 12.3 %collective-permute-start.35 = (bf16[128,512]{1,0:T(8,128)(2,1)S(1)}, bf16[128,512]{1,0:T(8,128)(2,1)S(1)}, u32[]{:S(2)}, u32[]{:S(2)}) collective-permute-start(bf16[128,512]{1,0:T(8,128)(2,1)S(1)} %shard_map.193), channel_id=1, source_target_pairs={{8,0},{12,4},{0,8},{4,12},{9,1},{13,5},{1,9},{5,13},{10,2},{14,6},... | collective-permute-start | bytes 393224 | tf_op jit(solution)/shard_map/ppermute | solution.py:390

commit v5 on v4

--- a/solution.py
+++ b/solution.py
@@ -230,21 +230,21 @@
         pre[at : at + BLOCK, :] = dot(here[skip + at : skip + at + BLOCK, :], table[...])
 
 
-def stack_halo(halos, halo):
+def stack_halo(meta, halos, halo):
     at = 0
     for blocks in halos:
         rows = blocks[0][...]
         if len(blocks) > 1:
-            rows = (rows.astype(f32) + blocks[1][...].astype(f32)).astype(bf16)
+            rows = jnp.where(meta[0] == 1, rows.astype(f32), blocks[1][...].astype(f32)).astype(bf16)
         halo[at : at + rows.shape[0], :] = rows
         at += rows.shape[0]
     if at < halo.shape[0]:
         halo[at:, :] = jnp.zeros((halo.shape[0] - at, halo.shape[1]), bf16)
 
 
-def node_sum(pres, halos, halo_here, there, slope_out, halo, act_out):
+def node_sum(meta, pres, halos, halo_here, there, slope_out, halo, act_out):
     nodes = there.shape[0] // 2
-    stack_halo(halos, halo)
+    stack_halo(meta, halos, halo)
     half = pres[0].shape[0]
     for at in range(0, 2 * half, BLOCK):
         block = slice(at, at + BLOCK)
@@ -264,12 +264,12 @@
 
 
 def layer_kernel(layer, inward, spots, *refs):
-    hidden, pres = refs[0], refs[1:3]
-    halos, refs = split(refs[3:], inward)
+    meta, hidden, pres = refs[0], refs[1], refs[2:4]
+    halos, refs = split(refs[4:], inward)
     halo_here, there, w_out, gain, w_send, list_here = refs[:6]
     hidden_out, agg_out, slope_out, sent_out = refs[6:10]
     outs = refs[10:-2]
-    total = node_sum(pres, halos, halo_here, there, slope_out, *refs[-2:])
+    total = node_sum(meta, pres, halos, halo_here, there, slope_out, *refs[-2:])
     agg = dot(total.astype(bf16), w_out[layer])
     agg_out[...] = agg
     fresh = (hidden[...].astype(f32) + agg * norm_scale(agg) * gain[layer : layer + 1, :]).astype(bf16)
@@ -290,13 +290,13 @@
 
 
 def turn_kernel(layer, inward, spots, *refs):
-    hidden, pres = refs[0], refs[1:3]
-    halos, refs = split(refs[3:], inward)
+    meta, hidden, pres = refs[0], refs[1], refs[2:4]
+    halos, refs = split(refs[4:], inward)
     halo_here, there, w_out, gain, here, halo_there, cot = refs[:7]
     hidden_out, grad_pre = refs[7:9]
     outs = refs[9:-2]
     slope, halo = refs[-2:]
-    total = node_sum(pres, halos, halo_here, there, slope, halo, grad_pre)
+    total = node_sum(meta, pres, halos, halo_here, there, slope, halo, grad_pre)
     agg = dot(total.astype(bf16), w_out[layer])
     gain_row = gain[layer : layer + 1, :]
     hidden_out[...] = (hidden[...].astype(f32) + agg * norm_scale(agg) * gain_row).astype(bf16)
@@ -309,20 +309,20 @@
     rest[...] = upstream[...].astype(f32) + dot_back(sums, weights[layer])
 
 
-def arrived(rest, returned, list_there, w_send, halo):
-    stack_halo(returned, halo)
+def arrived(meta, rest, returned, list_there, w_send, halo):
+    stack_halo(meta, returned, halo)
     projected = dot_back(halo[...], w_send).astype(bf16)
     return rest[...] + dot(list_there[...], projected)
 
 
 def back_kernel(layer, inward, spots, *refs):
-    rest = refs[0]
-    returned, refs = split(refs[1:], inward)
+    meta, rest = refs[:2]
+    returned, refs = split(refs[2:], inward)
     list_there, w_send, agg, slope, gain, w_out, here, halo_there = refs[:8]
     upstream_out, grad_pre = refs[8:10]
     outs = refs[10:-1]
     halo = refs[-1]
-    upstream = arrived(rest, returned, list_there, w_send[layer + 1], halo)
+    upstream = arrived(meta, rest, returned, list_there, w_send[layer + 1], halo)
     upstream_out[...] = upstream
     grad_agg = norm_back(agg[...], gain[layer : layer + 1, :], upstream)
     edge_grads(grad_agg, w_out[layer], here, halo_there, slope, grad_pre, outs, spots)
@@ -333,11 +333,11 @@
 
 
 def finish_kernel(inward, *refs):
-    rest = refs[0]
-    returned, refs = split(refs[1:], inward)
+    meta, rest = refs[:2]
+    returned, refs = split(refs[2:], inward)
     list_there, w_send, enc_sum, gain, w_enc_out, pick, slope = refs[:7]
     spread_out, outs, halo = refs[7], refs[8:-1], refs[-1]
-    upstream = arrived(rest, returned, list_there, w_send[0], halo)
+    upstream = arrived(meta, rest, returned, list_there, w_send[0], halo)
     spread = dot_back(norm_back(enc_sum[...], gain[...], upstream).astype(bf16), w_enc_out[...]).astype(bf16)
     spread_out[...] = spread
     at = 0
@@ -523,13 +523,13 @@
         first = lax.ppermute(
             blocks[0], ("mesh", "rep"), [(2 * at + side, 2 * (at ^ 1 + side) + side) for at in range(4) for side in range(2)]
         )
-        third = lax.ppermute(blocks[1], ("mesh", "rep"), [(2 * at + 1, 2 * (at ^ 3) + 1) for at in range(4)])
+        third = lax.ppermute(blocks[1], ("mesh", "rep"), [(2 * at + side, 2 * (at ^ 3 * side) + side) for at in range(4) for side in range(2)])
         first, third, early = lax.optimization_barrier((first, third, early))
         return [
             first,
             lax.ppermute(first, "rep", [(0, 1), (1, 0)]),
             third,
-            lax.ppermute(third, "rep", [(1, 0)]),
+            lax.ppermute(third, "rep", [(0, 1), (1, 0)]),
         ], early
 
     hidden, enc_sum, sent, *outgoing = call(
@@ -549,7 +549,7 @@
         )(hidden, sent, here, w_recv)
         halos, (pre, both_tables) = exchange(outgoing, sent_to, early)
         (more,) = call(local_more_kernel, [half_f32], (), [half_product])(both_tables, here)
-        return hidden, pre, more, *halos
+        return meta, hidden, pre, more, *halos
 
     records = []
     for layer in range(LAYERS - 1):
@@ -583,7 +583,7 @@
                 [node_f32, edge_bf16] + listed,
                 [back_halo],
                 backward_products + [(listed_rows, width, width), (nodes, listed_rows, width)],
-            )(rest, *returned, list_there, w_send, agg, slope, layer_gain, w_out, here, halo_there)
+            )(meta, rest, *returned, list_there, w_send, agg, slope, layer_gain, w_out, here, halo_there)
     relayed = shards == 4
     pieces = 2 if relayed else 1
     piece = ((grid // pieces, width), bf16)
@@ -593,7 +593,7 @@
         [node_bf16] + [piece] * pieces,
         [back_halo],
         [square, (listed_rows, width, width), (nodes, listed_rows, width), one],
-    )(rest, *returned, list_there, w_send, enc_sum, enc_gain, w_enc_out, enc_picks[-1], enc_slopes[-1])
+    )(meta, rest, *returned, list_there, w_send, enc_sum, enc_gain, w_enc_out, enc_picks[-1], enc_slopes[-1])
     if relayed:
         passed = [sent_back(block, 1) for block in far]
     blocks = call(

time: 148 us -> 139 us (0.939)
  starting transfers between devices: 52.8 us -> 43.6 us
  Pallas kernels: 49.3 us -> 52.9 us
  waiting for transfers between devices: 41.2 us -> 38.8 us
    ppermute x12, starting transfers between devices: 12 us -> 4.39 us  [the longest x6 4.31 us: exchange(): lax.ppermute(blocks[1], ('mesh', 'rep'), [(2 * at + side, 2 * (at ^ 3 * s...]
    pallas_call x28, Pallas kernels: 49.3 us -> 52.9 us  [run(): pl.pallas_call(body, out_shape=tuple((jax.ShapeDtypeStruct(shape, dtype)...]
    ppermute x12, waiting for transfers between devices: 2.04 us -> 0.03 us  [the longest x6 0.02 us: exchange(): lax.ppermute(blocks[1], ('mesh', 'rep'), [(2 * at + side, 2 * (at ^ 3 * s...]
  transfers between devices with their start and end apart: 37 -> 37, of which waited for: 21 -> 16; matrix products, arithmetic and copies ran while one was open for 2% -> 2% of each run, Pallas kernels for 17% -> 18%
where the time goes in v5:
time: 139 us
  Pallas kernels  52.9 us (38%)
  starting transfers between devices  43.6 us (31%)
  waiting for transfers between devices  38.8 us (28%)
  other arithmetic  1.83 us (1%)
    pallas_call x28, Pallas kernels, run(): pl.pallas_call(body, out_shape=tuple((jax.ShapeDtypeStruct(shape, dtype)...  52.9 us
    ppermute x6, starting transfers between devices, exchange(): lax.ppermute(first, 'rep', [(0, 1), (1, 0)])  20 us
    ppermute x5, waiting for transfers between devices, sent_back(): lax.ppermute(value, 'mesh', [(partner(at, step, size), at) for at in rang...  14.9 us
    ppermute x5, waiting for transfers between devices, shifted(): lax.ppermute(value, axis, [(at, (at + by) % size) for at in range(size)])  12.4 us
    ppermute x6, waiting for transfers between devices, exchange(): lax.ppermute(blocks[0], ('mesh', 'rep'), [(2 * at + side, 2 * (at ^ 1 + s...  6.84 us
    ppermute x3, starting transfers between devices, sent_to(): lax.ppermute(value, 'mesh', [(at, partner(at, step, size)) for at in rang...  6.13 us
    ppermute x5, starting transfers between devices, sent_back(): lax.ppermute(value, 'mesh', [(partner(at, step, size), at) for at in rang...  6.06 us
    ppermute x3, waiting for transfers between devices, sent_to(): lax.ppermute(value, 'mesh', [(at, partner(at, step, size)) for at in rang...  4.6 us
  transfers between devices with their start and end apart: 37, of which 16 were waited for; matrix products, arithmetic and copies ran while one was open for 2% of the time, Pallas kernels for 18%

profile of v5, /device:TPU:0, one launch (start us, length us, event | category | flops | bytes accessed | tf_op | source)
XLA Modules:
  0.0 139.2 jit_solution(606493042509695829)
XLA Ops:
  0.6 1.0 shard_map.167.refs_5_
  1.6 3.1 %collective-permute-start.3 = (bf16[272,512]{1,0:T(8,128)(2,1)S(1)}, bf16[272,512]{1,0:T(8,128)(2,1)S(1)}, u32[]{:S(2)}, u32[]{:S(2)}) collective-permute-start(bf16[272,512]{1,0:T(8,128)(2,1)S(1)} %shard_map.167.refs_5_), channel_id=1, source_target_pairs={{0,4},{4,0},{8,12},{12,8},{1,5},{5,1},{9,13},{13,9},{2,6},{6,2},{1... | collective-permute-start | bytes 835592 | tf_op jit(solution)/shard_map/ppermute | solution.py:385
  4.7 2.6 %collective-permute-start = (bf16[272,512]{1,0:T(8,128)(2,1)S(1)}, bf16[272,512]{1,0:T(8,128)(2,1)S(1)}, u32[]{:S(2)}, u32[]{:S(2)}) collective-permute-start(bf16[272,512]{1,0:T(8,128)(2,1)S(1)} %shard_map.167.refs_5_), channel_id=1, source_target_pairs={{0,8},{4,12},{8,0},{12,4},{1,9},{5,13},{9,1},{13,5},{2,10},{6,14},... | collective-permute-start | bytes 835592 | tf_op jit(solution)/shard_map/ppermute | solution.py:385
  7.3 0.7 compare_select_fusion.1
  8.0 0.7 fusion.11
  10.1 1.6 %collective-permute-start.2 = (s32[2,2,512]{2,0,1:T(2,128)S(1)}, s32[2,2,512]{2,0,1:T(2,128)S(1)}, u32[]{:S(2)}, u32[]{:S(2)}) collective-permute-start(s32[2,2,512]{2,0,1:T(2,128)S(1)} %fusion.1), channel_id=1, source_target_pairs={{0,2},{2,0},{1,3},{3,1},{4,6},{6,4},{5,7},{7,5},{8,10},{10,8},{9,1... | collective-permute-start | bytes 24584 | tf_op jit(solution)/shard_map/ppermute | solution.py:376
  11.7 2.1 %collective-permute-done.2 = s32[2,2,512]{2,0,1:T(2,128)S(1)} collective-permute-done((s32[2,2,512]{2,0,1:T(2,128)S(1)}, s32[2,2,512]{2,0,1:T(2,128)S(1)}, u32[]{:S(2)}, u32[]{:S(2)}) %collective-permute-start.2) | collective-permute-done | bytes 8224 | tf_op jit(solution)/shard_map/ppermute | solution.py:376
  14.0 3.5 %shard_map.168 = (bf16[2048,1024]{1,0:T(8,128)(2,1)S(1)}, bf16[1024,2048]{1,0:T(8,128)(2,1)S(1)}, bf16[2048,128]{1,0:T(8,128)(2,1)S(1)}, bf16[128,2048]{1,0:T(8,...) custom-call(s32[1,2048]{1,0:T(1,128)S(1)} %fusion.2.slots, s32[1,2048]{1,0:T(1,128)S(1)} %bitcast.28, ...), custom_call_target="tpu_custom_call" | custom-call | flops 3221225472 | bytes 9650560 | tf_op jit(solution)/shard_map/pallas_call | solution.py:82
  17.5 2.3 %collective-permute-done.refs_4_ = bf16[272,512]{1,0:T(8,128)(2,1)S(1)} collective-permute-done((bf16[272,512]{1,0:T(8,128)(2,1)S(1)}, bf16[272,512]{1,0:T(8,128)(2,1)S(1)}, u32[]{:S(2)}, u32[]{:S(2)}) %collective-permute-start) | collective-permute-done | bytes 278560 | tf_op jit(solution)/shard_map/ppermute | solution.py:385
  20.3 2.2 %shard_map.169 = (bf16[256,512]{1,0:T(8,128)(2,1)S(1)}, bf16[256,512]{1,0:T(8,128)(2,1)S(1)}, bf16[256,512]{1,0:T(8,128)(2,1)S(1)}, bf16[256,512]{1,0:T(8,128)(2...) custom-call(s32[2]{0:T(128)S(1)} %pad_add_fusion.3.refs_0_, bf16[512,512]{1,0:T(8,128)(2,1)S(1)} %copy-done.8, ...), custom_call_target="tpu_custom_call" | custom-call | flops 1073741824 | bytes 4849672 | tf_op jit(solution)/shard_map/pallas_call | solution.py:82
  22.5 1.4 %shard_map.170 = (bf16[256,512]{1,0:T(8,128)(2,1)S(1)}, bf16[256,512]{1,0:T(8,128)(2,1)S(1)}, f32[512,512]{1,0:T(8,128)S(1)}) custom-call(s32[2]{0:T(128)S(1)} %pad_add_fusion.3.refs_0_, bf16[512,512]{1,0:T(8,128)(2,1)S(1)} %get-tuple-element.89.refs_1_, bf16[512,512]{1,0:T(8,128)(2,1)S(1)} %copy-done.5, f32[512,512]{1,0:T(8,128)S(1)} %get-tuple-element.90.refs_3_, ...), custom_call_target="tpu_custom_call" | custom-call | flops 402653184 | bytes 3948552 | tf_op jit(solution)/shard_map/pallas_call | solution.py:82
  24.0 2.3 %collective-permute-done.4.refs_4_ = bf16[272,512]{1,0:T(8,128)(2,1)S(1)} collective-permute-done((bf16[272,512]{1,0:T(8,128)(2,1)S(1)}, bf16[272,512]{1,0:T(8,128)(2,1)S(1)}, u32[]{:S(2)}, u32[]{:S(2)}) %collective-permute-start.4) | collective-permute-done | bytes 278560 | tf_op jit(solution)/shard_map/ppermute | solution.py:385
  26.3 1.6 %shard_map.171 = (bf16[256,512]{1,0:T(8,128)(2,1)S(1)}, bf16[256,512]{1,0:T(8,128)(2,1)S(1)}, f32[256,512]{1,0:T(8,128)S(1)}, bf16[256,512]{1,0:T(8,128)(2,1)S(1)}) custom-call(s32[2]{0:T(128)S(1)} %pad_add_fusion.3.refs_0_, bf16[512,512]{1,0:T(8,128)(2,1)S(1)} %get-tuple-element.89.refs_1_, bf16[512,512]{1,0:T(8,128)(2,1)S(1)} %copy-done.5, ...), custom_call_target="tpu_custom_call" | custom-call | flops 402653184 | bytes 3686408 | tf_op jit(solution)/shard_map/pallas_call | solution.py:82
  28.0 1.5 %collective-permute-done.5 = bf16[256,512]{1,0:T(8,128)(2,1)S(1)} collective-permute-done((bf16[256,512]{1,0:T(8,128)(2,1)S(1)}, bf16[256,512]{1,0:T(8,128)(2,1)S(1)}, u32[]{:S(2)}, u32[]{:S(2)}) %collective-permute-start.5) | collective-permute-done | bytes 262176 | tf_op jit(solution)/shard_map/ppermute | solution.py:376
  29.6 1.6 %collective-permute-start.6 = (bf16[256,512]{1,0:T(8,128)(2,1)S(1)}, bf16[256,512]{1,0:T(8,128)(2,1)S(1)}, u32[]{:S(2)}, u32[]{:S(2)}) collective-permute-start(bf16[256,512]{1,0:T(8,128)(2,1)S(1)} %add_convert_fusion.1), channel_id=1, source_target_pairs={{0,2},{2,0},{1,3},{3,1},{4,6},{6,4},{5,7},{7,5},{8,10},{10,8},{9,1... | collective-permute-start | bytes 786440 | tf_op jit(solution)/shard_map/ppermute | solution.py:376
  31.1 6.9 %collective-permute-done.6 = bf16[256,512]{1,0:T(8,128)(2,1)S(1)} collective-permute-done((bf16[256,512]{1,0:T(8,128)(2,1)S(1)}, bf16[256,512]{1,0:T(8,128)(2,1)S(1)}, u32[]{:S(2)}, u32[]{:S(2)}) %collective-permute-start.6) | collective-permute-done | bytes 262176 | tf_op jit(solution)/shard_map/ppermute | solution.py:376
  38.2 1.5 %collective-permute-done.7.refs_2_ = bf16[256,512]{1,0:T(8,128)(2,1)S(1)} collective-permute-done((bf16[256,512]{1,0:T(8,128)(2,1)S(1)}, bf16[256,512]{1,0:T(8,128)(2,1)S(1)}, u32[]{:S(2)}, u32[]{:S(2)}) %collective-permute-start.7) | collective-permute-done | bytes 262176 | tf_op jit(solution)/shard_map/ppermute | solution.py:376
  39.7 1.6 %shard_map.172 = (bf16[512,512]{1,0:T(8,128)(2,1)S(1)}, f32[512,512]{1,0:T(8,128)S(1)}, bf16[512,512]{1,0:T(8,128)(2,1)S(1)}, bf16[32,512]{1,0:T(8,128)(2,1)S(1)}, bf16[32,512]{1,0:T(8,128)(2,1)S(1)}) custom-call(s32[2]{0:T(128)S(1)} %pad_add_fusion.3.refs_0_, bf16[256,512]{1,0:T(8,128)(2,1)S(1)} %add_convert_fusion.refs_1_, ...), custom_call_target="tpu_custom_call" | custom-call | flops 587202560 | bytes 5408776 | tf_op jit(solution)/shard_map/pallas_call | solution.py:82
  41.2 1.4 %collective-permute-start.8 = (bf16[32,512]{1,0:T(8,128)(2,1)S(1)}, bf16[32,512]{1,0:T(8,128)(2,1)S(1)}, u32[]{:S(2)}, u32[]{:S(2)}) collective-permute-start(bf16[32,512]{1,0:T(8,128)(2,1)S(1)} %get-tuple-element.96), channel_id=1, source_target_pairs={{0,4},{1,9},{4,0},{5,13},{8,12},{9,1},{12,8},{13,5},{2,6},{3,11},{... | collective-permute-start | bytes 98312 | tf_op jit(solution)/shard_map/ppermute | solution.py:523
  42.7 0.7 collective-permute-start.9
  43.4 1.5 %shard_map.173 = (f32[1024,512]{1,0:T(8,128)S(1)}, bf16[1024,512]{1,0:T(8,128)(2,1)S(1)}) custom-call(bf16[512,512]{1,0:T(8,128)(2,1)S(1)} %get-tuple-element.95.hidden.refs_1_, bf16[512,512]{1,0:T(8,128)(2,1)S(1)} %get-tuple-element.98.sent, bf16[2048,1024]{1,0:T(8,128)(2,1)S(1)} %get-tuple-element.99.here.refs_12_, bf16[3,512,512]{2,1,0:T(8,128)(2,1)S(1)} %copy-done.3), custom_call_target="tpu_custom_call" | custom-call | flops 1342177280 | bytes 9961472 | tf_op jit(solution)/shard_map/pallas_call | solution.py:82
  44.9 0.7 collective-permute-done.8.refs_4_
  45.6 3.3 %collective-permute-start.10 = (bf16[32,512]{1,0:T(8,128)(2,1)S(1)}, bf16[32,512]{1,0:T(8,128)(2,1)S(1)}, u32[]{:S(2)}, u32[]{:S(2)}) collective-permute-start(bf16[32,512]{1,0:T(8,128)(2,1)S(1)} %collective-permute-done.8.refs_4_), channel_id=1, source_target_pairs={{0,1},{1,0},{2,3},{3,2},{4,5},{5,4},{6,7},{7,6},{8,9},{9,8},{10,11... | collective-permute-start | bytes 98312 | tf_op jit(solution)/shard_map/ppermute | solution.py:530
  48.9 1.2 shard_map.174.refs_3_
  50.2 3.8 %shard_map.175 = (bf16[512,512]{1,0:T(8,128)(2,1)S(1)}, f32[512,512]{1,0:T(8,128)S(1)}, bf16[2048,512]{1,0:T(8,128)(2,1)S(1)}, bf16[512,512]{1,0:T(8,128)(2,1)S(...) custom-call(s32[2]{0:T(128)S(1)} %pad_add_fusion.3.refs_0_, ...), custom_call_target="tpu_custom_call" | custom-call | flops 1929379840 | bytes 17078280 | tf_op jit(solution)/shard_map/pallas_call | solution.py:82
  54.2 0.8 collective-permute-start.13
  55.1 1.5 %shard_map.176 = (f32[1024,512]{1,0:T(8,128)S(1)}, bf16[1024,512]{1,0:T(8,128)(2,1)S(1)}) custom-call(bf16[512,512]{1,0:T(8,128)(2,1)S(1)} %get-tuple-element.108.hidden.refs_1_, bf16[512,512]{1,0:T(8,128)(2,1)S(1)} %get-tuple-element.111.sent, bf16[2048,1024]{1,0:T(8,128)(2,1)S(1)} %get-tuple-element.99.here.refs_12_, bf16[3,512,512]{2,1,0:T(8,128)(2,1)S(1)} %copy-done.3), custom_call_target="tpu_custom_call" | custom-call | flops 1342177280 | bytes 9961472 | tf_op jit(solution)/shard_map/pallas_call | solution.py:82
  56.6 1.4 %collective-permute-done.12.refs_4_ = bf16[32,512]{1,0:T(8,128)(2,1)S(1)} collective-permute-done((bf16[32,512]{1,0:T(8,128)(2,1)S(1)}, bf16[32,512]{1,0:T(8,128)(2,1)S(1)}, u32[]{:S(2)}, u32[]{:S(2)}) %collective-permute-start.12) | collective-permute-done | bytes 32800 | tf_op jit(solution)/shard_map/ppermute | solution.py:523
  58.0 3.0 %collective-permute-start.14 = (bf16[32,512]{1,0:T(8,128)(2,1)S(1)}, bf16[32,512]{1,0:T(8,128)(2,1)S(1)}, u32[]{:S(2)}, u32[]{:S(2)}) collective-permute-start(bf16[32,512]{1,0:T(8,128)(2,1)S(1)} %collective-permute-done.12.refs_4_), channel_id=1, source_target_pairs={{0,1},{1,0},{2,3},{3,2},{4,5},{5,4},{6,7},{7,6},{8,9},{9,8},{10,11... | collective-permute-start | bytes 98312 | tf_op jit(solution)/shard_map/ppermute | solution.py:530
  61.0 1.3 shard_map.177.refs_3_
  62.3 3.8 %shard_map.178 = (bf16[512,512]{1,0:T(8,128)(2,1)S(1)}, f32[512,512]{1,0:T(8,128)S(1)}, bf16[2048,512]{1,0:T(8,128)(2,1)S(1)}, bf16[512,512]{1,0:T(8,128)(2,1)S(...) custom-call(s32[2]{0:T(128)S(1)} %pad_add_fusion.3.refs_0_, ...), custom_call_target="tpu_custom_call" | custom-call | flops 1929379840 | bytes 17078280 | tf_op jit(solution)/shard_map/pallas_call | solution.py:82
  66.2 1.0 collective-permute-start.16
  67.2 0.7 collective-permute-start.17
  67.8 1.5 %shard_map.179 = (f32[1024,512]{1,0:T(8,128)S(1)}, bf16[1024,512]{1,0:T(8,128)(2,1)S(1)}) custom-call(bf16[512,512]{1,0:T(8,128)(2,1)S(1)} %get-tuple-element.118.hidden.refs_1_, bf16[512,512]{1,0:T(8,128)(2,1)S(1)} %get-tuple-element.121.sent, bf16[2048,1024]{1,0:T(8,128)(2,1)S(1)} %get-tuple-element.99.here.refs_12_, bf16[3,512,512]{2,1,0:T(8,128)(2,1)S(1)} %copy-done.3), custom_call_target="tpu_custom_call" | custom-call | flops 1342177280 | bytes 9961472 | tf_op jit(solution)/shard_map/pallas_call | solution.py:82
  69.4 0.7 collective-permute-done.16.refs_4_
  70.1 4.0 %collective-permute-start.18 = (bf16[32,512]{1,0:T(8,128)(2,1)S(1)}, bf16[32,512]{1,0:T(8,128)(2,1)S(1)}, u32[]{:S(2)}, u32[]{:S(2)}) collective-permute-start(bf16[32,512]{1,0:T(8,128)(2,1)S(1)} %collective-permute-done.16.refs_4_), channel_id=1, source_target_pairs={{0,1},{1,0},{2,3},{3,2},{4,5},{5,4},{6,7},{7,6},{8,9},{9,8},{10,11... | collective-permute-start | bytes 98312 | tf_op jit(solution)/shard_map/ppermute | solution.py:530
  74.1 1.3 shard_map.180.refs_3_
  75.4 6.3 %shard_map.181 = (bf16[512,512]{1,0:T(8,128)(2,1)}, bf16[2048,512]{1,0:T(8,128)(2,1)S(1)}, bf16[32,512]{1,0:T(8,128)(2,1)S(1)}, bf16[32,512]{1,0:T(8,128)(2,1)S(1)}) custom-call(s32[2]{0:T(128)S(1)} %pad_add_fusion.3.refs_0_, bf16[512,512]{1,0:T(8,128)(2,1)S(1)} %get-tuple-element.118.hidden.refs_1_, f32[1024,512]{1,0:T(8,128)S(1)} %get-tuple-element.124.refs_2_, ...), custom_call_target="tpu_custom_call" | custom-call | flops 3221225472 | bytes 19077128 | tf_op jit(solution)/shard_map/pallas_call | solution.py:82
  81.7 0.9 collective-permute-start.21
  82.6 1.5 %shard_map.182.upstream = f32[512,512]{1,0:T(8,128)S(1)} custom-call(bf16[512,512]{1,0:T(8,128)(2,1)S(1)} %copy-done.6, bf16[2048,512]{1,0:T(8,128)(2,1)S(1)} %get-tuple-element.132.grad_pre, bf16[1024,2048]{1,0:T(8,128)(2,1)S(1)} %get-tuple-element.107.refs_9_.there, bf16[3,512,512]{2,1,0:T(8,128)(2,1)S(1)} %copy-done.2), custom_call_target="tpu_custom_call" | custom-call | flops 1342177280 | bytes 9437184 | tf_op jit(solution)/shard_map/pallas_call | solution.py:82
  84.1 1.5 %collective-permute-done.20.refs_2_ = bf16[32,512]{1,0:T(8,128)(2,1)S(1)} collective-permute-done((bf16[32,512]{1,0:T(8,128)(2,1)S(1)}, bf16[32,512]{1,0:T(8,128)(2,1)S(1)}, u32[]{:S(2)}, u32[]{:S(2)}) %collective-permute-start.20) | collective-permute-done | bytes 32800 | tf_op jit(solution)/shard_map/ppermute | solution.py:523
  85.6 3.1 %collective-permute-start.22 = (bf16[32,512]{1,0:T(8,128)(2,1)S(1)}, bf16[32,512]{1,0:T(8,128)(2,1)S(1)}, u32[]{:S(2)}, u32[]{:S(2)}) collective-permute-start(bf16[32,512]{1,0:T(8,128)(2,1)S(1)} %collective-permute-done.20.refs_2_), channel_id=1, source_target_pairs={{0,1},{1,0},{2,3},{3,2},{4,5},{5,4},{6,7},{7,6},{8,9},{9,8},{10,11... | collective-permute-start | bytes 98312 | tf_op jit(solution)/shard_map/ppermute | solution.py:530
  88.7 1.5 %shard_map.183.refs_1_ = f32[512,512]{1,0:T(8,128)S(1)} custom-call(f32[512,512]{1,0:T(8,128)S(1)} %shard_map.182.upstream, bf16[2048,512]{1,0:T(8,128)(2,1)S(1)} %get-tuple-element.132.grad_pre, bf16[1024,2048]{1,0:T(8,128)(2,1)S(1)} %get-tuple-element.107.refs_9_.there, bf16[3,512,512]{2,1,0:T(8,128)(2,1)S(1)} %copy-done.3), custom_call_target="tpu_custom_call" | custom-call | flops 1342177280 | bytes 9961472 | tf_op jit(solution)/shard_map/pallas_call | solution.py:82
  90.2 3.2 %shard_map.184 = (f32[512,512]{1,0:T(8,128)S(1)}, bf16[2048,512]{1,0:T(8,128)(2,1)S(1)}, bf16[32,512]{1,0:T(8,128)(2,1)S(1)}, bf16[32,512]{1,0:T(8,128)(2,1)S(1)}) custom-call(s32[2]{0:T(128)S(1)} %pad_add_fusion.3.refs_0_, f32[512,512]{1,0:T(8,128)S(1)} %shard_map.183.refs_1_, bf16[32,512]{1,0:T(8,128)(2,1)S(1)} %collective-permute-done.20.refs_2_, ...), custom_call_target="tpu_custom_call" | custom-call | flops 1711276032 | bytes 15505416 | tf_op jit(solution)/shard_map/pallas_call | solution.py:82
  93.4 1.0 collective-permute-start.24
  95.0 1.5 %shard_map.185.upstream = f32[512,512]{1,0:T(8,128)S(1)} custom-call(f32[512,512]{1,0:T(8,128)S(1)} %get-tuple-element.141.upstream, bf16[2048,512]{1,0:T(8,128)(2,1)S(1)} %get-tuple-element.142.grad_pre, bf16[1024,2048]{1,0:T(8,128)(2,1)S(1)} %get-tuple-element.107.refs_9_.there, bf16[3,512,512]{2,1,0:T(8,128)(2,1)S(1)} %copy-done.2), custom_call_target="tpu_custom_call" | custom-call | flops 1342177280 | bytes 9961472 | tf_op jit(solution)/shard_map/pallas_call | solution.py:82
  96.5 0.8 collective-permute-done.24.refs_2_
  97.4 3.6 %collective-permute-start.26 = (bf16[32,512]{1,0:T(8,128)(2,1)S(1)}, bf16[32,512]{1,0:T(8,128)(2,1)S(1)}, u32[]{:S(2)}, u32[]{:S(2)}) collective-permute-start(bf16[32,512]{1,0:T(8,128)(2,1)S(1)} %collective-permute-done.24.refs_2_), channel_id=1, source_target_pairs={{0,1},{1,0},{2,3},{3,2},{4,5},{5,4},{6,7},{7,6},{8,9},{9,8},{10,11... | collective-permute-start | bytes 98312 | tf_op jit(solution)/shard_map/ppermute | solution.py:530
  101.0 1.5 %shard_map.186.refs_1_ = f32[512,512]{1,0:T(8,128)S(1)} custom-call(f32[512,512]{1,0:T(8,128)S(1)} %shard_map.185.upstream, bf16[2048,512]{1,0:T(8,128)(2,1)S(1)} %get-tuple-element.142.grad_pre, bf16[1024,2048]{1,0:T(8,128)(2,1)S(1)} %get-tuple-element.107.refs_9_.there, bf16[3,512,512]{2,1,0:T(8,128)(2,1)S(1)} %copy-done.3), custom_call_target="tpu_custom_call" | custom-call | flops 1342177280 | bytes 9961472 | tf_op jit(solution)/shard_map/pallas_call | solution.py:82
  102.5 3.2 %shard_map.187 = (f32[512,512]{1,0:T(8,128)S(1)}, bf16[2048,512]{1,0:T(8,128)(2,1)S(1)}, bf16[32,512]{1,0:T(8,128)(2,1)S(1)}, bf16[32,512]{1,0:T(8,128)(2,1)S(1)}) custom-call(s32[2]{0:T(128)S(1)} %pad_add_fusion.3.refs_0_, f32[512,512]{1,0:T(8,128)S(1)} %shard_map.186.refs_1_, bf16[32,512]{1,0:T(8,128)(2,1)S(1)} %collective-permute-done.24.refs_2_, ...), custom_call_target="tpu_custom_call" | custom-call | flops 1711276032 | bytes 15505416 | tf_op jit(solution)/shard_map/pallas_call | solution.py:82
  106.4 1.5 %shard_map.188.upstream = f32[512,512]{1,0:T(8,128)S(1)} custom-call(f32[512,512]{1,0:T(8,128)S(1)} %get-tuple-element.150.upstream, bf16[2048,512]{1,0:T(8,128)(2,1)S(1)} %get-tuple-element.151.grad_pre, bf16[1024,2048]{1,0:T(8,128)(2,1)S(1)} %get-tuple-element.107.refs_9_.there, bf16[3,512,512]{2,1,0:T(8,128)(2,1)S(1)} %copy-done.2), custom_call_target="tpu_custom_call" | custom-call | flops 1342177280 | bytes 9961472 | tf_op jit(solution)/shard_map/pallas_call | solution.py:82
  108.0 1.7 %collective-permute-done.28.refs_2_ = bf16[32,512]{1,0:T(8,128)(2,1)S(1)} collective-permute-done((bf16[32,512]{1,0:T(8,128)(2,1)S(1)}, bf16[32,512]{1,0:T(8,128)(2,1)S(1)}, u32[]{:S(2)}, u32[]{:S(2)}) %collective-permute-start.28) | collective-permute-done | bytes 32800 | tf_op jit(solution)/shard_map/ppermute | solution.py:523
  109.6 3.1 %collective-permute-start.30 = (bf16[32,512]{1,0:T(8,128)(2,1)S(1)}, bf16[32,512]{1,0:T(8,128)(2,1)S(1)}, u32[]{:S(2)}, u32[]{:S(2)}) collective-permute-start(bf16[32,512]{1,0:T(8,128)(2,1)S(1)} %collective-permute-done.28.refs_2_), channel_id=1, source_target_pairs={{0,1},{1,0},{2,3},{3,2},{4,5},{5,4},{6,7},{7,6},{8,9},{9,8},{10,11... | collective-permute-start | bytes 98312 | tf_op jit(solution)/shard_map/ppermute | solution.py:530
  112.7 1.5 %shard_map.189.refs_1_ = f32[512,512]{1,0:T(8,128)S(1)} custom-call(f32[512,512]{1,0:T(8,128)S(1)} %shard_map.188.upstream, bf16[2048,512]{1,0:T(8,128)(2,1)S(1)} %get-tuple-element.151.grad_pre, bf16[1024,2048]{1,0:T(8,128)(2,1)S(1)} %get-tuple-element.107.refs_9_.there, bf16[3,512,512]{2,1,0:T(8,128)(2,1)S(1)} %copy-done.3), custom_call_target="tpu_custom_call" | custom-call | flops 1342177280 | bytes 9961472 | tf_op jit(solution)/shard_map/pallas_call | solution.py:82
  114.3 2.0 %shard_map.190 = (bf16[512,512]{1,0:T(8,128)(2,1)S(1)}, bf16[128,512]{1,0:T(8,128)(2,1)S(1)}, bf16[128,512]{1,0:T(8,128)(2,1)S(1)}) custom-call(s32[2]{0:T(128)S(1)} %pad_add_fusion.3.refs_0_, f32[512,512]{1,0:T(8,128)S(1)} %shard_map.189.refs_1_, bf16[32,512]{1,0:T(8,128)(2,1)S(1)} %collective-permute-done.28.refs_2_, ...), custom_call_target="tpu_custom_call" | custom-call | flops 503316480 | bytes 5736456 | tf_op jit(solution)/shard_map/pallas_call | solution.py:82
  116.2 1.0 collective-permute-start.32
  117.2 1.1 collective-permute-start.34
  118.9 3.7 %collective-permute-done.32.passed = bf16[128,512]{1,0:T(8,128)(2,1)S(1)} collective-permute-done((bf16[128,512]{1,0:T(8,128)(2,1)S(1)}, bf16[128,512]{1,0:T(8,128)(2,1)S(1)}, u32[]{:S(2)}, u32[]{:S(2)}) %collective-permute-start.32) | collective-permute-done | bytes 131104 | tf_op jit(solution)/shard_map/ppermute | solution.py:390
  122.6 1.0 collective-permute-start.33
  123.6 2.1 %collective-permute-start.36 = (bf16[128,512]{1,0:T(8,128)(2,1)S(1)}, bf16[128,512]{1,0:T(8,128)(2,1)S(1)}, u32[]{:S(2)}, u32[]{:S(2)}) collective-permute-start(bf16[128,512]{1,0:T(8,128)(2,1)S(1)} %get-tuple-element.171), channel_id=1, source_target_pairs={{8,0},{12,4},{0,8},{4,12},{9,1},{13,5},{1,9},{5,13},{10,2},{14,6},... | collective-permute-start | bytes 393224 | tf_op jit(solution)/shard_map/ppermute | solution.py:390
  125.7 0.9 collective-permute-start.35
  126.6 6.6 %collective-permute-done.36.refs_3_ = bf16[128,512]{1,0:T(8,128)(2,1)S(1)} collective-permute-done((bf16[128,512]{1,0:T(8,128)(2,1)S(1)}, bf16[128,512]{1,0:T(8,128)(2,1)S(1)}, u32[]{:S(2)}, u32[]{:S(2)}) %collective-permute-start.36) | collective-permute-done | bytes 131104 | tf_op jit(solution)/shard_map/ppermute | solution.py:390
  133.2 4.7 %collective-permute-done.35.refs_2_ = bf16[128,512]{1,0:T(8,128)(2,1)S(1)} collective-permute-done((bf16[128,512]{1,0:T(8,128)(2,1)S(1)}, bf16[128,512]{1,0:T(8,128)(2,1)S(1)}, u32[]{:S(2)}, u32[]{:S(2)}) %collective-permute-start.35) | collective-permute-done | bytes 131104 | tf_op jit(solution)/shard_map/ppermute | solution.py:390
  137.9 1.3 shard_map.194
  (87 shorter events, 4.7 us)
Async XLA Ops:
  0.6 8.1 %copy-start = (s32[1,4,32]{2,1,0:T(4,128)S(1)}, s32[1,4,32]{2,1,0:T(4,128)}, u32[]{:S(2)}) copy-start(s32[1,4,32]{2,1,0:T(4,128)} %param.22) | copy-start | bytes 1540
  1.6 18.6 %collective-permute-start.3 = (bf16[272,512]{1,0:T(8,128)(2,1)S(1)}, bf16[272,512]{1,0:T(8,128)(2,1)S(1)}, u32[]{:S(2)}, u32[]{:S(2)}) collective-permute-start(bf16[272,512]{1,0:T(8,128)(2,1)S(1)} %shard_map.167.refs_5_), channel_id=1, source_target_pairs={{0,4},{4,0},{8,12},{12,8},{1,5},{5,1},{9,13},{13,9},{2,6},{6,2},{1... | collective-permute-start | bytes 835592 | tf_op jit(solution)/shard_map/ppermute | solution.py:385
  4.7 15.0 %collective-permute-start = (bf16[272,512]{1,0:T(8,128)(2,1)S(1)}, bf16[272,512]{1,0:T(8,128)(2,1)S(1)}, u32[]{:S(2)}, u32[]{:S(2)}) collective-permute-start(bf16[272,512]{1,0:T(8,128)(2,1)S(1)} %shard_map.167.refs_5_), channel_id=1, source_target_pairs={{0,8},{4,12},{8,0},{12,4},{1,9},{5,13},{9,1},{13,5},{2,10},{6,14},... | collective-permute-start | bytes 835592 | tf_op jit(solution)/shard_map/ppermute | solution.py:385
  8.7 1.2 collective-permute-start.1
  10.1 3.7 %collective-permute-start.2 = (s32[2,2,512]{2,0,1:T(2,128)S(1)}, s32[2,2,512]{2,0,1:T(2,128)S(1)}, u32[]{:S(2)}, u32[]{:S(2)}) collective-permute-start(s32[2,2,512]{2,0,1:T(2,128)S(1)} %fusion.1), channel_id=1, source_target_pairs={{0,2},{2,0},{1,3},{3,1},{4,6},{6,4},{5,7},{7,5},{8,10},{10,8},{9,1... | collective-permute-start | bytes 24584 | tf_op jit(solution)/shard_map/ppermute | solution.py:376
  13.9 6.4 %copy-start.5 = (bf16[512,512]{1,0:T(8,128)(2,1)S(1)}, bf16[512,512]{1,0:T(8,128)(2,1)}, u32[]{:S(2)}) copy-start(bf16[512,512]{1,0:T(8,128)(2,1)} %refs_4_.3) | copy-start | bytes 1572868
  13.9 6.3 %copy-start.8 = (bf16[512,512]{1,0:T(8,128)(2,1)S(1)}, bf16[512,512]{1,0:T(8,128)(2,1)}, u32[]{:S(2)}) copy-start(bf16[512,512]{1,0:T(8,128)(2,1)} %refs_3_.3) | copy-start | bytes 1572868
  14.0 6.3 %copy-start.11 = (bf16[512,512]{1,0:T(8,128)(2,1)S(1)}, bf16[512,512]{1,0:T(8,128)(2,1)}, u32[]{:S(2)}) copy-start(bf16[512,512]{1,0:T(8,128)(2,1)} %refs_3_.2) | copy-start | bytes 1572868
  19.8 6.5 %collective-permute-start.4 = (bf16[272,512]{1,0:T(8,128)(2,1)S(1)}, bf16[272,512]{1,0:T(8,128)(2,1)S(1)}, u32[]{:S(2)}, u32[]{:S(2)}) collective-permute-start(bf16[272,512]{1,0:T(8,128)(2,1)S(1)} %collective-permute-done.refs_4_), channel_id=1, source_target_pairs={{0,4},{4,0},{8,12},{12,8},{1,5},{5,1},{9,13},{13,9},{2,6},{6,2},{1... | collective-permute-start | bytes 835592 | tf_op jit(solution)/shard_map/ppermute | solution.py:385
  26.3 13.4 %copy-start.2 = (bf16[3,512,512]{2,1,0:T(8,128)(2,1)S(1)}, bf16[3,512,512]{2,1,0:T(8,128)(2,1)}, u32[]{:S(2)}) copy-start(bf16[3,512,512]{2,1,0:T(8,128)(2,1)} %refs_7_.5) | copy-start | bytes 4718596
  26.3 13.4 %copy-start.7 = (bf16[512,512]{1,0:T(8,128)(2,1)S(1)}, bf16[512,512]{1,0:T(8,128)(2,1)}, u32[]{:S(2)}) copy-start(bf16[512,512]{1,0:T(8,128)(2,1)} %refs_10_.11) | copy-start | bytes 1572868
  26.3 13.4 %copy-start.10 = (f32[512]{0:T(512)S(1)}, f32[512]{0:T(512)}, u32[]{:S(2)}) copy-start(f32[512]{0:T(512)} %param.26) | copy-start | bytes 6148
  27.9 1.6 %collective-permute-start.5 = (bf16[256,512]{1,0:T(8,128)(2,1)S(1)}, bf16[256,512]{1,0:T(8,128)(2,1)S(1)}, u32[]{:S(2)}, u32[]{:S(2)}) collective-permute-start(bf16[256,512]{1,0:T(8,128)(2,1)S(1)} %get-tuple-element.94), channel_id=1, source_target_pairs={{0,1},{1,0},{2,3},{3,2},{4,5},{5,4},{6,7},{7,6},{8,9},{9,8},{10,11... | collective-permute-start | bytes 786440 | tf_op jit(solution)/shard_map/ppermute | solution.py:376
  29.6 13.8 %copy-start.3 = (bf16[3,512,512]{2,1,0:T(8,128)(2,1)S(1)}, bf16[3,512,512]{2,1,0:T(8,128)(2,1)}, u32[]{:S(2)}) copy-start(bf16[3,512,512]{2,1,0:T(8,128)(2,1)} %weights.11) | copy-start | bytes 4718596
  29.6 8.4 %collective-permute-start.6 = (bf16[256,512]{1,0:T(8,128)(2,1)S(1)}, bf16[256,512]{1,0:T(8,128)(2,1)S(1)}, u32[]{:S(2)}, u32[]{:S(2)}) collective-permute-start(bf16[256,512]{1,0:T(8,128)(2,1)S(1)} %add_convert_fusion.1), channel_id=1, source_target_pairs={{0,2},{2,0},{1,3},{3,1},{4,6},{6,4},{5,7},{7,5},{8,10},{10,8},{9,1... | collective-permute-start | bytes 786440 | tf_op jit(solution)/shard_map/ppermute | solution.py:376
  38.1 1.6 %collective-permute-start.7 = (bf16[256,512]{1,0:T(8,128)(2,1)S(1)}, bf16[256,512]{1,0:T(8,128)(2,1)S(1)}, u32[]{:S(2)}, u32[]{:S(2)}) collective-permute-start(bf16[256,512]{1,0:T(8,128)(2,1)S(1)} %add_convert_fusion.refs_1_), channel_id=1, source_target_pairs={{0,1},{1,0},{2,3},{3,2},{4,5},{5,4},{6,7},{7,6},{8,9},{9,8},{10,11... | collective-permute-start | bytes 786440 | tf_op jit(solution)/shard_map/ppermute | solution.py:376
  41.2 4.3 %collective-permute-start.8 = (bf16[32,512]{1,0:T(8,128)(2,1)S(1)}, bf16[32,512]{1,0:T(8,128)(2,1)S(1)}, u32[]{:S(2)}, u32[]{:S(2)}) collective-permute-start(bf16[32,512]{1,0:T(8,128)(2,1)S(1)} %get-tuple-element.96), channel_id=1, source_target_pairs={{0,4},{1,9},{4,0},{5,13},{8,12},{9,1},{12,8},{13,5},{2,6},{3,11},{... | collective-permute-start | bytes 98312 | tf_op jit(solution)/shard_map/ppermute | solution.py:523
  42.7 2.9 %collective-permute-start.9 = (bf16[32,512]{1,0:T(8,128)(2,1)S(1)}, bf16[32,512]{1,0:T(8,128)(2,1)S(1)}, u32[]{:S(2)}, u32[]{:S(2)}) collective-permute-start(bf16[32,512]{1,0:T(8,128)(2,1)S(1)} %get-tuple-element.97), channel_id=1, source_target_pairs={{0,0},{1,13},{4,4},{5,9},{8,8},{9,5},{12,12},{13,1},{2,2},{3,15},{... | collective-permute-start | bytes 98312 | tf_op jit(solution)/shard_map/ppermute | solution.py:526
  45.6 4.6 %copy-start.4 = (bf16[3,512,512]{2,1,0:T(8,128)(2,1)S(1)}, bf16[3,512,512]{2,1,0:T(8,128)(2,1)}, u32[]{:S(2)}) copy-start(bf16[3,512,512]{2,1,0:T(8,128)(2,1)} %refs_11_.9) | copy-start | bytes 4718596
  45.6 4.6 %copy-start.9 = (f32[3,512]{1,0:T(4,128)S(1)}, f32[3,512]{1,0:T(4,128)}, u32[]{:S(2)}) copy-start(f32[3,512]{1,0:T(4,128)} %refs_10_.10) | copy-start | bytes 18436
  45.6 4.6 %collective-permute-start.10 = (bf16[32,512]{1,0:T(8,128)(2,1)S(1)}, bf16[32,512]{1,0:T(8,128)(2,1)S(1)}, u32[]{:S(2)}, u32[]{:S(2)}) collective-permute-start(bf16[32,512]{1,0:T(8,128)(2,1)S(1)} %collective-permute-done.8.refs_4_), channel_id=1, source_target_pairs={{0,1},{1,0},{2,3},{3,2},{4,5},{5,4},{6,7},{7,6},{8,9},{9,8},{10,11... | collective-permute-start | bytes 98312 | tf_op jit(solution)/shard_map/ppermute | solution.py:530
  48.9 1.3 collective-permute-start.11
  54.1 4.0 %collective-permute-start.12 = (bf16[32,512]{1,0:T(8,128)(2,1)S(1)}, bf16[32,512]{1,0:T(8,128)(2,1)S(1)}, u32[]{:S(2)}, u32[]{:S(2)}) collective-permute-start(bf16[32,512]{1,0:T(8,128)(2,1)S(1)} %get-tuple-element.109), channel_id=1, source_target_pairs={{0,4},{1,9},{4,0},{5,13},{8,12},{9,1},{12,8},{13,5},{2,6},{3,11},{... | collective-permute-start | bytes 98312 | tf_op jit(solution)/shard_map/ppermute | solution.py:523
  54.2 3.8 %collective-permute-start.13 = (bf16[32,512]{1,0:T(8,128)(2,1)S(1)}, bf16[32,512]{1,0:T(8,128)(2,1)S(1)}, u32[]{:S(2)}, u32[]{:S(2)}) collective-permute-start(bf16[32,512]{1,0:T(8,128)(2,1)S(1)} %get-tuple-element.110), channel_id=1, source_target_pairs={{0,0},{1,13},{4,4},{5,9},{8,8},{9,5},{12,12},{13,1},{2,2},{3,15},{... | collective-permute-start | bytes 98312 | tf_op jit(solution)/shard_map/ppermute | solution.py:526
  58.0 4.3 %collective-permute-start.14 = (bf16[32,512]{1,0:T(8,128)(2,1)S(1)}, bf16[32,512]{1,0:T(8,128)(2,1)S(1)}, u32[]{:S(2)}, u32[]{:S(2)}) collective-permute-start(bf16[32,512]{1,0:T(8,128)(2,1)S(1)} %collective-permute-done.12.refs_4_), channel_id=1, source_target_pairs={{0,1},{1,0},{2,3},{3,2},{4,5},{5,4},{6,7},{7,6},{8,9},{9,8},{10,11... | collective-permute-start | bytes 98312 | tf_op jit(solution)/shard_map/ppermute | solution.py:530
  61.0 1.3 collective-permute-start.15
  66.2 4.0 %collective-permute-start.16 = (bf16[32,512]{1,0:T(8,128)(2,1)S(1)}, bf16[32,512]{1,0:T(8,128)(2,1)S(1)}, u32[]{:S(2)}, u32[]{:S(2)}) collective-permute-start(bf16[32,512]{1,0:T(8,128)(2,1)S(1)} %get-tuple-element.119), channel_id=1, source_target_pairs={{0,4},{1,9},{4,0},{5,13},{8,12},{9,1},{12,8},{13,5},{2,6},{3,11},{... | collective-permute-start | bytes 98312 | tf_op jit(solution)/shard_map/ppermute | solution.py:523
  67.2 2.9 %collective-permute-start.17 = (bf16[32,512]{1,0:T(8,128)(2,1)S(1)}, bf16[32,512]{1,0:T(8,128)(2,1)S(1)}, u32[]{:S(2)}, u32[]{:S(2)}) collective-permute-start(bf16[32,512]{1,0:T(8,128)(2,1)S(1)} %get-tuple-element.120), channel_id=1, source_target_pairs={{0,0},{1,13},{4,4},{5,9},{8,8},{9,5},{12,12},{13,1},{2,2},{3,15},{... | collective-permute-start | bytes 98312 | tf_op jit(solution)/shard_map/ppermute | solution.py:526
  70.1 5.3 %copy-start.6 = (bf16[512,512]{1,0:T(8,128)(2,1)S(1)}, bf16[512,512]{1,0:T(8,128)(2,1)}, u32[]{:S(2)}) copy-start(bf16[512,512]{1,0:T(8,128)(2,1)} %upstream.1) | copy-start | bytes 1572868
  70.1 5.2 %collective-permute-start.18 = (bf16[32,512]{1,0:T(8,128)(2,1)S(1)}, bf16[32,512]{1,0:T(8,128)(2,1)S(1)}, u32[]{:S(2)}, u32[]{:S(2)}) collective-permute-start(bf16[32,512]{1,0:T(8,128)(2,1)S(1)} %collective-permute-done.16.refs_4_), channel_id=1, source_target_pairs={{0,1},{1,0},{2,3},{3,2},{4,5},{5,4},{6,7},{7,6},{8,9},{9,8},{10,11... | collective-permute-start | bytes 98312 | tf_op jit(solution)/shard_map/ppermute | solution.py:530
  74.1 1.3 collective-permute-start.19
  81.7 3.9 %collective-permute-start.20 = (bf16[32,512]{1,0:T(8,128)(2,1)S(1)}, bf16[32,512]{1,0:T(8,128)(2,1)S(1)}, u32[]{:S(2)}, u32[]{:S(2)}) collective-permute-start(bf16[32,512]{1,0:T(8,128)(2,1)S(1)} %get-tuple-element.130), channel_id=1, source_target_pairs={{0,4},{1,9},{4,0},{5,13},{8,12},{9,1},{12,8},{13,5},{2,6},{3,11},{... | collective-permute-start | bytes 98312 | tf_op jit(solution)/shard_map/ppermute | solution.py:523
  81.7 3.9 %collective-permute-start.21 = (bf16[32,512]{1,0:T(8,128)(2,1)S(1)}, bf16[32,512]{1,0:T(8,128)(2,1)S(1)}, u32[]{:S(2)}, u32[]{:S(2)}) collective-permute-start(bf16[32,512]{1,0:T(8,128)(2,1)S(1)} %get-tuple-element.131), channel_id=1, source_target_pairs={{0,0},{1,13},{4,4},{5,9},{8,8},{9,5},{12,12},{13,1},{2,2},{3,15},{... | collective-permute-start | bytes 98312 | tf_op jit(solution)/shard_map/ppermute | solution.py:526
  85.6 4.6 %collective-permute-start.22 = (bf16[32,512]{1,0:T(8,128)(2,1)S(1)}, bf16[32,512]{1,0:T(8,128)(2,1)S(1)}, u32[]{:S(2)}, u32[]{:S(2)}) collective-permute-start(bf16[32,512]{1,0:T(8,128)(2,1)S(1)} %collective-permute-done.20.refs_2_), channel_id=1, source_target_pairs={{0,1},{1,0},{2,3},{3,2},{4,5},{5,4},{6,7},{7,6},{8,9},{9,8},{10,11... | collective-permute-start | bytes 98312 | tf_op jit(solution)/shard_map/ppermute | solution.py:530
  88.7 1.5 %collective-permute-start.23 = (bf16[32,512]{1,0:T(8,128)(2,1)S(1)}, bf16[32,512]{1,0:T(8,128)(2,1)S(1)}, u32[]{:S(2)}, u32[]{:S(2)}) collective-permute-start(bf16[32,512]{1,0:T(8,128)(2,1)S(1)} %collective-permute-done.21.refs_4_), channel_id=1, source_target_pairs={{0,1},{1,0},{2,3},{3,2},{4,5},{5,4},{6,7},{7,6},{8,9},{9,8},{10,11... | collective-permute-start | bytes 98312 | tf_op jit(solution)/shard_map/ppermute | solution.py:532
  93.4 4.0 %collective-permute-start.24 = (bf16[32,512]{1,0:T(8,128)(2,1)S(1)}, bf16[32,512]{1,0:T(8,128)(2,1)S(1)}, u32[]{:S(2)}, u32[]{:S(2)}) collective-permute-start(bf16[32,512]{1,0:T(8,128)(2,1)S(1)} %get-tuple-element.139), channel_id=1, source_target_pairs={{0,4},{1,9},{4,0},{5,13},{8,12},{9,1},{12,8},{13,5},{2,6},{3,11},{... | collective-permute-start | bytes 98312 | tf_op jit(solution)/shard_map/ppermute | solution.py:523
  94.3 3.0 %collective-permute-start.25 = (bf16[32,512]{1,0:T(8,128)(2,1)S(1)}, bf16[32,512]{1,0:T(8,128)(2,1)S(1)}, u32[]{:S(2)}, u32[]{:S(2)}) collective-permute-start(bf16[32,512]{1,0:T(8,128)(2,1)S(1)} %get-tuple-element.140), channel_id=1, source_target_pairs={{0,0},{1,13},{4,4},{5,9},{8,8},{9,5},{12,12},{13,1},{2,2},{3,15},{... | collective-permute-start | bytes 98312 | tf_op jit(solution)/shard_map/ppermute | solution.py:526
  97.4 5.1 %collective-permute-start.26 = (bf16[32,512]{1,0:T(8,128)(2,1)S(1)}, bf16[32,512]{1,0:T(8,128)(2,1)S(1)}, u32[]{:S(2)}, u32[]{:S(2)}) collective-permute-start(bf16[32,512]{1,0:T(8,128)(2,1)S(1)} %collective-permute-done.24.refs_2_), channel_id=1, source_target_pairs={{0,1},{1,0},{2,3},{3,2},{4,5},{5,4},{6,7},{7,6},{8,9},{9,8},{10,11... | collective-permute-start | bytes 98312 | tf_op jit(solution)/shard_map/ppermute | solution.py:530
  101.0 1.5 %collective-permute-start.27 = (bf16[32,512]{1,0:T(8,128)(2,1)S(1)}, bf16[32,512]{1,0:T(8,128)(2,1)S(1)}, u32[]{:S(2)}, u32[]{:S(2)}) collective-permute-start(bf16[32,512]{1,0:T(8,128)(2,1)S(1)} %collective-permute-done.25.refs_4_), channel_id=1, source_target_pairs={{0,1},{1,0},{2,3},{3,2},{4,5},{5,4},{6,7},{7,6},{8,9},{9,8},{10,11... | collective-permute-start | bytes 98312 | tf_op jit(solution)/shard_map/ppermute | solution.py:532
  105.7 4.0 %collective-permute-start.28 = (bf16[32,512]{1,0:T(8,128)(2,1)S(1)}, bf16[32,512]{1,0:T(8,128)(2,1)S(1)}, u32[]{:S(2)}, u32[]{:S(2)}) collective-permute-start(bf16[32,512]{1,0:T(8,128)(2,1)S(1)} %get-tuple-element.148), channel_id=1, source_target_pairs={{0,4},{1,9},{4,0},{5,13},{8,12},{9,1},{12,8},{13,5},{2,6},{3,11},{... | collective-permute-start | bytes 98312 | tf_op jit(solution)/shard_map/ppermute | solution.py:523
  105.8 3.9 %collective-permute-start.29 = (bf16[32,512]{1,0:T(8,128)(2,1)S(1)}, bf16[32,512]{1,0:T(8,128)(2,1)S(1)}, u32[]{:S(2)}, u32[]{:S(2)}) collective-permute-start(bf16[32,512]{1,0:T(8,128)(2,1)S(1)} %get-tuple-element.149), channel_id=1, source_target_pairs={{0,0},{1,13},{4,4},{5,9},{8,8},{9,5},{12,12},{13,1},{2,2},{3,15},{... | collective-permute-start | bytes 98312 | tf_op jit(solution)/shard_map/ppermute | solution.py:526
  109.6 4.6 %collective-permute-start.30 = (bf16[32,512]{1,0:T(8,128)(2,1)S(1)}, bf16[32,512]{1,0:T(8,128)(2,1)S(1)}, u32[]{:S(2)}, u32[]{:S(2)}) collective-permute-start(bf16[32,512]{1,0:T(8,128)(2,1)S(1)} %collective-permute-done.28.refs_2_), channel_id=1, source_target_pairs={{0,1},{1,0},{2,3},{3,2},{4,5},{5,4},{6,7},{7,6},{8,9},{9,8},{10,11... | collective-permute-start | bytes 98312 | tf_op jit(solution)/shard_map/ppermute | solution.py:530
  112.7 1.5 %collective-permute-start.31 = (bf16[32,512]{1,0:T(8,128)(2,1)S(1)}, bf16[32,512]{1,0:T(8,128)(2,1)S(1)}, u32[]{:S(2)}, u32[]{:S(2)}) collective-permute-start(bf16[32,512]{1,0:T(8,128)(2,1)S(1)} %collective-permute-done.29.refs_4_), channel_id=1, source_target_pairs={{0,1},{1,0},{2,3},{3,2},{4,5},{5,4},{6,7},{7,6},{8,9},{9,8},{10,11... | collective-permute-start | bytes 98312 | tf_op jit(solution)/shard_map/ppermute | solution.py:532
  116.2 6.4 %collective-permute-start.32 = (bf16[128,512]{1,0:T(8,128)(2,1)S(1)}, bf16[128,512]{1,0:T(8,128)(2,1)S(1)}, u32[]{:S(2)}, u32[]{:S(2)}) collective-permute-start(bf16[128,512]{1,0:T(8,128)(2,1)S(1)} %get-tuple-element.167), channel_id=1, source_target_pairs={{4,0},{0,4},{12,8},{8,12},{5,1},{1,5},{13,9},{9,13},{6,2},{2,6},{1... | collective-permute-start | bytes 393224 | tf_op jit(solution)/shard_map/ppermute | solution.py:390
  117.2 8.5 %collective-permute-start.34 = (bf16[128,512]{1,0:T(8,128)(2,1)S(1)}, bf16[128,512]{1,0:T(8,128)(2,1)S(1)}, u32[]{:S(2)}, u32[]{:S(2)}) collective-permute-start(bf16[128,512]{1,0:T(8,128)(2,1)S(1)} %get-tuple-element.170), channel_id=1, source_target_pairs={{4,0},{0,4},{12,8},{8,12},{5,1},{1,5},{13,9},{9,13},{6,2},{2,6},{1... | collective-permute-start | bytes 393224 | tf_op jit(solution)/shard_map/ppermute | solution.py:390
  118.3 20.9 %copy-start.1 = (s32[1,4,32]{2,1,0:T(4,128)S(1)}, s32[1,4,32]{2,1,0:T(4,128)}, u32[]{:S(2)}) copy-start(s32[1,4,32]{2,1,0:T(4,128)} %param.22) | copy-start | bytes 1540
  122.6 15.3 %collective-permute-start.33 = (bf16[256,512]{1,0:T(8,128)(2,1)S(1)}, bf16[256,512]{1,0:T(8,128)(2,1)S(1)}, u32[]{:S(2)}, u32[]{:S(2)}) collective-permute-start(bf16[256,512]{1,0:T(8,128)(2,1)S(1)} %get-tuple-element.169), channel_id=1, source_target_pairs={{4,0},{0,4},{12,8},{8,12},{5,1},{1,5},{13,9},{9,13},{6,2},{2,6},{1... | collective-permute-start | bytes 786440 | tf_op jit(solution)/shard_map/ppermute | solution.py:390
  123.6 9.6 %collective-permute-start.36 = (bf16[128,512]{1,0:T(8,128)(2,1)S(1)}, bf16[128,512]{1,0:T(8,128)(2,1)S(1)}, u32[]{:S(2)}, u32[]{:S(2)}) collective-permute-start(bf16[128,512]{1,0:T(8,128)(2,1)S(1)} %get-tuple-element.171), channel_id=1, source_target_pairs={{8,0},{12,4},{0,8},{4,12},{9,1},{13,5},{1,9},{5,13},{10,2},{14,6},... | collective-permute-start | bytes 393224 | tf_op jit(solution)/shard_map/ppermute | solution.py:390
  125.7 12.2 %collective-permute-start.35 = (bf16[128,512]{1,0:T(8,128)(2,1)S(1)}, bf16[128,512]{1,0:T(8,128)(2,1)S(1)}, u32[]{:S(2)}, u32[]{:S(2)}) collective-permute-start(bf16[128,512]{1,0:T(8,128)(2,1)S(1)} %shard_map.193), channel_id=1, source_target_pairs={{8,0},{12,4},{0,8},{4,12},{9,1},{13,5},{1,9},{5,13},{10,2},{14,6},... | collective-permute-start | bytes 393224 | tf_op jit(solution)/shard_map/ppermute | solution.py:390

commit v6 on v4

--- a/solution.py
+++ b/solution.py
@@ -78,7 +78,7 @@
         own = sum(size(*held) for held in scratch) + (10 << 20)
         moved = sum(array.dtype.itemsize * array.size for array in args) + sum(size(*out) for out in outs)
         limit = own if own + moved < 40 << 20 else min(own + moved, 60 << 20)
-        semaphores = [pltpu.SemaphoreType.DMA((len(args),))] if copied else []
+        semaphores = [pltpu.SemaphoreType.DMA((2 + len(outs),))] if copied else []
         return pl.pallas_call(
             body,
             out_shape=tuple(jax.ShapeDtypeStruct(shape, dtype) for shape, dtype in outs),
@@ -118,29 +118,43 @@
 
 
 def note_kernel(rows, shards, nodes, payload, shard_rows, node_rows, arrived):
-    grid = rows.shape[0]
+    grid = shards.shape[1]
+    first = payload.shape[0] - EXTRA
     copies = [
-        pltpu.make_async_copy(rows, payload.at[0:grid], arrived.at[0]),
-        pltpu.make_async_copy(shards, shard_rows, arrived.at[1]),
-        pltpu.make_async_copy(nodes, node_rows, arrived.at[2]),
+        pltpu.make_async_copy(shards, shard_rows, arrived.at[0]),
+        pltpu.make_async_copy(nodes, node_rows, arrived.at[1]),
+        pltpu.make_async_copy(rows.at[0:first], payload.at[0:first], arrived.at[2]),
     ]
     for copy in copies:
         copy.start()
-    copies[1].wait()
-    copies[2].wait()
+    for copy in copies[:2]:
+        copy.wait()
     row = lax.broadcasted_iota(i32, (EXTRA, grid), 0)
     notes = jnp.full((EXTRA, grid), -1, i32)
     for top in range(shards.shape[0]):
         node = node_rows[top : top + 1, :]
         for at, value in enumerate((shard_rows[top : top + 1, :], node & 255, node >> 8)):
             notes = jnp.where(row == 3 * top + at, value, notes)
-    payload[grid:, 0:grid] = notes.astype(f32).astype(bf16)
+    payload[first:, 0:grid] = notes.astype(f32).astype(bf16)
     if grid < payload.shape[1]:
-        payload[grid:, grid:] = jnp.zeros((EXTRA, payload.shape[1] - grid), bf16)
-    copies[0].wait()
-
-
-def encode_kernel(steps, first, last, halves, *refs):
+        payload[first:, grid:] = jnp.zeros((EXTRA, payload.shape[1] - grid), bf16)
+    copies[2].wait()
+
+
+def left_kernel(first, rows, notes, _, left, payload, arrived):
+    grid = rows.shape[0]
+    copies = [
+        pltpu.make_async_copy(rows.at[first:], left, arrived.at[0]),
+        pltpu.make_async_copy(rows, payload.at[0:grid], arrived.at[1]),
+        pltpu.make_async_copy(notes.at[first:], payload.at[grid:], arrived.at[2]),
+    ]
+    for copy in copies:
+        copy.start()
+    for copy in copies:
+        copy.wait()
+
+
+def encode_kernel(counts, first, last, halves, *refs):
     refs = list(refs)
     meta, base, w_grid = refs[:3]
     del refs[:3]
@@ -150,24 +164,28 @@
     else:
         total_in = refs.pop(0)
         projected = base[...]
-    payloads = refs[:steps]
-    del refs[:steps]
+    payloads = []
+    for count in counts:
+        payloads.append(refs[:count])
+        del refs[:count]
+    steps = len(counts)
     picks, slopes = refs[:steps], refs[steps : 2 * steps]
     del refs[: 2 * steps]
     total = None if first else total_in[...]
     nodes = projected.shape[0]
     for payload, pick, slope_out in zip(payloads, picks, slopes):
         grid = pick.shape[0]
-        notes = payload[grid:, 0:grid].astype(f32)
+        rows = jnp.concatenate([piece[0 : grid // len(payload), :] for piece in payload], axis=0)
+        notes = payload[0][grid // len(payload) :, 0:grid].astype(f32)
         target = jnp.full((1, grid), -1.0, f32)
         for at in range(0, notes.shape[0] // 3 * 3, 3):
-            named = notes[at : at + 1] == meta[1].astype(f32)
+            named = notes[at : at + 1] == meta[1:2, 0:grid].astype(f32)
             target = jnp.where(named, notes[at + 1 : at + 2] + 256.0 * notes[at + 2 : at + 3], target)
         target = target.astype(i32)
         column = jnp.concatenate([upright(target[:, at : at + LANES]) for at in range(0, grid, LANES)], axis=0)
         picked = pick_rows(column, 0, nodes)
         pick[...] = picked
-        pre = dot(payload[0:grid, :], w_grid[...]) + dot(picked, projected)
+        pre = dot(rows, w_grid[...]) + dot(picked, projected)
         act, slope = gated(pre)
         slope_out[...] = slope.astype(bf16)
         added = dot(pick_columns(target, 0, nodes), act.astype(bf16))
@@ -177,13 +195,15 @@
     if not last:
         refs[0][...] = total
         return
-    keep, sends, whole = refs[0], refs[1:halves], refs[-1]
-    whole[...] = total
+    keep, sends = refs[0], refs[1:halves]
     part = nodes // halves
+    own = meta[0:1, :]
 
     def half(shift):
-        at = lax.rem(meta[0] + shift, halves)
-        return whole[pl.ds(pl.multiple_of(at * part, part), part), :]
+        rows = total[0:part]
+        for at in range(1, halves):
+            rows = jnp.where(own == (at - shift) % halves, total[at * part : (at + 1) * part], rows)
+        return rows
 
     keep[...] = half(0)
     for shift in range(1, halves):
@@ -204,9 +224,12 @@
     outs = refs[9 + halves : -1]
     whole = refs[-1]
     part = parts[0].shape[0]
-    for shift in range(halves):
-        at = lax.rem(meta[0] + shift, halves)
-        whole[pl.ds(pl.multiple_of(at * part, part), part), :] = parts[shift][...]
+    own = meta[0:1, :]
+    for at in range(halves):
+        rows = parts[0][...].astype(f32)
+        for shift in range(1, halves):
+            rows = jnp.where(own == (at - shift) % halves, parts[shift][...].astype(f32), rows)
+        whole[at * part : (at + 1) * part, :] = rows.astype(bf16)
     enc_sum = dot(whole[...], w_enc_out[...])
     enc_sum_out[...] = enc_sum
     hidden = (mesh_init[...].astype(f32) + enc_sum * norm_scale(enc_sum) * gain[...]).astype(bf16)
@@ -232,12 +255,9 @@
 
 def stack_halo(halos, halo):
     at = 0
-    for blocks in halos:
-        rows = blocks[0][...]
-        if len(blocks) > 1:
-            rows = (rows.astype(f32) + blocks[1][...].astype(f32)).astype(bf16)
-        halo[at : at + rows.shape[0], :] = rows
-        at += rows.shape[0]
+    for block in halos:
+        halo[at : at + block.shape[0], :] = block[...]
+        at += block.shape[0]
     if at < halo.shape[0]:
         halo[at:, :] = jnp.zeros((halo.shape[0] - at, halo.shape[1]), bf16)
 
@@ -255,17 +275,9 @@
     return dot(there[nodes:, :], act_out[...])
 
 
-def split(refs, inward):
-    groups = []
-    for count in inward:
-        groups.append(refs[:count])
-        refs = refs[count:]
-    return groups, refs
-
-
-def layer_kernel(layer, inward, spots, *refs):
+def layer_kernel(layer, shifts, spots, *refs):
     hidden, pres = refs[0], refs[1:3]
-    halos, refs = split(refs[3:], inward)
+    halos, refs = refs[3 : 3 + shifts], refs[3 + shifts :]
     halo_here, there, w_out, gain, w_send, list_here = refs[:6]
     hidden_out, agg_out, slope_out, sent_out = refs[6:10]
     outs = refs[10:-2]
@@ -289,9 +301,9 @@
     hand_out(dot(halo_there[...], grad_pre[...]), outs, spots)
 
 
-def turn_kernel(layer, inward, spots, *refs):
+def turn_kernel(layer, shifts, spots, *refs):
     hidden, pres = refs[0], refs[1:3]
-    halos, refs = split(refs[3:], inward)
+    halos, refs = refs[3 : 3 + shifts], refs[3 + shifts :]
     halo_here, there, w_out, gain, here, halo_there, cot = refs[:7]
     hidden_out, grad_pre = refs[7:9]
     outs = refs[9:-2]
@@ -315,9 +327,9 @@
     return rest[...] + dot(list_there[...], projected)
 
 
-def back_kernel(layer, inward, spots, *refs):
+def back_kernel(layer, shifts, spots, *refs):
     rest = refs[0]
-    returned, refs = split(refs[1:], inward)
+    returned, refs = refs[1 : 1 + shifts], refs[1 + shifts :]
     list_there, w_send, agg, slope, gain, w_out, here, halo_there = refs[:8]
     upstream_out, grad_pre = refs[8:10]
     outs = refs[10:-1]
@@ -332,43 +344,55 @@
     return (dot(pick, spread) * slope.astype(f32)).astype(bf16)
 
 
-def finish_kernel(inward, *refs):
+def finish_kernel(shifts, *refs):
     rest = refs[0]
-    returned, refs = split(refs[1:], inward)
-    list_there, w_send, enc_sum, gain, w_enc_out, pick, slope = refs[:7]
-    spread_out, outs, halo = refs[7], refs[8:-1], refs[-1]
+    returned, refs = refs[1 : 1 + shifts], refs[1 + shifts :]
+    list_there, w_send, enc_sum, gain, w_enc_out, pick, slope, spread_out = refs[:8]
+    outs, halo = refs[8:-1], refs[-1]
     upstream = arrived(rest, returned, list_there, w_send[0], halo)
     spread = dot_back(norm_back(enc_sum[...], gain[...], upstream).astype(bf16), w_enc_out[...]).astype(bf16)
     spread_out[...] = spread
     at = 0
     for out in outs:
-        piece = slice(at, at + out.shape[0])
-        out[...] = pair_grads(spread, pick[piece, :], slope[piece, :])
+        rows = slice(at, at + out.shape[0])
+        out[...] = pair_grads(spread, pick[rows, :], slope[rows, :])
         at += out.shape[0]
 
 
 def others_kernel(count, *refs):
     spread = refs[0][...]
     picks, slopes, outs = refs[1 : 1 + count], refs[1 + count : 1 + 2 * count], refs[1 + 2 * count :]
-    for pick, slope, out in zip(picks, slopes, outs):
-        out[...] = pair_grads(spread, pick[...], slope[...])
-
-
-def relay_kernel(first, count, own, passed, held, *refs):
+    for pick, slope, out in reversed(list(zip(picks, slopes, outs))):
+        skip = pick.shape[0] - out.shape[0]
+        out[...] = pair_grads(spread, pick[skip:, :], slope[skip:, :])
+
+
+def relay_kernel(first, own, passed, *refs):
     rows = passed.shape[0]
-    refs[0][...] = (own[first : first + rows, :].astype(f32) + passed[...].astype(f32)).astype(bf16)
-    if count > 1:
-        refs[1][...] = held[...]
+    out = refs[0] if len(refs) == 1 else refs[-2]
+    out[...] = (own[first : first + rows, :].astype(f32) + passed[...].astype(f32)).astype(bf16)
+    if len(refs) > 1:
+        refs[-1][...] = refs[0][...]
+
+
+def sum_kernel(own, piece, total):
+    total[...] = own[0 : piece.shape[0], :].astype(f32) + piece[...].astype(f32)
 
 
 def grid_kernel(whole, *refs):
-    blocks, pieces, w_grid, out = refs[:whole], refs[whole:-2], refs[-2], refs[-1]
-    step = out.shape[0] // max(len(pieces), 1)
-    for at in range(0, out.shape[0], step):
-        total = pieces[at // step][...].astype(f32) if pieces else 0.0
-        for block in blocks:
-            total = total + block[at : at + step, :].astype(f32)
-        out[at : at + step, :] = dot_back(total.astype(bf16), w_grid[...])
+    blocks, pieces, (w_grid, out) = refs[:whole], refs[whole:-2], refs[-2:]
+    if not pieces:
+        total = blocks[0][...].astype(f32)
+        for block in blocks[1:]:
+            total = total + block[...].astype(f32)
+        out[...] = dot_back(total.astype(bf16), w_grid[...])
+        return
+    (own, near), (summed, second) = blocks, pieces
+    first = summed.shape[0]
+    total = summed[...] + near[0:first, :].astype(f32)
+    out[0:first, :] = dot_back(total.astype(bf16), w_grid[...])
+    total = own[first:, :].astype(f32) + near[first:, :].astype(f32) + second[...].astype(f32)
+    out[first:, :] = dot_back(total.astype(bf16), w_grid[...])
 
 
 def shifted(value, axis, by):
@@ -426,14 +450,16 @@
     all_edges = edges * halves * feats
     enc_gain = enc_gain[None, :]
 
+    relayed = shards == 4
+    cuts = 2 if relayed else 1
+    piece_rows = grid // cuts
+    in_place = [pltpu.with_memory_space_constraint(array, pltpu.HBM) for array in (grid_feats, g2m_shard.T, g2m_node.T)]
     (payload,) = call(
-        note_kernel, [((grid + EXTRA, width), bf16)], [((tops, grid), i32), ((tops, grid), i32)], copied=True
-    )(*(pltpu.with_memory_space_constraint(array, pltpu.HBM) for array in (grid_feats, g2m_shard.T, g2m_node.T)))
-    if shards == 4:
-        across = sent_to(payload, 2)
-        payloads = [payload, sent_to(payload, 1), across]
-    else:
-        payloads = [payload] + [sent_to(payload, step) for step in range(1, shards)]
+        note_kernel,
+        [((piece_rows + EXTRA, width), bf16)],
+        [((tops, grid), i32), ((tops, grid), i32)],
+        copied=True,
+    )(*in_place)
 
     place = sender_slots - nodes
     away = partner(shard, place // depth, shards)
@@ -446,7 +472,18 @@
         steps = jnp.where((core == 1) & (steps < 3), 3 - steps, steps)
     slots = jnp.where(sender_slots < nodes, sender_slots, nodes + (away - 1) * depth + place % depth)
     both = jnp.stack([slots, receivers])
-    both = in_order([both] + [shifted(both, "rep", step) for step in range(1, halves)], "rep")
+    others = [shifted(both, "rep", step) for step in range(1, halves)]
+    if relayed:
+        left, whole = call(
+            functools.partial(left_kernel, piece_rows),
+            [((grid - piece_rows, width), bf16), ((grid + EXTRA, width), bf16)],
+            copied=True,
+        )(in_place[0], payload, others[0])
+        across = [sent_to(payload, 2), sent_to(left, 2)]
+        payloads = [[whole], [sent_to(whole, 1)], across, [sent_to(across[0], 1)]]
+    else:
+        payloads = [[payload]] + [[sent_to(payload, step)] for step in range(1, shards)]
+    both = in_order([both] + others, "rep")
     both = in_order([both] + [shifted(both, "feat", step) for step in range(1, feats)], "feat")
     both = both.reshape(feats * halves, 2, edges)
     all_slots, all_receivers = both[:, 0].reshape(1, -1), both[:, 1].reshape(1, -1)
@@ -470,11 +507,11 @@
         products=[(all_edges, nodes, width), (all_edges, 2 * nodes, width)],
     )(all_slots, all_receivers, lists)
 
-    if shards == 4:
-        across, list_here = lax.optimization_barrier((across, list_here))
-        payloads.append(sent_to(across, 1))
-
-    meta = jnp.stack([lax.axis_index("rep"), shard]).astype(i32)
+    if relayed:
+        across[-1], list_here = lax.optimization_barrier((across[-1], list_here))
+        payloads[-1].append(sent_to(across[-1], 1))
+
+    meta = jnp.broadcast_to(jnp.stack([core, shard]).astype(i32)[:, None], (2, width))
     node_f32, node_bf16 = ((nodes, width), f32), ((nodes, width), bf16)
     row_shape, half = ((grid, width), bf16), nodes // halves
     square = (nodes, width, width)
@@ -489,12 +526,12 @@
         outs += [((half, width), f32)] + [((half, width), bf16)] * (halves - 1) if last else [node_f32]
         got = list(
             call(
-                functools.partial(encode_kernel, count, first, last, halves),
+                functools.partial(encode_kernel, [len(block) for block in group], first, last, halves),
                 outs,
-                [node_f32] if last else [],
+                (),
                 [square] * first + [(grid, width, width), (grid, nodes, width), (nodes, grid, width)] * count,
             )(
-                meta, base, w_enc_grid, *((w_enc_mesh, list_here) if first else (total,)), *group
+                meta, base, w_enc_grid, *((w_enc_mesh, list_here) if first else (total,)), *(piece for block in group for piece in block)
             )
         )
         enc_picks += got[:count]
@@ -514,7 +551,6 @@
     parts = [part] + [shifted(part, "rep", -step) for step in range(1, halves)]
 
     spots = (0, 2 * depth) if shared else tuple(range(0, listed_rows, depth))
-    inward = (1, 1, 2) if shared else (1,) * shifts
     listed = [((depth, width), bf16)] * len(spots)
 
     def exchange(blocks, send, early):
@@ -523,14 +559,9 @@
         first = lax.ppermute(
             blocks[0], ("mesh", "rep"), [(2 * at + side, 2 * (at ^ 1 + side) + side) for at in range(4) for side in range(2)]
         )
-        third = lax.ppermute(blocks[1], ("mesh", "rep"), [(2 * at + 1, 2 * (at ^ 3) + 1) for at in range(4)])
+        third = send(blocks[1], 3)
         first, third, early = lax.optimization_barrier((first, third, early))
-        return [
-            first,
-            lax.ppermute(first, "rep", [(0, 1), (1, 0)]),
-            third,
-            lax.ppermute(third, "rep", [(1, 0)]),
-        ], early
+        return [first, shifted(first, "rep", 1), third], early
 
     hidden, enc_sum, sent, *outgoing = call(
         functools.partial(start_kernel, halves, spots), [node_bf16, node_f32, node_bf16] + listed, [node_bf16],
@@ -554,7 +585,7 @@
     records = []
     for layer in range(LAYERS - 1):
         hidden, agg, slope, sent, *outgoing = call(
-            functools.partial(layer_kernel, layer, inward, spots),
+            functools.partial(layer_kernel, layer, shifts, spots),
             [node_bf16, node_f32, edge_bf16, node_bf16] + listed,
             [halo, edge_bf16],
             forward_products + [square, (listed_rows, nodes, width)],
@@ -562,7 +593,7 @@
         records.append((agg, slope))
     last = LAYERS - 1
     final_mesh, grad_pre, *outgoing = call(
-        functools.partial(turn_kernel, last, inward, spots), [node_bf16, edge_bf16] + listed, [edge_bf16, halo],
+        functools.partial(turn_kernel, last, shifts, spots), [node_bf16, edge_bf16] + listed, [edge_bf16, halo],
         forward_products + backward_products,
     )(*arriving(last), halo_here, there, w_out, layer_gain, here, halo_there, out_cot)
     upstream = out_cot
@@ -579,41 +610,38 @@
         if layer:
             agg, slope = records[layer - 1]
             upstream, grad_pre, *outgoing = call(
-                functools.partial(back_kernel, layer - 1, inward, spots),
+                functools.partial(back_kernel, layer - 1, shifts, spots),
                 [node_f32, edge_bf16] + listed,
                 [back_halo],
                 backward_products + [(listed_rows, width, width), (nodes, listed_rows, width)],
             )(rest, *returned, list_there, w_send, agg, slope, layer_gain, w_out, here, halo_there)
-    relayed = shards == 4
-    pieces = 2 if relayed else 1
-    piece = ((grid // pieces, width), bf16)
+    piece = ((piece_rows, width), bf16)
     one = (grid, nodes, width)
     spread, *far = call(
-        functools.partial(finish_kernel, inward),
-        [node_bf16] + [piece] * pieces,
+        functools.partial(finish_kernel, shifts),
+        [node_bf16] + [piece] * cuts,
         [back_halo],
         [square, (listed_rows, width, width), (nodes, listed_rows, width), one],
     )(rest, *returned, list_there, w_send, enc_sum, enc_gain, w_enc_out, enc_picks[-1], enc_slopes[-1])
-    if relayed:
-        passed = [sent_back(block, 1) for block in far]
     blocks = call(
         functools.partial(others_kernel, shards - 1), [row_shape] * (shards - 1), products=[one] * (shards - 1)
     )(spread, *enc_picks[:-1], *enc_slopes[:-1])
     if relayed:
-        summed, near = [], blocks[1]
-        for at, block in enumerate(passed):
-            last = at == pieces - 1
-            got = call(
-                functools.partial(relay_kernel, at * piece[0][0], 1 + last), [piece] + [row_shape] * last
-            )(blocks[2], block, blocks[1])
-            summed.append(sent_back(got[0], 2))
-        parts = [blocks[0], sent_back(got[1], 1)], summed
+        passed = [sent_back(block, 1) for block in far]
+        first, near = call(functools.partial(relay_kernel, 0), [piece, row_shape])(blocks[2], passed[0], blocks[1])
+        (second,) = call(functools.partial(relay_kernel, piece_rows), [piece])(blocks[2], passed[1])
+        near = sent_back(near, 1)
+        first, second = sent_back(first, 2), sent_back(second, 2)
+        (summed,) = call(sum_kernel, [((piece_rows, width), f32)])(blocks[0], first)
+        (grid_grad,) = call(
+            functools.partial(grid_kernel, 2), [((grid, width), f32)], products=[(grid, width, width)]
+        )(blocks[0], near, summed, second, w_enc_grid)
     else:
-        blocks = [*blocks, far[0]]
-        parts = [blocks[0]] + [sent_back(block, step) for step, block in enumerate(blocks) if step], []
-    (grid_grad,) = call(
-        functools.partial(grid_kernel, len(parts[0])), [((grid, width), f32)], products=[(grid, width, width)]
-    )(*parts[0], *parts[1], w_enc_grid)
+        blocks = [*blocks, *far]
+        blocks = [blocks[0]] + [sent_back(block, step) for step, block in enumerate(blocks) if step]
+        (grid_grad,) = call(
+            functools.partial(grid_kernel, shards), [((grid, width), f32)], products=[(grid, width, width)]
+        )(*blocks, w_enc_grid)
     return (final_mesh, grid_grad)
 
 

time: 148 us -> 134 us (0.905)
  starting transfers between devices: 52.8 us -> 37.1 us
  waiting for transfers between devices: 41.2 us -> 44.3 us
    ppermute x18 -> x0, starting transfers between devices: 33.3 us -> none  [the longest x6 21.3 us: exchange(): lax.ppermute(first, 'rep', [(0, 1), (1, 0)])]
    ppermute x3 -> x8, starting transfers between devices: 6.13 us -> 18.9 us  [sent_to(): lax.ppermute(value, 'mesh', [(at, partner(at, step, size)) for at in rang...]
    ppermute x3 -> x8, waiting for transfers between devices: 4.61 us -> 11.9 us  [sent_to(): lax.ppermute(value, 'mesh', [(at, partner(at, step, size)) for at in rang...]
    ppermute x5 -> x8, waiting for transfers between devices: 15.1 us -> 21.6 us  [sent_back(): lax.ppermute(value, 'mesh', [(partner(at, step, size), at) for at in rang...]
    ppermute x6, waiting for transfers between devices: 6.95 us -> 0.61 us  [exchange(): lax.ppermute(blocks[0], ('mesh', 'rep'), [(2 * at + side, 2 * (at ^ 1 + s...]
    ppermute x5 -> x8, starting transfers between devices: 6.05 us -> 11.8 us  [sent_back(): lax.ppermute(value, 'mesh', [(partner(at, step, size), at) for at in rang...]
    ppermute x5 -> x11, waiting for transfers between devices: 12.4 us -> 10.3 us  [shifted(): lax.ppermute(value, axis, [(at, (at + by) % size) for at in range(size)])]
    ppermute x18 -> x0, waiting for transfers between devices: 2.05 us -> none  [the longest x6 2.02 us: exchange(): lax.ppermute(third, 'rep', [(1, 0)])]
  transfers between devices with their start and end apart: 37 -> 33, of which waited for: 21 -> 18; matrix products, arithmetic and copies ran while one was open for 2% -> 1% of each run, Pallas kernels for 17% -> 20%
where the time goes in v6:
time: 134 us
  Pallas kernels  48.5 us (36%)
  waiting for transfers between devices  44.3 us (33%)
  starting transfers between devices  37.1 us (28%)
  other arithmetic  1.8 us (1%)
    pallas_call x30, Pallas kernels, run(): pl.pallas_call(body, out_shape=tuple((jax.ShapeDtypeStruct(shape, dtype)...  48.5 us
    ppermute x8, waiting for transfers between devices, sent_back(): lax.ppermute(value, 'mesh', [(partner(at, step, size), at) for at in rang...  21.6 us
    ppermute x8, starting transfers between devices, sent_to(): lax.ppermute(value, 'mesh', [(at, partner(at, step, size)) for at in rang...  18.9 us
    ppermute x8, waiting for transfers between devices, sent_to(): lax.ppermute(value, 'mesh', [(at, partner(at, step, size)) for at in rang...  11.9 us
    ppermute x8, starting transfers between devices, sent_back(): lax.ppermute(value, 'mesh', [(partner(at, step, size), at) for at in rang...  11.8 us
    ppermute x11, waiting for transfers between devices, shifted(): lax.ppermute(value, axis, [(at, (at + by) % size) for at in range(size)])  10.3 us
    ppermute x11, starting transfers between devices, shifted(): lax.ppermute(value, axis, [(at, (at + by) % size) for at in range(size)])  3.76 us
  transfers between devices with their start and end apart: 33, of which 18 were waited for; matrix products, arithmetic and copies ran while one was open for 1% of the time, Pallas kernels for 20%

profile of v6, /device:TPU:0, one launch (start us, length us, event | category | flops | bytes accessed | tf_op | source)
XLA Modules:
  0.0 133.7 jit_solution(17052917767283011863)
XLA Ops:
  0.7 0.7 compare_select_fusion.1
  1.4 0.7 fusion.11
  2.5 1.0 shard_map.167.notes
  3.5 3.7 %collective-permute-start.4 = (bf16[144,512]{1,0:T(8,128)(2,1)S(1)}, bf16[144,512]{1,0:T(8,128)(2,1)S(1)}, u32[]{:S(2)}, u32[]{:S(2)}) collective-permute-start(bf16[144,512]{1,0:T(8,128)(2,1)S(1)} %shard_map.167.notes), channel_id=1, source_target_pairs={{0,8},{4,12},{8,0},{12,4},{1,9},{5,13},{9,1},{13,5},{2,10},{6,14},... | collective-permute-start | bytes 442376 | tf_op jit(solution)/shard_map/ppermute | solution.py:409
  7.2 0.6 gather_fusion
  8.0 1.6 %collective-permute-start.2 = (s32[2,2,512]{2,1,0:T(2,128)S(1)}, s32[2,2,512]{2,1,0:T(2,128)S(1)}, u32[]{:S(2)}, u32[]{:S(2)}) collective-permute-start(s32[2,2,512]{2,1,0:T(2,128)S(1)} %fusion.1), channel_id=1, source_target_pairs={{0,2},{2,0},{1,3},{3,1},{4,6},{6,4},{5,7},{7,5},{8,10},{10,8},{9,1... | collective-permute-start | bytes 24584 | tf_op jit(solution)/shard_map/ppermute | solution.py:400
  9.6 1.1 shard_map.168
  11.1 1.6 %collective-permute-start.3 = (bf16[272,512]{1,0:T(8,128)(2,1)S(1)}, bf16[272,512]{1,0:T(8,128)(2,1)S(1)}, u32[]{:S(2)}, u32[]{:S(2)}) collective-permute-start(bf16[272,512]{1,0:T(8,128)(2,1)S(1)} %get-tuple-element.92.refs_5_), channel_id=1, source_target_pairs={{0,4},{4,0},{8,12},{12,8},{1,5},{5,1},{9,13},{13,9},{2,6},{6,2},{1... | collective-permute-start | bytes 835592 | tf_op jit(solution)/shard_map/ppermute | solution.py:409
  12.7 2.3 %collective-permute-done.4.refs_4_ = bf16[144,512]{1,0:T(8,128)(2,1)S(1)} collective-permute-done((bf16[144,512]{1,0:T(8,128)(2,1)S(1)}, bf16[144,512]{1,0:T(8,128)(2,1)S(1)}, u32[]{:S(2)}, u32[]{:S(2)}) %collective-permute-start.4) | collective-permute-done | bytes 147488 | tf_op jit(solution)/shard_map/ppermute | solution.py:409
  15.1 3.3 %collective-permute-start.5 = (bf16[144,512]{1,0:T(8,128)(2,1)S(1)}, bf16[144,512]{1,0:T(8,128)(2,1)S(1)}, u32[]{:S(2)}, u32[]{:S(2)}) collective-permute-start(bf16[144,512]{1,0:T(8,128)(2,1)S(1)} %collective-permute-done.4.refs_4_), channel_id=1, source_target_pairs={{0,4},{4,0},{8,12},{12,8},{1,5},{5,1},{9,13},{13,9},{2,6},{6,2},{1... | collective-permute-start | bytes 442376 | tf_op jit(solution)/shard_map/ppermute | solution.py:409
  18.4 3.5 %shard_map.169 = (bf16[2048,1024]{1,0:T(8,128)(2,1)S(1)}, bf16[1024,2048]{1,0:T(8,128)(2,1)S(1)}, bf16[2048,128]{1,0:T(8,128)(2,1)S(1)}, bf16[128,2048]{1,0:T(8,...) custom-call(s32[1,2048]{1,0:T(1,128)S(1)} %fusion.2.slots, s32[1,2048]{1,0:T(1,128)S(1)} %bitcast.21, ...), custom_call_target="tpu_custom_call" | custom-call | flops 3221225472 | bytes 9650560 | tf_op jit(solution)/shard_map/pallas_call | solution.py:82
  22.0 1.7 %collective-permute-done.3.refs_6_ = bf16[272,512]{1,0:T(8,128)(2,1)S(1)} collective-permute-done((bf16[272,512]{1,0:T(8,128)(2,1)S(1)}, bf16[272,512]{1,0:T(8,128)(2,1)S(1)}, u32[]{:S(2)}, u32[]{:S(2)}) %collective-permute-start.3) | collective-permute-done | bytes 278560 | tf_op jit(solution)/shard_map/ppermute | solution.py:409
  23.7 1.7 %shard_map.170 = (bf16[256,512]{1,0:T(8,128)(2,1)S(1)}, bf16[256,512]{1,0:T(8,128)(2,1)S(1)}, bf16[256,512]{1,0:T(8,128)(2,1)S(1)}, bf16[256,512]{1,0:T(8,128)(2...) custom-call(s32[2,512]{1,0:T(2,128)S(1)} %broadcast_in_dim.27.refs_0_, bf16[512,512]{1,0:T(8,128)(2,1)S(1)} %copy-done.8, ...), custom_call_target="tpu_custom_call" | custom-call | flops 1073741824 | bytes 4853760 | tf_op jit(solution)/shard_map/pallas_call | solution.py:82
  25.4 0.9 shard_map.171
  26.3 3.2 %collective-permute-done.6.refs_5_ = bf16[128,512]{1,0:T(8,128)(2,1)S(1)} collective-permute-done((bf16[128,512]{1,0:T(8,128)(2,1)S(1)}, bf16[128,512]{1,0:T(8,128)(2,1)S(1)}, u32[]{:S(2)}, u32[]{:S(2)}) %collective-permute-start.6) | collective-permute-done | bytes 131104 | tf_op jit(solution)/shard_map/ppermute | solution.py:409
  29.6 0.9 shard_map.172
  30.6 1.5 %collective-permute-done.7 = bf16[256,512]{1,0:T(8,128)(2,1)S(1)} collective-permute-done((bf16[256,512]{1,0:T(8,128)(2,1)S(1)}, bf16[256,512]{1,0:T(8,128)(2,1)S(1)}, u32[]{:S(2)}, u32[]{:S(2)}) %collective-permute-start.7) | collective-permute-done | bytes 262176 | tf_op jit(solution)/shard_map/ppermute | solution.py:400
  32.2 1.2 collective-permute-start.8
  33.4 7.2 %collective-permute-done.8 = bf16[256,512]{1,0:T(8,128)(2,1)S(1)} collective-permute-done((bf16[256,512]{1,0:T(8,128)(2,1)S(1)}, bf16[256,512]{1,0:T(8,128)(2,1)S(1)}, u32[]{:S(2)}, u32[]{:S(2)}) %collective-permute-start.8) | collective-permute-done | bytes 262176 | tf_op jit(solution)/shard_map/ppermute | solution.py:400
  40.7 1.5 %collective-permute-done.9.refs_2_ = bf16[256,512]{1,0:T(8,128)(2,1)S(1)} collective-permute-done((bf16[256,512]{1,0:T(8,128)(2,1)S(1)}, bf16[256,512]{1,0:T(8,128)(2,1)S(1)}, u32[]{:S(2)}, u32[]{:S(2)}) %collective-permute-start.9) | collective-permute-done | bytes 262176 | tf_op jit(solution)/shard_map/ppermute | solution.py:400
  42.3 1.0 shard_map.173
  43.4 5.1 %collective-permute-start.11 = (bf16[32,512]{1,0:T(8,128)(2,1)S(1)}, bf16[32,512]{1,0:T(8,128)(2,1)S(1)}, u32[]{:S(2)}, u32[]{:S(2)}) collective-permute-start(bf16[32,512]{1,0:T(8,128)(2,1)S(1)} %get-tuple-element.101), channel_id=1, source_target_pairs={{0,12},{4,8},{8,4},{12,0},{1,13},{5,9},{9,5},{13,1},{2,14},{6,10},... | collective-permute-start | bytes 98312 | tf_op jit(solution)/shard_map/ppermute | solution.py:409
  48.5 1.5 %shard_map.174 = (f32[1024,512]{1,0:T(8,128)S(1)}, bf16[1024,512]{1,0:T(8,128)(2,1)S(1)}) custom-call(bf16[512,512]{1,0:T(8,128)(2,1)S(1)} %get-tuple-element.99.hidden.refs_0_, bf16[512,512]{1,0:T(8,128)(2,1)S(1)} %get-tuple-element.102.sent, bf16[2048,1024]{1,0:T(8,128)(2,1)S(1)} %get-tuple-element.103.here.refs_10_, bf16[3,512,512]{2,1,0:T(8,128)(2,1)S(1)} %copy-done.3), custom_call_target="tpu_custom_call" | custom-call | flops 1342177280 | bytes 9961472 | tf_op jit(solution)/shard_map/pallas_call | solution.py:82
  50.0 0.6 collective-permute-done.11.refs_5_
  51.0 1.2 shard_map.175.refs_2_
  52.2 3.2 %shard_map.176 = (bf16[512,512]{1,0:T(8,128)(2,1)S(1)}, f32[512,512]{1,0:T(8,128)S(1)}, bf16[2048,512]{1,0:T(8,128)(2,1)S(1)}, bf16[512,512]{1,0:T(8,128)(2,1)S(...) custom-call(bf16[512,512]{1,0:T(8,128)(2,1)S(1)} %get-tuple-element.99.hidden.refs_0_, ...), custom_call_target="tpu_custom_call" | custom-call | flops 1929379840 | bytes 17045504 | tf_op jit(solution)/shard_map/pallas_call | solution.py:82
  55.5 1.4 %collective-permute-start.13 = (bf16[32,512]{1,0:T(8,128)(2,1)S(1)}, bf16[32,512]{1,0:T(8,128)(2,1)S(1)}, u32[]{:S(2)}, u32[]{:S(2)}) collective-permute-start(bf16[32,512]{1,0:T(8,128)(2,1)S(1)} %get-tuple-element.113), channel_id=1, source_target_pairs={{0,4},{1,9},{4,0},{5,13},{8,12},{9,1},{12,8},{13,5},{2,6},{3,11},{... | collective-permute-start | bytes 98312 | tf_op jit(solution)/shard_map/ppermute | solution.py:559
  56.9 2.2 %collective-permute-start.14 = (bf16[32,512]{1,0:T(8,128)(2,1)S(1)}, bf16[32,512]{1,0:T(8,128)(2,1)S(1)}, u32[]{:S(2)}, u32[]{:S(2)}) collective-permute-start(bf16[32,512]{1,0:T(8,128)(2,1)S(1)} %get-tuple-element.114), channel_id=1, source_target_pairs={{0,12},{4,8},{8,4},{12,0},{1,13},{5,9},{9,5},{13,1},{2,14},{6,10},... | collective-permute-start | bytes 98312 | tf_op jit(solution)/shard_map/ppermute | solution.py:409
  59.1 1.5 %shard_map.177 = (f32[1024,512]{1,0:T(8,128)S(1)}, bf16[1024,512]{1,0:T(8,128)(2,1)S(1)}) custom-call(bf16[512,512]{1,0:T(8,128)(2,1)S(1)} %get-tuple-element.112.hidden.refs_0_, bf16[512,512]{1,0:T(8,128)(2,1)S(1)} %get-tuple-element.115.sent, bf16[2048,1024]{1,0:T(8,128)(2,1)S(1)} %get-tuple-element.103.here.refs_10_, bf16[3,512,512]{2,1,0:T(8,128)(2,1)S(1)} %copy-done.3), custom_call_target="tpu_custom_call" | custom-call | flops 1342177280 | bytes 9961472 | tf_op jit(solution)/shard_map/pallas_call | solution.py:82
  60.6 2.2 %collective-permute-done.14.refs_5_ = bf16[32,512]{1,0:T(8,128)(2,1)S(1)} collective-permute-done((bf16[32,512]{1,0:T(8,128)(2,1)S(1)}, bf16[32,512]{1,0:T(8,128)(2,1)S(1)}, u32[]{:S(2)}, u32[]{:S(2)}) %collective-permute-start.14) | collective-permute-done | bytes 32800 | tf_op jit(solution)/shard_map/ppermute | solution.py:409
  62.8 1.2 shard_map.178.refs_2_
  64.1 3.5 %shard_map.179 = (bf16[512,512]{1,0:T(8,128)(2,1)S(1)}, f32[512,512]{1,0:T(8,128)S(1)}, bf16[2048,512]{1,0:T(8,128)(2,1)S(1)}, bf16[512,512]{1,0:T(8,128)(2,1)S(...) custom-call(bf16[512,512]{1,0:T(8,128)(2,1)S(1)} %get-tuple-element.112.hidden.refs_0_, ...), custom_call_target="tpu_custom_call" | custom-call | flops 1929379840 | bytes 17045504 | tf_op jit(solution)/shard_map/pallas_call | solution.py:82
  67.7 2.6 %collective-permute-start.17 = (bf16[32,512]{1,0:T(8,128)(2,1)S(1)}, bf16[32,512]{1,0:T(8,128)(2,1)S(1)}, u32[]{:S(2)}, u32[]{:S(2)}) collective-permute-start(bf16[32,512]{1,0:T(8,128)(2,1)S(1)} %get-tuple-element.124), channel_id=1, source_target_pairs={{0,12},{4,8},{8,4},{12,0},{1,13},{5,9},{9,5},{13,1},{2,14},{6,10},... | collective-permute-start | bytes 98312 | tf_op jit(solution)/shard_map/ppermute | solution.py:409
  70.2 1.5 %shard_map.180 = (f32[1024,512]{1,0:T(8,128)S(1)}, bf16[1024,512]{1,0:T(8,128)(2,1)S(1)}) custom-call(bf16[512,512]{1,0:T(8,128)(2,1)S(1)} %get-tuple-element.122.hidden.refs_0_, bf16[512,512]{1,0:T(8,128)(2,1)S(1)} %get-tuple-element.125.sent, bf16[2048,1024]{1,0:T(8,128)(2,1)S(1)} %get-tuple-element.103.here.refs_10_, bf16[3,512,512]{2,1,0:T(8,128)(2,1)S(1)} %copy-done.3), custom_call_target="tpu_custom_call" | custom-call | flops 1342177280 | bytes 9961472 | tf_op jit(solution)/shard_map/pallas_call | solution.py:82
  71.8 1.8 %collective-permute-done.17.refs_5_ = bf16[32,512]{1,0:T(8,128)(2,1)S(1)} collective-permute-done((bf16[32,512]{1,0:T(8,128)(2,1)S(1)}, bf16[32,512]{1,0:T(8,128)(2,1)S(1)}, u32[]{:S(2)}, u32[]{:S(2)}) %collective-permute-start.17) | collective-permute-done | bytes 32800 | tf_op jit(solution)/shard_map/ppermute | solution.py:409
  73.7 1.2 shard_map.181.refs_2_
  75.0 5.7 %shard_map.182 = (bf16[512,512]{1,0:T(8,128)(2,1)}, bf16[2048,512]{1,0:T(8,128)(2,1)S(1)}, bf16[32,512]{1,0:T(8,128)(2,1)S(1)}, bf16[32,512]{1,0:T(8,128)(2,1)S(1)}) custom-call(bf16[512,512]{1,0:T(8,128)(2,1)S(1)} %get-tuple-element.122.hidden.refs_0_, f32[1024,512]{1,0:T(8,128)S(1)} %get-tuple-element.128.refs_1_, f32[1024,512]{1,0:T(8,128)S(1)} %shard_map.181.refs_2_, ...), custom_call_target="tpu_custom_call" | custom-call | flops 3221225472 | bytes 19044352 | tf_op jit(solution)/shard_map/pallas_call | solution.py:82
  80.7 2.2 %collective-permute-start.20 = (bf16[32,512]{1,0:T(8,128)(2,1)S(1)}, bf16[32,512]{1,0:T(8,128)(2,1)S(1)}, u32[]{:S(2)}, u32[]{:S(2)}) collective-permute-start(bf16[32,512]{1,0:T(8,128)(2,1)S(1)} %get-tuple-element.135), channel_id=1, source_target_pairs={{12,0},{8,4},{4,8},{0,12},{13,1},{9,5},{5,9},{1,13},{14,2},{10,6},... | collective-permute-start | bytes 98312 | tf_op jit(solution)/shard_map/ppermute | solution.py:414
  82.9 1.5 %shard_map.183.upstream = f32[512,512]{1,0:T(8,128)S(1)} custom-call(bf16[512,512]{1,0:T(8,128)(2,1)S(1)} %copy-done.6, bf16[2048,512]{1,0:T(8,128)(2,1)S(1)} %get-tuple-element.136.grad_pre, bf16[1024,2048]{1,0:T(8,128)(2,1)S(1)} %get-tuple-element.111.refs_7_.there, bf16[3,512,512]{2,1,0:T(8,128)(2,1)S(1)} %copy-done.2), custom_call_target="tpu_custom_call" | custom-call | flops 1342177280 | bytes 9437184 | tf_op jit(solution)/shard_map/pallas_call | solution.py:82
  84.6 2.2 %collective-permute-done.20.refs_3_ = bf16[32,512]{1,0:T(8,128)(2,1)S(1)} collective-permute-done((bf16[32,512]{1,0:T(8,128)(2,1)S(1)}, bf16[32,512]{1,0:T(8,128)(2,1)S(1)}, u32[]{:S(2)}, u32[]{:S(2)}) %collective-permute-start.20) | collective-permute-done | bytes 32800 | tf_op jit(solution)/shard_map/ppermute | solution.py:414
  86.8 1.5 %shard_map.184.refs_0_ = f32[512,512]{1,0:T(8,128)S(1)} custom-call(f32[512,512]{1,0:T(8,128)S(1)} %shard_map.183.upstream, bf16[2048,512]{1,0:T(8,128)(2,1)S(1)} %get-tuple-element.136.grad_pre, bf16[1024,2048]{1,0:T(8,128)(2,1)S(1)} %get-tuple-element.111.refs_7_.there, bf16[3,512,512]{2,1,0:T(8,128)(2,1)S(1)} %copy-done.3), custom_call_target="tpu_custom_call" | custom-call | flops 1342177280 | bytes 9961472 | tf_op jit(solution)/shard_map/pallas_call | solution.py:82
  88.4 2.6 %shard_map.185 = (f32[512,512]{1,0:T(8,128)S(1)}, bf16[2048,512]{1,0:T(8,128)(2,1)S(1)}, bf16[32,512]{1,0:T(8,128)(2,1)S(1)}, bf16[32,512]{1,0:T(8,128)(2,1)S(1)}) custom-call(f32[512,512]{1,0:T(8,128)S(1)} %shard_map.184.refs_0_, bf16[32,512]{1,0:T(8,128)(2,1)S(1)} %collective-permute-done.19.refs_1_, bf16[32,512]{1,0:T(8,128)(2,1)S(1)} %collective-permute-done.21.refs_2_, ...), custom_call_target="tpu_custom_call" | custom-call | flops 1711276032 | bytes 15472640 | tf_op jit(solution)/shard_map/pallas_call | solution.py:82
  91.0 0.9 collective-permute-start.22
  91.9 1.7 %collective-permute-start.23 = (bf16[32,512]{1,0:T(8,128)(2,1)S(1)}, bf16[32,512]{1,0:T(8,128)(2,1)S(1)}, u32[]{:S(2)}, u32[]{:S(2)}) collective-permute-start(bf16[32,512]{1,0:T(8,128)(2,1)S(1)} %get-tuple-element.144), channel_id=1, source_target_pairs={{12,0},{8,4},{4,8},{0,12},{13,1},{9,5},{5,9},{1,13},{14,2},{10,6},... | collective-permute-start | bytes 98312 | tf_op jit(solution)/shard_map/ppermute | solution.py:414
  93.6 1.5 %shard_map.186.upstream = f32[512,512]{1,0:T(8,128)S(1)} custom-call(f32[512,512]{1,0:T(8,128)S(1)} %get-tuple-element.145.upstream, bf16[2048,512]{1,0:T(8,128)(2,1)S(1)} %get-tuple-element.146.grad_pre, bf16[1024,2048]{1,0:T(8,128)(2,1)S(1)} %get-tuple-element.111.refs_7_.there, bf16[3,512,512]{2,1,0:T(8,128)(2,1)S(1)} %copy-done.2), custom_call_target="tpu_custom_call" | custom-call | flops 1342177280 | bytes 9961472 | tf_op jit(solution)/shard_map/pallas_call | solution.py:82
  95.1 2.5 %collective-permute-done.23.refs_3_ = bf16[32,512]{1,0:T(8,128)(2,1)S(1)} collective-permute-done((bf16[32,512]{1,0:T(8,128)(2,1)S(1)}, bf16[32,512]{1,0:T(8,128)(2,1)S(1)}, u32[]{:S(2)}, u32[]{:S(2)}) %collective-permute-start.23) | collective-permute-done | bytes 32800 | tf_op jit(solution)/shard_map/ppermute | solution.py:414
  97.6 1.8 %shard_map.187.refs_0_ = f32[512,512]{1,0:T(8,128)S(1)} custom-call(f32[512,512]{1,0:T(8,128)S(1)} %shard_map.186.upstream, bf16[2048,512]{1,0:T(8,128)(2,1)S(1)} %get-tuple-element.146.grad_pre, bf16[1024,2048]{1,0:T(8,128)(2,1)S(1)} %get-tuple-element.111.refs_7_.there, bf16[3,512,512]{2,1,0:T(8,128)(2,1)S(1)} %copy-done.3), custom_call_target="tpu_custom_call" | custom-call | flops 1342177280 | bytes 9961472 | tf_op jit(solution)/shard_map/pallas_call | solution.py:82
  99.4 2.6 %shard_map.188 = (f32[512,512]{1,0:T(8,128)S(1)}, bf16[2048,512]{1,0:T(8,128)(2,1)S(1)}, bf16[32,512]{1,0:T(8,128)(2,1)S(1)}, bf16[32,512]{1,0:T(8,128)(2,1)S(1)}) custom-call(f32[512,512]{1,0:T(8,128)S(1)} %shard_map.187.refs_0_, bf16[32,512]{1,0:T(8,128)(2,1)S(1)} %collective-permute-done.22.refs_1_, bf16[32,512]{1,0:T(8,128)(2,1)S(1)} %collective-permute-done.24.refs_2_, ...), custom_call_target="tpu_custom_call" | custom-call | flops 1711276032 | bytes 15472640 | tf_op jit(solution)/shard_map/pallas_call | solution.py:82
  102.0 1.9 %collective-permute-start.26 = (bf16[32,512]{1,0:T(8,128)(2,1)S(1)}, bf16[32,512]{1,0:T(8,128)(2,1)S(1)}, u32[]{:S(2)}, u32[]{:S(2)}) collective-permute-start(bf16[32,512]{1,0:T(8,128)(2,1)S(1)} %get-tuple-element.153), channel_id=1, source_target_pairs={{12,0},{8,4},{4,8},{0,12},{13,1},{9,5},{5,9},{1,13},{14,2},{10,6},... | collective-permute-start | bytes 98312 | tf_op jit(solution)/shard_map/ppermute | solution.py:414
  104.0 1.5 %shard_map.189.upstream = f32[512,512]{1,0:T(8,128)S(1)} custom-call(f32[512,512]{1,0:T(8,128)S(1)} %get-tuple-element.154.upstream, bf16[2048,512]{1,0:T(8,128)(2,1)S(1)} %get-tuple-element.155.grad_pre, bf16[1024,2048]{1,0:T(8,128)(2,1)S(1)} %get-tuple-element.111.refs_7_.there, bf16[3,512,512]{2,1,0:T(8,128)(2,1)S(1)} %copy-done.2), custom_call_target="tpu_custom_call" | custom-call | flops 1342177280 | bytes 9961472 | tf_op jit(solution)/shard_map/pallas_call | solution.py:82
  105.5 0.5 collective-permute-done.25.refs_1_
  105.9 1.9 %collective-permute-done.26.refs_3_ = bf16[32,512]{1,0:T(8,128)(2,1)S(1)} collective-permute-done((bf16[32,512]{1,0:T(8,128)(2,1)S(1)}, bf16[32,512]{1,0:T(8,128)(2,1)S(1)}, u32[]{:S(2)}, u32[]{:S(2)}) %collective-permute-start.26) | collective-permute-done | bytes 32800 | tf_op jit(solution)/shard_map/ppermute | solution.py:414
  107.9 1.5 %shard_map.190.refs_0_ = f32[512,512]{1,0:T(8,128)S(1)} custom-call(f32[512,512]{1,0:T(8,128)S(1)} %shard_map.189.upstream, bf16[2048,512]{1,0:T(8,128)(2,1)S(1)} %get-tuple-element.155.grad_pre, bf16[1024,2048]{1,0:T(8,128)(2,1)S(1)} %get-tuple-element.111.refs_7_.there, bf16[3,512,512]{2,1,0:T(8,128)(2,1)S(1)} %copy-done.3), custom_call_target="tpu_custom_call" | custom-call | flops 1342177280 | bytes 9961472 | tf_op jit(solution)/shard_map/pallas_call | solution.py:82
  109.4 1.4 %shard_map.191 = (bf16[512,512]{1,0:T(8,128)(2,1)S(1)}, bf16[128,512]{1,0:T(8,128)(2,1)S(1)}, bf16[128,512]{1,0:T(8,128)(2,1)S(1)}) custom-call(f32[512,512]{1,0:T(8,128)S(1)} %shard_map.190.refs_0_, bf16[32,512]{1,0:T(8,128)(2,1)S(1)} %collective-permute-done.25.refs_1_, bf16[32,512]{1,0:T(8,128)(2,1)S(1)} %collective-permute-done.27.refs_2_, ...), custom_call_target="tpu_custom_call" | custom-call | flops 503316480 | bytes 5703680 | tf_op jit(solution)/shard_map/pallas_call | solution.py:82
  110.8 0.9 collective-permute-start.28
  111.7 1.2 collective-permute-start.31
  112.9 0.6 shard_map.192
  113.5 3.7 %collective-permute-done.28.passed = bf16[128,512]{1,0:T(8,128)(2,1)S(1)} collective-permute-done((bf16[128,512]{1,0:T(8,128)(2,1)S(1)}, bf16[128,512]{1,0:T(8,128)(2,1)S(1)}, u32[]{:S(2)}, u32[]{:S(2)}) %collective-permute-start.28) | collective-permute-done | bytes 131104 | tf_op jit(solution)/shard_map/ppermute | solution.py:414
  117.2 0.9 collective-permute-start.29
  118.1 1.6 %collective-permute-start.30 = (bf16[128,512]{1,0:T(8,128)(2,1)S(1)}, bf16[128,512]{1,0:T(8,128)(2,1)S(1)}, u32[]{:S(2)}, u32[]{:S(2)}) collective-permute-start(bf16[128,512]{1,0:T(8,128)(2,1)S(1)} %get-tuple-element.174), channel_id=1, source_target_pairs={{8,0},{12,4},{0,8},{4,12},{9,1},{13,5},{1,9},{5,13},{10,2},{14,6},... | collective-permute-start | bytes 393224 | tf_op jit(solution)/shard_map/ppermute | solution.py:414
  119.9 1.4 %collective-permute-start.32 = (bf16[128,512]{1,0:T(8,128)(2,1)S(1)}, bf16[128,512]{1,0:T(8,128)(2,1)S(1)}, u32[]{:S(2)}, u32[]{:S(2)}) collective-permute-start(bf16[128,512]{1,0:T(8,128)(2,1)S(1)} %shard_map.195), channel_id=1, source_target_pairs={{8,0},{12,4},{0,8},{4,12},{9,1},{13,5},{1,9},{5,13},{10,2},{14,6},... | collective-permute-start | bytes 393224 | tf_op jit(solution)/shard_map/ppermute | solution.py:414
  121.3 6.4 %collective-permute-done.30.piece = bf16[128,512]{1,0:T(8,128)(2,1)S(1)} collective-permute-done((bf16[128,512]{1,0:T(8,128)(2,1)S(1)}, bf16[128,512]{1,0:T(8,128)(2,1)S(1)}, u32[]{:S(2)}, u32[]{:S(2)}) %collective-permute-start.30) | collective-permute-done | bytes 131104 | tf_op jit(solution)/shard_map/ppermute | solution.py:414
  127.7 4.6 %collective-permute-done.32.refs_3_ = bf16[128,512]{1,0:T(8,128)(2,1)S(1)} collective-permute-done((bf16[128,512]{1,0:T(8,128)(2,1)S(1)}, bf16[128,512]{1,0:T(8,128)(2,1)S(1)}, u32[]{:S(2)}, u32[]{:S(2)}) %collective-permute-start.32) | collective-permute-done | bytes 131104 | tf_op jit(solution)/shard_map/ppermute | solution.py:414
  132.4 1.3 shard_map.196
  (77 shorter events, 2.9 us)
Async XLA Ops:
  0.6 6.5 %copy-start = (s32[1,4,32]{2,1,0:T(4,128)S(1)}, s32[1,4,32]{2,1,0:T(4,128)}, u32[]{:S(2)}) copy-start(s32[1,4,32]{2,1,0:T(4,128)} %param.22) | copy-start | bytes 1540
  2.0 5.9 %collective-permute-start = (s32[2,512]{1,0:T(2,128)S(1)}, s32[2,512]{1,0:T(2,128)S(1)}, u32[]{:S(2)}, u32[]{:S(2)}) collective-permute-start(s32[2,512]{1,0:T(2,128)S(1)} %get-tuple-element.179), channel_id=1, source_target_pairs={{0,1},{1,0},{2,3},{3,2},{4,5},{5,4},{6,7},{7,6},{8,9},{9,8},{10,11... | collective-permute-start | bytes 12296 | tf_op jit(solution)/shard_map/ppermute | solution.py:400
  3.5 11.6 %collective-permute-start.4 = (bf16[144,512]{1,0:T(8,128)(2,1)S(1)}, bf16[144,512]{1,0:T(8,128)(2,1)S(1)}, u32[]{:S(2)}, u32[]{:S(2)}) collective-permute-start(bf16[144,512]{1,0:T(8,128)(2,1)S(1)} %shard_map.167.notes), channel_id=1, source_target_pairs={{0,8},{4,12},{8,0},{12,4},{1,9},{5,13},{9,1},{13,5},{2,10},{6,14},... | collective-permute-start | bytes 442376 | tf_op jit(solution)/shard_map/ppermute | solution.py:409
  8.0 4.6 %collective-permute-start.2 = (s32[2,2,512]{2,1,0:T(2,128)S(1)}, s32[2,2,512]{2,1,0:T(2,128)S(1)}, u32[]{:S(2)}, u32[]{:S(2)}) collective-permute-start(s32[2,2,512]{2,1,0:T(2,128)S(1)} %fusion.1), channel_id=1, source_target_pairs={{0,2},{2,0},{1,3},{3,1},{4,6},{6,4},{5,7},{7,5},{8,10},{10,8},{9,1... | collective-permute-start | bytes 24584 | tf_op jit(solution)/shard_map/ppermute | solution.py:400
  10.7 11.3 %collective-permute-start.1 = (bf16[128,512]{1,0:T(8,128)(2,1)S(1)}, bf16[128,512]{1,0:T(8,128)(2,1)S(1)}, u32[]{:S(2)}, u32[]{:S(2)}) collective-permute-start(bf16[128,512]{1,0:T(8,128)(2,1)S(1)} %get-tuple-element.89), channel_id=1, source_target_pairs={{0,8},{4,12},{8,0},{12,4},{1,9},{5,13},{9,1},{13,5},{2,10},{6,14},... | collective-permute-start | bytes 393224 | tf_op jit(solution)/shard_map/ppermute | solution.py:409
  11.1 12.6 %collective-permute-start.3 = (bf16[272,512]{1,0:T(8,128)(2,1)S(1)}, bf16[272,512]{1,0:T(8,128)(2,1)S(1)}, u32[]{:S(2)}, u32[]{:S(2)}) collective-permute-start(bf16[272,512]{1,0:T(8,128)(2,1)S(1)} %get-tuple-element.92.refs_5_), channel_id=1, source_target_pairs={{0,4},{4,0},{8,12},{12,8},{1,5},{5,1},{9,13},{13,9},{2,6},{6,2},{1... | collective-permute-start | bytes 835592 | tf_op jit(solution)/shard_map/ppermute | solution.py:409
  15.1 14.5 %collective-permute-start.5 = (bf16[144,512]{1,0:T(8,128)(2,1)S(1)}, bf16[144,512]{1,0:T(8,128)(2,1)S(1)}, u32[]{:S(2)}, u32[]{:S(2)}) collective-permute-start(bf16[144,512]{1,0:T(8,128)(2,1)S(1)} %collective-permute-done.4.refs_4_), channel_id=1, source_target_pairs={{0,4},{4,0},{8,12},{12,8},{1,5},{5,1},{9,13},{13,9},{2,6},{6,2},{1... | collective-permute-start | bytes 442376 | tf_op jit(solution)/shard_map/ppermute | solution.py:409
  18.4 5.3 %copy-start.5 = (bf16[512,512]{1,0:T(8,128)(2,1)S(1)}, bf16[512,512]{1,0:T(8,128)(2,1)}, u32[]{:S(2)}) copy-start(bf16[512,512]{1,0:T(8,128)(2,1)} %refs_4_.3) | copy-start | bytes 1572868
  18.4 5.3 %copy-start.8 = (bf16[512,512]{1,0:T(8,128)(2,1)S(1)}, bf16[512,512]{1,0:T(8,128)(2,1)}, u32[]{:S(2)}) copy-start(bf16[512,512]{1,0:T(8,128)(2,1)} %refs_3_.3) | copy-start | bytes 1572868
  18.4 5.3 %copy-start.11 = (bf16[512,512]{1,0:T(8,128)(2,1)S(1)}, bf16[512,512]{1,0:T(8,128)(2,1)}, u32[]{:S(2)}) copy-start(bf16[512,512]{1,0:T(8,128)(2,1)} %refs_3_.2) | copy-start | bytes 1572868
  21.9 7.6 %collective-permute-start.6 = (bf16[128,512]{1,0:T(8,128)(2,1)S(1)}, bf16[128,512]{1,0:T(8,128)(2,1)S(1)}, u32[]{:S(2)}, u32[]{:S(2)}) collective-permute-start(bf16[128,512]{1,0:T(8,128)(2,1)S(1)} %collective-permute-done.1.refs_5_), channel_id=1, source_target_pairs={{0,4},{4,0},{8,12},{12,8},{1,5},{5,1},{9,13},{13,9},{2,6},{6,2},{1... | collective-permute-start | bytes 393224 | tf_op jit(solution)/shard_map/ppermute | solution.py:409
  29.5 12.7 %copy-start.2 = (bf16[3,512,512]{2,1,0:T(8,128)(2,1)S(1)}, bf16[3,512,512]{2,1,0:T(8,128)(2,1)}, u32[]{:S(2)}) copy-start(bf16[3,512,512]{2,1,0:T(8,128)(2,1)} %refs_5_.5) | copy-start | bytes 4718596
  29.6 12.7 %copy-start.7 = (bf16[512,512]{1,0:T(8,128)(2,1)S(1)}, bf16[512,512]{1,0:T(8,128)(2,1)}, u32[]{:S(2)}) copy-start(bf16[512,512]{1,0:T(8,128)(2,1)} %refs_8_.11) | copy-start | bytes 1572868
  29.6 12.7 %copy-start.10 = (f32[512]{0:T(512)S(1)}, f32[512]{0:T(512)}, u32[]{:S(2)}) copy-start(f32[512]{0:T(512)} %param.26) | copy-start | bytes 6148
  30.5 1.6 %collective-permute-start.7 = (bf16[256,512]{1,0:T(8,128)(2,1)S(1)}, bf16[256,512]{1,0:T(8,128)(2,1)S(1)}, u32[]{:S(2)}, u32[]{:S(2)}) collective-permute-start(bf16[256,512]{1,0:T(8,128)(2,1)S(1)} %get-tuple-element.98), channel_id=1, source_target_pairs={{0,1},{1,0},{2,3},{3,2},{4,5},{5,4},{6,7},{7,6},{8,9},{9,8},{10,11... | collective-permute-start | bytes 786440 | tf_op jit(solution)/shard_map/ppermute | solution.py:400
  32.2 16.3 %copy-start.3 = (bf16[3,512,512]{2,1,0:T(8,128)(2,1)S(1)}, bf16[3,512,512]{2,1,0:T(8,128)(2,1)}, u32[]{:S(2)}) copy-start(bf16[3,512,512]{2,1,0:T(8,128)(2,1)} %weights.11) | copy-start | bytes 4718596
  32.2 8.4 %collective-permute-start.8 = (bf16[256,512]{1,0:T(8,128)(2,1)S(1)}, bf16[256,512]{1,0:T(8,128)(2,1)S(1)}, u32[]{:S(2)}, u32[]{:S(2)}) collective-permute-start(bf16[256,512]{1,0:T(8,128)(2,1)S(1)} %add_convert_fusion.1), channel_id=1, source_target_pairs={{0,2},{2,0},{1,3},{3,1},{4,6},{6,4},{5,7},{7,5},{8,10},{10,8},{9,1... | collective-permute-start | bytes 786440 | tf_op jit(solution)/shard_map/ppermute | solution.py:400
  40.7 1.6 %collective-permute-start.9 = (bf16[256,512]{1,0:T(8,128)(2,1)S(1)}, bf16[256,512]{1,0:T(8,128)(2,1)S(1)}, u32[]{:S(2)}, u32[]{:S(2)}) collective-permute-start(bf16[256,512]{1,0:T(8,128)(2,1)S(1)} %add_convert_fusion.refs_1_), channel_id=1, source_target_pairs={{0,1},{1,0},{2,3},{3,2},{4,5},{5,4},{6,7},{7,6},{8,9},{9,8},{10,11... | collective-permute-start | bytes 786440 | tf_op jit(solution)/shard_map/ppermute | solution.py:400
  43.3 6.7 %collective-permute-start.10 = (bf16[32,512]{1,0:T(8,128)(2,1)S(1)}, bf16[32,512]{1,0:T(8,128)(2,1)S(1)}, u32[]{:S(2)}, u32[]{:S(2)}) collective-permute-start(bf16[32,512]{1,0:T(8,128)(2,1)S(1)} %get-tuple-element.100), channel_id=1, source_target_pairs={{0,4},{1,9},{4,0},{5,13},{8,12},{9,1},{12,8},{13,5},{2,6},{3,11},{... | collective-permute-start | bytes 98312 | tf_op jit(solution)/shard_map/ppermute | solution.py:559
  43.4 7.3 %collective-permute-start.11 = (bf16[32,512]{1,0:T(8,128)(2,1)S(1)}, bf16[32,512]{1,0:T(8,128)(2,1)S(1)}, u32[]{:S(2)}, u32[]{:S(2)}) collective-permute-start(bf16[32,512]{1,0:T(8,128)(2,1)S(1)} %get-tuple-element.101), channel_id=1, source_target_pairs={{0,12},{4,8},{8,4},{12,0},{1,13},{5,9},{9,5},{13,1},{2,14},{6,10},... | collective-permute-start | bytes 98312 | tf_op jit(solution)/shard_map/ppermute | solution.py:409
  50.7 1.5 %copy-start.4 = (bf16[3,512,512]{2,1,0:T(8,128)(2,1)S(1)}, bf16[3,512,512]{2,1,0:T(8,128)(2,1)}, u32[]{:S(2)}) copy-start(bf16[3,512,512]{2,1,0:T(8,128)(2,1)} %refs_9_.9) | copy-start | bytes 4718596
  50.7 1.5 %copy-start.9 = (f32[3,512]{1,0:T(4,128)S(1)}, f32[3,512]{1,0:T(4,128)}, u32[]{:S(2)}) copy-start(f32[3,512]{1,0:T(4,128)} %refs_8_.10) | copy-start | bytes 18436
  50.7 1.5 %collective-permute-start.12 = (bf16[32,512]{1,0:T(8,128)(2,1)S(1)}, bf16[32,512]{1,0:T(8,128)(2,1)S(1)}, u32[]{:S(2)}, u32[]{:S(2)}) collective-permute-start(bf16[32,512]{1,0:T(8,128)(2,1)S(1)} %collective-permute-done.10.refs_3_), channel_id=1, source_target_pairs={{0,1},{1,0},{2,3},{3,2},{4,5},{5,4},{6,7},{7,6},{8,9},{9,8},{10,11... | collective-permute-start | bytes 98312 | tf_op jit(solution)/shard_map/ppermute | solution.py:400
  55.5 5.1 %collective-permute-start.13 = (bf16[32,512]{1,0:T(8,128)(2,1)S(1)}, bf16[32,512]{1,0:T(8,128)(2,1)S(1)}, u32[]{:S(2)}, u32[]{:S(2)}) collective-permute-start(bf16[32,512]{1,0:T(8,128)(2,1)S(1)} %get-tuple-element.113), channel_id=1, source_target_pairs={{0,4},{1,9},{4,0},{5,13},{8,12},{9,1},{12,8},{13,5},{2,6},{3,11},{... | collective-permute-start | bytes 98312 | tf_op jit(solution)/shard_map/ppermute | solution.py:559
  56.9 5.9 %collective-permute-start.14 = (bf16[32,512]{1,0:T(8,128)(2,1)S(1)}, bf16[32,512]{1,0:T(8,128)(2,1)S(1)}, u32[]{:S(2)}, u32[]{:S(2)}) collective-permute-start(bf16[32,512]{1,0:T(8,128)(2,1)S(1)} %get-tuple-element.114), channel_id=1, source_target_pairs={{0,12},{4,8},{8,4},{12,0},{1,13},{5,9},{9,5},{13,1},{2,14},{6,10},... | collective-permute-start | bytes 98312 | tf_op jit(solution)/shard_map/ppermute | solution.py:409
  62.8 1.3 collective-permute-start.15
  67.6 4.2 %collective-permute-start.16 = (bf16[32,512]{1,0:T(8,128)(2,1)S(1)}, bf16[32,512]{1,0:T(8,128)(2,1)S(1)}, u32[]{:S(2)}, u32[]{:S(2)}) collective-permute-start(bf16[32,512]{1,0:T(8,128)(2,1)S(1)} %get-tuple-element.123), channel_id=1, source_target_pairs={{0,4},{1,9},{4,0},{5,13},{8,12},{9,1},{12,8},{13,5},{2,6},{3,11},{... | collective-permute-start | bytes 98312 | tf_op jit(solution)/shard_map/ppermute | solution.py:559
  67.7 5.9 %collective-permute-start.17 = (bf16[32,512]{1,0:T(8,128)(2,1)S(1)}, bf16[32,512]{1,0:T(8,128)(2,1)S(1)}, u32[]{:S(2)}, u32[]{:S(2)}) collective-permute-start(bf16[32,512]{1,0:T(8,128)(2,1)S(1)} %get-tuple-element.124), channel_id=1, source_target_pairs={{0,12},{4,8},{8,4},{12,0},{1,13},{5,9},{9,5},{13,1},{2,14},{6,10},... | collective-permute-start | bytes 98312 | tf_op jit(solution)/shard_map/ppermute | solution.py:409
  73.6 1.4 %copy-start.6 = (bf16[512,512]{1,0:T(8,128)(2,1)S(1)}, bf16[512,512]{1,0:T(8,128)(2,1)}, u32[]{:S(2)}) copy-start(bf16[512,512]{1,0:T(8,128)(2,1)} %upstream.1) | copy-start | bytes 1572868
  73.6 1.4 %collective-permute-start.18 = (bf16[32,512]{1,0:T(8,128)(2,1)S(1)}, bf16[32,512]{1,0:T(8,128)(2,1)S(1)}, u32[]{:S(2)}, u32[]{:S(2)}) collective-permute-start(bf16[32,512]{1,0:T(8,128)(2,1)S(1)} %collective-permute-done.16.refs_3_), channel_id=1, source_target_pairs={{0,1},{1,0},{2,3},{3,2},{4,5},{5,4},{6,7},{7,6},{8,9},{9,8},{10,11... | collective-permute-start | bytes 98312 | tf_op jit(solution)/shard_map/ppermute | solution.py:400
  80.6 3.9 %collective-permute-start.19 = (bf16[32,512]{1,0:T(8,128)(2,1)S(1)}, bf16[32,512]{1,0:T(8,128)(2,1)S(1)}, u32[]{:S(2)}, u32[]{:S(2)}) collective-permute-start(bf16[32,512]{1,0:T(8,128)(2,1)S(1)} %get-tuple-element.134), channel_id=1, source_target_pairs={{0,4},{1,9},{4,0},{5,13},{8,12},{9,1},{12,8},{13,5},{2,6},{3,11},{... | collective-permute-start | bytes 98312 | tf_op jit(solution)/shard_map/ppermute | solution.py:559
  80.7 6.1 %collective-permute-start.20 = (bf16[32,512]{1,0:T(8,128)(2,1)S(1)}, bf16[32,512]{1,0:T(8,128)(2,1)S(1)}, u32[]{:S(2)}, u32[]{:S(2)}) collective-permute-start(bf16[32,512]{1,0:T(8,128)(2,1)S(1)} %get-tuple-element.135), channel_id=1, source_target_pairs={{12,0},{8,4},{4,8},{0,12},{13,1},{9,5},{5,9},{1,13},{14,2},{10,6},... | collective-permute-start | bytes 98312 | tf_op jit(solution)/shard_map/ppermute | solution.py:414
  86.8 1.5 %collective-permute-start.21 = (bf16[32,512]{1,0:T(8,128)(2,1)S(1)}, bf16[32,512]{1,0:T(8,128)(2,1)S(1)}, u32[]{:S(2)}, u32[]{:S(2)}) collective-permute-start(bf16[32,512]{1,0:T(8,128)(2,1)S(1)} %collective-permute-done.19.refs_1_), channel_id=1, source_target_pairs={{0,1},{1,0},{2,3},{3,2},{4,5},{5,4},{6,7},{7,6},{8,9},{9,8},{10,11... | collective-permute-start | bytes 98312 | tf_op jit(solution)/shard_map/ppermute | solution.py:400
  91.0 4.2 %collective-permute-start.22 = (bf16[32,512]{1,0:T(8,128)(2,1)S(1)}, bf16[32,512]{1,0:T(8,128)(2,1)S(1)}, u32[]{:S(2)}, u32[]{:S(2)}) collective-permute-start(bf16[32,512]{1,0:T(8,128)(2,1)S(1)} %get-tuple-element.143), channel_id=1, source_target_pairs={{0,4},{1,9},{4,0},{5,13},{8,12},{9,1},{12,8},{13,5},{2,6},{3,11},{... | collective-permute-start | bytes 98312 | tf_op jit(solution)/shard_map/ppermute | solution.py:559
  91.9 5.7 %collective-permute-start.23 = (bf16[32,512]{1,0:T(8,128)(2,1)S(1)}, bf16[32,512]{1,0:T(8,128)(2,1)S(1)}, u32[]{:S(2)}, u32[]{:S(2)}) collective-permute-start(bf16[32,512]{1,0:T(8,128)(2,1)S(1)} %get-tuple-element.144), channel_id=1, source_target_pairs={{12,0},{8,4},{4,8},{0,12},{13,1},{9,5},{5,9},{1,13},{14,2},{10,6},... | collective-permute-start | bytes 98312 | tf_op jit(solution)/shard_map/ppermute | solution.py:414
  97.6 1.8 %collective-permute-start.24 = (bf16[32,512]{1,0:T(8,128)(2,1)S(1)}, bf16[32,512]{1,0:T(8,128)(2,1)S(1)}, u32[]{:S(2)}, u32[]{:S(2)}) collective-permute-start(bf16[32,512]{1,0:T(8,128)(2,1)S(1)} %collective-permute-done.22.refs_1_), channel_id=1, source_target_pairs={{0,1},{1,0},{2,3},{3,2},{4,5},{5,4},{6,7},{7,6},{8,9},{9,8},{10,11... | collective-permute-start | bytes 98312 | tf_op jit(solution)/shard_map/ppermute | solution.py:400
  102.0 4.0 %collective-permute-start.25 = (bf16[32,512]{1,0:T(8,128)(2,1)S(1)}, bf16[32,512]{1,0:T(8,128)(2,1)S(1)}, u32[]{:S(2)}, u32[]{:S(2)}) collective-permute-start(bf16[32,512]{1,0:T(8,128)(2,1)S(1)} %get-tuple-element.152), channel_id=1, source_target_pairs={{0,4},{1,9},{4,0},{5,13},{8,12},{9,1},{12,8},{13,5},{2,6},{3,11},{... | collective-permute-start | bytes 98312 | tf_op jit(solution)/shard_map/ppermute | solution.py:559
  102.0 5.8 %collective-permute-start.26 = (bf16[32,512]{1,0:T(8,128)(2,1)S(1)}, bf16[32,512]{1,0:T(8,128)(2,1)S(1)}, u32[]{:S(2)}, u32[]{:S(2)}) collective-permute-start(bf16[32,512]{1,0:T(8,128)(2,1)S(1)} %get-tuple-element.153), channel_id=1, source_target_pairs={{12,0},{8,4},{4,8},{0,12},{13,1},{9,5},{5,9},{1,13},{14,2},{10,6},... | collective-permute-start | bytes 98312 | tf_op jit(solution)/shard_map/ppermute | solution.py:414
  107.9 1.5 %collective-permute-start.27 = (bf16[32,512]{1,0:T(8,128)(2,1)S(1)}, bf16[32,512]{1,0:T(8,128)(2,1)S(1)}, u32[]{:S(2)}, u32[]{:S(2)}) collective-permute-start(bf16[32,512]{1,0:T(8,128)(2,1)S(1)} %collective-permute-done.25.refs_1_), channel_id=1, source_target_pairs={{0,1},{1,0},{2,3},{3,2},{4,5},{5,4},{6,7},{7,6},{8,9},{9,8},{10,11... | collective-permute-start | bytes 98312 | tf_op jit(solution)/shard_map/ppermute | solution.py:400
  110.8 6.4 %collective-permute-start.28 = (bf16[128,512]{1,0:T(8,128)(2,1)S(1)}, bf16[128,512]{1,0:T(8,128)(2,1)S(1)}, u32[]{:S(2)}, u32[]{:S(2)}) collective-permute-start(bf16[128,512]{1,0:T(8,128)(2,1)S(1)} %get-tuple-element.171), channel_id=1, source_target_pairs={{4,0},{0,4},{12,8},{8,12},{5,1},{1,5},{13,9},{9,13},{6,2},{2,6},{1... | collective-permute-start | bytes 393224 | tf_op jit(solution)/shard_map/ppermute | solution.py:414
  111.7 8.2 %collective-permute-start.31 = (bf16[128,512]{1,0:T(8,128)(2,1)S(1)}, bf16[128,512]{1,0:T(8,128)(2,1)S(1)}, u32[]{:S(2)}, u32[]{:S(2)}) collective-permute-start(bf16[128,512]{1,0:T(8,128)(2,1)S(1)} %get-tuple-element.175), channel_id=1, source_target_pairs={{4,0},{0,4},{12,8},{8,12},{5,1},{1,5},{13,9},{9,13},{6,2},{2,6},{1... | collective-permute-start | bytes 393224 | tf_op jit(solution)/shard_map/ppermute | solution.py:414
  112.9 20.8 %copy-start.1 = (s32[1,4,32]{2,1,0:T(4,128)S(1)}, s32[1,4,32]{2,1,0:T(4,128)}, u32[]{:S(2)}) copy-start(s32[1,4,32]{2,1,0:T(4,128)} %param.22) | copy-start | bytes 1540
  117.2 15.2 %collective-permute-start.29 = (bf16[256,512]{1,0:T(8,128)(2,1)S(1)}, bf16[256,512]{1,0:T(8,128)(2,1)S(1)}, u32[]{:S(2)}, u32[]{:S(2)}) collective-permute-start(bf16[256,512]{1,0:T(8,128)(2,1)S(1)} %get-tuple-element.173), channel_id=1, source_target_pairs={{4,0},{0,4},{12,8},{8,12},{5,1},{1,5},{13,9},{9,13},{6,2},{2,6},{1... | collective-permute-start | bytes 786440 | tf_op jit(solution)/shard_map/ppermute | solution.py:414
  118.1 9.6 %collective-permute-start.30 = (bf16[128,512]{1,0:T(8,128)(2,1)S(1)}, bf16[128,512]{1,0:T(8,128)(2,1)S(1)}, u32[]{:S(2)}, u32[]{:S(2)}) collective-permute-start(bf16[128,512]{1,0:T(8,128)(2,1)S(1)} %get-tuple-element.174), channel_id=1, source_target_pairs={{8,0},{12,4},{0,8},{4,12},{9,1},{13,5},{1,9},{5,13},{10,2},{14,6},... | collective-permute-start | bytes 393224 | tf_op jit(solution)/shard_map/ppermute | solution.py:414
  119.9 12.4 %collective-permute-start.32 = (bf16[128,512]{1,0:T(8,128)(2,1)S(1)}, bf16[128,512]{1,0:T(8,128)(2,1)S(1)}, u32[]{:S(2)}, u32[]{:S(2)}) collective-permute-start(bf16[128,512]{1,0:T(8,128)(2,1)S(1)} %shard_map.195), channel_id=1, source_target_pairs={{8,0},{12,4},{0,8},{4,12},{9,1},{13,5},{1,9},{5,13},{10,2},{14,6},... | collective-permute-start | bytes 393224 | tf_op jit(solution)/shard_map/ppermute | solution.py:414

commit v7 on v6

--- a/solution.py
+++ b/solution.py
@@ -141,20 +141,13 @@
     copies[2].wait()
 
 
-def left_kernel(first, rows, notes, _, left, payload, arrived):
-    grid = rows.shape[0]
-    copies = [
-        pltpu.make_async_copy(rows.at[first:], left, arrived.at[0]),
-        pltpu.make_async_copy(rows, payload.at[0:grid], arrived.at[1]),
-        pltpu.make_async_copy(notes.at[first:], payload.at[grid:], arrived.at[2]),
-    ]
-    for copy in copies:
-        copy.start()
-    for copy in copies:
-        copy.wait()
-
-
-def encode_kernel(counts, first, last, halves, *refs):
+def again_kernel(payload, _, out, arrived):
+    copy = pltpu.make_async_copy(payload, out, arrived.at[0])
+    copy.start()
+    copy.wait()
+
+
+def encode_kernel(steps, first, last, halves, *refs):
     refs = list(refs)
     meta, base, w_grid = refs[:3]
     del refs[:3]
@@ -164,19 +157,15 @@
     else:
         total_in = refs.pop(0)
         projected = base[...]
-    payloads = []
-    for count in counts:
-        payloads.append(refs[:count])
-        del refs[:count]
-    steps = len(counts)
+    payloads = refs[:steps]
+    del refs[:steps]
     picks, slopes = refs[:steps], refs[steps : 2 * steps]
     del refs[: 2 * steps]
     total = None if first else total_in[...]
     nodes = projected.shape[0]
     for payload, pick, slope_out in zip(payloads, picks, slopes):
         grid = pick.shape[0]
-        rows = jnp.concatenate([piece[0 : grid // len(payload), :] for piece in payload], axis=0)
-        notes = payload[0][grid // len(payload) :, 0:grid].astype(f32)
+        notes = payload[grid:, 0:grid].astype(f32)
         target = jnp.full((1, grid), -1.0, f32)
         for at in range(0, notes.shape[0] // 3 * 3, 3):
             named = notes[at : at + 1] == meta[1:2, 0:grid].astype(f32)
@@ -185,7 +174,7 @@
         column = jnp.concatenate([upright(target[:, at : at + LANES]) for at in range(0, grid, LANES)], axis=0)
         picked = pick_rows(column, 0, nodes)
         pick[...] = picked
-        pre = dot(rows, w_grid[...]) + dot(picked, projected)
+        pre = dot(payload[0:grid, :], w_grid[...]) + dot(picked, projected)
         act, slope = gated(pre)
         slope_out[...] = slope.astype(bf16)
         added = dot(pick_columns(target, 0, nodes), act.astype(bf16))
@@ -212,8 +201,8 @@
 
 def hand_out(rows, outs, spots):
     rows = rows.astype(bf16)
-    for out, spot in zip(outs, spots):
-        out[...] = rows[spot : spot + out.shape[0]]
+    for out, (first, count) in zip(outs, spots):
+        out[...] = rows[first : first + count]
 
 
 def start_kernel(halves, spots, *refs):
@@ -253,18 +242,24 @@
         pre[at : at + BLOCK, :] = dot(here[skip + at : skip + at + BLOCK, :], table[...])
 
 
-def stack_halo(halos, halo):
+def pass_kernel(own, got, out):
+    rows = own.shape[0]
+    out[0:rows, :] = own[...]
+    out[rows:, :] = got[rows:, :]
+
+
+def stack_halo(inward, halos, halo):
     at = 0
-    for block in halos:
-        halo[at : at + block.shape[0], :] = block[...]
-        at += block.shape[0]
+    for rows, block in zip(inward, halos):
+        halo[at : at + rows, :] = block[0:rows, :]
+        at += rows
     if at < halo.shape[0]:
         halo[at:, :] = jnp.zeros((halo.shape[0] - at, halo.shape[1]), bf16)
 
 
-def node_sum(pres, halos, halo_here, there, slope_out, halo, act_out):
+def node_sum(inward, pres, halos, halo_here, there, slope_out, halo, act_out):
     nodes = there.shape[0] // 2
-    stack_halo(halos, halo)
+    stack_halo(inward, halos, halo)
     half = pres[0].shape[0]
     for at in range(0, 2 * half, BLOCK):
         block = slice(at, at + BLOCK)
@@ -275,13 +270,13 @@
     return dot(there[nodes:, :], act_out[...])
 
 
-def layer_kernel(layer, shifts, spots, *refs):
+def layer_kernel(layer, inward, spots, *refs):
     hidden, pres = refs[0], refs[1:3]
-    halos, refs = refs[3 : 3 + shifts], refs[3 + shifts :]
+    halos, refs = refs[3 : 3 + len(inward)], refs[3 + len(inward) :]
     halo_here, there, w_out, gain, w_send, list_here = refs[:6]
     hidden_out, agg_out, slope_out, sent_out = refs[6:10]
     outs = refs[10:-2]
-    total = node_sum(pres, halos, halo_here, there, slope_out, *refs[-2:])
+    total = node_sum(inward, pres, halos, halo_here, there, slope_out, *refs[-2:])
     agg = dot(total.astype(bf16), w_out[layer])
     agg_out[...] = agg
     fresh = (hidden[...].astype(f32) + agg * norm_scale(agg) * gain[layer : layer + 1, :]).astype(bf16)
@@ -301,14 +296,14 @@
     hand_out(dot(halo_there[...], grad_pre[...]), outs, spots)
 
 
-def turn_kernel(layer, shifts, spots, *refs):
+def turn_kernel(layer, inward, spots, *refs):
     hidden, pres = refs[0], refs[1:3]
-    halos, refs = refs[3 : 3 + shifts], refs[3 + shifts :]
+    halos, refs = refs[3 : 3 + len(inward)], refs[3 + len(inward) :]
     halo_here, there, w_out, gain, here, halo_there, cot = refs[:7]
     hidden_out, grad_pre = refs[7:9]
     outs = refs[9:-2]
     slope, halo = refs[-2:]
-    total = node_sum(pres, halos, halo_here, there, slope, halo, grad_pre)
+    total = node_sum(inward, pres, halos, halo_here, there, slope, halo, grad_pre)
     agg = dot(total.astype(bf16), w_out[layer])
     gain_row = gain[layer : layer + 1, :]
     hidden_out[...] = (hidden[...].astype(f32) + agg * norm_scale(agg) * gain_row).astype(bf16)
@@ -321,20 +316,20 @@
     rest[...] = upstream[...].astype(f32) + dot_back(sums, weights[layer])
 
 
-def arrived(rest, returned, list_there, w_send, halo):
-    stack_halo(returned, halo)
+def arrived(inward, rest, returned, list_there, w_send, halo):
+    stack_halo(inward, returned, halo)
     projected = dot_back(halo[...], w_send).astype(bf16)
     return rest[...] + dot(list_there[...], projected)
 
 
-def back_kernel(layer, shifts, spots, *refs):
+def back_kernel(layer, inward, spots, *refs):
     rest = refs[0]
-    returned, refs = refs[1 : 1 + shifts], refs[1 + shifts :]
+    returned, refs = refs[1 : 1 + len(inward)], refs[1 + len(inward) :]
     list_there, w_send, agg, slope, gain, w_out, here, halo_there = refs[:8]
     upstream_out, grad_pre = refs[8:10]
     outs = refs[10:-1]
     halo = refs[-1]
-    upstream = arrived(rest, returned, list_there, w_send[layer + 1], halo)
+    upstream = arrived(inward, rest, returned, list_there, w_send[layer + 1], halo)
     upstream_out[...] = upstream
     grad_agg = norm_back(agg[...], gain[layer : layer + 1, :], upstream)
     edge_grads(grad_agg, w_out[layer], here, halo_there, slope, grad_pre, outs, spots)
@@ -344,12 +339,12 @@
     return (dot(pick, spread) * slope.astype(f32)).astype(bf16)
 
 
-def finish_kernel(shifts, *refs):
+def finish_kernel(inward, *refs):
     rest = refs[0]
-    returned, refs = refs[1 : 1 + shifts], refs[1 + shifts :]
+    returned, refs = refs[1 : 1 + len(inward)], refs[1 + len(inward) :]
     list_there, w_send, enc_sum, gain, w_enc_out, pick, slope, spread_out = refs[:8]
     outs, halo = refs[8:-1], refs[-1]
-    upstream = arrived(rest, returned, list_there, w_send[0], halo)
+    upstream = arrived(inward, rest, returned, list_there, w_send[0], halo)
     spread = dot_back(norm_back(enc_sum[...], gain[...], upstream).astype(bf16), w_enc_out[...]).astype(bf16)
     spread_out[...] = spread
     at = 0
@@ -456,43 +451,32 @@
     in_place = [pltpu.with_memory_space_constraint(array, pltpu.HBM) for array in (grid_feats, g2m_shard.T, g2m_node.T)]
     (payload,) = call(
         note_kernel,
-        [((piece_rows + EXTRA, width), bf16)],
+        [((grid + EXTRA, width), bf16)],
         [((tops, grid), i32), ((tops, grid), i32)],
         copied=True,
     )(*in_place)
 
+    payload, sender_slots = lax.optimization_barrier((payload, sender_slots))
     place = sender_slots - nodes
     away = partner(shard, place // depth, shards)
     if shards & (shards - 1):
         away = lax.rem(shard - place // depth + shards, shards)
-    core = lax.axis_index("rep")
-    shared = shards == 4 and halves == 2
-    steps = jnp.arange(1, shards, dtype=i32)
-    if shared:
-        steps = jnp.where((core == 1) & (steps < 3), 3 - steps, steps)
+    if relayed:
+        away = jnp.where(away < 3, 3 - away, away)
     slots = jnp.where(sender_slots < nodes, sender_slots, nodes + (away - 1) * depth + place % depth)
     both = jnp.stack([slots, receivers])
     others = [shifted(both, "rep", step) for step in range(1, halves)]
     if relayed:
-        left, whole = call(
-            functools.partial(left_kernel, piece_rows),
-            [((grid - piece_rows, width), bf16), ((grid + EXTRA, width), bf16)],
-            copied=True,
-        )(in_place[0], payload, others[0])
-        across = [sent_to(payload, 2), sent_to(left, 2)]
-        payloads = [[whole], [sent_to(whole, 1)], across, [sent_to(across[0], 1)]]
+        across = sent_to(payload, 2)
+        (again,) = call(again_kernel, [((grid + EXTRA, width), bf16)], copied=True)(payload, others[0])
+        payloads = [again, sent_to(again, 1), across]
     else:
-        payloads = [[payload]] + [[sent_to(payload, step)] for step in range(1, shards)]
+        payloads = [payload] + [sent_to(payload, step) for step in range(1, shards)]
     both = in_order([both] + others, "rep")
     both = in_order([both] + [shifted(both, "feat", step) for step in range(1, feats)], "feat")
     both = both.reshape(feats * halves, 2, edges)
     all_slots, all_receivers = both[:, 0].reshape(1, -1), both[:, 1].reshape(1, -1)
-    if shared:
-        entry = all_slots - nodes
-        moved = jnp.where(entry < depth, depth, -depth)
-        turned = (core == 1) & (entry >= 0) & (entry < 2 * depth)
-        all_slots = all_slots + jnp.where(turned, moved, 0)
-    readers = partner(shard, steps, shards)
+    readers = partner(shard, jnp.arange(1, shards, dtype=i32), shards)
     lists = jnp.take(halo_index[0], readers, axis=0).reshape(1, -1)
     here, there, halo_here, halo_there, list_here, list_there = call(
         place_kernel,
@@ -508,10 +492,10 @@
     )(all_slots, all_receivers, lists)
 
     if relayed:
-        across[-1], list_here = lax.optimization_barrier((across[-1], list_here))
-        payloads[-1].append(sent_to(across[-1], 1))
-
-    meta = jnp.broadcast_to(jnp.stack([core, shard]).astype(i32)[:, None], (2, width))
+        across, list_here = lax.optimization_barrier((across, list_here))
+        payloads.append(sent_to(across, 1))
+
+    meta = jnp.broadcast_to(jnp.stack([lax.axis_index("rep"), shard]).astype(i32)[:, None], (2, width))
     node_f32, node_bf16 = ((nodes, width), f32), ((nodes, width), bf16)
     row_shape, half = ((grid, width), bf16), nodes // halves
     square = (nodes, width, width)
@@ -526,12 +510,12 @@
         outs += [((half, width), f32)] + [((half, width), bf16)] * (halves - 1) if last else [node_f32]
         got = list(
             call(
-                functools.partial(encode_kernel, [len(block) for block in group], first, last, halves),
+                functools.partial(encode_kernel, count, first, last, halves),
                 outs,
                 (),
                 [square] * first + [(grid, width, width), (grid, nodes, width), (nodes, grid, width)] * count,
             )(
-                meta, base, w_enc_grid, *((w_enc_mesh, list_here) if first else (total,)), *(piece for block in group for piece in block)
+                meta, base, w_enc_grid, *((w_enc_mesh, list_here) if first else (total,)), *group
             )
         )
         enc_picks += got[:count]
@@ -550,18 +534,17 @@
     part = sum(piece.astype(f32) for piece in pieces).astype(bf16)
     parts = [part] + [shifted(part, "rep", -step) for step in range(1, halves)]
 
-    spots = (0, 2 * depth) if shared else tuple(range(0, listed_rows, depth))
-    listed = [((depth, width), bf16)] * len(spots)
-
-    def exchange(blocks, send, early):
-        if not shared:
+    spots = [(depth, 2 * depth), (0, depth)] if relayed else [(at, depth) for at in range(0, listed_rows, depth)]
+    inward = [depth, 2 * depth] if relayed else [depth] * shifts
+    listed = [((rows, width), bf16) for _, rows in spots]
+
+    def exchange(blocks, send, early, stages):
+        if not relayed:
             return [send(block, step + 1) for step, block in enumerate(blocks)], early
-        first = lax.ppermute(
-            blocks[0], ("mesh", "rep"), [(2 * at + side, 2 * (at ^ 1 + side) + side) for at in range(4) for side in range(2)]
-        )
-        third = send(blocks[1], 3)
-        first, third, early = lax.optimization_barrier((first, third, early))
-        return [first, shifted(first, "rep", 1), third], early
+        got = send(blocks[0], stages[0])
+        got, early = lax.optimization_barrier((got, early))
+        (both_blocks,) = call(pass_kernel, [((2 * depth, width), bf16)])(blocks[1], got)
+        return [got, send(both_blocks, stages[1])], early
 
     hidden, enc_sum, sent, *outgoing = call(
         functools.partial(start_kernel, halves, spots), [node_bf16, node_f32, node_bf16] + listed, [node_bf16],
@@ -578,14 +561,14 @@
         early = call(
             functools.partial(local_kernel, layer), [half_f32, ((2 * nodes, width), bf16)], (), [square, half_product]
         )(hidden, sent, here, w_recv)
-        halos, (pre, both_tables) = exchange(outgoing, sent_to, early)
+        halos, (pre, both_tables) = exchange(outgoing, sent_to, early, (2, 1))
         (more,) = call(local_more_kernel, [half_f32], (), [half_product])(both_tables, here)
         return hidden, pre, more, *halos
 
     records = []
     for layer in range(LAYERS - 1):
         hidden, agg, slope, sent, *outgoing = call(
-            functools.partial(layer_kernel, layer, shifts, spots),
+            functools.partial(layer_kernel, layer, inward, spots),
             [node_bf16, node_f32, edge_bf16, node_bf16] + listed,
             [halo, edge_bf16],
             forward_products + [square, (listed_rows, nodes, width)],
@@ -593,7 +576,7 @@
         records.append((agg, slope))
     last = LAYERS - 1
     final_mesh, grad_pre, *outgoing = call(
-        functools.partial(turn_kernel, last, shifts, spots), [node_bf16, edge_bf16] + listed, [edge_bf16, halo],
+        functools.partial(turn_kernel, last, inward, spots), [node_bf16, edge_bf16] + listed, [edge_bf16, halo],
         forward_products + backward_products,
     )(*arriving(last), halo_here, there, w_out, layer_gain, here, halo_there, out_cot)
     upstream = out_cot
@@ -605,12 +588,12 @@
             )(upstream, grad_pre, there, weights)
             return rest
 
-        returned, early = exchange(outgoing, sent_back, rest_of(0, upstream, w_send))
+        returned, early = exchange(outgoing, sent_back, rest_of(0, upstream, w_send), (1, 2))
         rest = rest_of(1, early, w_recv)
         if layer:
             agg, slope = records[layer - 1]
             upstream, grad_pre, *outgoing = call(
-                functools.partial(back_kernel, layer - 1, shifts, spots),
+                functools.partial(back_kernel, layer - 1, inward, spots),
                 [node_f32, edge_bf16] + listed,
                 [back_halo],
                 backward_products + [(listed_rows, width, width), (nodes, listed_rows, width)],
@@ -618,7 +601,7 @@
     piece = ((piece_rows, width), bf16)
     one = (grid, nodes, width)
     spread, *far = call(
-        functools.partial(finish_kernel, shifts),
+        functools.partial(finish_kernel, inward),
         [node_bf16] + [piece] * cuts,
         [back_halo],
         [square, (listed_rows, width, width), (nodes, listed_rows, width), one],

time: 134 us -> 144 us (1.075)
  waiting for transfers between devices: 44.3 us -> 66.7 us
  starting transfers between devices: 37.1 us -> 26 us
    ppermute x8 -> x9, waiting for transfers between devices: 11.9 us -> 26.3 us  [sent_to(): lax.ppermute(value, 'mesh', [(at, partner(at, step, size)) for at in rang...]
    ppermute x8 -> x11, waiting for transfers between devices: 21.6 us -> 29.8 us  [sent_back(): lax.ppermute(value, 'mesh', [(partner(at, step, size), at) for at in rang...]
    ppermute x8 -> x9, starting transfers between devices: 18.9 us -> 12.8 us  [sent_to(): lax.ppermute(value, 'mesh', [(at, partner(at, step, size)) for at in rang...]
    ppermute x6 -> x0, starting transfers between devices: 2.65 us -> none  [exchange(): lax.ppermute(blocks[0], ('mesh', 'rep'), [(2 * at + side, 2 * (at ^ 1 + s...]
    ppermute x8 -> x11, starting transfers between devices: 11.8 us -> 9.68 us  [sent_back(): lax.ppermute(value, 'mesh', [(partner(at, step, size), at) for at in rang...]
    pallas_call x30 -> x36, Pallas kernels: 48.5 us -> 47.6 us  [run(): pl.pallas_call(body, out_shape=tuple((jax.ShapeDtypeStruct(shape, dtype)...]
    ppermute x11 -> x5, starting transfers between devices: 3.76 us -> 3.52 us  [shifted(): lax.ppermute(value, axis, [(at, (at + by) % size) for at in range(size)])]
    ppermute x11 -> x5, waiting for transfers between devices: 10.3 us -> 10.5 us  [shifted(): lax.ppermute(value, axis, [(at, (at + by) % size) for at in range(size)])]
  transfers between devices with their start and end apart: 33 -> 25, of which waited for: 18 -> 22; matrix products, arithmetic and copies ran while one was open for 1% -> 1% of each run, Pallas kernels for 20% -> 17%
where the time goes in v7:
time: 144 us
  waiting for transfers between devices  66.7 us (46%)
  Pallas kernels  47.6 us (33%)
  starting transfers between devices  26 us (18%)
  other arithmetic  1.76 us (1%)
    pallas_call x36, Pallas kernels, run(): pl.pallas_call(body, out_shape=tuple((jax.ShapeDtypeStruct(shape, dtype)...  47.6 us
    ppermute x11, waiting for transfers between devices, sent_back(): lax.ppermute(value, 'mesh', [(partner(at, step, size), at) for at in rang...  29.8 us
    ppermute x9, waiting for transfers between devices, sent_to(): lax.ppermute(value, 'mesh', [(at, partner(at, step, size)) for at in rang...  26.3 us
    ppermute x9, starting transfers between devices, sent_to(): lax.ppermute(value, 'mesh', [(at, partner(at, step, size)) for at in rang...  12.8 us
    ppermute x5, waiting for transfers between devices, shifted(): lax.ppermute(value, axis, [(at, (at + by) % size) for at in range(size)])  10.5 us
    ppermute x11, starting transfers between devices, sent_back(): lax.ppermute(value, 'mesh', [(partner(at, step, size), at) for at in rang...  9.68 us
    ppermute x5, starting transfers between devices, shifted(): lax.ppermute(value, axis, [(at, (at + by) % size) for at in range(size)])  3.52 us
  transfers between devices with their start and end apart: 25, of which 22 were waited for; matrix products, arithmetic and copies ran while one was open for 1% of the time, Pallas kernels for 17%

profile of v7, /device:TPU:0, one launch (start us, length us, event | category | flops | bytes accessed | tf_op | source)
XLA Modules:
  0.0 143.8 jit_solution(15278031731255554545)
XLA Ops:
  0.7 1.0 shard_map.167.payload
  1.7 0.7 compare_select_fusion.1
  2.4 0.7 fusion.8
  3.5 3.7 %collective-permute-start = (bf16[272,512]{1,0:T(8,128)(2,1)S(1)}, bf16[272,512]{1,0:T(8,128)(2,1)S(1)}, u32[]{:S(2)}, u32[]{:S(2)}) collective-permute-start(bf16[272,512]{1,0:T(8,128)(2,1)S(1)} %shard_map.167.payload), channel_id=1, source_target_pairs={{0,8},{4,12},{8,0},{12,4},{1,9},{5,13},{9,1},{13,5},{2,10},{6,14},... | collective-permute-start | bytes 835592 | tf_op jit(solution)/shard_map/ppermute | solution.py:404
  7.2 0.6 gather_fusion
  8.0 1.6 %collective-permute-start.2 = (s32[2,2,512]{2,1,0:T(2,128)S(1)}, s32[2,2,512]{2,1,0:T(2,128)S(1)}, u32[]{:S(2)}, u32[]{:S(2)}) collective-permute-start(s32[2,2,512]{2,1,0:T(2,128)S(1)} %fusion.1), channel_id=1, source_target_pairs={{0,2},{2,0},{1,3},{3,1},{4,6},{6,4},{5,7},{7,5},{8,10},{10,8},{9,1... | collective-permute-start | bytes 24584 | tf_op jit(solution)/shard_map/ppermute | solution.py:395
  9.6 1.6 %collective-permute-start.3 = (bf16[272,512]{1,0:T(8,128)(2,1)S(1)}, bf16[272,512]{1,0:T(8,128)(2,1)S(1)}, u32[]{:S(2)}, u32[]{:S(2)}) collective-permute-start(bf16[272,512]{1,0:T(8,128)(2,1)S(1)} %shard_map.169.refs_5_), channel_id=1, source_target_pairs={{0,4},{4,0},{8,12},{12,8},{1,5},{5,1},{9,13},{13,9},{2,6},{6,2},{1... | collective-permute-start | bytes 835592 | tf_op jit(solution)/shard_map/ppermute | solution.py:404
  11.8 3.5 %shard_map.168 = (bf16[2048,1024]{1,0:T(8,128)(2,1)S(1)}, bf16[1024,2048]{1,0:T(8,128)(2,1)S(1)}, bf16[2048,128]{1,0:T(8,128)(2,1)S(1)}, bf16[128,2048]{1,0:T(8,...) custom-call(s32[1,2048]{1,0:T(1,128)S(1)} %bitcast.22, s32[1,2048]{1,0:T(1,128)S(1)} %bitcast.21, ...), custom_call_target="tpu_custom_call" | custom-call | flops 3221225472 | bytes 9650560 | tf_op jit(solution)/shard_map/pallas_call | solution.py:82
  15.3 5.2 %collective-permute-done.refs_4_ = bf16[272,512]{1,0:T(8,128)(2,1)S(1)} collective-permute-done((bf16[272,512]{1,0:T(8,128)(2,1)S(1)}, bf16[272,512]{1,0:T(8,128)(2,1)S(1)}, u32[]{:S(2)}, u32[]{:S(2)}) %collective-permute-start) | collective-permute-done | bytes 278560 | tf_op jit(solution)/shard_map/ppermute | solution.py:404
  20.5 0.7 collective-permute-start.4
  21.3 1.7 %collective-permute-done.3.refs_6_ = bf16[272,512]{1,0:T(8,128)(2,1)S(1)} collective-permute-done((bf16[272,512]{1,0:T(8,128)(2,1)S(1)}, bf16[272,512]{1,0:T(8,128)(2,1)S(1)}, u32[]{:S(2)}, u32[]{:S(2)}) %collective-permute-start.3) | collective-permute-done | bytes 278560 | tf_op jit(solution)/shard_map/ppermute | solution.py:404
  23.0 1.7 %shard_map.170 = (bf16[256,512]{1,0:T(8,128)(2,1)S(1)}, bf16[256,512]{1,0:T(8,128)(2,1)S(1)}, bf16[256,512]{1,0:T(8,128)(2,1)S(1)}, bf16[256,512]{1,0:T(8,128)(2...) custom-call(s32[2,512]{1,0:T(2,128)S(1)} %broadcast_in_dim.19.refs_0_, bf16[512,512]{1,0:T(8,128)(2,1)S(1)} %copy-done.8, ...), custom_call_target="tpu_custom_call" | custom-call | flops 1073741824 | bytes 4853760 | tf_op jit(solution)/shard_map/pallas_call | solution.py:82
  24.7 0.9 shard_map.171
  25.6 3.3 %collective-permute-done.4.refs_4_ = bf16[272,512]{1,0:T(8,128)(2,1)S(1)} collective-permute-done((bf16[272,512]{1,0:T(8,128)(2,1)S(1)}, bf16[272,512]{1,0:T(8,128)(2,1)S(1)}, u32[]{:S(2)}, u32[]{:S(2)}) %collective-permute-start.4) | collective-permute-done | bytes 278560 | tf_op jit(solution)/shard_map/ppermute | solution.py:404
  28.9 0.9 shard_map.172
  29.9 1.5 %collective-permute-done.5 = bf16[256,512]{1,0:T(8,128)(2,1)S(1)} collective-permute-done((bf16[256,512]{1,0:T(8,128)(2,1)S(1)}, bf16[256,512]{1,0:T(8,128)(2,1)S(1)}, u32[]{:S(2)}, u32[]{:S(2)}) %collective-permute-start.5) | collective-permute-done | bytes 262176 | tf_op jit(solution)/shard_map/ppermute | solution.py:395
  31.5 1.4 collective-permute-start.6
  32.9 7.0 %collective-permute-done.6 = bf16[256,512]{1,0:T(8,128)(2,1)S(1)} collective-permute-done((bf16[256,512]{1,0:T(8,128)(2,1)S(1)}, bf16[256,512]{1,0:T(8,128)(2,1)S(1)}, u32[]{:S(2)}, u32[]{:S(2)}) %collective-permute-start.6) | collective-permute-done | bytes 262176 | tf_op jit(solution)/shard_map/ppermute | solution.py:395
  40.1 1.5 %collective-permute-done.7.refs_2_ = bf16[256,512]{1,0:T(8,128)(2,1)S(1)} collective-permute-done((bf16[256,512]{1,0:T(8,128)(2,1)S(1)}, bf16[256,512]{1,0:T(8,128)(2,1)S(1)}, u32[]{:S(2)}, u32[]{:S(2)}) %collective-permute-start.7) | collective-permute-done | bytes 262176 | tf_op jit(solution)/shard_map/ppermute | solution.py:395
  41.6 1.0 shard_map.173
  42.6 2.6 %collective-permute-start.8 = (bf16[64,512]{1,0:T(8,128)(2,1)S(1)}, bf16[64,512]{1,0:T(8,128)(2,1)S(1)}, u32[]{:S(2)}, u32[]{:S(2)}) collective-permute-start(bf16[64,512]{1,0:T(8,128)(2,1)S(1)} %get-tuple-element.94), channel_id=1, source_target_pairs={{0,8},{4,12},{8,0},{12,4},{1,9},{5,13},{9,1},{13,5},{2,10},{6,14},... | collective-permute-start | bytes 196616 | tf_op jit(solution)/shard_map/ppermute | solution.py:404
  45.3 1.5 %shard_map.174 = (f32[1024,512]{1,0:T(8,128)S(1)}, bf16[1024,512]{1,0:T(8,128)(2,1)S(1)}) custom-call(bf16[512,512]{1,0:T(8,128)(2,1)S(1)} %get-tuple-element.93.hidden.refs_0_, bf16[512,512]{1,0:T(8,128)(2,1)S(1)} %get-tuple-element.95.sent, bf16[2048,1024]{1,0:T(8,128)(2,1)S(1)} %get-tuple-element.96.here.refs_9_, bf16[3,512,512]{2,1,0:T(8,128)(2,1)S(1)} %copy-done.3), custom_call_target="tpu_custom_call" | custom-call | flops 1342177280 | bytes 9961472 | tf_op jit(solution)/shard_map/pallas_call | solution.py:82
  46.8 2.5 %collective-permute-done.8.got.refs_3_ = bf16[64,512]{1,0:T(8,128)(2,1)S(1)} collective-permute-done((bf16[64,512]{1,0:T(8,128)(2,1)S(1)}, bf16[64,512]{1,0:T(8,128)(2,1)S(1)}, u32[]{:S(2)}, u32[]{:S(2)}) %collective-permute-start.8) | collective-permute-done | bytes 65568 | tf_op jit(solution)/shard_map/ppermute | solution.py:404
  49.3 0.6 collective-permute-start.9
  49.8 1.2 shard_map.175.refs_2_
  51.1 2.5 %collective-permute-done.9.refs_4_ = bf16[64,512]{1,0:T(8,128)(2,1)S(1)} collective-permute-done((bf16[64,512]{1,0:T(8,128)(2,1)S(1)}, bf16[64,512]{1,0:T(8,128)(2,1)S(1)}, u32[]{:S(2)}, u32[]{:S(2)}) %collective-permute-start.9) | collective-permute-done | bytes 65568 | tf_op jit(solution)/shard_map/ppermute | solution.py:404
  53.6 3.2 %shard_map.177 = (bf16[512,512]{1,0:T(8,128)(2,1)S(1)}, f32[512,512]{1,0:T(8,128)S(1)}, bf16[2048,512]{1,0:T(8,128)(2,1)S(1)}, bf16[512,512]{1,0:T(8,128)(2,1)S(...) custom-call(bf16[512,512]{1,0:T(8,128)(2,1)S(1)} %get-tuple-element.93.hidden.refs_0_, ...), custom_call_target="tpu_custom_call" | custom-call | flops 1929379840 | bytes 17111040 | tf_op jit(solution)/shard_map/pallas_call | solution.py:82
  56.9 1.9 %collective-permute-start.10 = (bf16[64,512]{1,0:T(8,128)(2,1)S(1)}, bf16[64,512]{1,0:T(8,128)(2,1)S(1)}, u32[]{:S(2)}, u32[]{:S(2)}) collective-permute-start(bf16[64,512]{1,0:T(8,128)(2,1)S(1)} %get-tuple-element.106), channel_id=1, source_target_pairs={{0,8},{4,12},{8,0},{12,4},{1,9},{5,13},{9,1},{13,5},{2,10},{6,14},... | collective-permute-start | bytes 196616 | tf_op jit(solution)/shard_map/ppermute | solution.py:404
  58.8 1.5 %shard_map.178 = (f32[1024,512]{1,0:T(8,128)S(1)}, bf16[1024,512]{1,0:T(8,128)(2,1)S(1)}) custom-call(bf16[512,512]{1,0:T(8,128)(2,1)S(1)} %get-tuple-element.105.hidden.refs_0_, bf16[512,512]{1,0:T(8,128)(2,1)S(1)} %get-tuple-element.107.sent, bf16[2048,1024]{1,0:T(8,128)(2,1)S(1)} %get-tuple-element.96.here.refs_9_, bf16[3,512,512]{2,1,0:T(8,128)(2,1)S(1)} %copy-done.3), custom_call_target="tpu_custom_call" | custom-call | flops 1342177280 | bytes 9961472 | tf_op jit(solution)/shard_map/pallas_call | solution.py:82
  60.3 2.5 %collective-permute-done.10.got.refs_3_ = bf16[64,512]{1,0:T(8,128)(2,1)S(1)} collective-permute-done((bf16[64,512]{1,0:T(8,128)(2,1)S(1)}, bf16[64,512]{1,0:T(8,128)(2,1)S(1)}, u32[]{:S(2)}, u32[]{:S(2)}) %collective-permute-start.10) | collective-permute-done | bytes 65568 | tf_op jit(solution)/shard_map/ppermute | solution.py:404
  63.2 1.2 shard_map.179.refs_2_
  64.4 2.7 %collective-permute-done.11.refs_4_ = bf16[64,512]{1,0:T(8,128)(2,1)S(1)} collective-permute-done((bf16[64,512]{1,0:T(8,128)(2,1)S(1)}, bf16[64,512]{1,0:T(8,128)(2,1)S(1)}, u32[]{:S(2)}, u32[]{:S(2)}) %collective-permute-start.11) | collective-permute-done | bytes 65568 | tf_op jit(solution)/shard_map/ppermute | solution.py:404
  67.1 3.5 %shard_map.181 = (bf16[512,512]{1,0:T(8,128)(2,1)S(1)}, f32[512,512]{1,0:T(8,128)S(1)}, bf16[2048,512]{1,0:T(8,128)(2,1)S(1)}, bf16[512,512]{1,0:T(8,128)(2,1)S(...) custom-call(bf16[512,512]{1,0:T(8,128)(2,1)S(1)} %get-tuple-element.105.hidden.refs_0_, ...), custom_call_target="tpu_custom_call" | custom-call | flops 1929379840 | bytes 17111040 | tf_op jit(solution)/shard_map/pallas_call | solution.py:82
  70.6 1.3 collective-permute-start.12
  71.9 1.5 %shard_map.182 = (f32[1024,512]{1,0:T(8,128)S(1)}, bf16[1024,512]{1,0:T(8,128)(2,1)S(1)}) custom-call(bf16[512,512]{1,0:T(8,128)(2,1)S(1)} %get-tuple-element.114.hidden.refs_0_, bf16[512,512]{1,0:T(8,128)(2,1)S(1)} %get-tuple-element.116.sent, bf16[2048,1024]{1,0:T(8,128)(2,1)S(1)} %get-tuple-element.96.here.refs_9_, bf16[3,512,512]{2,1,0:T(8,128)(2,1)S(1)} %copy-done.3), custom_call_target="tpu_custom_call" | custom-call | flops 1342177280 | bytes 9961472 | tf_op jit(solution)/shard_map/pallas_call | solution.py:82
  73.4 2.9 %collective-permute-done.12.got.refs_3_ = bf16[64,512]{1,0:T(8,128)(2,1)S(1)} collective-permute-done((bf16[64,512]{1,0:T(8,128)(2,1)S(1)}, bf16[64,512]{1,0:T(8,128)(2,1)S(1)}, u32[]{:S(2)}, u32[]{:S(2)}) %collective-permute-start.12) | collective-permute-done | bytes 65568 | tf_op jit(solution)/shard_map/ppermute | solution.py:404
  76.4 1.2 shard_map.183.refs_2_
  77.7 3.0 %collective-permute-done.13.refs_4_ = bf16[64,512]{1,0:T(8,128)(2,1)S(1)} collective-permute-done((bf16[64,512]{1,0:T(8,128)(2,1)S(1)}, bf16[64,512]{1,0:T(8,128)(2,1)S(1)}, u32[]{:S(2)}, u32[]{:S(2)}) %collective-permute-start.13) | collective-permute-done | bytes 65568 | tf_op jit(solution)/shard_map/ppermute | solution.py:404
  80.7 5.7 %shard_map.185 = (bf16[512,512]{1,0:T(8,128)(2,1)}, bf16[2048,512]{1,0:T(8,128)(2,1)S(1)}, bf16[64,512]{1,0:T(8,128)(2,1)S(1)}, bf16[32,512]{1,0:T(8,128)(2,1)S(1)}) custom-call(bf16[512,512]{1,0:T(8,128)(2,1)S(1)} %get-tuple-element.114.hidden.refs_0_, f32[1024,512]{1,0:T(8,128)S(1)} %get-tuple-element.119.refs_1_, f32[1024,512]{1,0:T(8,128)S(1)} %shard_map.183.refs_2_, ...), custom_call_target="tpu_custom_call" | custom-call | flops 3221225472 | bytes 19109888 | tf_op jit(solution)/shard_map/pallas_call | solution.py:82
  86.4 1.5 %shard_map.186.upstream = f32[512,512]{1,0:T(8,128)S(1)} custom-call(bf16[512,512]{1,0:T(8,128)(2,1)S(1)} %copy-done.6, bf16[2048,512]{1,0:T(8,128)(2,1)S(1)} %get-tuple-element.126.grad_pre, bf16[1024,2048]{1,0:T(8,128)(2,1)S(1)} %get-tuple-element.104.refs_6_.there, bf16[3,512,512]{2,1,0:T(8,128)(2,1)S(1)} %copy-done.2), custom_call_target="tpu_custom_call" | custom-call | flops 1342177280 | bytes 9437184 | tf_op jit(solution)/shard_map/pallas_call | solution.py:82
  87.9 2.7 %collective-permute-done.14.got.refs_1_ = bf16[64,512]{1,0:T(8,128)(2,1)S(1)} collective-permute-done((bf16[64,512]{1,0:T(8,128)(2,1)S(1)}, bf16[64,512]{1,0:T(8,128)(2,1)S(1)}, u32[]{:S(2)}, u32[]{:S(2)}) %collective-permute-start.14) | collective-permute-done | bytes 65568 | tf_op jit(solution)/shard_map/ppermute | solution.py:409
  90.6 0.9 collective-permute-start.15
  91.6 1.5 %shard_map.187.refs_0_ = f32[512,512]{1,0:T(8,128)S(1)} custom-call(f32[512,512]{1,0:T(8,128)S(1)} %shard_map.186.upstream, bf16[2048,512]{1,0:T(8,128)(2,1)S(1)} %get-tuple-element.126.grad_pre, bf16[1024,2048]{1,0:T(8,128)(2,1)S(1)} %get-tuple-element.104.refs_6_.there, bf16[3,512,512]{2,1,0:T(8,128)(2,1)S(1)} %copy-done.3), custom_call_target="tpu_custom_call" | custom-call | flops 1342177280 | bytes 9961472 | tf_op jit(solution)/shard_map/pallas_call | solution.py:82
  93.1 3.0 %collective-permute-done.15.refs_2_ = bf16[64,512]{1,0:T(8,128)(2,1)S(1)} collective-permute-done((bf16[64,512]{1,0:T(8,128)(2,1)S(1)}, bf16[64,512]{1,0:T(8,128)(2,1)S(1)}, u32[]{:S(2)}, u32[]{:S(2)}) %collective-permute-start.15) | collective-permute-done | bytes 65568 | tf_op jit(solution)/shard_map/ppermute | solution.py:409
  96.1 2.6 %shard_map.189 = (f32[512,512]{1,0:T(8,128)S(1)}, bf16[2048,512]{1,0:T(8,128)(2,1)S(1)}, bf16[64,512]{1,0:T(8,128)(2,1)S(1)}, bf16[32,512]{1,0:T(8,128)(2,1)S(1)}) custom-call(f32[512,512]{1,0:T(8,128)S(1)} %shard_map.187.refs_0_, bf16[64,512]{1,0:T(8,128)(2,1)S(1)} %collective-permute-done.14.got.refs_1_, ...), custom_call_target="tpu_custom_call" | custom-call | flops 1711276032 | bytes 15538176 | tf_op jit(solution)/shard_map/pallas_call | solution.py:82
  98.9 1.5 %shard_map.190.upstream = f32[512,512]{1,0:T(8,128)S(1)} custom-call(f32[512,512]{1,0:T(8,128)S(1)} %get-tuple-element.134.upstream, bf16[2048,512]{1,0:T(8,128)(2,1)S(1)} %get-tuple-element.135.grad_pre, bf16[1024,2048]{1,0:T(8,128)(2,1)S(1)} %get-tuple-element.104.refs_6_.there, bf16[3,512,512]{2,1,0:T(8,128)(2,1)S(1)} %copy-done.2), custom_call_target="tpu_custom_call" | custom-call | flops 1342177280 | bytes 9961472 | tf_op jit(solution)/shard_map/pallas_call | solution.py:82
  100.4 2.6 %collective-permute-done.16.got.refs_1_ = bf16[64,512]{1,0:T(8,128)(2,1)S(1)} collective-permute-done((bf16[64,512]{1,0:T(8,128)(2,1)S(1)}, bf16[64,512]{1,0:T(8,128)(2,1)S(1)}, u32[]{:S(2)}, u32[]{:S(2)}) %collective-permute-start.16) | collective-permute-done | bytes 65568 | tf_op jit(solution)/shard_map/ppermute | solution.py:409
  103.0 0.8 collective-permute-start.17
  103.8 1.5 %shard_map.191.refs_0_ = f32[512,512]{1,0:T(8,128)S(1)} custom-call(f32[512,512]{1,0:T(8,128)S(1)} %shard_map.190.upstream, bf16[2048,512]{1,0:T(8,128)(2,1)S(1)} %get-tuple-element.135.grad_pre, bf16[1024,2048]{1,0:T(8,128)(2,1)S(1)} %get-tuple-element.104.refs_6_.there, bf16[3,512,512]{2,1,0:T(8,128)(2,1)S(1)} %copy-done.3), custom_call_target="tpu_custom_call" | custom-call | flops 1342177280 | bytes 9961472 | tf_op jit(solution)/shard_map/pallas_call | solution.py:82
  105.3 3.4 %collective-permute-done.17.refs_2_ = bf16[64,512]{1,0:T(8,128)(2,1)S(1)} collective-permute-done((bf16[64,512]{1,0:T(8,128)(2,1)S(1)}, bf16[64,512]{1,0:T(8,128)(2,1)S(1)}, u32[]{:S(2)}, u32[]{:S(2)}) %collective-permute-start.17) | collective-permute-done | bytes 65568 | tf_op jit(solution)/shard_map/ppermute | solution.py:409
  108.7 2.8 %shard_map.193 = (f32[512,512]{1,0:T(8,128)S(1)}, bf16[2048,512]{1,0:T(8,128)(2,1)S(1)}, bf16[64,512]{1,0:T(8,128)(2,1)S(1)}, bf16[32,512]{1,0:T(8,128)(2,1)S(1)}) custom-call(f32[512,512]{1,0:T(8,128)S(1)} %shard_map.191.refs_0_, bf16[64,512]{1,0:T(8,128)(2,1)S(1)} %collective-permute-done.16.got.refs_1_, ...), custom_call_target="tpu_custom_call" | custom-call | flops 1711276032 | bytes 15538176 | tf_op jit(solution)/shard_map/pallas_call | solution.py:82
  111.6 1.5 %shard_map.194.upstream = f32[512,512]{1,0:T(8,128)S(1)} custom-call(f32[512,512]{1,0:T(8,128)S(1)} %get-tuple-element.142.upstream, bf16[2048,512]{1,0:T(8,128)(2,1)S(1)} %get-tuple-element.143.grad_pre, bf16[1024,2048]{1,0:T(8,128)(2,1)S(1)} %get-tuple-element.104.refs_6_.there, bf16[3,512,512]{2,1,0:T(8,128)(2,1)S(1)} %copy-done.2), custom_call_target="tpu_custom_call" | custom-call | flops 1342177280 | bytes 9961472 | tf_op jit(solution)/shard_map/pallas_call | solution.py:82
  113.1 3.5 %collective-permute-done.18.got.refs_1_ = bf16[64,512]{1,0:T(8,128)(2,1)S(1)} collective-permute-done((bf16[64,512]{1,0:T(8,128)(2,1)S(1)}, bf16[64,512]{1,0:T(8,128)(2,1)S(1)}, u32[]{:S(2)}, u32[]{:S(2)}) %collective-permute-start.18) | collective-permute-done | bytes 65568 | tf_op jit(solution)/shard_map/ppermute | solution.py:409
  116.9 1.5 %shard_map.195.refs_0_ = f32[512,512]{1,0:T(8,128)S(1)} custom-call(f32[512,512]{1,0:T(8,128)S(1)} %shard_map.194.upstream, bf16[2048,512]{1,0:T(8,128)(2,1)S(1)} %get-tuple-element.143.grad_pre, bf16[1024,2048]{1,0:T(8,128)(2,1)S(1)} %get-tuple-element.104.refs_6_.there, bf16[3,512,512]{2,1,0:T(8,128)(2,1)S(1)} %copy-done.3), custom_call_target="tpu_custom_call" | custom-call | flops 1342177280 | bytes 9961472 | tf_op jit(solution)/shard_map/pallas_call | solution.py:82
  118.5 4.4 %collective-permute-done.19.refs_2_ = bf16[64,512]{1,0:T(8,128)(2,1)S(1)} collective-permute-done((bf16[64,512]{1,0:T(8,128)(2,1)S(1)}, bf16[64,512]{1,0:T(8,128)(2,1)S(1)}, u32[]{:S(2)}, u32[]{:S(2)}) %collective-permute-start.19) | collective-permute-done | bytes 65568 | tf_op jit(solution)/shard_map/ppermute | solution.py:409
  122.9 1.4 shard_map.197
  124.3 1.7 %collective-permute-start.20 = (bf16[128,512]{1,0:T(8,128)(2,1)S(1)}, bf16[128,512]{1,0:T(8,128)(2,1)S(1)}, u32[]{:S(2)}, u32[]{:S(2)}) collective-permute-start(bf16[128,512]{1,0:T(8,128)(2,1)S(1)} %get-tuple-element.159), channel_id=1, source_target_pairs={{4,0},{0,4},{12,8},{8,12},{5,1},{1,5},{13,9},{9,13},{6,2},{2,6},{1... | collective-permute-start | bytes 393224 | tf_op jit(solution)/shard_map/ppermute | solution.py:409
  126.4 0.6 shard_map.198
  127.0 2.4 %collective-permute-done.20.passed = bf16[128,512]{1,0:T(8,128)(2,1)S(1)} collective-permute-done((bf16[128,512]{1,0:T(8,128)(2,1)S(1)}, bf16[128,512]{1,0:T(8,128)(2,1)S(1)}, u32[]{:S(2)}, u32[]{:S(2)}) %collective-permute-start.20) | collective-permute-done | bytes 131104 | tf_op jit(solution)/shard_map/ppermute | solution.py:409
  129.4 1.7 %collective-permute-start.21 = (bf16[256,512]{1,0:T(8,128)(2,1)S(1)}, bf16[256,512]{1,0:T(8,128)(2,1)S(1)}, u32[]{:S(2)}, u32[]{:S(2)}) collective-permute-start(bf16[256,512]{1,0:T(8,128)(2,1)S(1)} %get-tuple-element.161), channel_id=1, source_target_pairs={{4,0},{0,4},{12,8},{8,12},{5,1},{1,5},{13,9},{9,13},{6,2},{2,6},{1... | collective-permute-start | bytes 786440 | tf_op jit(solution)/shard_map/ppermute | solution.py:409
  131.0 3.5 %collective-permute-start.22 = (bf16[128,512]{1,0:T(8,128)(2,1)S(1)}, bf16[128,512]{1,0:T(8,128)(2,1)S(1)}, u32[]{:S(2)}, u32[]{:S(2)}) collective-permute-start(bf16[128,512]{1,0:T(8,128)(2,1)S(1)} %get-tuple-element.162), channel_id=1, source_target_pairs={{8,0},{12,4},{0,8},{4,12},{9,1},{13,5},{1,9},{5,13},{10,2},{14,6},... | collective-permute-start | bytes 393224 | tf_op jit(solution)/shard_map/ppermute | solution.py:409
  134.7 2.8 %collective-permute-done.22.piece = bf16[128,512]{1,0:T(8,128)(2,1)S(1)} collective-permute-done((bf16[128,512]{1,0:T(8,128)(2,1)S(1)}, bf16[128,512]{1,0:T(8,128)(2,1)S(1)}, u32[]{:S(2)}, u32[]{:S(2)}) %collective-permute-start.22) | collective-permute-done | bytes 131104 | tf_op jit(solution)/shard_map/ppermute | solution.py:409
  137.5 5.0 %collective-permute-done.24.refs_3_ = bf16[128,512]{1,0:T(8,128)(2,1)S(1)} collective-permute-done((bf16[128,512]{1,0:T(8,128)(2,1)S(1)}, bf16[128,512]{1,0:T(8,128)(2,1)S(1)}, u32[]{:S(2)}, u32[]{:S(2)}) %collective-permute-start.24) | collective-permute-done | bytes 131104 | tf_op jit(solution)/shard_map/ppermute | solution.py:409
  142.6 1.3 shard_map.202
  (66 shorter events, 3.4 us)
Async XLA Ops:
  0.6 6.6 %copy-start = (s32[1,4,32]{2,1,0:T(4,128)S(1)}, s32[1,4,32]{2,1,0:T(4,128)}, u32[]{:S(2)}) copy-start(s32[1,4,32]{2,1,0:T(4,128)} %param.22) | copy-start | bytes 1540
  3.1 4.9 %collective-permute-start.1 = (s32[2,512]{1,0:T(2,128)S(1)}, s32[2,512]{1,0:T(2,128)S(1)}, u32[]{:S(2)}, u32[]{:S(2)}) collective-permute-start(s32[2,512]{1,0:T(2,128)S(1)} %get-tuple-element.167), channel_id=1, source_target_pairs={{0,1},{1,0},{2,3},{3,2},{4,5},{5,4},{6,7},{7,6},{8,9},{9,8},{10,11... | collective-permute-start | bytes 12296 | tf_op jit(solution)/shard_map/ppermute | solution.py:395
  3.5 17.0 %collective-permute-start = (bf16[272,512]{1,0:T(8,128)(2,1)S(1)}, bf16[272,512]{1,0:T(8,128)(2,1)S(1)}, u32[]{:S(2)}, u32[]{:S(2)}) collective-permute-start(bf16[272,512]{1,0:T(8,128)(2,1)S(1)} %shard_map.167.payload), channel_id=1, source_target_pairs={{0,8},{4,12},{8,0},{12,4},{1,9},{5,13},{9,1},{13,5},{2,10},{6,14},... | collective-permute-start | bytes 835592 | tf_op jit(solution)/shard_map/ppermute | solution.py:404
  8.0 3.7 %collective-permute-start.2 = (s32[2,2,512]{2,1,0:T(2,128)S(1)}, s32[2,2,512]{2,1,0:T(2,128)S(1)}, u32[]{:S(2)}, u32[]{:S(2)}) collective-permute-start(s32[2,2,512]{2,1,0:T(2,128)S(1)} %fusion.1), channel_id=1, source_target_pairs={{0,2},{2,0},{1,3},{3,1},{4,6},{6,4},{5,7},{7,5},{8,10},{10,8},{9,1... | collective-permute-start | bytes 24584 | tf_op jit(solution)/shard_map/ppermute | solution.py:395
  9.6 13.3 %collective-permute-start.3 = (bf16[272,512]{1,0:T(8,128)(2,1)S(1)}, bf16[272,512]{1,0:T(8,128)(2,1)S(1)}, u32[]{:S(2)}, u32[]{:S(2)}) collective-permute-start(bf16[272,512]{1,0:T(8,128)(2,1)S(1)} %shard_map.169.refs_5_), channel_id=1, source_target_pairs={{0,4},{4,0},{8,12},{12,8},{1,5},{5,1},{9,13},{13,9},{2,6},{6,2},{1... | collective-permute-start | bytes 835592 | tf_op jit(solution)/shard_map/ppermute | solution.py:404
  11.7 11.3 %copy-start.5 = (bf16[512,512]{1,0:T(8,128)(2,1)S(1)}, bf16[512,512]{1,0:T(8,128)(2,1)}, u32[]{:S(2)}) copy-start(bf16[512,512]{1,0:T(8,128)(2,1)} %refs_4_.9) | copy-start | bytes 1572868
  11.8 11.2 %copy-start.8 = (bf16[512,512]{1,0:T(8,128)(2,1)S(1)}, bf16[512,512]{1,0:T(8,128)(2,1)}, u32[]{:S(2)}) copy-start(bf16[512,512]{1,0:T(8,128)(2,1)} %refs_3_.3) | copy-start | bytes 1572868
  11.8 11.2 %copy-start.11 = (bf16[512,512]{1,0:T(8,128)(2,1)S(1)}, bf16[512,512]{1,0:T(8,128)(2,1)}, u32[]{:S(2)}) copy-start(bf16[512,512]{1,0:T(8,128)(2,1)} %refs_3_.2) | copy-start | bytes 1572868
  20.5 8.4 %collective-permute-start.4 = (bf16[272,512]{1,0:T(8,128)(2,1)S(1)}, bf16[272,512]{1,0:T(8,128)(2,1)S(1)}, u32[]{:S(2)}, u32[]{:S(2)}) collective-permute-start(bf16[272,512]{1,0:T(8,128)(2,1)S(1)} %collective-permute-done.refs_4_), channel_id=1, source_target_pairs={{0,4},{4,0},{8,12},{12,8},{1,5},{5,1},{9,13},{13,9},{2,6},{6,2},{1... | collective-permute-start | bytes 835592 | tf_op jit(solution)/shard_map/ppermute | solution.py:404
  28.9 12.7 %copy-start.2 = (bf16[3,512,512]{2,1,0:T(8,128)(2,1)S(1)}, bf16[3,512,512]{2,1,0:T(8,128)(2,1)}, u32[]{:S(2)}) copy-start(bf16[3,512,512]{2,1,0:T(8,128)(2,1)} %refs_4_.8) | copy-start | bytes 4718596
  28.9 12.7 %copy-start.7 = (bf16[512,512]{1,0:T(8,128)(2,1)S(1)}, bf16[512,512]{1,0:T(8,128)(2,1)}, u32[]{:S(2)}) copy-start(bf16[512,512]{1,0:T(8,128)(2,1)} %refs_7_.11) | copy-start | bytes 1572868
  28.9 12.7 %copy-start.10 = (f32[512]{0:T(512)S(1)}, f32[512]{0:T(512)}, u32[]{:S(2)}) copy-start(f32[512]{0:T(512)} %param.26) | copy-start | bytes 6148
  29.8 1.6 %collective-permute-start.5 = (bf16[256,512]{1,0:T(8,128)(2,1)S(1)}, bf16[256,512]{1,0:T(8,128)(2,1)S(1)}, u32[]{:S(2)}, u32[]{:S(2)}) collective-permute-start(bf16[256,512]{1,0:T(8,128)(2,1)S(1)} %get-tuple-element.92), channel_id=1, source_target_pairs={{0,1},{1,0},{2,3},{3,2},{4,5},{5,4},{6,7},{7,6},{8,9},{9,8},{10,11... | collective-permute-start | bytes 786440 | tf_op jit(solution)/shard_map/ppermute | solution.py:395
  31.5 13.7 %copy-start.3 = (bf16[3,512,512]{2,1,0:T(8,128)(2,1)S(1)}, bf16[3,512,512]{2,1,0:T(8,128)(2,1)}, u32[]{:S(2)}) copy-start(bf16[3,512,512]{2,1,0:T(8,128)(2,1)} %weights.11) | copy-start | bytes 4718596
  31.5 8.4 %collective-permute-start.6 = (bf16[256,512]{1,0:T(8,128)(2,1)S(1)}, bf16[256,512]{1,0:T(8,128)(2,1)S(1)}, u32[]{:S(2)}, u32[]{:S(2)}) collective-permute-start(bf16[256,512]{1,0:T(8,128)(2,1)S(1)} %add_convert_fusion.1), channel_id=1, source_target_pairs={{0,2},{2,0},{1,3},{3,1},{4,6},{6,4},{5,7},{7,5},{8,10},{10,8},{9,1... | collective-permute-start | bytes 786440 | tf_op jit(solution)/shard_map/ppermute | solution.py:395
  40.0 1.6 %collective-permute-start.7 = (bf16[256,512]{1,0:T(8,128)(2,1)S(1)}, bf16[256,512]{1,0:T(8,128)(2,1)S(1)}, u32[]{:S(2)}, u32[]{:S(2)}) collective-permute-start(bf16[256,512]{1,0:T(8,128)(2,1)S(1)} %add_convert_fusion.refs_1_), channel_id=1, source_target_pairs={{0,1},{1,0},{2,3},{3,2},{4,5},{5,4},{6,7},{7,6},{8,9},{9,8},{10,11... | collective-permute-start | bytes 786440 | tf_op jit(solution)/shard_map/ppermute | solution.py:395
  42.6 6.6 %collective-permute-start.8 = (bf16[64,512]{1,0:T(8,128)(2,1)S(1)}, bf16[64,512]{1,0:T(8,128)(2,1)S(1)}, u32[]{:S(2)}, u32[]{:S(2)}) collective-permute-start(bf16[64,512]{1,0:T(8,128)(2,1)S(1)} %get-tuple-element.94), channel_id=1, source_target_pairs={{0,8},{4,12},{8,0},{12,4},{1,9},{5,13},{9,1},{13,5},{2,10},{6,14},... | collective-permute-start | bytes 196616 | tf_op jit(solution)/shard_map/ppermute | solution.py:404
  49.3 4.4 %copy-start.4 = (bf16[3,512,512]{2,1,0:T(8,128)(2,1)S(1)}, bf16[3,512,512]{2,1,0:T(8,128)(2,1)}, u32[]{:S(2)}) copy-start(bf16[3,512,512]{2,1,0:T(8,128)(2,1)} %refs_8_.9) | copy-start | bytes 4718596
  49.3 4.3 %copy-start.9 = (f32[3,512]{1,0:T(4,128)S(1)}, f32[3,512]{1,0:T(4,128)}, u32[]{:S(2)}) copy-start(f32[3,512]{1,0:T(4,128)} %refs_7_.10) | copy-start | bytes 18436
  49.3 4.3 %collective-permute-start.9 = (bf16[64,512]{1,0:T(8,128)(2,1)S(1)}, bf16[64,512]{1,0:T(8,128)(2,1)S(1)}, u32[]{:S(2)}, u32[]{:S(2)}) collective-permute-start(bf16[64,512]{1,0:T(8,128)(2,1)S(1)} %shard_map.176), channel_id=1, source_target_pairs={{0,4},{4,0},{8,12},{12,8},{1,5},{5,1},{9,13},{13,9},{2,6},{6,2},{1... | collective-permute-start | bytes 196616 | tf_op jit(solution)/shard_map/ppermute | solution.py:404
  56.9 5.9 %collective-permute-start.10 = (bf16[64,512]{1,0:T(8,128)(2,1)S(1)}, bf16[64,512]{1,0:T(8,128)(2,1)S(1)}, u32[]{:S(2)}, u32[]{:S(2)}) collective-permute-start(bf16[64,512]{1,0:T(8,128)(2,1)S(1)} %get-tuple-element.106), channel_id=1, source_target_pairs={{0,8},{4,12},{8,0},{12,4},{1,9},{5,13},{9,1},{13,5},{2,10},{6,14},... | collective-permute-start | bytes 196616 | tf_op jit(solution)/shard_map/ppermute | solution.py:404
  62.8 4.3 %collective-permute-start.11 = (bf16[64,512]{1,0:T(8,128)(2,1)S(1)}, bf16[64,512]{1,0:T(8,128)(2,1)S(1)}, u32[]{:S(2)}, u32[]{:S(2)}) collective-permute-start(bf16[64,512]{1,0:T(8,128)(2,1)S(1)} %shard_map.180), channel_id=1, source_target_pairs={{0,4},{4,0},{8,12},{12,8},{1,5},{5,1},{9,13},{13,9},{2,6},{6,2},{1... | collective-permute-start | bytes 196616 | tf_op jit(solution)/shard_map/ppermute | solution.py:404
  70.6 5.8 %collective-permute-start.12 = (bf16[64,512]{1,0:T(8,128)(2,1)S(1)}, bf16[64,512]{1,0:T(8,128)(2,1)S(1)}, u32[]{:S(2)}, u32[]{:S(2)}) collective-permute-start(bf16[64,512]{1,0:T(8,128)(2,1)S(1)} %get-tuple-element.115), channel_id=1, source_target_pairs={{0,8},{4,12},{8,0},{12,4},{1,9},{5,13},{9,1},{13,5},{2,10},{6,14},... | collective-permute-start | bytes 196616 | tf_op jit(solution)/shard_map/ppermute | solution.py:404
  76.3 4.3 %copy-start.6 = (bf16[512,512]{1,0:T(8,128)(2,1)S(1)}, bf16[512,512]{1,0:T(8,128)(2,1)}, u32[]{:S(2)}) copy-start(bf16[512,512]{1,0:T(8,128)(2,1)} %upstream.1) | copy-start | bytes 1572868
  76.3 4.3 %collective-permute-start.13 = (bf16[64,512]{1,0:T(8,128)(2,1)S(1)}, bf16[64,512]{1,0:T(8,128)(2,1)S(1)}, u32[]{:S(2)}, u32[]{:S(2)}) collective-permute-start(bf16[64,512]{1,0:T(8,128)(2,1)S(1)} %shard_map.184), channel_id=1, source_target_pairs={{0,4},{4,0},{8,12},{12,8},{1,5},{5,1},{9,13},{13,9},{2,6},{6,2},{1... | collective-permute-start | bytes 196616 | tf_op jit(solution)/shard_map/ppermute | solution.py:404
  86.4 4.3 %collective-permute-start.14 = (bf16[64,512]{1,0:T(8,128)(2,1)S(1)}, bf16[64,512]{1,0:T(8,128)(2,1)S(1)}, u32[]{:S(2)}, u32[]{:S(2)}) collective-permute-start(bf16[64,512]{1,0:T(8,128)(2,1)S(1)} %get-tuple-element.125), channel_id=1, source_target_pairs={{4,0},{0,4},{12,8},{8,12},{5,1},{1,5},{13,9},{9,13},{6,2},{2,6},{1... | collective-permute-start | bytes 196616 | tf_op jit(solution)/shard_map/ppermute | solution.py:409
  90.6 5.4 %collective-permute-start.15 = (bf16[64,512]{1,0:T(8,128)(2,1)S(1)}, bf16[64,512]{1,0:T(8,128)(2,1)S(1)}, u32[]{:S(2)}, u32[]{:S(2)}) collective-permute-start(bf16[64,512]{1,0:T(8,128)(2,1)S(1)} %shard_map.188), channel_id=1, source_target_pairs={{8,0},{12,4},{0,8},{4,12},{9,1},{13,5},{1,9},{5,13},{10,2},{14,6},... | collective-permute-start | bytes 196616 | tf_op jit(solution)/shard_map/ppermute | solution.py:409
  98.7 4.3 %collective-permute-start.16 = (bf16[64,512]{1,0:T(8,128)(2,1)S(1)}, bf16[64,512]{1,0:T(8,128)(2,1)S(1)}, u32[]{:S(2)}, u32[]{:S(2)}) collective-permute-start(bf16[64,512]{1,0:T(8,128)(2,1)S(1)} %get-tuple-element.133), channel_id=1, source_target_pairs={{4,0},{0,4},{12,8},{8,12},{5,1},{1,5},{13,9},{9,13},{6,2},{2,6},{1... | collective-permute-start | bytes 196616 | tf_op jit(solution)/shard_map/ppermute | solution.py:409
  103.0 5.7 %collective-permute-start.17 = (bf16[64,512]{1,0:T(8,128)(2,1)S(1)}, bf16[64,512]{1,0:T(8,128)(2,1)S(1)}, u32[]{:S(2)}, u32[]{:S(2)}) collective-permute-start(bf16[64,512]{1,0:T(8,128)(2,1)S(1)} %shard_map.192), channel_id=1, source_target_pairs={{8,0},{12,4},{0,8},{4,12},{9,1},{13,5},{1,9},{5,13},{10,2},{14,6},... | collective-permute-start | bytes 196616 | tf_op jit(solution)/shard_map/ppermute | solution.py:409
  111.5 5.1 %collective-permute-start.18 = (bf16[64,512]{1,0:T(8,128)(2,1)S(1)}, bf16[64,512]{1,0:T(8,128)(2,1)S(1)}, u32[]{:S(2)}, u32[]{:S(2)}) collective-permute-start(bf16[64,512]{1,0:T(8,128)(2,1)S(1)} %get-tuple-element.141), channel_id=1, source_target_pairs={{4,0},{0,4},{12,8},{8,12},{5,1},{1,5},{13,9},{9,13},{6,2},{2,6},{1... | collective-permute-start | bytes 196616 | tf_op jit(solution)/shard_map/ppermute | solution.py:409
  116.6 6.3 %collective-permute-start.19 = (bf16[64,512]{1,0:T(8,128)(2,1)S(1)}, bf16[64,512]{1,0:T(8,128)(2,1)S(1)}, u32[]{:S(2)}, u32[]{:S(2)}) collective-permute-start(bf16[64,512]{1,0:T(8,128)(2,1)S(1)} %shard_map.196), channel_id=1, source_target_pairs={{8,0},{12,4},{0,8},{4,12},{9,1},{13,5},{1,9},{5,13},{10,2},{14,6},... | collective-permute-start | bytes 196616 | tf_op jit(solution)/shard_map/ppermute | solution.py:409
  124.3 5.0 %collective-permute-start.20 = (bf16[128,512]{1,0:T(8,128)(2,1)S(1)}, bf16[128,512]{1,0:T(8,128)(2,1)S(1)}, u32[]{:S(2)}, u32[]{:S(2)}) collective-permute-start(bf16[128,512]{1,0:T(8,128)(2,1)S(1)} %get-tuple-element.159), channel_id=1, source_target_pairs={{4,0},{0,4},{12,8},{8,12},{5,1},{1,5},{13,9},{9,13},{6,2},{2,6},{1... | collective-permute-start | bytes 393224 | tf_op jit(solution)/shard_map/ppermute | solution.py:409
  126.0 8.6 %collective-permute-start.23 = (bf16[128,512]{1,0:T(8,128)(2,1)S(1)}, bf16[128,512]{1,0:T(8,128)(2,1)S(1)}, u32[]{:S(2)}, u32[]{:S(2)}) collective-permute-start(bf16[128,512]{1,0:T(8,128)(2,1)S(1)} %get-tuple-element.163), channel_id=1, source_target_pairs={{4,0},{0,4},{12,8},{8,12},{5,1},{1,5},{13,9},{9,13},{6,2},{2,6},{1... | collective-permute-start | bytes 393224 | tf_op jit(solution)/shard_map/ppermute | solution.py:409
  126.4 17.5 %copy-start.1 = (s32[1,4,32]{2,1,0:T(4,128)S(1)}, s32[1,4,32]{2,1,0:T(4,128)}, u32[]{:S(2)}) copy-start(s32[1,4,32]{2,1,0:T(4,128)} %param.22) | copy-start | bytes 1540
  129.4 13.2 %collective-permute-start.21 = (bf16[256,512]{1,0:T(8,128)(2,1)S(1)}, bf16[256,512]{1,0:T(8,128)(2,1)S(1)}, u32[]{:S(2)}, u32[]{:S(2)}) collective-permute-start(bf16[256,512]{1,0:T(8,128)(2,1)S(1)} %get-tuple-element.161), channel_id=1, source_target_pairs={{4,0},{0,4},{12,8},{8,12},{5,1},{1,5},{13,9},{9,13},{6,2},{2,6},{1... | collective-permute-start | bytes 786440 | tf_op jit(solution)/shard_map/ppermute | solution.py:409
  131.0 6.5 %collective-permute-start.22 = (bf16[128,512]{1,0:T(8,128)(2,1)S(1)}, bf16[128,512]{1,0:T(8,128)(2,1)S(1)}, u32[]{:S(2)}, u32[]{:S(2)}) collective-permute-start(bf16[128,512]{1,0:T(8,128)(2,1)S(1)} %get-tuple-element.162), channel_id=1, source_target_pairs={{8,0},{12,4},{0,8},{4,12},{9,1},{13,5},{1,9},{5,13},{10,2},{14,6},... | collective-permute-start | bytes 393224 | tf_op jit(solution)/shard_map/ppermute | solution.py:409
  134.6 8.0 %collective-permute-start.24 = (bf16[128,512]{1,0:T(8,128)(2,1)S(1)}, bf16[128,512]{1,0:T(8,128)(2,1)S(1)}, u32[]{:S(2)}, u32[]{:S(2)}) collective-permute-start(bf16[128,512]{1,0:T(8,128)(2,1)S(1)} %shard_map.201), channel_id=1, source_target_pairs={{8,0},{12,4},{0,8},{4,12},{9,1},{13,5},{1,9},{5,13},{10,2},{14,6},... | collective-permute-start | bytes 393224 | tf_op jit(solution)/shard_map/ppermute | solution.py:409

commit v8 on v7

--- a/solution.py
+++ b/solution.py
@@ -139,12 +139,6 @@
     if grid < payload.shape[1]:
         payload[first:, grid:] = jnp.zeros((EXTRA, payload.shape[1] - grid), bf16)
     copies[2].wait()
-
-
-def again_kernel(payload, _, out, arrived):
-    copy = pltpu.make_async_copy(payload, out, arrived.at[0])
-    copy.start()
-    copy.wait()
 
 
 def encode_kernel(steps, first, last, halves, *refs):
@@ -199,13 +193,15 @@
         sends[shift - 1][...] = half(shift).astype(bf16)
 
 
-def hand_out(rows, outs, spots):
+def hand_out(rows, outs):
     rows = rows.astype(bf16)
-    for out, (first, count) in zip(outs, spots):
-        out[...] = rows[first : first + count]
-
-
-def start_kernel(halves, spots, *refs):
+    at = 0
+    for out in outs:
+        out[...] = rows[at : at + out.shape[0]]
+        at += out.shape[0]
+
+
+def start_kernel(halves, *refs):
     meta = refs[0]
     parts = refs[1 : 1 + halves]
     mesh_init, w_enc_out, gain, w_send, list_here = refs[1 + halves : 6 + halves]
@@ -225,7 +221,7 @@
     hidden_out[...] = hidden
     projected = dot(hidden, w_send[0]).astype(bf16)
     sent[...] = projected
-    hand_out(dot(list_here[...], projected), outs, spots)
+    hand_out(dot(list_here[...], projected), outs)
 
 
 def local_kernel(layer, hidden, sent, here, w_recv, pre, table):
@@ -236,115 +232,105 @@
         pre[at : at + BLOCK, :] = dot(here[at : at + BLOCK, :], table[...])
 
 
-def local_more_kernel(table, here, pre):
-    skip = here.shape[0] - pre.shape[0]
-    for at in range(0, pre.shape[0], BLOCK):
-        pre[at : at + BLOCK, :] = dot(here[skip + at : skip + at + BLOCK, :], table[...])
-
-
-def pass_kernel(own, got, out):
-    rows = own.shape[0]
-    out[0:rows, :] = own[...]
-    out[rows:, :] = got[rows:, :]
-
-
-def stack_halo(inward, halos, halo):
+def stack_halo(halos, halo):
     at = 0
-    for rows, block in zip(inward, halos):
-        halo[at : at + rows, :] = block[0:rows, :]
-        at += rows
+    for block in halos:
+        halo[at : at + block.shape[0], :] = block[...]
+        at += block.shape[0]
     if at < halo.shape[0]:
         halo[at:, :] = jnp.zeros((halo.shape[0] - at, halo.shape[1]), bf16)
 
 
-def node_sum(inward, pres, halos, halo_here, there, slope_out, halo, act_out):
+def node_sum(pre, halos, halo_here, there, slope_out, halo, act_out):
     nodes = there.shape[0] // 2
-    stack_halo(inward, halos, halo)
-    half = pres[0].shape[0]
-    for at in range(0, 2 * half, BLOCK):
+    stack_halo(halos, halo)
+    for at in range(0, pre.shape[0], BLOCK):
         block = slice(at, at + BLOCK)
-        pre = pres[at // half][at % half : at % half + BLOCK, :]
-        act, slope = gated(pre + dot(halo_here[block, :], halo[...]))
+        act, slope = gated(pre[block, :] + dot(halo_here[block, :], halo[...]))
         slope_out[block, :] = slope.astype(bf16)
         act_out[block, :] = act.astype(bf16)
     return dot(there[nodes:, :], act_out[...])
 
 
-def layer_kernel(layer, inward, spots, *refs):
-    hidden, pres = refs[0], refs[1:3]
-    halos, refs = refs[3 : 3 + len(inward)], refs[3 + len(inward) :]
+def layer_kernel(layer, shifts, *refs):
+    hidden, pre = refs[:2]
+    halos, refs = refs[2 : 2 + shifts], refs[2 + shifts :]
     halo_here, there, w_out, gain, w_send, list_here = refs[:6]
     hidden_out, agg_out, slope_out, sent_out = refs[6:10]
     outs = refs[10:-2]
-    total = node_sum(inward, pres, halos, halo_here, there, slope_out, *refs[-2:])
+    total = node_sum(pre, halos, halo_here, there, slope_out, *refs[-2:])
     agg = dot(total.astype(bf16), w_out[layer])
     agg_out[...] = agg
     fresh = (hidden[...].astype(f32) + agg * norm_scale(agg) * gain[layer : layer + 1, :]).astype(bf16)
     hidden_out[...] = fresh
     projected = dot(fresh, w_send[layer + 1]).astype(bf16)
     sent_out[...] = projected
-    hand_out(dot(list_here[...], projected), outs, spots)
-
-
-def edge_grads(grad_agg, w_out, here, halo_there, slope, grad_pre, outs, spots):
+    hand_out(dot(list_here[...], projected), outs)
+
+
+def edge_grads(grad_agg, w_out, here, halo_there, slope, grad_pre, outs):
     nodes = grad_agg.shape[0]
     spread = dot_back(grad_agg.astype(bf16), w_out).astype(bf16)
     for at in range(0, slope.shape[0], BLOCK):
         block = slice(at, at + BLOCK)
         grad_act = dot(here[block, nodes:], spread)
         grad_pre[block, :] = (grad_act * slope[block, :].astype(f32)).astype(bf16)
-    hand_out(dot(halo_there[...], grad_pre[...]), outs, spots)
-
-
-def turn_kernel(layer, inward, spots, *refs):
-    hidden, pres = refs[0], refs[1:3]
-    halos, refs = refs[3 : 3 + len(inward)], refs[3 + len(inward) :]
+    hand_out(dot(halo_there[...], grad_pre[...]), outs)
+
+
+def turn_kernel(layer, shifts, *refs):
+    hidden, pre = refs[:2]
+    halos, refs = refs[2 : 2 + shifts], refs[2 + shifts :]
     halo_here, there, w_out, gain, here, halo_there, cot = refs[:7]
     hidden_out, grad_pre = refs[7:9]
     outs = refs[9:-2]
     slope, halo = refs[-2:]
-    total = node_sum(inward, pres, halos, halo_here, there, slope, halo, grad_pre)
+    total = node_sum(pre, halos, halo_here, there, slope, halo, grad_pre)
     agg = dot(total.astype(bf16), w_out[layer])
     gain_row = gain[layer : layer + 1, :]
     hidden_out[...] = (hidden[...].astype(f32) + agg * norm_scale(agg) * gain_row).astype(bf16)
-    edge_grads(norm_back(agg, gain_row, cot[...].astype(f32)), w_out[layer], here, halo_there, slope, grad_pre, outs, spots)
-
-
-def rest_kernel(layer, side, upstream, grad_pre, there, weights, rest):
+    edge_grads(norm_back(agg, gain_row, cot[...].astype(f32)), w_out[layer], here, halo_there, slope, grad_pre, outs)
+
+
+def rest_kernel(layer, upstream, grad_pre, there, w_send, w_recv, rest):
     nodes = upstream.shape[0]
-    sums = dot(there[side * nodes : (side + 1) * nodes, :], grad_pre[...]).astype(bf16)
-    rest[...] = upstream[...].astype(f32) + dot_back(sums, weights[layer])
-
-
-def arrived(inward, rest, returned, list_there, w_send, halo):
-    stack_halo(inward, returned, halo)
+    sums = dot(there[...], grad_pre[...]).astype(bf16)
+    rest[...] = (
+        upstream[...].astype(f32)
+        + dot_back(sums[0:nodes], w_send[layer])
+        + dot_back(sums[nodes:], w_recv[layer])
+    )
+
+
+def arrived(rest, returned, list_there, w_send, halo):
+    stack_halo(returned, halo)
     projected = dot_back(halo[...], w_send).astype(bf16)
     return rest[...] + dot(list_there[...], projected)
 
 
-def back_kernel(layer, inward, spots, *refs):
+def back_kernel(layer, shifts, *refs):
     rest = refs[0]
-    returned, refs = refs[1 : 1 + len(inward)], refs[1 + len(inward) :]
+    returned, refs = refs[1 : 1 + shifts], refs[1 + shifts :]
     list_there, w_send, agg, slope, gain, w_out, here, halo_there = refs[:8]
     upstream_out, grad_pre = refs[8:10]
     outs = refs[10:-1]
     halo = refs[-1]
-    upstream = arrived(inward, rest, returned, list_there, w_send[layer + 1], halo)
+    upstream = arrived(rest, returned, list_there, w_send[layer + 1], halo)
     upstream_out[...] = upstream
     grad_agg = norm_back(agg[...], gain[layer : layer + 1, :], upstream)
-    edge_grads(grad_agg, w_out[layer], here, halo_there, slope, grad_pre, outs, spots)
+    edge_grads(grad_agg, w_out[layer], here, halo_there, slope, grad_pre, outs)
 
 
 def pair_grads(spread, pick, slope):
     return (dot(pick, spread) * slope.astype(f32)).astype(bf16)
 
 
-def finish_kernel(inward, *refs):
+def finish_kernel(shifts, *refs):
     rest = refs[0]
-    returned, refs = refs[1 : 1 + len(inward)], refs[1 + len(inward) :]
+    returned, refs = refs[1 : 1 + shifts], refs[1 + shifts :]
     list_there, w_send, enc_sum, gain, w_enc_out, pick, slope, spread_out = refs[:8]
     outs, halo = refs[8:-1], refs[-1]
-    upstream = arrived(inward, rest, returned, list_there, w_send[0], halo)
+    upstream = arrived(rest, returned, list_there, w_send[0], halo)
     spread = dot_back(norm_back(enc_sum[...], gain[...], upstream).astype(bf16), w_enc_out[...]).astype(bf16)
     spread_out[...] = spread
     at = 0
@@ -456,27 +442,23 @@
         copied=True,
     )(*in_place)
 
-    payload, sender_slots = lax.optimization_barrier((payload, sender_slots))
     place = sender_slots - nodes
     away = partner(shard, place // depth, shards)
     if shards & (shards - 1):
         away = lax.rem(shard - place // depth + shards, shards)
-    if relayed:
-        away = jnp.where(away < 3, 3 - away, away)
-    slots = jnp.where(sender_slots < nodes, sender_slots, nodes + (away - 1) * depth + place % depth)
+    slots = jnp.where(sender_slots < nodes, sender_slots, nodes + (shifts - away) * depth + place % depth)
     both = jnp.stack([slots, receivers])
     others = [shifted(both, "rep", step) for step in range(1, halves)]
     if relayed:
         across = sent_to(payload, 2)
-        (again,) = call(again_kernel, [((grid + EXTRA, width), bf16)], copied=True)(payload, others[0])
-        payloads = [again, sent_to(again, 1), across]
+        payloads = [payload, sent_to(payload, 1), across]
     else:
         payloads = [payload] + [sent_to(payload, step) for step in range(1, shards)]
     both = in_order([both] + others, "rep")
     both = in_order([both] + [shifted(both, "feat", step) for step in range(1, feats)], "feat")
     both = both.reshape(feats * halves, 2, edges)
     all_slots, all_receivers = both[:, 0].reshape(1, -1), both[:, 1].reshape(1, -1)
-    readers = partner(shard, jnp.arange(1, shards, dtype=i32), shards)
+    readers = partner(shard, shards - jnp.arange(1, shards, dtype=i32), shards)
     lists = jnp.take(halo_index[0], readers, axis=0).reshape(1, -1)
     here, there, halo_here, halo_there, list_here, list_there = call(
         place_kernel,
@@ -534,41 +516,34 @@
     part = sum(piece.astype(f32) for piece in pieces).astype(bf16)
     parts = [part] + [shifted(part, "rep", -step) for step in range(1, halves)]
 
-    spots = [(depth, 2 * depth), (0, depth)] if relayed else [(at, depth) for at in range(0, listed_rows, depth)]
-    inward = [depth, 2 * depth] if relayed else [depth] * shifts
-    listed = [((rows, width), bf16) for _, rows in spots]
-
-    def exchange(blocks, send, early, stages):
-        if not relayed:
-            return [send(block, step + 1) for step, block in enumerate(blocks)], early
-        got = send(blocks[0], stages[0])
-        got, early = lax.optimization_barrier((got, early))
-        (both_blocks,) = call(pass_kernel, [((2 * depth, width), bf16)])(blocks[1], got)
-        return [got, send(both_blocks, stages[1])], early
+    listed = [((depth, width), bf16)] * shifts
+
+    def exchange(blocks, send):
+        return [send(block, shifts - at) for at, block in enumerate(blocks)]
 
     hidden, enc_sum, sent, *outgoing = call(
-        functools.partial(start_kernel, halves, spots), [node_bf16, node_f32, node_bf16] + listed, [node_bf16],
+        functools.partial(start_kernel, halves), [node_bf16, node_f32, node_bf16] + listed, [node_bf16],
         [square, square, (listed_rows, nodes, width)],
     )(meta, *parts, mesh_init, w_enc_out, enc_gain, w_send, list_here)
 
-    half_f32, edge_bf16 = ((all_edges // 2, width), f32), ((all_edges, width), bf16)
+    edge_f32, edge_bf16 = ((all_edges, width), f32), ((all_edges, width), bf16)
     halo, back_halo = ((wide, width), bf16), ((listed_rows, width), bf16)
     forward_products = [(all_edges, wide, width), (nodes, all_edges, width), square]
     backward_products = [square, (all_edges, nodes, width), (wide, all_edges, width)]
-    half_product = (all_edges // 2, 2 * nodes, width)
 
     def arriving(layer):
-        early = call(
-            functools.partial(local_kernel, layer), [half_f32, ((2 * nodes, width), bf16)], (), [square, half_product]
+        (pre,) = call(
+            functools.partial(local_kernel, layer),
+            [edge_f32],
+            [((2 * nodes, width), bf16)],
+            [square, (all_edges, 2 * nodes, width)],
         )(hidden, sent, here, w_recv)
-        halos, (pre, both_tables) = exchange(outgoing, sent_to, early, (2, 1))
-        (more,) = call(local_more_kernel, [half_f32], (), [half_product])(both_tables, here)
-        return hidden, pre, more, *halos
+        return hidden, pre, *exchange(outgoing, sent_to)
 
     records = []
     for layer in range(LAYERS - 1):
         hidden, agg, slope, sent, *outgoing = call(
-            functools.partial(layer_kernel, layer, inward, spots),
+            functools.partial(layer_kernel, layer, shifts),
             [node_bf16, node_f32, edge_bf16, node_bf16] + listed,
             [halo, edge_bf16],
             forward_products + [square, (listed_rows, nodes, width)],
@@ -576,24 +551,19 @@
         records.append((agg, slope))
     last = LAYERS - 1
     final_mesh, grad_pre, *outgoing = call(
-        functools.partial(turn_kernel, last, inward, spots), [node_bf16, edge_bf16] + listed, [edge_bf16, halo],
+        functools.partial(turn_kernel, last, shifts), [node_bf16, edge_bf16] + listed, [edge_bf16, halo],
         forward_products + backward_products,
     )(*arriving(last), halo_here, there, w_out, layer_gain, here, halo_there, out_cot)
     upstream = out_cot
     for layer in reversed(range(LAYERS)):
-
-        def rest_of(side, upstream, weights):
-            (rest,) = call(
-                functools.partial(rest_kernel, layer, side), [node_f32], (), [(nodes, all_edges, width), square]
-            )(upstream, grad_pre, there, weights)
-            return rest
-
-        returned, early = exchange(outgoing, sent_back, rest_of(0, upstream, w_send), (1, 2))
-        rest = rest_of(1, early, w_recv)
+        returned = exchange(outgoing, sent_back)
+        (rest,) = call(
+            functools.partial(rest_kernel, layer), [node_f32], (), [(2 * nodes, all_edges, width), square, square]
+        )(upstream, grad_pre, there, w_send, w_recv)
         if layer:
             agg, slope = records[layer - 1]
             upstream, grad_pre, *outgoing = call(
-                functools.partial(back_kernel, layer - 1, inward, spots),
+                functools.partial(back_kernel, layer - 1, shifts),
                 [node_f32, edge_bf16] + listed,
                 [back_halo],
                 backward_products + [(listed_rows, width, width), (nodes, listed_rows, width)],
@@ -601,7 +571,7 @@
     piece = ((piece_rows, width), bf16)
     one = (grid, nodes, width)
     spread, *far = call(
-        functools.partial(finish_kernel, inward),
+        functools.partial(finish_kernel, shifts),
         [node_bf16] + [piece] * cuts,
         [back_halo],
         [square, (listed_rows, width, width), (nodes, listed_rows, width), one],

time: 144 us -> 124 us (0.86)
  waiting for transfers between devices: 66.7 us -> 32.5 us
  starting transfers between devices: 26 us -> 41.3 us
    ppermute x9 -> x12, waiting for transfers between devices: 26.3 us -> 6.28 us  [sent_to(): lax.ppermute(value, 'mesh', [(at, partner(at, step, size)) for at in rang...]
    ppermute x11 -> x14, waiting for transfers between devices: 29.8 us -> 13.8 us  [sent_back(): lax.ppermute(value, 'mesh', [(partner(at, step, size), at) for at in rang...]
    ppermute x11 -> x14, starting transfers between devices: 9.68 us -> 18.5 us  [sent_back(): lax.ppermute(value, 'mesh', [(partner(at, step, size), at) for at in rang...]
    ppermute x9 -> x12, starting transfers between devices: 12.8 us -> 19.5 us  [sent_to(): lax.ppermute(value, 'mesh', [(at, partner(at, step, size)) for at in rang...]
    ppermute x5, waiting for transfers between devices: 10.5 us -> 12.4 us  [shifted(): lax.ppermute(value, axis, [(at, (at + by) % size) for at in range(size)])]
    pallas_call x36 -> x23, Pallas kernels: 47.6 us -> 46.5 us  [run(): pl.pallas_call(body, out_shape=tuple((jax.ShapeDtypeStruct(shape, dtype)...]
  transfers between devices with their start and end apart: 25 -> 31, of which waited for: 22 -> 12; matrix products, arithmetic and copies ran while one was open for 1% -> 2% of each run, Pallas kernels for 17% -> 19%
where the time goes in v8:
time: 124 us
  Pallas kernels  46.5 us (38%)
  starting transfers between devices  41.3 us (33%)
  waiting for transfers between devices  32.5 us (26%)
  other arithmetic  1.79 us (1%)
    pallas_call x23, Pallas kernels, run(): pl.pallas_call(body, out_shape=tuple((jax.ShapeDtypeStruct(shape, dtype)...  46.5 us
    ppermute x12, starting transfers between devices, sent_to(): lax.ppermute(value, 'mesh', [(at, partner(at, step, size)) for at in rang...  19.5 us
    ppermute x14, starting transfers between devices, sent_back(): lax.ppermute(value, 'mesh', [(partner(at, step, size), at) for at in rang...  18.5 us
    ppermute x14, waiting for transfers between devices, sent_back(): lax.ppermute(value, 'mesh', [(partner(at, step, size), at) for at in rang...  13.8 us
    ppermute x5, waiting for transfers between devices, shifted(): lax.ppermute(value, axis, [(at, (at + by) % size) for at in range(size)])  12.4 us
    ppermute x12, waiting for transfers between devices, sent_to(): lax.ppermute(value, 'mesh', [(at, partner(at, step, size)) for at in rang...  6.28 us
    ppermute x5, starting transfers between devices, shifted(): lax.ppermute(value, axis, [(at, (at + by) % size) for at in range(size)])  3.26 us
  transfers between devices with their start and end apart: 31, of which 12 were waited for; matrix products, arithmetic and copies ran while one was open for 2% of the time, Pallas kernels for 19%

profile of v8, /device:TPU:0, one launch (start us, length us, event | category | flops | bytes accessed | tf_op | source)
XLA Modules:
  0.0 124.1 jit_solution(1444540358149248026)
XLA Ops:
  0.6 1.0 shard_map.167.refs_5_
  1.7 3.1 %collective-permute-start.3 = (bf16[272,512]{1,0:T(8,128)(2,1)S(1)}, bf16[272,512]{1,0:T(8,128)(2,1)S(1)}, u32[]{:S(2)}, u32[]{:S(2)}) collective-permute-start(bf16[272,512]{1,0:T(8,128)(2,1)S(1)} %shard_map.167.refs_5_), channel_id=1, source_target_pairs={{0,4},{4,0},{8,12},{12,8},{1,5},{5,1},{9,13},{13,9},{2,6},{6,2},{1... | collective-permute-start | bytes 835592 | tf_op jit(solution)/shard_map/ppermute | solution.py:390
  4.8 2.6 %collective-permute-start = (bf16[272,512]{1,0:T(8,128)(2,1)S(1)}, bf16[272,512]{1,0:T(8,128)(2,1)S(1)}, u32[]{:S(2)}, u32[]{:S(2)}) collective-permute-start(bf16[272,512]{1,0:T(8,128)(2,1)S(1)} %shard_map.167.refs_5_), channel_id=1, source_target_pairs={{0,8},{4,12},{8,0},{12,4},{1,9},{5,13},{9,1},{13,5},{2,10},{6,14},... | collective-permute-start | bytes 835592 | tf_op jit(solution)/shard_map/ppermute | solution.py:390
  7.3 0.7 compare_select_fusion
  8.0 0.7 fusion.10
  8.8 0.6 gather_fusion
  9.4 0.1 select_n.77.order
  9.5 0.4 collective-permute-done.1
  9.9 0.1 rev.6
  10.1 1.6 %collective-permute-start.2 = (s32[2,2,512]{2,0,1:T(2,128)S(1)}, s32[2,2,512]{2,0,1:T(2,128)S(1)}, u32[]{:S(2)}, u32[]{:S(2)}) collective-permute-start(s32[2,2,512]{2,0,1:T(2,128)S(1)} %fusion.1), channel_id=1, source_target_pairs={{0,2},{2,0},{1,3},{3,1},{4,6},{6,4},{5,7},{7,5},{8,10},{10,8},{9,1... | collective-permute-start | bytes 24584 | tf_op jit(solution)/shard_map/ppermute | solution.py:381
  11.7 2.1 %collective-permute-done.2 = s32[2,2,512]{2,0,1:T(2,128)S(1)} collective-permute-done((s32[2,2,512]{2,0,1:T(2,128)S(1)}, s32[2,2,512]{2,0,1:T(2,128)S(1)}, u32[]{:S(2)}, u32[]{:S(2)}) %collective-permute-start.2) | collective-permute-done | bytes 8224 | tf_op jit(solution)/shard_map/ppermute | solution.py:381
  14.0 3.5 %shard_map.168 = (bf16[2048,1024]{1,0:T(8,128)(2,1)S(1)}, bf16[1024,2048]{1,0:T(8,128)(2,1)S(1)}, bf16[2048,128]{1,0:T(8,128)(2,1)S(1)}, bf16[128,2048]{1,0:T(8,...) custom-call(s32[1,2048]{1,0:T(1,128)S(1)} %bitcast.27, s32[1,2048]{1,0:T(1,128)S(1)} %bitcast.26, ...), custom_call_target="tpu_custom_call" | custom-call | flops 3221225472 | bytes 9650560 | tf_op jit(solution)/shard_map/pallas_call | solution.py:82
  17.5 2.3 %collective-permute-done.refs_4_ = bf16[272,512]{1,0:T(8,128)(2,1)S(1)} collective-permute-done((bf16[272,512]{1,0:T(8,128)(2,1)S(1)}, bf16[272,512]{1,0:T(8,128)(2,1)S(1)}, u32[]{:S(2)}, u32[]{:S(2)}) %collective-permute-start) | collective-permute-done | bytes 278560 | tf_op jit(solution)/shard_map/ppermute | solution.py:390
  19.8 0.4 collective-permute-start.4
  20.4 1.7 %shard_map.169 = (bf16[256,512]{1,0:T(8,128)(2,1)S(1)}, bf16[256,512]{1,0:T(8,128)(2,1)S(1)}, bf16[256,512]{1,0:T(8,128)(2,1)S(1)}, bf16[256,512]{1,0:T(8,128)(2...) custom-call(s32[2,512]{1,0:T(2,128)S(1)} %broadcast_in_dim.19.refs_0_, bf16[512,512]{1,0:T(8,128)(2,1)S(1)} %copy-done.7, ...), custom_call_target="tpu_custom_call" | custom-call | flops 1073741824 | bytes 4853760 | tf_op jit(solution)/shard_map/pallas_call | solution.py:82
  22.1 0.9 shard_map.170
  23.0 3.3 %collective-permute-done.4.refs_4_ = bf16[272,512]{1,0:T(8,128)(2,1)S(1)} collective-permute-done((bf16[272,512]{1,0:T(8,128)(2,1)S(1)}, bf16[272,512]{1,0:T(8,128)(2,1)S(1)}, u32[]{:S(2)}, u32[]{:S(2)}) %collective-permute-start.4) | collective-permute-done | bytes 278560 | tf_op jit(solution)/shard_map/ppermute | solution.py:390
  26.3 0.9 shard_map.171
  27.4 1.5 %collective-permute-done.5 = bf16[256,512]{1,0:T(8,128)(2,1)S(1)} collective-permute-done((bf16[256,512]{1,0:T(8,128)(2,1)S(1)}, bf16[256,512]{1,0:T(8,128)(2,1)S(1)}, u32[]{:S(2)}, u32[]{:S(2)}) %collective-permute-start.5) | collective-permute-done | bytes 262176 | tf_op jit(solution)/shard_map/ppermute | solution.py:381
  29.0 1.6 %collective-permute-start.6 = (bf16[256,512]{1,0:T(8,128)(2,1)S(1)}, bf16[256,512]{1,0:T(8,128)(2,1)S(1)}, u32[]{:S(2)}, u32[]{:S(2)}) collective-permute-start(bf16[256,512]{1,0:T(8,128)(2,1)S(1)} %add_convert_fusion.1), channel_id=1, source_target_pairs={{0,2},{2,0},{1,3},{3,1},{4,6},{6,4},{5,7},{7,5},{8,10},{10,8},{9,1... | collective-permute-start | bytes 786440 | tf_op jit(solution)/shard_map/ppermute | solution.py:381
  30.5 6.9 %collective-permute-done.6 = bf16[256,512]{1,0:T(8,128)(2,1)S(1)} collective-permute-done((bf16[256,512]{1,0:T(8,128)(2,1)S(1)}, bf16[256,512]{1,0:T(8,128)(2,1)S(1)}, u32[]{:S(2)}, u32[]{:S(2)}) %collective-permute-start.6) | collective-permute-done | bytes 262176 | tf_op jit(solution)/shard_map/ppermute | solution.py:381
  37.5 1.5 %collective-permute-done.7.refs_2_ = bf16[256,512]{1,0:T(8,128)(2,1)S(1)} collective-permute-done((bf16[256,512]{1,0:T(8,128)(2,1)S(1)}, bf16[256,512]{1,0:T(8,128)(2,1)S(1)}, u32[]{:S(2)}, u32[]{:S(2)}) %collective-permute-start.7) | collective-permute-done | bytes 262176 | tf_op jit(solution)/shard_map/ppermute | solution.py:381
  39.1 1.0 shard_map.172
  40.1 2.6 %collective-permute-start.8 = (bf16[32,512]{1,0:T(8,128)(2,1)S(1)}, bf16[32,512]{1,0:T(8,128)(2,1)S(1)}, u32[]{:S(2)}, u32[]{:S(2)}) collective-permute-start(bf16[32,512]{1,0:T(8,128)(2,1)S(1)} %get-tuple-element.77), channel_id=1, source_target_pairs={{0,12},{4,8},{8,4},{12,0},{1,13},{5,9},{9,5},{13,1},{2,14},{6,10},... | collective-permute-start | bytes 98312 | tf_op jit(solution)/shard_map/ppermute | solution.py:390
  42.7 0.3 collective-permute-start.9
  43.0 1.6 %collective-permute-start.10 = (bf16[32,512]{1,0:T(8,128)(2,1)S(1)}, bf16[32,512]{1,0:T(8,128)(2,1)S(1)}, u32[]{:S(2)}, u32[]{:S(2)}) collective-permute-start(bf16[32,512]{1,0:T(8,128)(2,1)S(1)} %get-tuple-element.79), channel_id=1, source_target_pairs={{0,4},{4,0},{8,12},{12,8},{1,5},{5,1},{9,13},{13,9},{2,6},{6,2},{1... | collective-permute-start | bytes 98312 | tf_op jit(solution)/shard_map/ppermute | solution.py:390
  44.5 2.6 %shard_map.173.refs_1_ = f32[2048,512]{1,0:T(8,128)S(1)} custom-call(bf16[512,512]{1,0:T(8,128)(2,1)S(1)} %get-tuple-element.74.hidden.refs_0_, bf16[512,512]{1,0:T(8,128)(2,1)S(1)} %get-tuple-element.75.sent, bf16[2048,1024]{1,0:T(8,128)(2,1)S(1)} %get-tuple-element.76.here.refs_9_.refs_10_, bf16[3,512,512]{2,1,0:T(8,128)(2,1)S(1)} %copy-done.2), custom_call_target="tpu_custom_call" | custom-call | flops 2415919104 | bytes 11010048 | tf_op jit(solution)/shard_map/pallas_call | solution.py:82
  47.2 0.4 collective-permute-done.9.refs_3_
  47.5 3.2 %shard_map.174 = (bf16[512,512]{1,0:T(8,128)(2,1)S(1)}, f32[512,512]{1,0:T(8,128)S(1)}, bf16[2048,512]{1,0:T(8,128)(2,1)S(1)}, bf16[512,512]{1,0:T(8,128)(2,1)S(...) custom-call(bf16[512,512]{1,0:T(8,128)(2,1)S(1)} %get-tuple-element.74.hidden.refs_0_, ...), custom_call_target="tpu_custom_call" | custom-call | flops 1929379840 | bytes 17078272 | tf_op jit(solution)/shard_map/pallas_call | solution.py:82
  50.8 2.3 %collective-permute-start.11 = (bf16[32,512]{1,0:T(8,128)(2,1)S(1)}, bf16[32,512]{1,0:T(8,128)(2,1)S(1)}, u32[]{:S(2)}, u32[]{:S(2)}) collective-permute-start(bf16[32,512]{1,0:T(8,128)(2,1)S(1)} %get-tuple-element.84), channel_id=1, source_target_pairs={{0,12},{4,8},{8,4},{12,0},{1,13},{5,9},{9,5},{13,1},{2,14},{6,10},... | collective-permute-start | bytes 98312 | tf_op jit(solution)/shard_map/ppermute | solution.py:390
  53.1 0.1 collective-permute-start.12
  53.2 2.0 %collective-permute-start.13 = (bf16[32,512]{1,0:T(8,128)(2,1)S(1)}, bf16[32,512]{1,0:T(8,128)(2,1)S(1)}, u32[]{:S(2)}, u32[]{:S(2)}) collective-permute-start(bf16[32,512]{1,0:T(8,128)(2,1)S(1)} %get-tuple-element.86), channel_id=1, source_target_pairs={{0,4},{4,0},{8,12},{12,8},{1,5},{5,1},{9,13},{13,9},{2,6},{6,2},{1... | collective-permute-start | bytes 98312 | tf_op jit(solution)/shard_map/ppermute | solution.py:390
  55.2 2.6 %shard_map.175.refs_1_ = f32[2048,512]{1,0:T(8,128)S(1)} custom-call(bf16[512,512]{1,0:T(8,128)(2,1)S(1)} %get-tuple-element.82.hidden.refs_0_, bf16[512,512]{1,0:T(8,128)(2,1)S(1)} %get-tuple-element.83.sent, bf16[2048,1024]{1,0:T(8,128)(2,1)S(1)} %get-tuple-element.76.here.refs_9_.refs_10_, bf16[3,512,512]{2,1,0:T(8,128)(2,1)S(1)} %copy-done.2), custom_call_target="tpu_custom_call" | custom-call | flops 2415919104 | bytes 11010048 | tf_op jit(solution)/shard_map/pallas_call | solution.py:82
  57.8 0.2 collective-permute-done.12.refs_3_
  58.1 3.4 %shard_map.176 = (bf16[512,512]{1,0:T(8,128)(2,1)S(1)}, f32[512,512]{1,0:T(8,128)S(1)}, bf16[2048,512]{1,0:T(8,128)(2,1)S(1)}, bf16[512,512]{1,0:T(8,128)(2,1)S(...) custom-call(bf16[512,512]{1,0:T(8,128)(2,1)S(1)} %get-tuple-element.82.hidden.refs_0_, ...), custom_call_target="tpu_custom_call" | custom-call | flops 1929379840 | bytes 17078272 | tf_op jit(solution)/shard_map/pallas_call | solution.py:82
  61.5 2.1 %collective-permute-start.14 = (bf16[32,512]{1,0:T(8,128)(2,1)S(1)}, bf16[32,512]{1,0:T(8,128)(2,1)S(1)}, u32[]{:S(2)}, u32[]{:S(2)}) collective-permute-start(bf16[32,512]{1,0:T(8,128)(2,1)S(1)} %get-tuple-element.89), channel_id=1, source_target_pairs={{0,12},{4,8},{8,4},{12,0},{1,13},{5,9},{9,5},{13,1},{2,14},{6,10},... | collective-permute-start | bytes 98312 | tf_op jit(solution)/shard_map/ppermute | solution.py:390
  63.6 0.5 collective-permute-start.15
  64.1 1.9 %collective-permute-start.16 = (bf16[32,512]{1,0:T(8,128)(2,1)S(1)}, bf16[32,512]{1,0:T(8,128)(2,1)S(1)}, u32[]{:S(2)}, u32[]{:S(2)}) collective-permute-start(bf16[32,512]{1,0:T(8,128)(2,1)S(1)} %get-tuple-element.91), channel_id=1, source_target_pairs={{0,4},{4,0},{8,12},{12,8},{1,5},{5,1},{9,13},{13,9},{2,6},{6,2},{1... | collective-permute-start | bytes 98312 | tf_op jit(solution)/shard_map/ppermute | solution.py:390
  66.0 2.6 %shard_map.177.refs_1_ = f32[2048,512]{1,0:T(8,128)S(1)} custom-call(bf16[512,512]{1,0:T(8,128)(2,1)S(1)} %get-tuple-element.87.hidden.refs_0_, bf16[512,512]{1,0:T(8,128)(2,1)S(1)} %get-tuple-element.88.sent, bf16[2048,1024]{1,0:T(8,128)(2,1)S(1)} %get-tuple-element.76.here.refs_9_.refs_10_, bf16[3,512,512]{2,1,0:T(8,128)(2,1)S(1)} %copy-done.2), custom_call_target="tpu_custom_call" | custom-call | flops 2415919104 | bytes 11010048 | tf_op jit(solution)/shard_map/pallas_call | solution.py:82
  68.6 5.7 %shard_map.178 = (bf16[512,512]{1,0:T(8,128)(2,1)}, bf16[2048,512]{1,0:T(8,128)(2,1)S(1)}, bf16[32,512]{1,0:T(8,128)(2,1)S(1)}, bf16[32,512]{1,0:T(8,128)(2,1)S(1)}, bf16[32,512]{1,0:T(8,128)(2,1)S(1)}) custom-call(bf16[512,512]{1,0:T(8,128)(2,1)S(1)} %get-tuple-element.87.hidden.refs_0_, f32[2048,512]{1,0:T(8,128)S(1)} %shard_map.177.refs_1_, ...), custom_call_target="tpu_custom_call" | custom-call | flops 3221225472 | bytes 19077120 | tf_op jit(solution)/shard_map/pallas_call | solution.py:82
  74.4 2.0 %collective-permute-start.17 = (bf16[32,512]{1,0:T(8,128)(2,1)S(1)}, bf16[32,512]{1,0:T(8,128)(2,1)S(1)}, u32[]{:S(2)}, u32[]{:S(2)}) collective-permute-start(bf16[32,512]{1,0:T(8,128)(2,1)S(1)} %get-tuple-element.95), channel_id=1, source_target_pairs={{12,0},{8,4},{4,8},{0,12},{13,1},{9,5},{5,9},{1,13},{14,2},{10,6},... | collective-permute-start | bytes 98312 | tf_op jit(solution)/shard_map/ppermute | solution.py:395
  76.4 0.7 collective-permute-start.18
  77.1 1.7 %collective-permute-start.19 = (bf16[32,512]{1,0:T(8,128)(2,1)S(1)}, bf16[32,512]{1,0:T(8,128)(2,1)S(1)}, u32[]{:S(2)}, u32[]{:S(2)}) collective-permute-start(bf16[32,512]{1,0:T(8,128)(2,1)S(1)} %get-tuple-element.97), channel_id=1, source_target_pairs={{4,0},{0,4},{12,8},{8,12},{5,1},{1,5},{13,9},{9,13},{6,2},{2,6},{1... | collective-permute-start | bytes 98312 | tf_op jit(solution)/shard_map/ppermute | solution.py:395
  78.8 2.9 %shard_map.179.refs_0_ = f32[512,512]{1,0:T(8,128)S(1)} custom-call(bf16[512,512]{1,0:T(8,128)(2,1)S(1)} %copy-done.6, bf16[2048,512]{1,0:T(8,128)(2,1)S(1)} %get-tuple-element.94.grad_pre, bf16[1024,2048]{1,0:T(8,128)(2,1)S(1)} %get-tuple-element.81.refs_6_.there, bf16[3,512,512]{2,1,0:T(8,128)(2,1)S(1)} %copy-done.1, bf16[3,512,512]{2,1,0:T(8,128)(2,1)S(1)} %copy-done.2), custom_call_target="tpu_custom_call" | custom-call | flops 2684354560 | bytes 11010048 | tf_op jit(solution)/shard_map/pallas_call | solution.py:82
  81.7 2.6 %shard_map.180 = (f32[512,512]{1,0:T(8,128)S(1)}, bf16[2048,512]{1,0:T(8,128)(2,1)S(1)}, bf16[32,512]{1,0:T(8,128)(2,1)S(1)}, bf16[32,512]{1,0:T(8,128)(2,1)S(1)}, bf16[32,512]{1,0:T(8,128)(2,1)S(1)}) custom-call(f32[512,512]{1,0:T(8,128)S(1)} %shard_map.179.refs_0_, bf16[32,512]{1,0:T(8,128)(2,1)S(1)} %collective-permute-done.17.refs_1_, ...), custom_call_target="tpu_custom_call" | custom-call | flops 1711276032 | bytes 15505408 | tf_op jit(solution)/shard_map/pallas_call | solution.py:82
  84.2 2.1 %collective-permute-start.20 = (bf16[32,512]{1,0:T(8,128)(2,1)S(1)}, bf16[32,512]{1,0:T(8,128)(2,1)S(1)}, u32[]{:S(2)}, u32[]{:S(2)}) collective-permute-start(bf16[32,512]{1,0:T(8,128)(2,1)S(1)} %get-tuple-element.103), channel_id=1, source_target_pairs={{12,0},{8,4},{4,8},{0,12},{13,1},{9,5},{5,9},{1,13},{14,2},{10,6},... | collective-permute-start | bytes 98312 | tf_op jit(solution)/shard_map/ppermute | solution.py:395
  86.3 0.4 collective-permute-start.21
  86.8 1.9 %collective-permute-start.22 = (bf16[32,512]{1,0:T(8,128)(2,1)S(1)}, bf16[32,512]{1,0:T(8,128)(2,1)S(1)}, u32[]{:S(2)}, u32[]{:S(2)}) collective-permute-start(bf16[32,512]{1,0:T(8,128)(2,1)S(1)} %get-tuple-element.105), channel_id=1, source_target_pairs={{4,0},{0,4},{12,8},{8,12},{5,1},{1,5},{13,9},{9,13},{6,2},{2,6},{1... | collective-permute-start | bytes 98312 | tf_op jit(solution)/shard_map/ppermute | solution.py:395
  88.7 2.9 %shard_map.181.refs_0_ = f32[512,512]{1,0:T(8,128)S(1)} custom-call(f32[512,512]{1,0:T(8,128)S(1)} %get-tuple-element.101.upstream, bf16[2048,512]{1,0:T(8,128)(2,1)S(1)} %get-tuple-element.102.grad_pre, bf16[1024,2048]{1,0:T(8,128)(2,1)S(1)} %get-tuple-element.81.refs_6_.there, bf16[3,512,512]{2,1,0:T(8,128)(2,1)S(1)} %copy-done.1, ...), custom_call_target="tpu_custom_call" | custom-call | flops 2684354560 | bytes 11534336 | tf_op jit(solution)/shard_map/pallas_call | solution.py:82
  91.6 2.8 %shard_map.182 = (f32[512,512]{1,0:T(8,128)S(1)}, bf16[2048,512]{1,0:T(8,128)(2,1)S(1)}, bf16[32,512]{1,0:T(8,128)(2,1)S(1)}, bf16[32,512]{1,0:T(8,128)(2,1)S(1)}, bf16[32,512]{1,0:T(8,128)(2,1)S(1)}) custom-call(f32[512,512]{1,0:T(8,128)S(1)} %shard_map.181.refs_0_, bf16[32,512]{1,0:T(8,128)(2,1)S(1)} %collective-permute-done.20.refs_1_, ...), custom_call_target="tpu_custom_call" | custom-call | flops 1711276032 | bytes 15505408 | tf_op jit(solution)/shard_map/pallas_call | solution.py:82
  94.4 2.1 %collective-permute-start.23 = (bf16[32,512]{1,0:T(8,128)(2,1)S(1)}, bf16[32,512]{1,0:T(8,128)(2,1)S(1)}, u32[]{:S(2)}, u32[]{:S(2)}) collective-permute-start(bf16[32,512]{1,0:T(8,128)(2,1)S(1)} %get-tuple-element.110), channel_id=1, source_target_pairs={{12,0},{8,4},{4,8},{0,12},{13,1},{9,5},{5,9},{1,13},{14,2},{10,6},... | collective-permute-start | bytes 98312 | tf_op jit(solution)/shard_map/ppermute | solution.py:395
  96.5 0.4 collective-permute-start.24
  96.9 1.9 %collective-permute-start.25 = (bf16[32,512]{1,0:T(8,128)(2,1)S(1)}, bf16[32,512]{1,0:T(8,128)(2,1)S(1)}, u32[]{:S(2)}, u32[]{:S(2)}) collective-permute-start(bf16[32,512]{1,0:T(8,128)(2,1)S(1)} %get-tuple-element.112), channel_id=1, source_target_pairs={{4,0},{0,4},{12,8},{8,12},{5,1},{1,5},{13,9},{9,13},{6,2},{2,6},{1... | collective-permute-start | bytes 98312 | tf_op jit(solution)/shard_map/ppermute | solution.py:395
  98.8 2.9 %shard_map.183.refs_0_ = f32[512,512]{1,0:T(8,128)S(1)} custom-call(f32[512,512]{1,0:T(8,128)S(1)} %get-tuple-element.108.upstream, bf16[2048,512]{1,0:T(8,128)(2,1)S(1)} %get-tuple-element.109.grad_pre, bf16[1024,2048]{1,0:T(8,128)(2,1)S(1)} %get-tuple-element.81.refs_6_.there, bf16[3,512,512]{2,1,0:T(8,128)(2,1)S(1)} %copy-done.1, ...), custom_call_target="tpu_custom_call" | custom-call | flops 2684354560 | bytes 11534336 | tf_op jit(solution)/shard_map/pallas_call | solution.py:82
  101.7 1.4 %shard_map.184 = (bf16[512,512]{1,0:T(8,128)(2,1)S(1)}, bf16[128,512]{1,0:T(8,128)(2,1)S(1)}, bf16[128,512]{1,0:T(8,128)(2,1)S(1)}) custom-call(f32[512,512]{1,0:T(8,128)S(1)} %shard_map.183.refs_0_, bf16[32,512]{1,0:T(8,128)(2,1)S(1)} %collective-permute-done.23.refs_1_, bf16[32,512]{1,0:T(8,128)(2,1)S(1)} %collective-permute-done.24.refs_2_, ...), custom_call_target="tpu_custom_call" | custom-call | flops 503316480 | bytes 5703680 | tf_op jit(solution)/shard_map/pallas_call | solution.py:82
  103.1 1.5 %collective-permute-start.26 = (bf16[128,512]{1,0:T(8,128)(2,1)S(1)}, bf16[128,512]{1,0:T(8,128)(2,1)S(1)}, u32[]{:S(2)}, u32[]{:S(2)}) collective-permute-start(bf16[128,512]{1,0:T(8,128)(2,1)S(1)} %get-tuple-element.125), channel_id=1, source_target_pairs={{4,0},{0,4},{12,8},{8,12},{5,1},{1,5},{13,9},{9,13},{6,2},{2,6},{1... | collective-permute-start | bytes 393224 | tf_op jit(solution)/shard_map/ppermute | solution.py:395
  104.6 0.6 collective-permute-start.29
  105.2 0.6 shard_map.185
  105.8 6.1 %collective-permute-done.26.passed = bf16[128,512]{1,0:T(8,128)(2,1)S(1)} collective-permute-done((bf16[128,512]{1,0:T(8,128)(2,1)S(1)}, bf16[128,512]{1,0:T(8,128)(2,1)S(1)}, u32[]{:S(2)}, u32[]{:S(2)}) %collective-permute-start.26) | collective-permute-done | bytes 131104 | tf_op jit(solution)/shard_map/ppermute | solution.py:395
  112.0 2.8 %collective-permute-start.28 = (bf16[128,512]{1,0:T(8,128)(2,1)S(1)}, bf16[128,512]{1,0:T(8,128)(2,1)S(1)}, u32[]{:S(2)}, u32[]{:S(2)}) collective-permute-start(bf16[128,512]{1,0:T(8,128)(2,1)S(1)} %get-tuple-element.128), channel_id=1, source_target_pairs={{8,0},{12,4},{0,8},{4,12},{9,1},{13,5},{1,9},{5,13},{10,2},{14,6},... | collective-permute-start | bytes 393224 | tf_op jit(solution)/shard_map/ppermute | solution.py:395
  114.9 0.2 collective-permute-start.30
  115.1 2.9 %collective-permute-done.28.piece = bf16[128,512]{1,0:T(8,128)(2,1)S(1)} collective-permute-done((bf16[128,512]{1,0:T(8,128)(2,1)S(1)}, bf16[128,512]{1,0:T(8,128)(2,1)S(1)}, u32[]{:S(2)}, u32[]{:S(2)}) %collective-permute-start.28) | collective-permute-done | bytes 131104 | tf_op jit(solution)/shard_map/ppermute | solution.py:395
  118.1 4.8 %collective-permute-done.30.refs_3_ = bf16[128,512]{1,0:T(8,128)(2,1)S(1)} collective-permute-done((bf16[128,512]{1,0:T(8,128)(2,1)S(1)}, bf16[128,512]{1,0:T(8,128)(2,1)S(1)}, u32[]{:S(2)}, u32[]{:S(2)}) %collective-permute-start.30) | collective-permute-done | bytes 131104 | tf_op jit(solution)/shard_map/ppermute | solution.py:395
  122.8 1.3 %shard_map.189 = f32[256,512]{1,0:T(8,128)} custom-call(bf16[256,512]{1,0:T(8,128)(2,1)S(1)} %get-tuple-element.123.own.refs_0_, bf16[256,512]{1,0:T(8,128)(2,1)S(1)} %collective-permute-done.27.refs_1_, f32[128,512]{1,0:T(8,128)S(1)} %shard_map.187.refs_2_, bf16[128,512]{1,0:T(8,128)(2,1)S(1)} %collective-permute-done.30.refs_3_, bf16[512,512]{1,0:T(8,128)(2,1)S(1)} %copy-done.4), custom_call_target="tpu_custom_call" | custom-call | flops 134217728 | bytes 1966080 | tf_op jit(solution)/shard_map/pallas_call | solution.py:82
  (68 shorter events, 1.0 us)
Async XLA Ops:
  0.6 8.2 %copy-start = (s32[1,4,32]{2,1,0:T(4,128)S(1)}, s32[1,4,32]{2,1,0:T(4,128)}, u32[]{:S(2)}) copy-start(s32[1,4,32]{2,1,0:T(4,128)} %param.22) | copy-start | bytes 1540
  1.7 18.6 %collective-permute-start.3 = (bf16[272,512]{1,0:T(8,128)(2,1)S(1)}, bf16[272,512]{1,0:T(8,128)(2,1)S(1)}, u32[]{:S(2)}, u32[]{:S(2)}) collective-permute-start(bf16[272,512]{1,0:T(8,128)(2,1)S(1)} %shard_map.167.refs_5_), channel_id=1, source_target_pairs={{0,4},{4,0},{8,12},{12,8},{1,5},{5,1},{9,13},{13,9},{2,6},{6,2},{1... | collective-permute-start | bytes 835592 | tf_op jit(solution)/shard_map/ppermute | solution.py:390
  4.8 15.0 %collective-permute-start = (bf16[272,512]{1,0:T(8,128)(2,1)S(1)}, bf16[272,512]{1,0:T(8,128)(2,1)S(1)}, u32[]{:S(2)}, u32[]{:S(2)}) collective-permute-start(bf16[272,512]{1,0:T(8,128)(2,1)S(1)} %shard_map.167.refs_5_), channel_id=1, source_target_pairs={{0,8},{4,12},{8,0},{12,4},{1,9},{5,13},{9,1},{13,5},{2,10},{6,14},... | collective-permute-start | bytes 835592 | tf_op jit(solution)/shard_map/ppermute | solution.py:390
  8.7 1.2 collective-permute-start.1
  10.1 3.7 %collective-permute-start.2 = (s32[2,2,512]{2,0,1:T(2,128)S(1)}, s32[2,2,512]{2,0,1:T(2,128)S(1)}, u32[]{:S(2)}, u32[]{:S(2)}) collective-permute-start(s32[2,2,512]{2,0,1:T(2,128)S(1)} %fusion.1), channel_id=1, source_target_pairs={{0,2},{2,0},{1,3},{3,1},{4,6},{6,4},{5,7},{7,5},{8,10},{10,8},{9,1... | collective-permute-start | bytes 24584 | tf_op jit(solution)/shard_map/ppermute | solution.py:381
  13.9 6.5 %copy-start.4 = (bf16[512,512]{1,0:T(8,128)(2,1)S(1)}, bf16[512,512]{1,0:T(8,128)(2,1)}, u32[]{:S(2)}) copy-start(bf16[512,512]{1,0:T(8,128)(2,1)} %refs_4_.3) | copy-start | bytes 1572868
  13.9 6.5 %copy-start.7 = (bf16[512,512]{1,0:T(8,128)(2,1)S(1)}, bf16[512,512]{1,0:T(8,128)(2,1)}, u32[]{:S(2)}) copy-start(bf16[512,512]{1,0:T(8,128)(2,1)} %refs_3_.3) | copy-start | bytes 1572868
  14.0 6.4 %copy-start.10 = (bf16[512,512]{1,0:T(8,128)(2,1)S(1)}, bf16[512,512]{1,0:T(8,128)(2,1)}, u32[]{:S(2)}) copy-start(bf16[512,512]{1,0:T(8,128)(2,1)} %refs_3_.2) | copy-start | bytes 1572868
  19.8 6.5 %collective-permute-start.4 = (bf16[272,512]{1,0:T(8,128)(2,1)S(1)}, bf16[272,512]{1,0:T(8,128)(2,1)S(1)}, u32[]{:S(2)}, u32[]{:S(2)}) collective-permute-start(bf16[272,512]{1,0:T(8,128)(2,1)S(1)} %collective-permute-done.refs_4_), channel_id=1, source_target_pairs={{0,4},{4,0},{8,12},{12,8},{1,5},{5,1},{9,13},{13,9},{2,6},{6,2},{1... | collective-permute-start | bytes 835592 | tf_op jit(solution)/shard_map/ppermute | solution.py:390
  26.3 12.7 %copy-start.1 = (bf16[3,512,512]{2,1,0:T(8,128)(2,1)S(1)}, bf16[3,512,512]{2,1,0:T(8,128)(2,1)}, u32[]{:S(2)}) copy-start(bf16[3,512,512]{2,1,0:T(8,128)(2,1)} %refs_5_.5) | copy-start | bytes 4718596
  26.3 12.7 %copy-start.5 = (bf16[512,512]{1,0:T(8,128)(2,1)S(1)}, bf16[512,512]{1,0:T(8,128)(2,1)}, u32[]{:S(2)}) copy-start(bf16[512,512]{1,0:T(8,128)(2,1)} %refs_8_.11) | copy-start | bytes 1572868
  26.3 12.7 %copy-start.9 = (f32[512]{0:T(512)S(1)}, f32[512]{0:T(512)}, u32[]{:S(2)}) copy-start(f32[512]{0:T(512)} %param.26) | copy-start | bytes 6148
  27.3 1.6 %collective-permute-start.5 = (bf16[256,512]{1,0:T(8,128)(2,1)S(1)}, bf16[256,512]{1,0:T(8,128)(2,1)S(1)}, u32[]{:S(2)}, u32[]{:S(2)}) collective-permute-start(bf16[256,512]{1,0:T(8,128)(2,1)S(1)} %get-tuple-element.73), channel_id=1, source_target_pairs={{0,1},{1,0},{2,3},{3,2},{4,5},{5,4},{6,7},{7,6},{8,9},{9,8},{10,11... | collective-permute-start | bytes 786440 | tf_op jit(solution)/shard_map/ppermute | solution.py:381
  29.0 15.6 %copy-start.2 = (bf16[3,512,512]{2,1,0:T(8,128)(2,1)S(1)}, bf16[3,512,512]{2,1,0:T(8,128)(2,1)}, u32[]{:S(2)}) copy-start(bf16[3,512,512]{2,1,0:T(8,128)(2,1)} %w_recv.11) | copy-start | bytes 4718596
  29.0 8.4 %collective-permute-start.6 = (bf16[256,512]{1,0:T(8,128)(2,1)S(1)}, bf16[256,512]{1,0:T(8,128)(2,1)S(1)}, u32[]{:S(2)}, u32[]{:S(2)}) collective-permute-start(bf16[256,512]{1,0:T(8,128)(2,1)S(1)} %add_convert_fusion.1), channel_id=1, source_target_pairs={{0,2},{2,0},{1,3},{3,1},{4,6},{6,4},{5,7},{7,5},{8,10},{10,8},{9,1... | collective-permute-start | bytes 786440 | tf_op jit(solution)/shard_map/ppermute | solution.py:381
  37.5 1.6 %collective-permute-start.7 = (bf16[256,512]{1,0:T(8,128)(2,1)S(1)}, bf16[256,512]{1,0:T(8,128)(2,1)S(1)}, u32[]{:S(2)}, u32[]{:S(2)}) collective-permute-start(bf16[256,512]{1,0:T(8,128)(2,1)S(1)} %add_convert_fusion.refs_1_), channel_id=1, source_target_pairs={{0,1},{1,0},{2,3},{3,2},{4,5},{5,4},{6,7},{7,6},{8,9},{9,8},{10,11... | collective-permute-start | bytes 786440 | tf_op jit(solution)/shard_map/ppermute | solution.py:381
  40.1 7.1 %collective-permute-start.8 = (bf16[32,512]{1,0:T(8,128)(2,1)S(1)}, bf16[32,512]{1,0:T(8,128)(2,1)S(1)}, u32[]{:S(2)}, u32[]{:S(2)}) collective-permute-start(bf16[32,512]{1,0:T(8,128)(2,1)S(1)} %get-tuple-element.77), channel_id=1, source_target_pairs={{0,12},{4,8},{8,4},{12,0},{1,13},{5,9},{9,5},{13,1},{2,14},{6,10},... | collective-permute-start | bytes 98312 | tf_op jit(solution)/shard_map/ppermute | solution.py:390
  42.7 4.8 %collective-permute-start.9 = (bf16[32,512]{1,0:T(8,128)(2,1)S(1)}, bf16[32,512]{1,0:T(8,128)(2,1)S(1)}, u32[]{:S(2)}, u32[]{:S(2)}) collective-permute-start(bf16[32,512]{1,0:T(8,128)(2,1)S(1)} %get-tuple-element.78), channel_id=1, source_target_pairs={{0,8},{4,12},{8,0},{12,4},{1,9},{5,13},{9,1},{13,5},{2,10},{6,14},... | collective-permute-start | bytes 98312 | tf_op jit(solution)/shard_map/ppermute | solution.py:390
  43.0 4.6 %collective-permute-start.10 = (bf16[32,512]{1,0:T(8,128)(2,1)S(1)}, bf16[32,512]{1,0:T(8,128)(2,1)S(1)}, u32[]{:S(2)}, u32[]{:S(2)}) collective-permute-start(bf16[32,512]{1,0:T(8,128)(2,1)S(1)} %get-tuple-element.79), channel_id=1, source_target_pairs={{0,4},{4,0},{8,12},{12,8},{1,5},{5,1},{9,13},{13,9},{2,6},{6,2},{1... | collective-permute-start | bytes 98312 | tf_op jit(solution)/shard_map/ppermute | solution.py:390
  44.5 3.0 %copy-start.3 = (bf16[3,512,512]{2,1,0:T(8,128)(2,1)S(1)}, bf16[3,512,512]{2,1,0:T(8,128)(2,1)}, u32[]{:S(2)}) copy-start(bf16[3,512,512]{2,1,0:T(8,128)(2,1)} %refs_9_.7) | copy-start | bytes 4718596
  44.5 3.0 %copy-start.8 = (f32[3,512]{1,0:T(4,128)S(1)}, f32[3,512]{1,0:T(4,128)}, u32[]{:S(2)}) copy-start(f32[3,512]{1,0:T(4,128)} %refs_8_.10) | copy-start | bytes 18436
  50.8 7.1 %collective-permute-start.11 = (bf16[32,512]{1,0:T(8,128)(2,1)S(1)}, bf16[32,512]{1,0:T(8,128)(2,1)S(1)}, u32[]{:S(2)}, u32[]{:S(2)}) collective-permute-start(bf16[32,512]{1,0:T(8,128)(2,1)S(1)} %get-tuple-element.84), channel_id=1, source_target_pairs={{0,12},{4,8},{8,4},{12,0},{1,13},{5,9},{9,5},{13,1},{2,14},{6,10},... | collective-permute-start | bytes 98312 | tf_op jit(solution)/shard_map/ppermute | solution.py:390
  53.1 5.0 %collective-permute-start.12 = (bf16[32,512]{1,0:T(8,128)(2,1)S(1)}, bf16[32,512]{1,0:T(8,128)(2,1)S(1)}, u32[]{:S(2)}, u32[]{:S(2)}) collective-permute-start(bf16[32,512]{1,0:T(8,128)(2,1)S(1)} %get-tuple-element.85), channel_id=1, source_target_pairs={{0,8},{4,12},{8,0},{12,4},{1,9},{5,13},{9,1},{13,5},{2,10},{6,14},... | collective-permute-start | bytes 98312 | tf_op jit(solution)/shard_map/ppermute | solution.py:390
  53.2 4.9 %collective-permute-start.13 = (bf16[32,512]{1,0:T(8,128)(2,1)S(1)}, bf16[32,512]{1,0:T(8,128)(2,1)S(1)}, u32[]{:S(2)}, u32[]{:S(2)}) collective-permute-start(bf16[32,512]{1,0:T(8,128)(2,1)S(1)} %get-tuple-element.86), channel_id=1, source_target_pairs={{0,4},{4,0},{8,12},{12,8},{1,5},{5,1},{9,13},{13,9},{2,6},{6,2},{1... | collective-permute-start | bytes 98312 | tf_op jit(solution)/shard_map/ppermute | solution.py:390
  61.5 7.1 %collective-permute-start.14 = (bf16[32,512]{1,0:T(8,128)(2,1)S(1)}, bf16[32,512]{1,0:T(8,128)(2,1)S(1)}, u32[]{:S(2)}, u32[]{:S(2)}) collective-permute-start(bf16[32,512]{1,0:T(8,128)(2,1)S(1)} %get-tuple-element.89), channel_id=1, source_target_pairs={{0,12},{4,8},{8,4},{12,0},{1,13},{5,9},{9,5},{13,1},{2,14},{6,10},... | collective-permute-start | bytes 98312 | tf_op jit(solution)/shard_map/ppermute | solution.py:390
  63.6 5.0 %collective-permute-start.15 = (bf16[32,512]{1,0:T(8,128)(2,1)S(1)}, bf16[32,512]{1,0:T(8,128)(2,1)S(1)}, u32[]{:S(2)}, u32[]{:S(2)}) collective-permute-start(bf16[32,512]{1,0:T(8,128)(2,1)S(1)} %get-tuple-element.90), channel_id=1, source_target_pairs={{0,8},{4,12},{8,0},{12,4},{1,9},{5,13},{9,1},{13,5},{2,10},{6,14},... | collective-permute-start | bytes 98312 | tf_op jit(solution)/shard_map/ppermute | solution.py:390
  64.1 4.5 %collective-permute-start.16 = (bf16[32,512]{1,0:T(8,128)(2,1)S(1)}, bf16[32,512]{1,0:T(8,128)(2,1)S(1)}, u32[]{:S(2)}, u32[]{:S(2)}) collective-permute-start(bf16[32,512]{1,0:T(8,128)(2,1)S(1)} %get-tuple-element.91), channel_id=1, source_target_pairs={{0,4},{4,0},{8,12},{12,8},{1,5},{5,1},{9,13},{13,9},{2,6},{6,2},{1... | collective-permute-start | bytes 98312 | tf_op jit(solution)/shard_map/ppermute | solution.py:390
  66.0 2.6 %copy-start.6 = (bf16[512,512]{1,0:T(8,128)(2,1)S(1)}, bf16[512,512]{1,0:T(8,128)(2,1)}, u32[]{:S(2)}) copy-start(bf16[512,512]{1,0:T(8,128)(2,1)} %upstream.1) | copy-start | bytes 1572868
  74.4 7.3 %collective-permute-start.17 = (bf16[32,512]{1,0:T(8,128)(2,1)S(1)}, bf16[32,512]{1,0:T(8,128)(2,1)S(1)}, u32[]{:S(2)}, u32[]{:S(2)}) collective-permute-start(bf16[32,512]{1,0:T(8,128)(2,1)S(1)} %get-tuple-element.95), channel_id=1, source_target_pairs={{12,0},{8,4},{4,8},{0,12},{13,1},{9,5},{5,9},{1,13},{14,2},{10,6},... | collective-permute-start | bytes 98312 | tf_op jit(solution)/shard_map/ppermute | solution.py:395
  76.4 5.2 %collective-permute-start.18 = (bf16[32,512]{1,0:T(8,128)(2,1)S(1)}, bf16[32,512]{1,0:T(8,128)(2,1)S(1)}, u32[]{:S(2)}, u32[]{:S(2)}) collective-permute-start(bf16[32,512]{1,0:T(8,128)(2,1)S(1)} %get-tuple-element.96), channel_id=1, source_target_pairs={{8,0},{12,4},{0,8},{4,12},{9,1},{13,5},{1,9},{5,13},{10,2},{14,6},... | collective-permute-start | bytes 98312 | tf_op jit(solution)/shard_map/ppermute | solution.py:395
  77.1 4.5 %collective-permute-start.19 = (bf16[32,512]{1,0:T(8,128)(2,1)S(1)}, bf16[32,512]{1,0:T(8,128)(2,1)S(1)}, u32[]{:S(2)}, u32[]{:S(2)}) collective-permute-start(bf16[32,512]{1,0:T(8,128)(2,1)S(1)} %get-tuple-element.97), channel_id=1, source_target_pairs={{4,0},{0,4},{12,8},{8,12},{5,1},{1,5},{13,9},{9,13},{6,2},{2,6},{1... | collective-permute-start | bytes 98312 | tf_op jit(solution)/shard_map/ppermute | solution.py:395
  84.2 7.3 %collective-permute-start.20 = (bf16[32,512]{1,0:T(8,128)(2,1)S(1)}, bf16[32,512]{1,0:T(8,128)(2,1)S(1)}, u32[]{:S(2)}, u32[]{:S(2)}) collective-permute-start(bf16[32,512]{1,0:T(8,128)(2,1)S(1)} %get-tuple-element.103), channel_id=1, source_target_pairs={{12,0},{8,4},{4,8},{0,12},{13,1},{9,5},{5,9},{1,13},{14,2},{10,6},... | collective-permute-start | bytes 98312 | tf_op jit(solution)/shard_map/ppermute | solution.py:395
  86.3 5.2 %collective-permute-start.21 = (bf16[32,512]{1,0:T(8,128)(2,1)S(1)}, bf16[32,512]{1,0:T(8,128)(2,1)S(1)}, u32[]{:S(2)}, u32[]{:S(2)}) collective-permute-start(bf16[32,512]{1,0:T(8,128)(2,1)S(1)} %get-tuple-element.104), channel_id=1, source_target_pairs={{8,0},{12,4},{0,8},{4,12},{9,1},{13,5},{1,9},{5,13},{10,2},{14,6},... | collective-permute-start | bytes 98312 | tf_op jit(solution)/shard_map/ppermute | solution.py:395
  86.8 4.8 %collective-permute-start.22 = (bf16[32,512]{1,0:T(8,128)(2,1)S(1)}, bf16[32,512]{1,0:T(8,128)(2,1)S(1)}, u32[]{:S(2)}, u32[]{:S(2)}) collective-permute-start(bf16[32,512]{1,0:T(8,128)(2,1)S(1)} %get-tuple-element.105), channel_id=1, source_target_pairs={{4,0},{0,4},{12,8},{8,12},{5,1},{1,5},{13,9},{9,13},{6,2},{2,6},{1... | collective-permute-start | bytes 98312 | tf_op jit(solution)/shard_map/ppermute | solution.py:395
  94.4 7.3 %collective-permute-start.23 = (bf16[32,512]{1,0:T(8,128)(2,1)S(1)}, bf16[32,512]{1,0:T(8,128)(2,1)S(1)}, u32[]{:S(2)}, u32[]{:S(2)}) collective-permute-start(bf16[32,512]{1,0:T(8,128)(2,1)S(1)} %get-tuple-element.110), channel_id=1, source_target_pairs={{12,0},{8,4},{4,8},{0,12},{13,1},{9,5},{5,9},{1,13},{14,2},{10,6},... | collective-permute-start | bytes 98312 | tf_op jit(solution)/shard_map/ppermute | solution.py:395
  96.5 5.2 %collective-permute-start.24 = (bf16[32,512]{1,0:T(8,128)(2,1)S(1)}, bf16[32,512]{1,0:T(8,128)(2,1)S(1)}, u32[]{:S(2)}, u32[]{:S(2)}) collective-permute-start(bf16[32,512]{1,0:T(8,128)(2,1)S(1)} %get-tuple-element.111), channel_id=1, source_target_pairs={{8,0},{12,4},{0,8},{4,12},{9,1},{13,5},{1,9},{5,13},{10,2},{14,6},... | collective-permute-start | bytes 98312 | tf_op jit(solution)/shard_map/ppermute | solution.py:395
  96.9 4.8 %collective-permute-start.25 = (bf16[32,512]{1,0:T(8,128)(2,1)S(1)}, bf16[32,512]{1,0:T(8,128)(2,1)S(1)}, u32[]{:S(2)}, u32[]{:S(2)}) collective-permute-start(bf16[32,512]{1,0:T(8,128)(2,1)S(1)} %get-tuple-element.112), channel_id=1, source_target_pairs={{4,0},{0,4},{12,8},{8,12},{5,1},{1,5},{13,9},{9,13},{6,2},{2,6},{1... | collective-permute-start | bytes 98312 | tf_op jit(solution)/shard_map/ppermute | solution.py:395
  103.1 8.7 %collective-permute-start.26 = (bf16[128,512]{1,0:T(8,128)(2,1)S(1)}, bf16[128,512]{1,0:T(8,128)(2,1)S(1)}, u32[]{:S(2)}, u32[]{:S(2)}) collective-permute-start(bf16[128,512]{1,0:T(8,128)(2,1)S(1)} %get-tuple-element.125), channel_id=1, source_target_pairs={{4,0},{0,4},{12,8},{8,12},{5,1},{1,5},{13,9},{9,13},{6,2},{2,6},{1... | collective-permute-start | bytes 393224 | tf_op jit(solution)/shard_map/ppermute | solution.py:395
  104.6 10.2 %collective-permute-start.29 = (bf16[128,512]{1,0:T(8,128)(2,1)S(1)}, bf16[128,512]{1,0:T(8,128)(2,1)S(1)}, u32[]{:S(2)}, u32[]{:S(2)}) collective-permute-start(bf16[128,512]{1,0:T(8,128)(2,1)S(1)} %get-tuple-element.129), channel_id=1, source_target_pairs={{4,0},{0,4},{12,8},{8,12},{5,1},{1,5},{13,9},{9,13},{6,2},{2,6},{1... | collective-permute-start | bytes 393224 | tf_op jit(solution)/shard_map/ppermute | solution.py:395
  111.9 10.9 %collective-permute-start.27 = (bf16[256,512]{1,0:T(8,128)(2,1)S(1)}, bf16[256,512]{1,0:T(8,128)(2,1)S(1)}, u32[]{:S(2)}, u32[]{:S(2)}) collective-permute-start(bf16[256,512]{1,0:T(8,128)(2,1)S(1)} %get-tuple-element.127), channel_id=1, source_target_pairs={{4,0},{0,4},{12,8},{8,12},{5,1},{1,5},{13,9},{9,13},{6,2},{2,6},{1... | collective-permute-start | bytes 786440 | tf_op jit(solution)/shard_map/ppermute | solution.py:395
  112.0 6.0 %collective-permute-start.28 = (bf16[128,512]{1,0:T(8,128)(2,1)S(1)}, bf16[128,512]{1,0:T(8,128)(2,1)S(1)}, u32[]{:S(2)}, u32[]{:S(2)}) collective-permute-start(bf16[128,512]{1,0:T(8,128)(2,1)S(1)} %get-tuple-element.128), channel_id=1, source_target_pairs={{8,0},{12,4},{0,8},{4,12},{9,1},{13,5},{1,9},{5,13},{10,2},{14,6},... | collective-permute-start | bytes 393224 | tf_op jit(solution)/shard_map/ppermute | solution.py:395
  114.9 8.0 %collective-permute-start.30 = (bf16[128,512]{1,0:T(8,128)(2,1)S(1)}, bf16[128,512]{1,0:T(8,128)(2,1)S(1)}, u32[]{:S(2)}, u32[]{:S(2)}) collective-permute-start(bf16[128,512]{1,0:T(8,128)(2,1)S(1)} %shard_map.188), channel_id=1, source_target_pairs={{8,0},{12,4},{0,8},{4,12},{9,1},{13,5},{1,9},{5,13},{10,2},{14,6},... | collective-permute-start | bytes 393224 | tf_op jit(solution)/shard_map/ppermute | solution.py:395

commit v9 on v8

--- a/solution.py
+++ b/solution.py
@@ -195,10 +195,11 @@
 
 def hand_out(rows, outs):
     rows = rows.astype(bf16)
-    at = 0
-    for out in outs:
-        out[...] = rows[at : at + out.shape[0]]
-        at += out.shape[0]
+    depth = outs[0].shape[0]
+    count = rows.shape[0] // depth
+    for at, out in enumerate(outs):
+        first = 0 if at == 0 else (count - len(outs) + at) * depth
+        out[...] = rows[first : first + depth]
 
 
 def start_kernel(halves, *refs):
@@ -232,6 +233,12 @@
         pre[at : at + BLOCK, :] = dot(here[at : at + BLOCK, :], table[...])
 
 
+def local_more_kernel(table, here, pre):
+    skip = here.shape[0] - pre.shape[0]
+    for at in range(0, pre.shape[0], BLOCK):
+        pre[at : at + BLOCK, :] = dot(here[skip + at : skip + at + BLOCK, :], table[...])
+
+
 def stack_halo(halos, halo):
     at = 0
     for block in halos:
@@ -241,24 +248,26 @@
         halo[at:, :] = jnp.zeros((halo.shape[0] - at, halo.shape[1]), bf16)
 
 
-def node_sum(pre, halos, halo_here, there, slope_out, halo, act_out):
+def node_sum(pres, halos, halo_here, there, slope_out, halo, act_out):
     nodes = there.shape[0] // 2
     stack_halo(halos, halo)
-    for at in range(0, pre.shape[0], BLOCK):
+    half = pres[0].shape[0]
+    for at in range(0, 2 * half, BLOCK):
         block = slice(at, at + BLOCK)
-        act, slope = gated(pre[block, :] + dot(halo_here[block, :], halo[...]))
+        pre = pres[at // half][at % half : at % half + BLOCK, :]
+        act, slope = gated(pre + dot(halo_here[block, :], halo[...]))
         slope_out[block, :] = slope.astype(bf16)
         act_out[block, :] = act.astype(bf16)
     return dot(there[nodes:, :], act_out[...])
 
 
 def layer_kernel(layer, shifts, *refs):
-    hidden, pre = refs[:2]
-    halos, refs = refs[2 : 2 + shifts], refs[2 + shifts :]
+    hidden, pres = refs[0], refs[1:3]
+    halos, refs = refs[3 : 3 + shifts], refs[3 + shifts :]
     halo_here, there, w_out, gain, w_send, list_here = refs[:6]
     hidden_out, agg_out, slope_out, sent_out = refs[6:10]
     outs = refs[10:-2]
-    total = node_sum(pre, halos, halo_here, there, slope_out, *refs[-2:])
+    total = node_sum(pres, halos, halo_here, there, slope_out, *refs[-2:])
     agg = dot(total.astype(bf16), w_out[layer])
     agg_out[...] = agg
     fresh = (hidden[...].astype(f32) + agg * norm_scale(agg) * gain[layer : layer + 1, :]).astype(bf16)
@@ -268,38 +277,34 @@
     hand_out(dot(list_here[...], projected), outs)
 
 
-def edge_grads(grad_agg, w_out, here, halo_there, slope, grad_pre, outs):
+def edge_grads(listed, grad_agg, w_out, here, halo_there, slope, grad_pre, outs):
     nodes = grad_agg.shape[0]
     spread = dot_back(grad_agg.astype(bf16), w_out).astype(bf16)
     for at in range(0, slope.shape[0], BLOCK):
         block = slice(at, at + BLOCK)
         grad_act = dot(here[block, nodes:], spread)
         grad_pre[block, :] = (grad_act * slope[block, :].astype(f32)).astype(bf16)
-    hand_out(dot(halo_there[...], grad_pre[...]), outs)
+    hand_out(dot(halo_there[...], grad_pre[...])[0:listed], outs)
 
 
 def turn_kernel(layer, shifts, *refs):
-    hidden, pre = refs[:2]
-    halos, refs = refs[2 : 2 + shifts], refs[2 + shifts :]
+    hidden, pres = refs[0], refs[1:3]
+    halos, refs = refs[3 : 3 + shifts], refs[3 + shifts :]
     halo_here, there, w_out, gain, here, halo_there, cot = refs[:7]
     hidden_out, grad_pre = refs[7:9]
     outs = refs[9:-2]
     slope, halo = refs[-2:]
-    total = node_sum(pre, halos, halo_here, there, slope, halo, grad_pre)
+    total = node_sum(pres, halos, halo_here, there, slope, halo, grad_pre)
     agg = dot(total.astype(bf16), w_out[layer])
     gain_row = gain[layer : layer + 1, :]
     hidden_out[...] = (hidden[...].astype(f32) + agg * norm_scale(agg) * gain_row).astype(bf16)
-    edge_grads(norm_back(agg, gain_row, cot[...].astype(f32)), w_out[layer], here, halo_there, slope, grad_pre, outs)
-
-
-def rest_kernel(layer, upstream, grad_pre, there, w_send, w_recv, rest):
+    edge_grads(shifts * outs[0].shape[0], norm_back(agg, gain_row, cot[...].astype(f32)), w_out[layer], here, halo_there, slope, grad_pre, outs)
+
+
+def rest_kernel(layer, side, upstream, grad_pre, there, weights, rest):
     nodes = upstream.shape[0]
-    sums = dot(there[...], grad_pre[...]).astype(bf16)
-    rest[...] = (
-        upstream[...].astype(f32)
-        + dot_back(sums[0:nodes], w_send[layer])
-        + dot_back(sums[nodes:], w_recv[layer])
-    )
+    sums = dot(there[side * nodes : (side + 1) * nodes, :], grad_pre[...]).astype(bf16)
+    rest[...] = upstream[...].astype(f32) + dot_back(sums, weights[layer])
 
 
 def arrived(rest, returned, list_there, w_send, halo):
@@ -318,7 +323,7 @@
     upstream = arrived(rest, returned, list_there, w_send[layer + 1], halo)
     upstream_out[...] = upstream
     grad_agg = norm_back(agg[...], gain[layer : layer + 1, :], upstream)
-    edge_grads(grad_agg, w_out[layer], here, halo_there, slope, grad_pre, outs)
+    edge_grads(shifts * outs[0].shape[0], grad_agg, w_out[layer], here, halo_there, slope, grad_pre, outs)
 
 
 def pair_grads(spread, pick, slope):
@@ -433,6 +438,7 @@
 
     relayed = shards == 4
     cuts = 2 if relayed else 1
+    shared = relayed and halves == 2
     piece_rows = grid // cuts
     in_place = [pltpu.with_memory_space_constraint(array, pltpu.HBM) for array in (grid_feats, g2m_shard.T, g2m_node.T)]
     (payload,) = call(
@@ -458,7 +464,14 @@
     both = in_order([both] + [shifted(both, "feat", step) for step in range(1, feats)], "feat")
     both = both.reshape(feats * halves, 2, edges)
     all_slots, all_receivers = both[:, 0].reshape(1, -1), both[:, 1].reshape(1, -1)
-    readers = partner(shard, shards - jnp.arange(1, shards, dtype=i32), shards)
+    steps = shards - jnp.arange(1, shards, dtype=i32)
+    if shared:
+        core = lax.axis_index("rep")
+        steps = jnp.where((core == 0) & (steps > 1), 5 - steps, steps)
+        entry = all_slots - nodes
+        turned = (core == 0) & (entry >= 0) & (entry < 2 * depth)
+        all_slots = all_slots + jnp.where(turned, jnp.where(entry < depth, depth, -depth), 0)
+    readers = partner(shard, steps, shards)
     lists = jnp.take(halo_index[0], readers, axis=0).reshape(1, -1)
     here, there, halo_here, halo_there, list_here, list_there = call(
         place_kernel,
@@ -516,29 +529,36 @@
     part = sum(piece.astype(f32) for piece in pieces).astype(bf16)
     parts = [part] + [shifted(part, "rep", -step) for step in range(1, halves)]
 
-    listed = [((depth, width), bf16)] * shifts
-
-    def exchange(blocks, send):
-        return [send(block, shifts - at) for at, block in enumerate(blocks)]
+    listed = [((depth, width), bf16)] * (2 if shared else shifts)
+
+    def exchange(blocks, send, early):
+        if not shared:
+            return [send(block, shifts - at) for at, block in enumerate(blocks)], early
+        far = lax.ppermute(
+            blocks[0], ("mesh", "rep"), [(2 * at + side, 2 * (at ^ (2 + side)) + side) for at in range(4) for side in range(2)]
+        )
+        near = send(blocks[1], 1)
+        far, early = lax.optimization_barrier((far, early))
+        return [far, shifted(far, "rep", 1), near], early
 
     hidden, enc_sum, sent, *outgoing = call(
         functools.partial(start_kernel, halves), [node_bf16, node_f32, node_bf16] + listed, [node_bf16],
         [square, square, (listed_rows, nodes, width)],
     )(meta, *parts, mesh_init, w_enc_out, enc_gain, w_send, list_here)
 
-    edge_f32, edge_bf16 = ((all_edges, width), f32), ((all_edges, width), bf16)
+    half_f32, edge_bf16 = ((all_edges // 2, width), f32), ((all_edges, width), bf16)
     halo, back_halo = ((wide, width), bf16), ((listed_rows, width), bf16)
     forward_products = [(all_edges, wide, width), (nodes, all_edges, width), square]
     backward_products = [square, (all_edges, nodes, width), (wide, all_edges, width)]
+    half_product = (all_edges // 2, 2 * nodes, width)
 
     def arriving(layer):
-        (pre,) = call(
-            functools.partial(local_kernel, layer),
-            [edge_f32],
-            [((2 * nodes, width), bf16)],
-            [square, (all_edges, 2 * nodes, width)],
+        early = call(
+            functools.partial(local_kernel, layer), [half_f32, ((2 * nodes, width), bf16)], (), [square, half_product]
         )(hidden, sent, here, w_recv)
-        return hidden, pre, *exchange(outgoing, sent_to)
+        halos, (pre, both_tables) = exchange(outgoing, sent_to, early)
+        (more,) = call(local_more_kernel, [half_f32], (), [half_product])(both_tables, here)
+        return hidden, pre, more, *halos
 
     records = []
     for layer in range(LAYERS - 1):
@@ -556,10 +576,15 @@
     )(*arriving(last), halo_here, there, w_out, layer_gain, here, halo_there, out_cot)
     upstream = out_cot
     for layer in reversed(range(LAYERS)):
-        returned = exchange(outgoing, sent_back)
-        (rest,) = call(
-            functools.partial(rest_kernel, layer), [node_f32], (), [(2 * nodes, all_edges, width), square, square]
-        )(upstream, grad_pre, there, w_send, w_recv)
+
+        def rest_of(side, upstream, weights):
+            (rest,) = call(
+                functools.partial(rest_kernel, layer, side), [node_f32], (), [(nodes, all_edges, width), square]
+            )(upstream, grad_pre, there, weights)
+            return rest
+
+        returned, early = exchange(outgoing, sent_back, rest_of(0, upstream, w_send))
+        rest = rest_of(1, early, w_recv)
         if layer:
             agg, slope = records[layer - 1]
             upstream, grad_pre, *outgoing = call(

time: 124 us -> 123 us (level)
  starting transfers between devices: 41.3 us -> 32 us
  waiting for transfers between devices: 32.5 us -> 38.8 us
    ppermute x14 -> x8, starting transfers between devices: 18.5 us -> 11.2 us  [sent_back(): lax.ppermute(value, 'mesh', [(partner(at, step, size), at) for at in rang...]
    ppermute x12 -> x6, starting transfers between devices: 19.5 us -> 12.7 us  [sent_to(): lax.ppermute(value, 'mesh', [(at, partner(at, step, size)) for at in rang...]
    ppermute x0 -> x6, waiting for transfers between devices: none -> 6.09 us  [exchange(): lax.ppermute(blocks[0], ('mesh', 'rep'), [(2 * at + side, 2 * (at ^ 2 + s...]
    ppermute x0 -> x6, starting transfers between devices: none -> 4.22 us  [exchange(): lax.ppermute(blocks[0], ('mesh', 'rep'), [(2 * at + side, 2 * (at ^ 2 + s...]
    pallas_call x23 -> x29, Pallas kernels: 46.5 us -> 47.5 us  [run(): pl.pallas_call(body, out_shape=tuple((jax.ShapeDtypeStruct(shape, dtype)...]
    ppermute x14 -> x8, waiting for transfers between devices: 13.8 us -> 14.6 us  [sent_back(): lax.ppermute(value, 'mesh', [(partner(at, step, size), at) for at in rang...]
    ppermute x12 -> x6, waiting for transfers between devices: 6.28 us -> 5.65 us  [sent_to(): lax.ppermute(value, 'mesh', [(at, partner(at, step, size)) for at in rang...]
    ppermute x5 -> x11, starting transfers between devices: 3.26 us -> 3.87 us  [shifted(): lax.ppermute(value, axis, [(at, (at + by) % size) for at in range(size)])]
  transfers between devices with their start and end apart: 31 -> 31, of which waited for: 12 -> 16; matrix products, arithmetic and copies ran while one was open for 2% -> 2% of each run, Pallas kernels for 19% -> 20%
where the time goes in v9:
time: 123 us; the launch traced here: 122 us
  Pallas kernels  47.5 us (39%)
  waiting for transfers between devices  38.8 us (32%)
  starting transfers between devices  32 us (26%)
  other arithmetic  1.82 us (1%)
    pallas_call x29, Pallas kernels, run(): pl.pallas_call(body, out_shape=tuple((jax.ShapeDtypeStruct(shape, dtype)...  47.5 us
    ppermute x8, waiting for transfers between devices, sent_back(): lax.ppermute(value, 'mesh', [(partner(at, step, size), at) for at in rang...  14.6 us
    ppermute x6, starting transfers between devices, sent_to(): lax.ppermute(value, 'mesh', [(at, partner(at, step, size)) for at in rang...  12.7 us
    ppermute x11, waiting for transfers between devices, shifted(): lax.ppermute(value, axis, [(at, (at + by) % size) for at in range(size)])  12.4 us
    ppermute x8, starting transfers between devices, sent_back(): lax.ppermute(value, 'mesh', [(partner(at, step, size), at) for at in rang...  11.2 us
    ppermute x6, waiting for transfers between devices, exchange(): lax.ppermute(blocks[0], ('mesh', 'rep'), [(2 * at + side, 2 * (at ^ 2 + s...  6.09 us
    ppermute x6, waiting for transfers between devices, sent_to(): lax.ppermute(value, 'mesh', [(at, partner(at, step, size)) for at in rang...  5.65 us
    ppermute x6, starting transfers between devices, exchange(): lax.ppermute(blocks[0], ('mesh', 'rep'), [(2 * at + side, 2 * (at ^ 2 + s...  4.22 us
  transfers between devices with their start and end apart: 31, of which 16 were waited for; matrix products, arithmetic and copies ran while one was open for 2% of the time, Pallas kernels for 20%

profile of v9, /device:TPU:0, one launch (start us, length us, event | category | flops | bytes accessed | tf_op | source)
XLA Modules:
  0.0 122.3 jit_solution(2807522094286176690)
XLA Ops:
  0.6 1.0 shard_map.167.refs_5_
  1.7 3.1 %collective-permute-start.3 = (bf16[272,512]{1,0:T(8,128)(2,1)S(1)}, bf16[272,512]{1,0:T(8,128)(2,1)S(1)}, u32[]{:S(2)}, u32[]{:S(2)}) collective-permute-start(bf16[272,512]{1,0:T(8,128)(2,1)S(1)} %shard_map.167.refs_5_), channel_id=1, source_target_pairs={{0,4},{4,0},{8,12},{12,8},{1,5},{5,1},{9,13},{13,9},{2,6},{6,2},{1... | collective-permute-start | bytes 835592 | tf_op jit(solution)/shard_map/ppermute | solution.py:395
  4.8 2.6 %collective-permute-start = (bf16[272,512]{1,0:T(8,128)(2,1)S(1)}, bf16[272,512]{1,0:T(8,128)(2,1)S(1)}, u32[]{:S(2)}, u32[]{:S(2)}) collective-permute-start(bf16[272,512]{1,0:T(8,128)(2,1)S(1)} %shard_map.167.refs_5_), channel_id=1, source_target_pairs={{0,8},{4,12},{8,0},{12,4},{1,9},{5,13},{9,1},{13,5},{2,10},{6,14},... | collective-permute-start | bytes 835592 | tf_op jit(solution)/shard_map/ppermute | solution.py:395
  7.3 0.7 compare_select_fusion.1
  8.0 0.7 fusion.11
  8.8 0.6 gather_fusion
  9.5 0.4 collective-permute-done.1
  10.1 1.6 %collective-permute-start.2 = (s32[2,2,512]{2,0,1:T(2,128)S(1)}, s32[2,2,512]{2,0,1:T(2,128)S(1)}, u32[]{:S(2)}, u32[]{:S(2)}) collective-permute-start(s32[2,2,512]{2,0,1:T(2,128)S(1)} %fusion.1), channel_id=1, source_target_pairs={{0,2},{2,0},{1,3},{3,1},{4,6},{6,4},{5,7},{7,5},{8,10},{10,8},{9,1... | collective-permute-start | bytes 24584 | tf_op jit(solution)/shard_map/ppermute | solution.py:386
  11.7 2.1 %collective-permute-done.2 = s32[2,2,512]{2,0,1:T(2,128)S(1)} collective-permute-done((s32[2,2,512]{2,0,1:T(2,128)S(1)}, s32[2,2,512]{2,0,1:T(2,128)S(1)}, u32[]{:S(2)}, u32[]{:S(2)}) %collective-permute-start.2) | collective-permute-done | bytes 8224 | tf_op jit(solution)/shard_map/ppermute | solution.py:386
  14.0 3.5 %shard_map.168 = (bf16[2048,1024]{1,0:T(8,128)(2,1)S(1)}, bf16[1024,2048]{1,0:T(8,128)(2,1)S(1)}, bf16[2048,128]{1,0:T(8,128)(2,1)S(1)}, bf16[128,2048]{1,0:T(8,...) custom-call(s32[1,2048]{1,0:T(1,128)S(1)} %fusion.2.slots, s32[1,2048]{1,0:T(1,128)S(1)} %bitcast.26, ...), custom_call_target="tpu_custom_call" | custom-call | flops 3221225472 | bytes 9650560 | tf_op jit(solution)/shard_map/pallas_call | solution.py:82
  17.5 2.3 %collective-permute-done.refs_4_ = bf16[272,512]{1,0:T(8,128)(2,1)S(1)} collective-permute-done((bf16[272,512]{1,0:T(8,128)(2,1)S(1)}, bf16[272,512]{1,0:T(8,128)(2,1)S(1)}, u32[]{:S(2)}, u32[]{:S(2)}) %collective-permute-start) | collective-permute-done | bytes 278560 | tf_op jit(solution)/shard_map/ppermute | solution.py:395
  19.8 0.4 collective-permute-start.4
  20.4 1.7 %shard_map.169 = (bf16[256,512]{1,0:T(8,128)(2,1)S(1)}, bf16[256,512]{1,0:T(8,128)(2,1)S(1)}, bf16[256,512]{1,0:T(8,128)(2,1)S(1)}, bf16[256,512]{1,0:T(8,128)(2...) custom-call(s32[2,512]{1,0:T(2,128)S(1)} %broadcast_in_dim.27.refs_0_, bf16[512,512]{1,0:T(8,128)(2,1)S(1)} %copy-done.8, ...), custom_call_target="tpu_custom_call" | custom-call | flops 1073741824 | bytes 4853760 | tf_op jit(solution)/shard_map/pallas_call | solution.py:82
  22.1 0.9 shard_map.170
  23.0 3.4 %collective-permute-done.4.refs_4_ = bf16[272,512]{1,0:T(8,128)(2,1)S(1)} collective-permute-done((bf16[272,512]{1,0:T(8,128)(2,1)S(1)}, bf16[272,512]{1,0:T(8,128)(2,1)S(1)}, u32[]{:S(2)}, u32[]{:S(2)}) %collective-permute-start.4) | collective-permute-done | bytes 278560 | tf_op jit(solution)/shard_map/ppermute | solution.py:395
  26.3 0.9 shard_map.171
  27.4 1.5 %collective-permute-done.5 = bf16[256,512]{1,0:T(8,128)(2,1)S(1)} collective-permute-done((bf16[256,512]{1,0:T(8,128)(2,1)S(1)}, bf16[256,512]{1,0:T(8,128)(2,1)S(1)}, u32[]{:S(2)}, u32[]{:S(2)}) %collective-permute-start.5) | collective-permute-done | bytes 262176 | tf_op jit(solution)/shard_map/ppermute | solution.py:386
  29.0 1.6 %collective-permute-start.6 = (bf16[256,512]{1,0:T(8,128)(2,1)S(1)}, bf16[256,512]{1,0:T(8,128)(2,1)S(1)}, u32[]{:S(2)}, u32[]{:S(2)}) collective-permute-start(bf16[256,512]{1,0:T(8,128)(2,1)S(1)} %add_convert_fusion.1), channel_id=1, source_target_pairs={{0,2},{2,0},{1,3},{3,1},{4,6},{6,4},{5,7},{7,5},{8,10},{10,8},{9,1... | collective-permute-start | bytes 786440 | tf_op jit(solution)/shard_map/ppermute | solution.py:386
  30.5 6.9 %collective-permute-done.6 = bf16[256,512]{1,0:T(8,128)(2,1)S(1)} collective-permute-done((bf16[256,512]{1,0:T(8,128)(2,1)S(1)}, bf16[256,512]{1,0:T(8,128)(2,1)S(1)}, u32[]{:S(2)}, u32[]{:S(2)}) %collective-permute-start.6) | collective-permute-done | bytes 262176 | tf_op jit(solution)/shard_map/ppermute | solution.py:386
  37.5 1.5 %collective-permute-done.7.refs_2_ = bf16[256,512]{1,0:T(8,128)(2,1)S(1)} collective-permute-done((bf16[256,512]{1,0:T(8,128)(2,1)S(1)}, bf16[256,512]{1,0:T(8,128)(2,1)S(1)}, u32[]{:S(2)}, u32[]{:S(2)}) %collective-permute-start.7) | collective-permute-done | bytes 262176 | tf_op jit(solution)/shard_map/ppermute | solution.py:386
  39.1 1.0 shard_map.172
  40.1 1.3 %collective-permute-start.8 = (bf16[32,512]{1,0:T(8,128)(2,1)S(1)}, bf16[32,512]{1,0:T(8,128)(2,1)S(1)}, u32[]{:S(2)}, u32[]{:S(2)}) collective-permute-start(bf16[32,512]{1,0:T(8,128)(2,1)S(1)} %get-tuple-element.90), channel_id=1, source_target_pairs={{0,8},{1,13},{4,12},{5,9},{8,0},{9,5},{12,4},{13,1},{2,10},{3,15},... | collective-permute-start | bytes 98312 | tf_op jit(solution)/shard_map/ppermute | solution.py:537
  41.4 1.9 %collective-permute-start.10 = (bf16[32,512]{1,0:T(8,128)(2,1)S(1)}, bf16[32,512]{1,0:T(8,128)(2,1)S(1)}, u32[]{:S(2)}, u32[]{:S(2)}) collective-permute-start(bf16[32,512]{1,0:T(8,128)(2,1)S(1)} %get-tuple-element.98), channel_id=1, source_target_pairs={{0,4},{4,0},{8,12},{12,8},{1,5},{5,1},{9,13},{13,9},{2,6},{6,2},{1... | collective-permute-start | bytes 98312 | tf_op jit(solution)/shard_map/ppermute | solution.py:395
  43.3 1.5 %shard_map.173 = (f32[1024,512]{1,0:T(8,128)S(1)}, bf16[1024,512]{1,0:T(8,128)(2,1)S(1)}) custom-call(bf16[512,512]{1,0:T(8,128)(2,1)S(1)} %get-tuple-element.89.hidden.refs_0_, bf16[512,512]{1,0:T(8,128)(2,1)S(1)} %get-tuple-element.91.sent, bf16[2048,1024]{1,0:T(8,128)(2,1)S(1)} %get-tuple-element.92.here.refs_10_, bf16[3,512,512]{2,1,0:T(8,128)(2,1)S(1)} %copy-done.3), custom_call_target="tpu_custom_call" | custom-call | flops 1342177280 | bytes 9961472 | tf_op jit(solution)/shard_map/pallas_call | solution.py:82
  44.8 0.5 collective-permute-done.8.refs_3_
  45.4 1.2 %shard_map.174.refs_2_ = f32[1024,512]{1,0:T(8,128)S(1)} custom-call(bf16[1024,512]{1,0:T(8,128)(2,1)S(1)} %get-tuple-element.96.table, bf16[2048,1024]{1,0:T(8,128)(2,1)S(1)} %get-tuple-element.92.here.refs_10_), custom_call_target="tpu_custom_call" | custom-call | flops 1073741824 | bytes 7340032 | tf_op jit(solution)/shard_map/pallas_call | solution.py:82
  46.8 3.2 %shard_map.175 = (bf16[512,512]{1,0:T(8,128)(2,1)S(1)}, f32[512,512]{1,0:T(8,128)S(1)}, bf16[2048,512]{1,0:T(8,128)(2,1)S(1)}, bf16[512,512]{1,0:T(8,128)(2,1)S(...) custom-call(bf16[512,512]{1,0:T(8,128)(2,1)S(1)} %get-tuple-element.89.hidden.refs_0_, ...), custom_call_target="tpu_custom_call" | custom-call | flops 1929379840 | bytes 17045504 | tf_op jit(solution)/shard_map/pallas_call | solution.py:82
  50.0 0.9 collective-permute-start.11
  50.9 2.3 %collective-permute-start.13 = (bf16[32,512]{1,0:T(8,128)(2,1)S(1)}, bf16[32,512]{1,0:T(8,128)(2,1)S(1)}, u32[]{:S(2)}, u32[]{:S(2)}) collective-permute-start(bf16[32,512]{1,0:T(8,128)(2,1)S(1)} %get-tuple-element.109), channel_id=1, source_target_pairs={{0,4},{4,0},{8,12},{12,8},{1,5},{5,1},{9,13},{13,9},{2,6},{6,2},{1... | collective-permute-start | bytes 98312 | tf_op jit(solution)/shard_map/ppermute | solution.py:395
  53.2 1.5 %shard_map.176 = (f32[1024,512]{1,0:T(8,128)S(1)}, bf16[1024,512]{1,0:T(8,128)(2,1)S(1)}) custom-call(bf16[512,512]{1,0:T(8,128)(2,1)S(1)} %get-tuple-element.101.hidden.refs_0_, bf16[512,512]{1,0:T(8,128)(2,1)S(1)} %get-tuple-element.103.sent, bf16[2048,1024]{1,0:T(8,128)(2,1)S(1)} %get-tuple-element.92.here.refs_10_, bf16[3,512,512]{2,1,0:T(8,128)(2,1)S(1)} %copy-done.3), custom_call_target="tpu_custom_call" | custom-call | flops 1342177280 | bytes 9961472 | tf_op jit(solution)/shard_map/pallas_call | solution.py:82
  54.9 0.4 collective-permute-start.12
  55.3 1.2 %shard_map.177.refs_2_ = f32[1024,512]{1,0:T(8,128)S(1)} custom-call(bf16[1024,512]{1,0:T(8,128)(2,1)S(1)} %get-tuple-element.107.table, bf16[2048,1024]{1,0:T(8,128)(2,1)S(1)} %get-tuple-element.92.here.refs_10_), custom_call_target="tpu_custom_call" | custom-call | flops 1073741824 | bytes 7340032 | tf_op jit(solution)/shard_map/pallas_call | solution.py:82
  56.6 3.5 %shard_map.178 = (bf16[512,512]{1,0:T(8,128)(2,1)S(1)}, f32[512,512]{1,0:T(8,128)S(1)}, bf16[2048,512]{1,0:T(8,128)(2,1)S(1)}, bf16[512,512]{1,0:T(8,128)(2,1)S(...) custom-call(bf16[512,512]{1,0:T(8,128)(2,1)S(1)} %get-tuple-element.101.hidden.refs_0_, ...), custom_call_target="tpu_custom_call" | custom-call | flops 1929379840 | bytes 17045504 | tf_op jit(solution)/shard_map/pallas_call | solution.py:82
  60.1 0.6 collective-permute-start.14
  60.7 2.4 %collective-permute-start.16 = (bf16[32,512]{1,0:T(8,128)(2,1)S(1)}, bf16[32,512]{1,0:T(8,128)(2,1)S(1)}, u32[]{:S(2)}, u32[]{:S(2)}) collective-permute-start(bf16[32,512]{1,0:T(8,128)(2,1)S(1)} %get-tuple-element.118), channel_id=1, source_target_pairs={{0,4},{4,0},{8,12},{12,8},{1,5},{5,1},{9,13},{13,9},{2,6},{6,2},{1... | collective-permute-start | bytes 98312 | tf_op jit(solution)/shard_map/ppermute | solution.py:395
  63.1 1.5 %shard_map.179 = (f32[1024,512]{1,0:T(8,128)S(1)}, bf16[1024,512]{1,0:T(8,128)(2,1)S(1)}) custom-call(bf16[512,512]{1,0:T(8,128)(2,1)S(1)} %get-tuple-element.110.hidden.refs_0_, bf16[512,512]{1,0:T(8,128)(2,1)S(1)} %get-tuple-element.112.sent, bf16[2048,1024]{1,0:T(8,128)(2,1)S(1)} %get-tuple-element.92.here.refs_10_, bf16[3,512,512]{2,1,0:T(8,128)(2,1)S(1)} %copy-done.3), custom_call_target="tpu_custom_call" | custom-call | flops 1342177280 | bytes 9961472 | tf_op jit(solution)/shard_map/pallas_call | solution.py:82
  64.6 1.0 collective-permute-done.14.refs_3_
  65.7 1.2 %shard_map.180.refs_2_ = f32[1024,512]{1,0:T(8,128)S(1)} custom-call(bf16[1024,512]{1,0:T(8,128)(2,1)S(1)} %get-tuple-element.116.table, bf16[2048,1024]{1,0:T(8,128)(2,1)S(1)} %get-tuple-element.92.here.refs_10_), custom_call_target="tpu_custom_call" | custom-call | flops 1073741824 | bytes 7340032 | tf_op jit(solution)/shard_map/pallas_call | solution.py:82
  66.9 5.7 %shard_map.181 = (bf16[512,512]{1,0:T(8,128)(2,1)}, bf16[2048,512]{1,0:T(8,128)(2,1)S(1)}, bf16[32,512]{1,0:T(8,128)(2,1)S(1)}, bf16[32,512]{1,0:T(8,128)(2,1)S(1)}) custom-call(bf16[512,512]{1,0:T(8,128)(2,1)S(1)} %get-tuple-element.110.hidden.refs_0_, f32[1024,512]{1,0:T(8,128)S(1)} %get-tuple-element.115.refs_1_, f32[1024,512]{1,0:T(8,128)S(1)} %shard_map.180.refs_2_, ...), custom_call_target="tpu_custom_call" | custom-call | flops 3221225472 | bytes 19044352 | tf_op jit(solution)/shard_map/pallas_call | solution.py:82
  72.7 2.5 %collective-permute-start.19 = (bf16[32,512]{1,0:T(8,128)(2,1)S(1)}, bf16[32,512]{1,0:T(8,128)(2,1)S(1)}, u32[]{:S(2)}, u32[]{:S(2)}) collective-permute-start(bf16[32,512]{1,0:T(8,128)(2,1)S(1)} %get-tuple-element.125), channel_id=1, source_target_pairs={{4,0},{0,4},{12,8},{8,12},{5,1},{1,5},{13,9},{9,13},{6,2},{2,6},{1... | collective-permute-start | bytes 98312 | tf_op jit(solution)/shard_map/ppermute | solution.py:400
  75.1 1.5 %shard_map.182.upstream = f32[512,512]{1,0:T(8,128)S(1)} custom-call(bf16[512,512]{1,0:T(8,128)(2,1)S(1)} %copy-done.6, bf16[2048,512]{1,0:T(8,128)(2,1)S(1)} %get-tuple-element.122.grad_pre, bf16[1024,2048]{1,0:T(8,128)(2,1)S(1)} %get-tuple-element.100.refs_7_.there, bf16[3,512,512]{2,1,0:T(8,128)(2,1)S(1)} %copy-done.2), custom_call_target="tpu_custom_call" | custom-call | flops 1342177280 | bytes 9437184 | tf_op jit(solution)/shard_map/pallas_call | solution.py:82
  76.7 1.5 %collective-permute-done.17.refs_1_ = bf16[32,512]{1,0:T(8,128)(2,1)S(1)} collective-permute-done((bf16[32,512]{1,0:T(8,128)(2,1)S(1)}, bf16[32,512]{1,0:T(8,128)(2,1)S(1)}, u32[]{:S(2)}, u32[]{:S(2)}) %collective-permute-start.17) | collective-permute-done | bytes 32800 | tf_op jit(solution)/shard_map/ppermute | solution.py:537
  78.2 1.5 %shard_map.183.refs_0_ = f32[512,512]{1,0:T(8,128)S(1)} custom-call(f32[512,512]{1,0:T(8,128)S(1)} %shard_map.182.upstream, bf16[2048,512]{1,0:T(8,128)(2,1)S(1)} %get-tuple-element.122.grad_pre, bf16[1024,2048]{1,0:T(8,128)(2,1)S(1)} %get-tuple-element.100.refs_7_.there, bf16[3,512,512]{2,1,0:T(8,128)(2,1)S(1)} %copy-done.3), custom_call_target="tpu_custom_call" | custom-call | flops 1342177280 | bytes 9961472 | tf_op jit(solution)/shard_map/pallas_call | solution.py:82
  79.8 2.6 %shard_map.184 = (f32[512,512]{1,0:T(8,128)S(1)}, bf16[2048,512]{1,0:T(8,128)(2,1)S(1)}, bf16[32,512]{1,0:T(8,128)(2,1)S(1)}, bf16[32,512]{1,0:T(8,128)(2,1)S(1)}) custom-call(f32[512,512]{1,0:T(8,128)S(1)} %shard_map.183.refs_0_, bf16[32,512]{1,0:T(8,128)(2,1)S(1)} %collective-permute-done.17.refs_1_, bf16[32,512]{1,0:T(8,128)(2,1)S(1)} %collective-permute-done.18.refs_2_, ...), custom_call_target="tpu_custom_call" | custom-call | flops 1711276032 | bytes 15472640 | tf_op jit(solution)/shard_map/pallas_call | solution.py:82
  82.3 0.4 collective-permute-start.20
  82.7 1.7 %collective-permute-start.22 = (bf16[32,512]{1,0:T(8,128)(2,1)S(1)}, bf16[32,512]{1,0:T(8,128)(2,1)S(1)}, u32[]{:S(2)}, u32[]{:S(2)}) collective-permute-start(bf16[32,512]{1,0:T(8,128)(2,1)S(1)} %get-tuple-element.134), channel_id=1, source_target_pairs={{4,0},{0,4},{12,8},{8,12},{5,1},{1,5},{13,9},{9,13},{6,2},{2,6},{1... | collective-permute-start | bytes 98312 | tf_op jit(solution)/shard_map/ppermute | solution.py:400
  84.4 1.5 %shard_map.185.upstream = f32[512,512]{1,0:T(8,128)S(1)} custom-call(f32[512,512]{1,0:T(8,128)S(1)} %get-tuple-element.130.upstream, bf16[2048,512]{1,0:T(8,128)(2,1)S(1)} %get-tuple-element.131.grad_pre, bf16[1024,2048]{1,0:T(8,128)(2,1)S(1)} %get-tuple-element.100.refs_7_.there, bf16[3,512,512]{2,1,0:T(8,128)(2,1)S(1)} %copy-done.2), custom_call_target="tpu_custom_call" | custom-call | flops 1342177280 | bytes 9961472 | tf_op jit(solution)/shard_map/pallas_call | solution.py:82
  85.9 1.4 %collective-permute-done.20.refs_1_ = bf16[32,512]{1,0:T(8,128)(2,1)S(1)} collective-permute-done((bf16[32,512]{1,0:T(8,128)(2,1)S(1)}, bf16[32,512]{1,0:T(8,128)(2,1)S(1)}, u32[]{:S(2)}, u32[]{:S(2)}) %collective-permute-start.20) | collective-permute-done | bytes 32800 | tf_op jit(solution)/shard_map/ppermute | solution.py:537
  87.5 1.8 %shard_map.186.refs_0_ = f32[512,512]{1,0:T(8,128)S(1)} custom-call(f32[512,512]{1,0:T(8,128)S(1)} %shard_map.185.upstream, bf16[2048,512]{1,0:T(8,128)(2,1)S(1)} %get-tuple-element.131.grad_pre, bf16[1024,2048]{1,0:T(8,128)(2,1)S(1)} %get-tuple-element.100.refs_7_.there, bf16[3,512,512]{2,1,0:T(8,128)(2,1)S(1)} %copy-done.3), custom_call_target="tpu_custom_call" | custom-call | flops 1342177280 | bytes 9961472 | tf_op jit(solution)/shard_map/pallas_call | solution.py:82
  89.3 2.6 %shard_map.187 = (f32[512,512]{1,0:T(8,128)S(1)}, bf16[2048,512]{1,0:T(8,128)(2,1)S(1)}, bf16[32,512]{1,0:T(8,128)(2,1)S(1)}, bf16[32,512]{1,0:T(8,128)(2,1)S(1)}) custom-call(f32[512,512]{1,0:T(8,128)S(1)} %shard_map.186.refs_0_, bf16[32,512]{1,0:T(8,128)(2,1)S(1)} %collective-permute-done.20.refs_1_, bf16[32,512]{1,0:T(8,128)(2,1)S(1)} %collective-permute-done.21.refs_2_, ...), custom_call_target="tpu_custom_call" | custom-call | flops 1711276032 | bytes 15472640 | tf_op jit(solution)/shard_map/pallas_call | solution.py:82
  91.9 0.9 collective-permute-start.23
  92.8 1.5 %collective-permute-start.25 = (bf16[32,512]{1,0:T(8,128)(2,1)S(1)}, bf16[32,512]{1,0:T(8,128)(2,1)S(1)}, u32[]{:S(2)}, u32[]{:S(2)}) collective-permute-start(bf16[32,512]{1,0:T(8,128)(2,1)S(1)} %get-tuple-element.142), channel_id=1, source_target_pairs={{4,0},{0,4},{12,8},{8,12},{5,1},{1,5},{13,9},{9,13},{6,2},{2,6},{1... | collective-permute-start | bytes 98312 | tf_op jit(solution)/shard_map/ppermute | solution.py:400
  94.3 1.5 %shard_map.188.upstream = f32[512,512]{1,0:T(8,128)S(1)} custom-call(f32[512,512]{1,0:T(8,128)S(1)} %get-tuple-element.138.upstream, bf16[2048,512]{1,0:T(8,128)(2,1)S(1)} %get-tuple-element.139.grad_pre, bf16[1024,2048]{1,0:T(8,128)(2,1)S(1)} %get-tuple-element.100.refs_7_.there, bf16[3,512,512]{2,1,0:T(8,128)(2,1)S(1)} %copy-done.2), custom_call_target="tpu_custom_call" | custom-call | flops 1342177280 | bytes 9961472 | tf_op jit(solution)/shard_map/pallas_call | solution.py:82
  95.8 1.4 %collective-permute-done.23.refs_1_ = bf16[32,512]{1,0:T(8,128)(2,1)S(1)} collective-permute-done((bf16[32,512]{1,0:T(8,128)(2,1)S(1)}, bf16[32,512]{1,0:T(8,128)(2,1)S(1)}, u32[]{:S(2)}, u32[]{:S(2)}) %collective-permute-start.23) | collective-permute-done | bytes 32800 | tf_op jit(solution)/shard_map/ppermute | solution.py:537
  97.2 1.5 %shard_map.189.refs_0_ = f32[512,512]{1,0:T(8,128)S(1)} custom-call(f32[512,512]{1,0:T(8,128)S(1)} %shard_map.188.upstream, bf16[2048,512]{1,0:T(8,128)(2,1)S(1)} %get-tuple-element.139.grad_pre, bf16[1024,2048]{1,0:T(8,128)(2,1)S(1)} %get-tuple-element.100.refs_7_.there, bf16[3,512,512]{2,1,0:T(8,128)(2,1)S(1)} %copy-done.3), custom_call_target="tpu_custom_call" | custom-call | flops 1342177280 | bytes 9961472 | tf_op jit(solution)/shard_map/pallas_call | solution.py:82
  98.8 1.4 %shard_map.190 = (bf16[512,512]{1,0:T(8,128)(2,1)S(1)}, bf16[128,512]{1,0:T(8,128)(2,1)S(1)}, bf16[128,512]{1,0:T(8,128)(2,1)S(1)}) custom-call(f32[512,512]{1,0:T(8,128)S(1)} %shard_map.189.refs_0_, bf16[32,512]{1,0:T(8,128)(2,1)S(1)} %collective-permute-done.23.refs_1_, bf16[32,512]{1,0:T(8,128)(2,1)S(1)} %collective-permute-done.24.refs_2_, ...), custom_call_target="tpu_custom_call" | custom-call | flops 503316480 | bytes 5703680 | tf_op jit(solution)/shard_map/pallas_call | solution.py:82
  100.3 2.0 %collective-permute-start.29 = (bf16[128,512]{1,0:T(8,128)(2,1)S(1)}, bf16[128,512]{1,0:T(8,128)(2,1)S(1)}, u32[]{:S(2)}, u32[]{:S(2)}) collective-permute-start(bf16[128,512]{1,0:T(8,128)(2,1)S(1)} %get-tuple-element.159), channel_id=1, source_target_pairs={{4,0},{0,4},{12,8},{8,12},{5,1},{1,5},{13,9},{9,13},{6,2},{2,6},{1... | collective-permute-start | bytes 393224 | tf_op jit(solution)/shard_map/ppermute | solution.py:400
  102.3 0.6 shard_map.191
  102.9 3.7 %collective-permute-done.26.passed = bf16[128,512]{1,0:T(8,128)(2,1)S(1)} collective-permute-done((bf16[128,512]{1,0:T(8,128)(2,1)S(1)}, bf16[128,512]{1,0:T(8,128)(2,1)S(1)}, u32[]{:S(2)}, u32[]{:S(2)}) %collective-permute-start.26) | collective-permute-done | bytes 131104 | tf_op jit(solution)/shard_map/ppermute | solution.py:400
  106.8 2.5 %collective-permute-start.28 = (bf16[128,512]{1,0:T(8,128)(2,1)S(1)}, bf16[128,512]{1,0:T(8,128)(2,1)S(1)}, u32[]{:S(2)}, u32[]{:S(2)}) collective-permute-start(bf16[128,512]{1,0:T(8,128)(2,1)S(1)} %get-tuple-element.158), channel_id=1, source_target_pairs={{8,0},{12,4},{0,8},{4,12},{9,1},{13,5},{1,9},{5,13},{10,2},{14,6},... | collective-permute-start | bytes 393224 | tf_op jit(solution)/shard_map/ppermute | solution.py:400
  109.3 0.7 collective-permute-start.30
  110.1 6.3 %collective-permute-done.28.piece = bf16[128,512]{1,0:T(8,128)(2,1)S(1)} collective-permute-done((bf16[128,512]{1,0:T(8,128)(2,1)S(1)}, bf16[128,512]{1,0:T(8,128)(2,1)S(1)}, u32[]{:S(2)}, u32[]{:S(2)}) %collective-permute-start.28) | collective-permute-done | bytes 131104 | tf_op jit(solution)/shard_map/ppermute | solution.py:400
  116.4 4.7 %collective-permute-done.30.refs_3_ = bf16[128,512]{1,0:T(8,128)(2,1)S(1)} collective-permute-done((bf16[128,512]{1,0:T(8,128)(2,1)S(1)}, bf16[128,512]{1,0:T(8,128)(2,1)S(1)}, u32[]{:S(2)}, u32[]{:S(2)}) %collective-permute-start.30) | collective-permute-done | bytes 131104 | tf_op jit(solution)/shard_map/ppermute | solution.py:400
  121.1 1.3 %shard_map.195 = f32[256,512]{1,0:T(8,128)} custom-call(bf16[256,512]{1,0:T(8,128)(2,1)S(1)} %get-tuple-element.153.own.refs_0_, bf16[256,512]{1,0:T(8,128)(2,1)S(1)} %collective-permute-done.27.refs_1_, f32[128,512]{1,0:T(8,128)S(1)} %shard_map.193.refs_2_, bf16[128,512]{1,0:T(8,128)(2,1)S(1)} %collective-permute-done.30.refs_3_, bf16[512,512]{1,0:T(8,128)(2,1)S(1)} %copy-done.5), custom_call_target="tpu_custom_call" | custom-call | flops 134217728 | bytes 1966080 | tf_op jit(solution)/shard_map/pallas_call | solution.py:82
  (77 shorter events, 2.0 us)
Async XLA Ops:
  0.6 8.2 %copy-start = (s32[1,4,32]{2,1,0:T(4,128)S(1)}, s32[1,4,32]{2,1,0:T(4,128)}, u32[]{:S(2)}) copy-start(s32[1,4,32]{2,1,0:T(4,128)} %param.22) | copy-start | bytes 1540
  1.7 18.6 %collective-permute-start.3 = (bf16[272,512]{1,0:T(8,128)(2,1)S(1)}, bf16[272,512]{1,0:T(8,128)(2,1)S(1)}, u32[]{:S(2)}, u32[]{:S(2)}) collective-permute-start(bf16[272,512]{1,0:T(8,128)(2,1)S(1)} %shard_map.167.refs_5_), channel_id=1, source_target_pairs={{0,4},{4,0},{8,12},{12,8},{1,5},{5,1},{9,13},{13,9},{2,6},{6,2},{1... | collective-permute-start | bytes 835592 | tf_op jit(solution)/shard_map/ppermute | solution.py:395
  4.8 15.0 %collective-permute-start = (bf16[272,512]{1,0:T(8,128)(2,1)S(1)}, bf16[272,512]{1,0:T(8,128)(2,1)S(1)}, u32[]{:S(2)}, u32[]{:S(2)}) collective-permute-start(bf16[272,512]{1,0:T(8,128)(2,1)S(1)} %shard_map.167.refs_5_), channel_id=1, source_target_pairs={{0,8},{4,12},{8,0},{12,4},{1,9},{5,13},{9,1},{13,5},{2,10},{6,14},... | collective-permute-start | bytes 835592 | tf_op jit(solution)/shard_map/ppermute | solution.py:395
  8.7 1.2 collective-permute-start.1
  10.1 3.7 %collective-permute-start.2 = (s32[2,2,512]{2,0,1:T(2,128)S(1)}, s32[2,2,512]{2,0,1:T(2,128)S(1)}, u32[]{:S(2)}, u32[]{:S(2)}) collective-permute-start(s32[2,2,512]{2,0,1:T(2,128)S(1)} %fusion.1), channel_id=1, source_target_pairs={{0,2},{2,0},{1,3},{3,1},{4,6},{6,4},{5,7},{7,5},{8,10},{10,8},{9,1... | collective-permute-start | bytes 24584 | tf_op jit(solution)/shard_map/ppermute | solution.py:386
  14.0 6.4 %copy-start.5 = (bf16[512,512]{1,0:T(8,128)(2,1)S(1)}, bf16[512,512]{1,0:T(8,128)(2,1)}, u32[]{:S(2)}) copy-start(bf16[512,512]{1,0:T(8,128)(2,1)} %refs_4_.3) | copy-start | bytes 1572868
  14.0 6.4 %copy-start.8 = (bf16[512,512]{1,0:T(8,128)(2,1)S(1)}, bf16[512,512]{1,0:T(8,128)(2,1)}, u32[]{:S(2)}) copy-start(bf16[512,512]{1,0:T(8,128)(2,1)} %refs_3_.3) | copy-start | bytes 1572868
  14.0 6.4 %copy-start.11 = (bf16[512,512]{1,0:T(8,128)(2,1)S(1)}, bf16[512,512]{1,0:T(8,128)(2,1)}, u32[]{:S(2)}) copy-start(bf16[512,512]{1,0:T(8,128)(2,1)} %refs_3_.2) | copy-start | bytes 1572868
  19.8 6.5 %collective-permute-start.4 = (bf16[272,512]{1,0:T(8,128)(2,1)S(1)}, bf16[272,512]{1,0:T(8,128)(2,1)S(1)}, u32[]{:S(2)}, u32[]{:S(2)}) collective-permute-start(bf16[272,512]{1,0:T(8,128)(2,1)S(1)} %collective-permute-done.refs_4_), channel_id=1, source_target_pairs={{0,4},{4,0},{8,12},{12,8},{1,5},{5,1},{9,13},{13,9},{2,6},{6,2},{1... | collective-permute-start | bytes 835592 | tf_op jit(solution)/shard_map/ppermute | solution.py:395
  26.3 12.7 %copy-start.2 = (bf16[3,512,512]{2,1,0:T(8,128)(2,1)S(1)}, bf16[3,512,512]{2,1,0:T(8,128)(2,1)}, u32[]{:S(2)}) copy-start(bf16[3,512,512]{2,1,0:T(8,128)(2,1)} %refs_5_.5) | copy-start | bytes 4718596
  26.3 12.7 %copy-start.7 = (bf16[512,512]{1,0:T(8,128)(2,1)S(1)}, bf16[512,512]{1,0:T(8,128)(2,1)}, u32[]{:S(2)}) copy-start(bf16[512,512]{1,0:T(8,128)(2,1)} %refs_8_.11) | copy-start | bytes 1572868
  26.3 12.7 %copy-start.10 = (f32[512]{0:T(512)S(1)}, f32[512]{0:T(512)}, u32[]{:S(2)}) copy-start(f32[512]{0:T(512)} %param.26) | copy-start | bytes 6148
  27.3 1.6 %collective-permute-start.5 = (bf16[256,512]{1,0:T(8,128)(2,1)S(1)}, bf16[256,512]{1,0:T(8,128)(2,1)S(1)}, u32[]{:S(2)}, u32[]{:S(2)}) collective-permute-start(bf16[256,512]{1,0:T(8,128)(2,1)S(1)} %get-tuple-element.88), channel_id=1, source_target_pairs={{0,1},{1,0},{2,3},{3,2},{4,5},{5,4},{6,7},{7,6},{8,9},{9,8},{10,11... | collective-permute-start | bytes 786440 | tf_op jit(solution)/shard_map/ppermute | solution.py:386
  29.0 14.3 %copy-start.3 = (bf16[3,512,512]{2,1,0:T(8,128)(2,1)S(1)}, bf16[3,512,512]{2,1,0:T(8,128)(2,1)}, u32[]{:S(2)}) copy-start(bf16[3,512,512]{2,1,0:T(8,128)(2,1)} %weights.11) | copy-start | bytes 4718596
  29.0 8.4 %collective-permute-start.6 = (bf16[256,512]{1,0:T(8,128)(2,1)S(1)}, bf16[256,512]{1,0:T(8,128)(2,1)S(1)}, u32[]{:S(2)}, u32[]{:S(2)}) collective-permute-start(bf16[256,512]{1,0:T(8,128)(2,1)S(1)} %add_convert_fusion.1), channel_id=1, source_target_pairs={{0,2},{2,0},{1,3},{3,1},{4,6},{6,4},{5,7},{7,5},{8,10},{10,8},{9,1... | collective-permute-start | bytes 786440 | tf_op jit(solution)/shard_map/ppermute | solution.py:386
  37.4 1.6 %collective-permute-start.7 = (bf16[256,512]{1,0:T(8,128)(2,1)S(1)}, bf16[256,512]{1,0:T(8,128)(2,1)S(1)}, u32[]{:S(2)}, u32[]{:S(2)}) collective-permute-start(bf16[256,512]{1,0:T(8,128)(2,1)S(1)} %add_convert_fusion.refs_1_), channel_id=1, source_target_pairs={{0,1},{1,0},{2,3},{3,2},{4,5},{5,4},{6,7},{7,6},{8,9},{9,8},{10,11... | collective-permute-start | bytes 786440 | tf_op jit(solution)/shard_map/ppermute | solution.py:386
  40.1 5.3 %collective-permute-start.8 = (bf16[32,512]{1,0:T(8,128)(2,1)S(1)}, bf16[32,512]{1,0:T(8,128)(2,1)S(1)}, u32[]{:S(2)}, u32[]{:S(2)}) collective-permute-start(bf16[32,512]{1,0:T(8,128)(2,1)S(1)} %get-tuple-element.90), channel_id=1, source_target_pairs={{0,8},{1,13},{4,12},{5,9},{8,0},{9,5},{12,4},{13,1},{2,10},{3,15},... | collective-permute-start | bytes 98312 | tf_op jit(solution)/shard_map/ppermute | solution.py:537
  41.4 5.2 %collective-permute-start.10 = (bf16[32,512]{1,0:T(8,128)(2,1)S(1)}, bf16[32,512]{1,0:T(8,128)(2,1)S(1)}, u32[]{:S(2)}, u32[]{:S(2)}) collective-permute-start(bf16[32,512]{1,0:T(8,128)(2,1)S(1)} %get-tuple-element.98), channel_id=1, source_target_pairs={{0,4},{4,0},{8,12},{12,8},{1,5},{5,1},{9,13},{13,9},{2,6},{6,2},{1... | collective-permute-start | bytes 98312 | tf_op jit(solution)/shard_map/ppermute | solution.py:395
  45.3 1.4 %copy-start.4 = (bf16[3,512,512]{2,1,0:T(8,128)(2,1)S(1)}, bf16[3,512,512]{2,1,0:T(8,128)(2,1)}, u32[]{:S(2)}) copy-start(bf16[3,512,512]{2,1,0:T(8,128)(2,1)} %refs_9_.9) | copy-start | bytes 4718596
  45.3 1.4 %copy-start.9 = (f32[3,512]{1,0:T(4,128)S(1)}, f32[3,512]{1,0:T(4,128)}, u32[]{:S(2)}) copy-start(f32[3,512]{1,0:T(4,128)} %refs_8_.10) | copy-start | bytes 18436
  45.3 1.3 %collective-permute-start.9 = (bf16[32,512]{1,0:T(8,128)(2,1)S(1)}, bf16[32,512]{1,0:T(8,128)(2,1)S(1)}, u32[]{:S(2)}, u32[]{:S(2)}) collective-permute-start(bf16[32,512]{1,0:T(8,128)(2,1)S(1)} %collective-permute-done.8.refs_3_), channel_id=1, source_target_pairs={{0,1},{1,0},{2,3},{3,2},{4,5},{5,4},{6,7},{7,6},{8,9},{9,8},{10,11... | collective-permute-start | bytes 98312 | tf_op jit(solution)/shard_map/ppermute | solution.py:386
  50.0 4.9 %collective-permute-start.11 = (bf16[32,512]{1,0:T(8,128)(2,1)S(1)}, bf16[32,512]{1,0:T(8,128)(2,1)S(1)}, u32[]{:S(2)}, u32[]{:S(2)}) collective-permute-start(bf16[32,512]{1,0:T(8,128)(2,1)S(1)} %get-tuple-element.102), channel_id=1, source_target_pairs={{0,8},{1,13},{4,12},{5,9},{8,0},{9,5},{12,4},{13,1},{2,10},{3,15},... | collective-permute-start | bytes 98312 | tf_op jit(solution)/shard_map/ppermute | solution.py:537
  50.9 5.6 %collective-permute-start.13 = (bf16[32,512]{1,0:T(8,128)(2,1)S(1)}, bf16[32,512]{1,0:T(8,128)(2,1)S(1)}, u32[]{:S(2)}, u32[]{:S(2)}) collective-permute-start(bf16[32,512]{1,0:T(8,128)(2,1)S(1)} %get-tuple-element.109), channel_id=1, source_target_pairs={{0,4},{4,0},{8,12},{12,8},{1,5},{5,1},{9,13},{13,9},{2,6},{6,2},{1... | collective-permute-start | bytes 98312 | tf_op jit(solution)/shard_map/ppermute | solution.py:395
  54.9 1.7 %collective-permute-start.12 = (bf16[32,512]{1,0:T(8,128)(2,1)S(1)}, bf16[32,512]{1,0:T(8,128)(2,1)S(1)}, u32[]{:S(2)}, u32[]{:S(2)}) collective-permute-start(bf16[32,512]{1,0:T(8,128)(2,1)S(1)} %collective-permute-done.11.refs_3_), channel_id=1, source_target_pairs={{0,1},{1,0},{2,3},{3,2},{4,5},{5,4},{6,7},{7,6},{8,9},{9,8},{10,11... | collective-permute-start | bytes 98312 | tf_op jit(solution)/shard_map/ppermute | solution.py:386
  60.1 5.6 %collective-permute-start.14 = (bf16[32,512]{1,0:T(8,128)(2,1)S(1)}, bf16[32,512]{1,0:T(8,128)(2,1)S(1)}, u32[]{:S(2)}, u32[]{:S(2)}) collective-permute-start(bf16[32,512]{1,0:T(8,128)(2,1)S(1)} %get-tuple-element.111), channel_id=1, source_target_pairs={{0,8},{1,13},{4,12},{5,9},{8,0},{9,5},{12,4},{13,1},{2,10},{3,15},... | collective-permute-start | bytes 98312 | tf_op jit(solution)/shard_map/ppermute | solution.py:537
  60.7 6.2 %collective-permute-start.16 = (bf16[32,512]{1,0:T(8,128)(2,1)S(1)}, bf16[32,512]{1,0:T(8,128)(2,1)S(1)}, u32[]{:S(2)}, u32[]{:S(2)}) collective-permute-start(bf16[32,512]{1,0:T(8,128)(2,1)S(1)} %get-tuple-element.118), channel_id=1, source_target_pairs={{0,4},{4,0},{8,12},{12,8},{1,5},{5,1},{9,13},{13,9},{2,6},{6,2},{1... | collective-permute-start | bytes 98312 | tf_op jit(solution)/shard_map/ppermute | solution.py:395
  65.7 1.3 %copy-start.6 = (bf16[512,512]{1,0:T(8,128)(2,1)S(1)}, bf16[512,512]{1,0:T(8,128)(2,1)}, u32[]{:S(2)}) copy-start(bf16[512,512]{1,0:T(8,128)(2,1)} %upstream.1) | copy-start | bytes 1572868
  65.7 1.3 %collective-permute-start.15 = (bf16[32,512]{1,0:T(8,128)(2,1)S(1)}, bf16[32,512]{1,0:T(8,128)(2,1)S(1)}, u32[]{:S(2)}, u32[]{:S(2)}) collective-permute-start(bf16[32,512]{1,0:T(8,128)(2,1)S(1)} %collective-permute-done.14.refs_3_), channel_id=1, source_target_pairs={{0,1},{1,0},{2,3},{3,2},{4,5},{5,4},{6,7},{7,6},{8,9},{9,8},{10,11... | collective-permute-start | bytes 98312 | tf_op jit(solution)/shard_map/ppermute | solution.py:386
  72.6 5.6 %collective-permute-start.17 = (bf16[32,512]{1,0:T(8,128)(2,1)S(1)}, bf16[32,512]{1,0:T(8,128)(2,1)S(1)}, u32[]{:S(2)}, u32[]{:S(2)}) collective-permute-start(bf16[32,512]{1,0:T(8,128)(2,1)S(1)} %get-tuple-element.121), channel_id=1, source_target_pairs={{0,8},{1,13},{4,12},{5,9},{8,0},{9,5},{12,4},{13,1},{2,10},{3,15},... | collective-permute-start | bytes 98312 | tf_op jit(solution)/shard_map/ppermute | solution.py:537
  72.7 7.1 %collective-permute-start.19 = (bf16[32,512]{1,0:T(8,128)(2,1)S(1)}, bf16[32,512]{1,0:T(8,128)(2,1)S(1)}, u32[]{:S(2)}, u32[]{:S(2)}) collective-permute-start(bf16[32,512]{1,0:T(8,128)(2,1)S(1)} %get-tuple-element.125), channel_id=1, source_target_pairs={{4,0},{0,4},{12,8},{8,12},{5,1},{1,5},{13,9},{9,13},{6,2},{2,6},{1... | collective-permute-start | bytes 98312 | tf_op jit(solution)/shard_map/ppermute | solution.py:400
  78.2 1.5 %collective-permute-start.18 = (bf16[32,512]{1,0:T(8,128)(2,1)S(1)}, bf16[32,512]{1,0:T(8,128)(2,1)S(1)}, u32[]{:S(2)}, u32[]{:S(2)}) collective-permute-start(bf16[32,512]{1,0:T(8,128)(2,1)S(1)} %collective-permute-done.17.refs_1_), channel_id=1, source_target_pairs={{0,1},{1,0},{2,3},{3,2},{4,5},{5,4},{6,7},{7,6},{8,9},{9,8},{10,11... | collective-permute-start | bytes 98312 | tf_op jit(solution)/shard_map/ppermute | solution.py:386
  82.3 5.0 %collective-permute-start.20 = (bf16[32,512]{1,0:T(8,128)(2,1)S(1)}, bf16[32,512]{1,0:T(8,128)(2,1)S(1)}, u32[]{:S(2)}, u32[]{:S(2)}) collective-permute-start(bf16[32,512]{1,0:T(8,128)(2,1)S(1)} %get-tuple-element.129), channel_id=1, source_target_pairs={{0,8},{1,13},{4,12},{5,9},{8,0},{9,5},{12,4},{13,1},{2,10},{3,15},... | collective-permute-start | bytes 98312 | tf_op jit(solution)/shard_map/ppermute | solution.py:537
  82.7 6.6 %collective-permute-start.22 = (bf16[32,512]{1,0:T(8,128)(2,1)S(1)}, bf16[32,512]{1,0:T(8,128)(2,1)S(1)}, u32[]{:S(2)}, u32[]{:S(2)}) collective-permute-start(bf16[32,512]{1,0:T(8,128)(2,1)S(1)} %get-tuple-element.134), channel_id=1, source_target_pairs={{4,0},{0,4},{12,8},{8,12},{5,1},{1,5},{13,9},{9,13},{6,2},{2,6},{1... | collective-permute-start | bytes 98312 | tf_op jit(solution)/shard_map/ppermute | solution.py:400
  87.3 2.0 %collective-permute-start.21 = (bf16[32,512]{1,0:T(8,128)(2,1)S(1)}, bf16[32,512]{1,0:T(8,128)(2,1)S(1)}, u32[]{:S(2)}, u32[]{:S(2)}) collective-permute-start(bf16[32,512]{1,0:T(8,128)(2,1)S(1)} %collective-permute-done.20.refs_1_), channel_id=1, source_target_pairs={{0,1},{1,0},{2,3},{3,2},{4,5},{5,4},{6,7},{7,6},{8,9},{9,8},{10,11... | collective-permute-start | bytes 98312 | tf_op jit(solution)/shard_map/ppermute | solution.py:386
  91.9 5.3 %collective-permute-start.23 = (bf16[32,512]{1,0:T(8,128)(2,1)S(1)}, bf16[32,512]{1,0:T(8,128)(2,1)S(1)}, u32[]{:S(2)}, u32[]{:S(2)}) collective-permute-start(bf16[32,512]{1,0:T(8,128)(2,1)S(1)} %get-tuple-element.137), channel_id=1, source_target_pairs={{0,8},{1,13},{4,12},{5,9},{8,0},{9,5},{12,4},{13,1},{2,10},{3,15},... | collective-permute-start | bytes 98312 | tf_op jit(solution)/shard_map/ppermute | solution.py:537
  92.8 6.0 %collective-permute-start.25 = (bf16[32,512]{1,0:T(8,128)(2,1)S(1)}, bf16[32,512]{1,0:T(8,128)(2,1)S(1)}, u32[]{:S(2)}, u32[]{:S(2)}) collective-permute-start(bf16[32,512]{1,0:T(8,128)(2,1)S(1)} %get-tuple-element.142), channel_id=1, source_target_pairs={{4,0},{0,4},{12,8},{8,12},{5,1},{1,5},{13,9},{9,13},{6,2},{2,6},{1... | collective-permute-start | bytes 98312 | tf_op jit(solution)/shard_map/ppermute | solution.py:400
  97.2 1.5 %collective-permute-start.24 = (bf16[32,512]{1,0:T(8,128)(2,1)S(1)}, bf16[32,512]{1,0:T(8,128)(2,1)S(1)}, u32[]{:S(2)}, u32[]{:S(2)}) collective-permute-start(bf16[32,512]{1,0:T(8,128)(2,1)S(1)} %collective-permute-done.23.refs_1_), channel_id=1, source_target_pairs={{0,1},{1,0},{2,3},{3,2},{4,5},{5,4},{6,7},{7,6},{8,9},{9,8},{10,11... | collective-permute-start | bytes 98312 | tf_op jit(solution)/shard_map/ppermute | solution.py:386
  100.2 6.4 %collective-permute-start.26 = (bf16[128,512]{1,0:T(8,128)(2,1)S(1)}, bf16[128,512]{1,0:T(8,128)(2,1)S(1)}, u32[]{:S(2)}, u32[]{:S(2)}) collective-permute-start(bf16[128,512]{1,0:T(8,128)(2,1)S(1)} %get-tuple-element.155), channel_id=1, source_target_pairs={{4,0},{0,4},{12,8},{8,12},{5,1},{1,5},{13,9},{9,13},{6,2},{2,6},{1... | collective-permute-start | bytes 393224 | tf_op jit(solution)/shard_map/ppermute | solution.py:400
  100.3 9.0 %collective-permute-start.29 = (bf16[128,512]{1,0:T(8,128)(2,1)S(1)}, bf16[128,512]{1,0:T(8,128)(2,1)S(1)}, u32[]{:S(2)}, u32[]{:S(2)}) collective-permute-start(bf16[128,512]{1,0:T(8,128)(2,1)S(1)} %get-tuple-element.159), channel_id=1, source_target_pairs={{4,0},{0,4},{12,8},{8,12},{5,1},{1,5},{13,9},{9,13},{6,2},{2,6},{1... | collective-permute-start | bytes 393224 | tf_op jit(solution)/shard_map/ppermute | solution.py:400
  102.3 20.1 %copy-start.1 = (s32[1,4,32]{2,1,0:T(4,128)S(1)}, s32[1,4,32]{2,1,0:T(4,128)}, u32[]{:S(2)}) copy-start(s32[1,4,32]{2,1,0:T(4,128)} %param.22) | copy-start | bytes 1540
  106.6 14.5 %collective-permute-start.27 = (bf16[256,512]{1,0:T(8,128)(2,1)S(1)}, bf16[256,512]{1,0:T(8,128)(2,1)S(1)}, u32[]{:S(2)}, u32[]{:S(2)}) collective-permute-start(bf16[256,512]{1,0:T(8,128)(2,1)S(1)} %get-tuple-element.157), channel_id=1, source_target_pairs={{4,0},{0,4},{12,8},{8,12},{5,1},{1,5},{13,9},{9,13},{6,2},{2,6},{1... | collective-permute-start | bytes 786440 | tf_op jit(solution)/shard_map/ppermute | solution.py:400
  106.8 9.6 %collective-permute-start.28 = (bf16[128,512]{1,0:T(8,128)(2,1)S(1)}, bf16[128,512]{1,0:T(8,128)(2,1)S(1)}, u32[]{:S(2)}, u32[]{:S(2)}) collective-permute-start(bf16[128,512]{1,0:T(8,128)(2,1)S(1)} %get-tuple-element.158), channel_id=1, source_target_pairs={{8,0},{12,4},{0,8},{4,12},{9,1},{13,5},{1,9},{5,13},{10,2},{14,6},... | collective-permute-start | bytes 393224 | tf_op jit(solution)/shard_map/ppermute | solution.py:400
  109.3 11.7 %collective-permute-start.30 = (bf16[128,512]{1,0:T(8,128)(2,1)S(1)}, bf16[128,512]{1,0:T(8,128)(2,1)S(1)}, u32[]{:S(2)}, u32[]{:S(2)}) collective-permute-start(bf16[128,512]{1,0:T(8,128)(2,1)S(1)} %shard_map.194), channel_id=1, source_target_pairs={{8,0},{12,4},{0,8},{4,12},{9,1},{13,5},{1,9},{5,13},{10,2},{14,6},... | collective-permute-start | bytes 393224 | tf_op jit(solution)/shard_map/ppermute | solution.py:400

commit v10 on v9

--- a/solution.py
+++ b/solution.py
@@ -38,10 +38,11 @@
     return lax.dot_general(left, right, (((1,), (1,)), ((), ())), preferred_element_type=f32)
 
 
-def gated(pre):
-    sigma = 0.5 * jnp.tanh(0.5 * pre) + 0.5
-    act = pre * sigma
-    return act, sigma + act * (1.0 - sigma)
+def gated(half):
+    half = half.astype(bf16)
+    bend = jnp.tanh(half)
+    act = half + half * bend
+    return act, (1.0 + act) + bend * (1.0 - act)
 
 
 def as_mask(hit):
@@ -169,7 +170,7 @@
         picked = pick_rows(column, 0, nodes)
         pick[...] = picked
         pre = dot(payload[0:grid, :], w_grid[...]) + dot(picked, projected)
-        act, slope = gated(pre)
+        act, slope = gated(0.5 * pre)
         slope_out[...] = slope.astype(bf16)
         added = dot(pick_columns(target, 0, nodes), act.astype(bf16))
         total = added if total is None else total + added
@@ -220,7 +221,7 @@
     enc_sum_out[...] = enc_sum
     hidden = (mesh_init[...].astype(f32) + enc_sum * norm_scale(enc_sum) * gain[...]).astype(bf16)
     hidden_out[...] = hidden
-    projected = dot(hidden, w_send[0]).astype(bf16)
+    projected = (0.5 * dot(hidden, w_send[0])).astype(bf16)
     sent[...] = projected
     hand_out(dot(list_here[...], projected), outs)
 
@@ -228,7 +229,7 @@
 def local_kernel(layer, hidden, sent, here, w_recv, pre, table):
     nodes = hidden.shape[0]
     table[0:nodes, :] = sent[...]
-    table[nodes:, :] = dot(hidden[...], w_recv[layer]).astype(bf16)
+    table[nodes:, :] = (0.5 * dot(hidden[...], w_recv[layer])).astype(bf16)
     for at in range(0, pre.shape[0], BLOCK):
         pre[at : at + BLOCK, :] = dot(here[at : at + BLOCK, :], table[...])
 
@@ -272,14 +273,14 @@
     agg_out[...] = agg
     fresh = (hidden[...].astype(f32) + agg * norm_scale(agg) * gain[layer : layer + 1, :]).astype(bf16)
     hidden_out[...] = fresh
-    projected = dot(fresh, w_send[layer + 1]).astype(bf16)
+    projected = (0.5 * dot(fresh, w_send[layer + 1])).astype(bf16)
     sent_out[...] = projected
     hand_out(dot(list_here[...], projected), outs)
 
 
 def edge_grads(listed, grad_agg, w_out, here, halo_there, slope, grad_pre, outs):
     nodes = grad_agg.shape[0]
-    spread = dot_back(grad_agg.astype(bf16), w_out).astype(bf16)
+    spread = (0.5 * dot_back(grad_agg.astype(bf16), w_out)).astype(bf16)
     for at in range(0, slope.shape[0], BLOCK):
         block = slice(at, at + BLOCK)
         grad_act = dot(here[block, nodes:], spread)
@@ -336,7 +337,7 @@
     list_there, w_send, enc_sum, gain, w_enc_out, pick, slope, spread_out = refs[:8]
     outs, halo = refs[8:-1], refs[-1]
     upstream = arrived(rest, returned, list_there, w_send[0], halo)
-    spread = dot_back(norm_back(enc_sum[...], gain[...], upstream).astype(bf16), w_enc_out[...]).astype(bf16)
+    spread = (0.5 * dot_back(norm_back(enc_sum[...], gain[...], upstream).astype(bf16), w_enc_out[...])).astype(bf16)
     spread_out[...] = spread
     at = 0
     for out in outs:

time: 123 us -> 121 us (0.984)
  Pallas kernels: 47.5 us -> 45.6 us
    pallas_call x29, Pallas kernels: 47.5 us -> 45.6 us  [run(): pl.pallas_call(body, out_shape=tuple((jax.ShapeDtypeStruct(shape, dtype)...]
where the time goes in v10:
time: 121 us; the launch traced here: 120 us
  Pallas kernels  45.6 us (38%)
  waiting for transfers between devices  38.5 us (32%)
  starting transfers between devices  32.3 us (27%)
  other arithmetic  1.82 us (2%)
    pallas_call x29, Pallas kernels, run(): pl.pallas_call(body, out_shape=tuple((jax.ShapeDtypeStruct(shape, dtype)...  45.6 us
    ppermute x8, waiting for transfers between devices, sent_back(): lax.ppermute(value, 'mesh', [(partner(at, step, size), at) for at in rang...  14.7 us
    ppermute x6, starting transfers between devices, sent_to(): lax.ppermute(value, 'mesh', [(at, partner(at, step, size)) for at in rang...  12.7 us
    ppermute x11, waiting for transfers between devices, shifted(): lax.ppermute(value, axis, [(at, (at + by) % size) for at in range(size)])  12.4 us
    ppermute x8, starting transfers between devices, sent_back(): lax.ppermute(value, 'mesh', [(partner(at, step, size), at) for at in rang...  11.2 us
    ppermute x6, waiting for transfers between devices, sent_to(): lax.ppermute(value, 'mesh', [(at, partner(at, step, size)) for at in rang...  5.84 us
    ppermute x6, waiting for transfers between devices, exchange(): lax.ppermute(blocks[0], ('mesh', 'rep'), [(2 * at + side, 2 * (at ^ 2 + s...  5.56 us
    ppermute x6, starting transfers between devices, exchange(): lax.ppermute(blocks[0], ('mesh', 'rep'), [(2 * at + side, 2 * (at ^ 2 + s...  4.36 us
  transfers between devices with their start and end apart: 31, of which 16 were waited for; matrix products, arithmetic and copies ran while one was open for 2% of the time, Pallas kernels for 20%

profile of v10, /device:TPU:0, one launch (start us, length us, event | category | flops | bytes accessed | tf_op | source)
XLA Modules:
  0.0 120.4 jit_solution(2232225519984008139)
XLA Ops:
  0.6 1.0 shard_map.167.refs_5_
  1.7 3.1 %collective-permute-start.3 = (bf16[272,512]{1,0:T(8,128)(2,1)S(1)}, bf16[272,512]{1,0:T(8,128)(2,1)S(1)}, u32[]{:S(2)}, u32[]{:S(2)}) collective-permute-start(bf16[272,512]{1,0:T(8,128)(2,1)S(1)} %shard_map.167.refs_5_), channel_id=1, source_target_pairs={{0,4},{4,0},{8,12},{12,8},{1,5},{5,1},{9,13},{13,9},{2,6},{6,2},{1... | collective-permute-start | bytes 835592 | tf_op jit(solution)/shard_map/ppermute | solution.py:396
  4.8 2.6 %collective-permute-start = (bf16[272,512]{1,0:T(8,128)(2,1)S(1)}, bf16[272,512]{1,0:T(8,128)(2,1)S(1)}, u32[]{:S(2)}, u32[]{:S(2)}) collective-permute-start(bf16[272,512]{1,0:T(8,128)(2,1)S(1)} %shard_map.167.refs_5_), channel_id=1, source_target_pairs={{0,8},{4,12},{8,0},{12,4},{1,9},{5,13},{9,1},{13,5},{2,10},{6,14},... | collective-permute-start | bytes 835592 | tf_op jit(solution)/shard_map/ppermute | solution.py:396
  7.3 0.7 compare_select_fusion.1
  8.0 0.7 fusion.11
  8.8 0.6 gather_fusion
  9.5 0.4 collective-permute-done.1
  10.1 1.6 %collective-permute-start.2 = (s32[2,2,512]{2,0,1:T(2,128)S(1)}, s32[2,2,512]{2,0,1:T(2,128)S(1)}, u32[]{:S(2)}, u32[]{:S(2)}) collective-permute-start(s32[2,2,512]{2,0,1:T(2,128)S(1)} %fusion.1), channel_id=1, source_target_pairs={{0,2},{2,0},{1,3},{3,1},{4,6},{6,4},{5,7},{7,5},{8,10},{10,8},{9,1... | collective-permute-start | bytes 24584 | tf_op jit(solution)/shard_map/ppermute | solution.py:387
  11.7 2.1 %collective-permute-done.2 = s32[2,2,512]{2,0,1:T(2,128)S(1)} collective-permute-done((s32[2,2,512]{2,0,1:T(2,128)S(1)}, s32[2,2,512]{2,0,1:T(2,128)S(1)}, u32[]{:S(2)}, u32[]{:S(2)}) %collective-permute-start.2) | collective-permute-done | bytes 8224 | tf_op jit(solution)/shard_map/ppermute | solution.py:387
  14.0 3.5 %shard_map.168 = (bf16[2048,1024]{1,0:T(8,128)(2,1)S(1)}, bf16[1024,2048]{1,0:T(8,128)(2,1)S(1)}, bf16[2048,128]{1,0:T(8,128)(2,1)S(1)}, bf16[128,2048]{1,0:T(8,...) custom-call(s32[1,2048]{1,0:T(1,128)S(1)} %fusion.2.slots, s32[1,2048]{1,0:T(1,128)S(1)} %bitcast.26, ...), custom_call_target="tpu_custom_call" | custom-call | flops 3221225472 | bytes 9650560 | tf_op jit(solution)/shard_map/pallas_call | solution.py:83
  17.5 2.3 %collective-permute-done.refs_4_ = bf16[272,512]{1,0:T(8,128)(2,1)S(1)} collective-permute-done((bf16[272,512]{1,0:T(8,128)(2,1)S(1)}, bf16[272,512]{1,0:T(8,128)(2,1)S(1)}, u32[]{:S(2)}, u32[]{:S(2)}) %collective-permute-start) | collective-permute-done | bytes 278560 | tf_op jit(solution)/shard_map/ppermute | solution.py:396
  19.8 0.4 collective-permute-start.4
  20.4 1.6 %shard_map.169 = (bf16[256,512]{1,0:T(8,128)(2,1)S(1)}, bf16[256,512]{1,0:T(8,128)(2,1)S(1)}, bf16[256,512]{1,0:T(8,128)(2,1)S(1)}, bf16[256,512]{1,0:T(8,128)(2...) custom-call(s32[2,512]{1,0:T(2,128)S(1)} %broadcast_in_dim.27.refs_0_, bf16[512,512]{1,0:T(8,128)(2,1)S(1)} %copy-done.8, ...), custom_call_target="tpu_custom_call" | custom-call | flops 1073741824 | bytes 4853760 | tf_op jit(solution)/shard_map/pallas_call | solution.py:83
  22.0 0.8 shard_map.170
  22.8 3.5 %collective-permute-done.4.refs_4_ = bf16[272,512]{1,0:T(8,128)(2,1)S(1)} collective-permute-done((bf16[272,512]{1,0:T(8,128)(2,1)S(1)}, bf16[272,512]{1,0:T(8,128)(2,1)S(1)}, u32[]{:S(2)}, u32[]{:S(2)}) %collective-permute-start.4) | collective-permute-done | bytes 278560 | tf_op jit(solution)/shard_map/ppermute | solution.py:396
  26.3 0.8 shard_map.171
  27.3 1.5 %collective-permute-done.5 = bf16[256,512]{1,0:T(8,128)(2,1)S(1)} collective-permute-done((bf16[256,512]{1,0:T(8,128)(2,1)S(1)}, bf16[256,512]{1,0:T(8,128)(2,1)S(1)}, u32[]{:S(2)}, u32[]{:S(2)}) %collective-permute-start.5) | collective-permute-done | bytes 262176 | tf_op jit(solution)/shard_map/ppermute | solution.py:387
  28.9 1.6 %collective-permute-start.6 = (bf16[256,512]{1,0:T(8,128)(2,1)S(1)}, bf16[256,512]{1,0:T(8,128)(2,1)S(1)}, u32[]{:S(2)}, u32[]{:S(2)}) collective-permute-start(bf16[256,512]{1,0:T(8,128)(2,1)S(1)} %add_convert_fusion.1), channel_id=1, source_target_pairs={{0,2},{2,0},{1,3},{3,1},{4,6},{6,4},{5,7},{7,5},{8,10},{10,8},{9,1... | collective-permute-start | bytes 786440 | tf_op jit(solution)/shard_map/ppermute | solution.py:387
  30.4 6.9 %collective-permute-done.6 = bf16[256,512]{1,0:T(8,128)(2,1)S(1)} collective-permute-done((bf16[256,512]{1,0:T(8,128)(2,1)S(1)}, bf16[256,512]{1,0:T(8,128)(2,1)S(1)}, u32[]{:S(2)}, u32[]{:S(2)}) %collective-permute-start.6) | collective-permute-done | bytes 262176 | tf_op jit(solution)/shard_map/ppermute | solution.py:387
  37.5 1.5 %collective-permute-done.7.refs_2_ = bf16[256,512]{1,0:T(8,128)(2,1)S(1)} collective-permute-done((bf16[256,512]{1,0:T(8,128)(2,1)S(1)}, bf16[256,512]{1,0:T(8,128)(2,1)S(1)}, u32[]{:S(2)}, u32[]{:S(2)}) %collective-permute-start.7) | collective-permute-done | bytes 262176 | tf_op jit(solution)/shard_map/ppermute | solution.py:387
  39.0 1.0 shard_map.172
  40.0 1.3 %collective-permute-start.8 = (bf16[32,512]{1,0:T(8,128)(2,1)S(1)}, bf16[32,512]{1,0:T(8,128)(2,1)S(1)}, u32[]{:S(2)}, u32[]{:S(2)}) collective-permute-start(bf16[32,512]{1,0:T(8,128)(2,1)S(1)} %get-tuple-element.90), channel_id=1, source_target_pairs={{0,8},{1,13},{4,12},{5,9},{8,0},{9,5},{12,4},{13,1},{2,10},{3,15},... | collective-permute-start | bytes 98312 | tf_op jit(solution)/shard_map/ppermute | solution.py:538
  41.3 1.9 %collective-permute-start.10 = (bf16[32,512]{1,0:T(8,128)(2,1)S(1)}, bf16[32,512]{1,0:T(8,128)(2,1)S(1)}, u32[]{:S(2)}, u32[]{:S(2)}) collective-permute-start(bf16[32,512]{1,0:T(8,128)(2,1)S(1)} %get-tuple-element.98), channel_id=1, source_target_pairs={{0,4},{4,0},{8,12},{12,8},{1,5},{5,1},{9,13},{13,9},{2,6},{6,2},{1... | collective-permute-start | bytes 98312 | tf_op jit(solution)/shard_map/ppermute | solution.py:396
  43.2 1.5 %shard_map.173 = (f32[1024,512]{1,0:T(8,128)S(1)}, bf16[1024,512]{1,0:T(8,128)(2,1)S(1)}) custom-call(bf16[512,512]{1,0:T(8,128)(2,1)S(1)} %get-tuple-element.89.hidden.refs_0_, bf16[512,512]{1,0:T(8,128)(2,1)S(1)} %get-tuple-element.91.sent, bf16[2048,1024]{1,0:T(8,128)(2,1)S(1)} %get-tuple-element.92.here.refs_10_, bf16[3,512,512]{2,1,0:T(8,128)(2,1)S(1)} %copy-done.3), custom_call_target="tpu_custom_call" | custom-call | flops 1342177280 | bytes 9961472 | tf_op jit(solution)/shard_map/pallas_call | solution.py:83
  44.7 0.5 collective-permute-done.8.refs_3_
  45.3 1.2 %shard_map.174.refs_2_ = f32[1024,512]{1,0:T(8,128)S(1)} custom-call(bf16[1024,512]{1,0:T(8,128)(2,1)S(1)} %get-tuple-element.96.table, bf16[2048,1024]{1,0:T(8,128)(2,1)S(1)} %get-tuple-element.92.here.refs_10_), custom_call_target="tpu_custom_call" | custom-call | flops 1073741824 | bytes 7340032 | tf_op jit(solution)/shard_map/pallas_call | solution.py:83
  46.7 2.7 %shard_map.175 = (bf16[512,512]{1,0:T(8,128)(2,1)S(1)}, f32[512,512]{1,0:T(8,128)S(1)}, bf16[2048,512]{1,0:T(8,128)(2,1)S(1)}, bf16[512,512]{1,0:T(8,128)(2,1)S(...) custom-call(bf16[512,512]{1,0:T(8,128)(2,1)S(1)} %get-tuple-element.89.hidden.refs_0_, ...), custom_call_target="tpu_custom_call" | custom-call | flops 1929379840 | bytes 17045504 | tf_op jit(solution)/shard_map/pallas_call | solution.py:83
  49.4 0.9 collective-permute-start.11
  50.4 2.3 %collective-permute-start.13 = (bf16[32,512]{1,0:T(8,128)(2,1)S(1)}, bf16[32,512]{1,0:T(8,128)(2,1)S(1)}, u32[]{:S(2)}, u32[]{:S(2)}) collective-permute-start(bf16[32,512]{1,0:T(8,128)(2,1)S(1)} %get-tuple-element.109), channel_id=1, source_target_pairs={{0,4},{4,0},{8,12},{12,8},{1,5},{5,1},{9,13},{13,9},{2,6},{6,2},{1... | collective-permute-start | bytes 98312 | tf_op jit(solution)/shard_map/ppermute | solution.py:396
  52.6 1.5 %shard_map.176 = (f32[1024,512]{1,0:T(8,128)S(1)}, bf16[1024,512]{1,0:T(8,128)(2,1)S(1)}) custom-call(bf16[512,512]{1,0:T(8,128)(2,1)S(1)} %get-tuple-element.101.hidden.refs_0_, bf16[512,512]{1,0:T(8,128)(2,1)S(1)} %get-tuple-element.103.sent, bf16[2048,1024]{1,0:T(8,128)(2,1)S(1)} %get-tuple-element.92.here.refs_10_, bf16[3,512,512]{2,1,0:T(8,128)(2,1)S(1)} %copy-done.3), custom_call_target="tpu_custom_call" | custom-call | flops 1342177280 | bytes 9961472 | tf_op jit(solution)/shard_map/pallas_call | solution.py:83
  54.3 0.4 collective-permute-start.12
  54.7 1.2 %shard_map.177.refs_2_ = f32[1024,512]{1,0:T(8,128)S(1)} custom-call(bf16[1024,512]{1,0:T(8,128)(2,1)S(1)} %get-tuple-element.107.table, bf16[2048,1024]{1,0:T(8,128)(2,1)S(1)} %get-tuple-element.92.here.refs_10_), custom_call_target="tpu_custom_call" | custom-call | flops 1073741824 | bytes 7340032 | tf_op jit(solution)/shard_map/pallas_call | solution.py:83
  56.0 2.8 %shard_map.178 = (bf16[512,512]{1,0:T(8,128)(2,1)S(1)}, f32[512,512]{1,0:T(8,128)S(1)}, bf16[2048,512]{1,0:T(8,128)(2,1)S(1)}, bf16[512,512]{1,0:T(8,128)(2,1)S(...) custom-call(bf16[512,512]{1,0:T(8,128)(2,1)S(1)} %get-tuple-element.101.hidden.refs_0_, ...), custom_call_target="tpu_custom_call" | custom-call | flops 1929379840 | bytes 17045504 | tf_op jit(solution)/shard_map/pallas_call | solution.py:83
  58.8 0.7 collective-permute-start.14
  59.5 2.4 %collective-permute-start.16 = (bf16[32,512]{1,0:T(8,128)(2,1)S(1)}, bf16[32,512]{1,0:T(8,128)(2,1)S(1)}, u32[]{:S(2)}, u32[]{:S(2)}) collective-permute-start(bf16[32,512]{1,0:T(8,128)(2,1)S(1)} %get-tuple-element.118), channel_id=1, source_target_pairs={{0,4},{4,0},{8,12},{12,8},{1,5},{5,1},{9,13},{13,9},{2,6},{6,2},{1... | collective-permute-start | bytes 98312 | tf_op jit(solution)/shard_map/ppermute | solution.py:396
  61.9 1.7 %shard_map.179 = (f32[1024,512]{1,0:T(8,128)S(1)}, bf16[1024,512]{1,0:T(8,128)(2,1)S(1)}) custom-call(bf16[512,512]{1,0:T(8,128)(2,1)S(1)} %get-tuple-element.110.hidden.refs_0_, bf16[512,512]{1,0:T(8,128)(2,1)S(1)} %get-tuple-element.112.sent, bf16[2048,1024]{1,0:T(8,128)(2,1)S(1)} %get-tuple-element.92.here.refs_10_, bf16[3,512,512]{2,1,0:T(8,128)(2,1)S(1)} %copy-done.3), custom_call_target="tpu_custom_call" | custom-call | flops 1342177280 | bytes 9961472 | tf_op jit(solution)/shard_map/pallas_call | solution.py:83
  63.6 0.8 collective-permute-done.14.refs_3_
  64.4 1.2 %shard_map.180.refs_2_ = f32[1024,512]{1,0:T(8,128)S(1)} custom-call(bf16[1024,512]{1,0:T(8,128)(2,1)S(1)} %get-tuple-element.116.table, bf16[2048,1024]{1,0:T(8,128)(2,1)S(1)} %get-tuple-element.92.here.refs_10_), custom_call_target="tpu_custom_call" | custom-call | flops 1073741824 | bytes 7340032 | tf_op jit(solution)/shard_map/pallas_call | solution.py:83
  65.7 5.0 %shard_map.181 = (bf16[512,512]{1,0:T(8,128)(2,1)}, bf16[2048,512]{1,0:T(8,128)(2,1)S(1)}, bf16[32,512]{1,0:T(8,128)(2,1)S(1)}, bf16[32,512]{1,0:T(8,128)(2,1)S(1)}) custom-call(bf16[512,512]{1,0:T(8,128)(2,1)S(1)} %get-tuple-element.110.hidden.refs_0_, f32[1024,512]{1,0:T(8,128)S(1)} %get-tuple-element.115.refs_1_, f32[1024,512]{1,0:T(8,128)S(1)} %shard_map.180.refs_2_, ...), custom_call_target="tpu_custom_call" | custom-call | flops 3221225472 | bytes 19044352 | tf_op jit(solution)/shard_map/pallas_call | solution.py:83
  70.9 2.4 %collective-permute-start.19 = (bf16[32,512]{1,0:T(8,128)(2,1)S(1)}, bf16[32,512]{1,0:T(8,128)(2,1)S(1)}, u32[]{:S(2)}, u32[]{:S(2)}) collective-permute-start(bf16[32,512]{1,0:T(8,128)(2,1)S(1)} %get-tuple-element.125), channel_id=1, source_target_pairs={{4,0},{0,4},{12,8},{8,12},{5,1},{1,5},{13,9},{9,13},{6,2},{2,6},{1... | collective-permute-start | bytes 98312 | tf_op jit(solution)/shard_map/ppermute | solution.py:401
  73.3 1.5 %shard_map.182.upstream = f32[512,512]{1,0:T(8,128)S(1)} custom-call(bf16[512,512]{1,0:T(8,128)(2,1)S(1)} %copy-done.6, bf16[2048,512]{1,0:T(8,128)(2,1)S(1)} %get-tuple-element.122.grad_pre, bf16[1024,2048]{1,0:T(8,128)(2,1)S(1)} %get-tuple-element.100.refs_7_.there, bf16[3,512,512]{2,1,0:T(8,128)(2,1)S(1)} %copy-done.2), custom_call_target="tpu_custom_call" | custom-call | flops 1342177280 | bytes 9437184 | tf_op jit(solution)/shard_map/pallas_call | solution.py:83
  74.8 1.5 %collective-permute-done.17.refs_1_ = bf16[32,512]{1,0:T(8,128)(2,1)S(1)} collective-permute-done((bf16[32,512]{1,0:T(8,128)(2,1)S(1)}, bf16[32,512]{1,0:T(8,128)(2,1)S(1)}, u32[]{:S(2)}, u32[]{:S(2)}) %collective-permute-start.17) | collective-permute-done | bytes 32800 | tf_op jit(solution)/shard_map/ppermute | solution.py:538
  76.3 1.5 %shard_map.183.refs_0_ = f32[512,512]{1,0:T(8,128)S(1)} custom-call(f32[512,512]{1,0:T(8,128)S(1)} %shard_map.182.upstream, bf16[2048,512]{1,0:T(8,128)(2,1)S(1)} %get-tuple-element.122.grad_pre, bf16[1024,2048]{1,0:T(8,128)(2,1)S(1)} %get-tuple-element.100.refs_7_.there, bf16[3,512,512]{2,1,0:T(8,128)(2,1)S(1)} %copy-done.3), custom_call_target="tpu_custom_call" | custom-call | flops 1342177280 | bytes 9961472 | tf_op jit(solution)/shard_map/pallas_call | solution.py:83
  77.9 2.6 %shard_map.184 = (f32[512,512]{1,0:T(8,128)S(1)}, bf16[2048,512]{1,0:T(8,128)(2,1)S(1)}, bf16[32,512]{1,0:T(8,128)(2,1)S(1)}, bf16[32,512]{1,0:T(8,128)(2,1)S(1)}) custom-call(f32[512,512]{1,0:T(8,128)S(1)} %shard_map.183.refs_0_, bf16[32,512]{1,0:T(8,128)(2,1)S(1)} %collective-permute-done.17.refs_1_, bf16[32,512]{1,0:T(8,128)(2,1)S(1)} %collective-permute-done.18.refs_2_, ...), custom_call_target="tpu_custom_call" | custom-call | flops 1711276032 | bytes 15472640 | tf_op jit(solution)/shard_map/pallas_call | solution.py:83
  80.5 0.4 collective-permute-start.20
  80.8 1.7 %collective-permute-start.22 = (bf16[32,512]{1,0:T(8,128)(2,1)S(1)}, bf16[32,512]{1,0:T(8,128)(2,1)S(1)}, u32[]{:S(2)}, u32[]{:S(2)}) collective-permute-start(bf16[32,512]{1,0:T(8,128)(2,1)S(1)} %get-tuple-element.134), channel_id=1, source_target_pairs={{4,0},{0,4},{12,8},{8,12},{5,1},{1,5},{13,9},{9,13},{6,2},{2,6},{1... | collective-permute-start | bytes 98312 | tf_op jit(solution)/shard_map/ppermute | solution.py:401
  82.5 1.5 %shard_map.185.upstream = f32[512,512]{1,0:T(8,128)S(1)} custom-call(f32[512,512]{1,0:T(8,128)S(1)} %get-tuple-element.130.upstream, bf16[2048,512]{1,0:T(8,128)(2,1)S(1)} %get-tuple-element.131.grad_pre, bf16[1024,2048]{1,0:T(8,128)(2,1)S(1)} %get-tuple-element.100.refs_7_.there, bf16[3,512,512]{2,1,0:T(8,128)(2,1)S(1)} %copy-done.2), custom_call_target="tpu_custom_call" | custom-call | flops 1342177280 | bytes 9961472 | tf_op jit(solution)/shard_map/pallas_call | solution.py:83
  84.0 1.4 %collective-permute-done.20.refs_1_ = bf16[32,512]{1,0:T(8,128)(2,1)S(1)} collective-permute-done((bf16[32,512]{1,0:T(8,128)(2,1)S(1)}, bf16[32,512]{1,0:T(8,128)(2,1)S(1)}, u32[]{:S(2)}, u32[]{:S(2)}) %collective-permute-start.20) | collective-permute-done | bytes 32800 | tf_op jit(solution)/shard_map/ppermute | solution.py:538
  85.6 1.5 %shard_map.186.refs_0_ = f32[512,512]{1,0:T(8,128)S(1)} custom-call(f32[512,512]{1,0:T(8,128)S(1)} %shard_map.185.upstream, bf16[2048,512]{1,0:T(8,128)(2,1)S(1)} %get-tuple-element.131.grad_pre, bf16[1024,2048]{1,0:T(8,128)(2,1)S(1)} %get-tuple-element.100.refs_7_.there, bf16[3,512,512]{2,1,0:T(8,128)(2,1)S(1)} %copy-done.3), custom_call_target="tpu_custom_call" | custom-call | flops 1342177280 | bytes 9961472 | tf_op jit(solution)/shard_map/pallas_call | solution.py:83
  87.2 2.8 %shard_map.187 = (f32[512,512]{1,0:T(8,128)S(1)}, bf16[2048,512]{1,0:T(8,128)(2,1)S(1)}, bf16[32,512]{1,0:T(8,128)(2,1)S(1)}, bf16[32,512]{1,0:T(8,128)(2,1)S(1)}) custom-call(f32[512,512]{1,0:T(8,128)S(1)} %shard_map.186.refs_0_, bf16[32,512]{1,0:T(8,128)(2,1)S(1)} %collective-permute-done.20.refs_1_, bf16[32,512]{1,0:T(8,128)(2,1)S(1)} %collective-permute-done.21.refs_2_, ...), custom_call_target="tpu_custom_call" | custom-call | flops 1711276032 | bytes 15472640 | tf_op jit(solution)/shard_map/pallas_call | solution.py:83
  90.0 0.9 collective-permute-start.23
  90.9 1.5 %collective-permute-start.25 = (bf16[32,512]{1,0:T(8,128)(2,1)S(1)}, bf16[32,512]{1,0:T(8,128)(2,1)S(1)}, u32[]{:S(2)}, u32[]{:S(2)}) collective-permute-start(bf16[32,512]{1,0:T(8,128)(2,1)S(1)} %get-tuple-element.142), channel_id=1, source_target_pairs={{4,0},{0,4},{12,8},{8,12},{5,1},{1,5},{13,9},{9,13},{6,2},{2,6},{1... | collective-permute-start | bytes 98312 | tf_op jit(solution)/shard_map/ppermute | solution.py:401
  92.3 1.5 %shard_map.188.upstream = f32[512,512]{1,0:T(8,128)S(1)} custom-call(f32[512,512]{1,0:T(8,128)S(1)} %get-tuple-element.138.upstream, bf16[2048,512]{1,0:T(8,128)(2,1)S(1)} %get-tuple-element.139.grad_pre, bf16[1024,2048]{1,0:T(8,128)(2,1)S(1)} %get-tuple-element.100.refs_7_.there, bf16[3,512,512]{2,1,0:T(8,128)(2,1)S(1)} %copy-done.2), custom_call_target="tpu_custom_call" | custom-call | flops 1342177280 | bytes 9961472 | tf_op jit(solution)/shard_map/pallas_call | solution.py:83
  93.9 1.1 collective-permute-done.23.refs_1_
  95.1 1.5 %shard_map.189.refs_0_ = f32[512,512]{1,0:T(8,128)S(1)} custom-call(f32[512,512]{1,0:T(8,128)S(1)} %shard_map.188.upstream, bf16[2048,512]{1,0:T(8,128)(2,1)S(1)} %get-tuple-element.139.grad_pre, bf16[1024,2048]{1,0:T(8,128)(2,1)S(1)} %get-tuple-element.100.refs_7_.there, bf16[3,512,512]{2,1,0:T(8,128)(2,1)S(1)} %copy-done.3), custom_call_target="tpu_custom_call" | custom-call | flops 1342177280 | bytes 9961472 | tf_op jit(solution)/shard_map/pallas_call | solution.py:83
  96.7 1.4 %shard_map.190 = (bf16[512,512]{1,0:T(8,128)(2,1)S(1)}, bf16[128,512]{1,0:T(8,128)(2,1)S(1)}, bf16[128,512]{1,0:T(8,128)(2,1)S(1)}) custom-call(f32[512,512]{1,0:T(8,128)S(1)} %shard_map.189.refs_0_, bf16[32,512]{1,0:T(8,128)(2,1)S(1)} %collective-permute-done.23.refs_1_, bf16[32,512]{1,0:T(8,128)(2,1)S(1)} %collective-permute-done.24.refs_2_, ...), custom_call_target="tpu_custom_call" | custom-call | flops 503316480 | bytes 5703680 | tf_op jit(solution)/shard_map/pallas_call | solution.py:83
  98.4 1.8 %collective-permute-start.29 = (bf16[128,512]{1,0:T(8,128)(2,1)S(1)}, bf16[128,512]{1,0:T(8,128)(2,1)S(1)}, u32[]{:S(2)}, u32[]{:S(2)}) collective-permute-start(bf16[128,512]{1,0:T(8,128)(2,1)S(1)} %get-tuple-element.159), channel_id=1, source_target_pairs={{4,0},{0,4},{12,8},{8,12},{5,1},{1,5},{13,9},{9,13},{6,2},{2,6},{1... | collective-permute-start | bytes 393224 | tf_op jit(solution)/shard_map/ppermute | solution.py:401
  100.2 0.6 shard_map.191
  100.7 3.7 %collective-permute-done.26.passed = bf16[128,512]{1,0:T(8,128)(2,1)S(1)} collective-permute-done((bf16[128,512]{1,0:T(8,128)(2,1)S(1)}, bf16[128,512]{1,0:T(8,128)(2,1)S(1)}, u32[]{:S(2)}, u32[]{:S(2)}) %collective-permute-start.26) | collective-permute-done | bytes 131104 | tf_op jit(solution)/shard_map/ppermute | solution.py:401
  104.8 2.5 %collective-permute-start.28 = (bf16[128,512]{1,0:T(8,128)(2,1)S(1)}, bf16[128,512]{1,0:T(8,128)(2,1)S(1)}, u32[]{:S(2)}, u32[]{:S(2)}) collective-permute-start(bf16[128,512]{1,0:T(8,128)(2,1)S(1)} %get-tuple-element.158), channel_id=1, source_target_pairs={{8,0},{12,4},{0,8},{4,12},{9,1},{13,5},{1,9},{5,13},{10,2},{14,6},... | collective-permute-start | bytes 393224 | tf_op jit(solution)/shard_map/ppermute | solution.py:401
  107.4 0.7 collective-permute-start.30
  108.1 6.3 %collective-permute-done.28.piece = bf16[128,512]{1,0:T(8,128)(2,1)S(1)} collective-permute-done((bf16[128,512]{1,0:T(8,128)(2,1)S(1)}, bf16[128,512]{1,0:T(8,128)(2,1)S(1)}, u32[]{:S(2)}, u32[]{:S(2)}) %collective-permute-start.28) | collective-permute-done | bytes 131104 | tf_op jit(solution)/shard_map/ppermute | solution.py:401
  114.4 4.7 %collective-permute-done.30.refs_3_ = bf16[128,512]{1,0:T(8,128)(2,1)S(1)} collective-permute-done((bf16[128,512]{1,0:T(8,128)(2,1)S(1)}, bf16[128,512]{1,0:T(8,128)(2,1)S(1)}, u32[]{:S(2)}, u32[]{:S(2)}) %collective-permute-start.30) | collective-permute-done | bytes 131104 | tf_op jit(solution)/shard_map/ppermute | solution.py:401
  119.1 1.3 %shard_map.195 = f32[256,512]{1,0:T(8,128)} custom-call(bf16[256,512]{1,0:T(8,128)(2,1)S(1)} %get-tuple-element.153.own.refs_0_, bf16[256,512]{1,0:T(8,128)(2,1)S(1)} %collective-permute-done.27.refs_1_, f32[128,512]{1,0:T(8,128)S(1)} %shard_map.193.refs_2_, bf16[128,512]{1,0:T(8,128)(2,1)S(1)} %collective-permute-done.30.refs_3_, bf16[512,512]{1,0:T(8,128)(2,1)S(1)} %copy-done.5), custom_call_target="tpu_custom_call" | custom-call | flops 134217728 | bytes 1966080 | tf_op jit(solution)/shard_map/pallas_call | solution.py:83
  (77 shorter events, 2.5 us)
Async XLA Ops:
  0.6 8.2 %copy-start = (s32[1,4,32]{2,1,0:T(4,128)S(1)}, s32[1,4,32]{2,1,0:T(4,128)}, u32[]{:S(2)}) copy-start(s32[1,4,32]{2,1,0:T(4,128)} %param.22) | copy-start | bytes 1540
  1.7 18.6 %collective-permute-start.3 = (bf16[272,512]{1,0:T(8,128)(2,1)S(1)}, bf16[272,512]{1,0:T(8,128)(2,1)S(1)}, u32[]{:S(2)}, u32[]{:S(2)}) collective-permute-start(bf16[272,512]{1,0:T(8,128)(2,1)S(1)} %shard_map.167.refs_5_), channel_id=1, source_target_pairs={{0,4},{4,0},{8,12},{12,8},{1,5},{5,1},{9,13},{13,9},{2,6},{6,2},{1... | collective-permute-start | bytes 835592 | tf_op jit(solution)/shard_map/ppermute | solution.py:396
  4.8 15.0 %collective-permute-start = (bf16[272,512]{1,0:T(8,128)(2,1)S(1)}, bf16[272,512]{1,0:T(8,128)(2,1)S(1)}, u32[]{:S(2)}, u32[]{:S(2)}) collective-permute-start(bf16[272,512]{1,0:T(8,128)(2,1)S(1)} %shard_map.167.refs_5_), channel_id=1, source_target_pairs={{0,8},{4,12},{8,0},{12,4},{1,9},{5,13},{9,1},{13,5},{2,10},{6,14},... | collective-permute-start | bytes 835592 | tf_op jit(solution)/shard_map/ppermute | solution.py:396
  8.7 1.2 collective-permute-start.1
  10.1 3.7 %collective-permute-start.2 = (s32[2,2,512]{2,0,1:T(2,128)S(1)}, s32[2,2,512]{2,0,1:T(2,128)S(1)}, u32[]{:S(2)}, u32[]{:S(2)}) collective-permute-start(s32[2,2,512]{2,0,1:T(2,128)S(1)} %fusion.1), channel_id=1, source_target_pairs={{0,2},{2,0},{1,3},{3,1},{4,6},{6,4},{5,7},{7,5},{8,10},{10,8},{9,1... | collective-permute-start | bytes 24584 | tf_op jit(solution)/shard_map/ppermute | solution.py:387
  14.0 6.4 %copy-start.5 = (bf16[512,512]{1,0:T(8,128)(2,1)S(1)}, bf16[512,512]{1,0:T(8,128)(2,1)}, u32[]{:S(2)}) copy-start(bf16[512,512]{1,0:T(8,128)(2,1)} %refs_4_.3) | copy-start | bytes 1572868
  14.0 6.4 %copy-start.8 = (bf16[512,512]{1,0:T(8,128)(2,1)S(1)}, bf16[512,512]{1,0:T(8,128)(2,1)}, u32[]{:S(2)}) copy-start(bf16[512,512]{1,0:T(8,128)(2,1)} %refs_3_.3) | copy-start | bytes 1572868
  14.0 6.4 %copy-start.11 = (bf16[512,512]{1,0:T(8,128)(2,1)S(1)}, bf16[512,512]{1,0:T(8,128)(2,1)}, u32[]{:S(2)}) copy-start(bf16[512,512]{1,0:T(8,128)(2,1)} %refs_3_.2) | copy-start | bytes 1572868
  19.8 6.5 %collective-permute-start.4 = (bf16[272,512]{1,0:T(8,128)(2,1)S(1)}, bf16[272,512]{1,0:T(8,128)(2,1)S(1)}, u32[]{:S(2)}, u32[]{:S(2)}) collective-permute-start(bf16[272,512]{1,0:T(8,128)(2,1)S(1)} %collective-permute-done.refs_4_), channel_id=1, source_target_pairs={{0,4},{4,0},{8,12},{12,8},{1,5},{5,1},{9,13},{13,9},{2,6},{6,2},{1... | collective-permute-start | bytes 835592 | tf_op jit(solution)/shard_map/ppermute | solution.py:396
  26.3 12.6 %copy-start.2 = (bf16[3,512,512]{2,1,0:T(8,128)(2,1)S(1)}, bf16[3,512,512]{2,1,0:T(8,128)(2,1)}, u32[]{:S(2)}) copy-start(bf16[3,512,512]{2,1,0:T(8,128)(2,1)} %refs_5_.5) | copy-start | bytes 4718596
  26.3 12.6 %copy-start.7 = (bf16[512,512]{1,0:T(8,128)(2,1)S(1)}, bf16[512,512]{1,0:T(8,128)(2,1)}, u32[]{:S(2)}) copy-start(bf16[512,512]{1,0:T(8,128)(2,1)} %refs_8_.11) | copy-start | bytes 1572868
  26.3 12.6 %copy-start.10 = (f32[512]{0:T(512)S(1)}, f32[512]{0:T(512)}, u32[]{:S(2)}) copy-start(f32[512]{0:T(512)} %param.26) | copy-start | bytes 6148
  27.2 1.6 %collective-permute-start.5 = (bf16[256,512]{1,0:T(8,128)(2,1)S(1)}, bf16[256,512]{1,0:T(8,128)(2,1)S(1)}, u32[]{:S(2)}, u32[]{:S(2)}) collective-permute-start(bf16[256,512]{1,0:T(8,128)(2,1)S(1)} %get-tuple-element.88), channel_id=1, source_target_pairs={{0,1},{1,0},{2,3},{3,2},{4,5},{5,4},{6,7},{7,6},{8,9},{9,8},{10,11... | collective-permute-start | bytes 786440 | tf_op jit(solution)/shard_map/ppermute | solution.py:387
  28.9 14.3 %copy-start.3 = (bf16[3,512,512]{2,1,0:T(8,128)(2,1)S(1)}, bf16[3,512,512]{2,1,0:T(8,128)(2,1)}, u32[]{:S(2)}) copy-start(bf16[3,512,512]{2,1,0:T(8,128)(2,1)} %weights.11) | copy-start | bytes 4718596
  28.9 8.4 %collective-permute-start.6 = (bf16[256,512]{1,0:T(8,128)(2,1)S(1)}, bf16[256,512]{1,0:T(8,128)(2,1)S(1)}, u32[]{:S(2)}, u32[]{:S(2)}) collective-permute-start(bf16[256,512]{1,0:T(8,128)(2,1)S(1)} %add_convert_fusion.1), channel_id=1, source_target_pairs={{0,2},{2,0},{1,3},{3,1},{4,6},{6,4},{5,7},{7,5},{8,10},{10,8},{9,1... | collective-permute-start | bytes 786440 | tf_op jit(solution)/shard_map/ppermute | solution.py:387
  37.4 1.6 %collective-permute-start.7 = (bf16[256,512]{1,0:T(8,128)(2,1)S(1)}, bf16[256,512]{1,0:T(8,128)(2,1)S(1)}, u32[]{:S(2)}, u32[]{:S(2)}) collective-permute-start(bf16[256,512]{1,0:T(8,128)(2,1)S(1)} %add_convert_fusion.refs_1_), channel_id=1, source_target_pairs={{0,1},{1,0},{2,3},{3,2},{4,5},{5,4},{6,7},{7,6},{8,9},{9,8},{10,11... | collective-permute-start | bytes 786440 | tf_op jit(solution)/shard_map/ppermute | solution.py:387
  40.0 5.3 %collective-permute-start.8 = (bf16[32,512]{1,0:T(8,128)(2,1)S(1)}, bf16[32,512]{1,0:T(8,128)(2,1)S(1)}, u32[]{:S(2)}, u32[]{:S(2)}) collective-permute-start(bf16[32,512]{1,0:T(8,128)(2,1)S(1)} %get-tuple-element.90), channel_id=1, source_target_pairs={{0,8},{1,13},{4,12},{5,9},{8,0},{9,5},{12,4},{13,1},{2,10},{3,15},... | collective-permute-start | bytes 98312 | tf_op jit(solution)/shard_map/ppermute | solution.py:538
  41.3 5.2 %collective-permute-start.10 = (bf16[32,512]{1,0:T(8,128)(2,1)S(1)}, bf16[32,512]{1,0:T(8,128)(2,1)S(1)}, u32[]{:S(2)}, u32[]{:S(2)}) collective-permute-start(bf16[32,512]{1,0:T(8,128)(2,1)S(1)} %get-tuple-element.98), channel_id=1, source_target_pairs={{0,4},{4,0},{8,12},{12,8},{1,5},{5,1},{9,13},{13,9},{2,6},{6,2},{1... | collective-permute-start | bytes 98312 | tf_op jit(solution)/shard_map/ppermute | solution.py:396
  45.3 1.4 %copy-start.4 = (bf16[3,512,512]{2,1,0:T(8,128)(2,1)S(1)}, bf16[3,512,512]{2,1,0:T(8,128)(2,1)}, u32[]{:S(2)}) copy-start(bf16[3,512,512]{2,1,0:T(8,128)(2,1)} %refs_9_.9) | copy-start | bytes 4718596
  45.3 1.4 %copy-start.9 = (f32[3,512]{1,0:T(4,128)S(1)}, f32[3,512]{1,0:T(4,128)}, u32[]{:S(2)}) copy-start(f32[3,512]{1,0:T(4,128)} %refs_8_.10) | copy-start | bytes 18436
  45.3 1.3 %collective-permute-start.9 = (bf16[32,512]{1,0:T(8,128)(2,1)S(1)}, bf16[32,512]{1,0:T(8,128)(2,1)S(1)}, u32[]{:S(2)}, u32[]{:S(2)}) collective-permute-start(bf16[32,512]{1,0:T(8,128)(2,1)S(1)} %collective-permute-done.8.refs_3_), channel_id=1, source_target_pairs={{0,1},{1,0},{2,3},{3,2},{4,5},{5,4},{6,7},{7,6},{8,9},{9,8},{10,11... | collective-permute-start | bytes 98312 | tf_op jit(solution)/shard_map/ppermute | solution.py:387
  49.4 4.9 %collective-permute-start.11 = (bf16[32,512]{1,0:T(8,128)(2,1)S(1)}, bf16[32,512]{1,0:T(8,128)(2,1)S(1)}, u32[]{:S(2)}, u32[]{:S(2)}) collective-permute-start(bf16[32,512]{1,0:T(8,128)(2,1)S(1)} %get-tuple-element.102), channel_id=1, source_target_pairs={{0,8},{1,13},{4,12},{5,9},{8,0},{9,5},{12,4},{13,1},{2,10},{3,15},... | collective-permute-start | bytes 98312 | tf_op jit(solution)/shard_map/ppermute | solution.py:538
  50.4 5.6 %collective-permute-start.13 = (bf16[32,512]{1,0:T(8,128)(2,1)S(1)}, bf16[32,512]{1,0:T(8,128)(2,1)S(1)}, u32[]{:S(2)}, u32[]{:S(2)}) collective-permute-start(bf16[32,512]{1,0:T(8,128)(2,1)S(1)} %get-tuple-element.109), channel_id=1, source_target_pairs={{0,4},{4,0},{8,12},{12,8},{1,5},{5,1},{9,13},{13,9},{2,6},{6,2},{1... | collective-permute-start | bytes 98312 | tf_op jit(solution)/shard_map/ppermute | solution.py:396
  54.3 1.7 %collective-permute-start.12 = (bf16[32,512]{1,0:T(8,128)(2,1)S(1)}, bf16[32,512]{1,0:T(8,128)(2,1)S(1)}, u32[]{:S(2)}, u32[]{:S(2)}) collective-permute-start(bf16[32,512]{1,0:T(8,128)(2,1)S(1)} %collective-permute-done.11.refs_3_), channel_id=1, source_target_pairs={{0,1},{1,0},{2,3},{3,2},{4,5},{5,4},{6,7},{7,6},{8,9},{9,8},{10,11... | collective-permute-start | bytes 98312 | tf_op jit(solution)/shard_map/ppermute | solution.py:387
  58.8 5.6 %collective-permute-start.14 = (bf16[32,512]{1,0:T(8,128)(2,1)S(1)}, bf16[32,512]{1,0:T(8,128)(2,1)S(1)}, u32[]{:S(2)}, u32[]{:S(2)}) collective-permute-start(bf16[32,512]{1,0:T(8,128)(2,1)S(1)} %get-tuple-element.111), channel_id=1, source_target_pairs={{0,8},{1,13},{4,12},{5,9},{8,0},{9,5},{12,4},{13,1},{2,10},{3,15},... | collective-permute-start | bytes 98312 | tf_op jit(solution)/shard_map/ppermute | solution.py:538
  59.5 6.2 %collective-permute-start.16 = (bf16[32,512]{1,0:T(8,128)(2,1)S(1)}, bf16[32,512]{1,0:T(8,128)(2,1)S(1)}, u32[]{:S(2)}, u32[]{:S(2)}) collective-permute-start(bf16[32,512]{1,0:T(8,128)(2,1)S(1)} %get-tuple-element.118), channel_id=1, source_target_pairs={{0,4},{4,0},{8,12},{12,8},{1,5},{5,1},{9,13},{13,9},{2,6},{6,2},{1... | collective-permute-start | bytes 98312 | tf_op jit(solution)/shard_map/ppermute | solution.py:396
  64.4 1.3 %copy-start.6 = (bf16[512,512]{1,0:T(8,128)(2,1)S(1)}, bf16[512,512]{1,0:T(8,128)(2,1)}, u32[]{:S(2)}) copy-start(bf16[512,512]{1,0:T(8,128)(2,1)} %upstream.1) | copy-start | bytes 1572868
  64.4 1.3 %collective-permute-start.15 = (bf16[32,512]{1,0:T(8,128)(2,1)S(1)}, bf16[32,512]{1,0:T(8,128)(2,1)S(1)}, u32[]{:S(2)}, u32[]{:S(2)}) collective-permute-start(bf16[32,512]{1,0:T(8,128)(2,1)S(1)} %collective-permute-done.14.refs_3_), channel_id=1, source_target_pairs={{0,1},{1,0},{2,3},{3,2},{4,5},{5,4},{6,7},{7,6},{8,9},{9,8},{10,11... | collective-permute-start | bytes 98312 | tf_op jit(solution)/shard_map/ppermute | solution.py:387
  70.7 5.6 %collective-permute-start.17 = (bf16[32,512]{1,0:T(8,128)(2,1)S(1)}, bf16[32,512]{1,0:T(8,128)(2,1)S(1)}, u32[]{:S(2)}, u32[]{:S(2)}) collective-permute-start(bf16[32,512]{1,0:T(8,128)(2,1)S(1)} %get-tuple-element.121), channel_id=1, source_target_pairs={{0,8},{1,13},{4,12},{5,9},{8,0},{9,5},{12,4},{13,1},{2,10},{3,15},... | collective-permute-start | bytes 98312 | tf_op jit(solution)/shard_map/ppermute | solution.py:538
  70.9 7.0 %collective-permute-start.19 = (bf16[32,512]{1,0:T(8,128)(2,1)S(1)}, bf16[32,512]{1,0:T(8,128)(2,1)S(1)}, u32[]{:S(2)}, u32[]{:S(2)}) collective-permute-start(bf16[32,512]{1,0:T(8,128)(2,1)S(1)} %get-tuple-element.125), channel_id=1, source_target_pairs={{4,0},{0,4},{12,8},{8,12},{5,1},{1,5},{13,9},{9,13},{6,2},{2,6},{1... | collective-permute-start | bytes 98312 | tf_op jit(solution)/shard_map/ppermute | solution.py:401
  76.3 1.5 %collective-permute-start.18 = (bf16[32,512]{1,0:T(8,128)(2,1)S(1)}, bf16[32,512]{1,0:T(8,128)(2,1)S(1)}, u32[]{:S(2)}, u32[]{:S(2)}) collective-permute-start(bf16[32,512]{1,0:T(8,128)(2,1)S(1)} %collective-permute-done.17.refs_1_), channel_id=1, source_target_pairs={{0,1},{1,0},{2,3},{3,2},{4,5},{5,4},{6,7},{7,6},{8,9},{9,8},{10,11... | collective-permute-start | bytes 98312 | tf_op jit(solution)/shard_map/ppermute | solution.py:387
  80.5 5.0 %collective-permute-start.20 = (bf16[32,512]{1,0:T(8,128)(2,1)S(1)}, bf16[32,512]{1,0:T(8,128)(2,1)S(1)}, u32[]{:S(2)}, u32[]{:S(2)}) collective-permute-start(bf16[32,512]{1,0:T(8,128)(2,1)S(1)} %get-tuple-element.129), channel_id=1, source_target_pairs={{0,8},{1,13},{4,12},{5,9},{8,0},{9,5},{12,4},{13,1},{2,10},{3,15},... | collective-permute-start | bytes 98312 | tf_op jit(solution)/shard_map/ppermute | solution.py:538
  80.8 6.3 %collective-permute-start.22 = (bf16[32,512]{1,0:T(8,128)(2,1)S(1)}, bf16[32,512]{1,0:T(8,128)(2,1)S(1)}, u32[]{:S(2)}, u32[]{:S(2)}) collective-permute-start(bf16[32,512]{1,0:T(8,128)(2,1)S(1)} %get-tuple-element.134), channel_id=1, source_target_pairs={{4,0},{0,4},{12,8},{8,12},{5,1},{1,5},{13,9},{9,13},{6,2},{2,6},{1... | collective-permute-start | bytes 98312 | tf_op jit(solution)/shard_map/ppermute | solution.py:401
  85.4 1.7 %collective-permute-start.21 = (bf16[32,512]{1,0:T(8,128)(2,1)S(1)}, bf16[32,512]{1,0:T(8,128)(2,1)S(1)}, u32[]{:S(2)}, u32[]{:S(2)}) collective-permute-start(bf16[32,512]{1,0:T(8,128)(2,1)S(1)} %collective-permute-done.20.refs_1_), channel_id=1, source_target_pairs={{0,1},{1,0},{2,3},{3,2},{4,5},{5,4},{6,7},{7,6},{8,9},{9,8},{10,11... | collective-permute-start | bytes 98312 | tf_op jit(solution)/shard_map/ppermute | solution.py:387
  90.0 5.0 %collective-permute-start.23 = (bf16[32,512]{1,0:T(8,128)(2,1)S(1)}, bf16[32,512]{1,0:T(8,128)(2,1)S(1)}, u32[]{:S(2)}, u32[]{:S(2)}) collective-permute-start(bf16[32,512]{1,0:T(8,128)(2,1)S(1)} %get-tuple-element.137), channel_id=1, source_target_pairs={{0,8},{1,13},{4,12},{5,9},{8,0},{9,5},{12,4},{13,1},{2,10},{3,15},... | collective-permute-start | bytes 98312 | tf_op jit(solution)/shard_map/ppermute | solution.py:538
  90.9 5.8 %collective-permute-start.25 = (bf16[32,512]{1,0:T(8,128)(2,1)S(1)}, bf16[32,512]{1,0:T(8,128)(2,1)S(1)}, u32[]{:S(2)}, u32[]{:S(2)}) collective-permute-start(bf16[32,512]{1,0:T(8,128)(2,1)S(1)} %get-tuple-element.142), channel_id=1, source_target_pairs={{4,0},{0,4},{12,8},{8,12},{5,1},{1,5},{13,9},{9,13},{6,2},{2,6},{1... | collective-permute-start | bytes 98312 | tf_op jit(solution)/shard_map/ppermute | solution.py:401
  95.0 1.7 %collective-permute-start.24 = (bf16[32,512]{1,0:T(8,128)(2,1)S(1)}, bf16[32,512]{1,0:T(8,128)(2,1)S(1)}, u32[]{:S(2)}, u32[]{:S(2)}) collective-permute-start(bf16[32,512]{1,0:T(8,128)(2,1)S(1)} %collective-permute-done.23.refs_1_), channel_id=1, source_target_pairs={{0,1},{1,0},{2,3},{3,2},{4,5},{5,4},{6,7},{7,6},{8,9},{9,8},{10,11... | collective-permute-start | bytes 98312 | tf_op jit(solution)/shard_map/ppermute | solution.py:387
  98.1 6.4 %collective-permute-start.26 = (bf16[128,512]{1,0:T(8,128)(2,1)S(1)}, bf16[128,512]{1,0:T(8,128)(2,1)S(1)}, u32[]{:S(2)}, u32[]{:S(2)}) collective-permute-start(bf16[128,512]{1,0:T(8,128)(2,1)S(1)} %get-tuple-element.155), channel_id=1, source_target_pairs={{4,0},{0,4},{12,8},{8,12},{5,1},{1,5},{13,9},{9,13},{6,2},{2,6},{1... | collective-permute-start | bytes 393224 | tf_op jit(solution)/shard_map/ppermute | solution.py:401
  98.4 9.0 %collective-permute-start.29 = (bf16[128,512]{1,0:T(8,128)(2,1)S(1)}, bf16[128,512]{1,0:T(8,128)(2,1)S(1)}, u32[]{:S(2)}, u32[]{:S(2)}) collective-permute-start(bf16[128,512]{1,0:T(8,128)(2,1)S(1)} %get-tuple-element.159), channel_id=1, source_target_pairs={{4,0},{0,4},{12,8},{8,12},{5,1},{1,5},{13,9},{9,13},{6,2},{2,6},{1... | collective-permute-start | bytes 393224 | tf_op jit(solution)/shard_map/ppermute | solution.py:401
  100.2 20.2 %copy-start.1 = (s32[1,4,32]{2,1,0:T(4,128)S(1)}, s32[1,4,32]{2,1,0:T(4,128)}, u32[]{:S(2)}) copy-start(s32[1,4,32]{2,1,0:T(4,128)} %param.22) | copy-start | bytes 1540
  104.5 14.6 %collective-permute-start.27 = (bf16[256,512]{1,0:T(8,128)(2,1)S(1)}, bf16[256,512]{1,0:T(8,128)(2,1)S(1)}, u32[]{:S(2)}, u32[]{:S(2)}) collective-permute-start(bf16[256,512]{1,0:T(8,128)(2,1)S(1)} %get-tuple-element.157), channel_id=1, source_target_pairs={{4,0},{0,4},{12,8},{8,12},{5,1},{1,5},{13,9},{9,13},{6,2},{2,6},{1... | collective-permute-start | bytes 786440 | tf_op jit(solution)/shard_map/ppermute | solution.py:401
  104.8 9.6 %collective-permute-start.28 = (bf16[128,512]{1,0:T(8,128)(2,1)S(1)}, bf16[128,512]{1,0:T(8,128)(2,1)S(1)}, u32[]{:S(2)}, u32[]{:S(2)}) collective-permute-start(bf16[128,512]{1,0:T(8,128)(2,1)S(1)} %get-tuple-element.158), channel_id=1, source_target_pairs={{8,0},{12,4},{0,8},{4,12},{9,1},{13,5},{1,9},{5,13},{10,2},{14,6},... | collective-permute-start | bytes 393224 | tf_op jit(solution)/shard_map/ppermute | solution.py:401
  107.4 11.7 %collective-permute-start.30 = (bf16[128,512]{1,0:T(8,128)(2,1)S(1)}, bf16[128,512]{1,0:T(8,128)(2,1)S(1)}, u32[]{:S(2)}, u32[]{:S(2)}) collective-permute-start(bf16[128,512]{1,0:T(8,128)(2,1)S(1)} %shard_map.194), channel_id=1, source_target_pairs={{8,0},{12,4},{0,8},{4,12},{9,1},{13,5},{1,9},{5,13},{10,2},{14,6},... | collective-permute-start | bytes 393224 | tf_op jit(solution)/shard_map/ppermute | solution.py:401

commit v11 on v10

--- a/solution.py
+++ b/solution.py
@@ -284,7 +284,7 @@
     for at in range(0, slope.shape[0], BLOCK):
         block = slice(at, at + BLOCK)
         grad_act = dot(here[block, nodes:], spread)
-        grad_pre[block, :] = (grad_act * slope[block, :].astype(f32)).astype(bf16)
+        grad_pre[block, :] = grad_act.astype(bf16) * slope[block, :]
     hand_out(dot(halo_there[...], grad_pre[...])[0:listed], outs)
 
 
@@ -328,7 +328,7 @@
 
 
 def pair_grads(spread, pick, slope):
-    return (dot(pick, spread) * slope.astype(f32)).astype(bf16)
+    return dot(pick, spread).astype(bf16) * slope
 
 
 def finish_kernel(shifts, *refs):
@@ -538,7 +538,8 @@
         far = lax.ppermute(
             blocks[0], ("mesh", "rep"), [(2 * at + side, 2 * (at ^ (2 + side)) + side) for at in range(4) for side in range(2)]
         )
-        near = send(blocks[1], 1)
+        block, early = lax.optimization_barrier((blocks[1], early))
+        near = send(block, 1)
         far, early = lax.optimization_barrier((far, early))
         return [far, shifted(far, "rep", 1), near], early
 

time: 121 us -> 123 us (1.017)
  starting transfers between devices: 32.3 us -> 34.2 us
    ppermute x6, starting transfers between devices: 4.36 us -> 8.38 us  [exchange(): lax.ppermute(blocks[0], ('mesh', 'rep'), [(2 * at + side, 2 * (at ^ 2 + s...]
    ppermute x6, waiting for transfers between devices: 5.84 us -> 8.07 us  [sent_to(): lax.ppermute(value, 'mesh', [(at, partner(at, step, size)) for at in rang...]
    ppermute x6, waiting for transfers between devices: 5.56 us -> 3.57 us  [exchange(): lax.ppermute(blocks[0], ('mesh', 'rep'), [(2 * at + side, 2 * (at ^ 2 + s...]
    ppermute x6, starting transfers between devices: 12.7 us -> 11.3 us  [sent_to(): lax.ppermute(value, 'mesh', [(at, partner(at, step, size)) for at in rang...]
  transfers between devices with their start and end apart: 31 -> 31, of which waited for: 16 -> 21; matrix products, arithmetic and copies ran while one was open for 2% -> 2% of each run, Pallas kernels for 20% -> 20%
where the time goes in v11:
time: 123 us
  Pallas kernels  45.5 us (37%)
  waiting for transfers between devices  39.6 us (32%)
  starting transfers between devices  34.2 us (28%)
  other arithmetic  1.82 us (1%)
    pallas_call x29, Pallas kernels, run(): pl.pallas_call(body, out_shape=tuple((jax.ShapeDtypeStruct(shape, dtype)...  45.5 us
    ppermute x8, waiting for transfers between devices, sent_back(): lax.ppermute(value, 'mesh', [(partner(at, step, size), at) for at in rang...  15.6 us
    ppermute x11, waiting for transfers between devices, shifted(): lax.ppermute(value, axis, [(at, (at + by) % size) for at in range(size)])  12.4 us
    ppermute x6, starting transfers between devices, sent_to(): lax.ppermute(value, 'mesh', [(at, partner(at, step, size)) for at in rang...  11.3 us
    ppermute x8, starting transfers between devices, sent_back(): lax.ppermute(value, 'mesh', [(partner(at, step, size), at) for at in rang...  11.1 us
    ppermute x6, starting transfers between devices, exchange(): lax.ppermute(blocks[0], ('mesh', 'rep'), [(2 * at + side, 2 * (at ^ 2 + s...  8.38 us
    ppermute x6, waiting for transfers between devices, sent_to(): lax.ppermute(value, 'mesh', [(at, partner(at, step, size)) for at in rang...  8.07 us
    ppermute x6, waiting for transfers between devices, exchange(): lax.ppermute(blocks[0], ('mesh', 'rep'), [(2 * at + side, 2 * (at ^ 2 + s...  3.57 us
  transfers between devices with their start and end apart: 31, of which 21 were waited for; matrix products, arithmetic and copies ran while one was open for 2% of the time, Pallas kernels for 20%

profile of v11, /device:TPU:0, one launch (start us, length us, event | category | flops | bytes accessed | tf_op | source)
XLA Modules:
  0.0 123.2 jit_solution(9104916613237410779)
XLA Ops:
  0.6 1.0 shard_map.167.refs_5_
  1.7 3.1 %collective-permute-start.3 = (bf16[272,512]{1,0:T(8,128)(2,1)S(1)}, bf16[272,512]{1,0:T(8,128)(2,1)S(1)}, u32[]{:S(2)}, u32[]{:S(2)}) collective-permute-start(bf16[272,512]{1,0:T(8,128)(2,1)S(1)} %shard_map.167.refs_5_), channel_id=1, source_target_pairs={{0,4},{4,0},{8,12},{12,8},{1,5},{5,1},{9,13},{13,9},{2,6},{6,2},{1... | collective-permute-start | bytes 835592 | tf_op jit(solution)/shard_map/ppermute | solution.py:396
  4.8 2.6 %collective-permute-start = (bf16[272,512]{1,0:T(8,128)(2,1)S(1)}, bf16[272,512]{1,0:T(8,128)(2,1)S(1)}, u32[]{:S(2)}, u32[]{:S(2)}) collective-permute-start(bf16[272,512]{1,0:T(8,128)(2,1)S(1)} %shard_map.167.refs_5_), channel_id=1, source_target_pairs={{0,8},{4,12},{8,0},{12,4},{1,9},{5,13},{9,1},{13,5},{2,10},{6,14},... | collective-permute-start | bytes 835592 | tf_op jit(solution)/shard_map/ppermute | solution.py:396
  7.3 0.7 compare_select_fusion.1
  8.0 0.7 fusion.11
  10.1 1.6 %collective-permute-start.2 = (s32[2,2,512]{2,0,1:T(2,128)S(1)}, s32[2,2,512]{2,0,1:T(2,128)S(1)}, u32[]{:S(2)}, u32[]{:S(2)}) collective-permute-start(s32[2,2,512]{2,0,1:T(2,128)S(1)} %fusion.1), channel_id=1, source_target_pairs={{0,2},{2,0},{1,3},{3,1},{4,6},{6,4},{5,7},{7,5},{8,10},{10,8},{9,1... | collective-permute-start | bytes 24584 | tf_op jit(solution)/shard_map/ppermute | solution.py:387
  11.7 2.1 %collective-permute-done.2 = s32[2,2,512]{2,0,1:T(2,128)S(1)} collective-permute-done((s32[2,2,512]{2,0,1:T(2,128)S(1)}, s32[2,2,512]{2,0,1:T(2,128)S(1)}, u32[]{:S(2)}, u32[]{:S(2)}) %collective-permute-start.2) | collective-permute-done | bytes 8224 | tf_op jit(solution)/shard_map/ppermute | solution.py:387
  14.0 3.5 %shard_map.168 = (bf16[2048,1024]{1,0:T(8,128)(2,1)S(1)}, bf16[1024,2048]{1,0:T(8,128)(2,1)S(1)}, bf16[2048,128]{1,0:T(8,128)(2,1)S(1)}, bf16[128,2048]{1,0:T(8,...) custom-call(s32[1,2048]{1,0:T(1,128)S(1)} %fusion.2.slots, s32[1,2048]{1,0:T(1,128)S(1)} %bitcast.26, ...), custom_call_target="tpu_custom_call" | custom-call | flops 3221225472 | bytes 9650560 | tf_op jit(solution)/shard_map/pallas_call | solution.py:83
  17.5 2.3 %collective-permute-done.refs_4_ = bf16[272,512]{1,0:T(8,128)(2,1)S(1)} collective-permute-done((bf16[272,512]{1,0:T(8,128)(2,1)S(1)}, bf16[272,512]{1,0:T(8,128)(2,1)S(1)}, u32[]{:S(2)}, u32[]{:S(2)}) %collective-permute-start) | collective-permute-done | bytes 278560 | tf_op jit(solution)/shard_map/ppermute | solution.py:396
  20.4 1.6 %shard_map.169 = (bf16[256,512]{1,0:T(8,128)(2,1)S(1)}, bf16[256,512]{1,0:T(8,128)(2,1)S(1)}, bf16[256,512]{1,0:T(8,128)(2,1)S(1)}, bf16[256,512]{1,0:T(8,128)(2...) custom-call(s32[2,512]{1,0:T(2,128)S(1)} %broadcast_in_dim.27.refs_0_, bf16[512,512]{1,0:T(8,128)(2,1)S(1)} %copy-done.8, ...), custom_call_target="tpu_custom_call" | custom-call | flops 1073741824 | bytes 4853760 | tf_op jit(solution)/shard_map/pallas_call | solution.py:83
  22.0 0.8 shard_map.170
  22.8 3.5 %collective-permute-done.4.refs_4_ = bf16[272,512]{1,0:T(8,128)(2,1)S(1)} collective-permute-done((bf16[272,512]{1,0:T(8,128)(2,1)S(1)}, bf16[272,512]{1,0:T(8,128)(2,1)S(1)}, u32[]{:S(2)}, u32[]{:S(2)}) %collective-permute-start.4) | collective-permute-done | bytes 278560 | tf_op jit(solution)/shard_map/ppermute | solution.py:396
  26.3 0.8 shard_map.171
  27.3 1.5 %collective-permute-done.5 = bf16[256,512]{1,0:T(8,128)(2,1)S(1)} collective-permute-done((bf16[256,512]{1,0:T(8,128)(2,1)S(1)}, bf16[256,512]{1,0:T(8,128)(2,1)S(1)}, u32[]{:S(2)}, u32[]{:S(2)}) %collective-permute-start.5) | collective-permute-done | bytes 262176 | tf_op jit(solution)/shard_map/ppermute | solution.py:387
  28.9 1.6 %collective-permute-start.6 = (bf16[256,512]{1,0:T(8,128)(2,1)S(1)}, bf16[256,512]{1,0:T(8,128)(2,1)S(1)}, u32[]{:S(2)}, u32[]{:S(2)}) collective-permute-start(bf16[256,512]{1,0:T(8,128)(2,1)S(1)} %add_convert_fusion.1), channel_id=1, source_target_pairs={{0,2},{2,0},{1,3},{3,1},{4,6},{6,4},{5,7},{7,5},{8,10},{10,8},{9,1... | collective-permute-start | bytes 786440 | tf_op jit(solution)/shard_map/ppermute | solution.py:387
  30.4 6.9 %collective-permute-done.6 = bf16[256,512]{1,0:T(8,128)(2,1)S(1)} collective-permute-done((bf16[256,512]{1,0:T(8,128)(2,1)S(1)}, bf16[256,512]{1,0:T(8,128)(2,1)S(1)}, u32[]{:S(2)}, u32[]{:S(2)}) %collective-permute-start.6) | collective-permute-done | bytes 262176 | tf_op jit(solution)/shard_map/ppermute | solution.py:387
  37.5 1.5 %collective-permute-done.7.refs_2_ = bf16[256,512]{1,0:T(8,128)(2,1)S(1)} collective-permute-done((bf16[256,512]{1,0:T(8,128)(2,1)S(1)}, bf16[256,512]{1,0:T(8,128)(2,1)S(1)}, u32[]{:S(2)}, u32[]{:S(2)}) %collective-permute-start.7) | collective-permute-done | bytes 262176 | tf_op jit(solution)/shard_map/ppermute | solution.py:387
  39.0 1.0 shard_map.172
  40.0 1.3 %collective-permute-start.8 = (bf16[32,512]{1,0:T(8,128)(2,1)S(1)}, bf16[32,512]{1,0:T(8,128)(2,1)S(1)}, u32[]{:S(2)}, u32[]{:S(2)}) collective-permute-start(bf16[32,512]{1,0:T(8,128)(2,1)S(1)} %get-tuple-element.105), channel_id=1, source_target_pairs={{0,8},{1,13},{4,12},{5,9},{8,0},{9,5},{12,4},{13,1},{2,10},{3,15},... | collective-permute-start | bytes 98312 | tf_op jit(solution)/shard_map/ppermute | solution.py:538
  41.3 1.5 %shard_map.173 = (f32[1024,512]{1,0:T(8,128)S(1)}, bf16[1024,512]{1,0:T(8,128)(2,1)S(1)}) custom-call(bf16[512,512]{1,0:T(8,128)(2,1)S(1)} %get-tuple-element.104.hidden.refs_0_, bf16[512,512]{1,0:T(8,128)(2,1)S(1)} %get-tuple-element.107.sent, bf16[2048,1024]{1,0:T(8,128)(2,1)S(1)} %get-tuple-element.108.here.refs_10_, bf16[3,512,512]{2,1,0:T(8,128)(2,1)S(1)} %copy-done.3), custom_call_target="tpu_custom_call" | custom-call | flops 1342177280 | bytes 9961472 | tf_op jit(solution)/shard_map/pallas_call | solution.py:83
  42.9 1.9 %collective-permute-start.10 = (bf16[32,512]{1,0:T(8,128)(2,1)S(1)}, bf16[32,512]{1,0:T(8,128)(2,1)S(1)}, u32[]{:S(2)}, u32[]{:S(2)}) collective-permute-start(bf16[32,512]{1,0:T(8,128)(2,1)S(1)} %get-tuple-element.116), channel_id=1, source_target_pairs={{0,4},{4,0},{8,12},{12,8},{1,5},{5,1},{9,13},{13,9},{2,6},{6,2},{1... | collective-permute-start | bytes 98312 | tf_op jit(solution)/shard_map/ppermute | solution.py:396
  45.2 1.2 %shard_map.174.refs_2_ = f32[1024,512]{1,0:T(8,128)S(1)} custom-call(bf16[1024,512]{1,0:T(8,128)(2,1)S(1)} %get-tuple-element.114.table, bf16[2048,1024]{1,0:T(8,128)(2,1)S(1)} %get-tuple-element.108.here.refs_10_), custom_call_target="tpu_custom_call" | custom-call | flops 1073741824 | bytes 7340032 | tf_op jit(solution)/shard_map/pallas_call | solution.py:83
  47.0 2.7 %shard_map.175 = (bf16[512,512]{1,0:T(8,128)(2,1)S(1)}, f32[512,512]{1,0:T(8,128)S(1)}, bf16[2048,512]{1,0:T(8,128)(2,1)S(1)}, bf16[512,512]{1,0:T(8,128)(2,1)S(...) custom-call(bf16[512,512]{1,0:T(8,128)(2,1)S(1)} %get-tuple-element.104.hidden.refs_0_, ...), custom_call_target="tpu_custom_call" | custom-call | flops 1929379840 | bytes 17045504 | tf_op jit(solution)/shard_map/pallas_call | solution.py:83
  49.8 1.6 %collective-permute-start.11 = (bf16[32,512]{1,0:T(8,128)(2,1)S(1)}, bf16[32,512]{1,0:T(8,128)(2,1)S(1)}, u32[]{:S(2)}, u32[]{:S(2)}) collective-permute-start(bf16[32,512]{1,0:T(8,128)(2,1)S(1)} %get-tuple-element.120), channel_id=1, source_target_pairs={{0,8},{1,13},{4,12},{5,9},{8,0},{9,5},{12,4},{13,1},{2,10},{3,15},... | collective-permute-start | bytes 98312 | tf_op jit(solution)/shard_map/ppermute | solution.py:538
  51.4 1.5 %shard_map.176 = (f32[1024,512]{1,0:T(8,128)S(1)}, bf16[1024,512]{1,0:T(8,128)(2,1)S(1)}) custom-call(bf16[512,512]{1,0:T(8,128)(2,1)S(1)} %get-tuple-element.119.hidden.refs_0_, bf16[512,512]{1,0:T(8,128)(2,1)S(1)} %get-tuple-element.122.sent, bf16[2048,1024]{1,0:T(8,128)(2,1)S(1)} %get-tuple-element.108.here.refs_10_, bf16[3,512,512]{2,1,0:T(8,128)(2,1)S(1)} %copy-done.3), custom_call_target="tpu_custom_call" | custom-call | flops 1342177280 | bytes 9961472 | tf_op jit(solution)/shard_map/pallas_call | solution.py:83
  52.9 1.4 %collective-permute-start.13 = (bf16[32,512]{1,0:T(8,128)(2,1)S(1)}, bf16[32,512]{1,0:T(8,128)(2,1)S(1)}, u32[]{:S(2)}, u32[]{:S(2)}) collective-permute-start(bf16[32,512]{1,0:T(8,128)(2,1)S(1)} %get-tuple-element.130), channel_id=1, source_target_pairs={{0,4},{4,0},{8,12},{12,8},{1,5},{5,1},{9,13},{13,9},{2,6},{6,2},{1... | collective-permute-start | bytes 98312 | tf_op jit(solution)/shard_map/ppermute | solution.py:396
  54.3 0.7 collective-permute-done.11.refs_3_
  55.0 1.2 %shard_map.177.refs_2_ = f32[1024,512]{1,0:T(8,128)S(1)} custom-call(bf16[1024,512]{1,0:T(8,128)(2,1)S(1)} %get-tuple-element.128.table, bf16[2048,1024]{1,0:T(8,128)(2,1)S(1)} %get-tuple-element.108.here.refs_10_), custom_call_target="tpu_custom_call" | custom-call | flops 1073741824 | bytes 7340032 | tf_op jit(solution)/shard_map/pallas_call | solution.py:83
  56.2 0.8 collective-permute-done.13.refs_5_
  57.0 2.8 %shard_map.178 = (bf16[512,512]{1,0:T(8,128)(2,1)S(1)}, f32[512,512]{1,0:T(8,128)S(1)}, bf16[2048,512]{1,0:T(8,128)(2,1)S(1)}, bf16[512,512]{1,0:T(8,128)(2,1)S(...) custom-call(bf16[512,512]{1,0:T(8,128)(2,1)S(1)} %get-tuple-element.119.hidden.refs_0_, ...), custom_call_target="tpu_custom_call" | custom-call | flops 1929379840 | bytes 17045504 | tf_op jit(solution)/shard_map/pallas_call | solution.py:83
  59.8 1.3 %collective-permute-start.14 = (bf16[32,512]{1,0:T(8,128)(2,1)S(1)}, bf16[32,512]{1,0:T(8,128)(2,1)S(1)}, u32[]{:S(2)}, u32[]{:S(2)}) collective-permute-start(bf16[32,512]{1,0:T(8,128)(2,1)S(1)} %get-tuple-element.132), channel_id=1, source_target_pairs={{0,8},{1,13},{4,12},{5,9},{8,0},{9,5},{12,4},{13,1},{2,10},{3,15},... | collective-permute-start | bytes 98312 | tf_op jit(solution)/shard_map/ppermute | solution.py:538
  61.1 1.7 %shard_map.179 = (f32[1024,512]{1,0:T(8,128)S(1)}, bf16[1024,512]{1,0:T(8,128)(2,1)S(1)}) custom-call(bf16[512,512]{1,0:T(8,128)(2,1)S(1)} %get-tuple-element.131.hidden.refs_0_, bf16[512,512]{1,0:T(8,128)(2,1)S(1)} %get-tuple-element.134.sent, bf16[2048,1024]{1,0:T(8,128)(2,1)S(1)} %get-tuple-element.108.here.refs_10_, bf16[3,512,512]{2,1,0:T(8,128)(2,1)S(1)} %copy-done.3), custom_call_target="tpu_custom_call" | custom-call | flops 1342177280 | bytes 9961472 | tf_op jit(solution)/shard_map/pallas_call | solution.py:83
  62.8 1.8 %collective-permute-start.16 = (bf16[32,512]{1,0:T(8,128)(2,1)S(1)}, bf16[32,512]{1,0:T(8,128)(2,1)S(1)}, u32[]{:S(2)}, u32[]{:S(2)}) collective-permute-start(bf16[32,512]{1,0:T(8,128)(2,1)S(1)} %get-tuple-element.142), channel_id=1, source_target_pairs={{0,4},{4,0},{8,12},{12,8},{1,5},{5,1},{9,13},{13,9},{2,6},{6,2},{1... | collective-permute-start | bytes 98312 | tf_op jit(solution)/shard_map/ppermute | solution.py:396
  64.9 1.2 %shard_map.180.refs_2_ = f32[1024,512]{1,0:T(8,128)S(1)} custom-call(bf16[1024,512]{1,0:T(8,128)(2,1)S(1)} %get-tuple-element.140.table, bf16[2048,1024]{1,0:T(8,128)(2,1)S(1)} %get-tuple-element.108.here.refs_10_), custom_call_target="tpu_custom_call" | custom-call | flops 1073741824 | bytes 7340032 | tf_op jit(solution)/shard_map/pallas_call | solution.py:83
  66.2 1.0 collective-permute-done.16.refs_5_
  67.1 5.0 %shard_map.181 = (bf16[512,512]{1,0:T(8,128)(2,1)}, bf16[2048,512]{1,0:T(8,128)(2,1)S(1)}, bf16[32,512]{1,0:T(8,128)(2,1)S(1)}, bf16[32,512]{1,0:T(8,128)(2,1)S(1)}) custom-call(bf16[512,512]{1,0:T(8,128)(2,1)S(1)} %get-tuple-element.131.hidden.refs_0_, f32[1024,512]{1,0:T(8,128)S(1)} %get-tuple-element.139.refs_1_, f32[1024,512]{1,0:T(8,128)S(1)} %shard_map.180.refs_2_, ...), custom_call_target="tpu_custom_call" | custom-call | flops 3221225472 | bytes 19044352 | tf_op jit(solution)/shard_map/pallas_call | solution.py:83
  72.1 1.4 %collective-permute-start.17 = (bf16[32,512]{1,0:T(8,128)(2,1)S(1)}, bf16[32,512]{1,0:T(8,128)(2,1)S(1)}, u32[]{:S(2)}, u32[]{:S(2)}) collective-permute-start(bf16[32,512]{1,0:T(8,128)(2,1)S(1)} %get-tuple-element.145), channel_id=1, source_target_pairs={{0,8},{1,13},{4,12},{5,9},{8,0},{9,5},{12,4},{13,1},{2,10},{3,15},... | collective-permute-start | bytes 98312 | tf_op jit(solution)/shard_map/ppermute | solution.py:538
  73.5 1.5 %shard_map.182.upstream = f32[512,512]{1,0:T(8,128)S(1)} custom-call(bf16[512,512]{1,0:T(8,128)(2,1)S(1)} %copy-done.6, bf16[2048,512]{1,0:T(8,128)(2,1)S(1)} %get-tuple-element.147.grad_pre, bf16[1024,2048]{1,0:T(8,128)(2,1)S(1)} %get-tuple-element.118.refs_7_.there, bf16[3,512,512]{2,1,0:T(8,128)(2,1)S(1)} %copy-done.2), custom_call_target="tpu_custom_call" | custom-call | flops 1342177280 | bytes 9437184 | tf_op jit(solution)/shard_map/pallas_call | solution.py:83
  75.0 1.3 %collective-permute-start.19 = (bf16[32,512]{1,0:T(8,128)(2,1)S(1)}, bf16[32,512]{1,0:T(8,128)(2,1)S(1)}, u32[]{:S(2)}, u32[]{:S(2)}) collective-permute-start(bf16[32,512]{1,0:T(8,128)(2,1)S(1)} %get-tuple-element.151), channel_id=1, source_target_pairs={{4,0},{0,4},{12,8},{8,12},{5,1},{1,5},{13,9},{9,13},{6,2},{2,6},{1... | collective-permute-start | bytes 98312 | tf_op jit(solution)/shard_map/ppermute | solution.py:401
  76.3 1.0 collective-permute-done.17.refs_1_
  77.3 1.5 %shard_map.183.refs_0_ = f32[512,512]{1,0:T(8,128)S(1)} custom-call(f32[512,512]{1,0:T(8,128)S(1)} %shard_map.182.upstream, bf16[2048,512]{1,0:T(8,128)(2,1)S(1)} %get-tuple-element.147.grad_pre, bf16[1024,2048]{1,0:T(8,128)(2,1)S(1)} %get-tuple-element.118.refs_7_.there, bf16[3,512,512]{2,1,0:T(8,128)(2,1)S(1)} %copy-done.3), custom_call_target="tpu_custom_call" | custom-call | flops 1342177280 | bytes 9961472 | tf_op jit(solution)/shard_map/pallas_call | solution.py:83
  79.0 2.6 %shard_map.184 = (f32[512,512]{1,0:T(8,128)S(1)}, bf16[2048,512]{1,0:T(8,128)(2,1)S(1)}, bf16[32,512]{1,0:T(8,128)(2,1)S(1)}, bf16[32,512]{1,0:T(8,128)(2,1)S(1)}) custom-call(f32[512,512]{1,0:T(8,128)S(1)} %shard_map.183.refs_0_, bf16[32,512]{1,0:T(8,128)(2,1)S(1)} %collective-permute-done.17.refs_1_, bf16[32,512]{1,0:T(8,128)(2,1)S(1)} %collective-permute-done.18.refs_2_, ...), custom_call_target="tpu_custom_call" | custom-call | flops 1711276032 | bytes 15472640 | tf_op jit(solution)/shard_map/pallas_call | solution.py:83
  81.5 1.6 %collective-permute-start.20 = (bf16[32,512]{1,0:T(8,128)(2,1)S(1)}, bf16[32,512]{1,0:T(8,128)(2,1)S(1)}, u32[]{:S(2)}, u32[]{:S(2)}) collective-permute-start(bf16[32,512]{1,0:T(8,128)(2,1)S(1)} %get-tuple-element.155), channel_id=1, source_target_pairs={{0,8},{1,13},{4,12},{5,9},{8,0},{9,5},{12,4},{13,1},{2,10},{3,15},... | collective-permute-start | bytes 98312 | tf_op jit(solution)/shard_map/ppermute | solution.py:538
  83.2 1.5 %shard_map.185.upstream = f32[512,512]{1,0:T(8,128)S(1)} custom-call(f32[512,512]{1,0:T(8,128)S(1)} %get-tuple-element.157.upstream, bf16[2048,512]{1,0:T(8,128)(2,1)S(1)} %get-tuple-element.158.grad_pre, bf16[1024,2048]{1,0:T(8,128)(2,1)S(1)} %get-tuple-element.118.refs_7_.there, bf16[3,512,512]{2,1,0:T(8,128)(2,1)S(1)} %copy-done.2), custom_call_target="tpu_custom_call" | custom-call | flops 1342177280 | bytes 9961472 | tf_op jit(solution)/shard_map/pallas_call | solution.py:83
  84.7 1.5 %collective-permute-start.22 = (bf16[32,512]{1,0:T(8,128)(2,1)S(1)}, bf16[32,512]{1,0:T(8,128)(2,1)S(1)}, u32[]{:S(2)}, u32[]{:S(2)}) collective-permute-start(bf16[32,512]{1,0:T(8,128)(2,1)S(1)} %get-tuple-element.162), channel_id=1, source_target_pairs={{4,0},{0,4},{12,8},{8,12},{5,1},{1,5},{13,9},{9,13},{6,2},{2,6},{1... | collective-permute-start | bytes 98312 | tf_op jit(solution)/shard_map/ppermute | solution.py:401
  86.6 1.5 %shard_map.186.refs_0_ = f32[512,512]{1,0:T(8,128)S(1)} custom-call(f32[512,512]{1,0:T(8,128)S(1)} %shard_map.185.upstream, bf16[2048,512]{1,0:T(8,128)(2,1)S(1)} %get-tuple-element.158.grad_pre, bf16[1024,2048]{1,0:T(8,128)(2,1)S(1)} %get-tuple-element.118.refs_7_.there, bf16[3,512,512]{2,1,0:T(8,128)(2,1)S(1)} %copy-done.3), custom_call_target="tpu_custom_call" | custom-call | flops 1342177280 | bytes 9961472 | tf_op jit(solution)/shard_map/pallas_call | solution.py:83
  88.1 0.8 collective-permute-done.22.refs_3_
  88.9 2.6 %shard_map.187 = (f32[512,512]{1,0:T(8,128)S(1)}, bf16[2048,512]{1,0:T(8,128)(2,1)S(1)}, bf16[32,512]{1,0:T(8,128)(2,1)S(1)}, bf16[32,512]{1,0:T(8,128)(2,1)S(1)}) custom-call(f32[512,512]{1,0:T(8,128)S(1)} %shard_map.186.refs_0_, bf16[32,512]{1,0:T(8,128)(2,1)S(1)} %collective-permute-done.20.refs_1_, bf16[32,512]{1,0:T(8,128)(2,1)S(1)} %collective-permute-done.21.refs_2_, ...), custom_call_target="tpu_custom_call" | custom-call | flops 1711276032 | bytes 15472640 | tf_op jit(solution)/shard_map/pallas_call | solution.py:83
  91.5 1.2 collective-permute-start.23
  92.7 1.7 %shard_map.188.upstream = f32[512,512]{1,0:T(8,128)S(1)} custom-call(f32[512,512]{1,0:T(8,128)S(1)} %get-tuple-element.167.upstream, bf16[2048,512]{1,0:T(8,128)(2,1)S(1)} %get-tuple-element.168.grad_pre, bf16[1024,2048]{1,0:T(8,128)(2,1)S(1)} %get-tuple-element.118.refs_7_.there, bf16[3,512,512]{2,1,0:T(8,128)(2,1)S(1)} %copy-done.2), custom_call_target="tpu_custom_call" | custom-call | flops 1342177280 | bytes 9961472 | tf_op jit(solution)/shard_map/pallas_call | solution.py:83
  94.4 1.7 %collective-permute-start.25 = (bf16[32,512]{1,0:T(8,128)(2,1)S(1)}, bf16[32,512]{1,0:T(8,128)(2,1)S(1)}, u32[]{:S(2)}, u32[]{:S(2)}) collective-permute-start(bf16[32,512]{1,0:T(8,128)(2,1)S(1)} %get-tuple-element.172), channel_id=1, source_target_pairs={{4,0},{0,4},{12,8},{8,12},{5,1},{1,5},{13,9},{9,13},{6,2},{2,6},{1... | collective-permute-start | bytes 98312 | tf_op jit(solution)/shard_map/ppermute | solution.py:401
  96.1 0.9 collective-permute-done.23.refs_1_
  97.0 1.5 %shard_map.189.refs_0_ = f32[512,512]{1,0:T(8,128)S(1)} custom-call(f32[512,512]{1,0:T(8,128)S(1)} %shard_map.188.upstream, bf16[2048,512]{1,0:T(8,128)(2,1)S(1)} %get-tuple-element.168.grad_pre, bf16[1024,2048]{1,0:T(8,128)(2,1)S(1)} %get-tuple-element.118.refs_7_.there, bf16[3,512,512]{2,1,0:T(8,128)(2,1)S(1)} %copy-done.3), custom_call_target="tpu_custom_call" | custom-call | flops 1342177280 | bytes 9961472 | tf_op jit(solution)/shard_map/pallas_call | solution.py:83
  98.6 1.4 %shard_map.190 = (bf16[512,512]{1,0:T(8,128)(2,1)S(1)}, bf16[128,512]{1,0:T(8,128)(2,1)S(1)}, bf16[128,512]{1,0:T(8,128)(2,1)S(1)}) custom-call(f32[512,512]{1,0:T(8,128)S(1)} %shard_map.189.refs_0_, bf16[32,512]{1,0:T(8,128)(2,1)S(1)} %collective-permute-done.23.refs_1_, bf16[32,512]{1,0:T(8,128)(2,1)S(1)} %collective-permute-done.24.refs_2_, ...), custom_call_target="tpu_custom_call" | custom-call | flops 503316480 | bytes 5703680 | tf_op jit(solution)/shard_map/pallas_call | solution.py:83
  100.0 1.5 %collective-permute-start.26 = (bf16[128,512]{1,0:T(8,128)(2,1)S(1)}, bf16[128,512]{1,0:T(8,128)(2,1)S(1)}, u32[]{:S(2)}, u32[]{:S(2)}) collective-permute-start(bf16[128,512]{1,0:T(8,128)(2,1)S(1)} %get-tuple-element.185), channel_id=1, source_target_pairs={{4,0},{0,4},{12,8},{8,12},{5,1},{1,5},{13,9},{9,13},{6,2},{2,6},{1... | collective-permute-start | bytes 393224 | tf_op jit(solution)/shard_map/ppermute | solution.py:401
  101.5 0.6 collective-permute-start.29
  102.1 0.6 shard_map.191
  102.7 3.7 %collective-permute-done.26.passed = bf16[128,512]{1,0:T(8,128)(2,1)S(1)} collective-permute-done((bf16[128,512]{1,0:T(8,128)(2,1)S(1)}, bf16[128,512]{1,0:T(8,128)(2,1)S(1)}, u32[]{:S(2)}, u32[]{:S(2)}) %collective-permute-start.26) | collective-permute-done | bytes 131104 | tf_op jit(solution)/shard_map/ppermute | solution.py:401
  106.4 1.6 %collective-permute-start.27 = (bf16[256,512]{1,0:T(8,128)(2,1)S(1)}, bf16[256,512]{1,0:T(8,128)(2,1)S(1)}, u32[]{:S(2)}, u32[]{:S(2)}) collective-permute-start(bf16[256,512]{1,0:T(8,128)(2,1)S(1)} %get-tuple-element.187), channel_id=1, source_target_pairs={{4,0},{0,4},{12,8},{8,12},{5,1},{1,5},{13,9},{9,13},{6,2},{2,6},{1... | collective-permute-start | bytes 786440 | tf_op jit(solution)/shard_map/ppermute | solution.py:401
  108.0 1.3 %collective-permute-start.28 = (bf16[128,512]{1,0:T(8,128)(2,1)S(1)}, bf16[128,512]{1,0:T(8,128)(2,1)S(1)}, u32[]{:S(2)}, u32[]{:S(2)}) collective-permute-start(bf16[128,512]{1,0:T(8,128)(2,1)S(1)} %get-tuple-element.188), channel_id=1, source_target_pairs={{8,0},{12,4},{0,8},{4,12},{9,1},{13,5},{1,9},{5,13},{10,2},{14,6},... | collective-permute-start | bytes 393224 | tf_op jit(solution)/shard_map/ppermute | solution.py:401
  109.3 1.7 %collective-permute-start.30 = (bf16[128,512]{1,0:T(8,128)(2,1)S(1)}, bf16[128,512]{1,0:T(8,128)(2,1)S(1)}, u32[]{:S(2)}, u32[]{:S(2)}) collective-permute-start(bf16[128,512]{1,0:T(8,128)(2,1)S(1)} %shard_map.194), channel_id=1, source_target_pairs={{8,0},{12,4},{0,8},{4,12},{9,1},{13,5},{1,9},{5,13},{10,2},{14,6},... | collective-permute-start | bytes 393224 | tf_op jit(solution)/shard_map/ppermute | solution.py:401
  111.0 9.5 %collective-permute-done.28.piece = bf16[128,512]{1,0:T(8,128)(2,1)S(1)} collective-permute-done((bf16[128,512]{1,0:T(8,128)(2,1)S(1)}, bf16[128,512]{1,0:T(8,128)(2,1)S(1)}, u32[]{:S(2)}, u32[]{:S(2)}) %collective-permute-start.28) | collective-permute-done | bytes 131104 | tf_op jit(solution)/shard_map/ppermute | solution.py:401
  120.6 1.4 %collective-permute-done.30.refs_3_ = bf16[128,512]{1,0:T(8,128)(2,1)S(1)} collective-permute-done((bf16[128,512]{1,0:T(8,128)(2,1)S(1)}, bf16[128,512]{1,0:T(8,128)(2,1)S(1)}, u32[]{:S(2)}, u32[]{:S(2)}) %collective-permute-start.30) | collective-permute-done | bytes 131104 | tf_op jit(solution)/shard_map/ppermute | solution.py:401
  121.9 1.3 %shard_map.195 = f32[256,512]{1,0:T(8,128)} custom-call(bf16[256,512]{1,0:T(8,128)(2,1)S(1)} %get-tuple-element.183.own.refs_0_, bf16[256,512]{1,0:T(8,128)(2,1)S(1)} %collective-permute-done.27.refs_1_, f32[128,512]{1,0:T(8,128)S(1)} %shard_map.193.refs_2_, bf16[128,512]{1,0:T(8,128)(2,1)S(1)} %collective-permute-done.30.refs_3_, bf16[512,512]{1,0:T(8,128)(2,1)S(1)} %copy-done.5), custom_call_target="tpu_custom_call" | custom-call | flops 134217728 | bytes 1966080 | tf_op jit(solution)/shard_map/pallas_call | solution.py:83
  (77 shorter events, 4.3 us)
Async XLA Ops:
  0.6 8.2 %copy-start = (s32[1,4,32]{2,1,0:T(4,128)S(1)}, s32[1,4,32]{2,1,0:T(4,128)}, u32[]{:S(2)}) copy-start(s32[1,4,32]{2,1,0:T(4,128)} %param.22) | copy-start | bytes 1540
  1.7 18.6 %collective-permute-start.3 = (bf16[272,512]{1,0:T(8,128)(2,1)S(1)}, bf16[272,512]{1,0:T(8,128)(2,1)S(1)}, u32[]{:S(2)}, u32[]{:S(2)}) collective-permute-start(bf16[272,512]{1,0:T(8,128)(2,1)S(1)} %shard_map.167.refs_5_), channel_id=1, source_target_pairs={{0,4},{4,0},{8,12},{12,8},{1,5},{5,1},{9,13},{13,9},{2,6},{6,2},{1... | collective-permute-start | bytes 835592 | tf_op jit(solution)/shard_map/ppermute | solution.py:396
  4.8 15.0 %collective-permute-start = (bf16[272,512]{1,0:T(8,128)(2,1)S(1)}, bf16[272,512]{1,0:T(8,128)(2,1)S(1)}, u32[]{:S(2)}, u32[]{:S(2)}) collective-permute-start(bf16[272,512]{1,0:T(8,128)(2,1)S(1)} %shard_map.167.refs_5_), channel_id=1, source_target_pairs={{0,8},{4,12},{8,0},{12,4},{1,9},{5,13},{9,1},{13,5},{2,10},{6,14},... | collective-permute-start | bytes 835592 | tf_op jit(solution)/shard_map/ppermute | solution.py:396
  8.7 1.2 collective-permute-start.1
  10.1 3.7 %collective-permute-start.2 = (s32[2,2,512]{2,0,1:T(2,128)S(1)}, s32[2,2,512]{2,0,1:T(2,128)S(1)}, u32[]{:S(2)}, u32[]{:S(2)}) collective-permute-start(s32[2,2,512]{2,0,1:T(2,128)S(1)} %fusion.1), channel_id=1, source_target_pairs={{0,2},{2,0},{1,3},{3,1},{4,6},{6,4},{5,7},{7,5},{8,10},{10,8},{9,1... | collective-permute-start | bytes 24584 | tf_op jit(solution)/shard_map/ppermute | solution.py:387
  14.0 6.4 %copy-start.5 = (bf16[512,512]{1,0:T(8,128)(2,1)S(1)}, bf16[512,512]{1,0:T(8,128)(2,1)}, u32[]{:S(2)}) copy-start(bf16[512,512]{1,0:T(8,128)(2,1)} %refs_4_.3) | copy-start | bytes 1572868
  14.0 6.4 %copy-start.8 = (bf16[512,512]{1,0:T(8,128)(2,1)S(1)}, bf16[512,512]{1,0:T(8,128)(2,1)}, u32[]{:S(2)}) copy-start(bf16[512,512]{1,0:T(8,128)(2,1)} %refs_3_.3) | copy-start | bytes 1572868
  14.0 6.4 %copy-start.11 = (bf16[512,512]{1,0:T(8,128)(2,1)S(1)}, bf16[512,512]{1,0:T(8,128)(2,1)}, u32[]{:S(2)}) copy-start(bf16[512,512]{1,0:T(8,128)(2,1)} %refs_3_.2) | copy-start | bytes 1572868
  19.8 6.5 %collective-permute-start.4 = (bf16[272,512]{1,0:T(8,128)(2,1)S(1)}, bf16[272,512]{1,0:T(8,128)(2,1)S(1)}, u32[]{:S(2)}, u32[]{:S(2)}) collective-permute-start(bf16[272,512]{1,0:T(8,128)(2,1)S(1)} %collective-permute-done.refs_4_), channel_id=1, source_target_pairs={{0,4},{4,0},{8,12},{12,8},{1,5},{5,1},{9,13},{13,9},{2,6},{6,2},{1... | collective-permute-start | bytes 835592 | tf_op jit(solution)/shard_map/ppermute | solution.py:396
  26.3 12.6 %copy-start.2 = (bf16[3,512,512]{2,1,0:T(8,128)(2,1)S(1)}, bf16[3,512,512]{2,1,0:T(8,128)(2,1)}, u32[]{:S(2)}) copy-start(bf16[3,512,512]{2,1,0:T(8,128)(2,1)} %refs_5_.5) | copy-start | bytes 4718596
  26.3 12.6 %copy-start.7 = (bf16[512,512]{1,0:T(8,128)(2,1)S(1)}, bf16[512,512]{1,0:T(8,128)(2,1)}, u32[]{:S(2)}) copy-start(bf16[512,512]{1,0:T(8,128)(2,1)} %refs_8_.11) | copy-start | bytes 1572868
  26.3 12.6 %copy-start.10 = (f32[512]{0:T(512)S(1)}, f32[512]{0:T(512)}, u32[]{:S(2)}) copy-start(f32[512]{0:T(512)} %param.26) | copy-start | bytes 6148
  27.2 1.6 %collective-permute-start.5 = (bf16[256,512]{1,0:T(8,128)(2,1)S(1)}, bf16[256,512]{1,0:T(8,128)(2,1)S(1)}, u32[]{:S(2)}, u32[]{:S(2)}) collective-permute-start(bf16[256,512]{1,0:T(8,128)(2,1)S(1)} %get-tuple-element.103), channel_id=1, source_target_pairs={{0,1},{1,0},{2,3},{3,2},{4,5},{5,4},{6,7},{7,6},{8,9},{9,8},{10,11... | collective-permute-start | bytes 786440 | tf_op jit(solution)/shard_map/ppermute | solution.py:387
  28.9 12.4 %copy-start.3 = (bf16[3,512,512]{2,1,0:T(8,128)(2,1)S(1)}, bf16[3,512,512]{2,1,0:T(8,128)(2,1)}, u32[]{:S(2)}) copy-start(bf16[3,512,512]{2,1,0:T(8,128)(2,1)} %weights.11) | copy-start | bytes 4718596
  28.9 8.4 %collective-permute-start.6 = (bf16[256,512]{1,0:T(8,128)(2,1)S(1)}, bf16[256,512]{1,0:T(8,128)(2,1)S(1)}, u32[]{:S(2)}, u32[]{:S(2)}) collective-permute-start(bf16[256,512]{1,0:T(8,128)(2,1)S(1)} %add_convert_fusion.1), channel_id=1, source_target_pairs={{0,2},{2,0},{1,3},{3,1},{4,6},{6,4},{5,7},{7,5},{8,10},{10,8},{9,1... | collective-permute-start | bytes 786440 | tf_op jit(solution)/shard_map/ppermute | solution.py:387
  37.4 1.6 %collective-permute-start.7 = (bf16[256,512]{1,0:T(8,128)(2,1)S(1)}, bf16[256,512]{1,0:T(8,128)(2,1)S(1)}, u32[]{:S(2)}, u32[]{:S(2)}) collective-permute-start(bf16[256,512]{1,0:T(8,128)(2,1)S(1)} %add_convert_fusion.refs_1_), channel_id=1, source_target_pairs={{0,1},{1,0},{2,3},{3,2},{4,5},{5,4},{6,7},{7,6},{8,9},{9,8},{10,11... | collective-permute-start | bytes 786440 | tf_op jit(solution)/shard_map/ppermute | solution.py:387
  40.0 5.2 %collective-permute-start.8 = (bf16[32,512]{1,0:T(8,128)(2,1)S(1)}, bf16[32,512]{1,0:T(8,128)(2,1)S(1)}, u32[]{:S(2)}, u32[]{:S(2)}) collective-permute-start(bf16[32,512]{1,0:T(8,128)(2,1)S(1)} %get-tuple-element.105), channel_id=1, source_target_pairs={{0,8},{1,13},{4,12},{5,9},{8,0},{9,5},{12,4},{13,1},{2,10},{3,15},... | collective-permute-start | bytes 98312 | tf_op jit(solution)/shard_map/ppermute | solution.py:538
  42.9 4.2 %copy-start.4 = (bf16[3,512,512]{2,1,0:T(8,128)(2,1)S(1)}, bf16[3,512,512]{2,1,0:T(8,128)(2,1)}, u32[]{:S(2)}) copy-start(bf16[3,512,512]{2,1,0:T(8,128)(2,1)} %refs_9_.9) | copy-start | bytes 4718596
  42.9 4.1 %copy-start.9 = (f32[3,512]{1,0:T(4,128)S(1)}, f32[3,512]{1,0:T(4,128)}, u32[]{:S(2)}) copy-start(f32[3,512]{1,0:T(4,128)} %refs_8_.10) | copy-start | bytes 18436
  42.9 4.1 %collective-permute-start.10 = (bf16[32,512]{1,0:T(8,128)(2,1)S(1)}, bf16[32,512]{1,0:T(8,128)(2,1)S(1)}, u32[]{:S(2)}, u32[]{:S(2)}) collective-permute-start(bf16[32,512]{1,0:T(8,128)(2,1)S(1)} %get-tuple-element.116), channel_id=1, source_target_pairs={{0,4},{4,0},{8,12},{12,8},{1,5},{5,1},{9,13},{13,9},{2,6},{6,2},{1... | collective-permute-start | bytes 98312 | tf_op jit(solution)/shard_map/ppermute | solution.py:396
  45.2 1.8 %collective-permute-start.9 = (bf16[32,512]{1,0:T(8,128)(2,1)S(1)}, bf16[32,512]{1,0:T(8,128)(2,1)S(1)}, u32[]{:S(2)}, u32[]{:S(2)}) collective-permute-start(bf16[32,512]{1,0:T(8,128)(2,1)S(1)} %collective-permute-done.8.refs_3_), channel_id=1, source_target_pairs={{0,1},{1,0},{2,3},{3,2},{4,5},{5,4},{6,7},{7,6},{8,9},{9,8},{10,11... | collective-permute-start | bytes 98312 | tf_op jit(solution)/shard_map/ppermute | solution.py:387
  49.8 5.2 %collective-permute-start.11 = (bf16[32,512]{1,0:T(8,128)(2,1)S(1)}, bf16[32,512]{1,0:T(8,128)(2,1)S(1)}, u32[]{:S(2)}, u32[]{:S(2)}) collective-permute-start(bf16[32,512]{1,0:T(8,128)(2,1)S(1)} %get-tuple-element.120), channel_id=1, source_target_pairs={{0,8},{1,13},{4,12},{5,9},{8,0},{9,5},{12,4},{13,1},{2,10},{3,15},... | collective-permute-start | bytes 98312 | tf_op jit(solution)/shard_map/ppermute | solution.py:538
  52.9 4.1 %collective-permute-start.13 = (bf16[32,512]{1,0:T(8,128)(2,1)S(1)}, bf16[32,512]{1,0:T(8,128)(2,1)S(1)}, u32[]{:S(2)}, u32[]{:S(2)}) collective-permute-start(bf16[32,512]{1,0:T(8,128)(2,1)S(1)} %get-tuple-element.130), channel_id=1, source_target_pairs={{0,4},{4,0},{8,12},{12,8},{1,5},{5,1},{9,13},{13,9},{2,6},{6,2},{1... | collective-permute-start | bytes 98312 | tf_op jit(solution)/shard_map/ppermute | solution.py:396
  55.0 2.0 %collective-permute-start.12 = (bf16[32,512]{1,0:T(8,128)(2,1)S(1)}, bf16[32,512]{1,0:T(8,128)(2,1)S(1)}, u32[]{:S(2)}, u32[]{:S(2)}) collective-permute-start(bf16[32,512]{1,0:T(8,128)(2,1)S(1)} %collective-permute-done.11.refs_3_), channel_id=1, source_target_pairs={{0,1},{1,0},{2,3},{3,2},{4,5},{5,4},{6,7},{7,6},{8,9},{9,8},{10,11... | collective-permute-start | bytes 98312 | tf_op jit(solution)/shard_map/ppermute | solution.py:387
  59.8 5.1 %collective-permute-start.14 = (bf16[32,512]{1,0:T(8,128)(2,1)S(1)}, bf16[32,512]{1,0:T(8,128)(2,1)S(1)}, u32[]{:S(2)}, u32[]{:S(2)}) collective-permute-start(bf16[32,512]{1,0:T(8,128)(2,1)S(1)} %get-tuple-element.132), channel_id=1, source_target_pairs={{0,8},{1,13},{4,12},{5,9},{8,0},{9,5},{12,4},{13,1},{2,10},{3,15},... | collective-permute-start | bytes 98312 | tf_op jit(solution)/shard_map/ppermute | solution.py:538
  62.8 4.3 %copy-start.6 = (bf16[512,512]{1,0:T(8,128)(2,1)S(1)}, bf16[512,512]{1,0:T(8,128)(2,1)}, u32[]{:S(2)}) copy-start(bf16[512,512]{1,0:T(8,128)(2,1)} %upstream.1) | copy-start | bytes 1572868
  62.8 4.3 %collective-permute-start.16 = (bf16[32,512]{1,0:T(8,128)(2,1)S(1)}, bf16[32,512]{1,0:T(8,128)(2,1)S(1)}, u32[]{:S(2)}, u32[]{:S(2)}) collective-permute-start(bf16[32,512]{1,0:T(8,128)(2,1)S(1)} %get-tuple-element.142), channel_id=1, source_target_pairs={{0,4},{4,0},{8,12},{12,8},{1,5},{5,1},{9,13},{13,9},{2,6},{6,2},{1... | collective-permute-start | bytes 98312 | tf_op jit(solution)/shard_map/ppermute | solution.py:396
  64.9 2.2 %collective-permute-start.15 = (bf16[32,512]{1,0:T(8,128)(2,1)S(1)}, bf16[32,512]{1,0:T(8,128)(2,1)S(1)}, u32[]{:S(2)}, u32[]{:S(2)}) collective-permute-start(bf16[32,512]{1,0:T(8,128)(2,1)S(1)} %collective-permute-done.14.refs_3_), channel_id=1, source_target_pairs={{0,1},{1,0},{2,3},{3,2},{4,5},{5,4},{6,7},{7,6},{8,9},{9,8},{10,11... | collective-permute-start | bytes 98312 | tf_op jit(solution)/shard_map/ppermute | solution.py:387
  72.1 5.2 %collective-permute-start.17 = (bf16[32,512]{1,0:T(8,128)(2,1)S(1)}, bf16[32,512]{1,0:T(8,128)(2,1)S(1)}, u32[]{:S(2)}, u32[]{:S(2)}) collective-permute-start(bf16[32,512]{1,0:T(8,128)(2,1)S(1)} %get-tuple-element.145), channel_id=1, source_target_pairs={{0,8},{1,13},{4,12},{5,9},{8,0},{9,5},{12,4},{13,1},{2,10},{3,15},... | collective-permute-start | bytes 98312 | tf_op jit(solution)/shard_map/ppermute | solution.py:538
  75.0 4.0 %collective-permute-start.19 = (bf16[32,512]{1,0:T(8,128)(2,1)S(1)}, bf16[32,512]{1,0:T(8,128)(2,1)S(1)}, u32[]{:S(2)}, u32[]{:S(2)}) collective-permute-start(bf16[32,512]{1,0:T(8,128)(2,1)S(1)} %get-tuple-element.151), channel_id=1, source_target_pairs={{4,0},{0,4},{12,8},{8,12},{5,1},{1,5},{13,9},{9,13},{6,2},{2,6},{1... | collective-permute-start | bytes 98312 | tf_op jit(solution)/shard_map/ppermute | solution.py:401
  77.2 1.7 %collective-permute-start.18 = (bf16[32,512]{1,0:T(8,128)(2,1)S(1)}, bf16[32,512]{1,0:T(8,128)(2,1)S(1)}, u32[]{:S(2)}, u32[]{:S(2)}) collective-permute-start(bf16[32,512]{1,0:T(8,128)(2,1)S(1)} %collective-permute-done.17.refs_1_), channel_id=1, source_target_pairs={{0,1},{1,0},{2,3},{3,2},{4,5},{5,4},{6,7},{7,6},{8,9},{9,8},{10,11... | collective-permute-start | bytes 98312 | tf_op jit(solution)/shard_map/ppermute | solution.py:387
  81.5 4.9 %collective-permute-start.20 = (bf16[32,512]{1,0:T(8,128)(2,1)S(1)}, bf16[32,512]{1,0:T(8,128)(2,1)S(1)}, u32[]{:S(2)}, u32[]{:S(2)}) collective-permute-start(bf16[32,512]{1,0:T(8,128)(2,1)S(1)} %get-tuple-element.155), channel_id=1, source_target_pairs={{0,8},{1,13},{4,12},{5,9},{8,0},{9,5},{12,4},{13,1},{2,10},{3,15},... | collective-permute-start | bytes 98312 | tf_op jit(solution)/shard_map/ppermute | solution.py:538
  84.7 4.2 %collective-permute-start.22 = (bf16[32,512]{1,0:T(8,128)(2,1)S(1)}, bf16[32,512]{1,0:T(8,128)(2,1)S(1)}, u32[]{:S(2)}, u32[]{:S(2)}) collective-permute-start(bf16[32,512]{1,0:T(8,128)(2,1)S(1)} %get-tuple-element.162), channel_id=1, source_target_pairs={{4,0},{0,4},{12,8},{8,12},{5,1},{1,5},{13,9},{9,13},{6,2},{2,6},{1... | collective-permute-start | bytes 98312 | tf_op jit(solution)/shard_map/ppermute | solution.py:401
  86.4 2.5 %collective-permute-start.21 = (bf16[32,512]{1,0:T(8,128)(2,1)S(1)}, bf16[32,512]{1,0:T(8,128)(2,1)S(1)}, u32[]{:S(2)}, u32[]{:S(2)}) collective-permute-start(bf16[32,512]{1,0:T(8,128)(2,1)S(1)} %collective-permute-done.20.refs_1_), channel_id=1, source_target_pairs={{0,1},{1,0},{2,3},{3,2},{4,5},{5,4},{6,7},{7,6},{8,9},{9,8},{10,11... | collective-permute-start | bytes 98312 | tf_op jit(solution)/shard_map/ppermute | solution.py:387
  91.5 5.5 %collective-permute-start.23 = (bf16[32,512]{1,0:T(8,128)(2,1)S(1)}, bf16[32,512]{1,0:T(8,128)(2,1)S(1)}, u32[]{:S(2)}, u32[]{:S(2)}) collective-permute-start(bf16[32,512]{1,0:T(8,128)(2,1)S(1)} %get-tuple-element.165), channel_id=1, source_target_pairs={{0,8},{1,13},{4,12},{5,9},{8,0},{9,5},{12,4},{13,1},{2,10},{3,15},... | collective-permute-start | bytes 98312 | tf_op jit(solution)/shard_map/ppermute | solution.py:538
  94.4 4.1 %collective-permute-start.25 = (bf16[32,512]{1,0:T(8,128)(2,1)S(1)}, bf16[32,512]{1,0:T(8,128)(2,1)S(1)}, u32[]{:S(2)}, u32[]{:S(2)}) collective-permute-start(bf16[32,512]{1,0:T(8,128)(2,1)S(1)} %get-tuple-element.172), channel_id=1, source_target_pairs={{4,0},{0,4},{12,8},{8,12},{5,1},{1,5},{13,9},{9,13},{6,2},{2,6},{1... | collective-permute-start | bytes 98312 | tf_op jit(solution)/shard_map/ppermute | solution.py:401
  97.0 1.5 %collective-permute-start.24 = (bf16[32,512]{1,0:T(8,128)(2,1)S(1)}, bf16[32,512]{1,0:T(8,128)(2,1)S(1)}, u32[]{:S(2)}, u32[]{:S(2)}) collective-permute-start(bf16[32,512]{1,0:T(8,128)(2,1)S(1)} %collective-permute-done.23.refs_1_), channel_id=1, source_target_pairs={{0,1},{1,0},{2,3},{3,2},{4,5},{5,4},{6,7},{7,6},{8,9},{9,8},{10,11... | collective-permute-start | bytes 98312 | tf_op jit(solution)/shard_map/ppermute | solution.py:387
  100.0 6.4 %collective-permute-start.26 = (bf16[128,512]{1,0:T(8,128)(2,1)S(1)}, bf16[128,512]{1,0:T(8,128)(2,1)S(1)}, u32[]{:S(2)}, u32[]{:S(2)}) collective-permute-start(bf16[128,512]{1,0:T(8,128)(2,1)S(1)} %get-tuple-element.185), channel_id=1, source_target_pairs={{4,0},{0,4},{12,8},{8,12},{5,1},{1,5},{13,9},{9,13},{6,2},{2,6},{1... | collective-permute-start | bytes 393224 | tf_op jit(solution)/shard_map/ppermute | solution.py:401
  101.5 7.8 %collective-permute-start.29 = (bf16[128,512]{1,0:T(8,128)(2,1)S(1)}, bf16[128,512]{1,0:T(8,128)(2,1)S(1)}, u32[]{:S(2)}, u32[]{:S(2)}) collective-permute-start(bf16[128,512]{1,0:T(8,128)(2,1)S(1)} %get-tuple-element.189), channel_id=1, source_target_pairs={{4,0},{0,4},{12,8},{8,12},{5,1},{1,5},{13,9},{9,13},{6,2},{2,6},{1... | collective-permute-start | bytes 393224 | tf_op jit(solution)/shard_map/ppermute | solution.py:401
  102.1 21.1 %copy-start.1 = (s32[1,4,32]{2,1,0:T(4,128)S(1)}, s32[1,4,32]{2,1,0:T(4,128)}, u32[]{:S(2)}) copy-start(s32[1,4,32]{2,1,0:T(4,128)} %param.22) | copy-start | bytes 1540
  106.4 15.5 %collective-permute-start.27 = (bf16[256,512]{1,0:T(8,128)(2,1)S(1)}, bf16[256,512]{1,0:T(8,128)(2,1)S(1)}, u32[]{:S(2)}, u32[]{:S(2)}) collective-permute-start(bf16[256,512]{1,0:T(8,128)(2,1)S(1)} %get-tuple-element.187), channel_id=1, source_target_pairs={{4,0},{0,4},{12,8},{8,12},{5,1},{1,5},{13,9},{9,13},{6,2},{2,6},{1... | collective-permute-start | bytes 786440 | tf_op jit(solution)/shard_map/ppermute | solution.py:401
  108.0 12.5 %collective-permute-start.28 = (bf16[128,512]{1,0:T(8,128)(2,1)S(1)}, bf16[128,512]{1,0:T(8,128)(2,1)S(1)}, u32[]{:S(2)}, u32[]{:S(2)}) collective-permute-start(bf16[128,512]{1,0:T(8,128)(2,1)S(1)} %get-tuple-element.188), channel_id=1, source_target_pairs={{8,0},{12,4},{0,8},{4,12},{9,1},{13,5},{1,9},{5,13},{10,2},{14,6},... | collective-permute-start | bytes 393224 | tf_op jit(solution)/shard_map/ppermute | solution.py:401
  109.3 12.6 %collective-permute-start.30 = (bf16[128,512]{1,0:T(8,128)(2,1)S(1)}, bf16[128,512]{1,0:T(8,128)(2,1)S(1)}, u32[]{:S(2)}, u32[]{:S(2)}) collective-permute-start(bf16[128,512]{1,0:T(8,128)(2,1)S(1)} %shard_map.194), channel_id=1, source_target_pairs={{8,0},{12,4},{0,8},{4,12},{9,1},{13,5},{1,9},{5,13},{10,2},{14,6},... | collective-permute-start | bytes 393224 | tf_op jit(solution)/shard_map/ppermute | solution.py:401

commit v12 on v11

--- a/solution.py
+++ b/solution.py
@@ -203,13 +203,21 @@
         out[...] = rows[first : first + depth]
 
 
+def updated(hidden, total, w_out, gain_row):
+    agg = dot(total, w_out)
+    return (hidden.astype(f32) + agg * norm_scale(agg) * gain_row).astype(bf16), agg
+
+
+def listed_update(list_here, total, hidden, w_out, gain_row, w_send):
+    picks = list_here[...]
+    rows, kept = dot(picks, total).astype(bf16), dot(picks, hidden)
+    return 0.5 * dot(updated(kept, rows, w_out, gain_row)[0], w_send)
+
+
 def start_kernel(halves, *refs):
     meta = refs[0]
     parts = refs[1 : 1 + halves]
-    mesh_init, w_enc_out, gain, w_send, list_here = refs[1 + halves : 6 + halves]
-    hidden_out, enc_sum_out, sent = refs[6 + halves : 9 + halves]
-    outs = refs[9 + halves : -1]
-    whole = refs[-1]
+    mesh_init, w_enc_out, gain, w_send, list_here, whole = refs[1 + halves : 7 + halves]
     part = parts[0].shape[0]
     own = meta[0:1, :]
     for at in range(halves):
@@ -217,19 +225,21 @@
         for shift in range(1, halves):
             rows = jnp.where(own == (at - shift) % halves, parts[shift][...].astype(f32), rows)
         whole[at * part : (at + 1) * part, :] = rows.astype(bf16)
-    enc_sum = dot(whole[...], w_enc_out[...])
-    enc_sum_out[...] = enc_sum
-    hidden = (mesh_init[...].astype(f32) + enc_sum * norm_scale(enc_sum) * gain[...]).astype(bf16)
-    hidden_out[...] = hidden
-    projected = (0.5 * dot(hidden, w_send[0])).astype(bf16)
-    sent[...] = projected
-    hand_out(dot(list_here[...], projected), outs)
-
-
-def local_kernel(layer, hidden, sent, here, w_recv, pre, table):
+    hand_out(
+        listed_update(list_here, whole[...], mesh_init[...], w_enc_out[...], gain[...], w_send[0]), refs[7 + halves :]
+    )
+
+
+def local_kernel(layer, total, hidden, w_out, gain, w_send, w_recv, here, hidden_out, agg_out, pre, table):
     nodes = hidden.shape[0]
-    table[0:nodes, :] = sent[...]
-    table[nodes:, :] = (0.5 * dot(hidden[...], w_recv[layer])).astype(bf16)
+    if layer:
+        fresh, agg = updated(hidden[...], total[...], w_out[layer - 1], gain[layer - 1 : layer, :])
+    else:
+        fresh, agg = updated(hidden[...], total[...], w_out[...], gain[...])
+    hidden_out[...] = fresh
+    agg_out[...] = agg
+    table[0:nodes, :] = (0.5 * dot(fresh, w_send[layer])).astype(bf16)
+    table[nodes:, :] = (0.5 * dot(fresh, w_recv[layer])).astype(bf16)
     for at in range(0, pre.shape[0], BLOCK):
         pre[at : at + BLOCK, :] = dot(here[at : at + BLOCK, :], table[...])
 
@@ -266,16 +276,12 @@
     hidden, pres = refs[0], refs[1:3]
     halos, refs = refs[3 : 3 + shifts], refs[3 + shifts :]
     halo_here, there, w_out, gain, w_send, list_here = refs[:6]
-    hidden_out, agg_out, slope_out, sent_out = refs[6:10]
-    outs = refs[10:-2]
-    total = node_sum(pres, halos, halo_here, there, slope_out, *refs[-2:])
-    agg = dot(total.astype(bf16), w_out[layer])
-    agg_out[...] = agg
-    fresh = (hidden[...].astype(f32) + agg * norm_scale(agg) * gain[layer : layer + 1, :]).astype(bf16)
-    hidden_out[...] = fresh
-    projected = (0.5 * dot(fresh, w_send[layer + 1])).astype(bf16)
-    sent_out[...] = projected
-    hand_out(dot(list_here[...], projected), outs)
+    total_out, slope_out = refs[6:8]
+    outs = refs[8:-2]
+    total = node_sum(pres, halos, halo_here, there, slope_out, *refs[-2:]).astype(bf16)
+    total_out[...] = total
+    gain_row = gain[layer : layer + 1, :]
+    hand_out(listed_update(list_here, total, hidden[...], w_out[layer], gain_row, w_send[layer + 1]), outs)
 
 
 def edge_grads(listed, grad_agg, w_out, here, halo_there, slope, grad_pre, outs):
@@ -296,9 +302,9 @@
     outs = refs[9:-2]
     slope, halo = refs[-2:]
     total = node_sum(pres, halos, halo_here, there, slope, halo, grad_pre)
-    agg = dot(total.astype(bf16), w_out[layer])
     gain_row = gain[layer : layer + 1, :]
-    hidden_out[...] = (hidden[...].astype(f32) + agg * norm_scale(agg) * gain_row).astype(bf16)
+    fresh, agg = updated(hidden[...], total.astype(bf16), w_out[layer], gain_row)
+    hidden_out[...] = fresh
     edge_grads(shifts * outs[0].shape[0], norm_back(agg, gain_row, cot[...].astype(f32)), w_out[layer], here, halo_there, slope, grad_pre, outs)
 
 
@@ -538,15 +544,14 @@
         far = lax.ppermute(
             blocks[0], ("mesh", "rep"), [(2 * at + side, 2 * (at ^ (2 + side)) + side) for at in range(4) for side in range(2)]
         )
-        block, early = lax.optimization_barrier((blocks[1], early))
-        near = send(block, 1)
+        near = send(blocks[1], 1)
         far, early = lax.optimization_barrier((far, early))
         return [far, shifted(far, "rep", 1), near], early
 
-    hidden, enc_sum, sent, *outgoing = call(
-        functools.partial(start_kernel, halves), [node_bf16, node_f32, node_bf16] + listed, [node_bf16],
-        [square, square, (listed_rows, nodes, width)],
-    )(meta, *parts, mesh_init, w_enc_out, enc_gain, w_send, list_here)
+    listed_products = [(listed_rows, width, width)] * 2 + [(listed_rows, nodes, width)] * 2
+    total, *outgoing = call(functools.partial(start_kernel, halves), [node_bf16] + listed, (), listed_products)(
+        meta, *parts, mesh_init, w_enc_out, enc_gain, w_send, list_here
+    )
 
     half_f32, edge_bf16 = ((all_edges // 2, width), f32), ((all_edges, width), bf16)
     halo, back_halo = ((wide, width), bf16), ((listed_rows, width), bf16)
@@ -554,28 +559,32 @@
     backward_products = [square, (all_edges, nodes, width), (wide, all_edges, width)]
     half_product = (all_edges // 2, 2 * nodes, width)
 
-    def arriving(layer):
+    hidden, sums, slopes = mesh_init, [], []
+    for layer in range(LAYERS):
+        weights = (w_out, layer_gain) if layer else (w_enc_out, enc_gain)
         early = call(
-            functools.partial(local_kernel, layer), [half_f32, ((2 * nodes, width), bf16)], (), [square, half_product]
-        )(hidden, sent, here, w_recv)
-        halos, (pre, both_tables) = exchange(outgoing, sent_to, early)
+            functools.partial(local_kernel, layer),
+            [node_bf16, node_f32, half_f32, ((2 * nodes, width), bf16)],
+            (),
+            [square, square, square, half_product],
+        )(total, hidden, *weights, w_send, w_recv, here)
+        halos, (hidden, agg, pre, both_tables) = exchange(outgoing, sent_to, early)
         (more,) = call(local_more_kernel, [half_f32], (), [half_product])(both_tables, here)
-        return hidden, pre, more, *halos
-
-    records = []
-    for layer in range(LAYERS - 1):
-        hidden, agg, slope, sent, *outgoing = call(
+        sums.append(agg)
+        if layer == LAYERS - 1:
+            break
+        total, slope, *outgoing = call(
             functools.partial(layer_kernel, layer, shifts),
-            [node_bf16, node_f32, edge_bf16, node_bf16] + listed,
+            [node_bf16, edge_bf16] + listed,
             [halo, edge_bf16],
-            forward_products + [square, (listed_rows, nodes, width)],
-        )(*arriving(layer), halo_here, there, w_out, layer_gain, w_send, list_here)
-        records.append((agg, slope))
-    last = LAYERS - 1
+            forward_products[:2] + listed_products,
+        )(hidden, pre, more, *halos, halo_here, there, w_out, layer_gain, w_send, list_here)
+        slopes.append(slope)
+    enc_sum, records = sums[0], list(zip(sums[1:], slopes))
     final_mesh, grad_pre, *outgoing = call(
-        functools.partial(turn_kernel, last, shifts), [node_bf16, edge_bf16] + listed, [edge_bf16, halo],
+        functools.partial(turn_kernel, layer, shifts), [node_bf16, edge_bf16] + listed, [edge_bf16, halo],
         forward_products + backward_products,
-    )(*arriving(last), halo_here, there, w_out, layer_gain, here, halo_there, out_cot)
+    )(hidden, pre, more, *halos, halo_here, there, w_out, layer_gain, here, halo_there, out_cot)
     upstream = out_cot
     for layer in reversed(range(LAYERS)):
 

time: 123 us -> 120 us (0.976)
  waiting for transfers between devices: 39.6 us -> 33.7 us
  Pallas kernels: 45.5 us -> 46.9 us
  starting transfers between devices: 34.2 us -> 35.6 us
    ppermute x6, waiting for transfers between devices: 3.57 us -> 0.5 us  [exchange(): lax.ppermute(blocks[0], ('mesh', 'rep'), [(2 * at + side, 2 * (at ^ 2 + s...]
    ppermute x6, waiting for transfers between devices: 8.07 us -> 5.84 us  [sent_to(): lax.ppermute(value, 'mesh', [(at, partner(at, step, size)) for at in rang...]
    ppermute x8, starting transfers between devices: 11.1 us -> 12.7 us  [sent_back(): lax.ppermute(value, 'mesh', [(partner(at, step, size), at) for at in rang...]
    pallas_call x29, Pallas kernels: 45.5 us -> 46.9 us  [run(): pl.pallas_call(body, out_shape=tuple((jax.ShapeDtypeStruct(shape, dtype)...]
  transfers between devices with their start and end apart: 31 -> 31, of which waited for: 21 -> 12; matrix products, arithmetic and copies ran while one was open for 2% -> 2% of each run, Pallas kernels for 20% -> 22%
where the time goes in v12:
time: 120 us
  Pallas kernels  46.9 us (39%)
  starting transfers between devices  35.6 us (30%)
  waiting for transfers between devices  33.7 us (28%)
  other arithmetic  1.83 us (2%)
    pallas_call x29, Pallas kernels, run(): pl.pallas_call(body, out_shape=tuple((jax.ShapeDtypeStruct(shape, dtype)...  46.9 us
    ppermute x8, waiting for transfers between devices, sent_back(): lax.ppermute(value, 'mesh', [(partner(at, step, size), at) for at in rang...  15 us
    ppermute x8, starting transfers between devices, sent_back(): lax.ppermute(value, 'mesh', [(partner(at, step, size), at) for at in rang...  12.7 us
    ppermute x11, waiting for transfers between devices, shifted(): lax.ppermute(value, axis, [(at, (at + by) % size) for at in range(size)])  12.4 us
    ppermute x6, starting transfers between devices, sent_to(): lax.ppermute(value, 'mesh', [(at, partner(at, step, size)) for at in rang...  11.3 us
    ppermute x6, starting transfers between devices, exchange(): lax.ppermute(blocks[0], ('mesh', 'rep'), [(2 * at + side, 2 * (at ^ 2 + s...  7.42 us
    ppermute x6, waiting for transfers between devices, sent_to(): lax.ppermute(value, 'mesh', [(at, partner(at, step, size)) for at in rang...  5.84 us
    ppermute x11, starting transfers between devices, shifted(): lax.ppermute(value, axis, [(at, (at + by) % size) for at in range(size)])  4.28 us
  transfers between devices with their start and end apart: 31, of which 12 were waited for; matrix products, arithmetic and copies ran while one was open for 2% of the time, Pallas kernels for 22%

profile of v12, /device:TPU:0, one launch (start us, length us, event | category | flops | bytes accessed | tf_op | source)
XLA Modules:
  0.0 120.2 jit_solution(11394402622245610105)
XLA Ops:
  0.6 1.0 shard_map.167.refs_5_
  1.7 3.1 %collective-permute-start.3 = (bf16[272,512]{1,0:T(8,128)(2,1)S(1)}, bf16[272,512]{1,0:T(8,128)(2,1)S(1)}, u32[]{:S(2)}, u32[]{:S(2)}) collective-permute-start(bf16[272,512]{1,0:T(8,128)(2,1)S(1)} %shard_map.167.refs_5_), channel_id=1, source_target_pairs={{0,4},{4,0},{8,12},{12,8},{1,5},{5,1},{9,13},{13,9},{2,6},{6,2},{1... | collective-permute-start | bytes 835592 | tf_op jit(solution)/shard_map/ppermute | solution.py:402
  4.8 2.6 %collective-permute-start = (bf16[272,512]{1,0:T(8,128)(2,1)S(1)}, bf16[272,512]{1,0:T(8,128)(2,1)S(1)}, u32[]{:S(2)}, u32[]{:S(2)}) collective-permute-start(bf16[272,512]{1,0:T(8,128)(2,1)S(1)} %shard_map.167.refs_5_), channel_id=1, source_target_pairs={{0,8},{4,12},{8,0},{12,4},{1,9},{5,13},{9,1},{13,5},{2,10},{6,14},... | collective-permute-start | bytes 835592 | tf_op jit(solution)/shard_map/ppermute | solution.py:402
  7.3 0.7 compare_select_fusion.1
  8.0 0.7 fusion.11
  8.8 0.6 gather_fusion
  9.5 0.4 collective-permute-done.1
  10.1 1.6 %collective-permute-start.2 = (s32[2,2,512]{2,0,1:T(2,128)S(1)}, s32[2,2,512]{2,0,1:T(2,128)S(1)}, u32[]{:S(2)}, u32[]{:S(2)}) collective-permute-start(s32[2,2,512]{2,0,1:T(2,128)S(1)} %fusion.1), channel_id=1, source_target_pairs={{0,2},{2,0},{1,3},{3,1},{4,6},{6,4},{5,7},{7,5},{8,10},{10,8},{9,1... | collective-permute-start | bytes 24584 | tf_op jit(solution)/shard_map/ppermute | solution.py:393
  11.7 2.1 %collective-permute-done.2 = s32[2,2,512]{2,0,1:T(2,128)S(1)} collective-permute-done((s32[2,2,512]{2,0,1:T(2,128)S(1)}, s32[2,2,512]{2,0,1:T(2,128)S(1)}, u32[]{:S(2)}, u32[]{:S(2)}) %collective-permute-start.2) | collective-permute-done | bytes 8224 | tf_op jit(solution)/shard_map/ppermute | solution.py:393
  14.0 3.5 %shard_map.168 = (bf16[2048,1024]{1,0:T(8,128)(2,1)S(1)}, bf16[1024,2048]{1,0:T(8,128)(2,1)S(1)}, bf16[2048,128]{1,0:T(8,128)(2,1)S(1)}, bf16[128,2048]{1,0:T(8,...) custom-call(s32[1,2048]{1,0:T(1,128)S(1)} %fusion.2.slots, s32[1,2048]{1,0:T(1,128)S(1)} %bitcast.29, ...), custom_call_target="tpu_custom_call" | custom-call | flops 3221225472 | bytes 9650560 | tf_op jit(solution)/shard_map/pallas_call | solution.py:83
  17.5 2.3 %collective-permute-done.refs_4_ = bf16[272,512]{1,0:T(8,128)(2,1)S(1)} collective-permute-done((bf16[272,512]{1,0:T(8,128)(2,1)S(1)}, bf16[272,512]{1,0:T(8,128)(2,1)S(1)}, u32[]{:S(2)}, u32[]{:S(2)}) %collective-permute-start) | collective-permute-done | bytes 278560 | tf_op jit(solution)/shard_map/ppermute | solution.py:402
  19.8 0.4 collective-permute-start.4
  20.4 1.6 %shard_map.169 = (bf16[256,512]{1,0:T(8,128)(2,1)S(1)}, bf16[256,512]{1,0:T(8,128)(2,1)S(1)}, bf16[256,512]{1,0:T(8,128)(2,1)S(1)}, bf16[256,512]{1,0:T(8,128)(2...) custom-call(s32[2,512]{1,0:T(2,128)S(1)} %broadcast_in_dim.27.refs_0_, bf16[512,512]{1,0:T(8,128)(2,1)S(1)} %copy-done.8, ...), custom_call_target="tpu_custom_call" | custom-call | flops 1073741824 | bytes 4853760 | tf_op jit(solution)/shard_map/pallas_call | solution.py:83
  22.0 0.8 shard_map.170
  22.8 3.5 %collective-permute-done.4.refs_4_ = bf16[272,512]{1,0:T(8,128)(2,1)S(1)} collective-permute-done((bf16[272,512]{1,0:T(8,128)(2,1)S(1)}, bf16[272,512]{1,0:T(8,128)(2,1)S(1)}, u32[]{:S(2)}, u32[]{:S(2)}) %collective-permute-start.4) | collective-permute-done | bytes 278560 | tf_op jit(solution)/shard_map/ppermute | solution.py:402
  26.3 0.8 shard_map.171
  27.3 1.5 %collective-permute-done.5 = bf16[256,512]{1,0:T(8,128)(2,1)S(1)} collective-permute-done((bf16[256,512]{1,0:T(8,128)(2,1)S(1)}, bf16[256,512]{1,0:T(8,128)(2,1)S(1)}, u32[]{:S(2)}, u32[]{:S(2)}) %collective-permute-start.5) | collective-permute-done | bytes 262176 | tf_op jit(solution)/shard_map/ppermute | solution.py:393
  28.9 1.6 %collective-permute-start.6 = (bf16[256,512]{1,0:T(8,128)(2,1)S(1)}, bf16[256,512]{1,0:T(8,128)(2,1)S(1)}, u32[]{:S(2)}, u32[]{:S(2)}) collective-permute-start(bf16[256,512]{1,0:T(8,128)(2,1)S(1)} %add_convert_fusion.1), channel_id=1, source_target_pairs={{0,2},{2,0},{1,3},{3,1},{4,6},{6,4},{5,7},{7,5},{8,10},{10,8},{9,1... | collective-permute-start | bytes 786440 | tf_op jit(solution)/shard_map/ppermute | solution.py:393
  30.5 6.9 %collective-permute-done.6 = bf16[256,512]{1,0:T(8,128)(2,1)S(1)} collective-permute-done((bf16[256,512]{1,0:T(8,128)(2,1)S(1)}, bf16[256,512]{1,0:T(8,128)(2,1)S(1)}, u32[]{:S(2)}, u32[]{:S(2)}) %collective-permute-start.6) | collective-permute-done | bytes 262176 | tf_op jit(solution)/shard_map/ppermute | solution.py:393
  37.5 1.5 %collective-permute-done.7.refs_2_ = bf16[256,512]{1,0:T(8,128)(2,1)S(1)} collective-permute-done((bf16[256,512]{1,0:T(8,128)(2,1)S(1)}, bf16[256,512]{1,0:T(8,128)(2,1)S(1)}, u32[]{:S(2)}, u32[]{:S(2)}) %collective-permute-start.7) | collective-permute-done | bytes 262176 | tf_op jit(solution)/shard_map/ppermute | solution.py:393
  39.0 0.7 shard_map.172
  39.7 1.3 %collective-permute-start.8 = (bf16[32,512]{1,0:T(8,128)(2,1)S(1)}, bf16[32,512]{1,0:T(8,128)(2,1)S(1)}, u32[]{:S(2)}, u32[]{:S(2)}) collective-permute-start(bf16[32,512]{1,0:T(8,128)(2,1)S(1)} %get-tuple-element.95), channel_id=1, source_target_pairs={{0,8},{1,13},{4,12},{5,9},{8,0},{9,5},{12,4},{13,1},{2,10},{3,15},... | collective-permute-start | bytes 98312 | tf_op jit(solution)/shard_map/ppermute | solution.py:544
  41.1 1.9 %collective-permute-start.10 = (bf16[32,512]{1,0:T(8,128)(2,1)S(1)}, bf16[32,512]{1,0:T(8,128)(2,1)S(1)}, u32[]{:S(2)}, u32[]{:S(2)}) collective-permute-start(bf16[32,512]{1,0:T(8,128)(2,1)S(1)} %get-tuple-element.106), channel_id=1, source_target_pairs={{0,4},{4,0},{8,12},{12,8},{1,5},{5,1},{9,13},{13,9},{2,6},{6,2},{1... | collective-permute-start | bytes 98312 | tf_op jit(solution)/shard_map/ppermute | solution.py:402
  42.9 2.2 %shard_map.173 = (bf16[512,512]{1,0:T(8,128)(2,1)S(1)}, f32[512,512]{1,0:T(8,128)S(1)}, f32[1024,512]{1,0:T(8,128)S(1)}, bf16[1024,512]{1,0:T(8,128)(2,1)S(1)}) custom-call(bf16[512,512]{1,0:T(8,128)(2,1)S(1)} %get-tuple-element.96.total, bf16[512,512]{1,0:T(8,128)(2,1)S(1)} %copy-done.8, bf16[512,512]{1,0:T(8,128)(2,1)S(1)} %copy-done.5, ...), custom_call_target="tpu_custom_call" | custom-call | flops 1879048192 | bytes 13633536 | tf_op jit(solution)/shard_map/pallas_call | solution.py:83
  45.3 1.2 %shard_map.174.refs_2_ = f32[1024,512]{1,0:T(8,128)S(1)} custom-call(bf16[1024,512]{1,0:T(8,128)(2,1)S(1)} %get-tuple-element.104.table, bf16[2048,1024]{1,0:T(8,128)(2,1)S(1)} %get-tuple-element.97.here.refs_10_), custom_call_target="tpu_custom_call" | custom-call | flops 1073741824 | bytes 7340032 | tf_op jit(solution)/shard_map/pallas_call | solution.py:83
  46.6 2.5 %shard_map.175 = (bf16[512,512]{1,0:T(8,128)(2,1)S(1)}, bf16[2048,512]{1,0:T(8,128)(2,1)S(1)}, bf16[32,512]{1,0:T(8,128)(2,1)S(1)}, bf16[32,512]{1,0:T(8,128)(2,1)S(1)}) custom-call(bf16[512,512]{1,0:T(8,128)(2,1)S(1)} %get-tuple-element.102.refs_0_.hidden, f32[1024,512]{1,0:T(8,128)S(1)} %get-tuple-element.103.refs_1_, f32[1024,512]{1,0:T(8,128)S(1)} %shard_map.174.refs_2_, ...), custom_call_target="tpu_custom_call" | custom-call | flops 1543503872 | bytes 15472640 | tf_op jit(solution)/shard_map/pallas_call | solution.py:83
  49.1 1.2 %collective-permute-start.11 = (bf16[32,512]{1,0:T(8,128)(2,1)S(1)}, bf16[32,512]{1,0:T(8,128)(2,1)S(1)}, u32[]{:S(2)}, u32[]{:S(2)}) collective-permute-start(bf16[32,512]{1,0:T(8,128)(2,1)S(1)} %get-tuple-element.109), channel_id=1, source_target_pairs={{0,8},{1,13},{4,12},{5,9},{8,0},{9,5},{12,4},{13,1},{2,10},{3,15},... | collective-permute-start | bytes 98312 | tf_op jit(solution)/shard_map/ppermute | solution.py:544
  50.3 1.8 %collective-permute-start.13 = (bf16[32,512]{1,0:T(8,128)(2,1)S(1)}, bf16[32,512]{1,0:T(8,128)(2,1)S(1)}, u32[]{:S(2)}, u32[]{:S(2)}) collective-permute-start(bf16[32,512]{1,0:T(8,128)(2,1)S(1)} %get-tuple-element.119), channel_id=1, source_target_pairs={{0,4},{4,0},{8,12},{12,8},{1,5},{5,1},{9,13},{13,9},{2,6},{6,2},{1... | collective-permute-start | bytes 98312 | tf_op jit(solution)/shard_map/ppermute | solution.py:402
  52.1 2.2 %shard_map.176 = (bf16[512,512]{1,0:T(8,128)(2,1)S(1)}, f32[512,512]{1,0:T(8,128)S(1)}, f32[1024,512]{1,0:T(8,128)S(1)}, bf16[1024,512]{1,0:T(8,128)(2,1)S(1)}) custom-call(bf16[512,512]{1,0:T(8,128)(2,1)S(1)} %get-tuple-element.110.total, bf16[512,512]{1,0:T(8,128)(2,1)S(1)} %get-tuple-element.102.refs_0_.hidden, bf16[3,512,512]{2,1,0:T(8,128)(2,1)S(1)} %copy-done.3, ...), custom_call_target="tpu_custom_call" | custom-call | flops 1879048192 | bytes 14686208 | tf_op jit(solution)/shard_map/pallas_call | solution.py:83
  54.5 1.2 %shard_map.177.refs_2_ = f32[1024,512]{1,0:T(8,128)S(1)} custom-call(bf16[1024,512]{1,0:T(8,128)(2,1)S(1)} %get-tuple-element.117.table, bf16[2048,1024]{1,0:T(8,128)(2,1)S(1)} %get-tuple-element.97.here.refs_10_), custom_call_target="tpu_custom_call" | custom-call | flops 1073741824 | bytes 7340032 | tf_op jit(solution)/shard_map/pallas_call | solution.py:83
  55.8 2.6 %shard_map.178 = (bf16[512,512]{1,0:T(8,128)(2,1)S(1)}, bf16[2048,512]{1,0:T(8,128)(2,1)S(1)}, bf16[32,512]{1,0:T(8,128)(2,1)S(1)}, bf16[32,512]{1,0:T(8,128)(2,1)S(1)}) custom-call(bf16[512,512]{1,0:T(8,128)(2,1)S(1)} %get-tuple-element.115.refs_0_.hidden, f32[1024,512]{1,0:T(8,128)S(1)} %get-tuple-element.116.refs_1_, f32[1024,512]{1,0:T(8,128)S(1)} %shard_map.177.refs_2_, ...), custom_call_target="tpu_custom_call" | custom-call | flops 1543503872 | bytes 15472640 | tf_op jit(solution)/shard_map/pallas_call | solution.py:83
  58.3 1.3 %collective-permute-start.14 = (bf16[32,512]{1,0:T(8,128)(2,1)S(1)}, bf16[32,512]{1,0:T(8,128)(2,1)S(1)}, u32[]{:S(2)}, u32[]{:S(2)}) collective-permute-start(bf16[32,512]{1,0:T(8,128)(2,1)S(1)} %get-tuple-element.120), channel_id=1, source_target_pairs={{0,8},{1,13},{4,12},{5,9},{8,0},{9,5},{12,4},{13,1},{2,10},{3,15},... | collective-permute-start | bytes 98312 | tf_op jit(solution)/shard_map/ppermute | solution.py:544
  59.7 1.5 %collective-permute-start.16 = (bf16[32,512]{1,0:T(8,128)(2,1)S(1)}, bf16[32,512]{1,0:T(8,128)(2,1)S(1)}, u32[]{:S(2)}, u32[]{:S(2)}) collective-permute-start(bf16[32,512]{1,0:T(8,128)(2,1)S(1)} %get-tuple-element.130), channel_id=1, source_target_pairs={{0,4},{4,0},{8,12},{12,8},{1,5},{5,1},{9,13},{13,9},{2,6},{6,2},{1... | collective-permute-start | bytes 98312 | tf_op jit(solution)/shard_map/ppermute | solution.py:402
  61.1 2.4 %shard_map.179 = (bf16[512,512]{1,0:T(8,128)(2,1)S(1)}, f32[512,512]{1,0:T(8,128)S(1)}, f32[1024,512]{1,0:T(8,128)S(1)}, bf16[1024,512]{1,0:T(8,128)(2,1)S(1)}) custom-call(bf16[512,512]{1,0:T(8,128)(2,1)S(1)} %get-tuple-element.121.total, bf16[512,512]{1,0:T(8,128)(2,1)S(1)} %get-tuple-element.115.refs_0_.hidden, bf16[3,512,512]{2,1,0:T(8,128)(2,1)S(1)} %copy-done.3, ...), custom_call_target="tpu_custom_call" | custom-call | flops 1879048192 | bytes 14686208 | tf_op jit(solution)/shard_map/pallas_call | solution.py:83
  63.6 1.2 %shard_map.180.refs_2_ = f32[1024,512]{1,0:T(8,128)S(1)} custom-call(bf16[1024,512]{1,0:T(8,128)(2,1)S(1)} %get-tuple-element.128.table, bf16[2048,1024]{1,0:T(8,128)(2,1)S(1)} %get-tuple-element.97.here.refs_10_), custom_call_target="tpu_custom_call" | custom-call | flops 1073741824 | bytes 7340032 | tf_op jit(solution)/shard_map/pallas_call | solution.py:83
  64.9 5.0 %shard_map.181 = (bf16[512,512]{1,0:T(8,128)(2,1)}, bf16[2048,512]{1,0:T(8,128)(2,1)S(1)}, bf16[32,512]{1,0:T(8,128)(2,1)S(1)}, bf16[32,512]{1,0:T(8,128)(2,1)S(1)}) custom-call(bf16[512,512]{1,0:T(8,128)(2,1)S(1)} %get-tuple-element.126.refs_0_, f32[1024,512]{1,0:T(8,128)S(1)} %get-tuple-element.127.refs_1_, f32[1024,512]{1,0:T(8,128)S(1)} %shard_map.180.refs_2_, ...), custom_call_target="tpu_custom_call" | custom-call | flops 3221225472 | bytes 19044352 | tf_op jit(solution)/shard_map/pallas_call | solution.py:83
  69.8 1.5 %collective-permute-start.17 = (bf16[32,512]{1,0:T(8,128)(2,1)S(1)}, bf16[32,512]{1,0:T(8,128)(2,1)S(1)}, u32[]{:S(2)}, u32[]{:S(2)}) collective-permute-start(bf16[32,512]{1,0:T(8,128)(2,1)S(1)} %get-tuple-element.133), channel_id=1, source_target_pairs={{0,8},{1,13},{4,12},{5,9},{8,0},{9,5},{12,4},{13,1},{2,10},{3,15},... | collective-permute-start | bytes 98312 | tf_op jit(solution)/shard_map/ppermute | solution.py:544
  71.4 1.6 %collective-permute-start.19 = (bf16[32,512]{1,0:T(8,128)(2,1)S(1)}, bf16[32,512]{1,0:T(8,128)(2,1)S(1)}, u32[]{:S(2)}, u32[]{:S(2)}) collective-permute-start(bf16[32,512]{1,0:T(8,128)(2,1)S(1)} %get-tuple-element.137), channel_id=1, source_target_pairs={{4,0},{0,4},{12,8},{8,12},{5,1},{1,5},{13,9},{9,13},{6,2},{2,6},{1... | collective-permute-start | bytes 98312 | tf_op jit(solution)/shard_map/ppermute | solution.py:407
  72.9 1.5 %shard_map.182.upstream = f32[512,512]{1,0:T(8,128)S(1)} custom-call(bf16[512,512]{1,0:T(8,128)(2,1)S(1)} %copy-done.7, bf16[2048,512]{1,0:T(8,128)(2,1)S(1)} %get-tuple-element.134.grad_pre, bf16[1024,2048]{1,0:T(8,128)(2,1)S(1)} %get-tuple-element.108.refs_7_.there, bf16[3,512,512]{2,1,0:T(8,128)(2,1)S(1)} %copy-done.2), custom_call_target="tpu_custom_call" | custom-call | flops 1342177280 | bytes 9437184 | tf_op jit(solution)/shard_map/pallas_call | solution.py:83
  74.7 0.4 collective-permute-start.18
  75.0 1.5 %shard_map.183.refs_0_ = f32[512,512]{1,0:T(8,128)S(1)} custom-call(f32[512,512]{1,0:T(8,128)S(1)} %shard_map.182.upstream, bf16[2048,512]{1,0:T(8,128)(2,1)S(1)} %get-tuple-element.134.grad_pre, bf16[1024,2048]{1,0:T(8,128)(2,1)S(1)} %get-tuple-element.108.refs_7_.there, bf16[3,512,512]{2,1,0:T(8,128)(2,1)S(1)} %copy-done.4), custom_call_target="tpu_custom_call" | custom-call | flops 1342177280 | bytes 9961472 | tf_op jit(solution)/shard_map/pallas_call | solution.py:83
  76.6 2.6 %shard_map.184 = (f32[512,512]{1,0:T(8,128)S(1)}, bf16[2048,512]{1,0:T(8,128)(2,1)S(1)}, bf16[32,512]{1,0:T(8,128)(2,1)S(1)}, bf16[32,512]{1,0:T(8,128)(2,1)S(1)}) custom-call(f32[512,512]{1,0:T(8,128)S(1)} %shard_map.183.refs_0_, bf16[32,512]{1,0:T(8,128)(2,1)S(1)} %collective-permute-done.17.refs_1_, bf16[32,512]{1,0:T(8,128)(2,1)S(1)} %collective-permute-done.18.refs_2_, ...), custom_call_target="tpu_custom_call" | custom-call | flops 1711276032 | bytes 15472640 | tf_op jit(solution)/shard_map/pallas_call | solution.py:83
  79.1 1.2 %collective-permute-start.20 = (bf16[32,512]{1,0:T(8,128)(2,1)S(1)}, bf16[32,512]{1,0:T(8,128)(2,1)S(1)}, u32[]{:S(2)}, u32[]{:S(2)}) collective-permute-start(bf16[32,512]{1,0:T(8,128)(2,1)S(1)} %get-tuple-element.141), channel_id=1, source_target_pairs={{0,8},{1,13},{4,12},{5,9},{8,0},{9,5},{12,4},{13,1},{2,10},{3,15},... | collective-permute-start | bytes 98312 | tf_op jit(solution)/shard_map/ppermute | solution.py:544
  80.4 2.3 %collective-permute-start.22 = (bf16[32,512]{1,0:T(8,128)(2,1)S(1)}, bf16[32,512]{1,0:T(8,128)(2,1)S(1)}, u32[]{:S(2)}, u32[]{:S(2)}) collective-permute-start(bf16[32,512]{1,0:T(8,128)(2,1)S(1)} %get-tuple-element.146), channel_id=1, source_target_pairs={{4,0},{0,4},{12,8},{8,12},{5,1},{1,5},{13,9},{9,13},{6,2},{2,6},{1... | collective-permute-start | bytes 98312 | tf_op jit(solution)/shard_map/ppermute | solution.py:407
  82.6 1.5 %shard_map.185.upstream = f32[512,512]{1,0:T(8,128)S(1)} custom-call(f32[512,512]{1,0:T(8,128)S(1)} %get-tuple-element.142.upstream, bf16[2048,512]{1,0:T(8,128)(2,1)S(1)} %get-tuple-element.143.grad_pre, bf16[1024,2048]{1,0:T(8,128)(2,1)S(1)} %get-tuple-element.108.refs_7_.there, bf16[3,512,512]{2,1,0:T(8,128)(2,1)S(1)} %copy-done.2), custom_call_target="tpu_custom_call" | custom-call | flops 1342177280 | bytes 9961472 | tf_op jit(solution)/shard_map/pallas_call | solution.py:83
  84.1 0.3 collective-permute-done.20.refs_1_
  84.4 1.5 %shard_map.186.refs_0_ = f32[512,512]{1,0:T(8,128)S(1)} custom-call(f32[512,512]{1,0:T(8,128)S(1)} %shard_map.185.upstream, bf16[2048,512]{1,0:T(8,128)(2,1)S(1)} %get-tuple-element.143.grad_pre, bf16[1024,2048]{1,0:T(8,128)(2,1)S(1)} %get-tuple-element.108.refs_7_.there, bf16[3,512,512]{2,1,0:T(8,128)(2,1)S(1)} %copy-done.4), custom_call_target="tpu_custom_call" | custom-call | flops 1342177280 | bytes 9961472 | tf_op jit(solution)/shard_map/pallas_call | solution.py:83
  86.0 2.8 %shard_map.187 = (f32[512,512]{1,0:T(8,128)S(1)}, bf16[2048,512]{1,0:T(8,128)(2,1)S(1)}, bf16[32,512]{1,0:T(8,128)(2,1)S(1)}, bf16[32,512]{1,0:T(8,128)(2,1)S(1)}) custom-call(f32[512,512]{1,0:T(8,128)S(1)} %shard_map.186.refs_0_, bf16[32,512]{1,0:T(8,128)(2,1)S(1)} %collective-permute-done.20.refs_1_, bf16[32,512]{1,0:T(8,128)(2,1)S(1)} %collective-permute-done.21.refs_2_, ...), custom_call_target="tpu_custom_call" | custom-call | flops 1711276032 | bytes 15472640 | tf_op jit(solution)/shard_map/pallas_call | solution.py:83
  88.8 0.8 collective-permute-start.23
  89.6 2.6 %collective-permute-start.25 = (bf16[32,512]{1,0:T(8,128)(2,1)S(1)}, bf16[32,512]{1,0:T(8,128)(2,1)S(1)}, u32[]{:S(2)}, u32[]{:S(2)}) collective-permute-start(bf16[32,512]{1,0:T(8,128)(2,1)S(1)} %get-tuple-element.154), channel_id=1, source_target_pairs={{4,0},{0,4},{12,8},{8,12},{5,1},{1,5},{13,9},{9,13},{6,2},{2,6},{1... | collective-permute-start | bytes 98312 | tf_op jit(solution)/shard_map/ppermute | solution.py:407
  92.2 1.5 %shard_map.188.upstream = f32[512,512]{1,0:T(8,128)S(1)} custom-call(f32[512,512]{1,0:T(8,128)S(1)} %get-tuple-element.150.upstream, bf16[2048,512]{1,0:T(8,128)(2,1)S(1)} %get-tuple-element.151.grad_pre, bf16[1024,2048]{1,0:T(8,128)(2,1)S(1)} %get-tuple-element.108.refs_7_.there, bf16[3,512,512]{2,1,0:T(8,128)(2,1)S(1)} %copy-done.2), custom_call_target="tpu_custom_call" | custom-call | flops 1342177280 | bytes 9961472 | tf_op jit(solution)/shard_map/pallas_call | solution.py:83
  93.7 0.4 collective-permute-start.24
  94.1 1.5 %shard_map.189.refs_0_ = f32[512,512]{1,0:T(8,128)S(1)} custom-call(f32[512,512]{1,0:T(8,128)S(1)} %shard_map.188.upstream, bf16[2048,512]{1,0:T(8,128)(2,1)S(1)} %get-tuple-element.151.grad_pre, bf16[1024,2048]{1,0:T(8,128)(2,1)S(1)} %get-tuple-element.108.refs_7_.there, bf16[3,512,512]{2,1,0:T(8,128)(2,1)S(1)} %copy-done.4), custom_call_target="tpu_custom_call" | custom-call | flops 1342177280 | bytes 9961472 | tf_op jit(solution)/shard_map/pallas_call | solution.py:83
  95.6 1.4 %shard_map.190 = (bf16[512,512]{1,0:T(8,128)(2,1)S(1)}, bf16[128,512]{1,0:T(8,128)(2,1)S(1)}, bf16[128,512]{1,0:T(8,128)(2,1)S(1)}) custom-call(f32[512,512]{1,0:T(8,128)S(1)} %shard_map.189.refs_0_, bf16[32,512]{1,0:T(8,128)(2,1)S(1)} %collective-permute-done.23.refs_1_, bf16[32,512]{1,0:T(8,128)(2,1)S(1)} %collective-permute-done.24.refs_2_, ...), custom_call_target="tpu_custom_call" | custom-call | flops 503316480 | bytes 5703680 | tf_op jit(solution)/shard_map/pallas_call | solution.py:83
  97.0 1.2 %collective-permute-start.26 = (bf16[128,512]{1,0:T(8,128)(2,1)S(1)}, bf16[128,512]{1,0:T(8,128)(2,1)S(1)}, u32[]{:S(2)}, u32[]{:S(2)}) collective-permute-start(bf16[128,512]{1,0:T(8,128)(2,1)S(1)} %get-tuple-element.167), channel_id=1, source_target_pairs={{4,0},{0,4},{12,8},{8,12},{5,1},{1,5},{13,9},{9,13},{6,2},{2,6},{1... | collective-permute-start | bytes 393224 | tf_op jit(solution)/shard_map/ppermute | solution.py:407
  98.2 0.9 collective-permute-start.29
  99.1 0.6 shard_map.191
  99.7 3.7 %collective-permute-done.26.passed = bf16[128,512]{1,0:T(8,128)(2,1)S(1)} collective-permute-done((bf16[128,512]{1,0:T(8,128)(2,1)S(1)}, bf16[128,512]{1,0:T(8,128)(2,1)S(1)}, u32[]{:S(2)}, u32[]{:S(2)}) %collective-permute-start.26) | collective-permute-done | bytes 131104 | tf_op jit(solution)/shard_map/ppermute | solution.py:407
  103.5 1.2 collective-permute-start.27
  104.6 2.2 %collective-permute-start.28 = (bf16[128,512]{1,0:T(8,128)(2,1)S(1)}, bf16[128,512]{1,0:T(8,128)(2,1)S(1)}, u32[]{:S(2)}, u32[]{:S(2)}) collective-permute-start(bf16[128,512]{1,0:T(8,128)(2,1)S(1)} %get-tuple-element.170), channel_id=1, source_target_pairs={{8,0},{12,4},{0,8},{4,12},{9,1},{13,5},{1,9},{5,13},{10,2},{14,6},... | collective-permute-start | bytes 393224 | tf_op jit(solution)/shard_map/ppermute | solution.py:407
  106.9 0.8 collective-permute-start.30
  107.7 6.6 %collective-permute-done.28.piece = bf16[128,512]{1,0:T(8,128)(2,1)S(1)} collective-permute-done((bf16[128,512]{1,0:T(8,128)(2,1)S(1)}, bf16[128,512]{1,0:T(8,128)(2,1)S(1)}, u32[]{:S(2)}, u32[]{:S(2)}) %collective-permute-start.28) | collective-permute-done | bytes 131104 | tf_op jit(solution)/shard_map/ppermute | solution.py:407
  114.3 4.6 %collective-permute-done.30.refs_3_ = bf16[128,512]{1,0:T(8,128)(2,1)S(1)} collective-permute-done((bf16[128,512]{1,0:T(8,128)(2,1)S(1)}, bf16[128,512]{1,0:T(8,128)(2,1)S(1)}, u32[]{:S(2)}, u32[]{:S(2)}) %collective-permute-start.30) | collective-permute-done | bytes 131104 | tf_op jit(solution)/shard_map/ppermute | solution.py:407
  118.9 1.3 %shard_map.195 = f32[256,512]{1,0:T(8,128)} custom-call(bf16[256,512]{1,0:T(8,128)(2,1)S(1)} %get-tuple-element.165.own.refs_0_, bf16[256,512]{1,0:T(8,128)(2,1)S(1)} %collective-permute-done.27.refs_1_, f32[128,512]{1,0:T(8,128)S(1)} %shard_map.193.refs_2_, bf16[128,512]{1,0:T(8,128)(2,1)S(1)} %collective-permute-done.30.refs_3_, bf16[512,512]{1,0:T(8,128)(2,1)S(1)} %copy-done.6), custom_call_target="tpu_custom_call" | custom-call | flops 134217728 | bytes 1966080 | tf_op jit(solution)/shard_map/pallas_call | solution.py:83
  (77 shorter events, 1.7 us)
Async XLA Ops:
  0.6 8.2 %copy-start = (s32[1,4,32]{2,1,0:T(4,128)S(1)}, s32[1,4,32]{2,1,0:T(4,128)}, u32[]{:S(2)}) copy-start(s32[1,4,32]{2,1,0:T(4,128)} %param.22) | copy-start | bytes 1540
  1.7 18.6 %collective-permute-start.3 = (bf16[272,512]{1,0:T(8,128)(2,1)S(1)}, bf16[272,512]{1,0:T(8,128)(2,1)S(1)}, u32[]{:S(2)}, u32[]{:S(2)}) collective-permute-start(bf16[272,512]{1,0:T(8,128)(2,1)S(1)} %shard_map.167.refs_5_), channel_id=1, source_target_pairs={{0,4},{4,0},{8,12},{12,8},{1,5},{5,1},{9,13},{13,9},{2,6},{6,2},{1... | collective-permute-start | bytes 835592 | tf_op jit(solution)/shard_map/ppermute | solution.py:402
  4.8 15.0 %collective-permute-start = (bf16[272,512]{1,0:T(8,128)(2,1)S(1)}, bf16[272,512]{1,0:T(8,128)(2,1)S(1)}, u32[]{:S(2)}, u32[]{:S(2)}) collective-permute-start(bf16[272,512]{1,0:T(8,128)(2,1)S(1)} %shard_map.167.refs_5_), channel_id=1, source_target_pairs={{0,8},{4,12},{8,0},{12,4},{1,9},{5,13},{9,1},{13,5},{2,10},{6,14},... | collective-permute-start | bytes 835592 | tf_op jit(solution)/shard_map/ppermute | solution.py:402
  8.7 1.2 collective-permute-start.1
  10.1 3.7 %collective-permute-start.2 = (s32[2,2,512]{2,0,1:T(2,128)S(1)}, s32[2,2,512]{2,0,1:T(2,128)S(1)}, u32[]{:S(2)}, u32[]{:S(2)}) collective-permute-start(s32[2,2,512]{2,0,1:T(2,128)S(1)} %fusion.1), channel_id=1, source_target_pairs={{0,2},{2,0},{1,3},{3,1},{4,6},{6,4},{5,7},{7,5},{8,10},{10,8},{9,1... | collective-permute-start | bytes 24584 | tf_op jit(solution)/shard_map/ppermute | solution.py:393
  14.0 6.4 %copy-start.6 = (bf16[512,512]{1,0:T(8,128)(2,1)S(1)}, bf16[512,512]{1,0:T(8,128)(2,1)}, u32[]{:S(2)}) copy-start(bf16[512,512]{1,0:T(8,128)(2,1)} %refs_4_.3) | copy-start | bytes 1572868
  14.0 6.4 %copy-start.8 = (bf16[512,512]{1,0:T(8,128)(2,1)S(1)}, bf16[512,512]{1,0:T(8,128)(2,1)}, u32[]{:S(2)}) copy-start(bf16[512,512]{1,0:T(8,128)(2,1)} %hidden.1) | copy-start | bytes 1572868
  14.0 6.4 %copy-start.11 = (bf16[512,512]{1,0:T(8,128)(2,1)S(1)}, bf16[512,512]{1,0:T(8,128)(2,1)}, u32[]{:S(2)}) copy-start(bf16[512,512]{1,0:T(8,128)(2,1)} %refs_3_.2) | copy-start | bytes 1572868
  19.8 6.5 %collective-permute-start.4 = (bf16[272,512]{1,0:T(8,128)(2,1)S(1)}, bf16[272,512]{1,0:T(8,128)(2,1)S(1)}, u32[]{:S(2)}, u32[]{:S(2)}) collective-permute-start(bf16[272,512]{1,0:T(8,128)(2,1)S(1)} %collective-permute-done.refs_4_), channel_id=1, source_target_pairs={{0,4},{4,0},{8,12},{12,8},{1,5},{5,1},{9,13},{13,9},{2,6},{6,2},{1... | collective-permute-start | bytes 835592 | tf_op jit(solution)/shard_map/ppermute | solution.py:402
  26.3 12.6 %copy-start.2 = (bf16[3,512,512]{2,1,0:T(8,128)(2,1)S(1)}, bf16[3,512,512]{2,1,0:T(8,128)(2,1)}, u32[]{:S(2)}) copy-start(bf16[3,512,512]{2,1,0:T(8,128)(2,1)} %refs_5_.5) | copy-start | bytes 4718596
  26.3 12.6 %copy-start.5 = (bf16[512,512]{1,0:T(8,128)(2,1)S(1)}, bf16[512,512]{1,0:T(8,128)(2,1)}, u32[]{:S(2)}) copy-start(bf16[512,512]{1,0:T(8,128)(2,1)} %refs_8_.11) | copy-start | bytes 1572868
  26.3 12.6 %copy-start.10 = (f32[512]{0:T(512)S(1)}, f32[512]{0:T(512)}, u32[]{:S(2)}) copy-start(f32[512]{0:T(512)} %param.26) | copy-start | bytes 6148
  27.2 1.6 %collective-permute-start.5 = (bf16[256,512]{1,0:T(8,128)(2,1)S(1)}, bf16[256,512]{1,0:T(8,128)(2,1)S(1)}, u32[]{:S(2)}, u32[]{:S(2)}) collective-permute-start(bf16[256,512]{1,0:T(8,128)(2,1)S(1)} %get-tuple-element.94), channel_id=1, source_target_pairs={{0,1},{1,0},{2,3},{3,2},{4,5},{5,4},{6,7},{7,6},{8,9},{9,8},{10,11... | collective-permute-start | bytes 786440 | tf_op jit(solution)/shard_map/ppermute | solution.py:393
  28.9 14.0 %copy-start.4 = (bf16[3,512,512]{2,1,0:T(8,128)(2,1)S(1)}, bf16[3,512,512]{2,1,0:T(8,128)(2,1)}, u32[]{:S(2)}) copy-start(bf16[3,512,512]{2,1,0:T(8,128)(2,1)} %weights.11) | copy-start | bytes 4718596
  28.9 8.4 %collective-permute-start.6 = (bf16[256,512]{1,0:T(8,128)(2,1)S(1)}, bf16[256,512]{1,0:T(8,128)(2,1)S(1)}, u32[]{:S(2)}, u32[]{:S(2)}) collective-permute-start(bf16[256,512]{1,0:T(8,128)(2,1)S(1)} %add_convert_fusion.1), channel_id=1, source_target_pairs={{0,2},{2,0},{1,3},{3,1},{4,6},{6,4},{5,7},{7,5},{8,10},{10,8},{9,1... | collective-permute-start | bytes 786440 | tf_op jit(solution)/shard_map/ppermute | solution.py:393
  37.4 1.6 %collective-permute-start.7 = (bf16[256,512]{1,0:T(8,128)(2,1)S(1)}, bf16[256,512]{1,0:T(8,128)(2,1)S(1)}, u32[]{:S(2)}, u32[]{:S(2)}) collective-permute-start(bf16[256,512]{1,0:T(8,128)(2,1)S(1)} %add_convert_fusion.refs_1_), channel_id=1, source_target_pairs={{0,1},{1,0},{2,3},{3,2},{4,5},{5,4},{6,7},{7,6},{8,9},{9,8},{10,11... | collective-permute-start | bytes 786440 | tf_op jit(solution)/shard_map/ppermute | solution.py:393
  39.7 5.4 %collective-permute-start.8 = (bf16[32,512]{1,0:T(8,128)(2,1)S(1)}, bf16[32,512]{1,0:T(8,128)(2,1)S(1)}, u32[]{:S(2)}, u32[]{:S(2)}) collective-permute-start(bf16[32,512]{1,0:T(8,128)(2,1)S(1)} %get-tuple-element.95), channel_id=1, source_target_pairs={{0,8},{1,13},{4,12},{5,9},{8,0},{9,5},{12,4},{13,1},{2,10},{3,15},... | collective-permute-start | bytes 98312 | tf_op jit(solution)/shard_map/ppermute | solution.py:544
  41.1 5.5 %collective-permute-start.10 = (bf16[32,512]{1,0:T(8,128)(2,1)S(1)}, bf16[32,512]{1,0:T(8,128)(2,1)S(1)}, u32[]{:S(2)}, u32[]{:S(2)}) collective-permute-start(bf16[32,512]{1,0:T(8,128)(2,1)S(1)} %get-tuple-element.106), channel_id=1, source_target_pairs={{0,4},{4,0},{8,12},{12,8},{1,5},{5,1},{9,13},{13,9},{2,6},{6,2},{1... | collective-permute-start | bytes 98312 | tf_op jit(solution)/shard_map/ppermute | solution.py:402
  45.2 1.4 %copy-start.3 = (bf16[3,512,512]{2,1,0:T(8,128)(2,1)S(1)}, bf16[3,512,512]{2,1,0:T(8,128)(2,1)}, u32[]{:S(2)}) copy-start(bf16[3,512,512]{2,1,0:T(8,128)(2,1)} %refs_9_.9) | copy-start | bytes 4718596
  45.2 1.4 %copy-start.9 = (f32[3,512]{1,0:T(4,128)S(1)}, f32[3,512]{1,0:T(4,128)}, u32[]{:S(2)}) copy-start(f32[3,512]{1,0:T(4,128)} %refs_8_.10) | copy-start | bytes 18436
  45.2 1.3 %collective-permute-start.9 = (bf16[32,512]{1,0:T(8,128)(2,1)S(1)}, bf16[32,512]{1,0:T(8,128)(2,1)S(1)}, u32[]{:S(2)}, u32[]{:S(2)}) collective-permute-start(bf16[32,512]{1,0:T(8,128)(2,1)S(1)} %collective-permute-done.8.refs_3_), channel_id=1, source_target_pairs={{0,1},{1,0},{2,3},{3,2},{4,5},{5,4},{6,7},{7,6},{8,9},{9,8},{10,11... | collective-permute-start | bytes 98312 | tf_op jit(solution)/shard_map/ppermute | solution.py:393
  49.1 5.3 %collective-permute-start.11 = (bf16[32,512]{1,0:T(8,128)(2,1)S(1)}, bf16[32,512]{1,0:T(8,128)(2,1)S(1)}, u32[]{:S(2)}, u32[]{:S(2)}) collective-permute-start(bf16[32,512]{1,0:T(8,128)(2,1)S(1)} %get-tuple-element.109), channel_id=1, source_target_pairs={{0,8},{1,13},{4,12},{5,9},{8,0},{9,5},{12,4},{13,1},{2,10},{3,15},... | collective-permute-start | bytes 98312 | tf_op jit(solution)/shard_map/ppermute | solution.py:544
  50.3 5.4 %collective-permute-start.13 = (bf16[32,512]{1,0:T(8,128)(2,1)S(1)}, bf16[32,512]{1,0:T(8,128)(2,1)S(1)}, u32[]{:S(2)}, u32[]{:S(2)}) collective-permute-start(bf16[32,512]{1,0:T(8,128)(2,1)S(1)} %get-tuple-element.119), channel_id=1, source_target_pairs={{0,4},{4,0},{8,12},{12,8},{1,5},{5,1},{9,13},{13,9},{2,6},{6,2},{1... | collective-permute-start | bytes 98312 | tf_op jit(solution)/shard_map/ppermute | solution.py:402
  54.4 1.4 %collective-permute-start.12 = (bf16[32,512]{1,0:T(8,128)(2,1)S(1)}, bf16[32,512]{1,0:T(8,128)(2,1)S(1)}, u32[]{:S(2)}, u32[]{:S(2)}) collective-permute-start(bf16[32,512]{1,0:T(8,128)(2,1)S(1)} %collective-permute-done.11.refs_3_), channel_id=1, source_target_pairs={{0,1},{1,0},{2,3},{3,2},{4,5},{5,4},{6,7},{7,6},{8,9},{9,8},{10,11... | collective-permute-start | bytes 98312 | tf_op jit(solution)/shard_map/ppermute | solution.py:393
  58.3 5.2 %collective-permute-start.14 = (bf16[32,512]{1,0:T(8,128)(2,1)S(1)}, bf16[32,512]{1,0:T(8,128)(2,1)S(1)}, u32[]{:S(2)}, u32[]{:S(2)}) collective-permute-start(bf16[32,512]{1,0:T(8,128)(2,1)S(1)} %get-tuple-element.120), channel_id=1, source_target_pairs={{0,8},{1,13},{4,12},{5,9},{8,0},{9,5},{12,4},{13,1},{2,10},{3,15},... | collective-permute-start | bytes 98312 | tf_op jit(solution)/shard_map/ppermute | solution.py:544
  59.7 5.2 %collective-permute-start.16 = (bf16[32,512]{1,0:T(8,128)(2,1)S(1)}, bf16[32,512]{1,0:T(8,128)(2,1)S(1)}, u32[]{:S(2)}, u32[]{:S(2)}) collective-permute-start(bf16[32,512]{1,0:T(8,128)(2,1)S(1)} %get-tuple-element.130), channel_id=1, source_target_pairs={{0,4},{4,0},{8,12},{12,8},{1,5},{5,1},{9,13},{13,9},{2,6},{6,2},{1... | collective-permute-start | bytes 98312 | tf_op jit(solution)/shard_map/ppermute | solution.py:402
  63.5 1.4 %copy-start.7 = (bf16[512,512]{1,0:T(8,128)(2,1)S(1)}, bf16[512,512]{1,0:T(8,128)(2,1)}, u32[]{:S(2)}) copy-start(bf16[512,512]{1,0:T(8,128)(2,1)} %upstream.1) | copy-start | bytes 1572868
  63.5 1.3 %collective-permute-start.15 = (bf16[32,512]{1,0:T(8,128)(2,1)S(1)}, bf16[32,512]{1,0:T(8,128)(2,1)S(1)}, u32[]{:S(2)}, u32[]{:S(2)}) collective-permute-start(bf16[32,512]{1,0:T(8,128)(2,1)S(1)} %collective-permute-done.14.refs_3_), channel_id=1, source_target_pairs={{0,1},{1,0},{2,3},{3,2},{4,5},{5,4},{6,7},{7,6},{8,9},{9,8},{10,11... | collective-permute-start | bytes 98312 | tf_op jit(solution)/shard_map/ppermute | solution.py:393
  69.8 4.8 %collective-permute-start.17 = (bf16[32,512]{1,0:T(8,128)(2,1)S(1)}, bf16[32,512]{1,0:T(8,128)(2,1)S(1)}, u32[]{:S(2)}, u32[]{:S(2)}) collective-permute-start(bf16[32,512]{1,0:T(8,128)(2,1)S(1)} %get-tuple-element.133), channel_id=1, source_target_pairs={{0,8},{1,13},{4,12},{5,9},{8,0},{9,5},{12,4},{13,1},{2,10},{3,15},... | collective-permute-start | bytes 98312 | tf_op jit(solution)/shard_map/ppermute | solution.py:544
  71.4 5.2 %collective-permute-start.19 = (bf16[32,512]{1,0:T(8,128)(2,1)S(1)}, bf16[32,512]{1,0:T(8,128)(2,1)S(1)}, u32[]{:S(2)}, u32[]{:S(2)}) collective-permute-start(bf16[32,512]{1,0:T(8,128)(2,1)S(1)} %get-tuple-element.137), channel_id=1, source_target_pairs={{4,0},{0,4},{12,8},{8,12},{5,1},{1,5},{13,9},{9,13},{6,2},{2,6},{1... | collective-permute-start | bytes 98312 | tf_op jit(solution)/shard_map/ppermute | solution.py:407
  74.7 1.9 %collective-permute-start.18 = (bf16[32,512]{1,0:T(8,128)(2,1)S(1)}, bf16[32,512]{1,0:T(8,128)(2,1)S(1)}, u32[]{:S(2)}, u32[]{:S(2)}) collective-permute-start(bf16[32,512]{1,0:T(8,128)(2,1)S(1)} %collective-permute-done.17.refs_1_), channel_id=1, source_target_pairs={{0,1},{1,0},{2,3},{3,2},{4,5},{5,4},{6,7},{7,6},{8,9},{9,8},{10,11... | collective-permute-start | bytes 98312 | tf_op jit(solution)/shard_map/ppermute | solution.py:393
  79.1 5.3 %collective-permute-start.20 = (bf16[32,512]{1,0:T(8,128)(2,1)S(1)}, bf16[32,512]{1,0:T(8,128)(2,1)S(1)}, u32[]{:S(2)}, u32[]{:S(2)}) collective-permute-start(bf16[32,512]{1,0:T(8,128)(2,1)S(1)} %get-tuple-element.141), channel_id=1, source_target_pairs={{0,8},{1,13},{4,12},{5,9},{8,0},{9,5},{12,4},{13,1},{2,10},{3,15},... | collective-permute-start | bytes 98312 | tf_op jit(solution)/shard_map/ppermute | solution.py:544
  80.4 5.6 %collective-permute-start.22 = (bf16[32,512]{1,0:T(8,128)(2,1)S(1)}, bf16[32,512]{1,0:T(8,128)(2,1)S(1)}, u32[]{:S(2)}, u32[]{:S(2)}) collective-permute-start(bf16[32,512]{1,0:T(8,128)(2,1)S(1)} %get-tuple-element.146), channel_id=1, source_target_pairs={{4,0},{0,4},{12,8},{8,12},{5,1},{1,5},{13,9},{9,13},{6,2},{2,6},{1... | collective-permute-start | bytes 98312 | tf_op jit(solution)/shard_map/ppermute | solution.py:407
  84.4 1.5 %collective-permute-start.21 = (bf16[32,512]{1,0:T(8,128)(2,1)S(1)}, bf16[32,512]{1,0:T(8,128)(2,1)S(1)}, u32[]{:S(2)}, u32[]{:S(2)}) collective-permute-start(bf16[32,512]{1,0:T(8,128)(2,1)S(1)} %collective-permute-done.20.refs_1_), channel_id=1, source_target_pairs={{0,1},{1,0},{2,3},{3,2},{4,5},{5,4},{6,7},{7,6},{8,9},{9,8},{10,11... | collective-permute-start | bytes 98312 | tf_op jit(solution)/shard_map/ppermute | solution.py:393
  88.8 4.9 %collective-permute-start.23 = (bf16[32,512]{1,0:T(8,128)(2,1)S(1)}, bf16[32,512]{1,0:T(8,128)(2,1)S(1)}, u32[]{:S(2)}, u32[]{:S(2)}) collective-permute-start(bf16[32,512]{1,0:T(8,128)(2,1)S(1)} %get-tuple-element.149), channel_id=1, source_target_pairs={{0,8},{1,13},{4,12},{5,9},{8,0},{9,5},{12,4},{13,1},{2,10},{3,15},... | collective-permute-start | bytes 98312 | tf_op jit(solution)/shard_map/ppermute | solution.py:544
  89.6 6.0 %collective-permute-start.25 = (bf16[32,512]{1,0:T(8,128)(2,1)S(1)}, bf16[32,512]{1,0:T(8,128)(2,1)S(1)}, u32[]{:S(2)}, u32[]{:S(2)}) collective-permute-start(bf16[32,512]{1,0:T(8,128)(2,1)S(1)} %get-tuple-element.154), channel_id=1, source_target_pairs={{4,0},{0,4},{12,8},{8,12},{5,1},{1,5},{13,9},{9,13},{6,2},{2,6},{1... | collective-permute-start | bytes 98312 | tf_op jit(solution)/shard_map/ppermute | solution.py:407
  93.7 1.9 %collective-permute-start.24 = (bf16[32,512]{1,0:T(8,128)(2,1)S(1)}, bf16[32,512]{1,0:T(8,128)(2,1)S(1)}, u32[]{:S(2)}, u32[]{:S(2)}) collective-permute-start(bf16[32,512]{1,0:T(8,128)(2,1)S(1)} %collective-permute-done.23.refs_1_), channel_id=1, source_target_pairs={{0,1},{1,0},{2,3},{3,2},{4,5},{5,4},{6,7},{7,6},{8,9},{9,8},{10,11... | collective-permute-start | bytes 98312 | tf_op jit(solution)/shard_map/ppermute | solution.py:393
  97.0 6.4 %collective-permute-start.26 = (bf16[128,512]{1,0:T(8,128)(2,1)S(1)}, bf16[128,512]{1,0:T(8,128)(2,1)S(1)}, u32[]{:S(2)}, u32[]{:S(2)}) collective-permute-start(bf16[128,512]{1,0:T(8,128)(2,1)S(1)} %get-tuple-element.167), channel_id=1, source_target_pairs={{4,0},{0,4},{12,8},{8,12},{5,1},{1,5},{13,9},{9,13},{6,2},{2,6},{1... | collective-permute-start | bytes 393224 | tf_op jit(solution)/shard_map/ppermute | solution.py:407
  98.2 8.6 %collective-permute-start.29 = (bf16[128,512]{1,0:T(8,128)(2,1)S(1)}, bf16[128,512]{1,0:T(8,128)(2,1)S(1)}, u32[]{:S(2)}, u32[]{:S(2)}) collective-permute-start(bf16[128,512]{1,0:T(8,128)(2,1)S(1)} %get-tuple-element.171), channel_id=1, source_target_pairs={{4,0},{0,4},{12,8},{8,12},{5,1},{1,5},{13,9},{9,13},{6,2},{2,6},{1... | collective-permute-start | bytes 393224 | tf_op jit(solution)/shard_map/ppermute | solution.py:407
  99.1 21.1 %copy-start.1 = (s32[1,4,32]{2,1,0:T(4,128)S(1)}, s32[1,4,32]{2,1,0:T(4,128)}, u32[]{:S(2)}) copy-start(s32[1,4,32]{2,1,0:T(4,128)} %param.22) | copy-start | bytes 1540
  103.5 15.5 %collective-permute-start.27 = (bf16[256,512]{1,0:T(8,128)(2,1)S(1)}, bf16[256,512]{1,0:T(8,128)(2,1)S(1)}, u32[]{:S(2)}, u32[]{:S(2)}) collective-permute-start(bf16[256,512]{1,0:T(8,128)(2,1)S(1)} %get-tuple-element.169), channel_id=1, source_target_pairs={{4,0},{0,4},{12,8},{8,12},{5,1},{1,5},{13,9},{9,13},{6,2},{2,6},{1... | collective-permute-start | bytes 786440 | tf_op jit(solution)/shard_map/ppermute | solution.py:407
  104.6 9.6 %collective-permute-start.28 = (bf16[128,512]{1,0:T(8,128)(2,1)S(1)}, bf16[128,512]{1,0:T(8,128)(2,1)S(1)}, u32[]{:S(2)}, u32[]{:S(2)}) collective-permute-start(bf16[128,512]{1,0:T(8,128)(2,1)S(1)} %get-tuple-element.170), channel_id=1, source_target_pairs={{8,0},{12,4},{0,8},{4,12},{9,1},{13,5},{1,9},{5,13},{10,2},{14,6},... | collective-permute-start | bytes 393224 | tf_op jit(solution)/shard_map/ppermute | solution.py:407
  106.9 12.0 %collective-permute-start.30 = (bf16[128,512]{1,0:T(8,128)(2,1)S(1)}, bf16[128,512]{1,0:T(8,128)(2,1)S(1)}, u32[]{:S(2)}, u32[]{:S(2)}) collective-permute-start(bf16[128,512]{1,0:T(8,128)(2,1)S(1)} %shard_map.194), channel_id=1, source_target_pairs={{8,0},{12,4},{0,8},{4,12},{9,1},{13,5},{1,9},{5,13},{10,2},{14,6},... | collective-permute-start | bytes 393224 | tf_op jit(solution)/shard_map/ppermute | solution.py:407

commit v13 on v12

--- a/solution.py
+++ b/solution.py
@@ -95,7 +95,9 @@
     return run
 
 
-def place_kernel(slots, receivers, order, here, there, halo_here, halo_there, list_here, list_there):
+def place_kernel(
+    slots, receivers, order, latents, here, there, halo_here, halo_there, list_here, list_there, kept
+):
     nodes = here.shape[1] // 2
     wide = halo_here.shape[1]
 
@@ -116,6 +118,7 @@
         end = min(at + LANES, count)
         list_here[at:end, :] = pick_rows(upright(order[:, at:end]), 0, nodes)
     list_there[...] = pick_columns(order[...], 0, nodes)
+    kept[...] = dot(list_here[...], latents[...]).astype(bf16)
 
 
 def note_kernel(rows, shards, nodes, payload, shard_rows, node_rows, arrived):
@@ -208,16 +211,15 @@
     return (hidden.astype(f32) + agg * norm_scale(agg) * gain_row).astype(bf16), agg
 
 
-def listed_update(list_here, total, hidden, w_out, gain_row, w_send):
-    picks = list_here[...]
-    rows, kept = dot(picks, total).astype(bf16), dot(picks, hidden)
+def listed_update(list_here, total, kept, w_out, gain_row, w_send):
+    rows = dot(list_here[...], total).astype(bf16)
     return 0.5 * dot(updated(kept, rows, w_out, gain_row)[0], w_send)
 
 
 def start_kernel(halves, *refs):
     meta = refs[0]
     parts = refs[1 : 1 + halves]
-    mesh_init, w_enc_out, gain, w_send, list_here, whole = refs[1 + halves : 7 + halves]
+    kept, w_enc_out, gain, w_send, list_here, whole = refs[1 + halves : 7 + halves]
     part = parts[0].shape[0]
     own = meta[0:1, :]
     for at in range(halves):
@@ -226,11 +228,13 @@
             rows = jnp.where(own == (at - shift) % halves, parts[shift][...].astype(f32), rows)
         whole[at * part : (at + 1) * part, :] = rows.astype(bf16)
     hand_out(
-        listed_update(list_here, whole[...], mesh_init[...], w_enc_out[...], gain[...], w_send[0]), refs[7 + halves :]
+        listed_update(list_here, whole[...], kept[...], w_enc_out[...], gain[...], w_send[0]), refs[7 + halves :]
     )
 
 
-def local_kernel(layer, total, hidden, w_out, gain, w_send, w_recv, here, hidden_out, agg_out, pre, table):
+def local_kernel(
+    layer, total, hidden, w_out, gain, w_send, w_recv, here, list_here, hidden_out, agg_out, pre, table, kept_out
+):
     nodes = hidden.shape[0]
     if layer:
         fresh, agg = updated(hidden[...], total[...], w_out[layer - 1], gain[layer - 1 : layer, :])
@@ -238,6 +242,7 @@
         fresh, agg = updated(hidden[...], total[...], w_out[...], gain[...])
     hidden_out[...] = fresh
     agg_out[...] = agg
+    kept_out[...] = dot(list_here[...], fresh).astype(bf16)
     table[0:nodes, :] = (0.5 * dot(fresh, w_send[layer])).astype(bf16)
     table[nodes:, :] = (0.5 * dot(fresh, w_recv[layer])).astype(bf16)
     for at in range(0, pre.shape[0], BLOCK):
@@ -273,7 +278,7 @@
 
 
 def layer_kernel(layer, shifts, *refs):
-    hidden, pres = refs[0], refs[1:3]
+    kept, pres = refs[0], refs[1:3]
     halos, refs = refs[3 : 3 + shifts], refs[3 + shifts :]
     halo_here, there, w_out, gain, w_send, list_here = refs[:6]
     total_out, slope_out = refs[6:8]
@@ -281,7 +286,7 @@
     total = node_sum(pres, halos, halo_here, there, slope_out, *refs[-2:]).astype(bf16)
     total_out[...] = total
     gain_row = gain[layer : layer + 1, :]
-    hand_out(listed_update(list_here, total, hidden[...], w_out[layer], gain_row, w_send[layer + 1]), outs)
+    hand_out(listed_update(list_here, total, kept[...], w_out[layer], gain_row, w_send[layer + 1]), outs)
 
 
 def edge_grads(listed, grad_agg, w_out, here, halo_there, slope, grad_pre, outs):
@@ -480,7 +485,7 @@
         all_slots = all_slots + jnp.where(turned, jnp.where(entry < depth, depth, -depth), 0)
     readers = partner(shard, steps, shards)
     lists = jnp.take(halo_index[0], readers, axis=0).reshape(1, -1)
-    here, there, halo_here, halo_there, list_here, list_there = call(
+    here, there, halo_here, halo_there, list_here, list_there, kept = call(
         place_kernel,
         [
             ((all_edges, 2 * nodes), bf16),
@@ -489,9 +494,10 @@
             ((wide, all_edges), bf16),
             ((listed_rows, nodes), bf16),
             ((nodes, listed_rows), bf16),
+            ((listed_rows, width), bf16),
         ],
         products=[(all_edges, nodes, width), (all_edges, 2 * nodes, width)],
-    )(all_slots, all_receivers, lists)
+    )(all_slots, all_receivers, lists, mesh_init)
 
     if relayed:
         across, list_here = lax.optimization_barrier((across, list_here))
@@ -550,7 +556,7 @@
 
     listed_products = [(listed_rows, width, width)] * 2 + [(listed_rows, nodes, width)] * 2
     total, *outgoing = call(functools.partial(start_kernel, halves), [node_bf16] + listed, (), listed_products)(
-        meta, *parts, mesh_init, w_enc_out, enc_gain, w_send, list_here
+        meta, *parts, kept, w_enc_out, enc_gain, w_send, list_here
     )
 
     half_f32, edge_bf16 = ((all_edges // 2, width), f32), ((all_edges, width), bf16)
@@ -564,11 +570,11 @@
         weights = (w_out, layer_gain) if layer else (w_enc_out, enc_gain)
         early = call(
             functools.partial(local_kernel, layer),
-            [node_bf16, node_f32, half_f32, ((2 * nodes, width), bf16)],
+            [node_bf16, node_f32, half_f32, ((2 * nodes, width), bf16), back_halo],
             (),
             [square, square, square, half_product],
-        )(total, hidden, *weights, w_send, w_recv, here)
-        halos, (hidden, agg, pre, both_tables) = exchange(outgoing, sent_to, early)
+        )(total, hidden, *weights, w_send, w_recv, here, list_here)
+        halos, (hidden, agg, pre, both_tables, kept) = exchange(outgoing, sent_to, early)
         (more,) = call(local_more_kernel, [half_f32], (), [half_product])(both_tables, here)
         sums.append(agg)
         if layer == LAYERS - 1:
@@ -578,7 +584,7 @@
             [node_bf16, edge_bf16] + listed,
             [halo, edge_bf16],
             forward_products[:2] + listed_products,
-        )(hidden, pre, more, *halos, halo_here, there, w_out, layer_gain, w_send, list_here)
+        )(kept, pre, more, *halos, halo_here, there, w_out, layer_gain, w_send, list_here)
         slopes.append(slope)
     enc_sum, records = sums[0], list(zip(sums[1:], slopes))
     final_mesh, grad_pre, *outgoing = call(

time: 120 us -> 121 us (level)
  starting transfers between devices: 35.6 us -> 33.9 us
    pallas_call x29, Pallas kernels: 46.9 us -> 48.1 us  [run(): pl.pallas_call(body, out_shape=tuple((jax.ShapeDtypeStruct(shape, dtype)...]
  transfers between devices with their start and end apart: 31 -> 31, of which waited for: 12 -> 14; matrix products, arithmetic and copies ran while one was open for 2% -> 2% of each run, Pallas kernels for 22% -> 23%
where the time goes in v13:
time: 121 us
  Pallas kernels  48.1 us (40%)
  waiting for transfers between devices  34 us (28%)
  starting transfers between devices  33.9 us (28%)
  local copies, waits for them, and re-layouts  2.13 us (2%)
  other arithmetic  1.83 us (2%)
    pallas_call x29, Pallas kernels, run(): pl.pallas_call(body, out_shape=tuple((jax.ShapeDtypeStruct(shape, dtype)...  48.1 us
    ppermute x8, waiting for transfers between devices, sent_back(): lax.ppermute(value, 'mesh', [(partner(at, step, size), at) for at in rang...  15 us
    ppermute x11, waiting for transfers between devices, shifted(): lax.ppermute(value, axis, [(at, (at + by) % size) for at in range(size)])  12.4 us
    ppermute x8, starting transfers between devices, sent_back(): lax.ppermute(value, 'mesh', [(partner(at, step, size), at) for at in rang...  11.7 us
    ppermute x6, starting transfers between devices, sent_to(): lax.ppermute(value, 'mesh', [(at, partner(at, step, size)) for at in rang...  11 us
    ppermute x6, starting transfers between devices, exchange(): lax.ppermute(blocks[0], ('mesh', 'rep'), [(2 * at + side, 2 * (at ^ 2 + s...  6.81 us
    ppermute x6, waiting for transfers between devices, sent_to(): lax.ppermute(value, 'mesh', [(at, partner(at, step, size)) for at in rang...  4.96 us
    ppermute x11, starting transfers between devices, shifted(): lax.ppermute(value, axis, [(at, (at + by) % size) for at in range(size)])  4.41 us
  transfers between devices with their start and end apart: 31, of which 14 were waited for; matrix products, arithmetic and copies ran while one was open for 2% of the time, Pallas kernels for 23%

profile of v13, /device:TPU:0, one launch (start us, length us, event | category | flops | bytes accessed | tf_op | source)
XLA Modules:
  0.0 121.0 jit_solution(4652781387667618906)
XLA Ops:
  0.6 1.0 shard_map.167.refs_5_
  1.7 3.1 %collective-permute-start.3 = (bf16[272,512]{1,0:T(8,128)(2,1)S(1)}, bf16[272,512]{1,0:T(8,128)(2,1)S(1)}, u32[]{:S(2)}, u32[]{:S(2)}) collective-permute-start(bf16[272,512]{1,0:T(8,128)(2,1)S(1)} %shard_map.167.refs_5_), channel_id=1, source_target_pairs={{0,4},{4,0},{8,12},{12,8},{1,5},{5,1},{9,13},{13,9},{2,6},{6,2},{1... | collective-permute-start | bytes 835592 | tf_op jit(solution)/shard_map/ppermute | solution.py:407
  4.8 2.6 %collective-permute-start = (bf16[272,512]{1,0:T(8,128)(2,1)S(1)}, bf16[272,512]{1,0:T(8,128)(2,1)S(1)}, u32[]{:S(2)}, u32[]{:S(2)}) collective-permute-start(bf16[272,512]{1,0:T(8,128)(2,1)S(1)} %shard_map.167.refs_5_), channel_id=1, source_target_pairs={{0,8},{4,12},{8,0},{12,4},{1,9},{5,13},{9,1},{13,5},{2,10},{6,14},... | collective-permute-start | bytes 835592 | tf_op jit(solution)/shard_map/ppermute | solution.py:407
  7.3 0.7 compare_select_fusion.1
  8.0 0.7 fusion.11
  8.8 0.6 gather_fusion
  10.1 1.6 %collective-permute-start.2 = (s32[2,2,512]{2,0,1:T(2,128)S(1)}, s32[2,2,512]{2,0,1:T(2,128)S(1)}, u32[]{:S(2)}, u32[]{:S(2)}) collective-permute-start(s32[2,2,512]{2,0,1:T(2,128)S(1)} %fusion.1), channel_id=1, source_target_pairs={{0,2},{2,0},{1,3},{3,1},{4,6},{6,4},{5,7},{7,5},{8,10},{10,8},{9,1... | collective-permute-start | bytes 24584 | tf_op jit(solution)/shard_map/ppermute | solution.py:398
  11.7 2.1 %collective-permute-done.2 = s32[2,2,512]{2,0,1:T(2,128)S(1)} collective-permute-done((s32[2,2,512]{2,0,1:T(2,128)S(1)}, s32[2,2,512]{2,0,1:T(2,128)S(1)}, u32[]{:S(2)}, u32[]{:S(2)}) %collective-permute-start.2) | collective-permute-done | bytes 8224 | tf_op jit(solution)/shard_map/ppermute | solution.py:398
  14.0 1.0 copy-done.8
  15.0 3.7 %shard_map.168 = (bf16[2048,1024]{1,0:T(8,128)(2,1)S(1)}, bf16[1024,2048]{1,0:T(8,128)(2,1)S(1)}, bf16[2048,128]{1,0:T(8,128)(2,1)S(1)}, bf16[128,2048]{1,0:T(8,...) custom-call(s32[1,2048]{1,0:T(1,128)S(1)} %fusion.2.slots, ...), custom_call_target="tpu_custom_call" | custom-call | flops 3221225472 | bytes 10273152 | tf_op jit(solution)/shard_map/pallas_call | solution.py:83
  18.7 1.1 collective-permute-done.refs_4_
  19.8 0.4 collective-permute-start.4
  20.4 1.6 %shard_map.169 = (bf16[256,512]{1,0:T(8,128)(2,1)S(1)}, bf16[256,512]{1,0:T(8,128)(2,1)S(1)}, bf16[256,512]{1,0:T(8,128)(2,1)S(1)}, bf16[256,512]{1,0:T(8,128)(2...) custom-call(s32[2,512]{1,0:T(2,128)S(1)} %broadcast_in_dim.27.refs_0_, bf16[512,512]{1,0:T(8,128)(2,1)S(1)} %copy-done.8, ...), custom_call_target="tpu_custom_call" | custom-call | flops 1073741824 | bytes 4853760 | tf_op jit(solution)/shard_map/pallas_call | solution.py:83
  22.0 0.8 shard_map.170
  22.8 3.8 %collective-permute-done.4.refs_4_ = bf16[272,512]{1,0:T(8,128)(2,1)S(1)} collective-permute-done((bf16[272,512]{1,0:T(8,128)(2,1)S(1)}, bf16[272,512]{1,0:T(8,128)(2,1)S(1)}, u32[]{:S(2)}, u32[]{:S(2)}) %collective-permute-start.4) | collective-permute-done | bytes 278560 | tf_op jit(solution)/shard_map/ppermute | solution.py:407
  26.6 0.8 shard_map.171
  27.6 1.5 %collective-permute-done.5 = bf16[256,512]{1,0:T(8,128)(2,1)S(1)} collective-permute-done((bf16[256,512]{1,0:T(8,128)(2,1)S(1)}, bf16[256,512]{1,0:T(8,128)(2,1)S(1)}, u32[]{:S(2)}, u32[]{:S(2)}) %collective-permute-start.5) | collective-permute-done | bytes 262176 | tf_op jit(solution)/shard_map/ppermute | solution.py:398
  29.2 1.6 %collective-permute-start.6 = (bf16[256,512]{1,0:T(8,128)(2,1)S(1)}, bf16[256,512]{1,0:T(8,128)(2,1)S(1)}, u32[]{:S(2)}, u32[]{:S(2)}) collective-permute-start(bf16[256,512]{1,0:T(8,128)(2,1)S(1)} %add_convert_fusion.1), channel_id=1, source_target_pairs={{0,2},{2,0},{1,3},{3,1},{4,6},{6,4},{5,7},{7,5},{8,10},{10,8},{9,1... | collective-permute-start | bytes 786440 | tf_op jit(solution)/shard_map/ppermute | solution.py:398
  30.7 6.9 %collective-permute-done.6 = bf16[256,512]{1,0:T(8,128)(2,1)S(1)} collective-permute-done((bf16[256,512]{1,0:T(8,128)(2,1)S(1)}, bf16[256,512]{1,0:T(8,128)(2,1)S(1)}, u32[]{:S(2)}, u32[]{:S(2)}) %collective-permute-start.6) | collective-permute-done | bytes 262176 | tf_op jit(solution)/shard_map/ppermute | solution.py:398
  37.7 1.5 %collective-permute-done.7.refs_2_ = bf16[256,512]{1,0:T(8,128)(2,1)S(1)} collective-permute-done((bf16[256,512]{1,0:T(8,128)(2,1)S(1)}, bf16[256,512]{1,0:T(8,128)(2,1)S(1)}, u32[]{:S(2)}, u32[]{:S(2)}) %collective-permute-start.7) | collective-permute-done | bytes 262176 | tf_op jit(solution)/shard_map/ppermute | solution.py:398
  39.3 0.7 shard_map.172
  40.0 1.0 collective-permute-start.8
  41.0 1.9 %collective-permute-start.10 = (bf16[32,512]{1,0:T(8,128)(2,1)S(1)}, bf16[32,512]{1,0:T(8,128)(2,1)S(1)}, u32[]{:S(2)}, u32[]{:S(2)}) collective-permute-start(bf16[32,512]{1,0:T(8,128)(2,1)S(1)} %get-tuple-element.113), channel_id=1, source_target_pairs={{0,4},{4,0},{8,12},{12,8},{1,5},{5,1},{9,13},{13,9},{2,6},{6,2},{1... | collective-permute-start | bytes 98312 | tf_op jit(solution)/shard_map/ppermute | solution.py:407
  42.9 2.5 %shard_map.173 = (bf16[512,512]{1,0:T(8,128)(2,1)S(1)}, f32[512,512]{1,0:T(8,128)S(1)}, f32[1024,512]{1,0:T(8,128)S(1)}, bf16[1024,512]{1,0:T(8,128)(2,1)S(1)}, bf16[96,512]{1,0:T(8,128)(2,1)S(1)}) custom-call(bf16[512,512]{1,0:T(8,128)(2,1)S(1)} %get-tuple-element.102.total, bf16[512,512]{1,0:T(8,128)(2,1)S(1)} %copy-done.9, ...), custom_call_target="tpu_custom_call" | custom-call | flops 1879048192 | bytes 13830144 | tf_op jit(solution)/shard_map/pallas_call | solution.py:83
  45.5 1.3 %shard_map.174.refs_2_ = f32[1024,512]{1,0:T(8,128)S(1)} custom-call(bf16[1024,512]{1,0:T(8,128)(2,1)S(1)} %get-tuple-element.111.table, bf16[2048,1024]{1,0:T(8,128)(2,1)S(1)} %get-tuple-element.103.here.refs_10_), custom_call_target="tpu_custom_call" | custom-call | flops 1073741824 | bytes 7340032 | tf_op jit(solution)/shard_map/pallas_call | solution.py:83
  46.9 2.5 %shard_map.175 = (bf16[512,512]{1,0:T(8,128)(2,1)S(1)}, bf16[2048,512]{1,0:T(8,128)(2,1)S(1)}, bf16[32,512]{1,0:T(8,128)(2,1)S(1)}, bf16[32,512]{1,0:T(8,128)(2,1)S(1)}) custom-call(bf16[96,512]{1,0:T(8,128)(2,1)S(1)} %get-tuple-element.109.refs_0_, f32[1024,512]{1,0:T(8,128)S(1)} %get-tuple-element.110.refs_1_, f32[1024,512]{1,0:T(8,128)S(1)} %shard_map.174.refs_2_, ...), custom_call_target="tpu_custom_call" | custom-call | flops 1543503872 | bytes 15046656 | tf_op jit(solution)/shard_map/pallas_call | solution.py:83
  49.5 1.1 collective-permute-start.11
  50.6 1.6 %collective-permute-start.13 = (bf16[32,512]{1,0:T(8,128)(2,1)S(1)}, bf16[32,512]{1,0:T(8,128)(2,1)S(1)}, u32[]{:S(2)}, u32[]{:S(2)}) collective-permute-start(bf16[32,512]{1,0:T(8,128)(2,1)S(1)} %get-tuple-element.128), channel_id=1, source_target_pairs={{0,4},{4,0},{8,12},{12,8},{1,5},{5,1},{9,13},{13,9},{2,6},{6,2},{1... | collective-permute-start | bytes 98312 | tf_op jit(solution)/shard_map/ppermute | solution.py:407
  52.1 2.4 %shard_map.176 = (bf16[512,512]{1,0:T(8,128)(2,1)S(1)}, f32[512,512]{1,0:T(8,128)S(1)}, f32[1024,512]{1,0:T(8,128)S(1)}, bf16[1024,512]{1,0:T(8,128)(2,1)S(1)}, bf16[96,512]{1,0:T(8,128)(2,1)S(1)}) custom-call(bf16[512,512]{1,0:T(8,128)(2,1)S(1)} %get-tuple-element.117.total, bf16[512,512]{1,0:T(8,128)(2,1)S(1)} %get-tuple-element.118.hidden, ...), custom_call_target="tpu_custom_call" | custom-call | flops 1879048192 | bytes 14882816 | tf_op jit(solution)/shard_map/pallas_call | solution.py:83
  54.9 1.2 %shard_map.177.refs_2_ = f32[1024,512]{1,0:T(8,128)S(1)} custom-call(bf16[1024,512]{1,0:T(8,128)(2,1)S(1)} %get-tuple-element.126.table, bf16[2048,1024]{1,0:T(8,128)(2,1)S(1)} %get-tuple-element.103.here.refs_10_), custom_call_target="tpu_custom_call" | custom-call | flops 1073741824 | bytes 7340032 | tf_op jit(solution)/shard_map/pallas_call | solution.py:83
  56.1 2.7 %shard_map.178 = (bf16[512,512]{1,0:T(8,128)(2,1)S(1)}, bf16[2048,512]{1,0:T(8,128)(2,1)S(1)}, bf16[32,512]{1,0:T(8,128)(2,1)S(1)}, bf16[32,512]{1,0:T(8,128)(2,1)S(1)}) custom-call(bf16[96,512]{1,0:T(8,128)(2,1)S(1)} %get-tuple-element.124.refs_0_, f32[1024,512]{1,0:T(8,128)S(1)} %get-tuple-element.125.refs_1_, f32[1024,512]{1,0:T(8,128)S(1)} %shard_map.177.refs_2_, ...), custom_call_target="tpu_custom_call" | custom-call | flops 1543503872 | bytes 15046656 | tf_op jit(solution)/shard_map/pallas_call | solution.py:83
  58.8 1.5 %collective-permute-start.14 = (bf16[32,512]{1,0:T(8,128)(2,1)S(1)}, bf16[32,512]{1,0:T(8,128)(2,1)S(1)}, u32[]{:S(2)}, u32[]{:S(2)}) collective-permute-start(bf16[32,512]{1,0:T(8,128)(2,1)S(1)} %get-tuple-element.129), channel_id=1, source_target_pairs={{0,8},{1,13},{4,12},{5,9},{8,0},{9,5},{12,4},{13,1},{2,10},{3,15},... | collective-permute-start | bytes 98312 | tf_op jit(solution)/shard_map/ppermute | solution.py:550
  60.3 1.4 %collective-permute-start.16 = (bf16[32,512]{1,0:T(8,128)(2,1)S(1)}, bf16[32,512]{1,0:T(8,128)(2,1)S(1)}, u32[]{:S(2)}, u32[]{:S(2)}) collective-permute-start(bf16[32,512]{1,0:T(8,128)(2,1)S(1)} %get-tuple-element.140), channel_id=1, source_target_pairs={{0,4},{4,0},{8,12},{12,8},{1,5},{5,1},{9,13},{13,9},{2,6},{6,2},{1... | collective-permute-start | bytes 98312 | tf_op jit(solution)/shard_map/ppermute | solution.py:407
  61.7 2.8 %shard_map.179 = (bf16[512,512]{1,0:T(8,128)(2,1)S(1)}, f32[512,512]{1,0:T(8,128)S(1)}, f32[1024,512]{1,0:T(8,128)S(1)}, bf16[1024,512]{1,0:T(8,128)(2,1)S(1)}, bf16[96,512]{1,0:T(8,128)(2,1)}) custom-call(bf16[512,512]{1,0:T(8,128)(2,1)S(1)} %get-tuple-element.130.total, bf16[512,512]{1,0:T(8,128)(2,1)S(1)} %get-tuple-element.131.hidden, ...), custom_call_target="tpu_custom_call" | custom-call | flops 1879048192 | bytes 14882816 | tf_op jit(solution)/shard_map/pallas_call | solution.py:83
  64.5 1.2 %shard_map.180.refs_2_ = f32[1024,512]{1,0:T(8,128)S(1)} custom-call(bf16[1024,512]{1,0:T(8,128)(2,1)S(1)} %get-tuple-element.138.table, bf16[2048,1024]{1,0:T(8,128)(2,1)S(1)} %get-tuple-element.103.here.refs_10_), custom_call_target="tpu_custom_call" | custom-call | flops 1073741824 | bytes 7340032 | tf_op jit(solution)/shard_map/pallas_call | solution.py:83
  65.8 5.0 %shard_map.181 = (bf16[512,512]{1,0:T(8,128)(2,1)}, bf16[2048,512]{1,0:T(8,128)(2,1)S(1)}, bf16[32,512]{1,0:T(8,128)(2,1)S(1)}, bf16[32,512]{1,0:T(8,128)(2,1)S(1)}) custom-call(bf16[512,512]{1,0:T(8,128)(2,1)S(1)} %get-tuple-element.136.refs_0_, f32[1024,512]{1,0:T(8,128)S(1)} %get-tuple-element.137.refs_1_, f32[1024,512]{1,0:T(8,128)S(1)} %shard_map.180.refs_2_, ...), custom_call_target="tpu_custom_call" | custom-call | flops 3221225472 | bytes 19044352 | tf_op jit(solution)/shard_map/pallas_call | solution.py:83
  70.8 1.3 %collective-permute-start.17 = (bf16[32,512]{1,0:T(8,128)(2,1)S(1)}, bf16[32,512]{1,0:T(8,128)(2,1)S(1)}, u32[]{:S(2)}, u32[]{:S(2)}) collective-permute-start(bf16[32,512]{1,0:T(8,128)(2,1)S(1)} %get-tuple-element.143), channel_id=1, source_target_pairs={{0,8},{1,13},{4,12},{5,9},{8,0},{9,5},{12,4},{13,1},{2,10},{3,15},... | collective-permute-start | bytes 98312 | tf_op jit(solution)/shard_map/ppermute | solution.py:550
  72.1 1.4 %collective-permute-start.19 = (bf16[32,512]{1,0:T(8,128)(2,1)S(1)}, bf16[32,512]{1,0:T(8,128)(2,1)S(1)}, u32[]{:S(2)}, u32[]{:S(2)}) collective-permute-start(bf16[32,512]{1,0:T(8,128)(2,1)S(1)} %get-tuple-element.147), channel_id=1, source_target_pairs={{4,0},{0,4},{12,8},{8,12},{5,1},{1,5},{13,9},{9,13},{6,2},{2,6},{1... | collective-permute-start | bytes 98312 | tf_op jit(solution)/shard_map/ppermute | solution.py:412
  73.5 1.5 %shard_map.182.upstream = f32[512,512]{1,0:T(8,128)S(1)} custom-call(bf16[512,512]{1,0:T(8,128)(2,1)S(1)} %copy-done.7, bf16[2048,512]{1,0:T(8,128)(2,1)S(1)} %get-tuple-element.144.grad_pre, bf16[1024,2048]{1,0:T(8,128)(2,1)S(1)} %get-tuple-element.115.refs_7_.there, bf16[3,512,512]{2,1,0:T(8,128)(2,1)S(1)} %copy-done.2), custom_call_target="tpu_custom_call" | custom-call | flops 1342177280 | bytes 9437184 | tf_op jit(solution)/shard_map/pallas_call | solution.py:83
  75.0 0.6 collective-permute-done.17.refs_1_
  75.9 1.5 %shard_map.183.refs_0_ = f32[512,512]{1,0:T(8,128)S(1)} custom-call(f32[512,512]{1,0:T(8,128)S(1)} %shard_map.182.upstream, bf16[2048,512]{1,0:T(8,128)(2,1)S(1)} %get-tuple-element.144.grad_pre, bf16[1024,2048]{1,0:T(8,128)(2,1)S(1)} %get-tuple-element.115.refs_7_.there, bf16[3,512,512]{2,1,0:T(8,128)(2,1)S(1)} %copy-done.4), custom_call_target="tpu_custom_call" | custom-call | flops 1342177280 | bytes 9961472 | tf_op jit(solution)/shard_map/pallas_call | solution.py:83
  77.5 2.6 %shard_map.184 = (f32[512,512]{1,0:T(8,128)S(1)}, bf16[2048,512]{1,0:T(8,128)(2,1)S(1)}, bf16[32,512]{1,0:T(8,128)(2,1)S(1)}, bf16[32,512]{1,0:T(8,128)(2,1)S(1)}) custom-call(f32[512,512]{1,0:T(8,128)S(1)} %shard_map.183.refs_0_, bf16[32,512]{1,0:T(8,128)(2,1)S(1)} %collective-permute-done.17.refs_1_, bf16[32,512]{1,0:T(8,128)(2,1)S(1)} %collective-permute-done.18.refs_2_, ...), custom_call_target="tpu_custom_call" | custom-call | flops 1711276032 | bytes 15472640 | tf_op jit(solution)/shard_map/pallas_call | solution.py:83
  80.1 1.1 collective-permute-start.20
  81.2 2.0 %collective-permute-start.22 = (bf16[32,512]{1,0:T(8,128)(2,1)S(1)}, bf16[32,512]{1,0:T(8,128)(2,1)S(1)}, u32[]{:S(2)}, u32[]{:S(2)}) collective-permute-start(bf16[32,512]{1,0:T(8,128)(2,1)S(1)} %get-tuple-element.156), channel_id=1, source_target_pairs={{4,0},{0,4},{12,8},{8,12},{5,1},{1,5},{13,9},{9,13},{6,2},{2,6},{1... | collective-permute-start | bytes 98312 | tf_op jit(solution)/shard_map/ppermute | solution.py:412
  83.2 1.5 %shard_map.185.upstream = f32[512,512]{1,0:T(8,128)S(1)} custom-call(f32[512,512]{1,0:T(8,128)S(1)} %get-tuple-element.152.upstream, bf16[2048,512]{1,0:T(8,128)(2,1)S(1)} %get-tuple-element.153.grad_pre, bf16[1024,2048]{1,0:T(8,128)(2,1)S(1)} %get-tuple-element.115.refs_7_.there, bf16[3,512,512]{2,1,0:T(8,128)(2,1)S(1)} %copy-done.2), custom_call_target="tpu_custom_call" | custom-call | flops 1342177280 | bytes 9961472 | tf_op jit(solution)/shard_map/pallas_call | solution.py:83
  84.8 0.6 collective-permute-done.20.refs_1_
  85.4 1.5 %shard_map.186.refs_0_ = f32[512,512]{1,0:T(8,128)S(1)} custom-call(f32[512,512]{1,0:T(8,128)S(1)} %shard_map.185.upstream, bf16[2048,512]{1,0:T(8,128)(2,1)S(1)} %get-tuple-element.153.grad_pre, bf16[1024,2048]{1,0:T(8,128)(2,1)S(1)} %get-tuple-element.115.refs_7_.there, bf16[3,512,512]{2,1,0:T(8,128)(2,1)S(1)} %copy-done.4), custom_call_target="tpu_custom_call" | custom-call | flops 1342177280 | bytes 9961472 | tf_op jit(solution)/shard_map/pallas_call | solution.py:83
  86.9 2.8 %shard_map.187 = (f32[512,512]{1,0:T(8,128)S(1)}, bf16[2048,512]{1,0:T(8,128)(2,1)S(1)}, bf16[32,512]{1,0:T(8,128)(2,1)S(1)}, bf16[32,512]{1,0:T(8,128)(2,1)S(1)}) custom-call(f32[512,512]{1,0:T(8,128)S(1)} %shard_map.186.refs_0_, bf16[32,512]{1,0:T(8,128)(2,1)S(1)} %collective-permute-done.20.refs_1_, bf16[32,512]{1,0:T(8,128)(2,1)S(1)} %collective-permute-done.21.refs_2_, ...), custom_call_target="tpu_custom_call" | custom-call | flops 1711276032 | bytes 15472640 | tf_op jit(solution)/shard_map/pallas_call | solution.py:83
  89.7 0.7 collective-permute-start.23
  90.4 2.3 %collective-permute-start.25 = (bf16[32,512]{1,0:T(8,128)(2,1)S(1)}, bf16[32,512]{1,0:T(8,128)(2,1)S(1)}, u32[]{:S(2)}, u32[]{:S(2)}) collective-permute-start(bf16[32,512]{1,0:T(8,128)(2,1)S(1)} %get-tuple-element.164), channel_id=1, source_target_pairs={{4,0},{0,4},{12,8},{8,12},{5,1},{1,5},{13,9},{9,13},{6,2},{2,6},{1... | collective-permute-start | bytes 98312 | tf_op jit(solution)/shard_map/ppermute | solution.py:412
  92.8 1.5 %shard_map.188.upstream = f32[512,512]{1,0:T(8,128)S(1)} custom-call(f32[512,512]{1,0:T(8,128)S(1)} %get-tuple-element.160.upstream, bf16[2048,512]{1,0:T(8,128)(2,1)S(1)} %get-tuple-element.161.grad_pre, bf16[1024,2048]{1,0:T(8,128)(2,1)S(1)} %get-tuple-element.115.refs_7_.there, bf16[3,512,512]{2,1,0:T(8,128)(2,1)S(1)} %copy-done.2), custom_call_target="tpu_custom_call" | custom-call | flops 1342177280 | bytes 9961472 | tf_op jit(solution)/shard_map/pallas_call | solution.py:83
  94.6 0.5 collective-permute-start.24
  95.1 1.5 %shard_map.189.refs_0_ = f32[512,512]{1,0:T(8,128)S(1)} custom-call(f32[512,512]{1,0:T(8,128)S(1)} %shard_map.188.upstream, bf16[2048,512]{1,0:T(8,128)(2,1)S(1)} %get-tuple-element.161.grad_pre, bf16[1024,2048]{1,0:T(8,128)(2,1)S(1)} %get-tuple-element.115.refs_7_.there, bf16[3,512,512]{2,1,0:T(8,128)(2,1)S(1)} %copy-done.4), custom_call_target="tpu_custom_call" | custom-call | flops 1342177280 | bytes 9961472 | tf_op jit(solution)/shard_map/pallas_call | solution.py:83
  96.7 1.4 %shard_map.190 = (bf16[512,512]{1,0:T(8,128)(2,1)S(1)}, bf16[128,512]{1,0:T(8,128)(2,1)S(1)}, bf16[128,512]{1,0:T(8,128)(2,1)S(1)}) custom-call(f32[512,512]{1,0:T(8,128)S(1)} %shard_map.189.refs_0_, bf16[32,512]{1,0:T(8,128)(2,1)S(1)} %collective-permute-done.23.refs_1_, bf16[32,512]{1,0:T(8,128)(2,1)S(1)} %collective-permute-done.24.refs_2_, ...), custom_call_target="tpu_custom_call" | custom-call | flops 503316480 | bytes 5703680 | tf_op jit(solution)/shard_map/pallas_call | solution.py:83
  98.1 0.9 collective-permute-start.26
  99.0 1.1 collective-permute-start.29
  100.2 0.6 shard_map.191
  100.7 3.8 %collective-permute-done.26.passed = bf16[128,512]{1,0:T(8,128)(2,1)S(1)} collective-permute-done((bf16[128,512]{1,0:T(8,128)(2,1)S(1)}, bf16[128,512]{1,0:T(8,128)(2,1)S(1)}, u32[]{:S(2)}, u32[]{:S(2)}) %collective-permute-start.26) | collective-permute-done | bytes 131104 | tf_op jit(solution)/shard_map/ppermute | solution.py:412
  104.5 0.9 collective-permute-start.27
  105.4 2.0 %collective-permute-start.28 = (bf16[128,512]{1,0:T(8,128)(2,1)S(1)}, bf16[128,512]{1,0:T(8,128)(2,1)S(1)}, u32[]{:S(2)}, u32[]{:S(2)}) collective-permute-start(bf16[128,512]{1,0:T(8,128)(2,1)S(1)} %get-tuple-element.180), channel_id=1, source_target_pairs={{8,0},{12,4},{0,8},{4,12},{9,1},{13,5},{1,9},{5,13},{10,2},{14,6},... | collective-permute-start | bytes 393224 | tf_op jit(solution)/shard_map/ppermute | solution.py:412
  107.5 0.9 collective-permute-start.30
  108.5 6.6 %collective-permute-done.28.piece = bf16[128,512]{1,0:T(8,128)(2,1)S(1)} collective-permute-done((bf16[128,512]{1,0:T(8,128)(2,1)S(1)}, bf16[128,512]{1,0:T(8,128)(2,1)S(1)}, u32[]{:S(2)}, u32[]{:S(2)}) %collective-permute-start.28) | collective-permute-done | bytes 131104 | tf_op jit(solution)/shard_map/ppermute | solution.py:412
  115.1 4.6 %collective-permute-done.30.refs_3_ = bf16[128,512]{1,0:T(8,128)(2,1)S(1)} collective-permute-done((bf16[128,512]{1,0:T(8,128)(2,1)S(1)}, bf16[128,512]{1,0:T(8,128)(2,1)S(1)}, u32[]{:S(2)}, u32[]{:S(2)}) %collective-permute-start.30) | collective-permute-done | bytes 131104 | tf_op jit(solution)/shard_map/ppermute | solution.py:412
  119.7 1.3 %shard_map.195 = f32[256,512]{1,0:T(8,128)} custom-call(bf16[256,512]{1,0:T(8,128)(2,1)S(1)} %get-tuple-element.175.own.refs_0_, bf16[256,512]{1,0:T(8,128)(2,1)S(1)} %collective-permute-done.27.refs_1_, f32[128,512]{1,0:T(8,128)S(1)} %shard_map.193.refs_2_, bf16[128,512]{1,0:T(8,128)(2,1)S(1)} %collective-permute-done.30.refs_3_, bf16[512,512]{1,0:T(8,128)(2,1)S(1)} %copy-done.6), custom_call_target="tpu_custom_call" | custom-call | flops 134217728 | bytes 1966080 | tf_op jit(solution)/shard_map/pallas_call | solution.py:83
  (79 shorter events, 2.7 us)
Async XLA Ops:
  0.6 8.2 %copy-start = (s32[1,4,32]{2,1,0:T(4,128)S(1)}, s32[1,4,32]{2,1,0:T(4,128)}, u32[]{:S(2)}) copy-start(s32[1,4,32]{2,1,0:T(4,128)} %param.22) | copy-start | bytes 1540
  1.7 18.6 %collective-permute-start.3 = (bf16[272,512]{1,0:T(8,128)(2,1)S(1)}, bf16[272,512]{1,0:T(8,128)(2,1)S(1)}, u32[]{:S(2)}, u32[]{:S(2)}) collective-permute-start(bf16[272,512]{1,0:T(8,128)(2,1)S(1)} %shard_map.167.refs_5_), channel_id=1, source_target_pairs={{0,4},{4,0},{8,12},{12,8},{1,5},{5,1},{9,13},{13,9},{2,6},{6,2},{1... | collective-permute-start | bytes 835592 | tf_op jit(solution)/shard_map/ppermute | solution.py:407
  4.8 15.0 %collective-permute-start = (bf16[272,512]{1,0:T(8,128)(2,1)S(1)}, bf16[272,512]{1,0:T(8,128)(2,1)S(1)}, u32[]{:S(2)}, u32[]{:S(2)}) collective-permute-start(bf16[272,512]{1,0:T(8,128)(2,1)S(1)} %shard_map.167.refs_5_), channel_id=1, source_target_pairs={{0,8},{4,12},{8,0},{12,4},{1,9},{5,13},{9,1},{13,5},{2,10},{6,14},... | collective-permute-start | bytes 835592 | tf_op jit(solution)/shard_map/ppermute | solution.py:407
  8.7 1.2 collective-permute-start.1
  10.1 3.7 %collective-permute-start.2 = (s32[2,2,512]{2,0,1:T(2,128)S(1)}, s32[2,2,512]{2,0,1:T(2,128)S(1)}, u32[]{:S(2)}, u32[]{:S(2)}) collective-permute-start(s32[2,2,512]{2,0,1:T(2,128)S(1)} %fusion.1), channel_id=1, source_target_pairs={{0,2},{2,0},{1,3},{3,1},{4,6},{6,4},{5,7},{7,5},{8,10},{10,8},{9,1... | collective-permute-start | bytes 24584 | tf_op jit(solution)/shard_map/ppermute | solution.py:398
  14.0 1.0 copy-start.8
  15.0 5.4 %copy-start.6 = (bf16[512,512]{1,0:T(8,128)(2,1)S(1)}, bf16[512,512]{1,0:T(8,128)(2,1)}, u32[]{:S(2)}) copy-start(bf16[512,512]{1,0:T(8,128)(2,1)} %refs_4_.3) | copy-start | bytes 1572868
  15.0 5.4 %copy-start.12 = (bf16[512,512]{1,0:T(8,128)(2,1)S(1)}, bf16[512,512]{1,0:T(8,128)(2,1)}, u32[]{:S(2)}) copy-start(bf16[512,512]{1,0:T(8,128)(2,1)} %refs_3_.1) | copy-start | bytes 1572868
  19.8 6.8 %collective-permute-start.4 = (bf16[272,512]{1,0:T(8,128)(2,1)S(1)}, bf16[272,512]{1,0:T(8,128)(2,1)S(1)}, u32[]{:S(2)}, u32[]{:S(2)}) collective-permute-start(bf16[272,512]{1,0:T(8,128)(2,1)S(1)} %collective-permute-done.refs_4_), channel_id=1, source_target_pairs={{0,4},{4,0},{8,12},{12,8},{1,5},{5,1},{9,13},{13,9},{2,6},{6,2},{1... | collective-permute-start | bytes 835592 | tf_op jit(solution)/shard_map/ppermute | solution.py:407
  26.6 12.6 %copy-start.2 = (bf16[3,512,512]{2,1,0:T(8,128)(2,1)S(1)}, bf16[3,512,512]{2,1,0:T(8,128)(2,1)}, u32[]{:S(2)}) copy-start(bf16[3,512,512]{2,1,0:T(8,128)(2,1)} %refs_5_.5) | copy-start | bytes 4718596
  26.6 12.6 %copy-start.5 = (bf16[512,512]{1,0:T(8,128)(2,1)S(1)}, bf16[512,512]{1,0:T(8,128)(2,1)}, u32[]{:S(2)}) copy-start(bf16[512,512]{1,0:T(8,128)(2,1)} %refs_8_.11) | copy-start | bytes 1572868
  26.6 12.6 %copy-start.11 = (f32[512]{0:T(512)S(1)}, f32[512]{0:T(512)}, u32[]{:S(2)}) copy-start(f32[512]{0:T(512)} %param.26) | copy-start | bytes 6148
  27.5 1.6 %collective-permute-start.5 = (bf16[256,512]{1,0:T(8,128)(2,1)S(1)}, bf16[256,512]{1,0:T(8,128)(2,1)S(1)}, u32[]{:S(2)}, u32[]{:S(2)}) collective-permute-start(bf16[256,512]{1,0:T(8,128)(2,1)S(1)} %get-tuple-element.99), channel_id=1, source_target_pairs={{0,1},{1,0},{2,3},{3,2},{4,5},{5,4},{6,7},{7,6},{8,9},{9,8},{10,11... | collective-permute-start | bytes 786440 | tf_op jit(solution)/shard_map/ppermute | solution.py:398
  29.1 13.8 %copy-start.4 = (bf16[3,512,512]{2,1,0:T(8,128)(2,1)S(1)}, bf16[3,512,512]{2,1,0:T(8,128)(2,1)}, u32[]{:S(2)}) copy-start(bf16[3,512,512]{2,1,0:T(8,128)(2,1)} %weights.11) | copy-start | bytes 4718596
  29.1 13.8 %copy-start.9 = (bf16[512,512]{1,0:T(8,128)(2,1)S(1)}, bf16[512,512]{1,0:T(8,128)(2,1)}, u32[]{:S(2)}) copy-start(bf16[512,512]{1,0:T(8,128)(2,1)} %hidden.1) | copy-start | bytes 1572868
  29.2 8.4 %collective-permute-start.6 = (bf16[256,512]{1,0:T(8,128)(2,1)S(1)}, bf16[256,512]{1,0:T(8,128)(2,1)S(1)}, u32[]{:S(2)}, u32[]{:S(2)}) collective-permute-start(bf16[256,512]{1,0:T(8,128)(2,1)S(1)} %add_convert_fusion.1), channel_id=1, source_target_pairs={{0,2},{2,0},{1,3},{3,1},{4,6},{6,4},{5,7},{7,5},{8,10},{10,8},{9,1... | collective-permute-start | bytes 786440 | tf_op jit(solution)/shard_map/ppermute | solution.py:398
  37.7 1.6 %collective-permute-start.7 = (bf16[256,512]{1,0:T(8,128)(2,1)S(1)}, bf16[256,512]{1,0:T(8,128)(2,1)S(1)}, u32[]{:S(2)}, u32[]{:S(2)}) collective-permute-start(bf16[256,512]{1,0:T(8,128)(2,1)S(1)} %add_convert_fusion.refs_1_), channel_id=1, source_target_pairs={{0,1},{1,0},{2,3},{3,2},{4,5},{5,4},{6,7},{7,6},{8,9},{9,8},{10,11... | collective-permute-start | bytes 786440 | tf_op jit(solution)/shard_map/ppermute | solution.py:398
  40.0 5.5 %collective-permute-start.8 = (bf16[32,512]{1,0:T(8,128)(2,1)S(1)}, bf16[32,512]{1,0:T(8,128)(2,1)S(1)}, u32[]{:S(2)}, u32[]{:S(2)}) collective-permute-start(bf16[32,512]{1,0:T(8,128)(2,1)S(1)} %get-tuple-element.101), channel_id=1, source_target_pairs={{0,8},{1,13},{4,12},{5,9},{8,0},{9,5},{12,4},{13,1},{2,10},{3,15},... | collective-permute-start | bytes 98312 | tf_op jit(solution)/shard_map/ppermute | solution.py:550
  41.0 5.7 %collective-permute-start.10 = (bf16[32,512]{1,0:T(8,128)(2,1)S(1)}, bf16[32,512]{1,0:T(8,128)(2,1)S(1)}, u32[]{:S(2)}, u32[]{:S(2)}) collective-permute-start(bf16[32,512]{1,0:T(8,128)(2,1)S(1)} %get-tuple-element.113), channel_id=1, source_target_pairs={{0,4},{4,0},{8,12},{12,8},{1,5},{5,1},{9,13},{13,9},{2,6},{6,2},{1... | collective-permute-start | bytes 98312 | tf_op jit(solution)/shard_map/ppermute | solution.py:407
  45.5 1.4 %copy-start.3 = (bf16[3,512,512]{2,1,0:T(8,128)(2,1)S(1)}, bf16[3,512,512]{2,1,0:T(8,128)(2,1)}, u32[]{:S(2)}) copy-start(bf16[3,512,512]{2,1,0:T(8,128)(2,1)} %refs_9_.9) | copy-start | bytes 4718596
  45.5 1.4 %copy-start.10 = (f32[3,512]{1,0:T(4,128)S(1)}, f32[3,512]{1,0:T(4,128)}, u32[]{:S(2)}) copy-start(f32[3,512]{1,0:T(4,128)} %refs_8_.10) | copy-start | bytes 18436
  45.5 1.3 %collective-permute-start.9 = (bf16[32,512]{1,0:T(8,128)(2,1)S(1)}, bf16[32,512]{1,0:T(8,128)(2,1)S(1)}, u32[]{:S(2)}, u32[]{:S(2)}) collective-permute-start(bf16[32,512]{1,0:T(8,128)(2,1)S(1)} %collective-permute-done.8.refs_3_), channel_id=1, source_target_pairs={{0,1},{1,0},{2,3},{3,2},{4,5},{5,4},{6,7},{7,6},{8,9},{9,8},{10,11... | collective-permute-start | bytes 98312 | tf_op jit(solution)/shard_map/ppermute | solution.py:398
  49.5 5.1 %collective-permute-start.11 = (bf16[32,512]{1,0:T(8,128)(2,1)S(1)}, bf16[32,512]{1,0:T(8,128)(2,1)S(1)}, u32[]{:S(2)}, u32[]{:S(2)}) collective-permute-start(bf16[32,512]{1,0:T(8,128)(2,1)S(1)} %get-tuple-element.116), channel_id=1, source_target_pairs={{0,8},{1,13},{4,12},{5,9},{8,0},{9,5},{12,4},{13,1},{2,10},{3,15},... | collective-permute-start | bytes 98312 | tf_op jit(solution)/shard_map/ppermute | solution.py:550
  50.6 5.5 %collective-permute-start.13 = (bf16[32,512]{1,0:T(8,128)(2,1)S(1)}, bf16[32,512]{1,0:T(8,128)(2,1)S(1)}, u32[]{:S(2)}, u32[]{:S(2)}) collective-permute-start(bf16[32,512]{1,0:T(8,128)(2,1)S(1)} %get-tuple-element.128), channel_id=1, source_target_pairs={{0,4},{4,0},{8,12},{12,8},{1,5},{5,1},{9,13},{13,9},{2,6},{6,2},{1... | collective-permute-start | bytes 98312 | tf_op jit(solution)/shard_map/ppermute | solution.py:407
  54.6 1.5 %collective-permute-start.12 = (bf16[32,512]{1,0:T(8,128)(2,1)S(1)}, bf16[32,512]{1,0:T(8,128)(2,1)S(1)}, u32[]{:S(2)}, u32[]{:S(2)}) collective-permute-start(bf16[32,512]{1,0:T(8,128)(2,1)S(1)} %collective-permute-done.11.refs_3_), channel_id=1, source_target_pairs={{0,1},{1,0},{2,3},{3,2},{4,5},{5,4},{6,7},{7,6},{8,9},{9,8},{10,11... | collective-permute-start | bytes 98312 | tf_op jit(solution)/shard_map/ppermute | solution.py:398
  58.8 5.7 %collective-permute-start.14 = (bf16[32,512]{1,0:T(8,128)(2,1)S(1)}, bf16[32,512]{1,0:T(8,128)(2,1)S(1)}, u32[]{:S(2)}, u32[]{:S(2)}) collective-permute-start(bf16[32,512]{1,0:T(8,128)(2,1)S(1)} %get-tuple-element.129), channel_id=1, source_target_pairs={{0,8},{1,13},{4,12},{5,9},{8,0},{9,5},{12,4},{13,1},{2,10},{3,15},... | collective-permute-start | bytes 98312 | tf_op jit(solution)/shard_map/ppermute | solution.py:550
  60.3 5.5 %collective-permute-start.16 = (bf16[32,512]{1,0:T(8,128)(2,1)S(1)}, bf16[32,512]{1,0:T(8,128)(2,1)S(1)}, u32[]{:S(2)}, u32[]{:S(2)}) collective-permute-start(bf16[32,512]{1,0:T(8,128)(2,1)S(1)} %get-tuple-element.140), channel_id=1, source_target_pairs={{0,4},{4,0},{8,12},{12,8},{1,5},{5,1},{9,13},{13,9},{2,6},{6,2},{1... | collective-permute-start | bytes 98312 | tf_op jit(solution)/shard_map/ppermute | solution.py:407
  64.5 1.3 %copy-start.7 = (bf16[512,512]{1,0:T(8,128)(2,1)S(1)}, bf16[512,512]{1,0:T(8,128)(2,1)}, u32[]{:S(2)}) copy-start(bf16[512,512]{1,0:T(8,128)(2,1)} %upstream.1) | copy-start | bytes 1572868
  64.5 1.3 %collective-permute-start.15 = (bf16[32,512]{1,0:T(8,128)(2,1)S(1)}, bf16[32,512]{1,0:T(8,128)(2,1)S(1)}, u32[]{:S(2)}, u32[]{:S(2)}) collective-permute-start(bf16[32,512]{1,0:T(8,128)(2,1)S(1)} %collective-permute-done.14.refs_3_), channel_id=1, source_target_pairs={{0,1},{1,0},{2,3},{3,2},{4,5},{5,4},{6,7},{7,6},{8,9},{9,8},{10,11... | collective-permute-start | bytes 98312 | tf_op jit(solution)/shard_map/ppermute | solution.py:398
  70.8 4.8 %collective-permute-start.17 = (bf16[32,512]{1,0:T(8,128)(2,1)S(1)}, bf16[32,512]{1,0:T(8,128)(2,1)S(1)}, u32[]{:S(2)}, u32[]{:S(2)}) collective-permute-start(bf16[32,512]{1,0:T(8,128)(2,1)S(1)} %get-tuple-element.143), channel_id=1, source_target_pairs={{0,8},{1,13},{4,12},{5,9},{8,0},{9,5},{12,4},{13,1},{2,10},{3,15},... | collective-permute-start | bytes 98312 | tf_op jit(solution)/shard_map/ppermute | solution.py:550
  72.1 5.4 %collective-permute-start.19 = (bf16[32,512]{1,0:T(8,128)(2,1)S(1)}, bf16[32,512]{1,0:T(8,128)(2,1)S(1)}, u32[]{:S(2)}, u32[]{:S(2)}) collective-permute-start(bf16[32,512]{1,0:T(8,128)(2,1)S(1)} %get-tuple-element.147), channel_id=1, source_target_pairs={{4,0},{0,4},{12,8},{8,12},{5,1},{1,5},{13,9},{9,13},{6,2},{2,6},{1... | collective-permute-start | bytes 98312 | tf_op jit(solution)/shard_map/ppermute | solution.py:412
  75.6 1.9 %collective-permute-start.18 = (bf16[32,512]{1,0:T(8,128)(2,1)S(1)}, bf16[32,512]{1,0:T(8,128)(2,1)S(1)}, u32[]{:S(2)}, u32[]{:S(2)}) collective-permute-start(bf16[32,512]{1,0:T(8,128)(2,1)S(1)} %collective-permute-done.17.refs_1_), channel_id=1, source_target_pairs={{0,1},{1,0},{2,3},{3,2},{4,5},{5,4},{6,7},{7,6},{8,9},{9,8},{10,11... | collective-permute-start | bytes 98312 | tf_op jit(solution)/shard_map/ppermute | solution.py:398
  80.1 5.3 %collective-permute-start.20 = (bf16[32,512]{1,0:T(8,128)(2,1)S(1)}, bf16[32,512]{1,0:T(8,128)(2,1)S(1)}, u32[]{:S(2)}, u32[]{:S(2)}) collective-permute-start(bf16[32,512]{1,0:T(8,128)(2,1)S(1)} %get-tuple-element.151), channel_id=1, source_target_pairs={{0,8},{1,13},{4,12},{5,9},{8,0},{9,5},{12,4},{13,1},{2,10},{3,15},... | collective-permute-start | bytes 98312 | tf_op jit(solution)/shard_map/ppermute | solution.py:550
  81.2 5.7 %collective-permute-start.22 = (bf16[32,512]{1,0:T(8,128)(2,1)S(1)}, bf16[32,512]{1,0:T(8,128)(2,1)S(1)}, u32[]{:S(2)}, u32[]{:S(2)}) collective-permute-start(bf16[32,512]{1,0:T(8,128)(2,1)S(1)} %get-tuple-element.156), channel_id=1, source_target_pairs={{4,0},{0,4},{12,8},{8,12},{5,1},{1,5},{13,9},{9,13},{6,2},{2,6},{1... | collective-permute-start | bytes 98312 | tf_op jit(solution)/shard_map/ppermute | solution.py:412
  85.4 1.5 %collective-permute-start.21 = (bf16[32,512]{1,0:T(8,128)(2,1)S(1)}, bf16[32,512]{1,0:T(8,128)(2,1)S(1)}, u32[]{:S(2)}, u32[]{:S(2)}) collective-permute-start(bf16[32,512]{1,0:T(8,128)(2,1)S(1)} %collective-permute-done.20.refs_1_), channel_id=1, source_target_pairs={{0,1},{1,0},{2,3},{3,2},{4,5},{5,4},{6,7},{7,6},{8,9},{9,8},{10,11... | collective-permute-start | bytes 98312 | tf_op jit(solution)/shard_map/ppermute | solution.py:398
  89.7 4.9 %collective-permute-start.23 = (bf16[32,512]{1,0:T(8,128)(2,1)S(1)}, bf16[32,512]{1,0:T(8,128)(2,1)S(1)}, u32[]{:S(2)}, u32[]{:S(2)}) collective-permute-start(bf16[32,512]{1,0:T(8,128)(2,1)S(1)} %get-tuple-element.159), channel_id=1, source_target_pairs={{0,8},{1,13},{4,12},{5,9},{8,0},{9,5},{12,4},{13,1},{2,10},{3,15},... | collective-permute-start | bytes 98312 | tf_op jit(solution)/shard_map/ppermute | solution.py:550
  90.4 6.2 %collective-permute-start.25 = (bf16[32,512]{1,0:T(8,128)(2,1)S(1)}, bf16[32,512]{1,0:T(8,128)(2,1)S(1)}, u32[]{:S(2)}, u32[]{:S(2)}) collective-permute-start(bf16[32,512]{1,0:T(8,128)(2,1)S(1)} %get-tuple-element.164), channel_id=1, source_target_pairs={{4,0},{0,4},{12,8},{8,12},{5,1},{1,5},{13,9},{9,13},{6,2},{2,6},{1... | collective-permute-start | bytes 98312 | tf_op jit(solution)/shard_map/ppermute | solution.py:412
  94.6 2.0 %collective-permute-start.24 = (bf16[32,512]{1,0:T(8,128)(2,1)S(1)}, bf16[32,512]{1,0:T(8,128)(2,1)S(1)}, u32[]{:S(2)}, u32[]{:S(2)}) collective-permute-start(bf16[32,512]{1,0:T(8,128)(2,1)S(1)} %collective-permute-done.23.refs_1_), channel_id=1, source_target_pairs={{0,1},{1,0},{2,3},{3,2},{4,5},{5,4},{6,7},{7,6},{8,9},{9,8},{10,11... | collective-permute-start | bytes 98312 | tf_op jit(solution)/shard_map/ppermute | solution.py:398
  98.1 6.4 %collective-permute-start.26 = (bf16[128,512]{1,0:T(8,128)(2,1)S(1)}, bf16[128,512]{1,0:T(8,128)(2,1)S(1)}, u32[]{:S(2)}, u32[]{:S(2)}) collective-permute-start(bf16[128,512]{1,0:T(8,128)(2,1)S(1)} %get-tuple-element.177), channel_id=1, source_target_pairs={{4,0},{0,4},{12,8},{8,12},{5,1},{1,5},{13,9},{9,13},{6,2},{2,6},{1... | collective-permute-start | bytes 393224 | tf_op jit(solution)/shard_map/ppermute | solution.py:412
  99.0 8.4 %collective-permute-start.29 = (bf16[128,512]{1,0:T(8,128)(2,1)S(1)}, bf16[128,512]{1,0:T(8,128)(2,1)S(1)}, u32[]{:S(2)}, u32[]{:S(2)}) collective-permute-start(bf16[128,512]{1,0:T(8,128)(2,1)S(1)} %get-tuple-element.181), channel_id=1, source_target_pairs={{4,0},{0,4},{12,8},{8,12},{5,1},{1,5},{13,9},{9,13},{6,2},{2,6},{1... | collective-permute-start | bytes 393224 | tf_op jit(solution)/shard_map/ppermute | solution.py:412
  100.2 20.8 %copy-start.1 = (s32[1,4,32]{2,1,0:T(4,128)S(1)}, s32[1,4,32]{2,1,0:T(4,128)}, u32[]{:S(2)}) copy-start(s32[1,4,32]{2,1,0:T(4,128)} %param.22) | copy-start | bytes 1540
  104.5 15.2 %collective-permute-start.27 = (bf16[256,512]{1,0:T(8,128)(2,1)S(1)}, bf16[256,512]{1,0:T(8,128)(2,1)S(1)}, u32[]{:S(2)}, u32[]{:S(2)}) collective-permute-start(bf16[256,512]{1,0:T(8,128)(2,1)S(1)} %get-tuple-element.179), channel_id=1, source_target_pairs={{4,0},{0,4},{12,8},{8,12},{5,1},{1,5},{13,9},{9,13},{6,2},{2,6},{1... | collective-permute-start | bytes 786440 | tf_op jit(solution)/shard_map/ppermute | solution.py:412
  105.4 9.6 %collective-permute-start.28 = (bf16[128,512]{1,0:T(8,128)(2,1)S(1)}, bf16[128,512]{1,0:T(8,128)(2,1)S(1)}, u32[]{:S(2)}, u32[]{:S(2)}) collective-permute-start(bf16[128,512]{1,0:T(8,128)(2,1)S(1)} %get-tuple-element.180), channel_id=1, source_target_pairs={{8,0},{12,4},{0,8},{4,12},{9,1},{13,5},{1,9},{5,13},{10,2},{14,6},... | collective-permute-start | bytes 393224 | tf_op jit(solution)/shard_map/ppermute | solution.py:412
  107.5 12.2 %collective-permute-start.30 = (bf16[128,512]{1,0:T(8,128)(2,1)S(1)}, bf16[128,512]{1,0:T(8,128)(2,1)S(1)}, u32[]{:S(2)}, u32[]{:S(2)}) collective-permute-start(bf16[128,512]{1,0:T(8,128)(2,1)S(1)} %shard_map.194), channel_id=1, source_target_pairs={{8,0},{12,4},{0,8},{4,12},{9,1},{13,5},{1,9},{5,13},{10,2},{14,6},... | collective-permute-start | bytes 393224 | tf_op jit(solution)/shard_map/ppermute | solution.py:412

commit v14 on v12

--- a/solution.py
+++ b/solution.py
@@ -10,7 +10,7 @@
 
 LAYERS = 3
 LANES = 128
-BLOCK = 512
+BLOCK = 1024
 EXTRA = 16
 eps = 1e-05
 

time: 120 us -> 120 us (level)
  transfers between devices with their start and end apart: 31 -> 31, of which waited for: 12 -> 13; matrix products, arithmetic and copies ran while one was open for 2% -> 2% of each run, Pallas kernels for 22% -> 22%
where the time goes in v14:
time: 120 us
  Pallas kernels  46.8 us (39%)
  starting transfers between devices  35.2 us (29%)
  waiting for transfers between devices  34.2 us (29%)
  other arithmetic  1.83 us (2%)
    pallas_call x29, Pallas kernels, run(): pl.pallas_call(body, out_shape=tuple((jax.ShapeDtypeStruct(shape, dtype)...  46.8 us
    ppermute x8, waiting for transfers between devices, sent_back(): lax.ppermute(value, 'mesh', [(partner(at, step, size), at) for at in rang...  15 us
    ppermute x11, waiting for transfers between devices, shifted(): lax.ppermute(value, axis, [(at, (at + by) % size) for at in range(size)])  12.4 us
    ppermute x8, starting transfers between devices, sent_back(): lax.ppermute(value, 'mesh', [(partner(at, step, size), at) for at in rang...  12.4 us
    ppermute x6, starting transfers between devices, sent_to(): lax.ppermute(value, 'mesh', [(at, partner(at, step, size)) for at in rang...  11.5 us
    ppermute x6, starting transfers between devices, exchange(): lax.ppermute(blocks[0], ('mesh', 'rep'), [(2 * at + side, 2 * (at ^ 2 + s...  7.11 us
    ppermute x6, waiting for transfers between devices, sent_to(): lax.ppermute(value, 'mesh', [(at, partner(at, step, size)) for at in rang...  5.84 us
    ppermute x11, starting transfers between devices, shifted(): lax.ppermute(value, axis, [(at, (at + by) % size) for at in range(size)])  4.27 us
  transfers between devices with their start and end apart: 31, of which 13 were waited for; matrix products, arithmetic and copies ran while one was open for 2% of the time, Pallas kernels for 22%

profile of v14, /device:TPU:0, one launch (start us, length us, event | category | flops | bytes accessed | tf_op | source)
XLA Modules:
  0.0 120.2 jit_solution(17600115094771143274)
XLA Ops:
  0.6 1.0 shard_map.167.refs_5_
  1.7 3.1 %collective-permute-start.3 = (bf16[272,512]{1,0:T(8,128)(2,1)S(1)}, bf16[272,512]{1,0:T(8,128)(2,1)S(1)}, u32[]{:S(2)}, u32[]{:S(2)}) collective-permute-start(bf16[272,512]{1,0:T(8,128)(2,1)S(1)} %shard_map.167.refs_5_), channel_id=1, source_target_pairs={{0,4},{4,0},{8,12},{12,8},{1,5},{5,1},{9,13},{13,9},{2,6},{6,2},{1... | collective-permute-start | bytes 835592 | tf_op jit(solution)/shard_map/ppermute | solution.py:402
  4.8 2.6 %collective-permute-start = (bf16[272,512]{1,0:T(8,128)(2,1)S(1)}, bf16[272,512]{1,0:T(8,128)(2,1)S(1)}, u32[]{:S(2)}, u32[]{:S(2)}) collective-permute-start(bf16[272,512]{1,0:T(8,128)(2,1)S(1)} %shard_map.167.refs_5_), channel_id=1, source_target_pairs={{0,8},{4,12},{8,0},{12,4},{1,9},{5,13},{9,1},{13,5},{2,10},{6,14},... | collective-permute-start | bytes 835592 | tf_op jit(solution)/shard_map/ppermute | solution.py:402
  7.3 0.7 compare_select_fusion.1
  8.0 0.7 fusion.11
  8.8 0.6 gather_fusion
  9.5 0.4 collective-permute-done.1
  10.1 1.6 %collective-permute-start.2 = (s32[2,2,512]{2,0,1:T(2,128)S(1)}, s32[2,2,512]{2,0,1:T(2,128)S(1)}, u32[]{:S(2)}, u32[]{:S(2)}) collective-permute-start(s32[2,2,512]{2,0,1:T(2,128)S(1)} %fusion.1), channel_id=1, source_target_pairs={{0,2},{2,0},{1,3},{3,1},{4,6},{6,4},{5,7},{7,5},{8,10},{10,8},{9,1... | collective-permute-start | bytes 24584 | tf_op jit(solution)/shard_map/ppermute | solution.py:393
  11.7 2.1 %collective-permute-done.2 = s32[2,2,512]{2,0,1:T(2,128)S(1)} collective-permute-done((s32[2,2,512]{2,0,1:T(2,128)S(1)}, s32[2,2,512]{2,0,1:T(2,128)S(1)}, u32[]{:S(2)}, u32[]{:S(2)}) %collective-permute-start.2) | collective-permute-done | bytes 8224 | tf_op jit(solution)/shard_map/ppermute | solution.py:393
  14.0 3.5 %shard_map.168 = (bf16[2048,1024]{1,0:T(8,128)(2,1)S(1)}, bf16[1024,2048]{1,0:T(8,128)(2,1)S(1)}, bf16[2048,128]{1,0:T(8,128)(2,1)S(1)}, bf16[128,2048]{1,0:T(8,...) custom-call(s32[1,2048]{1,0:T(1,128)S(1)} %fusion.2.slots, s32[1,2048]{1,0:T(1,128)S(1)} %bitcast.29, ...), custom_call_target="tpu_custom_call" | custom-call | flops 3221225472 | bytes 9650560 | tf_op jit(solution)/shard_map/pallas_call | solution.py:83
  17.5 2.3 %collective-permute-done.refs_4_ = bf16[272,512]{1,0:T(8,128)(2,1)S(1)} collective-permute-done((bf16[272,512]{1,0:T(8,128)(2,1)S(1)}, bf16[272,512]{1,0:T(8,128)(2,1)S(1)}, u32[]{:S(2)}, u32[]{:S(2)}) %collective-permute-start) | collective-permute-done | bytes 278560 | tf_op jit(solution)/shard_map/ppermute | solution.py:402
  19.8 0.4 collective-permute-start.4
  20.4 1.6 %shard_map.169 = (bf16[256,512]{1,0:T(8,128)(2,1)S(1)}, bf16[256,512]{1,0:T(8,128)(2,1)S(1)}, bf16[256,512]{1,0:T(8,128)(2,1)S(1)}, bf16[256,512]{1,0:T(8,128)(2...) custom-call(s32[2,512]{1,0:T(2,128)S(1)} %broadcast_in_dim.27.refs_0_, bf16[512,512]{1,0:T(8,128)(2,1)S(1)} %copy-done.8, ...), custom_call_target="tpu_custom_call" | custom-call | flops 1073741824 | bytes 4853760 | tf_op jit(solution)/shard_map/pallas_call | solution.py:83
  22.0 0.8 shard_map.170
  22.8 3.5 %collective-permute-done.4.refs_4_ = bf16[272,512]{1,0:T(8,128)(2,1)S(1)} collective-permute-done((bf16[272,512]{1,0:T(8,128)(2,1)S(1)}, bf16[272,512]{1,0:T(8,128)(2,1)S(1)}, u32[]{:S(2)}, u32[]{:S(2)}) %collective-permute-start.4) | collective-permute-done | bytes 278560 | tf_op jit(solution)/shard_map/ppermute | solution.py:402
  26.3 0.8 shard_map.171
  27.3 1.5 %collective-permute-done.5 = bf16[256,512]{1,0:T(8,128)(2,1)S(1)} collective-permute-done((bf16[256,512]{1,0:T(8,128)(2,1)S(1)}, bf16[256,512]{1,0:T(8,128)(2,1)S(1)}, u32[]{:S(2)}, u32[]{:S(2)}) %collective-permute-start.5) | collective-permute-done | bytes 262176 | tf_op jit(solution)/shard_map/ppermute | solution.py:393
  28.9 1.6 %collective-permute-start.6 = (bf16[256,512]{1,0:T(8,128)(2,1)S(1)}, bf16[256,512]{1,0:T(8,128)(2,1)S(1)}, u32[]{:S(2)}, u32[]{:S(2)}) collective-permute-start(bf16[256,512]{1,0:T(8,128)(2,1)S(1)} %add_convert_fusion.1), channel_id=1, source_target_pairs={{0,2},{2,0},{1,3},{3,1},{4,6},{6,4},{5,7},{7,5},{8,10},{10,8},{9,1... | collective-permute-start | bytes 786440 | tf_op jit(solution)/shard_map/ppermute | solution.py:393
  30.5 6.9 %collective-permute-done.6 = bf16[256,512]{1,0:T(8,128)(2,1)S(1)} collective-permute-done((bf16[256,512]{1,0:T(8,128)(2,1)S(1)}, bf16[256,512]{1,0:T(8,128)(2,1)S(1)}, u32[]{:S(2)}, u32[]{:S(2)}) %collective-permute-start.6) | collective-permute-done | bytes 262176 | tf_op jit(solution)/shard_map/ppermute | solution.py:393
  37.5 1.5 %collective-permute-done.7.refs_2_ = bf16[256,512]{1,0:T(8,128)(2,1)S(1)} collective-permute-done((bf16[256,512]{1,0:T(8,128)(2,1)S(1)}, bf16[256,512]{1,0:T(8,128)(2,1)S(1)}, u32[]{:S(2)}, u32[]{:S(2)}) %collective-permute-start.7) | collective-permute-done | bytes 262176 | tf_op jit(solution)/shard_map/ppermute | solution.py:393
  39.0 0.7 shard_map.172
  39.7 1.3 %collective-permute-start.8 = (bf16[32,512]{1,0:T(8,128)(2,1)S(1)}, bf16[32,512]{1,0:T(8,128)(2,1)S(1)}, u32[]{:S(2)}, u32[]{:S(2)}) collective-permute-start(bf16[32,512]{1,0:T(8,128)(2,1)S(1)} %get-tuple-element.95), channel_id=1, source_target_pairs={{0,8},{1,13},{4,12},{5,9},{8,0},{9,5},{12,4},{13,1},{2,10},{3,15},... | collective-permute-start | bytes 98312 | tf_op jit(solution)/shard_map/ppermute | solution.py:544
  41.1 1.9 %collective-permute-start.10 = (bf16[32,512]{1,0:T(8,128)(2,1)S(1)}, bf16[32,512]{1,0:T(8,128)(2,1)S(1)}, u32[]{:S(2)}, u32[]{:S(2)}) collective-permute-start(bf16[32,512]{1,0:T(8,128)(2,1)S(1)} %get-tuple-element.106), channel_id=1, source_target_pairs={{0,4},{4,0},{8,12},{12,8},{1,5},{5,1},{9,13},{13,9},{2,6},{6,2},{1... | collective-permute-start | bytes 98312 | tf_op jit(solution)/shard_map/ppermute | solution.py:402
  42.9 2.2 %shard_map.173 = (bf16[512,512]{1,0:T(8,128)(2,1)S(1)}, f32[512,512]{1,0:T(8,128)S(1)}, f32[1024,512]{1,0:T(8,128)S(1)}, bf16[1024,512]{1,0:T(8,128)(2,1)S(1)}) custom-call(bf16[512,512]{1,0:T(8,128)(2,1)S(1)} %get-tuple-element.96.total, bf16[512,512]{1,0:T(8,128)(2,1)S(1)} %copy-done.8, bf16[512,512]{1,0:T(8,128)(2,1)S(1)} %copy-done.5, ...), custom_call_target="tpu_custom_call" | custom-call | flops 1879048192 | bytes 13633536 | tf_op jit(solution)/shard_map/pallas_call | solution.py:83
  45.3 1.2 %shard_map.174.refs_2_ = f32[1024,512]{1,0:T(8,128)S(1)} custom-call(bf16[1024,512]{1,0:T(8,128)(2,1)S(1)} %get-tuple-element.104.table, bf16[2048,1024]{1,0:T(8,128)(2,1)S(1)} %get-tuple-element.97.here.refs_10_), custom_call_target="tpu_custom_call" | custom-call | flops 1073741824 | bytes 7340032 | tf_op jit(solution)/shard_map/pallas_call | solution.py:83
  46.6 2.5 %shard_map.175 = (bf16[512,512]{1,0:T(8,128)(2,1)S(1)}, bf16[2048,512]{1,0:T(8,128)(2,1)S(1)}, bf16[32,512]{1,0:T(8,128)(2,1)S(1)}, bf16[32,512]{1,0:T(8,128)(2,1)S(1)}) custom-call(bf16[512,512]{1,0:T(8,128)(2,1)S(1)} %get-tuple-element.102.refs_0_.hidden, f32[1024,512]{1,0:T(8,128)S(1)} %get-tuple-element.103.refs_1_, f32[1024,512]{1,0:T(8,128)S(1)} %shard_map.174.refs_2_, ...), custom_call_target="tpu_custom_call" | custom-call | flops 1543503872 | bytes 15472640 | tf_op jit(solution)/shard_map/pallas_call | solution.py:83
  49.1 1.2 %collective-permute-start.11 = (bf16[32,512]{1,0:T(8,128)(2,1)S(1)}, bf16[32,512]{1,0:T(8,128)(2,1)S(1)}, u32[]{:S(2)}, u32[]{:S(2)}) collective-permute-start(bf16[32,512]{1,0:T(8,128)(2,1)S(1)} %get-tuple-element.109), channel_id=1, source_target_pairs={{0,8},{1,13},{4,12},{5,9},{8,0},{9,5},{12,4},{13,1},{2,10},{3,15},... | collective-permute-start | bytes 98312 | tf_op jit(solution)/shard_map/ppermute | solution.py:544
  50.3 1.8 %collective-permute-start.13 = (bf16[32,512]{1,0:T(8,128)(2,1)S(1)}, bf16[32,512]{1,0:T(8,128)(2,1)S(1)}, u32[]{:S(2)}, u32[]{:S(2)}) collective-permute-start(bf16[32,512]{1,0:T(8,128)(2,1)S(1)} %get-tuple-element.119), channel_id=1, source_target_pairs={{0,4},{4,0},{8,12},{12,8},{1,5},{5,1},{9,13},{13,9},{2,6},{6,2},{1... | collective-permute-start | bytes 98312 | tf_op jit(solution)/shard_map/ppermute | solution.py:402
  52.1 2.2 %shard_map.176 = (bf16[512,512]{1,0:T(8,128)(2,1)S(1)}, f32[512,512]{1,0:T(8,128)S(1)}, f32[1024,512]{1,0:T(8,128)S(1)}, bf16[1024,512]{1,0:T(8,128)(2,1)S(1)}) custom-call(bf16[512,512]{1,0:T(8,128)(2,1)S(1)} %get-tuple-element.110.total, bf16[512,512]{1,0:T(8,128)(2,1)S(1)} %get-tuple-element.102.refs_0_.hidden, bf16[3,512,512]{2,1,0:T(8,128)(2,1)S(1)} %copy-done.3, ...), custom_call_target="tpu_custom_call" | custom-call | flops 1879048192 | bytes 14686208 | tf_op jit(solution)/shard_map/pallas_call | solution.py:83
  54.5 1.2 %shard_map.177.refs_2_ = f32[1024,512]{1,0:T(8,128)S(1)} custom-call(bf16[1024,512]{1,0:T(8,128)(2,1)S(1)} %get-tuple-element.117.table, bf16[2048,1024]{1,0:T(8,128)(2,1)S(1)} %get-tuple-element.97.here.refs_10_), custom_call_target="tpu_custom_call" | custom-call | flops 1073741824 | bytes 7340032 | tf_op jit(solution)/shard_map/pallas_call | solution.py:83
  55.8 2.5 %shard_map.178 = (bf16[512,512]{1,0:T(8,128)(2,1)S(1)}, bf16[2048,512]{1,0:T(8,128)(2,1)S(1)}, bf16[32,512]{1,0:T(8,128)(2,1)S(1)}, bf16[32,512]{1,0:T(8,128)(2,1)S(1)}) custom-call(bf16[512,512]{1,0:T(8,128)(2,1)S(1)} %get-tuple-element.115.refs_0_.hidden, f32[1024,512]{1,0:T(8,128)S(1)} %get-tuple-element.116.refs_1_, f32[1024,512]{1,0:T(8,128)S(1)} %shard_map.177.refs_2_, ...), custom_call_target="tpu_custom_call" | custom-call | flops 1543503872 | bytes 15472640 | tf_op jit(solution)/shard_map/pallas_call | solution.py:83
  58.3 1.3 %collective-permute-start.14 = (bf16[32,512]{1,0:T(8,128)(2,1)S(1)}, bf16[32,512]{1,0:T(8,128)(2,1)S(1)}, u32[]{:S(2)}, u32[]{:S(2)}) collective-permute-start(bf16[32,512]{1,0:T(8,128)(2,1)S(1)} %get-tuple-element.120), channel_id=1, source_target_pairs={{0,8},{1,13},{4,12},{5,9},{8,0},{9,5},{12,4},{13,1},{2,10},{3,15},... | collective-permute-start | bytes 98312 | tf_op jit(solution)/shard_map/ppermute | solution.py:544
  59.6 1.7 %collective-permute-start.16 = (bf16[32,512]{1,0:T(8,128)(2,1)S(1)}, bf16[32,512]{1,0:T(8,128)(2,1)S(1)}, u32[]{:S(2)}, u32[]{:S(2)}) collective-permute-start(bf16[32,512]{1,0:T(8,128)(2,1)S(1)} %get-tuple-element.130), channel_id=1, source_target_pairs={{0,4},{4,0},{8,12},{12,8},{1,5},{5,1},{9,13},{13,9},{2,6},{6,2},{1... | collective-permute-start | bytes 98312 | tf_op jit(solution)/shard_map/ppermute | solution.py:402
  61.3 2.4 %shard_map.179 = (bf16[512,512]{1,0:T(8,128)(2,1)S(1)}, f32[512,512]{1,0:T(8,128)S(1)}, f32[1024,512]{1,0:T(8,128)S(1)}, bf16[1024,512]{1,0:T(8,128)(2,1)S(1)}) custom-call(bf16[512,512]{1,0:T(8,128)(2,1)S(1)} %get-tuple-element.121.total, bf16[512,512]{1,0:T(8,128)(2,1)S(1)} %get-tuple-element.115.refs_0_.hidden, bf16[3,512,512]{2,1,0:T(8,128)(2,1)S(1)} %copy-done.3, ...), custom_call_target="tpu_custom_call" | custom-call | flops 1879048192 | bytes 14686208 | tf_op jit(solution)/shard_map/pallas_call | solution.py:83
  63.8 1.2 %shard_map.180.refs_2_ = f32[1024,512]{1,0:T(8,128)S(1)} custom-call(bf16[1024,512]{1,0:T(8,128)(2,1)S(1)} %get-tuple-element.128.table, bf16[2048,1024]{1,0:T(8,128)(2,1)S(1)} %get-tuple-element.97.here.refs_10_), custom_call_target="tpu_custom_call" | custom-call | flops 1073741824 | bytes 7340032 | tf_op jit(solution)/shard_map/pallas_call | solution.py:83
  65.1 4.9 %shard_map.181 = (bf16[512,512]{1,0:T(8,128)(2,1)}, bf16[2048,512]{1,0:T(8,128)(2,1)S(1)}, bf16[32,512]{1,0:T(8,128)(2,1)S(1)}, bf16[32,512]{1,0:T(8,128)(2,1)S(1)}) custom-call(bf16[512,512]{1,0:T(8,128)(2,1)S(1)} %get-tuple-element.126.refs_0_, f32[1024,512]{1,0:T(8,128)S(1)} %get-tuple-element.127.refs_1_, f32[1024,512]{1,0:T(8,128)S(1)} %shard_map.180.refs_2_, ...), custom_call_target="tpu_custom_call" | custom-call | flops 3221225472 | bytes 19044352 | tf_op jit(solution)/shard_map/pallas_call | solution.py:83
  70.0 1.3 %collective-permute-start.17 = (bf16[32,512]{1,0:T(8,128)(2,1)S(1)}, bf16[32,512]{1,0:T(8,128)(2,1)S(1)}, u32[]{:S(2)}, u32[]{:S(2)}) collective-permute-start(bf16[32,512]{1,0:T(8,128)(2,1)S(1)} %get-tuple-element.133), channel_id=1, source_target_pairs={{0,8},{1,13},{4,12},{5,9},{8,0},{9,5},{12,4},{13,1},{2,10},{3,15},... | collective-permute-start | bytes 98312 | tf_op jit(solution)/shard_map/ppermute | solution.py:544
  71.3 1.6 %collective-permute-start.19 = (bf16[32,512]{1,0:T(8,128)(2,1)S(1)}, bf16[32,512]{1,0:T(8,128)(2,1)S(1)}, u32[]{:S(2)}, u32[]{:S(2)}) collective-permute-start(bf16[32,512]{1,0:T(8,128)(2,1)S(1)} %get-tuple-element.137), channel_id=1, source_target_pairs={{4,0},{0,4},{12,8},{8,12},{5,1},{1,5},{13,9},{9,13},{6,2},{2,6},{1... | collective-permute-start | bytes 98312 | tf_op jit(solution)/shard_map/ppermute | solution.py:407
  72.9 1.5 %shard_map.182.upstream = f32[512,512]{1,0:T(8,128)S(1)} custom-call(bf16[512,512]{1,0:T(8,128)(2,1)S(1)} %copy-done.7, bf16[2048,512]{1,0:T(8,128)(2,1)S(1)} %get-tuple-element.134.grad_pre, bf16[1024,2048]{1,0:T(8,128)(2,1)S(1)} %get-tuple-element.108.refs_7_.there, bf16[3,512,512]{2,1,0:T(8,128)(2,1)S(1)} %copy-done.2), custom_call_target="tpu_custom_call" | custom-call | flops 1342177280 | bytes 9437184 | tf_op jit(solution)/shard_map/pallas_call | solution.py:83
  74.4 0.4 collective-permute-done.17.refs_1_
  75.1 1.5 %shard_map.183.refs_0_ = f32[512,512]{1,0:T(8,128)S(1)} custom-call(f32[512,512]{1,0:T(8,128)S(1)} %shard_map.182.upstream, bf16[2048,512]{1,0:T(8,128)(2,1)S(1)} %get-tuple-element.134.grad_pre, bf16[1024,2048]{1,0:T(8,128)(2,1)S(1)} %get-tuple-element.108.refs_7_.there, bf16[3,512,512]{2,1,0:T(8,128)(2,1)S(1)} %copy-done.4), custom_call_target="tpu_custom_call" | custom-call | flops 1342177280 | bytes 9961472 | tf_op jit(solution)/shard_map/pallas_call | solution.py:83
  76.6 2.6 %shard_map.184 = (f32[512,512]{1,0:T(8,128)S(1)}, bf16[2048,512]{1,0:T(8,128)(2,1)S(1)}, bf16[32,512]{1,0:T(8,128)(2,1)S(1)}, bf16[32,512]{1,0:T(8,128)(2,1)S(1)}) custom-call(f32[512,512]{1,0:T(8,128)S(1)} %shard_map.183.refs_0_, bf16[32,512]{1,0:T(8,128)(2,1)S(1)} %collective-permute-done.17.refs_1_, bf16[32,512]{1,0:T(8,128)(2,1)S(1)} %collective-permute-done.18.refs_2_, ...), custom_call_target="tpu_custom_call" | custom-call | flops 1711276032 | bytes 15472640 | tf_op jit(solution)/shard_map/pallas_call | solution.py:83
  79.2 1.1 collective-permute-start.20
  80.3 2.2 %collective-permute-start.22 = (bf16[32,512]{1,0:T(8,128)(2,1)S(1)}, bf16[32,512]{1,0:T(8,128)(2,1)S(1)}, u32[]{:S(2)}, u32[]{:S(2)}) collective-permute-start(bf16[32,512]{1,0:T(8,128)(2,1)S(1)} %get-tuple-element.146), channel_id=1, source_target_pairs={{4,0},{0,4},{12,8},{8,12},{5,1},{1,5},{13,9},{9,13},{6,2},{2,6},{1... | collective-permute-start | bytes 98312 | tf_op jit(solution)/shard_map/ppermute | solution.py:407
  82.5 1.5 %shard_map.185.upstream = f32[512,512]{1,0:T(8,128)S(1)} custom-call(f32[512,512]{1,0:T(8,128)S(1)} %get-tuple-element.142.upstream, bf16[2048,512]{1,0:T(8,128)(2,1)S(1)} %get-tuple-element.143.grad_pre, bf16[1024,2048]{1,0:T(8,128)(2,1)S(1)} %get-tuple-element.108.refs_7_.there, bf16[3,512,512]{2,1,0:T(8,128)(2,1)S(1)} %copy-done.2), custom_call_target="tpu_custom_call" | custom-call | flops 1342177280 | bytes 9961472 | tf_op jit(solution)/shard_map/pallas_call | solution.py:83
  84.0 0.4 collective-permute-done.20.refs_1_
  84.5 1.5 %shard_map.186.refs_0_ = f32[512,512]{1,0:T(8,128)S(1)} custom-call(f32[512,512]{1,0:T(8,128)S(1)} %shard_map.185.upstream, bf16[2048,512]{1,0:T(8,128)(2,1)S(1)} %get-tuple-element.143.grad_pre, bf16[1024,2048]{1,0:T(8,128)(2,1)S(1)} %get-tuple-element.108.refs_7_.there, bf16[3,512,512]{2,1,0:T(8,128)(2,1)S(1)} %copy-done.4), custom_call_target="tpu_custom_call" | custom-call | flops 1342177280 | bytes 9961472 | tf_op jit(solution)/shard_map/pallas_call | solution.py:83
  86.0 2.8 %shard_map.187 = (f32[512,512]{1,0:T(8,128)S(1)}, bf16[2048,512]{1,0:T(8,128)(2,1)S(1)}, bf16[32,512]{1,0:T(8,128)(2,1)S(1)}, bf16[32,512]{1,0:T(8,128)(2,1)S(1)}) custom-call(f32[512,512]{1,0:T(8,128)S(1)} %shard_map.186.refs_0_, bf16[32,512]{1,0:T(8,128)(2,1)S(1)} %collective-permute-done.20.refs_1_, bf16[32,512]{1,0:T(8,128)(2,1)S(1)} %collective-permute-done.21.refs_2_, ...), custom_call_target="tpu_custom_call" | custom-call | flops 1711276032 | bytes 15472640 | tf_op jit(solution)/shard_map/pallas_call | solution.py:83
  88.8 0.8 collective-permute-start.23
  89.6 2.4 %collective-permute-start.25 = (bf16[32,512]{1,0:T(8,128)(2,1)S(1)}, bf16[32,512]{1,0:T(8,128)(2,1)S(1)}, u32[]{:S(2)}, u32[]{:S(2)}) collective-permute-start(bf16[32,512]{1,0:T(8,128)(2,1)S(1)} %get-tuple-element.154), channel_id=1, source_target_pairs={{4,0},{0,4},{12,8},{8,12},{5,1},{1,5},{13,9},{9,13},{6,2},{2,6},{1... | collective-permute-start | bytes 98312 | tf_op jit(solution)/shard_map/ppermute | solution.py:407
  92.1 1.5 %shard_map.188.upstream = f32[512,512]{1,0:T(8,128)S(1)} custom-call(f32[512,512]{1,0:T(8,128)S(1)} %get-tuple-element.150.upstream, bf16[2048,512]{1,0:T(8,128)(2,1)S(1)} %get-tuple-element.151.grad_pre, bf16[1024,2048]{1,0:T(8,128)(2,1)S(1)} %get-tuple-element.108.refs_7_.there, bf16[3,512,512]{2,1,0:T(8,128)(2,1)S(1)} %copy-done.2), custom_call_target="tpu_custom_call" | custom-call | flops 1342177280 | bytes 9961472 | tf_op jit(solution)/shard_map/pallas_call | solution.py:83
  93.7 0.4 collective-permute-start.24
  94.1 1.5 %shard_map.189.refs_0_ = f32[512,512]{1,0:T(8,128)S(1)} custom-call(f32[512,512]{1,0:T(8,128)S(1)} %shard_map.188.upstream, bf16[2048,512]{1,0:T(8,128)(2,1)S(1)} %get-tuple-element.151.grad_pre, bf16[1024,2048]{1,0:T(8,128)(2,1)S(1)} %get-tuple-element.108.refs_7_.there, bf16[3,512,512]{2,1,0:T(8,128)(2,1)S(1)} %copy-done.4), custom_call_target="tpu_custom_call" | custom-call | flops 1342177280 | bytes 9961472 | tf_op jit(solution)/shard_map/pallas_call | solution.py:83
  95.7 1.4 %shard_map.190 = (bf16[512,512]{1,0:T(8,128)(2,1)S(1)}, bf16[128,512]{1,0:T(8,128)(2,1)S(1)}, bf16[128,512]{1,0:T(8,128)(2,1)S(1)}) custom-call(f32[512,512]{1,0:T(8,128)S(1)} %shard_map.189.refs_0_, bf16[32,512]{1,0:T(8,128)(2,1)S(1)} %collective-permute-done.23.refs_1_, bf16[32,512]{1,0:T(8,128)(2,1)S(1)} %collective-permute-done.24.refs_2_, ...), custom_call_target="tpu_custom_call" | custom-call | flops 503316480 | bytes 5703680 | tf_op jit(solution)/shard_map/pallas_call | solution.py:83
  97.1 1.2 collective-permute-start.26
  98.2 0.9 collective-permute-start.29
  99.2 0.6 shard_map.191
  99.8 3.7 %collective-permute-done.26.passed = bf16[128,512]{1,0:T(8,128)(2,1)S(1)} collective-permute-done((bf16[128,512]{1,0:T(8,128)(2,1)S(1)}, bf16[128,512]{1,0:T(8,128)(2,1)S(1)}, u32[]{:S(2)}, u32[]{:S(2)}) %collective-permute-start.26) | collective-permute-done | bytes 131104 | tf_op jit(solution)/shard_map/ppermute | solution.py:407
  103.5 1.1 collective-permute-start.27
  104.6 2.1 %collective-permute-start.28 = (bf16[128,512]{1,0:T(8,128)(2,1)S(1)}, bf16[128,512]{1,0:T(8,128)(2,1)S(1)}, u32[]{:S(2)}, u32[]{:S(2)}) collective-permute-start(bf16[128,512]{1,0:T(8,128)(2,1)S(1)} %get-tuple-element.170), channel_id=1, source_target_pairs={{8,0},{12,4},{0,8},{4,12},{9,1},{13,5},{1,9},{5,13},{10,2},{14,6},... | collective-permute-start | bytes 393224 | tf_op jit(solution)/shard_map/ppermute | solution.py:407
  106.8 0.9 collective-permute-start.30
  107.7 6.6 %collective-permute-done.28.piece = bf16[128,512]{1,0:T(8,128)(2,1)S(1)} collective-permute-done((bf16[128,512]{1,0:T(8,128)(2,1)S(1)}, bf16[128,512]{1,0:T(8,128)(2,1)S(1)}, u32[]{:S(2)}, u32[]{:S(2)}) %collective-permute-start.28) | collective-permute-done | bytes 131104 | tf_op jit(solution)/shard_map/ppermute | solution.py:407
  114.3 4.6 %collective-permute-done.30.refs_3_ = bf16[128,512]{1,0:T(8,128)(2,1)S(1)} collective-permute-done((bf16[128,512]{1,0:T(8,128)(2,1)S(1)}, bf16[128,512]{1,0:T(8,128)(2,1)S(1)}, u32[]{:S(2)}, u32[]{:S(2)}) %collective-permute-start.30) | collective-permute-done | bytes 131104 | tf_op jit(solution)/shard_map/ppermute | solution.py:407
  118.9 1.3 %shard_map.195 = f32[256,512]{1,0:T(8,128)} custom-call(bf16[256,512]{1,0:T(8,128)(2,1)S(1)} %get-tuple-element.165.own.refs_0_, bf16[256,512]{1,0:T(8,128)(2,1)S(1)} %collective-permute-done.27.refs_1_, f32[128,512]{1,0:T(8,128)S(1)} %shard_map.193.refs_2_, bf16[128,512]{1,0:T(8,128)(2,1)S(1)} %collective-permute-done.30.refs_3_, bf16[512,512]{1,0:T(8,128)(2,1)S(1)} %copy-done.6), custom_call_target="tpu_custom_call" | custom-call | flops 134217728 | bytes 1966080 | tf_op jit(solution)/shard_map/pallas_call | solution.py:83
  (77 shorter events, 1.9 us)
Async XLA Ops:
  0.6 8.2 %copy-start = (s32[1,4,32]{2,1,0:T(4,128)S(1)}, s32[1,4,32]{2,1,0:T(4,128)}, u32[]{:S(2)}) copy-start(s32[1,4,32]{2,1,0:T(4,128)} %param.22) | copy-start | bytes 1540
  1.7 18.6 %collective-permute-start.3 = (bf16[272,512]{1,0:T(8,128)(2,1)S(1)}, bf16[272,512]{1,0:T(8,128)(2,1)S(1)}, u32[]{:S(2)}, u32[]{:S(2)}) collective-permute-start(bf16[272,512]{1,0:T(8,128)(2,1)S(1)} %shard_map.167.refs_5_), channel_id=1, source_target_pairs={{0,4},{4,0},{8,12},{12,8},{1,5},{5,1},{9,13},{13,9},{2,6},{6,2},{1... | collective-permute-start | bytes 835592 | tf_op jit(solution)/shard_map/ppermute | solution.py:402
  4.8 15.0 %collective-permute-start = (bf16[272,512]{1,0:T(8,128)(2,1)S(1)}, bf16[272,512]{1,0:T(8,128)(2,1)S(1)}, u32[]{:S(2)}, u32[]{:S(2)}) collective-permute-start(bf16[272,512]{1,0:T(8,128)(2,1)S(1)} %shard_map.167.refs_5_), channel_id=1, source_target_pairs={{0,8},{4,12},{8,0},{12,4},{1,9},{5,13},{9,1},{13,5},{2,10},{6,14},... | collective-permute-start | bytes 835592 | tf_op jit(solution)/shard_map/ppermute | solution.py:402
  8.7 1.2 collective-permute-start.1
  10.1 3.7 %collective-permute-start.2 = (s32[2,2,512]{2,0,1:T(2,128)S(1)}, s32[2,2,512]{2,0,1:T(2,128)S(1)}, u32[]{:S(2)}, u32[]{:S(2)}) collective-permute-start(s32[2,2,512]{2,0,1:T(2,128)S(1)} %fusion.1), channel_id=1, source_target_pairs={{0,2},{2,0},{1,3},{3,1},{4,6},{6,4},{5,7},{7,5},{8,10},{10,8},{9,1... | collective-permute-start | bytes 24584 | tf_op jit(solution)/shard_map/ppermute | solution.py:393
  14.0 6.4 %copy-start.6 = (bf16[512,512]{1,0:T(8,128)(2,1)S(1)}, bf16[512,512]{1,0:T(8,128)(2,1)}, u32[]{:S(2)}) copy-start(bf16[512,512]{1,0:T(8,128)(2,1)} %refs_4_.3) | copy-start | bytes 1572868
  14.0 6.4 %copy-start.8 = (bf16[512,512]{1,0:T(8,128)(2,1)S(1)}, bf16[512,512]{1,0:T(8,128)(2,1)}, u32[]{:S(2)}) copy-start(bf16[512,512]{1,0:T(8,128)(2,1)} %hidden.1) | copy-start | bytes 1572868
  14.0 6.4 %copy-start.11 = (bf16[512,512]{1,0:T(8,128)(2,1)S(1)}, bf16[512,512]{1,0:T(8,128)(2,1)}, u32[]{:S(2)}) copy-start(bf16[512,512]{1,0:T(8,128)(2,1)} %refs_3_.2) | copy-start | bytes 1572868
  19.8 6.5 %collective-permute-start.4 = (bf16[272,512]{1,0:T(8,128)(2,1)S(1)}, bf16[272,512]{1,0:T(8,128)(2,1)S(1)}, u32[]{:S(2)}, u32[]{:S(2)}) collective-permute-start(bf16[272,512]{1,0:T(8,128)(2,1)S(1)} %collective-permute-done.refs_4_), channel_id=1, source_target_pairs={{0,4},{4,0},{8,12},{12,8},{1,5},{5,1},{9,13},{13,9},{2,6},{6,2},{1... | collective-permute-start | bytes 835592 | tf_op jit(solution)/shard_map/ppermute | solution.py:402
  26.3 12.6 %copy-start.2 = (bf16[3,512,512]{2,1,0:T(8,128)(2,1)S(1)}, bf16[3,512,512]{2,1,0:T(8,128)(2,1)}, u32[]{:S(2)}) copy-start(bf16[3,512,512]{2,1,0:T(8,128)(2,1)} %refs_5_.5) | copy-start | bytes 4718596
  26.3 12.6 %copy-start.5 = (bf16[512,512]{1,0:T(8,128)(2,1)S(1)}, bf16[512,512]{1,0:T(8,128)(2,1)}, u32[]{:S(2)}) copy-start(bf16[512,512]{1,0:T(8,128)(2,1)} %refs_8_.11) | copy-start | bytes 1572868
  26.3 12.6 %copy-start.10 = (f32[512]{0:T(512)S(1)}, f32[512]{0:T(512)}, u32[]{:S(2)}) copy-start(f32[512]{0:T(512)} %param.26) | copy-start | bytes 6148
  27.2 1.6 %collective-permute-start.5 = (bf16[256,512]{1,0:T(8,128)(2,1)S(1)}, bf16[256,512]{1,0:T(8,128)(2,1)S(1)}, u32[]{:S(2)}, u32[]{:S(2)}) collective-permute-start(bf16[256,512]{1,0:T(8,128)(2,1)S(1)} %get-tuple-element.94), channel_id=1, source_target_pairs={{0,1},{1,0},{2,3},{3,2},{4,5},{5,4},{6,7},{7,6},{8,9},{9,8},{10,11... | collective-permute-start | bytes 786440 | tf_op jit(solution)/shard_map/ppermute | solution.py:393
  28.9 14.0 %copy-start.4 = (bf16[3,512,512]{2,1,0:T(8,128)(2,1)S(1)}, bf16[3,512,512]{2,1,0:T(8,128)(2,1)}, u32[]{:S(2)}) copy-start(bf16[3,512,512]{2,1,0:T(8,128)(2,1)} %weights.11) | copy-start | bytes 4718596
  28.9 8.4 %collective-permute-start.6 = (bf16[256,512]{1,0:T(8,128)(2,1)S(1)}, bf16[256,512]{1,0:T(8,128)(2,1)S(1)}, u32[]{:S(2)}, u32[]{:S(2)}) collective-permute-start(bf16[256,512]{1,0:T(8,128)(2,1)S(1)} %add_convert_fusion.1), channel_id=1, source_target_pairs={{0,2},{2,0},{1,3},{3,1},{4,6},{6,4},{5,7},{7,5},{8,10},{10,8},{9,1... | collective-permute-start | bytes 786440 | tf_op jit(solution)/shard_map/ppermute | solution.py:393
  37.4 1.6 %collective-permute-start.7 = (bf16[256,512]{1,0:T(8,128)(2,1)S(1)}, bf16[256,512]{1,0:T(8,128)(2,1)S(1)}, u32[]{:S(2)}, u32[]{:S(2)}) collective-permute-start(bf16[256,512]{1,0:T(8,128)(2,1)S(1)} %add_convert_fusion.refs_1_), channel_id=1, source_target_pairs={{0,1},{1,0},{2,3},{3,2},{4,5},{5,4},{6,7},{7,6},{8,9},{9,8},{10,11... | collective-permute-start | bytes 786440 | tf_op jit(solution)/shard_map/ppermute | solution.py:393
  39.7 5.4 %collective-permute-start.8 = (bf16[32,512]{1,0:T(8,128)(2,1)S(1)}, bf16[32,512]{1,0:T(8,128)(2,1)S(1)}, u32[]{:S(2)}, u32[]{:S(2)}) collective-permute-start(bf16[32,512]{1,0:T(8,128)(2,1)S(1)} %get-tuple-element.95), channel_id=1, source_target_pairs={{0,8},{1,13},{4,12},{5,9},{8,0},{9,5},{12,4},{13,1},{2,10},{3,15},... | collective-permute-start | bytes 98312 | tf_op jit(solution)/shard_map/ppermute | solution.py:544
  41.1 5.5 %collective-permute-start.10 = (bf16[32,512]{1,0:T(8,128)(2,1)S(1)}, bf16[32,512]{1,0:T(8,128)(2,1)S(1)}, u32[]{:S(2)}, u32[]{:S(2)}) collective-permute-start(bf16[32,512]{1,0:T(8,128)(2,1)S(1)} %get-tuple-element.106), channel_id=1, source_target_pairs={{0,4},{4,0},{8,12},{12,8},{1,5},{5,1},{9,13},{13,9},{2,6},{6,2},{1... | collective-permute-start | bytes 98312 | tf_op jit(solution)/shard_map/ppermute | solution.py:402
  45.2 1.4 %copy-start.3 = (bf16[3,512,512]{2,1,0:T(8,128)(2,1)S(1)}, bf16[3,512,512]{2,1,0:T(8,128)(2,1)}, u32[]{:S(2)}) copy-start(bf16[3,512,512]{2,1,0:T(8,128)(2,1)} %refs_9_.9) | copy-start | bytes 4718596
  45.2 1.4 %copy-start.9 = (f32[3,512]{1,0:T(4,128)S(1)}, f32[3,512]{1,0:T(4,128)}, u32[]{:S(2)}) copy-start(f32[3,512]{1,0:T(4,128)} %refs_8_.10) | copy-start | bytes 18436
  45.2 1.3 %collective-permute-start.9 = (bf16[32,512]{1,0:T(8,128)(2,1)S(1)}, bf16[32,512]{1,0:T(8,128)(2,1)S(1)}, u32[]{:S(2)}, u32[]{:S(2)}) collective-permute-start(bf16[32,512]{1,0:T(8,128)(2,1)S(1)} %collective-permute-done.8.refs_3_), channel_id=1, source_target_pairs={{0,1},{1,0},{2,3},{3,2},{4,5},{5,4},{6,7},{7,6},{8,9},{9,8},{10,11... | collective-permute-start | bytes 98312 | tf_op jit(solution)/shard_map/ppermute | solution.py:393
  49.1 5.3 %collective-permute-start.11 = (bf16[32,512]{1,0:T(8,128)(2,1)S(1)}, bf16[32,512]{1,0:T(8,128)(2,1)S(1)}, u32[]{:S(2)}, u32[]{:S(2)}) collective-permute-start(bf16[32,512]{1,0:T(8,128)(2,1)S(1)} %get-tuple-element.109), channel_id=1, source_target_pairs={{0,8},{1,13},{4,12},{5,9},{8,0},{9,5},{12,4},{13,1},{2,10},{3,15},... | collective-permute-start | bytes 98312 | tf_op jit(solution)/shard_map/ppermute | solution.py:544
  50.3 5.4 %collective-permute-start.13 = (bf16[32,512]{1,0:T(8,128)(2,1)S(1)}, bf16[32,512]{1,0:T(8,128)(2,1)S(1)}, u32[]{:S(2)}, u32[]{:S(2)}) collective-permute-start(bf16[32,512]{1,0:T(8,128)(2,1)S(1)} %get-tuple-element.119), channel_id=1, source_target_pairs={{0,4},{4,0},{8,12},{12,8},{1,5},{5,1},{9,13},{13,9},{2,6},{6,2},{1... | collective-permute-start | bytes 98312 | tf_op jit(solution)/shard_map/ppermute | solution.py:402
  54.3 1.4 %collective-permute-start.12 = (bf16[32,512]{1,0:T(8,128)(2,1)S(1)}, bf16[32,512]{1,0:T(8,128)(2,1)S(1)}, u32[]{:S(2)}, u32[]{:S(2)}) collective-permute-start(bf16[32,512]{1,0:T(8,128)(2,1)S(1)} %collective-permute-done.11.refs_3_), channel_id=1, source_target_pairs={{0,1},{1,0},{2,3},{3,2},{4,5},{5,4},{6,7},{7,6},{8,9},{9,8},{10,11... | collective-permute-start | bytes 98312 | tf_op jit(solution)/shard_map/ppermute | solution.py:393
  58.3 5.4 %collective-permute-start.14 = (bf16[32,512]{1,0:T(8,128)(2,1)S(1)}, bf16[32,512]{1,0:T(8,128)(2,1)S(1)}, u32[]{:S(2)}, u32[]{:S(2)}) collective-permute-start(bf16[32,512]{1,0:T(8,128)(2,1)S(1)} %get-tuple-element.120), channel_id=1, source_target_pairs={{0,8},{1,13},{4,12},{5,9},{8,0},{9,5},{12,4},{13,1},{2,10},{3,15},... | collective-permute-start | bytes 98312 | tf_op jit(solution)/shard_map/ppermute | solution.py:544
  59.6 5.4 %collective-permute-start.16 = (bf16[32,512]{1,0:T(8,128)(2,1)S(1)}, bf16[32,512]{1,0:T(8,128)(2,1)S(1)}, u32[]{:S(2)}, u32[]{:S(2)}) collective-permute-start(bf16[32,512]{1,0:T(8,128)(2,1)S(1)} %get-tuple-element.130), channel_id=1, source_target_pairs={{0,4},{4,0},{8,12},{12,8},{1,5},{5,1},{9,13},{13,9},{2,6},{6,2},{1... | collective-permute-start | bytes 98312 | tf_op jit(solution)/shard_map/ppermute | solution.py:402
  63.7 1.4 %copy-start.7 = (bf16[512,512]{1,0:T(8,128)(2,1)S(1)}, bf16[512,512]{1,0:T(8,128)(2,1)}, u32[]{:S(2)}) copy-start(bf16[512,512]{1,0:T(8,128)(2,1)} %upstream.1) | copy-start | bytes 1572868
  63.7 1.3 %collective-permute-start.15 = (bf16[32,512]{1,0:T(8,128)(2,1)S(1)}, bf16[32,512]{1,0:T(8,128)(2,1)S(1)}, u32[]{:S(2)}, u32[]{:S(2)}) collective-permute-start(bf16[32,512]{1,0:T(8,128)(2,1)S(1)} %collective-permute-done.14.refs_3_), channel_id=1, source_target_pairs={{0,1},{1,0},{2,3},{3,2},{4,5},{5,4},{6,7},{7,6},{8,9},{9,8},{10,11... | collective-permute-start | bytes 98312 | tf_op jit(solution)/shard_map/ppermute | solution.py:393
  70.0 4.8 %collective-permute-start.17 = (bf16[32,512]{1,0:T(8,128)(2,1)S(1)}, bf16[32,512]{1,0:T(8,128)(2,1)S(1)}, u32[]{:S(2)}, u32[]{:S(2)}) collective-permute-start(bf16[32,512]{1,0:T(8,128)(2,1)S(1)} %get-tuple-element.133), channel_id=1, source_target_pairs={{0,8},{1,13},{4,12},{5,9},{8,0},{9,5},{12,4},{13,1},{2,10},{3,15},... | collective-permute-start | bytes 98312 | tf_op jit(solution)/shard_map/ppermute | solution.py:544
  71.3 5.3 %collective-permute-start.19 = (bf16[32,512]{1,0:T(8,128)(2,1)S(1)}, bf16[32,512]{1,0:T(8,128)(2,1)S(1)}, u32[]{:S(2)}, u32[]{:S(2)}) collective-permute-start(bf16[32,512]{1,0:T(8,128)(2,1)S(1)} %get-tuple-element.137), channel_id=1, source_target_pairs={{4,0},{0,4},{12,8},{8,12},{5,1},{1,5},{13,9},{9,13},{6,2},{2,6},{1... | collective-permute-start | bytes 98312 | tf_op jit(solution)/shard_map/ppermute | solution.py:407
  74.8 1.8 %collective-permute-start.18 = (bf16[32,512]{1,0:T(8,128)(2,1)S(1)}, bf16[32,512]{1,0:T(8,128)(2,1)S(1)}, u32[]{:S(2)}, u32[]{:S(2)}) collective-permute-start(bf16[32,512]{1,0:T(8,128)(2,1)S(1)} %collective-permute-done.17.refs_1_), channel_id=1, source_target_pairs={{0,1},{1,0},{2,3},{3,2},{4,5},{5,4},{6,7},{7,6},{8,9},{9,8},{10,11... | collective-permute-start | bytes 98312 | tf_op jit(solution)/shard_map/ppermute | solution.py:393
  79.2 5.3 %collective-permute-start.20 = (bf16[32,512]{1,0:T(8,128)(2,1)S(1)}, bf16[32,512]{1,0:T(8,128)(2,1)S(1)}, u32[]{:S(2)}, u32[]{:S(2)}) collective-permute-start(bf16[32,512]{1,0:T(8,128)(2,1)S(1)} %get-tuple-element.141), channel_id=1, source_target_pairs={{0,8},{1,13},{4,12},{5,9},{8,0},{9,5},{12,4},{13,1},{2,10},{3,15},... | collective-permute-start | bytes 98312 | tf_op jit(solution)/shard_map/ppermute | solution.py:544
  80.3 5.7 %collective-permute-start.22 = (bf16[32,512]{1,0:T(8,128)(2,1)S(1)}, bf16[32,512]{1,0:T(8,128)(2,1)S(1)}, u32[]{:S(2)}, u32[]{:S(2)}) collective-permute-start(bf16[32,512]{1,0:T(8,128)(2,1)S(1)} %get-tuple-element.146), channel_id=1, source_target_pairs={{4,0},{0,4},{12,8},{8,12},{5,1},{1,5},{13,9},{9,13},{6,2},{2,6},{1... | collective-permute-start | bytes 98312 | tf_op jit(solution)/shard_map/ppermute | solution.py:407
  84.5 1.5 %collective-permute-start.21 = (bf16[32,512]{1,0:T(8,128)(2,1)S(1)}, bf16[32,512]{1,0:T(8,128)(2,1)S(1)}, u32[]{:S(2)}, u32[]{:S(2)}) collective-permute-start(bf16[32,512]{1,0:T(8,128)(2,1)S(1)} %collective-permute-done.20.refs_1_), channel_id=1, source_target_pairs={{0,1},{1,0},{2,3},{3,2},{4,5},{5,4},{6,7},{7,6},{8,9},{9,8},{10,11... | collective-permute-start | bytes 98312 | tf_op jit(solution)/shard_map/ppermute | solution.py:393
  88.8 4.9 %collective-permute-start.23 = (bf16[32,512]{1,0:T(8,128)(2,1)S(1)}, bf16[32,512]{1,0:T(8,128)(2,1)S(1)}, u32[]{:S(2)}, u32[]{:S(2)}) collective-permute-start(bf16[32,512]{1,0:T(8,128)(2,1)S(1)} %get-tuple-element.149), channel_id=1, source_target_pairs={{0,8},{1,13},{4,12},{5,9},{8,0},{9,5},{12,4},{13,1},{2,10},{3,15},... | collective-permute-start | bytes 98312 | tf_op jit(solution)/shard_map/ppermute | solution.py:544
  89.6 6.0 %collective-permute-start.25 = (bf16[32,512]{1,0:T(8,128)(2,1)S(1)}, bf16[32,512]{1,0:T(8,128)(2,1)S(1)}, u32[]{:S(2)}, u32[]{:S(2)}) collective-permute-start(bf16[32,512]{1,0:T(8,128)(2,1)S(1)} %get-tuple-element.154), channel_id=1, source_target_pairs={{4,0},{0,4},{12,8},{8,12},{5,1},{1,5},{13,9},{9,13},{6,2},{2,6},{1... | collective-permute-start | bytes 98312 | tf_op jit(solution)/shard_map/ppermute | solution.py:407
  93.7 2.0 %collective-permute-start.24 = (bf16[32,512]{1,0:T(8,128)(2,1)S(1)}, bf16[32,512]{1,0:T(8,128)(2,1)S(1)}, u32[]{:S(2)}, u32[]{:S(2)}) collective-permute-start(bf16[32,512]{1,0:T(8,128)(2,1)S(1)} %collective-permute-done.23.refs_1_), channel_id=1, source_target_pairs={{0,1},{1,0},{2,3},{3,2},{4,5},{5,4},{6,7},{7,6},{8,9},{9,8},{10,11... | collective-permute-start | bytes 98312 | tf_op jit(solution)/shard_map/ppermute | solution.py:393
  97.1 6.4 %collective-permute-start.26 = (bf16[128,512]{1,0:T(8,128)(2,1)S(1)}, bf16[128,512]{1,0:T(8,128)(2,1)S(1)}, u32[]{:S(2)}, u32[]{:S(2)}) collective-permute-start(bf16[128,512]{1,0:T(8,128)(2,1)S(1)} %get-tuple-element.167), channel_id=1, source_target_pairs={{4,0},{0,4},{12,8},{8,12},{5,1},{1,5},{13,9},{9,13},{6,2},{2,6},{1... | collective-permute-start | bytes 393224 | tf_op jit(solution)/shard_map/ppermute | solution.py:407
  98.2 8.5 %collective-permute-start.29 = (bf16[128,512]{1,0:T(8,128)(2,1)S(1)}, bf16[128,512]{1,0:T(8,128)(2,1)S(1)}, u32[]{:S(2)}, u32[]{:S(2)}) collective-permute-start(bf16[128,512]{1,0:T(8,128)(2,1)S(1)} %get-tuple-element.171), channel_id=1, source_target_pairs={{4,0},{0,4},{12,8},{8,12},{5,1},{1,5},{13,9},{9,13},{6,2},{2,6},{1... | collective-permute-start | bytes 393224 | tf_op jit(solution)/shard_map/ppermute | solution.py:407
  99.2 21.0 %copy-start.1 = (s32[1,4,32]{2,1,0:T(4,128)S(1)}, s32[1,4,32]{2,1,0:T(4,128)}, u32[]{:S(2)}) copy-start(s32[1,4,32]{2,1,0:T(4,128)} %param.22) | copy-start | bytes 1540
  103.5 15.4 %collective-permute-start.27 = (bf16[256,512]{1,0:T(8,128)(2,1)S(1)}, bf16[256,512]{1,0:T(8,128)(2,1)S(1)}, u32[]{:S(2)}, u32[]{:S(2)}) collective-permute-start(bf16[256,512]{1,0:T(8,128)(2,1)S(1)} %get-tuple-element.169), channel_id=1, source_target_pairs={{4,0},{0,4},{12,8},{8,12},{5,1},{1,5},{13,9},{9,13},{6,2},{2,6},{1... | collective-permute-start | bytes 786440 | tf_op jit(solution)/shard_map/ppermute | solution.py:407
  104.6 9.6 %collective-permute-start.28 = (bf16[128,512]{1,0:T(8,128)(2,1)S(1)}, bf16[128,512]{1,0:T(8,128)(2,1)S(1)}, u32[]{:S(2)}, u32[]{:S(2)}) collective-permute-start(bf16[128,512]{1,0:T(8,128)(2,1)S(1)} %get-tuple-element.170), channel_id=1, source_target_pairs={{8,0},{12,4},{0,8},{4,12},{9,1},{13,5},{1,9},{5,13},{10,2},{14,6},... | collective-permute-start | bytes 393224 | tf_op jit(solution)/shard_map/ppermute | solution.py:407
  106.8 12.2 %collective-permute-start.30 = (bf16[128,512]{1,0:T(8,128)(2,1)S(1)}, bf16[128,512]{1,0:T(8,128)(2,1)S(1)}, u32[]{:S(2)}, u32[]{:S(2)}) collective-permute-start(bf16[128,512]{1,0:T(8,128)(2,1)S(1)} %shard_map.194), channel_id=1, source_target_pairs={{8,0},{12,4},{0,8},{4,12},{9,1},{13,5},{1,9},{5,13},{10,2},{14,6},... | collective-permute-start | bytes 393224 | tf_op jit(solution)/shard_map/ppermute | solution.py:407

commit v15 on v12

--- a/solution.py
+++ b/solution.py
@@ -360,12 +360,9 @@
         out[...] = pair_grads(spread, pick[skip:, :], slope[skip:, :])
 
 
-def relay_kernel(first, own, passed, *refs):
+def relay_kernel(first, own, passed, out):
     rows = passed.shape[0]
-    out = refs[0] if len(refs) == 1 else refs[-2]
     out[...] = (own[first : first + rows, :].astype(f32) + passed[...].astype(f32)).astype(bf16)
-    if len(refs) > 1:
-        refs[-1][...] = refs[0][...]
 
 
 def sum_kernel(own, piece, total):
@@ -617,9 +614,9 @@
     )(spread, *enc_picks[:-1], *enc_slopes[:-1])
     if relayed:
         passed = [sent_back(block, 1) for block in far]
-        first, near = call(functools.partial(relay_kernel, 0), [piece, row_shape])(blocks[2], passed[0], blocks[1])
+        (first,) = call(functools.partial(relay_kernel, 0), [piece])(blocks[2], passed[0])
         (second,) = call(functools.partial(relay_kernel, piece_rows), [piece])(blocks[2], passed[1])
-        near = sent_back(near, 1)
+        near = sent_back(blocks[1], 1)
         first, second = sent_back(first, 2), sent_back(second, 2)
         (summed,) = call(sum_kernel, [((piece_rows, width), f32)])(blocks[0], first)
         (grid_grad,) = call(

time: 120 us -> 121 us (level)
  waiting for transfers between devices: 33.7 us -> 35.4 us
  starting transfers between devices: 35.6 us -> 34.2 us
    ppermute x8, waiting for transfers between devices: 15 us -> 16.7 us  [sent_back(): lax.ppermute(value, 'mesh', [(partner(at, step, size), at) for at in rang...]
    ppermute x8, starting transfers between devices: 12.7 us -> 11.2 us  [sent_back(): lax.ppermute(value, 'mesh', [(partner(at, step, size), at) for at in rang...]
  transfers between devices with their start and end apart: 31 -> 31, of which waited for: 12 -> 14; matrix products, arithmetic and copies ran while one was open for 2% -> 2% of each run, Pallas kernels for 22% -> 22%
where the time goes in v15:
time: 121 us; the launch traced here: 120 us
  Pallas kernels  46.8 us (39%)
  waiting for transfers between devices  35.4 us (29%)
  starting transfers between devices  34.2 us (28%)
  other arithmetic  1.83 us (2%)
    pallas_call x29, Pallas kernels, run(): pl.pallas_call(body, out_shape=tuple((jax.ShapeDtypeStruct(shape, dtype)...  46.8 us
    ppermute x8, waiting for transfers between devices, sent_back(): lax.ppermute(value, 'mesh', [(partner(at, step, size), at) for at in rang...  16.7 us
    ppermute x11, waiting for transfers between devices, shifted(): lax.ppermute(value, axis, [(at, (at + by) % size) for at in range(size)])  12.4 us
    ppermute x6, starting transfers between devices, sent_to(): lax.ppermute(value, 'mesh', [(at, partner(at, step, size)) for at in rang...  11.3 us
    ppermute x8, starting transfers between devices, sent_back(): lax.ppermute(value, 'mesh', [(partner(at, step, size), at) for at in rang...  11.2 us
    ppermute x6, starting transfers between devices, exchange(): lax.ppermute(blocks[0], ('mesh', 'rep'), [(2 * at + side, 2 * (at ^ 2 + s...  7.42 us
    ppermute x6, waiting for transfers between devices, sent_to(): lax.ppermute(value, 'mesh', [(at, partner(at, step, size)) for at in rang...  5.84 us
    ppermute x11, starting transfers between devices, shifted(): lax.ppermute(value, axis, [(at, (at + by) % size) for at in range(size)])  4.28 us
  transfers between devices with their start and end apart: 31, of which 14 were waited for; matrix products, arithmetic and copies ran while one was open for 2% of the time, Pallas kernels for 22%

profile of v15, /device:TPU:0, one launch (start us, length us, event | category | flops | bytes accessed | tf_op | source)
XLA Modules:
  0.0 120.5 jit_solution(16922198883982752212)
XLA Ops:
  0.6 1.0 shard_map.167.refs_5_
  1.7 3.1 %collective-permute-start.3 = (bf16[272,512]{1,0:T(8,128)(2,1)S(1)}, bf16[272,512]{1,0:T(8,128)(2,1)S(1)}, u32[]{:S(2)}, u32[]{:S(2)}) collective-permute-start(bf16[272,512]{1,0:T(8,128)(2,1)S(1)} %shard_map.167.refs_5_), channel_id=1, source_target_pairs={{0,4},{4,0},{8,12},{12,8},{1,5},{5,1},{9,13},{13,9},{2,6},{6,2},{1... | collective-permute-start | bytes 835592 | tf_op jit(solution)/shard_map/ppermute | solution.py:399
  4.8 2.6 %collective-permute-start = (bf16[272,512]{1,0:T(8,128)(2,1)S(1)}, bf16[272,512]{1,0:T(8,128)(2,1)S(1)}, u32[]{:S(2)}, u32[]{:S(2)}) collective-permute-start(bf16[272,512]{1,0:T(8,128)(2,1)S(1)} %shard_map.167.refs_5_), channel_id=1, source_target_pairs={{0,8},{4,12},{8,0},{12,4},{1,9},{5,13},{9,1},{13,5},{2,10},{6,14},... | collective-permute-start | bytes 835592 | tf_op jit(solution)/shard_map/ppermute | solution.py:399
  7.3 0.7 compare_select_fusion.1
  8.0 0.7 fusion.11
  8.8 0.6 gather_fusion
  9.5 0.4 collective-permute-done.1
  10.1 1.6 %collective-permute-start.2 = (s32[2,2,512]{2,0,1:T(2,128)S(1)}, s32[2,2,512]{2,0,1:T(2,128)S(1)}, u32[]{:S(2)}, u32[]{:S(2)}) collective-permute-start(s32[2,2,512]{2,0,1:T(2,128)S(1)} %fusion.1), channel_id=1, source_target_pairs={{0,2},{2,0},{1,3},{3,1},{4,6},{6,4},{5,7},{7,5},{8,10},{10,8},{9,1... | collective-permute-start | bytes 24584 | tf_op jit(solution)/shard_map/ppermute | solution.py:390
  11.7 2.1 %collective-permute-done.2 = s32[2,2,512]{2,0,1:T(2,128)S(1)} collective-permute-done((s32[2,2,512]{2,0,1:T(2,128)S(1)}, s32[2,2,512]{2,0,1:T(2,128)S(1)}, u32[]{:S(2)}, u32[]{:S(2)}) %collective-permute-start.2) | collective-permute-done | bytes 8224 | tf_op jit(solution)/shard_map/ppermute | solution.py:390
  14.0 3.5 %shard_map.168 = (bf16[2048,1024]{1,0:T(8,128)(2,1)S(1)}, bf16[1024,2048]{1,0:T(8,128)(2,1)S(1)}, bf16[2048,128]{1,0:T(8,128)(2,1)S(1)}, bf16[128,2048]{1,0:T(8,...) custom-call(s32[1,2048]{1,0:T(1,128)S(1)} %fusion.2.slots, s32[1,2048]{1,0:T(1,128)S(1)} %bitcast.29, ...), custom_call_target="tpu_custom_call" | custom-call | flops 3221225472 | bytes 9650560 | tf_op jit(solution)/shard_map/pallas_call | solution.py:83
  17.5 2.3 %collective-permute-done.refs_4_ = bf16[272,512]{1,0:T(8,128)(2,1)S(1)} collective-permute-done((bf16[272,512]{1,0:T(8,128)(2,1)S(1)}, bf16[272,512]{1,0:T(8,128)(2,1)S(1)}, u32[]{:S(2)}, u32[]{:S(2)}) %collective-permute-start) | collective-permute-done | bytes 278560 | tf_op jit(solution)/shard_map/ppermute | solution.py:399
  19.8 0.4 collective-permute-start.4
  20.4 1.6 %shard_map.169 = (bf16[256,512]{1,0:T(8,128)(2,1)S(1)}, bf16[256,512]{1,0:T(8,128)(2,1)S(1)}, bf16[256,512]{1,0:T(8,128)(2,1)S(1)}, bf16[256,512]{1,0:T(8,128)(2...) custom-call(s32[2,512]{1,0:T(2,128)S(1)} %broadcast_in_dim.27.refs_0_, bf16[512,512]{1,0:T(8,128)(2,1)S(1)} %copy-done.8, ...), custom_call_target="tpu_custom_call" | custom-call | flops 1073741824 | bytes 4853760 | tf_op jit(solution)/shard_map/pallas_call | solution.py:83
  22.0 0.8 shard_map.170
  22.8 3.5 %collective-permute-done.4.refs_4_ = bf16[272,512]{1,0:T(8,128)(2,1)S(1)} collective-permute-done((bf16[272,512]{1,0:T(8,128)(2,1)S(1)}, bf16[272,512]{1,0:T(8,128)(2,1)S(1)}, u32[]{:S(2)}, u32[]{:S(2)}) %collective-permute-start.4) | collective-permute-done | bytes 278560 | tf_op jit(solution)/shard_map/ppermute | solution.py:399
  26.3 0.8 shard_map.171
  27.3 1.5 %collective-permute-done.5 = bf16[256,512]{1,0:T(8,128)(2,1)S(1)} collective-permute-done((bf16[256,512]{1,0:T(8,128)(2,1)S(1)}, bf16[256,512]{1,0:T(8,128)(2,1)S(1)}, u32[]{:S(2)}, u32[]{:S(2)}) %collective-permute-start.5) | collective-permute-done | bytes 262176 | tf_op jit(solution)/shard_map/ppermute | solution.py:390
  28.9 1.6 %collective-permute-start.6 = (bf16[256,512]{1,0:T(8,128)(2,1)S(1)}, bf16[256,512]{1,0:T(8,128)(2,1)S(1)}, u32[]{:S(2)}, u32[]{:S(2)}) collective-permute-start(bf16[256,512]{1,0:T(8,128)(2,1)S(1)} %add_convert_fusion.1), channel_id=1, source_target_pairs={{0,2},{2,0},{1,3},{3,1},{4,6},{6,4},{5,7},{7,5},{8,10},{10,8},{9,1... | collective-permute-start | bytes 786440 | tf_op jit(solution)/shard_map/ppermute | solution.py:390
  30.5 6.9 %collective-permute-done.6 = bf16[256,512]{1,0:T(8,128)(2,1)S(1)} collective-permute-done((bf16[256,512]{1,0:T(8,128)(2,1)S(1)}, bf16[256,512]{1,0:T(8,128)(2,1)S(1)}, u32[]{:S(2)}, u32[]{:S(2)}) %collective-permute-start.6) | collective-permute-done | bytes 262176 | tf_op jit(solution)/shard_map/ppermute | solution.py:390
  37.5 1.5 %collective-permute-done.7.refs_2_ = bf16[256,512]{1,0:T(8,128)(2,1)S(1)} collective-permute-done((bf16[256,512]{1,0:T(8,128)(2,1)S(1)}, bf16[256,512]{1,0:T(8,128)(2,1)S(1)}, u32[]{:S(2)}, u32[]{:S(2)}) %collective-permute-start.7) | collective-permute-done | bytes 262176 | tf_op jit(solution)/shard_map/ppermute | solution.py:390
  39.0 0.7 shard_map.172
  39.7 1.3 %collective-permute-start.8 = (bf16[32,512]{1,0:T(8,128)(2,1)S(1)}, bf16[32,512]{1,0:T(8,128)(2,1)S(1)}, u32[]{:S(2)}, u32[]{:S(2)}) collective-permute-start(bf16[32,512]{1,0:T(8,128)(2,1)S(1)} %get-tuple-element.93), channel_id=1, source_target_pairs={{0,8},{1,13},{4,12},{5,9},{8,0},{9,5},{12,4},{13,1},{2,10},{3,15},... | collective-permute-start | bytes 98312 | tf_op jit(solution)/shard_map/ppermute | solution.py:541
  41.1 1.9 %collective-permute-start.10 = (bf16[32,512]{1,0:T(8,128)(2,1)S(1)}, bf16[32,512]{1,0:T(8,128)(2,1)S(1)}, u32[]{:S(2)}, u32[]{:S(2)}) collective-permute-start(bf16[32,512]{1,0:T(8,128)(2,1)S(1)} %get-tuple-element.104), channel_id=1, source_target_pairs={{0,4},{4,0},{8,12},{12,8},{1,5},{5,1},{9,13},{13,9},{2,6},{6,2},{1... | collective-permute-start | bytes 98312 | tf_op jit(solution)/shard_map/ppermute | solution.py:399
  42.9 2.2 %shard_map.173 = (bf16[512,512]{1,0:T(8,128)(2,1)S(1)}, f32[512,512]{1,0:T(8,128)S(1)}, f32[1024,512]{1,0:T(8,128)S(1)}, bf16[1024,512]{1,0:T(8,128)(2,1)S(1)}) custom-call(bf16[512,512]{1,0:T(8,128)(2,1)S(1)} %get-tuple-element.94.total, bf16[512,512]{1,0:T(8,128)(2,1)S(1)} %copy-done.8, bf16[512,512]{1,0:T(8,128)(2,1)S(1)} %copy-done.5, ...), custom_call_target="tpu_custom_call" | custom-call | flops 1879048192 | bytes 13633536 | tf_op jit(solution)/shard_map/pallas_call | solution.py:83
  45.3 1.2 %shard_map.174.refs_2_ = f32[1024,512]{1,0:T(8,128)S(1)} custom-call(bf16[1024,512]{1,0:T(8,128)(2,1)S(1)} %get-tuple-element.102.table, bf16[2048,1024]{1,0:T(8,128)(2,1)S(1)} %get-tuple-element.95.here.refs_10_), custom_call_target="tpu_custom_call" | custom-call | flops 1073741824 | bytes 7340032 | tf_op jit(solution)/shard_map/pallas_call | solution.py:83
  46.6 2.5 %shard_map.175 = (bf16[512,512]{1,0:T(8,128)(2,1)S(1)}, bf16[2048,512]{1,0:T(8,128)(2,1)S(1)}, bf16[32,512]{1,0:T(8,128)(2,1)S(1)}, bf16[32,512]{1,0:T(8,128)(2,1)S(1)}) custom-call(bf16[512,512]{1,0:T(8,128)(2,1)S(1)} %get-tuple-element.100.refs_0_.hidden, f32[1024,512]{1,0:T(8,128)S(1)} %get-tuple-element.101.refs_1_, f32[1024,512]{1,0:T(8,128)S(1)} %shard_map.174.refs_2_, ...), custom_call_target="tpu_custom_call" | custom-call | flops 1543503872 | bytes 15472640 | tf_op jit(solution)/shard_map/pallas_call | solution.py:83
  49.1 1.2 %collective-permute-start.11 = (bf16[32,512]{1,0:T(8,128)(2,1)S(1)}, bf16[32,512]{1,0:T(8,128)(2,1)S(1)}, u32[]{:S(2)}, u32[]{:S(2)}) collective-permute-start(bf16[32,512]{1,0:T(8,128)(2,1)S(1)} %get-tuple-element.107), channel_id=1, source_target_pairs={{0,8},{1,13},{4,12},{5,9},{8,0},{9,5},{12,4},{13,1},{2,10},{3,15},... | collective-permute-start | bytes 98312 | tf_op jit(solution)/shard_map/ppermute | solution.py:541
  50.3 1.8 %collective-permute-start.13 = (bf16[32,512]{1,0:T(8,128)(2,1)S(1)}, bf16[32,512]{1,0:T(8,128)(2,1)S(1)}, u32[]{:S(2)}, u32[]{:S(2)}) collective-permute-start(bf16[32,512]{1,0:T(8,128)(2,1)S(1)} %get-tuple-element.117), channel_id=1, source_target_pairs={{0,4},{4,0},{8,12},{12,8},{1,5},{5,1},{9,13},{13,9},{2,6},{6,2},{1... | collective-permute-start | bytes 98312 | tf_op jit(solution)/shard_map/ppermute | solution.py:399
  52.1 2.2 %shard_map.176 = (bf16[512,512]{1,0:T(8,128)(2,1)S(1)}, f32[512,512]{1,0:T(8,128)S(1)}, f32[1024,512]{1,0:T(8,128)S(1)}, bf16[1024,512]{1,0:T(8,128)(2,1)S(1)}) custom-call(bf16[512,512]{1,0:T(8,128)(2,1)S(1)} %get-tuple-element.108.total, bf16[512,512]{1,0:T(8,128)(2,1)S(1)} %get-tuple-element.100.refs_0_.hidden, bf16[3,512,512]{2,1,0:T(8,128)(2,1)S(1)} %copy-done.3, ...), custom_call_target="tpu_custom_call" | custom-call | flops 1879048192 | bytes 14686208 | tf_op jit(solution)/shard_map/pallas_call | solution.py:83
  54.5 1.2 %shard_map.177.refs_2_ = f32[1024,512]{1,0:T(8,128)S(1)} custom-call(bf16[1024,512]{1,0:T(8,128)(2,1)S(1)} %get-tuple-element.115.table, bf16[2048,1024]{1,0:T(8,128)(2,1)S(1)} %get-tuple-element.95.here.refs_10_), custom_call_target="tpu_custom_call" | custom-call | flops 1073741824 | bytes 7340032 | tf_op jit(solution)/shard_map/pallas_call | solution.py:83
  55.8 2.6 %shard_map.178 = (bf16[512,512]{1,0:T(8,128)(2,1)S(1)}, bf16[2048,512]{1,0:T(8,128)(2,1)S(1)}, bf16[32,512]{1,0:T(8,128)(2,1)S(1)}, bf16[32,512]{1,0:T(8,128)(2,1)S(1)}) custom-call(bf16[512,512]{1,0:T(8,128)(2,1)S(1)} %get-tuple-element.113.refs_0_.hidden, f32[1024,512]{1,0:T(8,128)S(1)} %get-tuple-element.114.refs_1_, f32[1024,512]{1,0:T(8,128)S(1)} %shard_map.177.refs_2_, ...), custom_call_target="tpu_custom_call" | custom-call | flops 1543503872 | bytes 15472640 | tf_op jit(solution)/shard_map/pallas_call | solution.py:83
  58.3 1.3 %collective-permute-start.14 = (bf16[32,512]{1,0:T(8,128)(2,1)S(1)}, bf16[32,512]{1,0:T(8,128)(2,1)S(1)}, u32[]{:S(2)}, u32[]{:S(2)}) collective-permute-start(bf16[32,512]{1,0:T(8,128)(2,1)S(1)} %get-tuple-element.118), channel_id=1, source_target_pairs={{0,8},{1,13},{4,12},{5,9},{8,0},{9,5},{12,4},{13,1},{2,10},{3,15},... | collective-permute-start | bytes 98312 | tf_op jit(solution)/shard_map/ppermute | solution.py:541
  59.7 1.5 %collective-permute-start.16 = (bf16[32,512]{1,0:T(8,128)(2,1)S(1)}, bf16[32,512]{1,0:T(8,128)(2,1)S(1)}, u32[]{:S(2)}, u32[]{:S(2)}) collective-permute-start(bf16[32,512]{1,0:T(8,128)(2,1)S(1)} %get-tuple-element.128), channel_id=1, source_target_pairs={{0,4},{4,0},{8,12},{12,8},{1,5},{5,1},{9,13},{13,9},{2,6},{6,2},{1... | collective-permute-start | bytes 98312 | tf_op jit(solution)/shard_map/ppermute | solution.py:399
  61.1 2.4 %shard_map.179 = (bf16[512,512]{1,0:T(8,128)(2,1)S(1)}, f32[512,512]{1,0:T(8,128)S(1)}, f32[1024,512]{1,0:T(8,128)S(1)}, bf16[1024,512]{1,0:T(8,128)(2,1)S(1)}) custom-call(bf16[512,512]{1,0:T(8,128)(2,1)S(1)} %get-tuple-element.119.total, bf16[512,512]{1,0:T(8,128)(2,1)S(1)} %get-tuple-element.113.refs_0_.hidden, bf16[3,512,512]{2,1,0:T(8,128)(2,1)S(1)} %copy-done.3, ...), custom_call_target="tpu_custom_call" | custom-call | flops 1879048192 | bytes 14686208 | tf_op jit(solution)/shard_map/pallas_call | solution.py:83
  63.6 1.2 %shard_map.180.refs_2_ = f32[1024,512]{1,0:T(8,128)S(1)} custom-call(bf16[1024,512]{1,0:T(8,128)(2,1)S(1)} %get-tuple-element.126.table, bf16[2048,1024]{1,0:T(8,128)(2,1)S(1)} %get-tuple-element.95.here.refs_10_), custom_call_target="tpu_custom_call" | custom-call | flops 1073741824 | bytes 7340032 | tf_op jit(solution)/shard_map/pallas_call | solution.py:83
  64.9 5.0 %shard_map.181 = (bf16[512,512]{1,0:T(8,128)(2,1)}, bf16[2048,512]{1,0:T(8,128)(2,1)S(1)}, bf16[32,512]{1,0:T(8,128)(2,1)S(1)}, bf16[32,512]{1,0:T(8,128)(2,1)S(1)}) custom-call(bf16[512,512]{1,0:T(8,128)(2,1)S(1)} %get-tuple-element.124.refs_0_, f32[1024,512]{1,0:T(8,128)S(1)} %get-tuple-element.125.refs_1_, f32[1024,512]{1,0:T(8,128)S(1)} %shard_map.180.refs_2_, ...), custom_call_target="tpu_custom_call" | custom-call | flops 3221225472 | bytes 19044352 | tf_op jit(solution)/shard_map/pallas_call | solution.py:83
  69.8 1.5 %collective-permute-start.17 = (bf16[32,512]{1,0:T(8,128)(2,1)S(1)}, bf16[32,512]{1,0:T(8,128)(2,1)S(1)}, u32[]{:S(2)}, u32[]{:S(2)}) collective-permute-start(bf16[32,512]{1,0:T(8,128)(2,1)S(1)} %get-tuple-element.131), channel_id=1, source_target_pairs={{0,8},{1,13},{4,12},{5,9},{8,0},{9,5},{12,4},{13,1},{2,10},{3,15},... | collective-permute-start | bytes 98312 | tf_op jit(solution)/shard_map/ppermute | solution.py:541
  71.4 1.6 %collective-permute-start.19 = (bf16[32,512]{1,0:T(8,128)(2,1)S(1)}, bf16[32,512]{1,0:T(8,128)(2,1)S(1)}, u32[]{:S(2)}, u32[]{:S(2)}) collective-permute-start(bf16[32,512]{1,0:T(8,128)(2,1)S(1)} %get-tuple-element.135), channel_id=1, source_target_pairs={{4,0},{0,4},{12,8},{8,12},{5,1},{1,5},{13,9},{9,13},{6,2},{2,6},{1... | collective-permute-start | bytes 98312 | tf_op jit(solution)/shard_map/ppermute | solution.py:404
  72.9 1.5 %shard_map.182.upstream = f32[512,512]{1,0:T(8,128)S(1)} custom-call(bf16[512,512]{1,0:T(8,128)(2,1)S(1)} %copy-done.7, bf16[2048,512]{1,0:T(8,128)(2,1)S(1)} %get-tuple-element.132.grad_pre, bf16[1024,2048]{1,0:T(8,128)(2,1)S(1)} %get-tuple-element.106.refs_7_.there, bf16[3,512,512]{2,1,0:T(8,128)(2,1)S(1)} %copy-done.2), custom_call_target="tpu_custom_call" | custom-call | flops 1342177280 | bytes 9437184 | tf_op jit(solution)/shard_map/pallas_call | solution.py:83
  74.7 0.4 collective-permute-start.18
  75.0 1.5 %shard_map.183.refs_0_ = f32[512,512]{1,0:T(8,128)S(1)} custom-call(f32[512,512]{1,0:T(8,128)S(1)} %shard_map.182.upstream, bf16[2048,512]{1,0:T(8,128)(2,1)S(1)} %get-tuple-element.132.grad_pre, bf16[1024,2048]{1,0:T(8,128)(2,1)S(1)} %get-tuple-element.106.refs_7_.there, bf16[3,512,512]{2,1,0:T(8,128)(2,1)S(1)} %copy-done.4), custom_call_target="tpu_custom_call" | custom-call | flops 1342177280 | bytes 9961472 | tf_op jit(solution)/shard_map/pallas_call | solution.py:83
  76.6 2.6 %shard_map.184 = (f32[512,512]{1,0:T(8,128)S(1)}, bf16[2048,512]{1,0:T(8,128)(2,1)S(1)}, bf16[32,512]{1,0:T(8,128)(2,1)S(1)}, bf16[32,512]{1,0:T(8,128)(2,1)S(1)}) custom-call(f32[512,512]{1,0:T(8,128)S(1)} %shard_map.183.refs_0_, bf16[32,512]{1,0:T(8,128)(2,1)S(1)} %collective-permute-done.17.refs_1_, bf16[32,512]{1,0:T(8,128)(2,1)S(1)} %collective-permute-done.18.refs_2_, ...), custom_call_target="tpu_custom_call" | custom-call | flops 1711276032 | bytes 15472640 | tf_op jit(solution)/shard_map/pallas_call | solution.py:83
  79.1 1.2 %collective-permute-start.20 = (bf16[32,512]{1,0:T(8,128)(2,1)S(1)}, bf16[32,512]{1,0:T(8,128)(2,1)S(1)}, u32[]{:S(2)}, u32[]{:S(2)}) collective-permute-start(bf16[32,512]{1,0:T(8,128)(2,1)S(1)} %get-tuple-element.139), channel_id=1, source_target_pairs={{0,8},{1,13},{4,12},{5,9},{8,0},{9,5},{12,4},{13,1},{2,10},{3,15},... | collective-permute-start | bytes 98312 | tf_op jit(solution)/shard_map/ppermute | solution.py:541
  80.4 2.3 %collective-permute-start.22 = (bf16[32,512]{1,0:T(8,128)(2,1)S(1)}, bf16[32,512]{1,0:T(8,128)(2,1)S(1)}, u32[]{:S(2)}, u32[]{:S(2)}) collective-permute-start(bf16[32,512]{1,0:T(8,128)(2,1)S(1)} %get-tuple-element.144), channel_id=1, source_target_pairs={{4,0},{0,4},{12,8},{8,12},{5,1},{1,5},{13,9},{9,13},{6,2},{2,6},{1... | collective-permute-start | bytes 98312 | tf_op jit(solution)/shard_map/ppermute | solution.py:404
  82.6 1.5 %shard_map.185.upstream = f32[512,512]{1,0:T(8,128)S(1)} custom-call(f32[512,512]{1,0:T(8,128)S(1)} %get-tuple-element.140.upstream, bf16[2048,512]{1,0:T(8,128)(2,1)S(1)} %get-tuple-element.141.grad_pre, bf16[1024,2048]{1,0:T(8,128)(2,1)S(1)} %get-tuple-element.106.refs_7_.there, bf16[3,512,512]{2,1,0:T(8,128)(2,1)S(1)} %copy-done.2), custom_call_target="tpu_custom_call" | custom-call | flops 1342177280 | bytes 9961472 | tf_op jit(solution)/shard_map/pallas_call | solution.py:83
  84.4 1.5 %shard_map.186.refs_0_ = f32[512,512]{1,0:T(8,128)S(1)} custom-call(f32[512,512]{1,0:T(8,128)S(1)} %shard_map.185.upstream, bf16[2048,512]{1,0:T(8,128)(2,1)S(1)} %get-tuple-element.141.grad_pre, bf16[1024,2048]{1,0:T(8,128)(2,1)S(1)} %get-tuple-element.106.refs_7_.there, bf16[3,512,512]{2,1,0:T(8,128)(2,1)S(1)} %copy-done.4), custom_call_target="tpu_custom_call" | custom-call | flops 1342177280 | bytes 9961472 | tf_op jit(solution)/shard_map/pallas_call | solution.py:83
  86.0 2.8 %shard_map.187 = (f32[512,512]{1,0:T(8,128)S(1)}, bf16[2048,512]{1,0:T(8,128)(2,1)S(1)}, bf16[32,512]{1,0:T(8,128)(2,1)S(1)}, bf16[32,512]{1,0:T(8,128)(2,1)S(1)}) custom-call(f32[512,512]{1,0:T(8,128)S(1)} %shard_map.186.refs_0_, bf16[32,512]{1,0:T(8,128)(2,1)S(1)} %collective-permute-done.20.refs_1_, bf16[32,512]{1,0:T(8,128)(2,1)S(1)} %collective-permute-done.21.refs_2_, ...), custom_call_target="tpu_custom_call" | custom-call | flops 1711276032 | bytes 15472640 | tf_op jit(solution)/shard_map/pallas_call | solution.py:83
  88.8 0.8 collective-permute-start.23
  89.6 2.6 %collective-permute-start.25 = (bf16[32,512]{1,0:T(8,128)(2,1)S(1)}, bf16[32,512]{1,0:T(8,128)(2,1)S(1)}, u32[]{:S(2)}, u32[]{:S(2)}) collective-permute-start(bf16[32,512]{1,0:T(8,128)(2,1)S(1)} %get-tuple-element.152), channel_id=1, source_target_pairs={{4,0},{0,4},{12,8},{8,12},{5,1},{1,5},{13,9},{9,13},{6,2},{2,6},{1... | collective-permute-start | bytes 98312 | tf_op jit(solution)/shard_map/ppermute | solution.py:404
  92.2 1.5 %shard_map.188.upstream = f32[512,512]{1,0:T(8,128)S(1)} custom-call(f32[512,512]{1,0:T(8,128)S(1)} %get-tuple-element.148.upstream, bf16[2048,512]{1,0:T(8,128)(2,1)S(1)} %get-tuple-element.149.grad_pre, bf16[1024,2048]{1,0:T(8,128)(2,1)S(1)} %get-tuple-element.106.refs_7_.there, bf16[3,512,512]{2,1,0:T(8,128)(2,1)S(1)} %copy-done.2), custom_call_target="tpu_custom_call" | custom-call | flops 1342177280 | bytes 9961472 | tf_op jit(solution)/shard_map/pallas_call | solution.py:83
  93.7 0.4 collective-permute-start.24
  94.1 1.5 %shard_map.189.refs_0_ = f32[512,512]{1,0:T(8,128)S(1)} custom-call(f32[512,512]{1,0:T(8,128)S(1)} %shard_map.188.upstream, bf16[2048,512]{1,0:T(8,128)(2,1)S(1)} %get-tuple-element.149.grad_pre, bf16[1024,2048]{1,0:T(8,128)(2,1)S(1)} %get-tuple-element.106.refs_7_.there, bf16[3,512,512]{2,1,0:T(8,128)(2,1)S(1)} %copy-done.4), custom_call_target="tpu_custom_call" | custom-call | flops 1342177280 | bytes 9961472 | tf_op jit(solution)/shard_map/pallas_call | solution.py:83
  95.6 1.4 %shard_map.190 = (bf16[512,512]{1,0:T(8,128)(2,1)S(1)}, bf16[128,512]{1,0:T(8,128)(2,1)S(1)}, bf16[128,512]{1,0:T(8,128)(2,1)S(1)}) custom-call(f32[512,512]{1,0:T(8,128)S(1)} %shard_map.189.refs_0_, bf16[32,512]{1,0:T(8,128)(2,1)S(1)} %collective-permute-done.23.refs_1_, bf16[32,512]{1,0:T(8,128)(2,1)S(1)} %collective-permute-done.24.refs_2_, ...), custom_call_target="tpu_custom_call" | custom-call | flops 503316480 | bytes 5703680 | tf_op jit(solution)/shard_map/pallas_call | solution.py:83
  97.0 1.2 %collective-permute-start.27 = (bf16[128,512]{1,0:T(8,128)(2,1)S(1)}, bf16[128,512]{1,0:T(8,128)(2,1)S(1)}, u32[]{:S(2)}, u32[]{:S(2)}) collective-permute-start(bf16[128,512]{1,0:T(8,128)(2,1)S(1)} %get-tuple-element.166), channel_id=1, source_target_pairs={{4,0},{0,4},{12,8},{8,12},{5,1},{1,5},{13,9},{9,13},{6,2},{2,6},{1... | collective-permute-start | bytes 393224 | tf_op jit(solution)/shard_map/ppermute | solution.py:404
  98.2 0.9 collective-permute-start.29
  99.1 0.6 shard_map.191
  99.7 1.2 %collective-permute-start.26 = (bf16[256,512]{1,0:T(8,128)(2,1)S(1)}, bf16[256,512]{1,0:T(8,128)(2,1)S(1)}, u32[]{:S(2)}, u32[]{:S(2)}) collective-permute-start(bf16[256,512]{1,0:T(8,128)(2,1)S(1)} %get-tuple-element.164), channel_id=1, source_target_pairs={{4,0},{0,4},{12,8},{8,12},{5,1},{1,5},{13,9},{9,13},{6,2},{2,6},{1... | collective-permute-start | bytes 786440 | tf_op jit(solution)/shard_map/ppermute | solution.py:404
  100.9 2.5 %collective-permute-done.27.passed = bf16[128,512]{1,0:T(8,128)(2,1)S(1)} collective-permute-done((bf16[128,512]{1,0:T(8,128)(2,1)S(1)}, bf16[128,512]{1,0:T(8,128)(2,1)S(1)}, u32[]{:S(2)}, u32[]{:S(2)}) %collective-permute-start.27) | collective-permute-done | bytes 131104 | tf_op jit(solution)/shard_map/ppermute | solution.py:404
  103.5 1.5 %collective-permute-start.28 = (bf16[128,512]{1,0:T(8,128)(2,1)S(1)}, bf16[128,512]{1,0:T(8,128)(2,1)S(1)}, u32[]{:S(2)}, u32[]{:S(2)}) collective-permute-start(bf16[128,512]{1,0:T(8,128)(2,1)S(1)} %shard_map.192), channel_id=1, source_target_pairs={{8,0},{12,4},{0,8},{4,12},{9,1},{13,5},{1,9},{5,13},{10,2},{14,6},... | collective-permute-start | bytes 393224 | tf_op jit(solution)/shard_map/ppermute | solution.py:404
  104.9 2.7 %collective-permute-done.29.passed = bf16[128,512]{1,0:T(8,128)(2,1)S(1)} collective-permute-done((bf16[128,512]{1,0:T(8,128)(2,1)S(1)}, bf16[128,512]{1,0:T(8,128)(2,1)S(1)}, u32[]{:S(2)}, u32[]{:S(2)}) %collective-permute-start.29) | collective-permute-done | bytes 131104 | tf_op jit(solution)/shard_map/ppermute | solution.py:404
  107.7 5.6 %collective-permute-done.28.piece = bf16[128,512]{1,0:T(8,128)(2,1)S(1)} collective-permute-done((bf16[128,512]{1,0:T(8,128)(2,1)S(1)}, bf16[128,512]{1,0:T(8,128)(2,1)S(1)}, u32[]{:S(2)}, u32[]{:S(2)}) %collective-permute-start.28) | collective-permute-done | bytes 131104 | tf_op jit(solution)/shard_map/ppermute | solution.py:404
  113.4 2.4 %collective-permute-done.26.refs_1_ = bf16[256,512]{1,0:T(8,128)(2,1)S(1)} collective-permute-done((bf16[256,512]{1,0:T(8,128)(2,1)S(1)}, bf16[256,512]{1,0:T(8,128)(2,1)S(1)}, u32[]{:S(2)}, u32[]{:S(2)}) %collective-permute-start.26) | collective-permute-done | bytes 262176 | tf_op jit(solution)/shard_map/ppermute | solution.py:404
  115.8 3.5 %collective-permute-done.30.refs_3_ = bf16[128,512]{1,0:T(8,128)(2,1)S(1)} collective-permute-done((bf16[128,512]{1,0:T(8,128)(2,1)S(1)}, bf16[128,512]{1,0:T(8,128)(2,1)S(1)}, u32[]{:S(2)}, u32[]{:S(2)}) %collective-permute-start.30) | collective-permute-done | bytes 131104 | tf_op jit(solution)/shard_map/ppermute | solution.py:404
  119.2 1.3 %shard_map.195 = f32[256,512]{1,0:T(8,128)} custom-call(bf16[256,512]{1,0:T(8,128)(2,1)S(1)} %get-tuple-element.163.own.refs_0_, bf16[256,512]{1,0:T(8,128)(2,1)S(1)} %collective-permute-done.26.refs_1_, f32[128,512]{1,0:T(8,128)S(1)} %shard_map.193.refs_2_, bf16[128,512]{1,0:T(8,128)(2,1)S(1)} %collective-permute-done.30.refs_3_, bf16[512,512]{1,0:T(8,128)(2,1)S(1)} %copy-done.6), custom_call_target="tpu_custom_call" | custom-call | flops 134217728 | bytes 1966080 | tf_op jit(solution)/shard_map/pallas_call | solution.py:83
  (77 shorter events, 2.0 us)
Async XLA Ops:
  0.6 8.2 %copy-start = (s32[1,4,32]{2,1,0:T(4,128)S(1)}, s32[1,4,32]{2,1,0:T(4,128)}, u32[]{:S(2)}) copy-start(s32[1,4,32]{2,1,0:T(4,128)} %param.22) | copy-start | bytes 1540
  1.7 18.6 %collective-permute-start.3 = (bf16[272,512]{1,0:T(8,128)(2,1)S(1)}, bf16[272,512]{1,0:T(8,128)(2,1)S(1)}, u32[]{:S(2)}, u32[]{:S(2)}) collective-permute-start(bf16[272,512]{1,0:T(8,128)(2,1)S(1)} %shard_map.167.refs_5_), channel_id=1, source_target_pairs={{0,4},{4,0},{8,12},{12,8},{1,5},{5,1},{9,13},{13,9},{2,6},{6,2},{1... | collective-permute-start | bytes 835592 | tf_op jit(solution)/shard_map/ppermute | solution.py:399
  4.8 15.0 %collective-permute-start = (bf16[272,512]{1,0:T(8,128)(2,1)S(1)}, bf16[272,512]{1,0:T(8,128)(2,1)S(1)}, u32[]{:S(2)}, u32[]{:S(2)}) collective-permute-start(bf16[272,512]{1,0:T(8,128)(2,1)S(1)} %shard_map.167.refs_5_), channel_id=1, source_target_pairs={{0,8},{4,12},{8,0},{12,4},{1,9},{5,13},{9,1},{13,5},{2,10},{6,14},... | collective-permute-start | bytes 835592 | tf_op jit(solution)/shard_map/ppermute | solution.py:399
  8.7 1.2 collective-permute-start.1
  10.1 3.7 %collective-permute-start.2 = (s32[2,2,512]{2,0,1:T(2,128)S(1)}, s32[2,2,512]{2,0,1:T(2,128)S(1)}, u32[]{:S(2)}, u32[]{:S(2)}) collective-permute-start(s32[2,2,512]{2,0,1:T(2,128)S(1)} %fusion.1), channel_id=1, source_target_pairs={{0,2},{2,0},{1,3},{3,1},{4,6},{6,4},{5,7},{7,5},{8,10},{10,8},{9,1... | collective-permute-start | bytes 24584 | tf_op jit(solution)/shard_map/ppermute | solution.py:390
  14.0 6.4 %copy-start.6 = (bf16[512,512]{1,0:T(8,128)(2,1)S(1)}, bf16[512,512]{1,0:T(8,128)(2,1)}, u32[]{:S(2)}) copy-start(bf16[512,512]{1,0:T(8,128)(2,1)} %refs_4_.3) | copy-start | bytes 1572868
  14.0 6.4 %copy-start.8 = (bf16[512,512]{1,0:T(8,128)(2,1)S(1)}, bf16[512,512]{1,0:T(8,128)(2,1)}, u32[]{:S(2)}) copy-start(bf16[512,512]{1,0:T(8,128)(2,1)} %hidden.1) | copy-start | bytes 1572868
  14.0 6.4 %copy-start.11 = (bf16[512,512]{1,0:T(8,128)(2,1)S(1)}, bf16[512,512]{1,0:T(8,128)(2,1)}, u32[]{:S(2)}) copy-start(bf16[512,512]{1,0:T(8,128)(2,1)} %refs_3_.2) | copy-start | bytes 1572868
  19.8 6.5 %collective-permute-start.4 = (bf16[272,512]{1,0:T(8,128)(2,1)S(1)}, bf16[272,512]{1,0:T(8,128)(2,1)S(1)}, u32[]{:S(2)}, u32[]{:S(2)}) collective-permute-start(bf16[272,512]{1,0:T(8,128)(2,1)S(1)} %collective-permute-done.refs_4_), channel_id=1, source_target_pairs={{0,4},{4,0},{8,12},{12,8},{1,5},{5,1},{9,13},{13,9},{2,6},{6,2},{1... | collective-permute-start | bytes 835592 | tf_op jit(solution)/shard_map/ppermute | solution.py:399
  26.3 12.6 %copy-start.2 = (bf16[3,512,512]{2,1,0:T(8,128)(2,1)S(1)}, bf16[3,512,512]{2,1,0:T(8,128)(2,1)}, u32[]{:S(2)}) copy-start(bf16[3,512,512]{2,1,0:T(8,128)(2,1)} %refs_5_.5) | copy-start | bytes 4718596
  26.3 12.6 %copy-start.5 = (bf16[512,512]{1,0:T(8,128)(2,1)S(1)}, bf16[512,512]{1,0:T(8,128)(2,1)}, u32[]{:S(2)}) copy-start(bf16[512,512]{1,0:T(8,128)(2,1)} %refs_8_.11) | copy-start | bytes 1572868
  26.3 12.6 %copy-start.10 = (f32[512]{0:T(512)S(1)}, f32[512]{0:T(512)}, u32[]{:S(2)}) copy-start(f32[512]{0:T(512)} %param.26) | copy-start | bytes 6148
  27.2 1.6 %collective-permute-start.5 = (bf16[256,512]{1,0:T(8,128)(2,1)S(1)}, bf16[256,512]{1,0:T(8,128)(2,1)S(1)}, u32[]{:S(2)}, u32[]{:S(2)}) collective-permute-start(bf16[256,512]{1,0:T(8,128)(2,1)S(1)} %get-tuple-element.92), channel_id=1, source_target_pairs={{0,1},{1,0},{2,3},{3,2},{4,5},{5,4},{6,7},{7,6},{8,9},{9,8},{10,11... | collective-permute-start | bytes 786440 | tf_op jit(solution)/shard_map/ppermute | solution.py:390
  28.9 14.0 %copy-start.4 = (bf16[3,512,512]{2,1,0:T(8,128)(2,1)S(1)}, bf16[3,512,512]{2,1,0:T(8,128)(2,1)}, u32[]{:S(2)}) copy-start(bf16[3,512,512]{2,1,0:T(8,128)(2,1)} %weights.11) | copy-start | bytes 4718596
  28.9 8.4 %collective-permute-start.6 = (bf16[256,512]{1,0:T(8,128)(2,1)S(1)}, bf16[256,512]{1,0:T(8,128)(2,1)S(1)}, u32[]{:S(2)}, u32[]{:S(2)}) collective-permute-start(bf16[256,512]{1,0:T(8,128)(2,1)S(1)} %add_convert_fusion.1), channel_id=1, source_target_pairs={{0,2},{2,0},{1,3},{3,1},{4,6},{6,4},{5,7},{7,5},{8,10},{10,8},{9,1... | collective-permute-start | bytes 786440 | tf_op jit(solution)/shard_map/ppermute | solution.py:390
  37.4 1.6 %collective-permute-start.7 = (bf16[256,512]{1,0:T(8,128)(2,1)S(1)}, bf16[256,512]{1,0:T(8,128)(2,1)S(1)}, u32[]{:S(2)}, u32[]{:S(2)}) collective-permute-start(bf16[256,512]{1,0:T(8,128)(2,1)S(1)} %add_convert_fusion.refs_1_), channel_id=1, source_target_pairs={{0,1},{1,0},{2,3},{3,2},{4,5},{5,4},{6,7},{7,6},{8,9},{9,8},{10,11... | collective-permute-start | bytes 786440 | tf_op jit(solution)/shard_map/ppermute | solution.py:390
  39.7 5.4 %collective-permute-start.8 = (bf16[32,512]{1,0:T(8,128)(2,1)S(1)}, bf16[32,512]{1,0:T(8,128)(2,1)S(1)}, u32[]{:S(2)}, u32[]{:S(2)}) collective-permute-start(bf16[32,512]{1,0:T(8,128)(2,1)S(1)} %get-tuple-element.93), channel_id=1, source_target_pairs={{0,8},{1,13},{4,12},{5,9},{8,0},{9,5},{12,4},{13,1},{2,10},{3,15},... | collective-permute-start | bytes 98312 | tf_op jit(solution)/shard_map/ppermute | solution.py:541
  41.1 5.5 %collective-permute-start.10 = (bf16[32,512]{1,0:T(8,128)(2,1)S(1)}, bf16[32,512]{1,0:T(8,128)(2,1)S(1)}, u32[]{:S(2)}, u32[]{:S(2)}) collective-permute-start(bf16[32,512]{1,0:T(8,128)(2,1)S(1)} %get-tuple-element.104), channel_id=1, source_target_pairs={{0,4},{4,0},{8,12},{12,8},{1,5},{5,1},{9,13},{13,9},{2,6},{6,2},{1... | collective-permute-start | bytes 98312 | tf_op jit(solution)/shard_map/ppermute | solution.py:399
  45.2 1.4 %copy-start.3 = (bf16[3,512,512]{2,1,0:T(8,128)(2,1)S(1)}, bf16[3,512,512]{2,1,0:T(8,128)(2,1)}, u32[]{:S(2)}) copy-start(bf16[3,512,512]{2,1,0:T(8,128)(2,1)} %refs_9_.9) | copy-start | bytes 4718596
  45.2 1.4 %copy-start.9 = (f32[3,512]{1,0:T(4,128)S(1)}, f32[3,512]{1,0:T(4,128)}, u32[]{:S(2)}) copy-start(f32[3,512]{1,0:T(4,128)} %refs_8_.10) | copy-start | bytes 18436
  45.2 1.3 %collective-permute-start.9 = (bf16[32,512]{1,0:T(8,128)(2,1)S(1)}, bf16[32,512]{1,0:T(8,128)(2,1)S(1)}, u32[]{:S(2)}, u32[]{:S(2)}) collective-permute-start(bf16[32,512]{1,0:T(8,128)(2,1)S(1)} %collective-permute-done.8.refs_3_), channel_id=1, source_target_pairs={{0,1},{1,0},{2,3},{3,2},{4,5},{5,4},{6,7},{7,6},{8,9},{9,8},{10,11... | collective-permute-start | bytes 98312 | tf_op jit(solution)/shard_map/ppermute | solution.py:390
  49.1 5.3 %collective-permute-start.11 = (bf16[32,512]{1,0:T(8,128)(2,1)S(1)}, bf16[32,512]{1,0:T(8,128)(2,1)S(1)}, u32[]{:S(2)}, u32[]{:S(2)}) collective-permute-start(bf16[32,512]{1,0:T(8,128)(2,1)S(1)} %get-tuple-element.107), channel_id=1, source_target_pairs={{0,8},{1,13},{4,12},{5,9},{8,0},{9,5},{12,4},{13,1},{2,10},{3,15},... | collective-permute-start | bytes 98312 | tf_op jit(solution)/shard_map/ppermute | solution.py:541
  50.3 5.4 %collective-permute-start.13 = (bf16[32,512]{1,0:T(8,128)(2,1)S(1)}, bf16[32,512]{1,0:T(8,128)(2,1)S(1)}, u32[]{:S(2)}, u32[]{:S(2)}) collective-permute-start(bf16[32,512]{1,0:T(8,128)(2,1)S(1)} %get-tuple-element.117), channel_id=1, source_target_pairs={{0,4},{4,0},{8,12},{12,8},{1,5},{5,1},{9,13},{13,9},{2,6},{6,2},{1... | collective-permute-start | bytes 98312 | tf_op jit(solution)/shard_map/ppermute | solution.py:399
  54.4 1.4 %collective-permute-start.12 = (bf16[32,512]{1,0:T(8,128)(2,1)S(1)}, bf16[32,512]{1,0:T(8,128)(2,1)S(1)}, u32[]{:S(2)}, u32[]{:S(2)}) collective-permute-start(bf16[32,512]{1,0:T(8,128)(2,1)S(1)} %collective-permute-done.11.refs_3_), channel_id=1, source_target_pairs={{0,1},{1,0},{2,3},{3,2},{4,5},{5,4},{6,7},{7,6},{8,9},{9,8},{10,11... | collective-permute-start | bytes 98312 | tf_op jit(solution)/shard_map/ppermute | solution.py:390
  58.3 5.2 %collective-permute-start.14 = (bf16[32,512]{1,0:T(8,128)(2,1)S(1)}, bf16[32,512]{1,0:T(8,128)(2,1)S(1)}, u32[]{:S(2)}, u32[]{:S(2)}) collective-permute-start(bf16[32,512]{1,0:T(8,128)(2,1)S(1)} %get-tuple-element.118), channel_id=1, source_target_pairs={{0,8},{1,13},{4,12},{5,9},{8,0},{9,5},{12,4},{13,1},{2,10},{3,15},... | collective-permute-start | bytes 98312 | tf_op jit(solution)/shard_map/ppermute | solution.py:541
  59.7 5.2 %collective-permute-start.16 = (bf16[32,512]{1,0:T(8,128)(2,1)S(1)}, bf16[32,512]{1,0:T(8,128)(2,1)S(1)}, u32[]{:S(2)}, u32[]{:S(2)}) collective-permute-start(bf16[32,512]{1,0:T(8,128)(2,1)S(1)} %get-tuple-element.128), channel_id=1, source_target_pairs={{0,4},{4,0},{8,12},{12,8},{1,5},{5,1},{9,13},{13,9},{2,6},{6,2},{1... | collective-permute-start | bytes 98312 | tf_op jit(solution)/shard_map/ppermute | solution.py:399
  63.5 1.4 %copy-start.7 = (bf16[512,512]{1,0:T(8,128)(2,1)S(1)}, bf16[512,512]{1,0:T(8,128)(2,1)}, u32[]{:S(2)}) copy-start(bf16[512,512]{1,0:T(8,128)(2,1)} %upstream.1) | copy-start | bytes 1572868
  63.5 1.3 %collective-permute-start.15 = (bf16[32,512]{1,0:T(8,128)(2,1)S(1)}, bf16[32,512]{1,0:T(8,128)(2,1)S(1)}, u32[]{:S(2)}, u32[]{:S(2)}) collective-permute-start(bf16[32,512]{1,0:T(8,128)(2,1)S(1)} %collective-permute-done.14.refs_3_), channel_id=1, source_target_pairs={{0,1},{1,0},{2,3},{3,2},{4,5},{5,4},{6,7},{7,6},{8,9},{9,8},{10,11... | collective-permute-start | bytes 98312 | tf_op jit(solution)/shard_map/ppermute | solution.py:390
  69.8 4.8 %collective-permute-start.17 = (bf16[32,512]{1,0:T(8,128)(2,1)S(1)}, bf16[32,512]{1,0:T(8,128)(2,1)S(1)}, u32[]{:S(2)}, u32[]{:S(2)}) collective-permute-start(bf16[32,512]{1,0:T(8,128)(2,1)S(1)} %get-tuple-element.131), channel_id=1, source_target_pairs={{0,8},{1,13},{4,12},{5,9},{8,0},{9,5},{12,4},{13,1},{2,10},{3,15},... | collective-permute-start | bytes 98312 | tf_op jit(solution)/shard_map/ppermute | solution.py:541
  71.4 5.2 %collective-permute-start.19 = (bf16[32,512]{1,0:T(8,128)(2,1)S(1)}, bf16[32,512]{1,0:T(8,128)(2,1)S(1)}, u32[]{:S(2)}, u32[]{:S(2)}) collective-permute-start(bf16[32,512]{1,0:T(8,128)(2,1)S(1)} %get-tuple-element.135), channel_id=1, source_target_pairs={{4,0},{0,4},{12,8},{8,12},{5,1},{1,5},{13,9},{9,13},{6,2},{2,6},{1... | collective-permute-start | bytes 98312 | tf_op jit(solution)/shard_map/ppermute | solution.py:404
  74.7 1.9 %collective-permute-start.18 = (bf16[32,512]{1,0:T(8,128)(2,1)S(1)}, bf16[32,512]{1,0:T(8,128)(2,1)S(1)}, u32[]{:S(2)}, u32[]{:S(2)}) collective-permute-start(bf16[32,512]{1,0:T(8,128)(2,1)S(1)} %collective-permute-done.17.refs_1_), channel_id=1, source_target_pairs={{0,1},{1,0},{2,3},{3,2},{4,5},{5,4},{6,7},{7,6},{8,9},{9,8},{10,11... | collective-permute-start | bytes 98312 | tf_op jit(solution)/shard_map/ppermute | solution.py:390
  79.1 5.3 %collective-permute-start.20 = (bf16[32,512]{1,0:T(8,128)(2,1)S(1)}, bf16[32,512]{1,0:T(8,128)(2,1)S(1)}, u32[]{:S(2)}, u32[]{:S(2)}) collective-permute-start(bf16[32,512]{1,0:T(8,128)(2,1)S(1)} %get-tuple-element.139), channel_id=1, source_target_pairs={{0,8},{1,13},{4,12},{5,9},{8,0},{9,5},{12,4},{13,1},{2,10},{3,15},... | collective-permute-start | bytes 98312 | tf_op jit(solution)/shard_map/ppermute | solution.py:541
  80.4 5.6 %collective-permute-start.22 = (bf16[32,512]{1,0:T(8,128)(2,1)S(1)}, bf16[32,512]{1,0:T(8,128)(2,1)S(1)}, u32[]{:S(2)}, u32[]{:S(2)}) collective-permute-start(bf16[32,512]{1,0:T(8,128)(2,1)S(1)} %get-tuple-element.144), channel_id=1, source_target_pairs={{4,0},{0,4},{12,8},{8,12},{5,1},{1,5},{13,9},{9,13},{6,2},{2,6},{1... | collective-permute-start | bytes 98312 | tf_op jit(solution)/shard_map/ppermute | solution.py:404
  84.4 1.5 %collective-permute-start.21 = (bf16[32,512]{1,0:T(8,128)(2,1)S(1)}, bf16[32,512]{1,0:T(8,128)(2,1)S(1)}, u32[]{:S(2)}, u32[]{:S(2)}) collective-permute-start(bf16[32,512]{1,0:T(8,128)(2,1)S(1)} %collective-permute-done.20.refs_1_), channel_id=1, source_target_pairs={{0,1},{1,0},{2,3},{3,2},{4,5},{5,4},{6,7},{7,6},{8,9},{9,8},{10,11... | collective-permute-start | bytes 98312 | tf_op jit(solution)/shard_map/ppermute | solution.py:390
  88.8 4.9 %collective-permute-start.23 = (bf16[32,512]{1,0:T(8,128)(2,1)S(1)}, bf16[32,512]{1,0:T(8,128)(2,1)S(1)}, u32[]{:S(2)}, u32[]{:S(2)}) collective-permute-start(bf16[32,512]{1,0:T(8,128)(2,1)S(1)} %get-tuple-element.147), channel_id=1, source_target_pairs={{0,8},{1,13},{4,12},{5,9},{8,0},{9,5},{12,4},{13,1},{2,10},{3,15},... | collective-permute-start | bytes 98312 | tf_op jit(solution)/shard_map/ppermute | solution.py:541
  89.6 6.0 %collective-permute-start.25 = (bf16[32,512]{1,0:T(8,128)(2,1)S(1)}, bf16[32,512]{1,0:T(8,128)(2,1)S(1)}, u32[]{:S(2)}, u32[]{:S(2)}) collective-permute-start(bf16[32,512]{1,0:T(8,128)(2,1)S(1)} %get-tuple-element.152), channel_id=1, source_target_pairs={{4,0},{0,4},{12,8},{8,12},{5,1},{1,5},{13,9},{9,13},{6,2},{2,6},{1... | collective-permute-start | bytes 98312 | tf_op jit(solution)/shard_map/ppermute | solution.py:404
  93.7 1.9 %collective-permute-start.24 = (bf16[32,512]{1,0:T(8,128)(2,1)S(1)}, bf16[32,512]{1,0:T(8,128)(2,1)S(1)}, u32[]{:S(2)}, u32[]{:S(2)}) collective-permute-start(bf16[32,512]{1,0:T(8,128)(2,1)S(1)} %collective-permute-done.23.refs_1_), channel_id=1, source_target_pairs={{0,1},{1,0},{2,3},{3,2},{4,5},{5,4},{6,7},{7,6},{8,9},{9,8},{10,11... | collective-permute-start | bytes 98312 | tf_op jit(solution)/shard_map/ppermute | solution.py:390
  97.0 6.4 %collective-permute-start.27 = (bf16[128,512]{1,0:T(8,128)(2,1)S(1)}, bf16[128,512]{1,0:T(8,128)(2,1)S(1)}, u32[]{:S(2)}, u32[]{:S(2)}) collective-permute-start(bf16[128,512]{1,0:T(8,128)(2,1)S(1)} %get-tuple-element.166), channel_id=1, source_target_pairs={{4,0},{0,4},{12,8},{8,12},{5,1},{1,5},{13,9},{9,13},{6,2},{2,6},{1... | collective-permute-start | bytes 393224 | tf_op jit(solution)/shard_map/ppermute | solution.py:404
  98.2 9.4 %collective-permute-start.29 = (bf16[128,512]{1,0:T(8,128)(2,1)S(1)}, bf16[128,512]{1,0:T(8,128)(2,1)S(1)}, u32[]{:S(2)}, u32[]{:S(2)}) collective-permute-start(bf16[128,512]{1,0:T(8,128)(2,1)S(1)} %get-tuple-element.167), channel_id=1, source_target_pairs={{4,0},{0,4},{12,8},{8,12},{5,1},{1,5},{13,9},{9,13},{6,2},{2,6},{1... | collective-permute-start | bytes 393224 | tf_op jit(solution)/shard_map/ppermute | solution.py:404
  99.1 21.4 %copy-start.1 = (s32[1,4,32]{2,1,0:T(4,128)S(1)}, s32[1,4,32]{2,1,0:T(4,128)}, u32[]{:S(2)}) copy-start(s32[1,4,32]{2,1,0:T(4,128)} %param.22) | copy-start | bytes 1540
  99.7 16.1 %collective-permute-start.26 = (bf16[256,512]{1,0:T(8,128)(2,1)S(1)}, bf16[256,512]{1,0:T(8,128)(2,1)S(1)}, u32[]{:S(2)}, u32[]{:S(2)}) collective-permute-start(bf16[256,512]{1,0:T(8,128)(2,1)S(1)} %get-tuple-element.164), channel_id=1, source_target_pairs={{4,0},{0,4},{12,8},{8,12},{5,1},{1,5},{13,9},{9,13},{6,2},{2,6},{1... | collective-permute-start | bytes 786440 | tf_op jit(solution)/shard_map/ppermute | solution.py:404
  103.5 9.9 %collective-permute-start.28 = (bf16[128,512]{1,0:T(8,128)(2,1)S(1)}, bf16[128,512]{1,0:T(8,128)(2,1)S(1)}, u32[]{:S(2)}, u32[]{:S(2)}) collective-permute-start(bf16[128,512]{1,0:T(8,128)(2,1)S(1)} %shard_map.192), channel_id=1, source_target_pairs={{8,0},{12,4},{0,8},{4,12},{9,1},{13,5},{1,9},{5,13},{10,2},{14,6},... | collective-permute-start | bytes 393224 | tf_op jit(solution)/shard_map/ppermute | solution.py:404
  107.7 11.6 %collective-permute-start.30 = (bf16[128,512]{1,0:T(8,128)(2,1)S(1)}, bf16[128,512]{1,0:T(8,128)(2,1)S(1)}, u32[]{:S(2)}, u32[]{:S(2)}) collective-permute-start(bf16[128,512]{1,0:T(8,128)(2,1)S(1)} %shard_map.194), channel_id=1, source_target_pairs={{8,0},{12,4},{0,8},{4,12},{9,1},{13,5},{1,9},{5,13},{10,2},{14,6},... | collective-permute-start | bytes 393224 | tf_op jit(solution)/shard_map/ppermute | solution.py:404
